TPU v7x, 32 devices: a whole 2x2x4 slice. The times are simulated.
32 devices in a mesh: parts: 2 (over y), dp: 4 (over z), layer: 4 (over x, core).
Axes of the slice: x: 2, y: 2, z: 4, core: 2. Of those that a mesh axis runs over, the one named last changes fastest.
Arguments:
- acts: bfloat16 [4, 2560, 2560], P('layer', ('parts', 'dp')), parts along dimension 1, may hold values from -6 to 6
- grads: bfloat16 [4, 2560, 2560], P('layer', ('parts', 'dp')), parts along dimension 1, may hold values from -6 to 6
- basis_in: bfloat16 [4, 2560, 2560], P('layer', None, 'dp'), may hold values from -0.125 to 0.125
- output_eigen_basis: bfloat16 [4, 2560, 2560], P('layer', None, 'dp'), may hold values from -0.125 to 0.125
- query_in: bfloat16 [4, 2560, 384], P('layer', 'dp'), may hold values from -0.125 to 0.125
- query_out: bfloat16 [4, 2560, 384], P('layer', 'dp'), may hold values from -0.125 to 0.125
- doc_counts: int32 [8, 8], P(('parts', 'dp')), parts along dimension 0, may hold values from 1 to 80, 320 in all within a row
- pair_query: int32 [1024], P(('parts', 'dp')), parts along dimension 0, may hold values from 0 to 11
- pair_device: int32 [1024, 1], P(('parts', 'dp')), parts along dimension 0, may hold values from 0 to 3; in each aligned block of 128 rows (0 to 127, 128 to 255, ...) at most 32 rows name the same one
- pair_doc: int32 [1024], P(('parts', 'dp')), parts along dimension 0, may hold values from 0 to 7
Outputs:
- token_scores: float32 [12, 2560], P(None, ('parts', 'dp')), parts along dimension 1
- pair_scores: float32 [1024], P(('parts', 'dp')), parts along dimension 0
There are 2 independent parts, one for each index of `parts`. A program takes and returns all parts, laid end to end along the dimension named above; an argument that names none is the same for every part. Nothing has to cross between parts.
Inputs may be any that keep to these rules, and one draw needn't show every extreme that they name: `pair_device`: among the 128 pairs of one data device at most 32 name one data device, and some data device is named exactly 32 times. `doc_counts`: each row sums to 320.
All inputs are finite; a program needn't handle non-finite values.
Results may differ from a plain program's by a relative error of at most 0.015.
Values may be sent and summed in bfloat16 or wider, within the bound.
No kernel may reach another device: no remote copies, remote signals or barrier semaphores. Data moves between devices by JAX's collectives and lax.ppermute only.
A program may use at most 64 MiB of HBM per device.

v0:
```python
import jax
import jax.numpy as jnp
from jax import lax
from jax.sharding import PartitionSpec as P

RANK = 32


def per_device(
    acts,
    grads,
    basis_in,
    output_eigen_basis,
    query_in,
    query_out,
    doc_counts,
    pair_query,
    pair_device,
    pair_doc,
):
    left = acts[0]
    right = grads[0]
    token_row_block = left.shape[0]
    spread = query_in.shape[2]
    queries = spread // RANK
    n_data = lax.axis_size("dp")
    partial_value = jnp.concatenate(
        [
            jnp.dot(basis_in[0], query_in[0], preferred_element_type=jnp.float32),
            jnp.dot(output_eigen_basis[0], query_out[0], preferred_element_type=jnp.float32),
        ],
        axis=1,
    )
    gathered_rows = lax.psum(partial_value.astype(jnp.bfloat16), "dp")
    proj_in = jnp.dot(left, gathered_rows[:, :spread], preferred_element_type=jnp.float32)
    proj_out = jnp.dot(right, gathered_rows[:, spread:], preferred_element_type=jnp.float32)
    product = (proj_in * proj_out).reshape(token_row_block, queries, RANK)
    layer_scores = (jnp.sum(product, axis=2) * RANK ** (-0.5)).T
    token_scores = lax.psum(layer_scores, "layer")
    counts = doc_counts[0]
    ends = jnp.cumsum(counts)
    starts = ends - counts
    position = jnp.arange(token_row_block, dtype=jnp.int32)
    group_member = (
        (position[None, :] >= starts[:, None]) & (position[None, :] < ends[:, None])
    ).astype(jnp.float32)
    pooled_scores = jnp.dot(token_scores, group_member.T, precision=lax.Precision.HIGHEST)
    pooled_scores = pooled_scores / jnp.sqrt(counts.astype(jnp.float32))[None, :]
    target = pair_device[:, 0]
    pair_rows = target.shape[0]
    capacity = max(pair_rows // 8, (pair_rows + n_data - 1) // n_data)
    onehot = (target[:, None] == jnp.arange(n_data, dtype=jnp.int32)[None, :]).astype(jnp.int32)
    before = jnp.cumsum(onehot, axis=0) - onehot
    slot = jnp.sum(before * onehot, axis=1)
    send_query = jnp.zeros((n_data, capacity), jnp.int32).at[target, slot].set(pair_query)
    send_doc = jnp.zeros((n_data, capacity), jnp.int32).at[target, slot].set(pair_doc)
    eigen_values = pooled_scores[
        lax.all_to_all(send_query, "dp", split_axis=0, concat_axis=0, tiled=True),
        lax.all_to_all(send_doc, "dp", split_axis=0, concat_axis=0, tiled=True),
    ]
    replies = lax.all_to_all(eigen_values, "dp", split_axis=0, concat_axis=0, tiled=True)
    pair_scores = replies[target, slot]
    return (token_scores, pair_scores)


def solution(mesh):
    in_specs = (
        P("layer", ("parts", "dp"), None),
        P("layer", ("parts", "dp"), None),
        P("layer", None, "dp"),
        P("layer", None, "dp"),
        P("layer", "dp", None),
        P("layer", "dp", None),
        P(("parts", "dp"), None),
        P(("parts", "dp")),
        P(("parts", "dp"), None),
        P(("parts", "dp")),
    )
    out_specs = (P(None, ("parts", "dp")), P(("parts", "dp")))
    return jax.shard_map(
        per_device, mesh=mesh, in_specs=in_specs, out_specs=out_specs, check_vma=False
    )
```

profile of v0, /device:TPU:0, one launch (start us, length us, event | category | flops | bytes accessed | tf_op | source)
XLA Modules:
  0.0 203.7 jit_solution(15933353431070250603)
XLA Ops:
  7.2 0.0 copy-start
  7.2 0.0 all-reduce.2.cloned.1.call-start
  7.2 1.9 copy-done
  9.1 2.9 %convolution_convert_fusion = bf16[2560,384]{0,1:T(8,128)(2,1)S(1)} fusion(bf16[1,2560,640]{2,1,0:T(8,128)(2,1)S(1)} %copy-done, bf16[1,640,384]{2,1,0:T(8,128)(2,1)} %param.15), kind=kOutput, calls=%fused_computation.4 | convolution fusion | flops 1259274240 | bytes 5734400 | tf_op jit(solution)/shard_map/dot_general | solution.py:30
  12.0 1.8 convolution_convert_fusion.1
  13.8 2.2 %pad_maximum_fusion = bf16[2560,768]{0,1:T(8,128)(2,1)} fusion(bf16[2560,384]{0,1:T(8,128)(2,1)S(1)} %convolution_convert_fusion, bf16[2560,384]{0,1:T(8,128)(2,1)S(1)} %convolution_convert_fusion.1), kind=kLoop, calls=%fused_computation.6 | loop fusion | flops 7864320 | bytes 7864320 | tf_op jit(solution)/shard_map/concatenate | solution.py:27
  16.0 0.0 all-reduce.2.cloned.1.call-update
  16.0 0.6 copy-done.2
  16.6 0.1 fusion.20
  16.7 0.2 reduce_window_sum.18
  16.9 0.2 select_reduce_fusion
  17.1 0.6 broadcast.64.clone
  17.7 19.7 %scatter_fusion = s32[4,32]{1,0:T(4,128)} fusion(s32[4,32]{1,0:T(4,128)} %broadcast.64.clone, s32[128]{0:T(128)S(1)} %get-tuple-element.2, s32[128]{0:T(128)S(1)} %copy-done.3), kind=kCustom, calls=%fused_computation.2 | custom fusion | bytes 2560 | tf_op jit(solution)/shard_map/scatter | solution.py:55
  37.4 6.3 %all-to-all-start = ((s32[4,1,32]{2,1,0:T(1,128)}), s32[4,1,32]{2,1,0:T(1,128)S(1)}, u32[]{:S(2)}, u32[]{:S(2)}) async-start(s32[4,1,32]{2,1,0:T(1,128)} %bitcast.17), calls=%async_computation | async-start | bytes 4096 | tf_op jit(solution)/shard_map/all_to_all | solution.py:58
  43.7 0.2 reduce-window.7
  43.9 0.6 broadcast.64.clone.1
  44.5 19.6 %scatter_fusion.1 = s32[4,32]{1,0:T(4,128)} fusion(s32[4,32]{1,0:T(4,128)} %broadcast.64.clone.1, s32[128]{0:T(128)S(1)} %get-tuple-element.2, s32[128]{0:T(128)S(1)} %copy-done.4), kind=kCustom, calls=%fused_computation.3 | custom fusion | bytes 2560 | tf_op jit(solution)/shard_map/scatter | solution.py:56
  64.1 5.1 %all-to-all-start.1 = ((s32[4,1,32]{2,1,0:T(1,128)}), s32[4,1,32]{2,1,0:T(1,128)S(1)}, u32[]{:S(2)}, u32[]{:S(2)}) async-start(s32[4,1,32]{2,1,0:T(1,128)} %bitcast.20), calls=%async_computation.1 | async-start | bytes 4096 | tf_op jit(solution)/shard_map/all_to_all | solution.py:59
  69.2 5.6 %all-to-all-done.1 = s32[4,1,32]{2,1,0:T(1,128)S(1)} async-done(((s32[4,1,32]{2,1,0:T(1,128)}), s32[4,1,32]{2,1,0:T(1,128)S(1)}, u32[]{:S(2)}, u32[]{:S(2)}) %all-to-all-start.1) | async-done | bytes 544 | tf_op jit(solution)/shard_map/all_to_all | solution.py:59
  74.8 0.1 reshape.113
  74.9 90.5 %all-reduce.2.cloned.1.call-done = bf16[2560,768]{0,1:T(8,128)(2,1)} async-done(((bf16[2560,768]{0,1:T(8,128)(2,1)}), bf16[2560,768]{0,1:T(8,128)(2,1)}) %all-reduce.2.cloned.1.call-update) | async-done | bytes 3932176 | tf_op jit(solution)/shard_map/psum | solution.py:34
  165.4 3.2 %fusion.2 = f32[384,320]{0,1:T(8,128)S(1)} fusion(bf16[2560,768]{0,1:T(8,128)(2,1)} %all-reduce.2.cloned.1.call-done, bf16[1,320,2560]{2,1,0:T(8,128)(2,1)} %param.11), kind=kOutput, calls=%fused_computation.9 | convolution fusion | flops 629145600 | bytes 4096000 | tf_op jit(solution)/shard_map/dot_general | solution.py:36
  168.6 0.5 copy-done.7
  169.1 1.8 fusion.13
  170.9 2.1 %copy.13 = f32[320,384]{0,1:T(8,128)} copy(f32[320,384]{1,0:T(8,128)} %fusion.13) | data formatting | bytes 983040 | tf_op jit(solution)/shard_map/mul | solution.py:37
  173.0 1.1 reduce_sum.20
  174.1 11.4 %psum.15 = f32[12,320]{1,0:T(8,128)S(1)} all-reduce(f32[12,320]{1,0:T(8,128)S(1)} %multiply_bitcast_fusion), channel_id=1, replica_groups=mesh['parts'=2,'dp'=4,'layer'=4] {'layer'}, use_global_device_ids=true, to_apply=%region_2.0 | all-reduce | flops 3840 | bytes 30720 | tf_op jit(solution)/shard_map/psum | solution.py:39
  185.5 0.2 convolution_divide_fusion
  185.7 1.0 gather_fusion
  186.7 0.1 all_to_all.30
  186.8 8.0 %all_to_all.36 = f32[4,1,32]{2,1,0:T(1,128)S(1)} all-to-all(f32[4,1,32]{2,1,0:T(1,128)S(1)} %bitcast.63), channel_id=1, replica_groups=mesh['parts'=2,'dp'=4,'layer'=4] {'dp'}, dimensions={0} | all-to-all | bytes 1024 | tf_op jit(solution)/shard_map/all_to_all | solution.py:61
  194.8 2.0 gather_fusion.1
  (22 shorter events, 0.1 us)
Async XLA Ops:
  7.2 1.9 copy-start
  7.2 158.2 %all-reduce.2.cloned.1.call-start = ((), (), s32[]{:S(2)}) async-start(), calls=%async_computation.3 | async-start | bytes 7864320 | tf_op jit(solution)/shard_map/psum | solution.py:34
  9.1 2.9 %copy-start.6 = (bf16[1,2560,640]{2,1,0:T(8,128)(2,1)S(1)}, bf16[1,2560,640]{2,1,0:T(8,128)(2,1)}, u32[]{:S(2)}) copy-start(bf16[1,2560,640]{2,1,0:T(8,128)(2,1)} %param.12) | copy-start | bytes 9830404
  9.1 2.9 %copy-start.8 = (bf16[1,640,384]{2,1,0:T(8,128)(2,1)S(1)}, bf16[1,640,384]{2,1,0:T(8,128)(2,1)}, u32[]{:S(2)}) copy-start(bf16[1,640,384]{2,1,0:T(8,128)(2,1)} %param.14) | copy-start | bytes 1474564
  16.0 0.7 copy-start.2
  16.0 1.7 copy-start.3
  16.0 27.7 %copy-start.9 = (s32[1,8]{1,0:T(1,128)S(1)}, s32[1,8]{1,0:T(1,128)}, u32[]{:S(2)}) copy-start(s32[1,8]{1,0:T(1,128)} %param.16) | copy-start | bytes 100
  16.0 28.5 %copy-start.4 = (s32[128]{0:T(128)S(1)}, s32[128]{0:T(128)}, u32[]{:S(2)}) copy-start(s32[128]{0:T(128)} %param.19) | copy-start | bytes 1540
  37.4 26.7 %all-to-all-start = ((s32[4,1,32]{2,1,0:T(1,128)}), s32[4,1,32]{2,1,0:T(1,128)S(1)}, u32[]{:S(2)}, u32[]{:S(2)}) async-start(s32[4,1,32]{2,1,0:T(1,128)} %bitcast.17), calls=%async_computation | async-start | bytes 4096 | tf_op jit(solution)/shard_map/all_to_all | solution.py:58
  64.1 10.7 %all-to-all-start.1 = ((s32[4,1,32]{2,1,0:T(1,128)}), s32[4,1,32]{2,1,0:T(1,128)S(1)}, u32[]{:S(2)}, u32[]{:S(2)}) async-start(s32[4,1,32]{2,1,0:T(1,128)} %bitcast.20), calls=%async_computation.1 | async-start | bytes 4096 | tf_op jit(solution)/shard_map/all_to_all | solution.py:59
  165.4 3.2 %copy-start.5 = (bf16[2560,768]{0,1:T(8,128)(2,1)S(1)}, bf16[2560,768]{0,1:T(8,128)(2,1)}, u32[]{:S(2)}) copy-start(bf16[2560,768]{0,1:T(8,128)(2,1)} %all-reduce.2.cloned.1.call-done) | copy-start | bytes 11796484
  165.4 3.7 %copy-start.7 = (bf16[1,320,2560]{2,1,0:T(8,128)(2,1)S(1)}, bf16[1,320,2560]{2,1,0:T(8,128)(2,1)}, u32[]{:S(2)}) copy-start(bf16[1,320,2560]{2,1,0:T(8,128)(2,1)} %param.10) | copy-start | bytes 4915204
  185.5 11.3 %copy-start.1 = (f32[12,320]{1,0:T(8,128)}, f32[12,320]{1,0:T(8,128)S(1)}, u32[]{:S(2)}) copy-start(f32[12,320]{1,0:T(8,128)S(1)} %psum.15) | copy-start | bytes 46084
Sparse Core Ops, SparseCore 0:
  16.1 149.2 all-reduce.1
where the time goes:
time: 205 us; the launch traced here: 204 us
  waiting for transfers between devices  96.1 us (47%)
  local copies, waits for them, and re-layouts  48.8 us (24%)
  blocking collectives  19.4 us (9%)
  between operations  14.1 us (7%)
  starting transfers between devices  11.4 us (6%)
  matrix products  9.88 us (5%)
  other arithmetic  3.93 us (2%)
    psum x1, waiting for transfers between devices, per_device(): gathered_rows = lax.psum(partial_value.astype(jnp.bfloat16), 'dp')  90.5 us
    scatter x1, local copies, waits for them, and re-layouts, per_device(): jnp.zeros((n_data, capacity), jnp.int32).at[target, slot].set(pair_query)  19.7 us
    scatter x1, local copies, waits for them, and re-layouts, per_device(): jnp.zeros((n_data, capacity), jnp.int32).at[target, slot].set(pair_doc)  19.6 us
    psum x1, blocking collectives, per_device(): token_scores = lax.psum(layer_scores, 'layer')  11.4 us
    all_to_all x1, blocking collectives, per_device(): lax.all_to_all(eigen_values, 'dp', split_axis=0, concat_axis=0, tiled=True)  8.01 us
    all_to_all x1, starting transfers between devices, per_device(): lax.all_to_all(send_query, 'dp', split_axis=0, concat_axis=0, tiled=True)  6.32 us
    all_to_all x1, waiting for transfers between devices, per_device(): lax.all_to_all(send_doc, 'dp', split_axis=0, concat_axis=0, tiled=True)  5.62 us
    all_to_all x1, starting transfers between devices, per_device(): lax.all_to_all(send_doc, 'dp', split_axis=0, concat_axis=0, tiled=True)  5.09 us
  transfers between devices with their start and end apart: 3, of which 2 were waited for; matrix products, arithmetic and copies ran while one was open for 20% of the time, Pallas kernels for 0%

commit v1 on v0

v1 whole, which is shorter than its diff:
```python
import functools

import jax
import jax.numpy as jnp
from jax import lax
from jax.experimental import pallas as pl
from jax.experimental.pallas import tpu as pltpu
from jax.sharding import PartitionSpec as P

RANK = 32
NT = (((1,), (1,)), ((), ()))


def pull_kernel(side_ref, basis_in_ref, basis_out_ref, query_in_ref, query_out_ref, out_ref):
    def go(basis_ref, query_ref):
        out_ref[...] = lax.dot_general(
            query_ref[...], basis_ref[...], (((0,), (1,)), ((), ())), preferred_element_type=jnp.float32
        ).astype(out_ref.dtype)

    @pl.when(side_ref[0] == 0)
    def _():
        go(basis_in_ref, query_in_ref)

    @pl.when(side_ref[0] != 0)
    def _():
        go(basis_out_ref, query_out_ref)


def pull(side, basis_in, basis_out, query_in, query_out):
    rows, depth = basis_in.shape
    spread = query_in.shape[1]
    block = 512 if rows % 512 == 0 else rows
    return pl.pallas_call(
        pull_kernel,
        out_shape=jax.ShapeDtypeStruct((spread, rows), jnp.bfloat16),
        grid_spec=pltpu.PrefetchScalarGridSpec(
            num_scalar_prefetch=1,
            grid=(rows // block,),
            in_specs=[
                pl.BlockSpec((block, depth), lambda i, s: (jnp.where(s[0] == 0, i, 0), 0)),
                pl.BlockSpec((block, depth), lambda i, s: (jnp.where(s[0] == 0, 0, i), 0)),
                pl.BlockSpec((depth, spread), lambda i, s: (0, 0)),
                pl.BlockSpec((depth, spread), lambda i, s: (0, 0)),
            ],
            out_specs=pl.BlockSpec((spread, block), lambda i, s: (0, i)),
        ),
        compiler_params=pltpu.CompilerParams(vmem_limit_bytes=24 * 1024 * 1024),
    )(side, basis_in, basis_out, query_in, query_out)


def score_kernel(side_ref, own_ref, other_ref, acts_ref, grads_ref, out_ref):
    def go(factor_in_ref, factor_out_ref):
        proj_in = lax.dot_general(factor_in_ref[...], acts_ref[...], NT, preferred_element_type=jnp.float32)
        proj_out = lax.dot_general(factor_out_ref[...], grads_ref[...], NT, preferred_element_type=jnp.float32)
        product = proj_in * proj_out
        queries = product.shape[0] // RANK
        out_ref[...] = jnp.sum(product.reshape(queries, RANK, product.shape[1]), axis=1) * RANK ** (-0.5)

    @pl.when(side_ref[0] == 0)
    def _():
        go(own_ref, other_ref)

    @pl.when(side_ref[0] != 0)
    def _():
        go(other_ref, own_ref)


def score(side, own, other, acts, grads):
    vmem = pl.BlockSpec(memory_space=pltpu.VMEM)
    return pl.pallas_call(
        score_kernel,
        out_shape=jax.ShapeDtypeStruct((own.shape[0] // RANK, acts.shape[0]), jnp.float32),
        in_specs=[pl.BlockSpec(memory_space=pltpu.SMEM), vmem, vmem, vmem, vmem],
        out_specs=vmem,
        compiler_params=pltpu.CompilerParams(vmem_limit_bytes=24 * 1024 * 1024),
    )(side, own, other, acts, grads)


def choose(at, options):
    picked = options[-1]
    for i in range(len(options) - 2, -1, -1):
        picked = jnp.where(at == i, options[i], picked)
    return picked


def sum_over_layers(value, layers):
    if layers & (layers - 1):
        return lax.psum(value, "layer")
    terms = [value] + [
        lax.ppermute(value, "layer", [(i, i ^ k) for i in range(layers)]) for k in range(1, layers)
    ]
    while len(terms) > 1:
        terms = [terms[i] + terms[i + 1] for i in range(0, len(terms), 2)]
    return terms[0]


def per_device(
    acts,
    grads,
    basis_in,
    output_eigen_basis,
    query_in,
    query_out,
    doc_counts,
    pair_query,
    pair_device,
    pair_doc,
):
    n = lax.axis_size("dp")
    layers = lax.axis_size("layer")
    side = lax.axis_index("parts")
    z = lax.axis_index("dp")
    side_array = side.astype(jnp.int32).reshape(1)
    tokens, features = acts.shape[1:]
    spread = query_in.shape[2]
    queries = spread // RANK
    chunks = queries
    width = spread // chunks

    own = pull(side_array, basis_in[0], output_eigen_basis[0], query_in[0], query_out[0])
    own = own.reshape(chunks, width, features)

    def own_chunk(c):
        return lax.dynamic_index_in_dim(own, jnp.clip(c, 0, chunks - 1), 0, keepdims=False)

    def add(a, b):
        return (a.astype(jnp.float32) + b.astype(jnp.float32)).astype(jnp.bfloat16)

    from_left, from_right, totals, swapped = [], [], [], []
    swap = [(0, 1), (1, 0)]
    group_ends = [4, 8, 11, 12] if chunks == 12 else [chunks]
    pieces, done = [], 0
    for step in range(chunks + n - 2):
        send_right, send_left = own_chunk(step - z), own_chunk(step - (n - 1 - z))
        if step:
            send_right, send_left = add(send_right, from_left[-1]), add(send_left, from_right[-1])
        from_left.append(
            lax.ppermute(send_right, "dp", [(i, i + 1) for i in range(n - 1) if 0 <= step - i < chunks])
        )
        from_right.append(
            lax.ppermute(send_left, "dp", [(n - 1 - i, n - 2 - i) for i in range(n - 1) if 0 <= step - i < chunks])
        )
        c = step - (n - 2)
        if c >= 0:
            zero = jnp.zeros((width, features), jnp.bfloat16)
            before = choose(z, [zero] + from_left[c : c + n - 1])
            after = choose(n - 1 - z, [zero] + from_right[c : c + n - 1])
            total = (
                own[c].astype(jnp.float32) + before.astype(jnp.float32) + after.astype(jnp.float32)
            ).astype(jnp.bfloat16)
            totals.append(total)
            swapped.append(lax.ppermute(total, "parts", swap))
            if c + 1 in group_ends:
                mine = jnp.concatenate(totals[done : c + 1], axis=0)
                theirs = jnp.concatenate(swapped[done : c + 1], axis=0)
                pieces.append(score(side_array, mine, theirs, acts[0], grads[0]))
                done = c + 1

    token_scores = sum_over_layers(jnp.concatenate(pieces, axis=0), layers)

    counts = doc_counts[0]
    ends = jnp.cumsum(counts)
    starts = ends - counts
    position = jnp.arange(tokens, dtype=jnp.int32)
    group_member = (
        (position[None, :] >= starts[:, None]) & (position[None, :] < ends[:, None])
    ).astype(jnp.float32)
    pooled = jnp.dot(token_scores, group_member.T, precision=lax.Precision.HIGHEST)
    pooled = pooled / jnp.sqrt(counts.astype(jnp.float32))[None, :]
    docs = counts.shape[0]
    cells = queries * docs
    flat = pooled.reshape(1, cells)
    target = pair_device[:, 0]
    cell = pair_query * docs + pair_doc
    if n <= 8:
        table = jnp.concatenate(
            [flat]
            + [lax.ppermute(flat, "dp", [(i, (i + k) % n) for i in range(n)]) for k in range(1, n)],
            axis=1,
        )
        column = lax.rem(z - target + n, n) * cells + cell
    else:
        table = lax.all_gather(flat, "dp", axis=1, tiled=True)
        column = target * cells + cell
    hit = column[:, None] == jnp.arange(n * cells, dtype=jnp.int32)[None, :]
    pair_scores = jnp.sum(jnp.where(hit, table, 0.0), axis=1)
    return (token_scores, pair_scores)


def solution(mesh):
    in_specs = (
        P("layer", ("parts", "dp"), None),
        P("layer", ("parts", "dp"), None),
        P("layer", None, "dp"),
        P("layer", None, "dp"),
        P("layer", "dp", None),
        P("layer", "dp", None),
        P(("parts", "dp"), None),
        P(("parts", "dp")),
        P(("parts", "dp"), None),
        P(("parts", "dp")),
    )
    out_specs = (P(None, ("parts", "dp")), P(("parts", "dp")))
    return jax.shard_map(
        per_device, mesh=mesh, in_specs=in_specs, out_specs=out_specs, check_vma=False
    )
```

time: 205 us -> 175 us (0.85)
  starting transfers between devices: 11.4 us -> 76.4 us
  local copies, waits for them, and re-layouts: 48.8 us -> 6.74 us
  waiting for transfers between devices: 96.1 us -> 75.6 us
  blocking collectives: 19.4 us -> 0 us
  between operations: 14.1 us -> 1.32 us
  matrix products: 9.88 us -> 0.19 us
  Pallas kernels: 0 us -> 7.36 us
  other arithmetic: 3.93 us -> 6.92 us
    psum x1 -> x0, waiting for transfers between devices: 90.5 us -> none  [per_device(): gathered_rows = lax.psum(partial_value.astype(jnp.bfloat16), 'dp')]
    ppermute x0 -> x46, starting transfers between devices: none -> 76.4 us  [the longest x14 37.6 us: per_device(): lax.ppermute(send_right, 'dp', [(i, i + 1) for i in range(n - 1) if 0 <=...]
    ppermute x0 -> x46, waiting for transfers between devices: none -> 75.6 us  [the longest x14 49 us: per_device(): lax.ppermute(send_left, 'dp', [(n - 1 - i, n - 2 - i) for i in range(n -...]
    scatter x2 -> x0, local copies, waits for them, and re-layouts: 39.3 us -> none  [the longest x1 19.7 us: per_device(): jnp.zeros((n_data, capacity), jnp.int32).at[target, slot].set(pair_query)]
    all_to_all x2 -> x0, starting transfers between devices: 11.4 us -> none  [the longest x1 6.32 us: per_device(): lax.all_to_all(send_query, 'dp', split_axis=0, concat_axis=0, tiled=True)]
    psum x1 -> x0, blocking collectives: 11.4 us -> none  [per_device(): token_scores = lax.psum(layer_scores, 'layer')]
    dot_general x4 -> x0, matrix products: 9.69 us -> none  [the longest x1 3.19 us: per_device(): jnp.dot(right, gathered_rows[:, spread:], preferred_element_type=jnp.floa...]
    all_to_all x1 -> x0, blocking collectives: 8.01 us -> none  [per_device(): lax.all_to_all(eigen_values, 'dp', split_axis=0, concat_axis=0, tiled=True)]
  transfers between devices with their start and end apart: 3 -> 46, of which waited for: 2 -> 29; matrix products, arithmetic and copies ran while one was open for 20% -> 2% of each run, Pallas kernels for 0% -> 2%
where the time goes in v1:
time: 175 us; the launch traced here: 174 us
  starting transfers between devices  76.4 us (44%)
  waiting for transfers between devices  75.6 us (43%)
  Pallas kernels  7.36 us (4%)
  other arithmetic  6.92 us (4%)
  local copies, waits for them, and re-layouts  6.74 us (4%)
    ppermute x14, waiting for transfers between devices, per_device(): lax.ppermute(send_left, 'dp', [(n - 1 - i, n - 2 - i) for i in range(n -...  49 us
    ppermute x14, starting transfers between devices, per_device(): lax.ppermute(send_right, 'dp', [(i, i + 1) for i in range(n - 1) if 0 <=...  37.6 us
    ppermute x14, starting transfers between devices, per_device(): lax.ppermute(send_left, 'dp', [(n - 1 - i, n - 2 - i) for i in range(n -...  16.8 us
    ppermute x12, starting transfers between devices, per_device(): swapped.append(lax.ppermute(total, 'parts', swap))  16.1 us
    ppermute x14, waiting for transfers between devices, per_device(): lax.ppermute(send_right, 'dp', [(i, i + 1) for i in range(n - 1) if 0 <=...  16 us
    unnamed x26, local copies, waits for them, and re-layouts  6.53 us
    ppermute x12, waiting for transfers between devices, per_device(): swapped.append(lax.ppermute(total, 'parts', swap))  5.44 us
    pallas_call x4, Pallas kernels, score(): pl.pallas_call(score_kernel, out_shape=jax.ShapeDtypeStruct((own.shape[0]...  4.57 us
  transfers between devices with their start and end apart: 46, of which 29 were waited for; matrix products, arithmetic and copies ran while one was open for 2% of the time, Pallas kernels for 2%

profile of v1, /device:TPU:0, one launch (start us, length us, event | category | flops | bytes accessed | tf_op | source)
XLA Modules:
  0.0 174.5 jit_solution(12636058472574413433)
XLA Ops:
  2.6 1.9 %copy-done.3 = bf16[1,2560,640]{2,1,0:T(8,128)(2,1)S(1)} copy-done((bf16[1,2560,640]{2,1,0:T(8,128)(2,1)S(1)}, bf16[1,2560,640]{2,1,0:T(8,128)(2,1)}, u32[]{:S(2)}) %copy-start.3) | copy-done | bytes 3276824
  6.6 2.8 %shard_map.113 = bf16[384,2560]{1,0:T(8,128)(2,1)S(1)} custom-call(s32[1]{0:T(128)} %bitcast.side_ref, bf16[2560,640]{1,0:T(8,128)(2,1)S(1)} %bitcast.122, bf16[2560,640]{1,0:T(8,128)(2,1)S(1)} %bitcast.123, bf16[640,384]{1,0:T(8,128)(2,1)S(1)} %bitcast.124, bf16[640,384]{1,0:T(8,128)(2,1)S(1)} %bitcast.125), custom_call_target="tpu_custom_call" | custom-call | tf_op jit(solution)/shard_map/pallas_call | solution.py:33
  9.4 4.9 %collective-permute-start = (bf16[32,2560]{1,0:T(8,128)(2,1)S(1)}, bf16[32,2560]{1,0:T(8,128)(2,1)S(1)}, u32[]{:S(2)}, u32[]{:S(2)}) collective-permute-start(bf16[32,2560]{1,0:T(8,128)(2,1)S(1)} %get-tuple-element.40), channel_id=1, source_target_pairs={{0,4},{1,5},{2,6},{3,7},{16,20},{17,21},{18,22},{19,23}} | collective-permute-start | bytes 491528 | tf_op jit(solution)/shard_map/ppermute | solution.py:138
  15.0 2.8 %collective-permute-done = bf16[32,2560]{1,0:T(8,128)(2,1)S(1)} collective-permute-done((bf16[32,2560]{1,0:T(8,128)(2,1)S(1)}, bf16[32,2560]{1,0:T(8,128)(2,1)S(1)}, u32[]{:S(2)}, u32[]{:S(2)}) %collective-permute-start) | collective-permute-done | bytes 163872 | tf_op jit(solution)/shard_map/ppermute | solution.py:138
  17.9 4.4 %collective-permute-start.1 = (bf16[32,2560]{1,0:T(8,128)(2,1)S(1)}, bf16[32,2560]{1,0:T(8,128)(2,1)S(1)}, u32[]{:S(2)}, u32[]{:S(2)}) collective-permute-start(bf16[32,2560]{1,0:T(8,128)(2,1)S(1)} %get-tuple-element.38), channel_id=1, source_target_pairs={{0,4},{4,8},{1,5},{5,9},{2,6},{6,10},{3,7},{7,11},{16,20},{20,24},... | collective-permute-start | bytes 491528 | tf_op jit(solution)/shard_map/ppermute | solution.py:138
  23.0 2.1 %collective-permute-done.1 = bf16[32,2560]{1,0:T(8,128)(2,1)S(1)} collective-permute-done((bf16[32,2560]{1,0:T(8,128)(2,1)S(1)}, bf16[32,2560]{1,0:T(8,128)(2,1)S(1)}, u32[]{:S(2)}, u32[]{:S(2)}) %collective-permute-start.1) | collective-permute-done | bytes 163872 | tf_op jit(solution)/shard_map/ppermute | solution.py:138
  25.2 8.6 %collective-permute-start.2 = (bf16[32,2560]{1,0:T(8,128)(2,1)S(1)}, bf16[32,2560]{1,0:T(8,128)(2,1)S(1)}, u32[]{:S(2)}, u32[]{:S(2)}) collective-permute-start(bf16[32,2560]{1,0:T(8,128)(2,1)S(1)} %get-tuple-element.36), channel_id=1, source_target_pairs={{0,4},{4,8},{8,12},{1,5},{5,9},{9,13},{2,6},{6,10},{10,14},{3,7},{... | collective-permute-start | bytes 491528 | tf_op jit(solution)/shard_map/ppermute | solution.py:138
  36.5 4.4 %collective-permute-done.5 = bf16[32,2560]{1,0:T(8,128)(2,1)S(1)} collective-permute-done((bf16[32,2560]{1,0:T(8,128)(2,1)S(1)}, bf16[32,2560]{1,0:T(8,128)(2,1)S(1)}, u32[]{:S(2)}, u32[]{:S(2)}) %collective-permute-start.5) | collective-permute-done | bytes 163872 | tf_op jit(solution)/shard_map/ppermute | solution.py:141
  46.3 4.4 %collective-permute-done.7 = bf16[32,2560]{1,0:T(8,128)(2,1)S(1)} collective-permute-done((bf16[32,2560]{1,0:T(8,128)(2,1)S(1)}, bf16[32,2560]{1,0:T(8,128)(2,1)S(1)}, u32[]{:S(2)}, u32[]{:S(2)}) %collective-permute-start.7) | collective-permute-done | bytes 163872 | tf_op jit(solution)/shard_map/ppermute | solution.py:141
  56.6 4.3 %collective-permute-done.9 = bf16[32,2560]{1,0:T(8,128)(2,1)S(1)} collective-permute-done((bf16[32,2560]{1,0:T(8,128)(2,1)}, bf16[32,2560]{1,0:T(8,128)(2,1)S(1)}, u32[]{:S(2)}, u32[]{:S(2)}) %collective-permute-start.9) | collective-permute-done | bytes 163872 | tf_op jit(solution)/shard_map/ppermute | solution.py:141
  61.7 2.6 %collective-permute-start.10 = (bf16[32,2560]{1,0:T(8,128)(2,1)}, bf16[32,2560]{1,0:T(8,128)(2,1)}, u32[]{:S(2)}, u32[]{:S(2)}) collective-permute-start(bf16[32,2560]{1,0:T(8,128)(2,1)} %get-tuple-element.30), channel_id=1, source_target_pairs={{0,4},{4,8},{8,12},{1,5},{5,9},{9,13},{2,6},{6,10},{10,14},{3,7},{... | collective-permute-start | bytes 491528 | tf_op jit(solution)/shard_map/ppermute | solution.py:138
  66.7 5.0 %collective-permute-done.11 = bf16[32,2560]{1,0:T(8,128)(2,1)} collective-permute-done((bf16[32,2560]{1,0:T(8,128)(2,1)}, bf16[32,2560]{1,0:T(8,128)(2,1)}, u32[]{:S(2)}, u32[]{:S(2)}) %collective-permute-start.11) | collective-permute-done | bytes 163872 | tf_op jit(solution)/shard_map/ppermute | solution.py:141
  75.6 3.0 %collective-permute-done.16 = bf16[32,2560]{1,0:T(8,128)(2,1)S(1)} collective-permute-done((bf16[32,2560]{1,0:T(8,128)(2,1)S(1)}, bf16[32,2560]{1,0:T(8,128)(2,1)S(1)}, u32[]{:S(2)}, u32[]{:S(2)}) %collective-permute-start.16) | collective-permute-done | bytes 163872 | tf_op jit(solution)/shard_map/ppermute | solution.py:138
  78.6 4.6 %collective-permute-done.17 = bf16[32,2560]{1,0:T(8,128)(2,1)S(1)} collective-permute-done((bf16[32,2560]{1,0:T(8,128)(2,1)S(1)}, bf16[32,2560]{1,0:T(8,128)(2,1)S(1)}, u32[]{:S(2)}, u32[]{:S(2)}) %collective-permute-start.17) | collective-permute-done | bytes 163872 | tf_op jit(solution)/shard_map/ppermute | solution.py:141
  90.2 2.6 %collective-permute-done.19 = bf16[32,2560]{1,0:T(8,128)(2,1)S(1)} collective-permute-done((bf16[32,2560]{1,0:T(8,128)(2,1)S(1)}, bf16[32,2560]{1,0:T(8,128)(2,1)S(1)}, u32[]{:S(2)}, u32[]{:S(2)}) %collective-permute-start.19) | collective-permute-done | bytes 163872 | tf_op jit(solution)/shard_map/ppermute | solution.py:141
  93.0 2.2 %collective-permute-start.20 = (bf16[32,2560]{1,0:T(8,128)(2,1)S(1)}, bf16[32,2560]{1,0:T(8,128)(2,1)S(1)}, u32[]{:S(2)}, u32[]{:S(2)}) collective-permute-start(bf16[32,2560]{1,0:T(8,128)(2,1)S(1)} %get-tuple-element.24), channel_id=1, source_target_pairs={{0,4},{4,8},{8,12},{1,5},{5,9},{9,13},{2,6},{6,10},{10,14},{3,7},{... | collective-permute-start | bytes 491528 | tf_op jit(solution)/shard_map/ppermute | solution.py:138
  98.0 4.3 %collective-permute-done.21 = bf16[32,2560]{1,0:T(8,128)(2,1)S(1)} collective-permute-done((bf16[32,2560]{1,0:T(8,128)(2,1)S(1)}, bf16[32,2560]{1,0:T(8,128)(2,1)S(1)}, u32[]{:S(2)}, u32[]{:S(2)}) %collective-permute-start.21) | collective-permute-done | bytes 163872 | tf_op jit(solution)/shard_map/ppermute | solution.py:141
  102.5 2.0 %collective-permute-start.22 = (bf16[32,2560]{1,0:T(8,128)(2,1)S(1)}, bf16[32,2560]{1,0:T(8,128)(2,1)S(1)}, u32[]{:S(2)}, u32[]{:S(2)}) collective-permute-start(bf16[32,2560]{1,0:T(8,128)(2,1)S(1)} %get-tuple-element.22), channel_id=1, source_target_pairs={{0,4},{4,8},{8,12},{1,5},{5,9},{9,13},{2,6},{6,10},{10,14},{3,7},{... | collective-permute-start | bytes 491528 | tf_op jit(solution)/shard_map/ppermute | solution.py:138
  105.8 1.9 %collective-permute-done.22 = bf16[32,2560]{1,0:T(8,128)(2,1)S(1)} collective-permute-done((bf16[32,2560]{1,0:T(8,128)(2,1)S(1)}, bf16[32,2560]{1,0:T(8,128)(2,1)S(1)}, u32[]{:S(2)}, u32[]{:S(2)}) %collective-permute-start.22) | collective-permute-done | bytes 163872 | tf_op jit(solution)/shard_map/ppermute | solution.py:138
  109.3 2.6 %collective-permute-done.23 = bf16[32,2560]{1,0:T(8,128)(2,1)S(1)} collective-permute-done((bf16[32,2560]{1,0:T(8,128)(2,1)S(1)}, bf16[32,2560]{1,0:T(8,128)(2,1)S(1)}, u32[]{:S(2)}, u32[]{:S(2)}) %collective-permute-start.23) | collective-permute-done | bytes 163872 | tf_op jit(solution)/shard_map/ppermute | solution.py:141
  114.1 2.4 %collective-permute-start.28 = (bf16[32,2560]{1,0:T(8,128)(2,1)S(1)}, bf16[32,2560]{1,0:T(8,128)(2,1)S(1)}, u32[]{:S(2)}, u32[]{:S(2)}) collective-permute-start(bf16[32,2560]{1,0:T(8,128)(2,1)S(1)} %get-tuple-element.20), channel_id=1, source_target_pairs={{0,4},{4,8},{8,12},{1,5},{5,9},{9,13},{2,6},{6,10},{10,14},{3,7},{... | collective-permute-start | bytes 491528 | tf_op jit(solution)/shard_map/ppermute | solution.py:138
  119.3 4.4 %collective-permute-done.29 = bf16[32,2560]{1,0:T(8,128)(2,1)S(1)} collective-permute-done((bf16[32,2560]{1,0:T(8,128)(2,1)S(1)}, bf16[32,2560]{1,0:T(8,128)(2,1)S(1)}, u32[]{:S(2)}, u32[]{:S(2)}) %collective-permute-start.29) | collective-permute-done | bytes 163872 | tf_op jit(solution)/shard_map/ppermute | solution.py:141
  123.8 2.2 %collective-permute-start.30 = (bf16[32,2560]{1,0:T(8,128)(2,1)S(1)}, bf16[32,2560]{1,0:T(8,128)(2,1)S(1)}, u32[]{:S(2)}, u32[]{:S(2)}) collective-permute-start(bf16[32,2560]{1,0:T(8,128)(2,1)S(1)} %get-tuple-element.18), channel_id=1, source_target_pairs={{0,4},{4,8},{8,12},{1,5},{5,9},{9,13},{2,6},{6,10},{10,14},{3,7},{... | collective-permute-start | bytes 491528 | tf_op jit(solution)/shard_map/ppermute | solution.py:138
  129.2 4.4 %collective-permute-done.31 = bf16[32,2560]{1,0:T(8,128)(2,1)S(1)} collective-permute-done((bf16[32,2560]{1,0:T(8,128)(2,1)S(1)}, bf16[32,2560]{1,0:T(8,128)(2,1)S(1)}, u32[]{:S(2)}, u32[]{:S(2)}) %collective-permute-start.31) | collective-permute-done | bytes 163872 | tf_op jit(solution)/shard_map/ppermute | solution.py:141
  135.8 2.6 %collective-permute-start.27 = (bf16[32,2560]{1,0:T(8,128)(2,1)S(1)}, bf16[32,2560]{1,0:T(8,128)(2,1)S(1)}, u32[]{:S(2)}, u32[]{:S(2)}) collective-permute-start(bf16[32,2560]{1,0:T(8,128)(2,1)S(1)} %get-tuple-element.9), channel_id=1, source_target_pairs={{0,16},{16,0},{1,17},{17,1},{2,18},{18,2},{3,19},{19,3},{4,20},{20... | collective-permute-start | bytes 491528 | tf_op jit(solution)/shard_map/ppermute | solution.py:152
  138.4 3.2 %collective-permute-done.33 = bf16[32,2560]{1,0:T(8,128)(2,1)S(1)} collective-permute-done((bf16[32,2560]{1,0:T(8,128)(2,1)S(1)}, bf16[32,2560]{1,0:T(8,128)(2,1)S(1)}, u32[]{:S(2)}, u32[]{:S(2)}) %collective-permute-start.33) | collective-permute-done | bytes 163872 | tf_op jit(solution)/shard_map/ppermute | solution.py:141
  141.6 2.5 %collective-permute-start.34 = (bf16[32,2560]{1,0:T(8,128)(2,1)S(1)}, bf16[32,2560]{1,0:T(8,128)(2,1)S(1)}, u32[]{:S(2)}, u32[]{:S(2)}) collective-permute-start(bf16[32,2560]{1,0:T(8,128)(2,1)S(1)} %get-tuple-element.10), channel_id=1, source_target_pairs={{0,16},{16,0},{1,17},{17,1},{2,18},{18,2},{3,19},{19,3},{4,20},{20... | collective-permute-start | bytes 491528 | tf_op jit(solution)/shard_map/ppermute | solution.py:152
  147.6 4.6 %collective-permute-done.38 = bf16[32,2560]{1,0:T(8,128)(2,1)S(1)} collective-permute-done((bf16[32,2560]{1,0:T(8,128)(2,1)S(1)}, bf16[32,2560]{1,0:T(8,128)(2,1)S(1)}, u32[]{:S(2)}, u32[]{:S(2)}) %collective-permute-start.38) | collective-permute-done | bytes 163872 | tf_op jit(solution)/shard_map/ppermute | solution.py:141
  152.5 2.0 %collective-permute-start.36 = (bf16[32,2560]{1,0:T(8,128)(2,1)S(1)}, bf16[32,2560]{1,0:T(8,128)(2,1)S(1)}, u32[]{:S(2)}, u32[]{:S(2)}) collective-permute-start(bf16[32,2560]{1,0:T(8,128)(2,1)S(1)} %get-tuple-element.12), channel_id=1, source_target_pairs={{0,16},{16,0},{1,17},{17,1},{2,18},{18,2},{3,19},{19,3},{4,20},{20... | collective-permute-start | bytes 491528 | tf_op jit(solution)/shard_map/ppermute | solution.py:152
  154.7 3.1 %collective-permute-done.35 = bf16[32,2560]{1,0:T(8,128)(2,1)S(1)} collective-permute-done((bf16[32,2560]{1,0:T(8,128)(2,1)S(1)}, bf16[32,2560]{1,0:T(8,128)(2,1)S(1)}, u32[]{:S(2)}, u32[]{:S(2)}) %collective-permute-start.35) | collective-permute-done | bytes 163872 | tf_op jit(solution)/shard_map/ppermute | solution.py:152
  164.3 2.0 %collective-permute-done.41 = f32[12,320]{1,0:T(8,128)S(1)} collective-permute-done((f32[12,320]{1,0:T(8,128)S(1)}, f32[12,320]{1,0:T(8,128)S(1)}, u32[]{:S(2)}, u32[]{:S(2)}) %collective-permute-start.41) | collective-permute-done | bytes 15392 | tf_op jit(solution)/shard_map/ppermute | solution.py:90
  167.9 3.7 %collective-permute-start.45 = (f32[1,96]{1,0:T(1,128)S(1)}, f32[1,96]{1,0:T(1,128)S(1)}, u32[]{:S(2)}, u32[]{:S(2)}) collective-permute-start(f32[1,96]{1,0:T(1,128)S(1)} %reshape.126), channel_id=1, source_target_pairs={{0,12},{4,0},{8,4},{12,8},{1,13},{5,1},{9,5},{13,9},{2,14},{6,2},{... | collective-permute-start | bytes 1160 | tf_op jit(solution)/shard_map/ppermute | solution.py:178
  (126 shorter events, 64.3 us)
Async XLA Ops:
  9.4 8.4 %collective-permute-start = (bf16[32,2560]{1,0:T(8,128)(2,1)S(1)}, bf16[32,2560]{1,0:T(8,128)(2,1)S(1)}, u32[]{:S(2)}, u32[]{:S(2)}) collective-permute-start(bf16[32,2560]{1,0:T(8,128)(2,1)S(1)} %get-tuple-element.40), channel_id=1, source_target_pairs={{0,4},{1,5},{2,6},{3,7},{16,20},{17,21},{18,22},{19,23}} | collective-permute-start | bytes 491528 | tf_op jit(solution)/shard_map/ppermute | solution.py:138
  17.9 7.2 %collective-permute-start.1 = (bf16[32,2560]{1,0:T(8,128)(2,1)S(1)}, bf16[32,2560]{1,0:T(8,128)(2,1)S(1)}, u32[]{:S(2)}, u32[]{:S(2)}) collective-permute-start(bf16[32,2560]{1,0:T(8,128)(2,1)S(1)} %get-tuple-element.38), channel_id=1, source_target_pairs={{0,4},{4,8},{1,5},{5,9},{2,6},{6,10},{3,7},{7,11},{16,20},{20,24},... | collective-permute-start | bytes 491528 | tf_op jit(solution)/shard_map/ppermute | solution.py:138
  25.2 11.4 %collective-permute-start.2 = (bf16[32,2560]{1,0:T(8,128)(2,1)S(1)}, bf16[32,2560]{1,0:T(8,128)(2,1)S(1)}, u32[]{:S(2)}, u32[]{:S(2)}) collective-permute-start(bf16[32,2560]{1,0:T(8,128)(2,1)S(1)} %get-tuple-element.36), channel_id=1, source_target_pairs={{0,4},{4,8},{8,12},{1,5},{5,9},{9,13},{2,6},{6,10},{10,14},{3,7},{... | collective-permute-start | bytes 491528 | tf_op jit(solution)/shard_map/ppermute | solution.py:138
  33.7 7.2 %collective-permute-start.5 = (bf16[32,2560]{1,0:T(8,128)(2,1)S(1)}, bf16[32,2560]{1,0:T(8,128)(2,1)S(1)}, u32[]{:S(2)}, u32[]{:S(2)}) collective-permute-start(bf16[32,2560]{1,0:T(8,128)(2,1)S(1)} %get-tuple-element.37), channel_id=1, source_target_pairs={{12,8},{8,4},{4,0},{13,9},{9,5},{5,1},{14,10},{10,6},{6,2},{15,11}... | collective-permute-start | bytes 491528 | tf_op jit(solution)/shard_map/ppermute | solution.py:141
  43.5 7.2 %collective-permute-start.7 = (bf16[32,2560]{1,0:T(8,128)(2,1)S(1)}, bf16[32,2560]{1,0:T(8,128)(2,1)S(1)}, u32[]{:S(2)}, u32[]{:S(2)}) collective-permute-start(bf16[32,2560]{1,0:T(8,128)(2,1)S(1)} %get-tuple-element.35), channel_id=1, source_target_pairs={{12,8},{8,4},{4,0},{13,9},{9,5},{5,1},{14,10},{10,6},{6,2},{15,11}... | collective-permute-start | bytes 491528 | tf_op jit(solution)/shard_map/ppermute | solution.py:141
  53.5 7.4 %collective-permute-start.9 = (bf16[32,2560]{1,0:T(8,128)(2,1)}, bf16[32,2560]{1,0:T(8,128)(2,1)S(1)}, u32[]{:S(2)}, u32[]{:S(2)}) collective-permute-start(bf16[32,2560]{1,0:T(8,128)(2,1)} %get-tuple-element.33), channel_id=1, source_target_pairs={{12,8},{8,4},{4,0},{13,9},{9,5},{5,1},{14,10},{10,6},{6,2},{15,11}... | collective-permute-start | bytes 491528 | tf_op jit(solution)/shard_map/ppermute | solution.py:141
  64.2 7.5 %collective-permute-start.11 = (bf16[32,2560]{1,0:T(8,128)(2,1)}, bf16[32,2560]{1,0:T(8,128)(2,1)}, u32[]{:S(2)}, u32[]{:S(2)}) collective-permute-start(bf16[32,2560]{1,0:T(8,128)(2,1)} %get-tuple-element.31), channel_id=1, source_target_pairs={{12,8},{8,4},{4,0},{13,9},{9,5},{5,1},{14,10},{10,6},{6,2},{15,11}... | collective-permute-start | bytes 491528 | tf_op jit(solution)/shard_map/ppermute | solution.py:141
  72.8 5.8 %collective-permute-start.16 = (bf16[32,2560]{1,0:T(8,128)(2,1)S(1)}, bf16[32,2560]{1,0:T(8,128)(2,1)S(1)}, u32[]{:S(2)}, u32[]{:S(2)}) collective-permute-start(bf16[32,2560]{1,0:T(8,128)(2,1)S(1)} %get-tuple-element.28), channel_id=1, source_target_pairs={{0,4},{4,8},{8,12},{1,5},{5,9},{9,13},{2,6},{6,10},{10,14},{3,7},{... | collective-permute-start | bytes 491528 | tf_op jit(solution)/shard_map/ppermute | solution.py:138
  74.3 8.9 %collective-permute-start.17 = (bf16[32,2560]{1,0:T(8,128)(2,1)S(1)}, bf16[32,2560]{1,0:T(8,128)(2,1)S(1)}, u32[]{:S(2)}, u32[]{:S(2)}) collective-permute-start(bf16[32,2560]{1,0:T(8,128)(2,1)S(1)} %get-tuple-element.29), channel_id=1, source_target_pairs={{12,8},{8,4},{4,0},{13,9},{9,5},{5,1},{14,10},{10,6},{6,2},{15,11}... | collective-permute-start | bytes 491528 | tf_op jit(solution)/shard_map/ppermute | solution.py:141
  83.3 6.9 %collective-permute-start.18 = (bf16[32,2560]{1,0:T(8,128)(2,1)S(1)}, bf16[32,2560]{1,0:T(8,128)(2,1)S(1)}, u32[]{:S(2)}, u32[]{:S(2)}) collective-permute-start(bf16[32,2560]{1,0:T(8,128)(2,1)S(1)} %get-tuple-element.26), channel_id=1, source_target_pairs={{0,4},{4,8},{8,12},{1,5},{5,9},{9,13},{2,6},{6,10},{10,14},{3,7},{... | collective-permute-start | bytes 491528 | tf_op jit(solution)/shard_map/ppermute | solution.py:138
  85.0 7.8 %collective-permute-start.19 = (bf16[32,2560]{1,0:T(8,128)(2,1)S(1)}, bf16[32,2560]{1,0:T(8,128)(2,1)S(1)}, u32[]{:S(2)}, u32[]{:S(2)}) collective-permute-start(bf16[32,2560]{1,0:T(8,128)(2,1)S(1)} %get-tuple-element.27), channel_id=1, source_target_pairs={{12,8},{8,4},{4,0},{13,9},{9,5},{5,1},{14,10},{10,6},{6,2},{15,11}... | collective-permute-start | bytes 491528 | tf_op jit(solution)/shard_map/ppermute | solution.py:141
  86.6 26.9 %collective-permute-start.12 = (bf16[32,2560]{1,0:T(8,128)(2,1)S(1)}, bf16[32,2560]{1,0:T(8,128)(2,1)S(1)}, u32[]{:S(2)}, u32[]{:S(2)}) collective-permute-start(bf16[32,2560]{1,0:T(8,128)(2,1)S(1)} %get-tuple-element.2), channel_id=1, source_target_pairs={{0,16},{16,0},{1,17},{17,1},{2,18},{18,2},{3,19},{19,3},{4,20},{20... | collective-permute-start | bytes 491528 | tf_op jit(solution)/shard_map/ppermute | solution.py:152
  88.2 25.9 %collective-permute-start.13 = (bf16[32,2560]{1,0:T(8,128)(2,1)S(1)}, bf16[32,2560]{1,0:T(8,128)(2,1)S(1)}, u32[]{:S(2)}, u32[]{:S(2)}) collective-permute-start(bf16[32,2560]{1,0:T(8,128)(2,1)S(1)} %get-tuple-element.3), channel_id=1, source_target_pairs={{0,16},{16,0},{1,17},{17,1},{2,18},{18,2},{3,19},{19,3},{4,20},{20... | collective-permute-start | bytes 491528 | tf_op jit(solution)/shard_map/ppermute | solution.py:152
  88.7 27.8 %collective-permute-start.14 = (bf16[32,2560]{1,0:T(8,128)(2,1)S(1)}, bf16[32,2560]{1,0:T(8,128)(2,1)S(1)}, u32[]{:S(2)}, u32[]{:S(2)}) collective-permute-start(bf16[32,2560]{1,0:T(8,128)(2,1)S(1)} %get-tuple-element.4), channel_id=1, source_target_pairs={{0,16},{16,0},{1,17},{17,1},{2,18},{18,2},{3,19},{19,3},{4,20},{20... | collective-permute-start | bytes 491528 | tf_op jit(solution)/shard_map/ppermute | solution.py:152
  95.2 7.2 %collective-permute-start.21 = (bf16[32,2560]{1,0:T(8,128)(2,1)S(1)}, bf16[32,2560]{1,0:T(8,128)(2,1)S(1)}, u32[]{:S(2)}, u32[]{:S(2)}) collective-permute-start(bf16[32,2560]{1,0:T(8,128)(2,1)S(1)} %get-tuple-element.25), channel_id=1, source_target_pairs={{12,8},{8,4},{4,0},{13,9},{9,5},{5,1},{14,10},{10,6},{6,2},{15,11}... | collective-permute-start | bytes 491528 | tf_op jit(solution)/shard_map/ppermute | solution.py:141
  104.4 7.5 %collective-permute-start.23 = (bf16[32,2560]{1,0:T(8,128)(2,1)S(1)}, bf16[32,2560]{1,0:T(8,128)(2,1)S(1)}, u32[]{:S(2)}, u32[]{:S(2)}) collective-permute-start(bf16[32,2560]{1,0:T(8,128)(2,1)S(1)} %get-tuple-element.23), channel_id=1, source_target_pairs={{12,8},{8,4},{4,0},{13,9},{9,5},{5,1},{14,10},{10,6},{6,2},{15,11}... | collective-permute-start | bytes 491528 | tf_op jit(solution)/shard_map/ppermute | solution.py:141
  107.8 10.1 %collective-permute-start.15 = (bf16[32,2560]{1,0:T(8,128)(2,1)S(1)}, bf16[32,2560]{1,0:T(8,128)(2,1)S(1)}, u32[]{:S(2)}, u32[]{:S(2)}) collective-permute-start(bf16[32,2560]{1,0:T(8,128)(2,1)S(1)} %get-tuple-element.5), channel_id=1, source_target_pairs={{0,16},{16,0},{1,17},{17,1},{2,18},{18,2},{3,19},{19,3},{4,20},{20... | collective-permute-start | bytes 491528 | tf_op jit(solution)/shard_map/ppermute | solution.py:152
  111.9 32.3 %collective-permute-start.24 = (bf16[32,2560]{1,0:T(8,128)(2,1)S(1)}, bf16[32,2560]{1,0:T(8,128)(2,1)S(1)}, u32[]{:S(2)}, u32[]{:S(2)}) collective-permute-start(bf16[32,2560]{1,0:T(8,128)(2,1)S(1)} %get-tuple-element.6), channel_id=1, source_target_pairs={{0,16},{16,0},{1,17},{17,1},{2,18},{18,2},{3,19},{19,3},{4,20},{20... | collective-permute-start | bytes 491528 | tf_op jit(solution)/shard_map/ppermute | solution.py:152
  113.5 31.4 %collective-permute-start.25 = (bf16[32,2560]{1,0:T(8,128)(2,1)S(1)}, bf16[32,2560]{1,0:T(8,128)(2,1)S(1)}, u32[]{:S(2)}, u32[]{:S(2)}) collective-permute-start(bf16[32,2560]{1,0:T(8,128)(2,1)S(1)} %get-tuple-element.7), channel_id=1, source_target_pairs={{0,16},{16,0},{1,17},{17,1},{2,18},{18,2},{3,19},{19,3},{4,20},{20... | collective-permute-start | bytes 491528 | tf_op jit(solution)/shard_map/ppermute | solution.py:152
  116.5 7.2 %collective-permute-start.29 = (bf16[32,2560]{1,0:T(8,128)(2,1)S(1)}, bf16[32,2560]{1,0:T(8,128)(2,1)S(1)}, u32[]{:S(2)}, u32[]{:S(2)}) collective-permute-start(bf16[32,2560]{1,0:T(8,128)(2,1)S(1)} %get-tuple-element.21), channel_id=1, source_target_pairs={{12,8},{8,4},{4,0},{13,9},{9,5},{5,1},{14,10},{10,6},{6,2},{15,11}... | collective-permute-start | bytes 491528 | tf_op jit(solution)/shard_map/ppermute | solution.py:141
  123.8 5.4 %collective-permute-start.30 = (bf16[32,2560]{1,0:T(8,128)(2,1)S(1)}, bf16[32,2560]{1,0:T(8,128)(2,1)S(1)}, u32[]{:S(2)}, u32[]{:S(2)}) collective-permute-start(bf16[32,2560]{1,0:T(8,128)(2,1)S(1)} %get-tuple-element.18), channel_id=1, source_target_pairs={{0,4},{4,8},{8,12},{1,5},{5,9},{9,13},{2,6},{6,10},{10,14},{3,7},{... | collective-permute-start | bytes 491528 | tf_op jit(solution)/shard_map/ppermute | solution.py:138
  126.0 7.6 %collective-permute-start.31 = (bf16[32,2560]{1,0:T(8,128)(2,1)S(1)}, bf16[32,2560]{1,0:T(8,128)(2,1)S(1)}, u32[]{:S(2)}, u32[]{:S(2)}) collective-permute-start(bf16[32,2560]{1,0:T(8,128)(2,1)S(1)} %get-tuple-element.19), channel_id=1, source_target_pairs={{12,8},{8,4},{4,0},{13,9},{9,5},{5,1},{14,10},{10,6},{6,2},{15,11}... | collective-permute-start | bytes 491528 | tf_op jit(solution)/shard_map/ppermute | solution.py:141
  127.6 18.6 %collective-permute-start.26 = (bf16[32,2560]{1,0:T(8,128)(2,1)S(1)}, bf16[32,2560]{1,0:T(8,128)(2,1)S(1)}, u32[]{:S(2)}, u32[]{:S(2)}) collective-permute-start(bf16[32,2560]{1,0:T(8,128)(2,1)S(1)} %get-tuple-element.8), channel_id=1, source_target_pairs={{0,16},{16,0},{1,17},{17,1},{2,18},{18,2},{3,19},{19,3},{4,20},{20... | collective-permute-start | bytes 491528 | tf_op jit(solution)/shard_map/ppermute | solution.py:152
  134.4 7.2 %collective-permute-start.33 = (bf16[32,2560]{1,0:T(8,128)(2,1)S(1)}, bf16[32,2560]{1,0:T(8,128)(2,1)S(1)}, u32[]{:S(2)}, u32[]{:S(2)}) collective-permute-start(bf16[32,2560]{1,0:T(8,128)(2,1)S(1)} %get-tuple-element.17), channel_id=1, source_target_pairs={{8,4},{4,0},{9,5},{5,1},{10,6},{6,2},{11,7},{7,3},{24,20},{20,16},... | collective-permute-start | bytes 491528 | tf_op jit(solution)/shard_map/ppermute | solution.py:141
  135.8 10.5 %collective-permute-start.27 = (bf16[32,2560]{1,0:T(8,128)(2,1)S(1)}, bf16[32,2560]{1,0:T(8,128)(2,1)S(1)}, u32[]{:S(2)}, u32[]{:S(2)}) collective-permute-start(bf16[32,2560]{1,0:T(8,128)(2,1)S(1)} %get-tuple-element.9), channel_id=1, source_target_pairs={{0,16},{16,0},{1,17},{17,1},{2,18},{18,2},{3,19},{19,3},{4,20},{20... | collective-permute-start | bytes 491528 | tf_op jit(solution)/shard_map/ppermute | solution.py:152
  141.6 13.1 %collective-permute-start.34 = (bf16[32,2560]{1,0:T(8,128)(2,1)S(1)}, bf16[32,2560]{1,0:T(8,128)(2,1)S(1)}, u32[]{:S(2)}, u32[]{:S(2)}) collective-permute-start(bf16[32,2560]{1,0:T(8,128)(2,1)S(1)} %get-tuple-element.10), channel_id=1, source_target_pairs={{0,16},{16,0},{1,17},{17,1},{2,18},{18,2},{3,19},{19,3},{4,20},{20... | collective-permute-start | bytes 491528 | tf_op jit(solution)/shard_map/ppermute | solution.py:152
  144.9 7.2 %collective-permute-start.38 = (bf16[32,2560]{1,0:T(8,128)(2,1)S(1)}, bf16[32,2560]{1,0:T(8,128)(2,1)S(1)}, u32[]{:S(2)}, u32[]{:S(2)}) collective-permute-start(bf16[32,2560]{1,0:T(8,128)(2,1)S(1)} %get-tuple-element.15), channel_id=1, source_target_pairs={{4,0},{5,1},{6,2},{7,3},{20,16},{21,17},{22,18},{23,19}} | collective-permute-start | bytes 491528 | tf_op jit(solution)/shard_map/ppermute | solution.py:141
  152.4 5.4 %collective-permute-start.35 = (bf16[32,2560]{1,0:T(8,128)(2,1)S(1)}, bf16[32,2560]{1,0:T(8,128)(2,1)S(1)}, u32[]{:S(2)}, u32[]{:S(2)}) collective-permute-start(bf16[32,2560]{1,0:T(8,128)(2,1)S(1)} %get-tuple-element.11), channel_id=1, source_target_pairs={{0,16},{16,0},{1,17},{17,1},{2,18},{18,2},{3,19},{19,3},{4,20},{20... | collective-permute-start | bytes 491528 | tf_op jit(solution)/shard_map/ppermute | solution.py:152
  152.5 7.1 %collective-permute-start.36 = (bf16[32,2560]{1,0:T(8,128)(2,1)S(1)}, bf16[32,2560]{1,0:T(8,128)(2,1)S(1)}, u32[]{:S(2)}, u32[]{:S(2)}) collective-permute-start(bf16[32,2560]{1,0:T(8,128)(2,1)S(1)} %get-tuple-element.12), channel_id=1, source_target_pairs={{0,16},{16,0},{1,17},{17,1},{2,18},{18,2},{3,19},{19,3},{4,20},{20... | collective-permute-start | bytes 491528 | tf_op jit(solution)/shard_map/ppermute | solution.py:152
  154.6 6.8 %collective-permute-start.39 = (bf16[32,2560]{1,0:T(8,128)(2,1)S(1)}, bf16[32,2560]{1,0:T(8,128)(2,1)S(1)}, u32[]{:S(2)}, u32[]{:S(2)}) collective-permute-start(bf16[32,2560]{1,0:T(8,128)(2,1)S(1)} %get-tuple-element.13.own_ref), channel_id=1, source_target_pairs={{0,16},{16,0},{1,17},{17,1},{2,18},{18,2},{3,19},{19,3},{4,20},{20... | collective-permute-start | bytes 491528 | tf_op jit(solution)/shard_map/ppermute | solution.py:152
  167.7 5.4 %collective-permute-start.43 = (f32[1,96]{1,0:T(1,128)S(1)}, f32[1,96]{1,0:T(1,128)S(1)}, u32[]{:S(2)}, u32[]{:S(2)}) collective-permute-start(f32[1,96]{1,0:T(1,128)S(1)} %reshape.126), channel_id=1, source_target_pairs={{0,4},{4,8},{8,12},{12,0},{1,5},{5,9},{9,13},{13,1},{2,6},{6,10},{... | collective-permute-start | bytes 1160 | tf_op jit(solution)/shard_map/ppermute | solution.py:178
  167.9 5.8 %collective-permute-start.45 = (f32[1,96]{1,0:T(1,128)S(1)}, f32[1,96]{1,0:T(1,128)S(1)}, u32[]{:S(2)}, u32[]{:S(2)}) collective-permute-start(f32[1,96]{1,0:T(1,128)S(1)} %reshape.126), channel_id=1, source_target_pairs={{0,12},{4,0},{8,4},{12,8},{1,13},{5,1},{9,5},{13,9},{2,14},{6,2},{... | collective-permute-start | bytes 1160 | tf_op jit(solution)/shard_map/ppermute | solution.py:178
  (27 other events, 178.2 us)

commit v2 on v1

v2 whole, which is shorter than its diff:
```python
import functools

import jax
import jax.numpy as jnp
from jax import lax
from jax.experimental import pallas as pl
from jax.experimental.pallas import tpu as pltpu
from jax.sharding import PartitionSpec as P

RANK = 32
PULL_VMEM = 123 * 512 * 1024
NT = (((1,), (1,)), ((), ()))


def pull_kernel(widths, side_ref, basis_in_ref, basis_out_ref, query_in_ref, query_out_ref, *rest):
    outs, (basis, query, turned, sems) = rest[: len(widths)], rest[len(widths) :]
    blocks, block = basis.shape[:2]

    def copies(basis_ref, query_ref):
        return [pltpu.make_async_copy(query_ref, query, sems.at[blocks])] + [
            pltpu.make_async_copy(basis_ref.at[pl.ds(i * block, block)], basis.at[i], sems.at[i])
            for i in range(blocks)
        ]

    @pl.when(side_ref[0] == 0)
    def _():
        for copy in copies(basis_in_ref, query_in_ref):
            copy.start()

    @pl.when(side_ref[0] != 0)
    def _():
        for copy in copies(basis_out_ref, query_out_ref):
            copy.start()

    landed = copies(basis_in_ref, query_in_ref)
    landed[0].wait()
    turned[...] = query[...].T
    for i in range(blocks):
        landed[1 + i].wait()
        pulled = lax.dot_general(turned[...], basis[i], NT, preferred_element_type=jnp.float32).astype(jnp.bfloat16)
        first = 0
        for out, width in zip(outs, widths):
            out[:, i * block : (i + 1) * block] = pulled[first : first + width]
            first += width


def pull(side, basis_in, basis_out, query_in, query_out, widths):
    rows, depth = basis_in.shape
    spread = query_in.shape[1]
    block = 512 if rows % 512 == 0 else rows
    blocks = rows // block
    hbm = pl.BlockSpec(memory_space=pltpu.HBM)
    return pl.pallas_call(
        functools.partial(pull_kernel, widths),
        out_shape=[jax.ShapeDtypeStruct((width, rows), jnp.bfloat16) for width in widths],
        in_specs=[pl.BlockSpec(memory_space=pltpu.SMEM)] + [hbm] * 4,
        out_specs=[pl.BlockSpec(memory_space=pltpu.VMEM)] * len(widths),
        scratch_shapes=[
            pltpu.VMEM((blocks, block, depth), jnp.bfloat16),
            pltpu.VMEM((depth, spread), jnp.bfloat16),
            pltpu.VMEM((spread, depth), jnp.bfloat16),
            pltpu.SemaphoreType.DMA((blocks + 1,)),
        ],
        compiler_params=pltpu.CompilerParams(vmem_limit_bytes=PULL_VMEM),
    )(side, basis_in, basis_out, query_in, query_out)


def total_kernel(mine_ref, came_ref, *rest):
    mine = mine_ref[...].astype(jnp.float32) + came_ref[...].astype(jnp.float32)
    rest[-1][...] = mine.astype(jnp.bfloat16)
    if len(rest) == 4:
        rest[2][...] = rest[1][...]


def total(after, mine, came, later=None):
    extra = [] if later is None else [later]
    vmem = pl.BlockSpec(memory_space=pltpu.VMEM)
    out = pl.pallas_call(
        total_kernel,
        out_shape=[jax.ShapeDtypeStruct(a.shape, a.dtype) for a in extra + [mine]],
        in_specs=[vmem] * 2 + [pl.BlockSpec(memory_space=pl.ANY)] + [vmem] * len(extra),
        out_specs=[vmem] * (1 + len(extra)),
        compiler_params=pltpu.CompilerParams(vmem_limit_bytes=8 * 1024 * 1024),
    )(mine, came, after, *extra)
    return out[-1], (out[0] if extra else None)


def take_kernel(flag_ref, mine_ref, came_ref, after_ref, out_ref):
    @pl.when(flag_ref[0] != 0)
    def _():
        out_ref[...] = came_ref[...]

    @pl.when(flag_ref[0] == 0)
    def _():
        out_ref[...] = mine_ref[...]


def take(after, flag, mine, came):
    vmem = pl.BlockSpec(memory_space=pltpu.VMEM)
    return pl.pallas_call(
        take_kernel,
        out_shape=jax.ShapeDtypeStruct(mine.shape, mine.dtype),
        in_specs=[pl.BlockSpec(memory_space=pltpu.SMEM), vmem, vmem, pl.BlockSpec(memory_space=pl.ANY)],
        out_specs=vmem,
        compiler_params=pltpu.CompilerParams(vmem_limit_bytes=8 * 1024 * 1024),
    )(flag, mine, came, after)


def score_kernel(side_ref, own_ref, other_ref, acts_ref, grads_ref, after_ref, out_ref):
    def go(factor_in_ref, factor_out_ref):
        proj_in = lax.dot_general(factor_in_ref[...], acts_ref[...], NT, preferred_element_type=jnp.float32)
        proj_out = lax.dot_general(factor_out_ref[...], grads_ref[...], NT, preferred_element_type=jnp.float32)
        product = proj_in * proj_out
        queries = product.shape[0] // RANK
        out_ref[...] = jnp.sum(product.reshape(queries, RANK, product.shape[1]), axis=1) * RANK ** (-0.5)

    @pl.when(side_ref[0] == 0)
    def _():
        go(own_ref, other_ref)

    @pl.when(side_ref[0] != 0)
    def _():
        go(other_ref, own_ref)


def score(after, side, own, other, acts, grads):
    vmem = pl.BlockSpec(memory_space=pltpu.VMEM)
    return pl.pallas_call(
        score_kernel,
        out_shape=jax.ShapeDtypeStruct((own.shape[0] // RANK, acts.shape[0]), jnp.float32),
        in_specs=[pl.BlockSpec(memory_space=pltpu.SMEM), vmem, vmem, vmem, vmem, pl.BlockSpec(memory_space=pl.ANY)],
        out_specs=vmem,
        compiler_params=pltpu.CompilerParams(vmem_limit_bytes=24 * 1024 * 1024),
    )(side, own, other, acts, grads, after)


def chunk_queries(queries):
    if queries < 4:
        return [1] * queries
    inner = queries - 2
    return [1] + [2] * (inner // 2) + [1] * (inner % 2) + [1]


def sum_over_layers(value, layers):
    if layers & (layers - 1):
        return lax.psum(value, "layer")
    terms = [value] + [
        lax.ppermute(value, "layer", [(i, i ^ k) for i in range(layers)]) for k in range(1, layers)
    ]
    while len(terms) > 1:
        terms = [terms[i] + terms[i + 1] for i in range(0, len(terms), 2)]
    return terms[0]


def per_device(
    acts,
    grads,
    basis_in,
    output_eigen_basis,
    query_in,
    query_out,
    doc_counts,
    pair_query,
    pair_device,
    pair_doc,
):
    n = lax.axis_size("dp")
    layers = lax.axis_size("layer")
    side = lax.axis_index("parts")
    z = lax.axis_index("dp")
    side_array = side.astype(jnp.int32).reshape(1)
    tokens, features = acts.shape[1:]
    spread = query_in.shape[2]
    queries = spread // RANK
    half = n // 2
    widths = [RANK * k for k in chunk_queries(queries)]
    chunks = len(widths)

    own = pull(side_array, basis_in[0], output_eigen_basis[0], query_in[0], query_out[0], widths)
    depth = jnp.minimum(z, n - 1 - z)
    at_hop = [(depth == hop).astype(jnp.int32).reshape(1) for hop in range(half - 1)]

    stages = [("in", hop) for hop in range(half - 1)] + [("mid", 0)]
    stages += [("out", hop) for hop in range(half - 2, -1, -1)] + [("swap", 0)]

    def transfer(kind, hop, value):
        if kind == "in":
            return lax.ppermute(value, "dp", [(hop, hop + 1), (n - 1 - hop, n - 2 - hop)])
        if kind == "mid":
            return lax.ppermute(value, "dp", [(half - 1, half), (half, half - 1)])
        if kind == "out":
            return lax.ppermute(value, "dp", [(hop + 1, hop), (n - 2 - hop, n - 1 - hop)])
        return lax.ppermute(value, "parts", [(0, 1), (1, 0)])

    part, came = list(own), [None] * chunks
    ahead = min(2, chunks)
    for c in range(ahead):
        came[c] = transfer(*stages[0], part[c])
    after = own[0]
    pieces = []
    for turn in range(chunks + len(stages) - 1):
        for s, (kind, hop) in enumerate(stages):
            c = turn - s
            if not 0 <= c < chunks:
                continue
            if kind == "swap":
                pieces.append(score(after, side_array, part[c], came[c], acts[0], grads[0]))
                after = pieces[-1]
                continue
            if kind == "out":
                part[c] = take(after, at_hop[hop], part[c], came[c])
            else:
                later = c + ahead if s == 0 and c + ahead < chunks else None
                part[c], moved = total(after, part[c], came[c], None if later is None else own[later])
                if later is not None:
                    came[later] = transfer(*stages[0], moved)
            after = part[c]
            came[c] = transfer(*stages[s + 1], part[c])

    token_scores = sum_over_layers(jnp.concatenate(pieces, axis=0), layers)

    counts = doc_counts[0]
    ends = jnp.cumsum(counts)
    starts = ends - counts
    position = jnp.arange(tokens, dtype=jnp.int32)
    group_member = (
        (position[None, :] >= starts[:, None]) & (position[None, :] < ends[:, None])
    ).astype(jnp.float32)
    pooled = jnp.dot(token_scores, group_member.T, precision=lax.Precision.HIGHEST)
    pooled = pooled / jnp.sqrt(counts.astype(jnp.float32))[None, :]
    docs = counts.shape[0]
    cells = queries * docs
    flat = pooled.reshape(1, cells)
    target = pair_device[:, 0]
    cell = pair_query * docs + pair_doc
    if n <= 8:
        table = jnp.concatenate(
            [flat]
            + [lax.ppermute(flat, "dp", [(i, (i + k) % n) for i in range(n)]) for k in range(1, n)],
            axis=1,
        )
        column = lax.rem(z - target + n, n) * cells + cell
    else:
        table = lax.all_gather(flat, "dp", axis=1, tiled=True)
        column = target * cells + cell
    hit = column[:, None] == jnp.arange(n * cells, dtype=jnp.int32)[None, :]
    pair_scores = jnp.sum(jnp.where(hit, table, 0.0), axis=1)
    return (token_scores, pair_scores)


def solution(mesh):
    in_specs = (
        P("layer", ("parts", "dp"), None),
        P("layer", ("parts", "dp"), None),
        P("layer", None, "dp"),
        P("layer", None, "dp"),
        P("layer", "dp", None),
        P("layer", "dp", None),
        P(("parts", "dp"), None),
        P(("parts", "dp")),
        P(("parts", "dp"), None),
        P(("parts", "dp")),
    )
    out_specs = (P(None, ("parts", "dp")), P(("parts", "dp")))
    return jax.shard_map(
        per_device, mesh=mesh, in_specs=in_specs, out_specs=out_specs, check_vma=False
    )
```

time: 175 us -> 130 us (0.74)
  waiting for transfers between devices: 75.6 us -> 22.8 us
  Pallas kernels: 7.36 us -> 25.1 us
  other arithmetic: 6.92 us -> 1 us
  starting transfers between devices: 76.4 us -> 70.8 us
    ppermute x40 -> x28, waiting for transfers between devices: 70.5 us -> 18.5 us  [the longest x7 9.76 us: transfer(): lax.ppermute(value, 'dp', [(hop, hop + 1), (n - 1 - hop, n - 2 - hop)])]
    pallas_call x1 -> x22, Pallas kernels: 2.8 us -> 15.8 us  [the longest x14 6.24 us: total(): pl.pallas_call(total_kernel, out_shape=[jax.ShapeDtypeStruct(a.shape, a.d...]
    ppermute x40 -> x28, starting transfers between devices: 70.6 us -> 63.8 us  [the longest x7 39.4 us: transfer(): lax.ppermute(value, 'dp', [(hop, hop + 1), (n - 1 - hop, n - 2 - hop)])]
    convert_element_type x17 -> x0, other arithmetic: 5.64 us -> none  [the longest x13 3.48 us: add(): return (a.astype(jnp.float32) + b.astype(jnp.float32)).astype(jnp.bfloat16)]
    pallas_call x4 -> x7, Pallas kernels: 4.57 us -> 9.31 us  [score(): pl.pallas_call(score_kernel, out_shape=jax.ShapeDtypeStruct((own.shape[0]...]
    unnamed x26 -> x36, local copies, waits for them, and re-layouts: 6.53 us -> 7.75 us
  transfers between devices with their start and end apart: 46 -> 34, of which waited for: 29 -> 14; matrix products, arithmetic and copies ran while one was open for 2% -> 0% of each run, Pallas kernels for 2% -> 15%
where the time goes in v2:
time: 130 us; the launch traced here: 129 us
  starting transfers between devices  70.8 us (54%)
  Pallas kernels  25.1 us (19%)
  waiting for transfers between devices  22.8 us (18%)
  local copies, waits for them, and re-layouts  8.07 us (6%)
    ppermute x7, starting transfers between devices, transfer(): lax.ppermute(value, 'dp', [(hop, hop + 1), (n - 1 - hop, n - 2 - hop)])  39.4 us
    ppermute x7, waiting for transfers between devices, transfer(): lax.ppermute(value, 'dp', [(hop, hop + 1), (n - 1 - hop, n - 2 - hop)])  9.76 us
    ppermute x7, starting transfers between devices, transfer(): return lax.ppermute(value, 'parts', [(0, 1), (1, 0)])  9.5 us
    pallas_call x7, Pallas kernels, score(): pl.pallas_call(score_kernel, out_shape=jax.ShapeDtypeStruct((own.shape[0]...  9.31 us
    ppermute x7, starting transfers between devices, transfer(): lax.ppermute(value, 'dp', [(hop + 1, hop), (n - 2 - hop, n - 1 - hop)])  9.03 us
    unnamed x36, local copies, waits for them, and re-layouts  7.75 us
    ppermute x7, waiting for transfers between devices, transfer(): return lax.ppermute(value, 'parts', [(0, 1), (1, 0)])  6.88 us
    pallas_call x14, Pallas kernels, total(): pl.pallas_call(total_kernel, out_shape=[jax.ShapeDtypeStruct(a.shape, a.d...  6.24 us
  transfers between devices with their start and end apart: 34, of which 14 were waited for; matrix products, arithmetic and copies ran while one was open for 0% of the time, Pallas kernels for 15%

profile of v2, /device:TPU:0, one launch (start us, length us, event | category | flops | bytes accessed | tf_op | source)
XLA Modules:
  0.0 129.1 jit_solution(138822827931079281)
XLA Ops:
  0.6 5.0 %shard_map.113 = (bf16[32,2560]{1,0:T(8,128)(2,1)}, bf16[64,2560]{1,0:T(8,128)(2,1)}, bf16[64,2560]{1,0:T(8,128)(2,1)}, bf16[64,2560]{1,0:T(8,128)(2,1)}, bf16[6...) custom-call(s32[1]{0:T(128)} %bitcast.side_ref, bf16[2560,640]{1,0:T(8,128)(2,1)} %bitcast.32, ...), custom_call_target="tpu_custom_call" | custom-call | tf_op jit(solution)/shard_map/pallas_call | solution.py:53
  5.7 4.9 %collective-permute-start.2 = (bf16[64,2560]{1,0:T(8,128)(2,1)}, bf16[64,2560]{1,0:T(8,128)(2,1)S(1)}, u32[]{:S(2)}, u32[]{:S(2)}) collective-permute-start(bf16[64,2560]{1,0:T(8,128)(2,1)} %get-tuple-element.22.mine_ref), channel_id=1, source_target_pairs={{0,4},{12,8},{1,5},{13,9},{2,6},{14,10},{3,7},{15,11},{16,20},{28,... | collective-permute-start | bytes 983048 | tf_op jit(solution)/shard_map/ppermute | solution.py:188
  10.6 1.3 %collective-permute-start = (bf16[32,2560]{1,0:T(8,128)(2,1)}, bf16[32,2560]{1,0:T(8,128)(2,1)S(1)}, u32[]{:S(2)}, u32[]{:S(2)}) collective-permute-start(bf16[32,2560]{1,0:T(8,128)(2,1)} %get-tuple-element.19.mine_ref.rest_0_), channel_id=1, source_target_pairs={{0,4},{12,8},{1,5},{13,9},{2,6},{14,10},{3,7},{15,11},{16,20},{28,... | collective-permute-start | bytes 491528 | tf_op jit(solution)/shard_map/ppermute | solution.py:188
  11.9 9.5 %collective-permute-done.came_ref = bf16[32,2560]{1,0:T(8,128)(2,1)S(1)} collective-permute-done((bf16[32,2560]{1,0:T(8,128)(2,1)}, bf16[32,2560]{1,0:T(8,128)(2,1)S(1)}, u32[]{:S(2)}, u32[]{:S(2)}) %collective-permute-start) | collective-permute-done | bytes 163872 | tf_op jit(solution)/shard_map/ppermute | solution.py:188
  23.3 4.3 %collective-permute-start.5 = (bf16[64,2560]{1,0:T(8,128)(2,1)S(1)}, bf16[64,2560]{1,0:T(8,128)(2,1)S(1)}, u32[]{:S(2)}, u32[]{:S(2)}) collective-permute-start(bf16[64,2560]{1,0:T(8,128)(2,1)S(1)} %get-tuple-element.25), channel_id=1, source_target_pairs={{0,4},{12,8},{1,5},{13,9},{2,6},{14,10},{3,7},{15,11},{16,20},{28,... | collective-permute-start | bytes 983048 | tf_op jit(solution)/shard_map/ppermute | solution.py:188
  31.7 6.5 %collective-permute-start.9 = (bf16[64,2560]{1,0:T(8,128)(2,1)}, bf16[64,2560]{1,0:T(8,128)(2,1)}, u32[]{:S(2)}, u32[]{:S(2)}) collective-permute-start(bf16[64,2560]{1,0:T(8,128)(2,1)} %get-tuple-element.28), channel_id=1, source_target_pairs={{0,4},{12,8},{1,5},{13,9},{2,6},{14,10},{3,7},{15,11},{16,20},{28,... | collective-permute-start | bytes 983048 | tf_op jit(solution)/shard_map/ppermute | solution.py:188
  38.3 1.3 %collective-permute-start.3 = (bf16[32,2560]{1,0:T(8,128)(2,1)S(1)}, bf16[32,2560]{1,0:T(8,128)(2,1)}, u32[]{:S(2)}, u32[]{:S(2)}) collective-permute-start(bf16[32,2560]{1,0:T(8,128)(2,1)S(1)} %shard_map.116.rest_0_.mine_ref), channel_id=1, source_target_pairs={{4,0},{8,12},{5,1},{9,13},{6,2},{10,14},{7,3},{11,15},{20,16},{24,... | collective-permute-start | bytes 491528 | tf_op jit(solution)/shard_map/ppermute | solution.py:192
  42.5 1.5 %collective-permute-start.8 = (bf16[64,2560]{1,0:T(8,128)(2,1)}, bf16[64,2560]{1,0:T(8,128)(2,1)}, u32[]{:S(2)}, u32[]{:S(2)}) collective-permute-start(bf16[64,2560]{1,0:T(8,128)(2,1)} %get-tuple-element.27.rest_0_.mine_ref), channel_id=1, source_target_pairs={{4,8},{8,4},{5,9},{9,5},{6,10},{10,6},{7,11},{11,7},{20,24},{24,20... | collective-permute-start | bytes 983048 | tf_op jit(solution)/shard_map/ppermute | solution.py:190
  44.8 1.3 collective-permute-start.7
  46.1 11.6 %collective-permute-start.13 = (bf16[64,2560]{1,0:T(8,128)(2,1)}, bf16[64,2560]{1,0:T(8,128)(2,1)}, u32[]{:S(2)}, u32[]{:S(2)}) collective-permute-start(bf16[64,2560]{1,0:T(8,128)(2,1)} %get-tuple-element.31), channel_id=1, source_target_pairs={{0,4},{12,8},{1,5},{13,9},{2,6},{14,10},{3,7},{15,11},{16,20},{28,... | collective-permute-start | bytes 983048 | tf_op jit(solution)/shard_map/ppermute | solution.py:188
  58.6 1.6 %collective-permute-start.6 = (bf16[32,2560]{1,0:T(8,128)(2,1)S(1)}, bf16[32,2560]{1,0:T(8,128)(2,1)S(1)}, u32[]{:S(2)}, u32[]{:S(2)}) collective-permute-start(bf16[32,2560]{1,0:T(8,128)(2,1)S(1)} %shard_map.119.rest_0_.own_ref), channel_id=1, source_target_pairs={{0,16},{16,0},{1,17},{17,1},{2,18},{18,2},{3,19},{19,3},{4,20},{20... | collective-permute-start | bytes 491528 | tf_op jit(solution)/shard_map/ppermute | solution.py:193
  64.0 1.2 shard_map.121.after_ref.mine_ref
  65.2 1.3 %collective-permute-start.11 = (bf16[64,2560]{1,0:T(8,128)(2,1)S(1)}, bf16[64,2560]{1,0:T(8,128)(2,1)S(1)}, u32[]{:S(2)}, u32[]{:S(2)}) collective-permute-start(bf16[64,2560]{1,0:T(8,128)(2,1)S(1)} %shard_map.121.after_ref.mine_ref), channel_id=1, source_target_pairs={{4,0},{8,12},{5,1},{9,13},{6,2},{10,14},{7,3},{11,15},{20,16},{24,... | collective-permute-start | bytes 983048 | tf_op jit(solution)/shard_map/ppermute | solution.py:192
  68.2 4.6 %collective-permute-start.17 = (bf16[64,2560]{1,0:T(8,128)(2,1)S(1)}, bf16[64,2560]{1,0:T(8,128)(2,1)S(1)}, u32[]{:S(2)}, u32[]{:S(2)}) collective-permute-start(bf16[64,2560]{1,0:T(8,128)(2,1)S(1)} %get-tuple-element.34), channel_id=1, source_target_pairs={{0,4},{12,8},{1,5},{13,9},{2,6},{14,10},{3,7},{15,11},{16,20},{28,... | collective-permute-start | bytes 983048 | tf_op jit(solution)/shard_map/ppermute | solution.py:188
  75.8 1.3 %collective-permute-start.15 = (bf16[64,2560]{1,0:T(8,128)(2,1)S(1)}, bf16[64,2560]{1,0:T(8,128)(2,1)S(1)}, u32[]{:S(2)}, u32[]{:S(2)}) collective-permute-start(bf16[64,2560]{1,0:T(8,128)(2,1)S(1)} %shard_map.125.after_ref.mine_ref), channel_id=1, source_target_pairs={{4,0},{8,12},{5,1},{9,13},{6,2},{10,14},{7,3},{11,15},{20,16},{24,... | collective-permute-start | bytes 983048 | tf_op jit(solution)/shard_map/ppermute | solution.py:192
  77.1 1.6 %collective-permute-start.14 = (bf16[64,2560]{1,0:T(8,128)(2,1)S(1)}, bf16[64,2560]{1,0:T(8,128)(2,1)S(1)}, u32[]{:S(2)}, u32[]{:S(2)}) collective-permute-start(bf16[64,2560]{1,0:T(8,128)(2,1)S(1)} %shard_map.126.after_ref.own_ref), channel_id=1, source_target_pairs={{0,16},{16,0},{1,17},{17,1},{2,18},{18,2},{3,19},{19,3},{4,20},{20... | collective-permute-start | bytes 983048 | tf_op jit(solution)/shard_map/ppermute | solution.py:193
  80.7 1.3 %collective-permute-start.19 = (bf16[64,2560]{1,0:T(8,128)(2,1)S(1)}, bf16[64,2560]{1,0:T(8,128)(2,1)S(1)}, u32[]{:S(2)}, u32[]{:S(2)}) collective-permute-start(bf16[64,2560]{1,0:T(8,128)(2,1)S(1)} %shard_map.129.after_ref.mine_ref), channel_id=1, source_target_pairs={{4,0},{8,12},{5,1},{9,13},{6,2},{10,14},{7,3},{11,15},{20,16},{24,... | collective-permute-start | bytes 983048 | tf_op jit(solution)/shard_map/ppermute | solution.py:192
  82.0 6.2 %collective-permute-start.21 = (bf16[32,2560]{1,0:T(8,128)(2,1)S(1)}, bf16[32,2560]{1,0:T(8,128)(2,1)S(1)}, u32[]{:S(2)}, u32[]{:S(2)}) collective-permute-start(bf16[32,2560]{1,0:T(8,128)(2,1)S(1)} %get-tuple-element.35), channel_id=1, source_target_pairs={{0,4},{12,8},{1,5},{13,9},{2,6},{14,10},{3,7},{15,11},{16,20},{28,... | collective-permute-start | bytes 491528 | tf_op jit(solution)/shard_map/ppermute | solution.py:188
  88.3 1.4 %collective-permute-start.18 = (bf16[64,2560]{1,0:T(8,128)(2,1)S(1)}, bf16[64,2560]{1,0:T(8,128)(2,1)S(1)}, u32[]{:S(2)}, u32[]{:S(2)}) collective-permute-start(bf16[64,2560]{1,0:T(8,128)(2,1)S(1)} %shard_map.130.after_ref.own_ref), channel_id=1, source_target_pairs={{0,16},{16,0},{1,17},{17,1},{2,18},{18,2},{3,19},{19,3},{4,20},{20... | collective-permute-start | bytes 983048 | tf_op jit(solution)/shard_map/ppermute | solution.py:193
  91.2 1.3 %collective-permute-start.23 = (bf16[64,2560]{1,0:T(8,128)(2,1)S(1)}, bf16[64,2560]{1,0:T(8,128)(2,1)S(1)}, u32[]{:S(2)}, u32[]{:S(2)}) collective-permute-start(bf16[64,2560]{1,0:T(8,128)(2,1)S(1)} %shard_map.133.after_ref.mine_ref), channel_id=1, source_target_pairs={{4,0},{8,12},{5,1},{9,13},{6,2},{10,14},{7,3},{11,15},{20,16},{24,... | collective-permute-start | bytes 983048 | tf_op jit(solution)/shard_map/ppermute | solution.py:192
  93.7 2.5 %collective-permute-start.22 = (bf16[64,2560]{1,0:T(8,128)(2,1)}, bf16[64,2560]{1,0:T(8,128)(2,1)}, u32[]{:S(2)}, u32[]{:S(2)}) collective-permute-start(bf16[64,2560]{1,0:T(8,128)(2,1)} %shard_map.134.after_ref.own_ref), channel_id=1, source_target_pairs={{0,16},{16,0},{1,17},{17,1},{2,18},{18,2},{3,19},{19,3},{4,20},{20... | collective-permute-start | bytes 983048 | tf_op jit(solution)/shard_map/ppermute | solution.py:193
  96.8 1.8 %collective-permute-done.18.other_ref = bf16[64,2560]{1,0:T(8,128)(2,1)S(1)} collective-permute-done((bf16[64,2560]{1,0:T(8,128)(2,1)S(1)}, bf16[64,2560]{1,0:T(8,128)(2,1)S(1)}, u32[]{:S(2)}, u32[]{:S(2)}) %collective-permute-start.18) | collective-permute-done | bytes 327712 | tf_op jit(solution)/shard_map/ppermute | solution.py:193
  99.8 1.3 %collective-permute-start.26 = (bf16[32,2560]{1,0:T(8,128)(2,1)S(1)}, bf16[32,2560]{1,0:T(8,128)(2,1)}, u32[]{:S(2)}, u32[]{:S(2)}) collective-permute-start(bf16[32,2560]{1,0:T(8,128)(2,1)S(1)} %shard_map.136.after_ref.mine_ref), channel_id=1, source_target_pairs={{4,0},{8,12},{5,1},{9,13},{6,2},{10,14},{7,3},{11,15},{20,16},{24,... | collective-permute-start | bytes 491528 | tf_op jit(solution)/shard_map/ppermute | solution.py:192
  103.2 2.6 %collective-permute-done.22.other_ref = bf16[64,2560]{1,0:T(8,128)(2,1)} collective-permute-done((bf16[64,2560]{1,0:T(8,128)(2,1)}, bf16[64,2560]{1,0:T(8,128)(2,1)}, u32[]{:S(2)}, u32[]{:S(2)}) %collective-permute-start.22) | collective-permute-done | bytes 327712 | tf_op jit(solution)/shard_map/ppermute | solution.py:193
  105.8 2.1 %shard_map.138.after_ref = f32[2,320]{1,0:T(2,128)S(1)} custom-call(s32[1]{0:T(128)} %bitcast.side_ref, bf16[64,2560]{1,0:T(8,128)(2,1)} %shard_map.134.after_ref.own_ref, bf16[64,2560]{1,0:T(8,128)(2,1)} %collective-permute-done.22.other_ref, bf16[320,2560]{1,0:T(8,128)(2,1)S(1)} %bitcast.22, bf16[320,2560]{1,0:T(8,128)(2,1)S(1)} %bitcast.29, ...), custom_call_target="tpu_custom_call" | custom-call | tf_op jit(solution)/shard_map/pallas_call | solution.py:128
  107.9 1.3 %collective-permute-done.26.came_ref = bf16[32,2560]{1,0:T(8,128)(2,1)} collective-permute-done((bf16[32,2560]{1,0:T(8,128)(2,1)S(1)}, bf16[32,2560]{1,0:T(8,128)(2,1)}, u32[]{:S(2)}, u32[]{:S(2)}) %collective-permute-start.26) | collective-permute-done | bytes 163872 | tf_op jit(solution)/shard_map/ppermute | solution.py:192
  111.3 2.1 %shard_map.140.after_ref = f32[2,320]{1,0:T(2,128)S(1)} custom-call(s32[1]{0:T(128)} %bitcast.side_ref, bf16[64,2560]{1,0:T(8,128)(2,1)} %shard_map.137.after_ref.own_ref, bf16[64,2560]{1,0:T(8,128)(2,1)} %collective-permute-done.25.other_ref, bf16[320,2560]{1,0:T(8,128)(2,1)S(1)} %bitcast.23, bf16[320,2560]{1,0:T(8,128)(2,1)S(1)} %bitcast.30, ...), custom_call_target="tpu_custom_call" | custom-call | tf_op jit(solution)/shard_map/pallas_call | solution.py:128
  113.4 2.1 %collective-permute-done.27.other_ref = bf16[32,2560]{1,0:T(8,128)(2,1)S(1)} collective-permute-done((bf16[32,2560]{1,0:T(8,128)(2,1)S(1)}, bf16[32,2560]{1,0:T(8,128)(2,1)S(1)}, u32[]{:S(2)}, u32[]{:S(2)}) %collective-permute-start.27) | collective-permute-done | bytes 163872 | tf_op jit(solution)/shard_map/ppermute | solution.py:193
  116.7 1.6 %collective-permute-start.29 = (f32[12,320]{1,0:T(8,128)S(1)}, f32[12,320]{1,0:T(8,128)S(1)}, u32[]{:S(2)}, u32[]{:S(2)}) collective-permute-start(f32[12,320]{1,0:T(8,128)S(1)} %concatenate.6), channel_id=1, source_target_pairs={{0,2},{1,3},{2,0},{3,1},{4,6},{5,7},{6,4},{7,5},{8,10},{9,11},{10,... | collective-permute-start | bytes 46088 | tf_op jit(solution)/shard_map/ppermute | solution.py:148
  118.6 2.0 %collective-permute-done.29 = f32[12,320]{1,0:T(8,128)S(1)} collective-permute-done((f32[12,320]{1,0:T(8,128)S(1)}, f32[12,320]{1,0:T(8,128)S(1)}, u32[]{:S(2)}, u32[]{:S(2)}) %collective-permute-start.29) | collective-permute-done | bytes 15392 | tf_op jit(solution)/shard_map/ppermute | solution.py:148
  121.9 1.3 %collective-permute-start.31 = (f32[1,96]{1,0:T(1,128)S(1)}, f32[1,96]{1,0:T(1,128)S(1)}, u32[]{:S(2)}, u32[]{:S(2)}) collective-permute-start(f32[1,96]{1,0:T(1,128)S(1)} %reshape.53), channel_id=1, source_target_pairs={{0,4},{4,8},{8,12},{12,0},{1,5},{5,9},{9,13},{13,1},{2,6},{6,10},{... | collective-permute-start | bytes 1160 | tf_op jit(solution)/shard_map/ppermute | solution.py:239
  124.2 2.8 %collective-permute-start.33 = (f32[1,96]{1,0:T(1,128)S(1)}, f32[1,96]{1,0:T(1,128)S(1)}, u32[]{:S(2)}, u32[]{:S(2)}) collective-permute-start(f32[1,96]{1,0:T(1,128)S(1)} %reshape.53), channel_id=1, source_target_pairs={{0,12},{4,0},{8,4},{12,8},{1,13},{5,1},{9,5},{13,9},{2,14},{6,2},{... | collective-permute-start | bytes 1160 | tf_op jit(solution)/shard_map/ppermute | solution.py:239
  (112 shorter events, 35.5 us)
Async XLA Ops:
  5.7 22.0 %collective-permute-start.2 = (bf16[64,2560]{1,0:T(8,128)(2,1)}, bf16[64,2560]{1,0:T(8,128)(2,1)S(1)}, u32[]{:S(2)}, u32[]{:S(2)}) collective-permute-start(bf16[64,2560]{1,0:T(8,128)(2,1)} %get-tuple-element.22.mine_ref), channel_id=1, source_target_pairs={{0,4},{12,8},{1,5},{13,9},{2,6},{14,10},{3,7},{15,11},{16,20},{28,... | collective-permute-start | bytes 983048 | tf_op jit(solution)/shard_map/ppermute | solution.py:188
  10.6 10.8 %collective-permute-start = (bf16[32,2560]{1,0:T(8,128)(2,1)}, bf16[32,2560]{1,0:T(8,128)(2,1)S(1)}, u32[]{:S(2)}, u32[]{:S(2)}) collective-permute-start(bf16[32,2560]{1,0:T(8,128)(2,1)} %get-tuple-element.19.mine_ref.rest_0_), channel_id=1, source_target_pairs={{0,4},{12,8},{1,5},{13,9},{2,6},{14,10},{3,7},{15,11},{16,20},{28,... | collective-permute-start | bytes 491528 | tf_op jit(solution)/shard_map/ppermute | solution.py:188
  23.3 16.3 %collective-permute-start.5 = (bf16[64,2560]{1,0:T(8,128)(2,1)S(1)}, bf16[64,2560]{1,0:T(8,128)(2,1)S(1)}, u32[]{:S(2)}, u32[]{:S(2)}) collective-permute-start(bf16[64,2560]{1,0:T(8,128)(2,1)S(1)} %get-tuple-element.25), channel_id=1, source_target_pairs={{0,4},{12,8},{1,5},{13,9},{2,6},{14,10},{3,7},{15,11},{16,20},{28,... | collective-permute-start | bytes 983048 | tf_op jit(solution)/shard_map/ppermute | solution.py:188
  30.4 13.6 %collective-permute-start.4 = (bf16[64,2560]{1,0:T(8,128)(2,1)S(1)}, bf16[64,2560]{1,0:T(8,128)(2,1)S(1)}, u32[]{:S(2)}, u32[]{:S(2)}) collective-permute-start(bf16[64,2560]{1,0:T(8,128)(2,1)S(1)} %get-tuple-element.24.rest_0_.mine_ref), channel_id=1, source_target_pairs={{4,8},{8,4},{5,9},{9,5},{6,10},{10,6},{7,11},{11,7},{20,24},{24,20... | collective-permute-start | bytes 983048 | tf_op jit(solution)/shard_map/ppermute | solution.py:190
  31.1 7.2 %collective-permute-start.1 = (bf16[32,2560]{1,0:T(8,128)(2,1)S(1)}, bf16[32,2560]{1,0:T(8,128)(2,1)S(1)}, u32[]{:S(2)}, u32[]{:S(2)}) collective-permute-start(bf16[32,2560]{1,0:T(8,128)(2,1)S(1)} %get-tuple-element.21.rest_0_.mine_ref), channel_id=1, source_target_pairs={{4,8},{8,4},{5,9},{9,5},{6,10},{10,6},{7,11},{11,7},{20,24},{24,20... | collective-permute-start | bytes 491528 | tf_op jit(solution)/shard_map/ppermute | solution.py:190
  31.7 28.5 %collective-permute-start.9 = (bf16[64,2560]{1,0:T(8,128)(2,1)}, bf16[64,2560]{1,0:T(8,128)(2,1)}, u32[]{:S(2)}, u32[]{:S(2)}) collective-permute-start(bf16[64,2560]{1,0:T(8,128)(2,1)} %get-tuple-element.28), channel_id=1, source_target_pairs={{0,4},{12,8},{1,5},{13,9},{2,6},{14,10},{3,7},{15,11},{16,20},{28,... | collective-permute-start | bytes 983048 | tf_op jit(solution)/shard_map/ppermute | solution.py:188
  38.3 19.3 %collective-permute-start.3 = (bf16[32,2560]{1,0:T(8,128)(2,1)S(1)}, bf16[32,2560]{1,0:T(8,128)(2,1)}, u32[]{:S(2)}, u32[]{:S(2)}) collective-permute-start(bf16[32,2560]{1,0:T(8,128)(2,1)S(1)} %shard_map.116.rest_0_.mine_ref), channel_id=1, source_target_pairs={{4,0},{8,12},{5,1},{9,13},{6,2},{10,14},{7,3},{11,15},{20,16},{24,... | collective-permute-start | bytes 491528 | tf_op jit(solution)/shard_map/ppermute | solution.py:192
  42.5 21.6 %collective-permute-start.8 = (bf16[64,2560]{1,0:T(8,128)(2,1)}, bf16[64,2560]{1,0:T(8,128)(2,1)}, u32[]{:S(2)}, u32[]{:S(2)}) collective-permute-start(bf16[64,2560]{1,0:T(8,128)(2,1)} %get-tuple-element.27.rest_0_.mine_ref), channel_id=1, source_target_pairs={{4,8},{8,4},{5,9},{9,5},{6,10},{10,6},{7,11},{11,7},{20,24},{24,20... | collective-permute-start | bytes 983048 | tf_op jit(solution)/shard_map/ppermute | solution.py:190
  44.8 21.7 %collective-permute-start.7 = (bf16[64,2560]{1,0:T(8,128)(2,1)}, bf16[64,2560]{1,0:T(8,128)(2,1)}, u32[]{:S(2)}, u32[]{:S(2)}) collective-permute-start(bf16[64,2560]{1,0:T(8,128)(2,1)} %shard_map.118.after_ref.mine_ref), channel_id=1, source_target_pairs={{4,0},{8,12},{5,1},{9,13},{6,2},{10,14},{7,3},{11,15},{20,16},{24,... | collective-permute-start | bytes 983048 | tf_op jit(solution)/shard_map/ppermute | solution.py:192
  46.1 27.7 %collective-permute-start.13 = (bf16[64,2560]{1,0:T(8,128)(2,1)}, bf16[64,2560]{1,0:T(8,128)(2,1)}, u32[]{:S(2)}, u32[]{:S(2)}) collective-permute-start(bf16[64,2560]{1,0:T(8,128)(2,1)} %get-tuple-element.31), channel_id=1, source_target_pairs={{0,4},{12,8},{1,5},{13,9},{2,6},{14,10},{3,7},{15,11},{16,20},{28,... | collective-permute-start | bytes 983048 | tf_op jit(solution)/shard_map/ppermute | solution.py:188
  58.6 9.6 %collective-permute-start.6 = (bf16[32,2560]{1,0:T(8,128)(2,1)S(1)}, bf16[32,2560]{1,0:T(8,128)(2,1)S(1)}, u32[]{:S(2)}, u32[]{:S(2)}) collective-permute-start(bf16[32,2560]{1,0:T(8,128)(2,1)S(1)} %shard_map.119.rest_0_.own_ref), channel_id=1, source_target_pairs={{0,16},{16,0},{1,17},{17,1},{2,18},{18,2},{3,19},{19,3},{4,20},{20... | collective-permute-start | bytes 491528 | tf_op jit(solution)/shard_map/ppermute | solution.py:193
  63.2 12.5 %collective-permute-start.12 = (bf16[64,2560]{1,0:T(8,128)(2,1)S(1)}, bf16[64,2560]{1,0:T(8,128)(2,1)S(1)}, u32[]{:S(2)}, u32[]{:S(2)}) collective-permute-start(bf16[64,2560]{1,0:T(8,128)(2,1)S(1)} %get-tuple-element.30.rest_0_.mine_ref), channel_id=1, source_target_pairs={{4,8},{8,4},{5,9},{9,5},{6,10},{10,6},{7,11},{11,7},{20,24},{24,20... | collective-permute-start | bytes 983048 | tf_op jit(solution)/shard_map/ppermute | solution.py:190
  65.2 11.9 %collective-permute-start.11 = (bf16[64,2560]{1,0:T(8,128)(2,1)S(1)}, bf16[64,2560]{1,0:T(8,128)(2,1)S(1)}, u32[]{:S(2)}, u32[]{:S(2)}) collective-permute-start(bf16[64,2560]{1,0:T(8,128)(2,1)S(1)} %shard_map.121.after_ref.mine_ref), channel_id=1, source_target_pairs={{4,0},{8,12},{5,1},{9,13},{6,2},{10,14},{7,3},{11,15},{20,16},{24,... | collective-permute-start | bytes 983048 | tf_op jit(solution)/shard_map/ppermute | solution.py:192
  67.6 11.1 %collective-permute-start.10 = (bf16[64,2560]{1,0:T(8,128)(2,1)S(1)}, bf16[64,2560]{1,0:T(8,128)(2,1)S(1)}, u32[]{:S(2)}, u32[]{:S(2)}) collective-permute-start(bf16[64,2560]{1,0:T(8,128)(2,1)S(1)} %shard_map.122.after_ref.own_ref), channel_id=1, source_target_pairs={{0,16},{16,0},{1,17},{17,1},{2,18},{18,2},{3,19},{19,3},{4,20},{20... | collective-permute-start | bytes 983048 | tf_op jit(solution)/shard_map/ppermute | solution.py:193
  68.2 11.6 %collective-permute-start.17 = (bf16[64,2560]{1,0:T(8,128)(2,1)S(1)}, bf16[64,2560]{1,0:T(8,128)(2,1)S(1)}, u32[]{:S(2)}, u32[]{:S(2)}) collective-permute-start(bf16[64,2560]{1,0:T(8,128)(2,1)S(1)} %get-tuple-element.34), channel_id=1, source_target_pairs={{0,4},{12,8},{1,5},{13,9},{2,6},{14,10},{3,7},{15,11},{16,20},{28,... | collective-permute-start | bytes 983048 | tf_op jit(solution)/shard_map/ppermute | solution.py:188
  74.9 5.7 %collective-permute-start.16 = (bf16[64,2560]{1,0:T(8,128)(2,1)S(1)}, bf16[64,2560]{1,0:T(8,128)(2,1)S(1)}, u32[]{:S(2)}, u32[]{:S(2)}) collective-permute-start(bf16[64,2560]{1,0:T(8,128)(2,1)S(1)} %get-tuple-element.33.rest_0_.mine_ref), channel_id=1, source_target_pairs={{4,8},{8,4},{5,9},{9,5},{6,10},{10,6},{7,11},{11,7},{20,24},{24,20... | collective-permute-start | bytes 983048 | tf_op jit(solution)/shard_map/ppermute | solution.py:190
  75.8 12.5 %collective-permute-start.15 = (bf16[64,2560]{1,0:T(8,128)(2,1)S(1)}, bf16[64,2560]{1,0:T(8,128)(2,1)S(1)}, u32[]{:S(2)}, u32[]{:S(2)}) collective-permute-start(bf16[64,2560]{1,0:T(8,128)(2,1)S(1)} %shard_map.125.after_ref.mine_ref), channel_id=1, source_target_pairs={{4,0},{8,12},{5,1},{9,13},{6,2},{10,14},{7,3},{11,15},{20,16},{24,... | collective-permute-start | bytes 983048 | tf_op jit(solution)/shard_map/ppermute | solution.py:192
  77.1 12.6 %collective-permute-start.14 = (bf16[64,2560]{1,0:T(8,128)(2,1)S(1)}, bf16[64,2560]{1,0:T(8,128)(2,1)S(1)}, u32[]{:S(2)}, u32[]{:S(2)}) collective-permute-start(bf16[64,2560]{1,0:T(8,128)(2,1)S(1)} %shard_map.126.after_ref.own_ref), channel_id=1, source_target_pairs={{0,16},{16,0},{1,17},{17,1},{2,18},{18,2},{3,19},{19,3},{4,20},{20... | collective-permute-start | bytes 983048 | tf_op jit(solution)/shard_map/ppermute | solution.py:193
  79.9 11.2 %collective-permute-start.20 = (bf16[64,2560]{1,0:T(8,128)(2,1)S(1)}, bf16[64,2560]{1,0:T(8,128)(2,1)S(1)}, u32[]{:S(2)}, u32[]{:S(2)}) collective-permute-start(bf16[64,2560]{1,0:T(8,128)(2,1)S(1)} %shard_map.128.rest_0_.mine_ref), channel_id=1, source_target_pairs={{4,8},{8,4},{5,9},{9,5},{6,10},{10,6},{7,11},{11,7},{20,24},{24,20... | collective-permute-start | bytes 983048 | tf_op jit(solution)/shard_map/ppermute | solution.py:190
  80.7 12.2 %collective-permute-start.19 = (bf16[64,2560]{1,0:T(8,128)(2,1)S(1)}, bf16[64,2560]{1,0:T(8,128)(2,1)S(1)}, u32[]{:S(2)}, u32[]{:S(2)}) collective-permute-start(bf16[64,2560]{1,0:T(8,128)(2,1)S(1)} %shard_map.129.after_ref.mine_ref), channel_id=1, source_target_pairs={{4,0},{8,12},{5,1},{9,13},{6,2},{10,14},{7,3},{11,15},{20,16},{24,... | collective-permute-start | bytes 983048 | tf_op jit(solution)/shard_map/ppermute | solution.py:192
  82.0 9.1 %collective-permute-start.21 = (bf16[32,2560]{1,0:T(8,128)(2,1)S(1)}, bf16[32,2560]{1,0:T(8,128)(2,1)S(1)}, u32[]{:S(2)}, u32[]{:S(2)}) collective-permute-start(bf16[32,2560]{1,0:T(8,128)(2,1)S(1)} %get-tuple-element.35), channel_id=1, source_target_pairs={{0,4},{12,8},{1,5},{13,9},{2,6},{14,10},{3,7},{15,11},{16,20},{28,... | collective-permute-start | bytes 491528 | tf_op jit(solution)/shard_map/ppermute | solution.py:188
  88.3 10.4 %collective-permute-start.18 = (bf16[64,2560]{1,0:T(8,128)(2,1)S(1)}, bf16[64,2560]{1,0:T(8,128)(2,1)S(1)}, u32[]{:S(2)}, u32[]{:S(2)}) collective-permute-start(bf16[64,2560]{1,0:T(8,128)(2,1)S(1)} %shard_map.130.after_ref.own_ref), channel_id=1, source_target_pairs={{0,16},{16,0},{1,17},{17,1},{2,18},{18,2},{3,19},{19,3},{4,20},{20... | collective-permute-start | bytes 983048 | tf_op jit(solution)/shard_map/ppermute | solution.py:193
  91.2 10.0 %collective-permute-start.23 = (bf16[64,2560]{1,0:T(8,128)(2,1)S(1)}, bf16[64,2560]{1,0:T(8,128)(2,1)S(1)}, u32[]{:S(2)}, u32[]{:S(2)}) collective-permute-start(bf16[64,2560]{1,0:T(8,128)(2,1)S(1)} %shard_map.133.after_ref.mine_ref), channel_id=1, source_target_pairs={{4,0},{8,12},{5,1},{9,13},{6,2},{10,14},{7,3},{11,15},{20,16},{24,... | collective-permute-start | bytes 983048 | tf_op jit(solution)/shard_map/ppermute | solution.py:192
  93.7 12.1 %collective-permute-start.22 = (bf16[64,2560]{1,0:T(8,128)(2,1)}, bf16[64,2560]{1,0:T(8,128)(2,1)}, u32[]{:S(2)}, u32[]{:S(2)}) collective-permute-start(bf16[64,2560]{1,0:T(8,128)(2,1)} %shard_map.134.after_ref.own_ref), channel_id=1, source_target_pairs={{0,16},{16,0},{1,17},{17,1},{2,18},{18,2},{3,19},{19,3},{4,20},{20... | collective-permute-start | bytes 983048 | tf_op jit(solution)/shard_map/ppermute | solution.py:193
  96.2 3.5 %collective-permute-start.24 = (bf16[32,2560]{1,0:T(8,128)(2,1)S(1)}, bf16[32,2560]{1,0:T(8,128)(2,1)S(1)}, u32[]{:S(2)}, u32[]{:S(2)}) collective-permute-start(bf16[32,2560]{1,0:T(8,128)(2,1)S(1)} %shard_map.132.rest_0_.mine_ref), channel_id=1, source_target_pairs={{4,8},{8,4},{5,9},{9,5},{6,10},{10,6},{7,11},{11,7},{20,24},{24,20... | collective-permute-start | bytes 491528 | tf_op jit(solution)/shard_map/ppermute | solution.py:190
  99.8 9.4 %collective-permute-start.26 = (bf16[32,2560]{1,0:T(8,128)(2,1)S(1)}, bf16[32,2560]{1,0:T(8,128)(2,1)}, u32[]{:S(2)}, u32[]{:S(2)}) collective-permute-start(bf16[32,2560]{1,0:T(8,128)(2,1)S(1)} %shard_map.136.after_ref.mine_ref), channel_id=1, source_target_pairs={{4,0},{8,12},{5,1},{9,13},{6,2},{10,14},{7,3},{11,15},{20,16},{24,... | collective-permute-start | bytes 491528 | tf_op jit(solution)/shard_map/ppermute | solution.py:192
  102.0 9.4 %collective-permute-start.25 = (bf16[64,2560]{1,0:T(8,128)(2,1)}, bf16[64,2560]{1,0:T(8,128)(2,1)}, u32[]{:S(2)}, u32[]{:S(2)}) collective-permute-start(bf16[64,2560]{1,0:T(8,128)(2,1)} %shard_map.137.after_ref.own_ref), channel_id=1, source_target_pairs={{0,16},{16,0},{1,17},{17,1},{2,18},{18,2},{3,19},{19,3},{4,20},{20... | collective-permute-start | bytes 983048 | tf_op jit(solution)/shard_map/ppermute | solution.py:193
  110.1 5.4 %collective-permute-start.27 = (bf16[32,2560]{1,0:T(8,128)(2,1)S(1)}, bf16[32,2560]{1,0:T(8,128)(2,1)S(1)}, u32[]{:S(2)}, u32[]{:S(2)}) collective-permute-start(bf16[32,2560]{1,0:T(8,128)(2,1)S(1)} %shard_map.139.after_ref.own_ref), channel_id=1, source_target_pairs={{0,16},{16,0},{1,17},{17,1},{2,18},{18,2},{3,19},{19,3},{4,20},{20... | collective-permute-start | bytes 491528 | tf_op jit(solution)/shard_map/ppermute | solution.py:193
  116.7 3.9 %collective-permute-start.29 = (f32[12,320]{1,0:T(8,128)S(1)}, f32[12,320]{1,0:T(8,128)S(1)}, u32[]{:S(2)}, u32[]{:S(2)}) collective-permute-start(f32[12,320]{1,0:T(8,128)S(1)} %concatenate.6), channel_id=1, source_target_pairs={{0,2},{1,3},{2,0},{3,1},{4,6},{5,7},{6,4},{7,5},{8,10},{9,11},{10,... | collective-permute-start | bytes 46088 | tf_op jit(solution)/shard_map/ppermute | solution.py:148
  121.9 5.4 %collective-permute-start.31 = (f32[1,96]{1,0:T(1,128)S(1)}, f32[1,96]{1,0:T(1,128)S(1)}, u32[]{:S(2)}, u32[]{:S(2)}) collective-permute-start(f32[1,96]{1,0:T(1,128)S(1)} %reshape.53), channel_id=1, source_target_pairs={{0,4},{4,8},{8,12},{12,0},{1,5},{5,9},{9,13},{13,1},{2,6},{6,10},{... | collective-permute-start | bytes 1160 | tf_op jit(solution)/shard_map/ppermute | solution.py:239
  123.2 4.4 %collective-permute-start.32 = (f32[1,96]{1,0:T(1,128)S(1)}, f32[1,96]{1,0:T(1,128)S(1)}, u32[]{:S(2)}, u32[]{:S(2)}) collective-permute-start(f32[1,96]{1,0:T(1,128)S(1)} %reshape.53), channel_id=1, source_target_pairs={{0,8},{4,12},{8,0},{12,4},{1,9},{5,13},{9,1},{13,5},{2,10},{6,14},... | collective-permute-start | bytes 1160 | tf_op jit(solution)/shard_map/ppermute | solution.py:239
  124.2 4.1 %collective-permute-start.33 = (f32[1,96]{1,0:T(1,128)S(1)}, f32[1,96]{1,0:T(1,128)S(1)}, u32[]{:S(2)}, u32[]{:S(2)}) collective-permute-start(f32[1,96]{1,0:T(1,128)S(1)} %reshape.53), channel_id=1, source_target_pairs={{0,12},{4,0},{8,4},{12,8},{1,13},{5,1},{9,5},{13,9},{2,14},{6,2},{... | collective-permute-start | bytes 1160 | tf_op jit(solution)/shard_map/ppermute | solution.py:239
  (20 other events, 166.7 us)

commit v3 on v2

--- a/solution.py
+++ b/solution.py
@@ -8,18 +8,16 @@
 from jax.sharding import PartitionSpec as P
 
 RANK = 32
-PULL_VMEM = 123 * 512 * 1024
 NT = (((1,), (1,)), ((), ()))
 
 
-def pull_kernel(widths, side_ref, basis_in_ref, basis_out_ref, query_in_ref, query_out_ref, *rest):
-    outs, (basis, query, turned, sems) = rest[: len(widths)], rest[len(widths) :]
-    blocks, block = basis.shape[:2]
-
-    def copies(basis_ref, query_ref):
-        return [pltpu.make_async_copy(query_ref, query, sems.at[blocks])] + [
-            pltpu.make_async_copy(basis_ref.at[pl.ds(i * block, block)], basis.at[i], sems.at[i])
-            for i in range(blocks)
+def first_pull_kernel(side_ref, basis_in_ref, basis_out_ref, query_in_ref, query_out_ref, out_ref, basis_ref, query_ref, turned_ref, sems):
+    rows = out_ref.shape[0]
+
+    def copies(from_basis, from_query):
+        return [
+            pltpu.make_async_copy(from_query, query_ref, sems.at[0]),
+            pltpu.make_async_copy(from_basis, basis_ref, sems.at[1]),
         ]
 
     @pl.when(side_ref[0] == 0)
@@ -34,35 +32,51 @@
 
     landed = copies(basis_in_ref, query_in_ref)
     landed[0].wait()
-    turned[...] = query[...].T
-    for i in range(blocks):
-        landed[1 + i].wait()
-        pulled = lax.dot_general(turned[...], basis[i], NT, preferred_element_type=jnp.float32).astype(jnp.bfloat16)
-        first = 0
-        for out, width in zip(outs, widths):
-            out[:, i * block : (i + 1) * block] = pulled[first : first + width]
-            first += width
-
-
-def pull(side, basis_in, basis_out, query_in, query_out, widths):
-    rows, depth = basis_in.shape
+    turned_ref[...] = query_ref[...].T
+    landed[1].wait()
+    out_ref[...] = lax.dot_general(
+        turned_ref[:rows], basis_ref[...], NT, preferred_element_type=jnp.float32
+    ).astype(jnp.bfloat16)
+
+
+def first_pull(side, basis_in, basis_out, query_in, query_out, rows):
+    features, depth = basis_in.shape
     spread = query_in.shape[1]
-    block = 512 if rows % 512 == 0 else rows
-    blocks = rows // block
-    hbm = pl.BlockSpec(memory_space=pltpu.HBM)
+    hbm = [pltpu.with_memory_space_constraint(a, pltpu.HBM) for a in (basis_in, basis_out, query_in, query_out)]
+    vmem = pl.BlockSpec(memory_space=pltpu.VMEM)
+    bf16 = functools.partial(jax.ShapeDtypeStruct, dtype=jnp.bfloat16)
+    out, basis, _, turned = pl.pallas_call(
+        first_pull_kernel,
+        out_shape=[bf16((rows, features)), bf16((features, depth)), bf16((depth, spread)), bf16((spread, depth))],
+        in_specs=[pl.BlockSpec(memory_space=pltpu.SMEM)] + [pl.BlockSpec(memory_space=pltpu.HBM)] * 4,
+        out_specs=[vmem] * 4,
+        scratch_shapes=[pltpu.SemaphoreType.DMA((2,))],
+        compiler_params=pltpu.CompilerParams(vmem_limit_bytes=16 * 1024 * 1024),
+    )(side, *hbm)
+    return out, basis, turned
+
+
+def pull_kernel(turned_ref, basis_ref, after_ref, *outs):
+    rows, features = outs[0].shape
+    block = 512 if features % 512 == 0 else features
+    for i in range(features // block):
+        pulled = lax.dot_general(
+            turned_ref[rows:], basis_ref[i * block : (i + 1) * block], NT, preferred_element_type=jnp.float32
+        ).astype(jnp.bfloat16)
+        for c, out in enumerate(outs):
+            out[:, i * block : (i + 1) * block] = pulled[c * rows : (c + 1) * rows]
+
+
+def pull(after, turned, basis, rows):
+    vmem = pl.BlockSpec(memory_space=pltpu.VMEM)
+    chunks = turned.shape[0] // rows - 1
     return pl.pallas_call(
-        functools.partial(pull_kernel, widths),
-        out_shape=[jax.ShapeDtypeStruct((width, rows), jnp.bfloat16) for width in widths],
-        in_specs=[pl.BlockSpec(memory_space=pltpu.SMEM)] + [hbm] * 4,
-        out_specs=[pl.BlockSpec(memory_space=pltpu.VMEM)] * len(widths),
-        scratch_shapes=[
-            pltpu.VMEM((blocks, block, depth), jnp.bfloat16),
-            pltpu.VMEM((depth, spread), jnp.bfloat16),
-            pltpu.VMEM((spread, depth), jnp.bfloat16),
-            pltpu.SemaphoreType.DMA((blocks + 1,)),
-        ],
-        compiler_params=pltpu.CompilerParams(vmem_limit_bytes=PULL_VMEM),
-    )(side, basis_in, basis_out, query_in, query_out)
+        pull_kernel,
+        out_shape=[jax.ShapeDtypeStruct((rows, basis.shape[0]), jnp.bfloat16)] * chunks,
+        in_specs=[vmem, vmem, pl.BlockSpec(memory_space=pl.ANY)],
+        out_specs=[vmem] * chunks,
+        compiler_params=pltpu.CompilerParams(vmem_limit_bytes=16 * 1024 * 1024),
+    )(turned, basis, after)
 
 
 def total_kernel(mine_ref, came_ref, *rest):
@@ -106,39 +120,46 @@
     )(flag, mine, came, after)
 
 
-def score_kernel(side_ref, own_ref, other_ref, acts_ref, grads_ref, after_ref, out_ref):
-    def go(factor_in_ref, factor_out_ref):
-        proj_in = lax.dot_general(factor_in_ref[...], acts_ref[...], NT, preferred_element_type=jnp.float32)
-        proj_out = lax.dot_general(factor_out_ref[...], grads_ref[...], NT, preferred_element_type=jnp.float32)
+def score_kernel(count, side_ref, acts_ref, grads_ref, after_ref, *rest):
+    own, other, out_ref = rest[:count], rest[count : 2 * count], rest[-1]
+
+    def go(factors_in, factors_out):
+        factor_in = jnp.concatenate([ref[...] for ref in factors_in], axis=0)
+        factor_out = jnp.concatenate([ref[...] for ref in factors_out], axis=0)
+        proj_in = lax.dot_general(factor_in, acts_ref[...], NT, preferred_element_type=jnp.float32)
+        proj_out = lax.dot_general(factor_out, grads_ref[...], NT, preferred_element_type=jnp.float32)
         product = proj_in * proj_out
         queries = product.shape[0] // RANK
         out_ref[...] = jnp.sum(product.reshape(queries, RANK, product.shape[1]), axis=1) * RANK ** (-0.5)
 
     @pl.when(side_ref[0] == 0)
     def _():
-        go(own_ref, other_ref)
+        go(own, other)
 
     @pl.when(side_ref[0] != 0)
     def _():
-        go(other_ref, own_ref)
+        go(other, own)
 
 
 def score(after, side, own, other, acts, grads):
     vmem = pl.BlockSpec(memory_space=pltpu.VMEM)
+    rows = sum(chunk.shape[0] for chunk in own)
     return pl.pallas_call(
-        score_kernel,
-        out_shape=jax.ShapeDtypeStruct((own.shape[0] // RANK, acts.shape[0]), jnp.float32),
-        in_specs=[pl.BlockSpec(memory_space=pltpu.SMEM), vmem, vmem, vmem, vmem, pl.BlockSpec(memory_space=pl.ANY)],
+        functools.partial(score_kernel, len(own)),
+        out_shape=jax.ShapeDtypeStruct((rows // RANK, acts.shape[0]), jnp.float32),
+        in_specs=[pl.BlockSpec(memory_space=pltpu.SMEM), vmem, vmem, pl.BlockSpec(memory_space=pl.ANY)]
+        + [vmem] * (2 * len(own)),
         out_specs=vmem,
-        compiler_params=pltpu.CompilerParams(vmem_limit_bytes=24 * 1024 * 1024),
-    )(side, own, other, acts, grads, after)
-
-
-def chunk_queries(queries):
-    if queries < 4:
-        return [1] * queries
-    inner = queries - 2
-    return [1] + [2] * (inner // 2) + [1] * (inner % 2) + [1]
+        compiler_params=pltpu.CompilerParams(vmem_limit_bytes=16 * 1024 * 1024),
+    )(side, acts, grads, after, *own, *other)
+
+
+def chunk_rows(spread):
+    for chunks, group in ((8, 2), (12, 1)):
+        rows = spread // chunks
+        if spread % chunks == 0 and rows % 16 == 0 and rows * group % RANK == 0:
+            return rows, group
+    return RANK, 1
 
 
 def sum_over_layers(value, layers):
@@ -173,10 +194,13 @@
     spread = query_in.shape[2]
     queries = spread // RANK
     half = n // 2
-    widths = [RANK * k for k in chunk_queries(queries)]
-    chunks = len(widths)
-
-    own = pull(side_array, basis_in[0], output_eigen_basis[0], query_in[0], query_out[0], widths)
+    rows, group = chunk_rows(spread)
+    chunks = spread // rows
+
+    first, basis, turned = first_pull(
+        side_array, basis_in[0], output_eigen_basis[0], query_in[0], query_out[0], rows
+    )
+    own = [first] + list(pull(first, turned, basis, rows))
     depth = jnp.minimum(z, n - 1 - z)
     at_hop = [(depth == hop).astype(jnp.int32).reshape(1) for hop in range(half - 1)]
 
@@ -204,8 +228,10 @@
             if not 0 <= c < chunks:
                 continue
             if kind == "swap":
-                pieces.append(score(after, side_array, part[c], came[c], acts[0], grads[0]))
-                after = pieces[-1]
+                if c % group == group - 1:
+                    span = slice(c + 1 - group, c + 1)
+                    pieces.append(score(after, side_array, part[span], came[span], acts[0], grads[0]))
+                    after = pieces[-1]
                 continue
             if kind == "out":
                 part[c] = take(after, at_hop[hop], part[c], came[c])
@@ -233,13 +259,12 @@
     flat = pooled.reshape(1, cells)
     target = pair_device[:, 0]
     cell = pair_query * docs + pair_doc
-    if n <= 8:
+    if n <= 8 and n & (n - 1) == 0:
         table = jnp.concatenate(
-            [flat]
-            + [lax.ppermute(flat, "dp", [(i, (i + k) % n) for i in range(n)]) for k in range(1, n)],
+            [flat] + [lax.ppermute(flat, "dp", [(i, i ^ k) for i in range(n)]) for k in range(1, n)],
             axis=1,
         )
-        column = lax.rem(z - target + n, n) * cells + cell
+        column = (z ^ target) * cells + cell
     else:
         table = lax.all_gather(flat, "dp", axis=1, tiled=True)
         column = target * cells + cell

time: 130 us -> 123 us (0.946)
  Pallas kernels: 25.1 us -> 17.3 us
  other arithmetic: 1 us -> 4.29 us
  starting transfers between devices: 70.8 us -> 67.6 us
  waiting for transfers between devices: 22.8 us -> 24.3 us
  local copies, waits for them, and re-layouts: 8.07 us -> 6.75 us
    ppermute x7 -> x8, waiting for transfers between devices: 1.88 us -> 10.6 us  [transfer(): lax.ppermute(value, 'dp', [(hop + 1, hop), (n - 2 - hop, n - 1 - hop)])]
    ppermute x7 -> x8, waiting for transfers between devices: 9.76 us -> 3.45 us  [transfer(): lax.ppermute(value, 'dp', [(hop, hop + 1), (n - 1 - hop, n - 2 - hop)])]
    pallas_call x8 -> x6, Pallas kernels: 14.3 us -> 11 us  [the longest x4 5.63 us: score(): pl.pallas_call(functools.partial(score_kernel, len(own)), out_shape=jax.S...]
    pallas_call x7 -> x8, Pallas kernels: 4.54 us -> 1.83 us  [take(): pl.pallas_call(take_kernel, out_shape=jax.ShapeDtypeStruct(mine.shape, mi...]
    ppermute x7 -> x8, starting transfers between devices: 9.5 us -> 7.05 us  [transfer(): return lax.ppermute(value, 'parts', [(0, 1), (1, 0)])]
    ppermute x7 -> x8, waiting for transfers between devices: 6.88 us -> 5 us  [transfer(): return lax.ppermute(value, 'parts', [(0, 1), (1, 0)])]
    pallas_call x14 -> x16, Pallas kernels: 6.24 us -> 4.44 us  [total(): pl.pallas_call(total_kernel, out_shape=[jax.ShapeDtypeStruct(a.shape, a.d...]
    ppermute x7 -> x8, starting transfers between devices: 39.4 us -> 37.6 us  [transfer(): lax.ppermute(value, 'dp', [(hop, hop + 1), (n - 1 - hop, n - 2 - hop)])]
  transfers between devices with their start and end apart: 34 -> 38, of which waited for: 14 -> 11; matrix products, arithmetic and copies ran while one was open for 0% -> 3% of each run, Pallas kernels for 15% -> 9%
where the time goes in v3:
time: 123 us; the launch traced here: 122 us
  starting transfers between devices  67.6 us (55%)
  waiting for transfers between devices  24.3 us (20%)
  Pallas kernels  17.3 us (14%)
  local copies, waits for them, and re-layouts  6.75 us (5%)
  other arithmetic  4.29 us (3%)
  between operations  1.41 us (1%)
    ppermute x8, starting transfers between devices, transfer(): lax.ppermute(value, 'dp', [(hop, hop + 1), (n - 1 - hop, n - 2 - hop)])  37.6 us
    ppermute x8, waiting for transfers between devices, transfer(): lax.ppermute(value, 'dp', [(hop + 1, hop), (n - 2 - hop, n - 1 - hop)])  10.6 us
    ppermute x8, starting transfers between devices, transfer(): lax.ppermute(value, 'dp', [(hop + 1, hop), (n - 2 - hop, n - 1 - hop)])  10.3 us
    ppermute x8, starting transfers between devices, transfer(): return lax.ppermute(value, 'parts', [(0, 1), (1, 0)])  7.05 us
    unnamed x44, local copies, waits for them, and re-layouts  6.57 us
    ppermute x8, starting transfers between devices, transfer(): return lax.ppermute(value, 'dp', [(half - 1, half), (half, half - 1)])  6.21 us
    pallas_call x4, Pallas kernels, score(): pl.pallas_call(functools.partial(score_kernel, len(own)), out_shape=jax.S...  5.63 us
    ppermute x8, waiting for transfers between devices, transfer(): return lax.ppermute(value, 'parts', [(0, 1), (1, 0)])  5 us
  transfers between devices with their start and end apart: 38, of which 11 were waited for; matrix products, arithmetic and copies ran while one was open for 3% of the time, Pallas kernels for 9%

profile of v3, /device:TPU:0, one launch (start us, length us, event | category | flops | bytes accessed | tf_op | source)
XLA Modules:
  0.0 121.8 jit_solution(13229979370164000125)
XLA Ops:
  0.6 3.8 %shard_map.113 = (bf16[48,2560]{1,0:T(8,128)(2,1)S(1)}, bf16[2560,640]{1,0:T(8,128)(2,1)S(1)}, bf16[640,384]{1,0:T(8,128)(2,1)}, bf16[384,640]{1,0:T(8,128)(2,1)S(1)}) custom-call(s32[1]{0:T(128)} %bitcast.side_ref, bf16[2560,640]{1,0:T(8,128)(2,1)} %bitcast.26, bf16[2560,640]{1,0:T(8,128)(2,1)} %bitcast.27, bf16[640,384]{1,0:T(8,128)(2,1)} %bitcast.28, ...), custom_call_target="tpu_custom_call" | custom-call | tf_op jit(solution)/shard_map/pallas_call | solution.py:48
  4.5 4.9 %collective-permute-start = (bf16[48,2560]{1,0:T(8,128)(2,1)S(1)}, bf16[48,2560]{1,0:T(8,128)(2,1)S(1)}, u32[]{:S(2)}, u32[]{:S(2)}) collective-permute-start(bf16[48,2560]{1,0:T(8,128)(2,1)S(1)} %get-tuple-element.26.after_ref.mine_ref.rest_0_), channel_id=1, source_target_pairs={{0,4},{12,8},{1,5},{13,9},{2,6},{14,10},{3,7},{15,11},{16,20},{28,... | collective-permute-start | bytes 737288 | tf_op jit(solution)/shard_map/ppermute | solution.py:212
  9.4 1.5 %shard_map.114 = (bf16[48,2560]{1,0:T(8,128)(2,1)S(1)}, bf16[48,2560]{1,0:T(8,128)(2,1)S(1)}, bf16[48,2560]{1,0:T(8,128)(2,1)S(1)}, bf16[48,2560]{1,0:T(8,128)(2...) custom-call(bf16[384,640]{1,0:T(8,128)(2,1)S(1)} %get-tuple-element.24.turned_ref,, ...), custom_call_target="tpu_custom_call" | custom-call | tf_op jit(solution)/shard_map/pallas_call | solution.py:73
  11.0 1.3 %collective-permute-start.3 = (bf16[48,2560]{1,0:T(8,128)(2,1)S(1)}, bf16[48,2560]{1,0:T(8,128)(2,1)S(1)}, u32[]{:S(2)}, u32[]{:S(2)}) collective-permute-start(bf16[48,2560]{1,0:T(8,128)(2,1)S(1)} %get-tuple-element.30.mine_ref), channel_id=1, source_target_pairs={{0,4},{12,8},{1,5},{13,9},{2,6},{14,10},{3,7},{15,11},{16,20},{28,... | collective-permute-start | bytes 737288 | tf_op jit(solution)/shard_map/ppermute | solution.py:212
  12.3 3.4 %collective-permute-done.came_ref = bf16[48,2560]{1,0:T(8,128)(2,1)S(1)} collective-permute-done((bf16[48,2560]{1,0:T(8,128)(2,1)S(1)}, bf16[48,2560]{1,0:T(8,128)(2,1)S(1)}, u32[]{:S(2)}, u32[]{:S(2)}) %collective-permute-start) | collective-permute-done | bytes 245792 | tf_op jit(solution)/shard_map/ppermute | solution.py:212
  16.5 7.2 %collective-permute-start.1 = (bf16[48,2560]{1,0:T(8,128)(2,1)S(1)}, bf16[48,2560]{1,0:T(8,128)(2,1)S(1)}, u32[]{:S(2)}, u32[]{:S(2)}) collective-permute-start(bf16[48,2560]{1,0:T(8,128)(2,1)S(1)} %get-tuple-element.28), channel_id=1, source_target_pairs={{0,4},{12,8},{1,5},{13,9},{2,6},{14,10},{3,7},{15,11},{16,20},{28,... | collective-permute-start | bytes 737288 | tf_op jit(solution)/shard_map/ppermute | solution.py:212
  25.2 1.3 %collective-permute-start.6 = (bf16[48,2560]{1,0:T(8,128)(2,1)S(1)}, bf16[48,2560]{1,0:T(8,128)(2,1)S(1)}, u32[]{:S(2)}, u32[]{:S(2)}) collective-permute-start(bf16[48,2560]{1,0:T(8,128)(2,1)S(1)} %shard_map.117.rest_0_.mine_ref), channel_id=1, source_target_pairs={{4,0},{8,12},{5,1},{9,13},{6,2},{10,14},{7,3},{11,15},{20,16},{24,... | collective-permute-start | bytes 737288 | tf_op jit(solution)/shard_map/ppermute | solution.py:216
  26.5 5.3 %collective-permute-start.5 = (bf16[48,2560]{1,0:T(8,128)(2,1)}, bf16[48,2560]{1,0:T(8,128)(2,1)}, u32[]{:S(2)}, u32[]{:S(2)}) collective-permute-start(bf16[48,2560]{1,0:T(8,128)(2,1)} %get-tuple-element.35), channel_id=1, source_target_pairs={{0,4},{12,8},{1,5},{13,9},{2,6},{14,10},{3,7},{15,11},{16,20},{28,... | collective-permute-start | bytes 737288 | tf_op jit(solution)/shard_map/ppermute | solution.py:212
  32.6 1.4 %collective-permute-start.4 = (bf16[48,2560]{1,0:T(8,128)(2,1)}, bf16[48,2560]{1,0:T(8,128)(2,1)}, u32[]{:S(2)}, u32[]{:S(2)}) collective-permute-start(bf16[48,2560]{1,0:T(8,128)(2,1)} %get-tuple-element.34.rest_0_.mine_ref), channel_id=1, source_target_pairs={{4,8},{8,4},{5,9},{9,5},{6,10},{10,6},{7,11},{11,7},{20,24},{24,20... | collective-permute-start | bytes 737288 | tf_op jit(solution)/shard_map/ppermute | solution.py:214
  34.1 1.3 %collective-permute-start.11 = (bf16[48,2560]{1,0:T(8,128)(2,1)S(1)}, bf16[48,2560]{1,0:T(8,128)(2,1)}, u32[]{:S(2)}, u32[]{:S(2)}) collective-permute-start(bf16[48,2560]{1,0:T(8,128)(2,1)S(1)} %shard_map.119.after_ref.mine_ref), channel_id=1, source_target_pairs={{4,0},{8,12},{5,1},{9,13},{6,2},{10,14},{7,3},{11,15},{20,16},{24,... | collective-permute-start | bytes 737288 | tf_op jit(solution)/shard_map/ppermute | solution.py:216
  35.4 5.2 %collective-permute-start.10 = (bf16[48,2560]{1,0:T(8,128)(2,1)}, bf16[48,2560]{1,0:T(8,128)(2,1)S(1)}, u32[]{:S(2)}, u32[]{:S(2)}) collective-permute-start(bf16[48,2560]{1,0:T(8,128)(2,1)} %get-tuple-element.38), channel_id=1, source_target_pairs={{0,4},{12,8},{1,5},{13,9},{2,6},{14,10},{3,7},{15,11},{16,20},{28,... | collective-permute-start | bytes 737288 | tf_op jit(solution)/shard_map/ppermute | solution.py:212
  48.2 1.3 %collective-permute-start.8 = (bf16[48,2560]{1,0:T(8,128)(2,1)S(1)}, bf16[48,2560]{1,0:T(8,128)(2,1)S(1)}, u32[]{:S(2)}, u32[]{:S(2)}) collective-permute-start(bf16[48,2560]{1,0:T(8,128)(2,1)S(1)} %shard_map.122.after_ref.mine_ref), channel_id=1, source_target_pairs={{4,0},{8,12},{5,1},{9,13},{6,2},{10,14},{7,3},{11,15},{20,16},{24,... | collective-permute-start | bytes 737288 | tf_op jit(solution)/shard_map/ppermute | solution.py:216
  50.5 1.6 %collective-permute-start.13 = (bf16[48,2560]{1,0:T(8,128)(2,1)S(1)}, bf16[48,2560]{1,0:T(8,128)(2,1)S(1)}, u32[]{:S(2)}, u32[]{:S(2)}) collective-permute-start(bf16[48,2560]{1,0:T(8,128)(2,1)S(1)} %shard_map.123.rest_0_.rest_1_), channel_id=1, source_target_pairs={{0,16},{16,0},{1,17},{17,1},{2,18},{18,2},{3,19},{19,3},{4,20},{20... | collective-permute-start | bytes 737288 | tf_op jit(solution)/shard_map/ppermute | solution.py:217
  52.6 4.6 %collective-permute-start.15 = (bf16[48,2560]{1,0:T(8,128)(2,1)S(1)}, bf16[48,2560]{1,0:T(8,128)(2,1)S(1)}, u32[]{:S(2)}, u32[]{:S(2)}) collective-permute-start(bf16[48,2560]{1,0:T(8,128)(2,1)S(1)} %get-tuple-element.41), channel_id=1, source_target_pairs={{0,4},{12,8},{1,5},{13,9},{2,6},{14,10},{3,7},{15,11},{16,20},{28,... | collective-permute-start | bytes 737288 | tf_op jit(solution)/shard_map/ppermute | solution.py:212
  60.0 1.3 %collective-permute-start.19 = (bf16[48,2560]{1,0:T(8,128)(2,1)S(1)}, bf16[48,2560]{1,0:T(8,128)(2,1)S(1)}, u32[]{:S(2)}, u32[]{:S(2)}) collective-permute-start(bf16[48,2560]{1,0:T(8,128)(2,1)S(1)} %shard_map.125.after_ref.mine_ref), channel_id=1, source_target_pairs={{4,0},{8,12},{5,1},{9,13},{6,2},{10,14},{7,3},{11,15},{20,16},{24,... | collective-permute-start | bytes 737288 | tf_op jit(solution)/shard_map/ppermute | solution.py:216
  61.3 4.6 %collective-permute-start.18 = (bf16[48,2560]{1,0:T(8,128)(2,1)S(1)}, bf16[48,2560]{1,0:T(8,128)(2,1)S(1)}, u32[]{:S(2)}, u32[]{:S(2)}) collective-permute-start(bf16[48,2560]{1,0:T(8,128)(2,1)S(1)} %get-tuple-element.44), channel_id=1, source_target_pairs={{0,4},{12,8},{1,5},{13,9},{2,6},{14,10},{3,7},{15,11},{16,20},{28,... | collective-permute-start | bytes 737288 | tf_op jit(solution)/shard_map/ppermute | solution.py:212
  65.9 1.6 %collective-permute-start.20 = (bf16[48,2560]{1,0:T(8,128)(2,1)S(1)}, bf16[48,2560]{1,0:T(8,128)(2,1)S(1)}, u32[]{:S(2)}, u32[]{:S(2)}) collective-permute-start(bf16[48,2560]{1,0:T(8,128)(2,1)S(1)} %shard_map.126.after_ref.rest_0_), channel_id=1, source_target_pairs={{0,16},{16,0},{1,17},{17,1},{2,18},{18,2},{3,19},{19,3},{4,20},{20... | collective-permute-start | bytes 737288 | tf_op jit(solution)/shard_map/ppermute | solution.py:217
  71.4 4.6 %collective-permute-start.23 = (bf16[48,2560]{1,0:T(8,128)(2,1)S(1)}, bf16[48,2560]{1,0:T(8,128)(2,1)S(1)}, u32[]{:S(2)}, u32[]{:S(2)}) collective-permute-start(bf16[48,2560]{1,0:T(8,128)(2,1)S(1)} %get-tuple-element.45), channel_id=1, source_target_pairs={{0,4},{12,8},{1,5},{13,9},{2,6},{14,10},{3,7},{15,11},{16,20},{28,... | collective-permute-start | bytes 737288 | tf_op jit(solution)/shard_map/ppermute | solution.py:212
  76.8 2.5 %collective-permute-done.16.came_ref = bf16[48,2560]{1,0:T(8,128)(2,1)S(1)} collective-permute-done((bf16[48,2560]{1,0:T(8,128)(2,1)S(1)}, bf16[48,2560]{1,0:T(8,128)(2,1)S(1)}, u32[]{:S(2)}, u32[]{:S(2)}) %collective-permute-start.16) | collective-permute-done | bytes 245792 | tf_op jit(solution)/shard_map/ppermute | solution.py:216
  84.0 4.6 %collective-permute-done.26.came_ref = bf16[48,2560]{1,0:T(8,128)(2,1)S(1)} collective-permute-done((bf16[48,2560]{1,0:T(8,128)(2,1)S(1)}, bf16[48,2560]{1,0:T(8,128)(2,1)S(1)}, u32[]{:S(2)}, u32[]{:S(2)}) %collective-permute-start.26) | collective-permute-done | bytes 245792 | tf_op jit(solution)/shard_map/ppermute | solution.py:216
  88.8 1.3 %collective-permute-start.29 = (bf16[48,2560]{1,0:T(8,128)(2,1)S(1)}, bf16[48,2560]{1,0:T(8,128)(2,1)S(1)}, u32[]{:S(2)}, u32[]{:S(2)}) collective-permute-start(bf16[48,2560]{1,0:T(8,128)(2,1)S(1)} %shard_map.138.after_ref.mine_ref), channel_id=1, source_target_pairs={{4,0},{8,12},{5,1},{9,13},{6,2},{10,14},{7,3},{11,15},{20,16},{24,... | collective-permute-start | bytes 737288 | tf_op jit(solution)/shard_map/ppermute | solution.py:216
  90.1 2.6 %collective-permute-done.24.came_ref = bf16[48,2560]{1,0:T(8,128)(2,1)S(1)} collective-permute-done((bf16[48,2560]{1,0:T(8,128)(2,1)S(1)}, bf16[48,2560]{1,0:T(8,128)(2,1)S(1)}, u32[]{:S(2)}, u32[]{:S(2)}) %collective-permute-start.24) | collective-permute-done | bytes 245792 | tf_op jit(solution)/shard_map/ppermute | solution.py:216
  92.7 1.9 %collective-permute-start.30 = (bf16[48,2560]{1,0:T(8,128)(2,1)S(1)}, bf16[48,2560]{1,0:T(8,128)(2,1)}, u32[]{:S(2)}, u32[]{:S(2)}) collective-permute-start(bf16[48,2560]{1,0:T(8,128)(2,1)S(1)} %shard_map.139.after_ref.rest_0_), channel_id=1, source_target_pairs={{0,16},{16,0},{1,17},{17,1},{2,18},{18,2},{3,19},{19,3},{4,20},{20... | collective-permute-start | bytes 737288 | tf_op jit(solution)/shard_map/ppermute | solution.py:217
  94.6 1.4 %collective-permute-done.28.rest_3_ = bf16[48,2560]{1,0:T(8,128)(2,1)S(1)} collective-permute-done((bf16[48,2560]{1,0:T(8,128)(2,1)S(1)}, bf16[48,2560]{1,0:T(8,128)(2,1)S(1)}, u32[]{:S(2)}, u32[]{:S(2)}) %collective-permute-start.28) | collective-permute-done | bytes 245792 | tf_op jit(solution)/shard_map/ppermute | solution.py:217
  99.6 1.4 %reduce-window.7 = s32[8,1]{0,1:T(1,128)} reduce-window(s32[8,1]{0,1:T(1,128)} %bitcast.30, s32[]{:T(128)} %constant.20.clone.1), window={size=8x1 pad=7_0x0_0}, to_apply=%region_0.0 | reduce-window | flops 56 | bytes 68 | tf_op jit(solution)/shard_map/reduce-window.2
  101.8 3.6 %collective-permute-done.31.rest_3_ = bf16[48,2560]{1,0:T(8,128)(2,1)} collective-permute-done((bf16[48,2560]{1,0:T(8,128)(2,1)}, bf16[48,2560]{1,0:T(8,128)(2,1)}, u32[]{:S(2)}, u32[]{:S(2)}) %collective-permute-start.31) | collective-permute-done | bytes 245792 | tf_op jit(solution)/shard_map/ppermute | solution.py:217
  105.4 2.3 %shard_map.142 = f32[3,320]{1,0:T(4,128)S(1)} custom-call(s32[1]{0:T(128)} %bitcast.side_ref, bf16[320,2560]{1,0:T(8,128)(2,1)S(1)} %bitcast.21, bf16[320,2560]{1,0:T(8,128)(2,1)S(1)} %bitcast.25, bf16[48,2560]{1,0:T(8,128)(2,1)} %shard_map.141.after_ref.rest_1_, bf16[48,2560]{1,0:T(8,128)(2,1)S(1)} %shard_map.139.after_ref.rest_0_, ...), custom_call_target="tpu_custom_call" | custom-call | tf_op jit(solution)/shard_map/pallas_call | solution.py:147
  107.8 1.6 %collective-permute-start.33 = (f32[12,320]{1,0:T(8,128)S(1)}, f32[12,320]{1,0:T(8,128)S(1)}, u32[]{:S(2)}, u32[]{:S(2)}) collective-permute-start(f32[12,320]{1,0:T(8,128)S(1)} %pad_maximum_fusion), channel_id=1, source_target_pairs={{0,2},{1,3},{2,0},{3,1},{4,6},{5,7},{6,4},{7,5},{8,10},{9,11},{10,... | collective-permute-start | bytes 46088 | tf_op jit(solution)/shard_map/ppermute | solution.py:169
  110.3 1.4 %collective-permute-done.33 = f32[12,320]{1,0:T(8,128)S(1)} collective-permute-done((f32[12,320]{1,0:T(8,128)S(1)}, f32[12,320]{1,0:T(8,128)S(1)}, u32[]{:S(2)}, u32[]{:S(2)}) %collective-permute-start.33) | collective-permute-done | bytes 15392 | tf_op jit(solution)/shard_map/ppermute | solution.py:169
  113.0 1.6 %collective-permute-start.35 = (f32[1,96]{1,0:T(1,128)S(1)}, f32[1,96]{1,0:T(1,128)S(1)}, u32[]{:S(2)}, u32[]{:S(2)}) collective-permute-start(f32[1,96]{1,0:T(1,128)S(1)} %reshape.53), channel_id=1, source_target_pairs={{0,4},{4,0},{8,12},{12,8},{1,5},{5,1},{9,13},{13,9},{2,6},{6,2},{1... | collective-permute-start | bytes 1160 | tf_op jit(solution)/shard_map/ppermute | solution.py:264
  115.7 1.7 %collective-permute-start.37 = (f32[1,96]{1,0:T(1,128)S(1)}, f32[1,96]{1,0:T(1,128)S(1)}, u32[]{:S(2)}, u32[]{:S(2)}) collective-permute-start(f32[1,96]{1,0:T(1,128)S(1)} %reshape.53), channel_id=1, source_target_pairs={{0,12},{4,8},{8,4},{12,0},{1,13},{5,9},{9,5},{13,1},{2,14},{6,10},... | collective-permute-start | bytes 1160 | tf_op jit(solution)/shard_map/ppermute | solution.py:264
  119.1 2.0 %collective-permute-done.37 = f32[1,96]{1,0:T(1,128)S(1)} collective-permute-done((f32[1,96]{1,0:T(1,128)S(1)}, f32[1,96]{1,0:T(1,128)S(1)}, u32[]{:S(2)}, u32[]{:S(2)}) %collective-permute-start.37) | collective-permute-done | bytes 416 | tf_op jit(solution)/shard_map/ppermute | solution.py:264
  (129 shorter events, 34.5 us)
Async XLA Ops:
  4.5 11.3 %collective-permute-start = (bf16[48,2560]{1,0:T(8,128)(2,1)S(1)}, bf16[48,2560]{1,0:T(8,128)(2,1)S(1)}, u32[]{:S(2)}, u32[]{:S(2)}) collective-permute-start(bf16[48,2560]{1,0:T(8,128)(2,1)S(1)} %get-tuple-element.26.after_ref.mine_ref.rest_0_), channel_id=1, source_target_pairs={{0,4},{12,8},{1,5},{13,9},{2,6},{14,10},{3,7},{15,11},{16,20},{28,... | collective-permute-start | bytes 737288 | tf_op jit(solution)/shard_map/ppermute | solution.py:212
  11.0 12.7 %collective-permute-start.3 = (bf16[48,2560]{1,0:T(8,128)(2,1)S(1)}, bf16[48,2560]{1,0:T(8,128)(2,1)S(1)}, u32[]{:S(2)}, u32[]{:S(2)}) collective-permute-start(bf16[48,2560]{1,0:T(8,128)(2,1)S(1)} %get-tuple-element.30.mine_ref), channel_id=1, source_target_pairs={{0,4},{12,8},{1,5},{13,9},{2,6},{14,10},{3,7},{15,11},{16,20},{28,... | collective-permute-start | bytes 737288 | tf_op jit(solution)/shard_map/ppermute | solution.py:212
  15.8 9.3 %collective-permute-start.2 = (bf16[48,2560]{1,0:T(8,128)(2,1)S(1)}, bf16[48,2560]{1,0:T(8,128)(2,1)S(1)}, u32[]{:S(2)}, u32[]{:S(2)}) collective-permute-start(bf16[48,2560]{1,0:T(8,128)(2,1)S(1)} %get-tuple-element.29.rest_0_.mine_ref), channel_id=1, source_target_pairs={{4,8},{8,4},{5,9},{9,5},{6,10},{10,6},{7,11},{11,7},{20,24},{24,20... | collective-permute-start | bytes 737288 | tf_op jit(solution)/shard_map/ppermute | solution.py:214
  16.5 15.3 %collective-permute-start.1 = (bf16[48,2560]{1,0:T(8,128)(2,1)S(1)}, bf16[48,2560]{1,0:T(8,128)(2,1)S(1)}, u32[]{:S(2)}, u32[]{:S(2)}) collective-permute-start(bf16[48,2560]{1,0:T(8,128)(2,1)S(1)} %get-tuple-element.28), channel_id=1, source_target_pairs={{0,4},{12,8},{1,5},{13,9},{2,6},{14,10},{3,7},{15,11},{16,20},{28,... | collective-permute-start | bytes 737288 | tf_op jit(solution)/shard_map/ppermute | solution.py:212
  24.5 9.5 %collective-permute-start.7 = (bf16[48,2560]{1,0:T(8,128)(2,1)S(1)}, bf16[48,2560]{1,0:T(8,128)(2,1)S(1)}, u32[]{:S(2)}, u32[]{:S(2)}) collective-permute-start(bf16[48,2560]{1,0:T(8,128)(2,1)S(1)} %get-tuple-element.32.rest_0_.mine_ref), channel_id=1, source_target_pairs={{4,8},{8,4},{5,9},{9,5},{6,10},{10,6},{7,11},{11,7},{20,24},{24,20... | collective-permute-start | bytes 737288 | tf_op jit(solution)/shard_map/ppermute | solution.py:214
  25.2 15.4 %collective-permute-start.6 = (bf16[48,2560]{1,0:T(8,128)(2,1)S(1)}, bf16[48,2560]{1,0:T(8,128)(2,1)S(1)}, u32[]{:S(2)}, u32[]{:S(2)}) collective-permute-start(bf16[48,2560]{1,0:T(8,128)(2,1)S(1)} %shard_map.117.rest_0_.mine_ref), channel_id=1, source_target_pairs={{4,0},{8,12},{5,1},{9,13},{6,2},{10,14},{7,3},{11,15},{20,16},{24,... | collective-permute-start | bytes 737288 | tf_op jit(solution)/shard_map/ppermute | solution.py:216
  26.5 16.8 %collective-permute-start.5 = (bf16[48,2560]{1,0:T(8,128)(2,1)}, bf16[48,2560]{1,0:T(8,128)(2,1)}, u32[]{:S(2)}, u32[]{:S(2)}) collective-permute-start(bf16[48,2560]{1,0:T(8,128)(2,1)} %get-tuple-element.35), channel_id=1, source_target_pairs={{0,4},{12,8},{1,5},{13,9},{2,6},{14,10},{3,7},{15,11},{16,20},{28,... | collective-permute-start | bytes 737288 | tf_op jit(solution)/shard_map/ppermute | solution.py:212
  32.6 14.4 %collective-permute-start.4 = (bf16[48,2560]{1,0:T(8,128)(2,1)}, bf16[48,2560]{1,0:T(8,128)(2,1)}, u32[]{:S(2)}, u32[]{:S(2)}) collective-permute-start(bf16[48,2560]{1,0:T(8,128)(2,1)} %get-tuple-element.34.rest_0_.mine_ref), channel_id=1, source_target_pairs={{4,8},{8,4},{5,9},{9,5},{6,10},{10,6},{7,11},{11,7},{20,24},{24,20... | collective-permute-start | bytes 737288 | tf_op jit(solution)/shard_map/ppermute | solution.py:214
  34.1 15.4 %collective-permute-start.11 = (bf16[48,2560]{1,0:T(8,128)(2,1)S(1)}, bf16[48,2560]{1,0:T(8,128)(2,1)}, u32[]{:S(2)}, u32[]{:S(2)}) collective-permute-start(bf16[48,2560]{1,0:T(8,128)(2,1)S(1)} %shard_map.119.after_ref.mine_ref), channel_id=1, source_target_pairs={{4,0},{8,12},{5,1},{9,13},{6,2},{10,14},{7,3},{11,15},{20,16},{24,... | collective-permute-start | bytes 737288 | tf_op jit(solution)/shard_map/ppermute | solution.py:216
  35.4 17.2 %collective-permute-start.10 = (bf16[48,2560]{1,0:T(8,128)(2,1)}, bf16[48,2560]{1,0:T(8,128)(2,1)S(1)}, u32[]{:S(2)}, u32[]{:S(2)}) collective-permute-start(bf16[48,2560]{1,0:T(8,128)(2,1)} %get-tuple-element.38), channel_id=1, source_target_pairs={{0,4},{12,8},{1,5},{13,9},{2,6},{14,10},{3,7},{15,11},{16,20},{28,... | collective-permute-start | bytes 737288 | tf_op jit(solution)/shard_map/ppermute | solution.py:212
  46.4 12.7 %collective-permute-start.9 = (bf16[48,2560]{1,0:T(8,128)(2,1)S(1)}, bf16[48,2560]{1,0:T(8,128)(2,1)S(1)}, u32[]{:S(2)}, u32[]{:S(2)}) collective-permute-start(bf16[48,2560]{1,0:T(8,128)(2,1)S(1)} %get-tuple-element.37.rest_0_.mine_ref), channel_id=1, source_target_pairs={{4,8},{8,4},{5,9},{9,5},{6,10},{10,6},{7,11},{11,7},{20,24},{24,20... | collective-permute-start | bytes 737288 | tf_op jit(solution)/shard_map/ppermute | solution.py:214
  48.2 11.8 %collective-permute-start.8 = (bf16[48,2560]{1,0:T(8,128)(2,1)S(1)}, bf16[48,2560]{1,0:T(8,128)(2,1)S(1)}, u32[]{:S(2)}, u32[]{:S(2)}) collective-permute-start(bf16[48,2560]{1,0:T(8,128)(2,1)S(1)} %shard_map.122.after_ref.mine_ref), channel_id=1, source_target_pairs={{4,0},{8,12},{5,1},{9,13},{6,2},{10,14},{7,3},{11,15},{20,16},{24,... | collective-permute-start | bytes 737288 | tf_op jit(solution)/shard_map/ppermute | solution.py:216
  50.5 10.8 %collective-permute-start.13 = (bf16[48,2560]{1,0:T(8,128)(2,1)S(1)}, bf16[48,2560]{1,0:T(8,128)(2,1)S(1)}, u32[]{:S(2)}, u32[]{:S(2)}) collective-permute-start(bf16[48,2560]{1,0:T(8,128)(2,1)S(1)} %shard_map.123.rest_0_.rest_1_), channel_id=1, source_target_pairs={{0,16},{16,0},{1,17},{17,1},{2,18},{18,2},{3,19},{19,3},{4,20},{20... | collective-permute-start | bytes 737288 | tf_op jit(solution)/shard_map/ppermute | solution.py:217
  52.1 13.9 %collective-permute-start.12 = (bf16[48,2560]{1,0:T(8,128)(2,1)S(1)}, bf16[48,2560]{1,0:T(8,128)(2,1)S(1)}, u32[]{:S(2)}, u32[]{:S(2)}) collective-permute-start(bf16[48,2560]{1,0:T(8,128)(2,1)S(1)} %shard_map.120.rest_0_), channel_id=1, source_target_pairs={{0,16},{16,0},{1,17},{17,1},{2,18},{18,2},{3,19},{19,3},{4,20},{20... | collective-permute-start | bytes 737288 | tf_op jit(solution)/shard_map/ppermute | solution.py:217
  52.6 16.1 %collective-permute-start.15 = (bf16[48,2560]{1,0:T(8,128)(2,1)S(1)}, bf16[48,2560]{1,0:T(8,128)(2,1)S(1)}, u32[]{:S(2)}, u32[]{:S(2)}) collective-permute-start(bf16[48,2560]{1,0:T(8,128)(2,1)S(1)} %get-tuple-element.41), channel_id=1, source_target_pairs={{0,4},{12,8},{1,5},{13,9},{2,6},{14,10},{3,7},{15,11},{16,20},{28,... | collective-permute-start | bytes 737288 | tf_op jit(solution)/shard_map/ppermute | solution.py:212
  59.1 10.3 %collective-permute-start.14 = (bf16[48,2560]{1,0:T(8,128)(2,1)S(1)}, bf16[48,2560]{1,0:T(8,128)(2,1)S(1)}, u32[]{:S(2)}, u32[]{:S(2)}) collective-permute-start(bf16[48,2560]{1,0:T(8,128)(2,1)S(1)} %get-tuple-element.40.rest_0_.mine_ref), channel_id=1, source_target_pairs={{4,8},{8,4},{5,9},{9,5},{6,10},{10,6},{7,11},{11,7},{20,24},{24,20... | collective-permute-start | bytes 737288 | tf_op jit(solution)/shard_map/ppermute | solution.py:214
  60.0 10.8 %collective-permute-start.19 = (bf16[48,2560]{1,0:T(8,128)(2,1)S(1)}, bf16[48,2560]{1,0:T(8,128)(2,1)S(1)}, u32[]{:S(2)}, u32[]{:S(2)}) collective-permute-start(bf16[48,2560]{1,0:T(8,128)(2,1)S(1)} %shard_map.125.after_ref.mine_ref), channel_id=1, source_target_pairs={{4,0},{8,12},{5,1},{9,13},{6,2},{10,14},{7,3},{11,15},{20,16},{24,... | collective-permute-start | bytes 737288 | tf_op jit(solution)/shard_map/ppermute | solution.py:216
  61.3 10.1 %collective-permute-start.18 = (bf16[48,2560]{1,0:T(8,128)(2,1)S(1)}, bf16[48,2560]{1,0:T(8,128)(2,1)S(1)}, u32[]{:S(2)}, u32[]{:S(2)}) collective-permute-start(bf16[48,2560]{1,0:T(8,128)(2,1)S(1)} %get-tuple-element.44), channel_id=1, source_target_pairs={{0,4},{12,8},{1,5},{13,9},{2,6},{14,10},{3,7},{15,11},{16,20},{28,... | collective-permute-start | bytes 737288 | tf_op jit(solution)/shard_map/ppermute | solution.py:212
  65.9 14.7 %collective-permute-start.20 = (bf16[48,2560]{1,0:T(8,128)(2,1)S(1)}, bf16[48,2560]{1,0:T(8,128)(2,1)S(1)}, u32[]{:S(2)}, u32[]{:S(2)}) collective-permute-start(bf16[48,2560]{1,0:T(8,128)(2,1)S(1)} %shard_map.126.after_ref.rest_0_), channel_id=1, source_target_pairs={{0,16},{16,0},{1,17},{17,1},{2,18},{18,2},{3,19},{19,3},{4,20},{20... | collective-permute-start | bytes 737288 | tf_op jit(solution)/shard_map/ppermute | solution.py:217
  68.8 7.3 %collective-permute-start.17 = (bf16[48,2560]{1,0:T(8,128)(2,1)S(1)}, bf16[48,2560]{1,0:T(8,128)(2,1)S(1)}, u32[]{:S(2)}, u32[]{:S(2)}) collective-permute-start(bf16[48,2560]{1,0:T(8,128)(2,1)S(1)} %get-tuple-element.43.rest_0_.mine_ref), channel_id=1, source_target_pairs={{4,8},{8,4},{5,9},{9,5},{6,10},{10,6},{7,11},{11,7},{20,24},{24,20... | collective-permute-start | bytes 737288 | tf_op jit(solution)/shard_map/ppermute | solution.py:214
  69.5 9.8 %collective-permute-start.16 = (bf16[48,2560]{1,0:T(8,128)(2,1)S(1)}, bf16[48,2560]{1,0:T(8,128)(2,1)S(1)}, u32[]{:S(2)}, u32[]{:S(2)}) collective-permute-start(bf16[48,2560]{1,0:T(8,128)(2,1)S(1)} %shard_map.129.after_ref.mine_ref), channel_id=1, source_target_pairs={{4,0},{8,12},{5,1},{9,13},{6,2},{10,14},{7,3},{11,15},{20,16},{24,... | collective-permute-start | bytes 737288 | tf_op jit(solution)/shard_map/ppermute | solution.py:216
  70.9 9.8 %collective-permute-start.21 = (bf16[48,2560]{1,0:T(8,128)(2,1)S(1)}, bf16[48,2560]{1,0:T(8,128)(2,1)S(1)}, u32[]{:S(2)}, u32[]{:S(2)}) collective-permute-start(bf16[48,2560]{1,0:T(8,128)(2,1)S(1)} %shard_map.130.rest_0_.rest_1_), channel_id=1, source_target_pairs={{0,16},{16,0},{1,17},{17,1},{2,18},{18,2},{3,19},{19,3},{4,20},{20... | collective-permute-start | bytes 737288 | tf_op jit(solution)/shard_map/ppermute | solution.py:217
  71.4 10.4 %collective-permute-start.23 = (bf16[48,2560]{1,0:T(8,128)(2,1)S(1)}, bf16[48,2560]{1,0:T(8,128)(2,1)S(1)}, u32[]{:S(2)}, u32[]{:S(2)}) collective-permute-start(bf16[48,2560]{1,0:T(8,128)(2,1)S(1)} %get-tuple-element.45), channel_id=1, source_target_pairs={{0,4},{12,8},{1,5},{13,9},{2,6},{14,10},{3,7},{15,11},{16,20},{28,... | collective-permute-start | bytes 737288 | tf_op jit(solution)/shard_map/ppermute | solution.py:212
  76.1 6.5 %collective-permute-start.22 = (bf16[48,2560]{1,0:T(8,128)(2,1)S(1)}, bf16[48,2560]{1,0:T(8,128)(2,1)S(1)}, u32[]{:S(2)}, u32[]{:S(2)}) collective-permute-start(bf16[48,2560]{1,0:T(8,128)(2,1)S(1)} %shard_map.131.rest_0_.mine_ref), channel_id=1, source_target_pairs={{4,8},{8,4},{5,9},{9,5},{6,10},{10,6},{7,11},{11,7},{20,24},{24,20... | collective-permute-start | bytes 737288 | tf_op jit(solution)/shard_map/ppermute | solution.py:214
  79.3 9.3 %collective-permute-start.26 = (bf16[48,2560]{1,0:T(8,128)(2,1)S(1)}, bf16[48,2560]{1,0:T(8,128)(2,1)S(1)}, u32[]{:S(2)}, u32[]{:S(2)}) collective-permute-start(bf16[48,2560]{1,0:T(8,128)(2,1)S(1)} %shard_map.132.after_ref.mine_ref), channel_id=1, source_target_pairs={{4,0},{8,12},{5,1},{9,13},{6,2},{10,14},{7,3},{11,15},{20,16},{24,... | collective-permute-start | bytes 737288 | tf_op jit(solution)/shard_map/ppermute | solution.py:216
  81.9 6.9 %collective-permute-start.25 = (bf16[48,2560]{1,0:T(8,128)(2,1)S(1)}, bf16[48,2560]{1,0:T(8,128)(2,1)S(1)}, u32[]{:S(2)}, u32[]{:S(2)}) collective-permute-start(bf16[48,2560]{1,0:T(8,128)(2,1)S(1)} %shard_map.135.rest_0_.mine_ref), channel_id=1, source_target_pairs={{4,8},{8,4},{5,9},{9,5},{6,10},{10,6},{7,11},{11,7},{20,24},{24,20... | collective-permute-start | bytes 737288 | tf_op jit(solution)/shard_map/ppermute | solution.py:214
  82.6 12.0 %collective-permute-start.27 = (bf16[48,2560]{1,0:T(8,128)(2,1)S(1)}, bf16[48,2560]{1,0:T(8,128)(2,1)S(1)}, u32[]{:S(2)}, u32[]{:S(2)}) collective-permute-start(bf16[48,2560]{1,0:T(8,128)(2,1)S(1)} %shard_map.133.after_ref.rest_0_), channel_id=1, source_target_pairs={{0,16},{16,0},{1,17},{17,1},{2,18},{18,2},{3,19},{19,3},{4,20},{20... | collective-permute-start | bytes 737288 | tf_op jit(solution)/shard_map/ppermute | solution.py:217
  82.7 10.0 %collective-permute-start.24 = (bf16[48,2560]{1,0:T(8,128)(2,1)S(1)}, bf16[48,2560]{1,0:T(8,128)(2,1)S(1)}, u32[]{:S(2)}, u32[]{:S(2)}) collective-permute-start(bf16[48,2560]{1,0:T(8,128)(2,1)S(1)} %shard_map.136.after_ref.mine_ref), channel_id=1, source_target_pairs={{4,0},{8,12},{5,1},{9,13},{6,2},{10,14},{7,3},{11,15},{20,16},{24,... | collective-permute-start | bytes 737288 | tf_op jit(solution)/shard_map/ppermute | solution.py:216
  88.7 7.3 %collective-permute-start.28 = (bf16[48,2560]{1,0:T(8,128)(2,1)S(1)}, bf16[48,2560]{1,0:T(8,128)(2,1)S(1)}, u32[]{:S(2)}, u32[]{:S(2)}) collective-permute-start(bf16[48,2560]{1,0:T(8,128)(2,1)S(1)} %shard_map.137.rest_0_.rest_1_), channel_id=1, source_target_pairs={{0,16},{16,0},{1,17},{17,1},{2,18},{18,2},{3,19},{19,3},{4,20},{20... | collective-permute-start | bytes 737288 | tf_op jit(solution)/shard_map/ppermute | solution.py:217
  88.8 9.3 %collective-permute-start.29 = (bf16[48,2560]{1,0:T(8,128)(2,1)S(1)}, bf16[48,2560]{1,0:T(8,128)(2,1)S(1)}, u32[]{:S(2)}, u32[]{:S(2)}) collective-permute-start(bf16[48,2560]{1,0:T(8,128)(2,1)S(1)} %shard_map.138.after_ref.mine_ref), channel_id=1, source_target_pairs={{4,0},{8,12},{5,1},{9,13},{6,2},{10,14},{7,3},{11,15},{20,16},{24,... | collective-permute-start | bytes 737288 | tf_op jit(solution)/shard_map/ppermute | solution.py:216
  92.7 9.1 %collective-permute-start.30 = (bf16[48,2560]{1,0:T(8,128)(2,1)S(1)}, bf16[48,2560]{1,0:T(8,128)(2,1)}, u32[]{:S(2)}, u32[]{:S(2)}) collective-permute-start(bf16[48,2560]{1,0:T(8,128)(2,1)S(1)} %shard_map.139.after_ref.rest_0_), channel_id=1, source_target_pairs={{0,16},{16,0},{1,17},{17,1},{2,18},{18,2},{3,19},{19,3},{4,20},{20... | collective-permute-start | bytes 737288 | tf_op jit(solution)/shard_map/ppermute | solution.py:217
  98.8 6.5 %collective-permute-start.31 = (bf16[48,2560]{1,0:T(8,128)(2,1)}, bf16[48,2560]{1,0:T(8,128)(2,1)}, u32[]{:S(2)}, u32[]{:S(2)}) collective-permute-start(bf16[48,2560]{1,0:T(8,128)(2,1)} %shard_map.141.after_ref.rest_1_), channel_id=1, source_target_pairs={{0,16},{16,0},{1,17},{17,1},{2,18},{18,2},{3,19},{19,3},{4,20},{20... | collective-permute-start | bytes 737288 | tf_op jit(solution)/shard_map/ppermute | solution.py:217
  (28 other events, 299.6 us)

commit v4 on v3

v4 whole, which is shorter than its diff:
```python
import functools

import jax
import jax.numpy as jnp
from jax import lax
from jax.experimental import pallas as pl
from jax.experimental.pallas import tpu as pltpu
from jax.sharding import PartitionSpec as P

RANK = 32
NT = (((1,), (1,)), ((), ()))


def first_pull_kernel(side_ref, basis_in_ref, basis_out_ref, query_in_ref, query_out_ref, out_ref, basis_ref, query_ref, turned_ref, sems):
    rows = out_ref.shape[0]

    def copies(from_basis, from_query):
        return [
            pltpu.make_async_copy(from_query, query_ref, sems.at[0]),
            pltpu.make_async_copy(from_basis, basis_ref, sems.at[1]),
        ]

    @pl.when(side_ref[0] == 0)
    def _():
        for copy in copies(basis_in_ref, query_in_ref):
            copy.start()

    @pl.when(side_ref[0] != 0)
    def _():
        for copy in copies(basis_out_ref, query_out_ref):
            copy.start()

    landed = copies(basis_in_ref, query_in_ref)
    landed[0].wait()
    turned_ref[...] = query_ref[...].T
    landed[1].wait()
    out_ref[...] = lax.dot_general(
        turned_ref[:rows], basis_ref[...], NT, preferred_element_type=jnp.float32
    ).astype(jnp.bfloat16)


def first_pull(side, basis_in, basis_out, query_in, query_out, rows):
    features, depth = basis_in.shape
    spread = query_in.shape[1]
    hbm = [pltpu.with_memory_space_constraint(a, pltpu.HBM) for a in (basis_in, basis_out, query_in, query_out)]
    vmem = pl.BlockSpec(memory_space=pltpu.VMEM)
    bf16 = functools.partial(jax.ShapeDtypeStruct, dtype=jnp.bfloat16)
    out, basis, _, turned = pl.pallas_call(
        first_pull_kernel,
        out_shape=[bf16((rows, features)), bf16((features, depth)), bf16((depth, spread)), bf16((spread, depth))],
        in_specs=[pl.BlockSpec(memory_space=pltpu.SMEM)] + [pl.BlockSpec(memory_space=pltpu.HBM)] * 4,
        out_specs=[vmem] * 4,
        scratch_shapes=[pltpu.SemaphoreType.DMA((2,))],
        compiler_params=pltpu.CompilerParams(vmem_limit_bytes=16 * 1024 * 1024),
    )(side, *hbm)
    return out, basis, turned


def pull_kernel(turned_ref, basis_ref, after_ref, *outs):
    rows, features = outs[0].shape
    block = 512 if features % 512 == 0 else features
    for i in range(features // block):
        pulled = lax.dot_general(
            turned_ref[rows:], basis_ref[i * block : (i + 1) * block], NT, preferred_element_type=jnp.float32
        ).astype(jnp.bfloat16)
        for c, out in enumerate(outs):
            out[:, i * block : (i + 1) * block] = pulled[c * rows : (c + 1) * rows]


def pull(after, turned, basis, rows):
    vmem = pl.BlockSpec(memory_space=pltpu.VMEM)
    chunks = turned.shape[0] // rows - 1
    return pl.pallas_call(
        pull_kernel,
        out_shape=[jax.ShapeDtypeStruct((rows, basis.shape[0]), jnp.bfloat16)] * chunks,
        in_specs=[vmem, vmem, pl.BlockSpec(memory_space=pl.ANY)],
        out_specs=[vmem] * chunks,
        compiler_params=pltpu.CompilerParams(vmem_limit_bytes=16 * 1024 * 1024),
    )(turned, basis, after)


def score_kernel(factors_ref, acts_ref, grads_ref, out_ref):
    spread = factors_ref.shape[0] // 2
    proj_in = lax.dot_general(factors_ref[:spread], acts_ref[...], NT, preferred_element_type=jnp.float32)
    proj_out = lax.dot_general(factors_ref[spread:], grads_ref[...], NT, preferred_element_type=jnp.float32)
    product = proj_in * proj_out
    queries = product.shape[0] // RANK
    out_ref[...] = jnp.sum(product.reshape(queries, RANK, product.shape[1]), axis=1) * RANK ** (-0.5)


def score(factors, acts, grads):
    vmem = pl.BlockSpec(memory_space=pltpu.VMEM)
    return pl.pallas_call(
        score_kernel,
        out_shape=jax.ShapeDtypeStruct((factors.shape[0] // 2 // RANK, acts.shape[0]), jnp.float32),
        in_specs=[vmem] * 3,
        out_specs=vmem,
        compiler_params=pltpu.CompilerParams(vmem_limit_bytes=24 * 1024 * 1024),
    )(factors, acts, grads)


def sum_over_layers(value, layers):
    if layers & (layers - 1):
        return lax.psum(value, "layer")
    terms = [value] + [
        lax.ppermute(value, "layer", [(i, i ^ k) for i in range(layers)]) for k in range(1, layers)
    ]
    while len(terms) > 1:
        terms = [terms[i] + terms[i + 1] for i in range(0, len(terms), 2)]
    return terms[0]


def per_device(
    acts,
    grads,
    basis_in,
    output_eigen_basis,
    query_in,
    query_out,
    doc_counts,
    pair_query,
    pair_device,
    pair_doc,
):
    n = lax.axis_size("dp")
    layers = lax.axis_size("layer")
    side = lax.axis_index("parts")
    z = lax.axis_index("dp")
    side_array = side.astype(jnp.int32).reshape(1)
    tokens, features = acts.shape[1:]
    spread = query_in.shape[2]
    queries = spread // RANK
    rows = spread // n
    first, basis, turned = first_pull(
        side_array, basis_in[0], output_eigen_basis[0], query_in[0], query_out[0], rows
    )
    own = jnp.concatenate([first] + list(pull(first, turned, basis, rows)), axis=0)
    shard = lax.psum_scatter(own, "dp", scatter_dimension=0, tiled=True)
    whole = lax.all_gather(shard, ("parts", "dp"), axis=0, tiled=True)
    scores = score(whole, acts[0], grads[0])

    token_scores = sum_over_layers(scores, layers)

    counts = doc_counts[0]
    ends = jnp.cumsum(counts)
    starts = ends - counts
    position = jnp.arange(tokens, dtype=jnp.int32)
    group_member = (
        (position[None, :] >= starts[:, None]) & (position[None, :] < ends[:, None])
    ).astype(jnp.float32)
    pooled = jnp.dot(token_scores, group_member.T, precision=lax.Precision.HIGHEST)
    pooled = pooled / jnp.sqrt(counts.astype(jnp.float32))[None, :]
    docs = counts.shape[0]
    cells = queries * docs
    flat = pooled.reshape(1, cells)
    target = pair_device[:, 0]
    cell = pair_query * docs + pair_doc
    if n <= 8 and n & (n - 1) == 0:
        table = jnp.concatenate(
            [flat] + [lax.ppermute(flat, "dp", [(i, i ^ k) for i in range(n)]) for k in range(1, n)],
            axis=1,
        )
        column = (z ^ target) * cells + cell
    else:
        table = lax.all_gather(flat, "dp", axis=1, tiled=True)
        column = target * cells + cell
    hit = column[:, None] == jnp.arange(n * cells, dtype=jnp.int32)[None, :]
    pair_scores = jnp.sum(jnp.where(hit, table, 0.0), axis=1)
    return (token_scores, pair_scores)


def solution(mesh):
    in_specs = (
        P("layer", ("parts", "dp"), None),
        P("layer", ("parts", "dp"), None),
        P("layer", None, "dp"),
        P("layer", None, "dp"),
        P("layer", "dp", None),
        P("layer", "dp", None),
        P(("parts", "dp"), None),
        P(("parts", "dp")),
        P(("parts", "dp"), None),
        P(("parts", "dp")),
    )
    out_specs = (P(None, ("parts", "dp")), P(("parts", "dp")))
    return jax.shard_map(
        per_device, mesh=mesh, in_specs=in_specs, out_specs=out_specs, check_vma=False
    )
```

time: 123 us -> 155 us (1.26)
  waiting for transfers between devices: 24.3 us -> 122 us
  starting transfers between devices: 67.6 us -> 6.47 us
  between operations: 1.41 us -> 14.1 us
  Pallas kernels: 17.3 us -> 7.41 us
  local copies, waits for them, and re-layouts: 6.75 us -> 2.33 us
  other arithmetic: 4.29 us -> 2.43 us
    all_gather x0 -> x1, waiting for transfers between devices: none -> 71.3 us  [per_device(): whole = lax.all_gather(shard, ('parts', 'dp'), axis=0, tiled=True)]
    ppermute x32 -> x0, starting transfers between devices: 61.2 us -> none  [the longest x8 37.6 us: transfer(): lax.ppermute(value, 'dp', [(hop, hop + 1), (n - 1 - hop, n - 2 - hop)])]
    reduce_scatter x0 -> x1, waiting for transfers between devices: none -> 44.2 us  [per_device(): shard = lax.psum_scatter(own, 'dp', scatter_dimension=0, tiled=True)]
    ppermute x32 -> x0, waiting for transfers between devices: 19.1 us -> none  [the longest x8 10.6 us: transfer(): lax.ppermute(value, 'dp', [(hop + 1, hop), (n - 2 - hop, n - 1 - hop)])]
    pallas_call x28 -> x1, Pallas kernels: 11.9 us -> 2.19 us  [score(): pl.pallas_call(score_kernel, out_shape=jax.ShapeDtypeStruct((factors.shap...]
    unnamed x44 -> x16, local copies, waits for them, and re-layouts: 6.57 us -> 2.15 us
  transfers between devices with their start and end apart: 38 -> 8, of which waited for: 11 -> 6; matrix products, arithmetic and copies ran while one was open for 3% -> 0% of each run, Pallas kernels for 9% -> 0%
where the time goes in v4:
time: 155 us
  waiting for transfers between devices  122 us (79%)
  between operations  14.1 us (9%)
  Pallas kernels  7.41 us (5%)
  starting transfers between devices  6.47 us (4%)
  other arithmetic  2.43 us (2%)
  local copies, waits for them, and re-layouts  2.33 us (2%)
    all_gather x1, waiting for transfers between devices, per_device(): whole = lax.all_gather(shard, ('parts', 'dp'), axis=0, tiled=True)  71.3 us
    reduce_scatter x1, waiting for transfers between devices, per_device(): shard = lax.psum_scatter(own, 'dp', scatter_dimension=0, tiled=True)  44.2 us
    ppermute x3, starting transfers between devices, per_device(): lax.ppermute(flat, 'dp', [(i, i ^ k) for i in range(n)])  4.45 us
    pallas_call x1, Pallas kernels, first_pull(): pl.pallas_call(first_pull_kernel, out_shape=[bf16((rows, features)), bf16...  3.87 us
    ppermute x3, waiting for transfers between devices, per_device(): lax.ppermute(flat, 'dp', [(i, i ^ k) for i in range(n)])  3.16 us
  transfers between devices with their start and end apart: 8, of which 6 were waited for; matrix products, arithmetic and copies ran while one was open for 0% of the time, Pallas kernels for 0%

profile of v4, /device:TPU:0, one launch (start us, length us, event | category | flops | bytes accessed | tf_op | source)
XLA Modules:
  0.0 154.6 jit_solution(6645388299687139010)
XLA Ops:
  7.2 0.0 reduce-scatter.2.cloned.1.call-start
  7.2 3.9 %shard_map.113 = (bf16[96,2560]{1,0:T(8,128)(2,1)S(1)}, bf16[2560,640]{1,0:T(8,128)(2,1)S(1)}, bf16[640,384]{1,0:T(8,128)(2,1)}, bf16[384,640]{1,0:T(8,128)(2,1)S(1)}) custom-call(s32[1]{0:T(128)} %bitcast.side_ref, bf16[2560,640]{1,0:T(8,128)(2,1)} %bitcast.19, bf16[2560,640]{1,0:T(8,128)(2,1)} %bitcast.20, bf16[640,384]{1,0:T(8,128)(2,1)} %bitcast.21, ...), custom_call_target="tpu_custom_call" | custom-call | tf_op jit(solution)/shard_map/pallas_call | solution.py:48
  11.1 1.4 shard_map.114
  12.5 0.0 copy-start.7
  12.5 0.0 copy-start.1
  12.5 0.0 copy-start.2
  12.5 1.4 pad_maximum_fusion
  13.9 0.0 reduce-scatter.2.cloned.1.call-update
  13.9 0.0 all-gather.2.cloned.1.call-start
  14.0 44.2 %reduce-scatter.2.cloned.1.call-done = bf16[96,2560]{1,0:T(8,128)(2,1)} async-done(((bf16[384,2560]{1,0:T(8,128)(2,1)}), bf16[96,2560]{1,0:T(8,128)(2,1)}) %reduce-scatter.2.cloned.1.call-update) | async-done | bytes 491536 | tf_op jit(solution)/shard_map/reduce_scatter | solution.py:138
  58.2 0.0 all-gather.2.cloned.1.call-update
  58.3 0.2 reduce-window.7
  58.5 71.3 %all-gather.2.cloned.1.call-done.factors_ref = bf16[768,2560]{1,0:T(8,128)(2,1)} async-done(((bf16[96,2560]{1,0:T(8,128)(2,1)}), bf16[768,2560]{1,0:T(8,128)(2,1)}) %all-gather.2.cloned.1.call-update) | async-done | bytes 3932176 | tf_op jit(solution)/shard_map/all_gather | solution.py:139
  129.7 2.1 %copy-done = bf16[768,2560]{1,0:T(8,128)(2,1)S(1)} copy-done((bf16[768,2560]{1,0:T(8,128)(2,1)S(1)}, bf16[768,2560]{1,0:T(8,128)(2,1)}, u32[]{:S(2)}) %copy-start) | copy-done | bytes 3932184
  131.9 2.2 %shard_map.115 = f32[12,320]{1,0:T(8,128)S(1)} custom-call(bf16[768,2560]{1,0:T(8,128)(2,1)S(1)} %copy-done, bf16[320,2560]{1,0:T(8,128)(2,1)S(1)} %bitcast.17, bf16[320,2560]{1,0:T(8,128)(2,1)S(1)} %bitcast.18), custom_call_target="tpu_custom_call" | custom-call | tf_op jit(solution)/shard_map/pallas_call | solution.py:93
  134.1 0.1 collective-permute-start
  134.1 1.5 collective-permute-start.1
  135.7 0.3 collective-permute-start.2
  136.0 0.0 collective-permute-done
  136.0 2.0 %collective-permute-done.1 = f32[12,320]{1,0:T(8,128)S(1)} collective-permute-done((f32[12,320]{1,0:T(8,128)S(1)}, f32[12,320]{1,0:T(8,128)S(1)}, u32[]{:S(2)}, u32[]{:S(2)}) %collective-permute-start.1) | collective-permute-done | bytes 15392 | tf_op jit(solution)/shard_map/ppermute | solution.py:106
  138.0 0.9 collective-permute-done.2
  138.9 0.0 copy-start.3
  138.9 0.2 convolution_divide_fusion
  139.1 0.1 copy.14
  139.2 0.1 reshape.46
  139.3 1.1 collective-permute-start.3
  140.4 1.2 collective-permute-start.4
  141.6 2.2 %collective-permute-start.5 = (f32[1,96]{1,0:T(1,128)S(1)}, f32[1,96]{1,0:T(1,128)S(1)}, u32[]{:S(2)}, u32[]{:S(2)}) collective-permute-start(f32[1,96]{1,0:T(1,128)S(1)} %reshape.46), channel_id=1, source_target_pairs={{0,12},{4,8},{8,4},{12,0},{1,13},{5,9},{9,5},{13,1},{2,14},{6,10},... | collective-permute-start | bytes 1160 | tf_op jit(solution)/shard_map/ppermute | solution.py:160
  143.8 1.0 collective-permute-done.4
  144.8 2.1 %collective-permute-done.5 = f32[1,96]{1,0:T(1,128)S(1)} collective-permute-done((f32[1,96]{1,0:T(1,128)S(1)}, f32[1,96]{1,0:T(1,128)S(1)}, u32[]{:S(2)}, u32[]{:S(2)}) %collective-permute-start.5) | collective-permute-done | bytes 416 | tf_op jit(solution)/shard_map/ppermute | solution.py:160
  146.9 0.1 maximum_reduce_fusion
  147.0 0.7 select_reduce_fusion
  (16 shorter events, 0.0 us)
Async XLA Ops:
  7.2 51.1 %reduce-scatter.2.cloned.1.call-start = ((), (), s32[]{:S(2)}) async-start(), calls=%async_computation.1 | async-start | bytes 2457600 | tf_op jit(solution)/shard_map/reduce_scatter | solution.py:138
  12.5 45.8 %copy-start.7 = (s32[1,8]{1,0:T(1,128)S(1)}, s32[1,8]{1,0:T(1,128)}, u32[]{:S(2)}) copy-start(s32[1,8]{1,0:T(1,128)} %param.16) | copy-start | bytes 100
  12.5 117.3 %copy-start.1 = (bf16[1,320,2560]{2,1,0:T(8,128)(2,1)S(1)}, bf16[1,320,2560]{2,1,0:T(8,128)(2,1)}, u32[]{:S(2)}) copy-start(bf16[1,320,2560]{2,1,0:T(8,128)(2,1)} %param.10) | copy-start | bytes 4915204
  12.5 117.3 %copy-start.2 = (bf16[1,320,2560]{2,1,0:T(8,128)(2,1)S(1)}, bf16[1,320,2560]{2,1,0:T(8,128)(2,1)}, u32[]{:S(2)}) copy-start(bf16[1,320,2560]{2,1,0:T(8,128)(2,1)} %param.11) | copy-start | bytes 4915204
  13.9 115.8 %all-gather.2.cloned.1.call-start = ((), (), s32[]{:S(2)}) async-start(), calls=%async_computation.2 | async-start | bytes 4423680 | tf_op jit(solution)/shard_map/all_gather | solution.py:139
  129.7 2.1 %copy-start = (bf16[768,2560]{1,0:T(8,128)(2,1)S(1)}, bf16[768,2560]{1,0:T(8,128)(2,1)}, u32[]{:S(2)}) copy-start(bf16[768,2560]{1,0:T(8,128)(2,1)} %all-gather.2.cloned.1.call-done.factors_ref) | copy-start | bytes 11796484
  131.9 11.9 %copy-start.4 = (s32[128]{0:T(128)S(1)}, s32[128]{0:T(128)}, u32[]{:S(2)}) copy-start(s32[128]{0:T(128)} %param.19) | copy-start | bytes 1540
  131.9 11.9 %copy-start.5 = (s32[128]{0:T(128)S(1)}, s32[128]{0:T(128)}, u32[]{:S(2)}) copy-start(s32[128]{0:T(128)} %param.17) | copy-start | bytes 1540
  131.9 11.9 %copy-start.6 = (s32[128,1]{0,1:T(1,128)S(1)}, s32[128,1]{0,1:T(1,128)}, u32[]{:S(2)}) copy-start(s32[128,1]{0,1:T(1,128)} %param.18) | copy-start | bytes 1540
  134.1 2.0 %collective-permute-start = (f32[12,320]{1,0:T(8,128)S(1)}, f32[12,320]{1,0:T(8,128)S(1)}, u32[]{:S(2)}, u32[]{:S(2)}) collective-permute-start(f32[12,320]{1,0:T(8,128)S(1)} %shard_map.115), channel_id=1, source_target_pairs={{0,1},{1,0},{2,3},{3,2},{4,5},{5,4},{6,7},{7,6},{8,9},{9,8},{10,11... | collective-permute-start | bytes 46088 | tf_op jit(solution)/shard_map/ppermute | solution.py:106
  134.1 3.9 %collective-permute-start.1 = (f32[12,320]{1,0:T(8,128)S(1)}, f32[12,320]{1,0:T(8,128)S(1)}, u32[]{:S(2)}, u32[]{:S(2)}) collective-permute-start(f32[12,320]{1,0:T(8,128)S(1)} %shard_map.115), channel_id=1, source_target_pairs={{0,2},{1,3},{2,0},{3,1},{4,6},{5,7},{6,4},{7,5},{8,10},{9,11},{10,... | collective-permute-start | bytes 46088 | tf_op jit(solution)/shard_map/ppermute | solution.py:106
  135.7 3.3 %collective-permute-start.2 = (f32[12,320]{1,0:T(8,128)S(1)}, f32[12,320]{1,0:T(8,128)S(1)}, u32[]{:S(2)}, u32[]{:S(2)}) collective-permute-start(f32[12,320]{1,0:T(8,128)S(1)} %shard_map.115), channel_id=1, source_target_pairs={{0,3},{1,2},{2,1},{3,0},{4,7},{5,6},{6,5},{7,4},{8,11},{9,10},{10,... | collective-permute-start | bytes 46088 | tf_op jit(solution)/shard_map/ppermute | solution.py:106
  138.9 8.8 %copy-start.3 = (f32[12,320]{1,0:T(8,128)}, f32[12,320]{1,0:T(8,128)S(1)}, u32[]{:S(2)}) copy-start(f32[12,320]{1,0:T(8,128)S(1)} %add_add_fusion) | copy-start | bytes 46084
  139.3 4.5 %collective-permute-start.3 = (f32[1,96]{1,0:T(1,128)S(1)}, f32[1,96]{1,0:T(1,128)S(1)}, u32[]{:S(2)}, u32[]{:S(2)}) collective-permute-start(f32[1,96]{1,0:T(1,128)S(1)} %reshape.46), channel_id=1, source_target_pairs={{0,4},{4,0},{8,12},{12,8},{1,5},{5,1},{9,13},{13,9},{2,6},{6,2},{1... | collective-permute-start | bytes 1160 | tf_op jit(solution)/shard_map/ppermute | solution.py:160
  140.4 4.4 %collective-permute-start.4 = (f32[1,96]{1,0:T(1,128)S(1)}, f32[1,96]{1,0:T(1,128)S(1)}, u32[]{:S(2)}, u32[]{:S(2)}) collective-permute-start(f32[1,96]{1,0:T(1,128)S(1)} %reshape.46), channel_id=1, source_target_pairs={{0,8},{4,12},{8,0},{12,4},{1,9},{5,13},{9,1},{13,5},{2,10},{6,14},... | collective-permute-start | bytes 1160 | tf_op jit(solution)/shard_map/ppermute | solution.py:160
  141.6 5.3 %collective-permute-start.5 = (f32[1,96]{1,0:T(1,128)S(1)}, f32[1,96]{1,0:T(1,128)S(1)}, u32[]{:S(2)}, u32[]{:S(2)}) collective-permute-start(f32[1,96]{1,0:T(1,128)S(1)} %reshape.46), channel_id=1, source_target_pairs={{0,12},{4,8},{8,4},{12,0},{1,13},{5,9},{9,5},{13,1},{2,14},{6,10},... | collective-permute-start | bytes 1160 | tf_op jit(solution)/shard_map/ppermute | solution.py:160
Sparse Core Ops, SparseCore 0:
  14.1 44.1 reduce-scatter.1
  60.3 69.3 all-gather.1

commit v5 on v3

v5 whole, which is shorter than its diff:
```python
import functools

import jax
import jax.numpy as jnp
from jax import lax
from jax.experimental import pallas as pl
from jax.experimental.pallas import tpu as pltpu
from jax.sharding import PartitionSpec as P

RANK = 32
NT = (((1,), (1,)), ((), ()))


VMEM = pl.BlockSpec(memory_space=pltpu.VMEM)
HBM = pl.BlockSpec(memory_space=pltpu.HBM)
ANY = pl.BlockSpec(memory_space=pl.ANY)
MIB = 1024 * 1024


def in_hbm(*arrays):
    return [pltpu.with_memory_space_constraint(array, pltpu.HBM) for array in arrays]


def bf16(*shape):
    return jax.ShapeDtypeStruct(shape, jnp.bfloat16)


def first_pull_kernel(basis_in_ref, basis_out_ref, query_in_ref, query_out_ref, out_ref, basis_ref, query_ref, turned_ref, sems):
    rows = out_ref.shape[0]
    features = basis_ref.shape[0]
    block = 512 if features % 512 == 0 else features
    spans = [pl.ds(first, block) for first in range(0, features, block)]

    def copies(from_basis, from_query):
        return [pltpu.make_async_copy(from_query, query_ref, sems.at[0])] + [
            pltpu.make_async_copy(from_basis.at[span], basis_ref.at[span], sems.at[1 + i])
            for i, span in enumerate(spans)
        ]

    side = lax.axis_index("parts")

    @pl.when(side == 0)
    def _():
        for copy in copies(basis_in_ref, query_in_ref):
            copy.start()

    @pl.when(side != 0)
    def _():
        for copy in copies(basis_out_ref, query_out_ref):
            copy.start()

    landed = copies(basis_in_ref, query_in_ref)
    landed[0].wait()
    turned_ref[...] = query_ref[...].T
    for copy, span in zip(landed[1:], spans):
        copy.wait()
        out_ref[:, span] = lax.dot_general(
            turned_ref[:rows], basis_ref[span], NT, preferred_element_type=jnp.float32
        ).astype(jnp.bfloat16)


def first_pull(basis_in, basis_out, query_in, query_out, rows):
    features, depth = basis_in.shape
    spread = query_in.shape[1]
    blocks = features // 512 if features % 512 == 0 else 1
    out, basis, _, turned = pl.pallas_call(
        first_pull_kernel,
        out_shape=[bf16(rows, features), bf16(features, depth), bf16(depth, spread), bf16(spread, depth)],
        in_specs=[HBM] * 4,
        out_specs=[VMEM] * 4,
        scratch_shapes=[pltpu.SemaphoreType.DMA((1 + blocks,))],
        compiler_params=pltpu.CompilerParams(vmem_limit_bytes=16 * MIB),
    )(*in_hbm(basis_in, basis_out, query_in, query_out))
    return out, basis, turned


def pull_kernel(turned_ref, basis_ref, after_ref, *outs):
    rows, features = outs[0].shape
    block = 512 if features % 512 == 0 else features
    for i in range(features // block):
        pulled = lax.dot_general(
            turned_ref[rows:], basis_ref[i * block : (i + 1) * block], NT, preferred_element_type=jnp.float32
        ).astype(jnp.bfloat16)
        for c, out in enumerate(outs):
            out[:, i * block : (i + 1) * block] = pulled[c * rows : (c + 1) * rows]


def pull(after, turned, basis, rows):
    chunks = turned.shape[0] // rows - 1
    return pl.pallas_call(
        pull_kernel,
        out_shape=[bf16(rows, basis.shape[0])] * chunks,
        in_specs=[VMEM, VMEM, ANY],
        out_specs=[VMEM] * chunks,
        compiler_params=pltpu.CompilerParams(vmem_limit_bytes=16 * MIB),
    )(turned, basis, after)


def deal_kernel(acts_ref, grads_ref, after_ref, mine_ref, theirs_ref, sems):
    def copies(mine, theirs):
        return [
            pltpu.make_async_copy(mine, mine_ref, sems.at[0]),
            pltpu.make_async_copy(theirs, theirs_ref, sems.at[1]),
        ]

    side = lax.axis_index("parts")

    @pl.when(side == 0)
    def _():
        for copy in copies(acts_ref, grads_ref):
            copy.start()

    @pl.when(side != 0)
    def _():
        for copy in copies(grads_ref, acts_ref):
            copy.start()

    for copy in copies(acts_ref, grads_ref):
        copy.wait()


def deal(after, acts, grads):
    return pl.pallas_call(
        deal_kernel,
        out_shape=[bf16(*acts.shape)] * 2,
        in_specs=[HBM, HBM, ANY],
        out_specs=[VMEM, VMEM],
        scratch_shapes=[pltpu.SemaphoreType.DMA((2,))],
        compiler_params=pltpu.CompilerParams(vmem_limit_bytes=8 * MIB),
    )(*in_hbm(acts, grads), after)


def total_kernel(mine_ref, came_ref, after_ref, *rest):
    mine = mine_ref[...].astype(jnp.float32) + came_ref[...].astype(jnp.float32)
    rest[-1][...] = mine.astype(jnp.bfloat16)
    if len(rest) == 3:
        rest[1][...] = rest[0][...]


def total(after, mine, came, later=None):
    extra = [] if later is None else [later]
    out = pl.pallas_call(
        total_kernel,
        out_shape=[bf16(*a.shape) for a in extra + [mine]],
        in_specs=[VMEM, VMEM, ANY] + [VMEM] * len(extra),
        out_specs=[VMEM] * (1 + len(extra)),
        compiler_params=pltpu.CompilerParams(vmem_limit_bytes=8 * MIB),
    )(mine, came, after, *extra)
    return out[-1], (out[0] if extra else None)


def take_kernel(hop, mine_ref, came_ref, after_ref, out_ref):
    z = lax.axis_index("dp")
    here = jnp.minimum(z, lax.axis_size("dp") - 1 - z) == hop

    @pl.when(here)
    def _():
        out_ref[...] = came_ref[...]

    @pl.when(jnp.logical_not(here))
    def _():
        out_ref[...] = mine_ref[...]


def take(after, hop, mine, came):
    return pl.pallas_call(
        functools.partial(take_kernel, hop),
        out_shape=bf16(*mine.shape),
        in_specs=[VMEM, VMEM, ANY],
        out_specs=VMEM,
        compiler_params=pltpu.CompilerParams(vmem_limit_bytes=8 * MIB),
    )(mine, came, after)


def project_kernel(tokens_ref, others_ref, after_ref, *rest):
    factors = jnp.concatenate([ref[...] for ref in rest[:-2]], axis=0)
    others = lax.dot_general(factors, others_ref[...], NT, preferred_element_type=jnp.float32)
    rest[-1][...] = others.astype(jnp.bfloat16)
    rest[-2][...] = lax.dot_general(factors, tokens_ref[...], NT, preferred_element_type=jnp.float32)


def project(after, factors, tokens, others):
    rows = sum(chunk.shape[0] for chunk in factors)
    return pl.pallas_call(
        project_kernel,
        out_shape=[jax.ShapeDtypeStruct((rows, tokens.shape[0]), jnp.float32), bf16(rows, others.shape[0])],
        in_specs=[VMEM, VMEM, ANY] + [VMEM] * len(factors),
        out_specs=[VMEM, VMEM],
        compiler_params=pltpu.CompilerParams(vmem_limit_bytes=16 * MIB),
    )(tokens, others, after, *factors)


def score_kernel(count, *refs):
    out_ref, first = refs[-1], 0
    for own_ref, other_ref in zip(refs[:count], refs[count : 2 * count]):
        product = own_ref[...] * other_ref[...].astype(jnp.float32)
        queries = product.shape[0] // RANK
        out_ref[first : first + queries] = jnp.sum(
            product.reshape(queries, RANK, product.shape[1]), axis=1
        ) * RANK ** (-0.5)
        first += queries


def score(own, other):
    rows = sum(piece.shape[0] for piece in own)
    return pl.pallas_call(
        functools.partial(score_kernel, len(own)),
        out_shape=jax.ShapeDtypeStruct((rows // RANK, own[0].shape[1]), jnp.float32),
        in_specs=[VMEM] * (2 * len(own)),
        out_specs=VMEM,
        compiler_params=pltpu.CompilerParams(vmem_limit_bytes=8 * MIB),
    )(*own, *other)


def pool_kernel(counts_ref, one_ref, two_ref, scores_ref, pooled_ref):
    scores = one_ref[...] + two_ref[...]
    scores_ref[...] = scores
    position = lax.broadcasted_iota(jnp.int32, scores.shape, 1)
    column = lax.broadcasted_iota(jnp.int32, pooled_ref.shape, 1)
    pooled = jnp.zeros(pooled_ref.shape, jnp.float32)
    start = jnp.int32(0)
    for k in range(counts_ref.shape[1]):
        count = counts_ref[0, k]
        inside = (position >= start) & (position < start + count)
        found = jnp.sum(jnp.where(inside, scores, 0.0), axis=1, keepdims=True)
        root = jnp.sqrt(jnp.full((1, 1), count, jnp.int32).astype(jnp.float32))
        pooled = jnp.where(column == k, found / root, pooled)
        start = start + count
    pooled_ref[...] = pooled


def pool(counts, one, two):
    return pl.pallas_call(
        pool_kernel,
        out_shape=[
            jax.ShapeDtypeStruct(one.shape, jnp.float32),
            jax.ShapeDtypeStruct((one.shape[0], counts.shape[1]), jnp.float32),
        ],
        in_specs=[pl.BlockSpec(memory_space=pltpu.SMEM), VMEM, VMEM],
        out_specs=[VMEM, VMEM],
        compiler_params=pltpu.CompilerParams(vmem_limit_bytes=8 * MIB),
    )(counts, one, two)


def chunk_rows(spread):
    for chunks, group in ((8, 2), (12, 1)):
        rows = spread // chunks
        if spread % chunks == 0 and rows % 16 == 0 and rows * group % RANK == 0:
            return rows, group
    return RANK, 1


def is_power(number):
    return number & (number - 1) == 0


def per_device(
    acts,
    grads,
    basis_in,
    output_eigen_basis,
    query_in,
    query_out,
    doc_counts,
    pair_query,
    pair_device,
    pair_doc,
):
    n = lax.axis_size("dp")
    layers = lax.axis_size("layer")
    z = lax.axis_index("dp")
    spread = query_in.shape[2]
    queries = spread // RANK
    half = n // 2
    rows, group = chunk_rows(spread)
    chunks = spread // rows

    first, basis, turned = first_pull(
        basis_in[0], output_eigen_basis[0], query_in[0], query_out[0], rows
    )
    own = [first] + list(pull(first, turned, basis, rows))
    swap = [(0, 1), (1, 0)]

    stages = [("in", hop) for hop in range(half - 1)] + [("mid", 0)]
    stages += [("out", hop) for hop in range(half - 2, -1, -1)]

    def transfer(kind, hop, value):
        if kind == "in":
            return lax.ppermute(value, "dp", [(hop, hop + 1), (n - 1 - hop, n - 2 - hop)])
        if kind == "mid":
            return lax.ppermute(value, "dp", [(half - 1, half), (half, half - 1)])
        return lax.ppermute(value, "dp", [(hop + 1, hop), (n - 2 - hop, n - 1 - hop)])

    part, came = list(own), [None] * chunks
    ahead = min(2, chunks)
    for c in range(ahead):
        came[c] = transfer(*stages[0], part[c])
    after = own[-1]
    tokens, theirs = deal(own[-1], acts[0], grads[0])
    others = lax.ppermute(theirs, "parts", swap)
    waiting, mine, back = [], [], []
    for turn in range(chunks + len(stages) - 1):
        for s, (kind, hop) in enumerate(stages):
            c = turn - s
            if not 0 <= c < chunks:
                continue
            if kind == "out":
                part[c] = take(after, hop, part[c], came[c])
            else:
                later = c + ahead if s == 0 and c + ahead < chunks else None
                part[c], moved = total(after, part[c], came[c], None if later is None else own[later])
                if later is not None:
                    came[later] = transfer(*stages[0], moved)
            after = part[c]
            if s + 1 < len(stages):
                came[c] = transfer(*stages[s + 1], part[c])
            elif c % group == group - 1:
                waiting.append(part[c + 1 - group : c + 1])
        while turn >= chunks - 1 and waiting:
            projected, away = project(after, waiting.pop(0), tokens, others)
            mine.append(projected)
            back.append(lax.ppermute(away, "parts", swap))
            after = projected

    scores = score(mine, back)
    if is_power(layers):
        step = 1
        while 2 * step < layers:
            scores = scores + lax.ppermute(scores, "layer", [(i, i ^ step) for i in range(layers)])
            step *= 2
        one, two = scores, lax.ppermute(scores, "layer", [(i, i ^ step) for i in range(layers)])
    else:
        one = lax.psum(scores, "layer")
        two = jnp.zeros_like(one)
    token_scores, pooled = pool(doc_counts, one, two)

    docs = doc_counts.shape[1]
    cells = queries * docs
    target = pair_device[:, 0]
    cell = pair_query * docs + pair_doc
    if n <= 8 and is_power(n):
        table, step = pooled[None], 1
        while step < n:
            table = jnp.concatenate(
                [table, lax.ppermute(table, "dp", [(i, i ^ step) for i in range(n)])], axis=0
            )
            step *= 2
        table = table.reshape(1, n * cells)
        column = (z ^ target) * cells + cell
    else:
        table = lax.all_gather(pooled.reshape(1, cells), "dp", axis=1, tiled=True)
        column = target * cells + cell
    hit = column[:, None] == jnp.arange(n * cells, dtype=jnp.int32)[None, :]
    pair_scores = jnp.sum(jnp.where(hit, table, 0.0), axis=1)
    return (token_scores, pair_scores)


def solution(mesh):
    in_specs = (
        P("layer", ("parts", "dp"), None),
        P("layer", ("parts", "dp"), None),
        P("layer", None, "dp"),
        P("layer", None, "dp"),
        P("layer", "dp", None),
        P("layer", "dp", None),
        P(("parts", "dp"), None),
        P(("parts", "dp")),
        P(("parts", "dp"), None),
        P(("parts", "dp")),
    )
    out_specs = (P(None, ("parts", "dp")), P(("parts", "dp")))
    return jax.shard_map(
        per_device, mesh=mesh, in_specs=in_specs, out_specs=out_specs, check_vma=False
    )
```

time: 123 us -> 102 us (0.83)
  starting transfers between devices: 67.6 us -> 56.8 us
  local copies, waits for them, and re-layouts: 6.75 us -> 0.3 us
  waiting for transfers between devices: 24.3 us -> 28.5 us
  other arithmetic: 4.29 us -> 0.73 us
  Pallas kernels: 17.3 us -> 13.8 us
    ppermute x14 -> x9, starting transfers between devices: 13.4 us -> 5.88 us  [the longest x4 2.75 us: per_device(): back.append(lax.ppermute(away, 'parts', swap))]
    unnamed x44 -> x8, local copies, waits for them, and re-layouts: 6.57 us -> 0.03 us
    pallas_call x4 -> x1, Pallas kernels: 5.63 us -> 0.11 us  [score(): pl.pallas_call(functools.partial(score_kernel, len(own)), out_shape=jax.S...]
    ppermute x14 -> x9, waiting for transfers between devices: 10.2 us -> 15.7 us  [the longest x2 8.11 us: per_device(): lax.ppermute(table, 'dp', [(i, i ^ step) for i in range(n)])]
    ppermute x8, waiting for transfers between devices: 3.45 us -> 0.07 us  [transfer(): lax.ppermute(value, 'dp', [(hop, hop + 1), (n - 1 - hop, n - 2 - hop)])]
    ppermute x8, starting transfers between devices: 37.6 us -> 35.2 us  [transfer(): lax.ppermute(value, 'dp', [(hop, hop + 1), (n - 1 - hop, n - 2 - hop)])]
    ppermute x8, waiting for transfers between devices: 10.6 us -> 12.7 us  [transfer(): lax.ppermute(value, 'dp', [(hop + 1, hop), (n - 2 - hop, n - 1 - hop)])]
    pallas_call x26 -> x32, Pallas kernels: 11.6 us -> 13.7 us  [the longest x4 4.37 us: project(): pl.pallas_call(project_kernel, out_shape=[jax.ShapeDtypeStruct((rows, tok...]
  transfers between devices with their start and end apart: 38 -> 33, of which waited for: 11 -> 12; matrix products, arithmetic and copies ran while one was open for 3% -> 0% of each run, Pallas kernels for 9% -> 9%
where the time goes in v5:
time: 102 us; the launch traced here: 101 us
  starting transfers between devices  56.8 us (56%)
  waiting for transfers between devices  28.5 us (28%)
  Pallas kernels  13.8 us (14%)
  between operations  1.23 us (1%)
    ppermute x8, starting transfers between devices, transfer(): lax.ppermute(value, 'dp', [(hop, hop + 1), (n - 1 - hop, n - 2 - hop)])  35.2 us
    ppermute x8, waiting for transfers between devices, transfer(): lax.ppermute(value, 'dp', [(hop + 1, hop), (n - 2 - hop, n - 1 - hop)])  12.7 us
    ppermute x8, starting transfers between devices, transfer(): lax.ppermute(value, 'dp', [(hop + 1, hop), (n - 2 - hop, n - 1 - hop)])  10.3 us
    ppermute x2, waiting for transfers between devices, per_device(): lax.ppermute(table, 'dp', [(i, i ^ step) for i in range(n)])  8.11 us
    ppermute x8, starting transfers between devices, transfer(): return lax.ppermute(value, 'dp', [(half - 1, half), (half, half - 1)])  5.41 us
    pallas_call x4, Pallas kernels, project(): pl.pallas_call(project_kernel, out_shape=[jax.ShapeDtypeStruct((rows, tok...  4.37 us
    ppermute x4, waiting for transfers between devices, per_device(): back.append(lax.ppermute(away, 'parts', swap))  4.05 us
    ppermute x2, waiting for transfers between devices, per_device(): lax.ppermute(scores, 'layer', [(i, i ^ step) for i in range(layers)])  3.54 us
  transfers between devices with their start and end apart: 33, of which 12 were waited for; matrix products, arithmetic and copies ran while one was open for 0% of the time, Pallas kernels for 9%

profile of v5, /device:TPU:0, one launch (start us, length us, event | category | flops | bytes accessed | tf_op | source)
XLA Modules:
  0.0 101.4 jit_solution(5813138778098391800)
XLA Ops:
  0.6 3.5 %shard_map.113 = (bf16[48,2560]{1,0:T(8,128)(2,1)S(1)}, bf16[2560,640]{1,0:T(8,128)(2,1)S(1)}, bf16[640,384]{1,0:T(8,128)(2,1)}, bf16[384,640]{1,0:T(8,128)(2,1)S(1)}) custom-call(bf16[2560,640]{1,0:T(8,128)(2,1)} %bitcast.9, bf16[2560,640]{1,0:T(8,128)(2,1)} %bitcast.10, bf16[640,384]{1,0:T(8,128)(2,1)} %bitcast.13, bf16[640,384]{1,0:T(8,128)(2,1)} %bitcast.14), custom_call_target="tpu_custom_call" | custom-call | tf_op jit(solution)/shard_map/pallas_call | solution.py:66
  4.1 4.9 %collective-permute-start.2 = (bf16[48,2560]{1,0:T(8,128)(2,1)S(1)}, bf16[48,2560]{1,0:T(8,128)(2,1)S(1)}, u32[]{:S(2)}, u32[]{:S(2)}) collective-permute-start(bf16[48,2560]{1,0:T(8,128)(2,1)S(1)} %get-tuple-element.38.after_ref.mine_ref), channel_id=1, source_target_pairs={{0,4},{12,8},{1,5},{13,9},{2,6},{14,10},{3,7},{15,11},{16,20},{28,... | collective-permute-start | bytes 737288 | tf_op jit(solution)/shard_map/ppermute | solution.py:289
  9.0 1.5 %shard_map.114 = (bf16[48,2560]{1,0:T(8,128)(2,1)S(1)}, bf16[48,2560]{1,0:T(8,128)(2,1)S(1)}, bf16[48,2560]{1,0:T(8,128)(2,1)S(1)}, bf16[48,2560]{1,0:T(8,128)(2...) custom-call(bf16[384,640]{1,0:T(8,128)(2,1)S(1)} %get-tuple-element.36.turned_ref,, ...), custom_call_target="tpu_custom_call" | custom-call | tf_op jit(solution)/shard_map/pallas_call | solution.py:90
  10.6 2.0 %shard_map.115 = (bf16[320,2560]{1,0:T(8,128)(2,1)S(1)}, bf16[320,2560]{1,0:T(8,128)(2,1)S(1)}) custom-call(bf16[320,2560]{1,0:T(8,128)(2,1)} %bitcast.11, bf16[320,2560]{1,0:T(8,128)(2,1)} %bitcast.12, bf16[48,2560]{1,0:T(8,128)(2,1)S(1)} %get-tuple-element.39.after_ref.rest_0_.mine_ref), custom_call_target="tpu_custom_call" | custom-call | tf_op jit(solution)/shard_map/pallas_call | solution.py:123
  12.5 1.6 %collective-permute-start = (bf16[320,2560]{1,0:T(8,128)(2,1)S(1)}, bf16[320,2560]{1,0:T(8,128)(2,1)S(1)}, u32[]{:S(2)}, u32[]{:S(2)}) collective-permute-start(bf16[320,2560]{1,0:T(8,128)(2,1)S(1)} %get-tuple-element.41), channel_id=1, source_target_pairs={{0,16},{16,0},{1,17},{17,1},{2,18},{18,2},{3,19},{19,3},{4,20},{20... | collective-permute-start | bytes 4915208 | tf_op jit(solution)/shard_map/ppermute | solution.py:300
  14.1 1.3 %collective-permute-start.1 = (bf16[48,2560]{1,0:T(8,128)(2,1)S(1)}, bf16[48,2560]{1,0:T(8,128)(2,1)S(1)}, u32[]{:S(2)}, u32[]{:S(2)}) collective-permute-start(bf16[48,2560]{1,0:T(8,128)(2,1)S(1)} %get-tuple-element.44.mine_ref), channel_id=1, source_target_pairs={{0,4},{12,8},{1,5},{13,9},{2,6},{14,10},{3,7},{15,11},{16,20},{28,... | collective-permute-start | bytes 737288 | tf_op jit(solution)/shard_map/ppermute | solution.py:289
  16.2 6.0 %collective-permute-start.7 = (bf16[48,2560]{1,0:T(8,128)(2,1)S(1)}, bf16[48,2560]{1,0:T(8,128)(2,1)S(1)}, u32[]{:S(2)}, u32[]{:S(2)}) collective-permute-start(bf16[48,2560]{1,0:T(8,128)(2,1)S(1)} %get-tuple-element.49), channel_id=1, source_target_pairs={{0,4},{12,8},{1,5},{13,9},{2,6},{14,10},{3,7},{15,11},{16,20},{28,... | collective-permute-start | bytes 737288 | tf_op jit(solution)/shard_map/ppermute | solution.py:289
  23.0 1.3 %collective-permute-start.5 = (bf16[48,2560]{1,0:T(8,128)(2,1)S(1)}, bf16[48,2560]{1,0:T(8,128)(2,1)S(1)}, u32[]{:S(2)}, u32[]{:S(2)}) collective-permute-start(bf16[48,2560]{1,0:T(8,128)(2,1)S(1)} %shard_map.118.after_ref.mine_ref), channel_id=1, source_target_pairs={{4,0},{8,12},{5,1},{9,13},{6,2},{10,14},{7,3},{11,15},{20,16},{24,... | collective-permute-start | bytes 737288 | tf_op jit(solution)/shard_map/ppermute | solution.py:292
  24.3 5.8 %collective-permute-start.3 = (bf16[48,2560]{1,0:T(8,128)(2,1)S(1)}, bf16[48,2560]{1,0:T(8,128)(2,1)S(1)}, u32[]{:S(2)}, u32[]{:S(2)}) collective-permute-start(bf16[48,2560]{1,0:T(8,128)(2,1)S(1)} %get-tuple-element.47), channel_id=1, source_target_pairs={{0,4},{12,8},{1,5},{13,9},{2,6},{14,10},{3,7},{15,11},{16,20},{28,... | collective-permute-start | bytes 737288 | tf_op jit(solution)/shard_map/ppermute | solution.py:289
  31.0 1.3 %collective-permute-start.13 = (bf16[48,2560]{1,0:T(8,128)(2,1)S(1)}, bf16[48,2560]{1,0:T(8,128)(2,1)S(1)}, u32[]{:S(2)}, u32[]{:S(2)}) collective-permute-start(bf16[48,2560]{1,0:T(8,128)(2,1)S(1)} %shard_map.120.after_ref.mine_ref), channel_id=1, source_target_pairs={{4,0},{8,12},{5,1},{9,13},{6,2},{10,14},{7,3},{11,15},{20,16},{24,... | collective-permute-start | bytes 737288 | tf_op jit(solution)/shard_map/ppermute | solution.py:292
  32.4 4.5 %collective-permute-start.12 = (bf16[48,2560]{1,0:T(8,128)(2,1)S(1)}, bf16[48,2560]{1,0:T(8,128)(2,1)S(1)}, u32[]{:S(2)}, u32[]{:S(2)}) collective-permute-start(bf16[48,2560]{1,0:T(8,128)(2,1)S(1)} %get-tuple-element.54), channel_id=1, source_target_pairs={{0,4},{12,8},{1,5},{13,9},{2,6},{14,10},{3,7},{15,11},{16,20},{28,... | collective-permute-start | bytes 737288 | tf_op jit(solution)/shard_map/ppermute | solution.py:289
  37.8 1.3 %collective-permute-start.10 = (bf16[48,2560]{1,0:T(8,128)(2,1)S(1)}, bf16[48,2560]{1,0:T(8,128)(2,1)S(1)}, u32[]{:S(2)}, u32[]{:S(2)}) collective-permute-start(bf16[48,2560]{1,0:T(8,128)(2,1)S(1)} %shard_map.123.after_ref.mine_ref), channel_id=1, source_target_pairs={{4,0},{8,12},{5,1},{9,13},{6,2},{10,14},{7,3},{11,15},{20,16},{24,... | collective-permute-start | bytes 737288 | tf_op jit(solution)/shard_map/ppermute | solution.py:292
  39.1 4.6 %collective-permute-start.8 = (bf16[48,2560]{1,0:T(8,128)(2,1)S(1)}, bf16[48,2560]{1,0:T(8,128)(2,1)S(1)}, u32[]{:S(2)}, u32[]{:S(2)}) collective-permute-start(bf16[48,2560]{1,0:T(8,128)(2,1)S(1)} %get-tuple-element.52), channel_id=1, source_target_pairs={{0,4},{12,8},{1,5},{13,9},{2,6},{14,10},{3,7},{15,11},{16,20},{28,... | collective-permute-start | bytes 737288 | tf_op jit(solution)/shard_map/ppermute | solution.py:289
  44.6 1.3 %collective-permute-start.16 = (bf16[48,2560]{1,0:T(8,128)(2,1)S(1)}, bf16[48,2560]{1,0:T(8,128)(2,1)S(1)}, u32[]{:S(2)}, u32[]{:S(2)}) collective-permute-start(bf16[48,2560]{1,0:T(8,128)(2,1)S(1)} %shard_map.126.after_ref.mine_ref), channel_id=1, source_target_pairs={{4,0},{8,12},{5,1},{9,13},{6,2},{10,14},{7,3},{11,15},{20,16},{24,... | collective-permute-start | bytes 737288 | tf_op jit(solution)/shard_map/ppermute | solution.py:292
  46.1 4.3 %collective-permute-start.15 = (bf16[48,2560]{1,0:T(8,128)(2,1)S(1)}, bf16[48,2560]{1,0:T(8,128)(2,1)S(1)}, u32[]{:S(2)}, u32[]{:S(2)}) collective-permute-start(bf16[48,2560]{1,0:T(8,128)(2,1)S(1)} %get-tuple-element.58), channel_id=1, source_target_pairs={{0,4},{12,8},{1,5},{13,9},{2,6},{14,10},{3,7},{15,11},{16,20},{28,... | collective-permute-start | bytes 737288 | tf_op jit(solution)/shard_map/ppermute | solution.py:289
  51.3 1.3 %collective-permute-start.21 = (bf16[48,2560]{1,0:T(8,128)(2,1)S(1)}, bf16[48,2560]{1,0:T(8,128)(2,1)S(1)}, u32[]{:S(2)}, u32[]{:S(2)}) collective-permute-start(bf16[48,2560]{1,0:T(8,128)(2,1)S(1)} %shard_map.129.after_ref.mine_ref), channel_id=1, source_target_pairs={{4,0},{8,12},{5,1},{9,13},{6,2},{10,14},{7,3},{11,15},{20,16},{24,... | collective-permute-start | bytes 737288 | tf_op jit(solution)/shard_map/ppermute | solution.py:292
  53.4 3.8 %collective-permute-start.20 = (bf16[48,2560]{1,0:T(8,128)(2,1)S(1)}, bf16[48,2560]{1,0:T(8,128)(2,1)S(1)}, u32[]{:S(2)}, u32[]{:S(2)}) collective-permute-start(bf16[48,2560]{1,0:T(8,128)(2,1)S(1)} %get-tuple-element.59), channel_id=1, source_target_pairs={{0,4},{12,8},{1,5},{13,9},{2,6},{14,10},{3,7},{15,11},{16,20},{28,... | collective-permute-start | bytes 737288 | tf_op jit(solution)/shard_map/ppermute | solution.py:289
  58.1 1.3 %collective-permute-start.18 = (bf16[48,2560]{1,0:T(8,128)(2,1)S(1)}, bf16[48,2560]{1,0:T(8,128)(2,1)S(1)}, u32[]{:S(2)}, u32[]{:S(2)}) collective-permute-start(bf16[48,2560]{1,0:T(8,128)(2,1)S(1)} %shard_map.132.after_ref.mine_ref), channel_id=1, source_target_pairs={{4,0},{8,12},{5,1},{9,13},{6,2},{10,14},{7,3},{11,15},{20,16},{24,... | collective-permute-start | bytes 737288 | tf_op jit(solution)/shard_map/ppermute | solution.py:292
  59.4 1.4 %collective-permute-done.21.came_ref = bf16[48,2560]{1,0:T(8,128)(2,1)S(1)} collective-permute-done((bf16[48,2560]{1,0:T(8,128)(2,1)S(1)}, bf16[48,2560]{1,0:T(8,128)(2,1)S(1)}, u32[]{:S(2)}, u32[]{:S(2)}) %collective-permute-start.21) | collective-permute-done | bytes 245792 | tf_op jit(solution)/shard_map/ppermute | solution.py:292
  61.7 1.3 %collective-permute-start.24 = (bf16[48,2560]{1,0:T(8,128)(2,1)S(1)}, bf16[48,2560]{1,0:T(8,128)(2,1)S(1)}, u32[]{:S(2)}, u32[]{:S(2)}) collective-permute-start(bf16[48,2560]{1,0:T(8,128)(2,1)S(1)} %shard_map.135.after_ref.mine_ref), channel_id=1, source_target_pairs={{4,0},{8,12},{5,1},{9,13},{6,2},{10,14},{7,3},{11,15},{20,16},{24,... | collective-permute-start | bytes 737288 | tf_op jit(solution)/shard_map/ppermute | solution.py:292
  63.0 5.8 %collective-permute-done.18.came_ref = bf16[48,2560]{1,0:T(8,128)(2,1)S(1)} collective-permute-done((bf16[48,2560]{1,0:T(8,128)(2,1)S(1)}, bf16[48,2560]{1,0:T(8,128)(2,1)S(1)}, u32[]{:S(2)}, u32[]{:S(2)}) %collective-permute-start.18) | collective-permute-done | bytes 245792 | tf_op jit(solution)/shard_map/ppermute | solution.py:292
  70.0 1.1 %shard_map.138 = (f32[96,320]{1,0:T(8,128)S(1)}, bf16[96,320]{1,0:T(8,128)(2,1)S(1)}) custom-call(bf16[320,2560]{1,0:T(8,128)(2,1)S(1)} %get-tuple-element.40.tokens_ref, bf16[320,2560]{1,0:T(8,128)(2,1)S(1)} %collective-permute-done.others_ref, f32[96,320]{1,0:T(8,128)S(1)} %get-tuple-element.60.after_ref.refs_0_, ...), custom_call_target="tpu_custom_call" | custom-call | tf_op jit(solution)/shard_map/pallas_call | solution.py:184
  72.2 1.3 %collective-permute-start.23 = (bf16[48,2560]{1,0:T(8,128)(2,1)S(1)}, bf16[48,2560]{1,0:T(8,128)(2,1)S(1)}, u32[]{:S(2)}, u32[]{:S(2)}) collective-permute-start(bf16[48,2560]{1,0:T(8,128)(2,1)S(1)} %shard_map.140.after_ref.mine_ref), channel_id=1, source_target_pairs={{4,0},{8,12},{5,1},{9,13},{6,2},{10,14},{7,3},{11,15},{20,16},{24,... | collective-permute-start | bytes 737288 | tf_op jit(solution)/shard_map/ppermute | solution.py:292
  73.9 1.7 %collective-permute-start.26 = (bf16[96,320]{1,0:T(8,128)(2,1)S(1)}, bf16[96,320]{1,0:T(8,128)(2,1)S(1)}, u32[]{:S(2)}, u32[]{:S(2)}) collective-permute-start(bf16[96,320]{1,0:T(8,128)(2,1)S(1)} %get-tuple-element.65), channel_id=1, source_target_pairs={{0,16},{16,0},{1,17},{17,1},{2,18},{18,2},{3,19},{19,3},{4,20},{20... | collective-permute-start | bytes 184328 | tf_op jit(solution)/shard_map/ppermute | solution.py:322
  75.9 4.4 %collective-permute-done.23.came_ref = bf16[48,2560]{1,0:T(8,128)(2,1)S(1)} collective-permute-done((bf16[48,2560]{1,0:T(8,128)(2,1)S(1)}, bf16[48,2560]{1,0:T(8,128)(2,1)S(1)}, u32[]{:S(2)}, u32[]{:S(2)}) %collective-permute-start.23) | collective-permute-done | bytes 245792 | tf_op jit(solution)/shard_map/ppermute | solution.py:292
  81.9 4.0 %collective-permute-done.28.refs_7_ = bf16[96,320]{1,0:T(8,128)(2,1)S(1)} collective-permute-done((bf16[96,320]{1,0:T(8,128)(2,1)S(1)}, bf16[96,320]{1,0:T(8,128)(2,1)S(1)}, u32[]{:S(2)}, u32[]{:S(2)}) %collective-permute-start.28) | collective-permute-done | bytes 61472 | tf_op jit(solution)/shard_map/ppermute | solution.py:322
  86.1 1.2 %collective-permute-done.29 = f32[12,320]{1,0:T(8,128)S(1)} collective-permute-done((f32[12,320]{1,0:T(8,128)S(1)}, f32[12,320]{1,0:T(8,128)S(1)}, u32[]{:S(2)}, u32[]{:S(2)}) %collective-permute-start.29) | collective-permute-done | bytes 15392 | tf_op jit(solution)/shard_map/ppermute | solution.py:329
  87.3 1.5 %collective-permute-start.30 = (f32[12,320]{1,0:T(8,128)S(1)}, f32[12,320]{1,0:T(8,128)S(1)}, u32[]{:S(2)}, u32[]{:S(2)}) collective-permute-start(f32[12,320]{1,0:T(8,128)S(1)} %add.9.one_ref), channel_id=1, source_target_pairs={{0,2},{1,3},{2,0},{3,1},{4,6},{5,7},{6,4},{7,5},{8,10},{9,11},{10,... | collective-permute-start | bytes 46088 | tf_op jit(solution)/shard_map/ppermute | solution.py:331
  88.7 2.4 %collective-permute-done.30.two_ref = f32[12,320]{1,0:T(8,128)S(1)} collective-permute-done((f32[12,320]{1,0:T(8,128)S(1)}, f32[12,320]{1,0:T(8,128)S(1)}, u32[]{:S(2)}, u32[]{:S(2)}) %collective-permute-start.30) | collective-permute-done | bytes 15392 | tf_op jit(solution)/shard_map/ppermute | solution.py:331
  91.1 1.2 %shard_map.145 = (f32[12,320]{1,0:T(8,128)}, f32[12,8]{1,0:T(8,128)S(1)}) custom-call(s32[1,8]{1,0:T(1,128)S(1)} %copy-done, f32[12,320]{1,0:T(8,128)S(1)} %add.9.one_ref, f32[12,320]{1,0:T(8,128)S(1)} %collective-permute-done.30.two_ref), custom_call_target="tpu_custom_call" | custom-call | tf_op jit(solution)/shard_map/pallas_call | solution.py:233
  92.3 3.6 %collective-permute-done.31 = f32[1,12,8]{1,2,0:T(8,128)S(1)} collective-permute-done((f32[1,12,8]{1,2,0:T(8,128)S(1)}, f32[1,12,8]{1,2,0:T(8,128)S(1)}, u32[]{:S(2)}, u32[]{:S(2)}) %collective-permute-start.31) | collective-permute-done | bytes 416 | tf_op jit(solution)/shard_map/ppermute | solution.py:345
  96.0 4.5 %collective-permute-done.32 = f32[2,12,8]{1,2,0:T(8,128)S(1)} collective-permute-done((f32[2,12,8]{1,2,0:T(8,128)S(1)}, f32[2,12,8]{1,2,0:T(8,128)S(1)}, u32[]{:S(2)}, u32[]{:S(2)}) %collective-permute-start.32) | collective-permute-done | bytes 800 | tf_op jit(solution)/shard_map/ppermute | solution.py:345
  (83 shorter events, 13.4 us)
Async XLA Ops:
  4.1 11.3 %collective-permute-start.2 = (bf16[48,2560]{1,0:T(8,128)(2,1)S(1)}, bf16[48,2560]{1,0:T(8,128)(2,1)S(1)}, u32[]{:S(2)}, u32[]{:S(2)}) collective-permute-start(bf16[48,2560]{1,0:T(8,128)(2,1)S(1)} %get-tuple-element.38.after_ref.mine_ref), channel_id=1, source_target_pairs={{0,4},{12,8},{1,5},{13,9},{2,6},{14,10},{3,7},{15,11},{16,20},{28,... | collective-permute-start | bytes 737288 | tf_op jit(solution)/shard_map/ppermute | solution.py:289
  12.5 56.3 %collective-permute-start = (bf16[320,2560]{1,0:T(8,128)(2,1)S(1)}, bf16[320,2560]{1,0:T(8,128)(2,1)S(1)}, u32[]{:S(2)}, u32[]{:S(2)}) collective-permute-start(bf16[320,2560]{1,0:T(8,128)(2,1)S(1)} %get-tuple-element.41), channel_id=1, source_target_pairs={{0,16},{16,0},{1,17},{17,1},{2,18},{18,2},{3,19},{19,3},{4,20},{20... | collective-permute-start | bytes 4915208 | tf_op jit(solution)/shard_map/ppermute | solution.py:300
  14.1 8.1 %collective-permute-start.1 = (bf16[48,2560]{1,0:T(8,128)(2,1)S(1)}, bf16[48,2560]{1,0:T(8,128)(2,1)S(1)}, u32[]{:S(2)}, u32[]{:S(2)}) collective-permute-start(bf16[48,2560]{1,0:T(8,128)(2,1)S(1)} %get-tuple-element.44.mine_ref), channel_id=1, source_target_pairs={{0,4},{12,8},{1,5},{13,9},{2,6},{14,10},{3,7},{15,11},{16,20},{28,... | collective-permute-start | bytes 737288 | tf_op jit(solution)/shard_map/ppermute | solution.py:289
  15.5 7.4 %collective-permute-start.4 = (bf16[48,2560]{1,0:T(8,128)(2,1)S(1)}, bf16[48,2560]{1,0:T(8,128)(2,1)S(1)}, u32[]{:S(2)}, u32[]{:S(2)}) collective-permute-start(bf16[48,2560]{1,0:T(8,128)(2,1)S(1)} %get-tuple-element.46.after_ref.mine_ref), channel_id=1, source_target_pairs={{4,8},{8,4},{5,9},{9,5},{6,10},{10,6},{7,11},{11,7},{20,24},{24,20... | collective-permute-start | bytes 737288 | tf_op jit(solution)/shard_map/ppermute | solution.py:291
  16.2 14.0 %collective-permute-start.7 = (bf16[48,2560]{1,0:T(8,128)(2,1)S(1)}, bf16[48,2560]{1,0:T(8,128)(2,1)S(1)}, u32[]{:S(2)}, u32[]{:S(2)}) collective-permute-start(bf16[48,2560]{1,0:T(8,128)(2,1)S(1)} %get-tuple-element.49), channel_id=1, source_target_pairs={{0,4},{12,8},{1,5},{13,9},{2,6},{14,10},{3,7},{15,11},{16,20},{28,... | collective-permute-start | bytes 737288 | tf_op jit(solution)/shard_map/ppermute | solution.py:289
  22.3 8.6 %collective-permute-start.6 = (bf16[48,2560]{1,0:T(8,128)(2,1)S(1)}, bf16[48,2560]{1,0:T(8,128)(2,1)S(1)}, u32[]{:S(2)}, u32[]{:S(2)}) collective-permute-start(bf16[48,2560]{1,0:T(8,128)(2,1)S(1)} %get-tuple-element.48.after_ref.mine_ref), channel_id=1, source_target_pairs={{4,8},{8,4},{5,9},{9,5},{6,10},{10,6},{7,11},{11,7},{20,24},{24,20... | collective-permute-start | bytes 737288 | tf_op jit(solution)/shard_map/ppermute | solution.py:291
  23.0 9.3 %collective-permute-start.5 = (bf16[48,2560]{1,0:T(8,128)(2,1)S(1)}, bf16[48,2560]{1,0:T(8,128)(2,1)S(1)}, u32[]{:S(2)}, u32[]{:S(2)}) collective-permute-start(bf16[48,2560]{1,0:T(8,128)(2,1)S(1)} %shard_map.118.after_ref.mine_ref), channel_id=1, source_target_pairs={{4,0},{8,12},{5,1},{9,13},{6,2},{10,14},{7,3},{11,15},{20,16},{24,... | collective-permute-start | bytes 737288 | tf_op jit(solution)/shard_map/ppermute | solution.py:292
  24.3 12.6 %collective-permute-start.3 = (bf16[48,2560]{1,0:T(8,128)(2,1)S(1)}, bf16[48,2560]{1,0:T(8,128)(2,1)S(1)}, u32[]{:S(2)}, u32[]{:S(2)}) collective-permute-start(bf16[48,2560]{1,0:T(8,128)(2,1)S(1)} %get-tuple-element.47), channel_id=1, source_target_pairs={{0,4},{12,8},{1,5},{13,9},{2,6},{14,10},{3,7},{15,11},{16,20},{28,... | collective-permute-start | bytes 737288 | tf_op jit(solution)/shard_map/ppermute | solution.py:289
  30.2 7.5 %collective-permute-start.9 = (bf16[48,2560]{1,0:T(8,128)(2,1)S(1)}, bf16[48,2560]{1,0:T(8,128)(2,1)S(1)}, u32[]{:S(2)}, u32[]{:S(2)}) collective-permute-start(bf16[48,2560]{1,0:T(8,128)(2,1)S(1)} %get-tuple-element.51.after_ref.mine_ref), channel_id=1, source_target_pairs={{4,8},{8,4},{5,9},{9,5},{6,10},{10,6},{7,11},{11,7},{20,24},{24,20... | collective-permute-start | bytes 737288 | tf_op jit(solution)/shard_map/ppermute | solution.py:291
  31.0 8.1 %collective-permute-start.13 = (bf16[48,2560]{1,0:T(8,128)(2,1)S(1)}, bf16[48,2560]{1,0:T(8,128)(2,1)S(1)}, u32[]{:S(2)}, u32[]{:S(2)}) collective-permute-start(bf16[48,2560]{1,0:T(8,128)(2,1)S(1)} %shard_map.120.after_ref.mine_ref), channel_id=1, source_target_pairs={{4,0},{8,12},{5,1},{9,13},{6,2},{10,14},{7,3},{11,15},{20,16},{24,... | collective-permute-start | bytes 737288 | tf_op jit(solution)/shard_map/ppermute | solution.py:292
  32.4 11.3 %collective-permute-start.12 = (bf16[48,2560]{1,0:T(8,128)(2,1)S(1)}, bf16[48,2560]{1,0:T(8,128)(2,1)S(1)}, u32[]{:S(2)}, u32[]{:S(2)}) collective-permute-start(bf16[48,2560]{1,0:T(8,128)(2,1)S(1)} %get-tuple-element.54), channel_id=1, source_target_pairs={{0,4},{12,8},{1,5},{13,9},{2,6},{14,10},{3,7},{15,11},{16,20},{28,... | collective-permute-start | bytes 737288 | tf_op jit(solution)/shard_map/ppermute | solution.py:289
  37.0 7.5 %collective-permute-start.11 = (bf16[48,2560]{1,0:T(8,128)(2,1)S(1)}, bf16[48,2560]{1,0:T(8,128)(2,1)S(1)}, u32[]{:S(2)}, u32[]{:S(2)}) collective-permute-start(bf16[48,2560]{1,0:T(8,128)(2,1)S(1)} %get-tuple-element.53.after_ref.mine_ref), channel_id=1, source_target_pairs={{4,8},{8,4},{5,9},{9,5},{6,10},{10,6},{7,11},{11,7},{20,24},{24,20... | collective-permute-start | bytes 737288 | tf_op jit(solution)/shard_map/ppermute | solution.py:291
  37.8 8.3 %collective-permute-start.10 = (bf16[48,2560]{1,0:T(8,128)(2,1)S(1)}, bf16[48,2560]{1,0:T(8,128)(2,1)S(1)}, u32[]{:S(2)}, u32[]{:S(2)}) collective-permute-start(bf16[48,2560]{1,0:T(8,128)(2,1)S(1)} %shard_map.123.after_ref.mine_ref), channel_id=1, source_target_pairs={{4,0},{8,12},{5,1},{9,13},{6,2},{10,14},{7,3},{11,15},{20,16},{24,... | collective-permute-start | bytes 737288 | tf_op jit(solution)/shard_map/ppermute | solution.py:292
  39.1 11.4 %collective-permute-start.8 = (bf16[48,2560]{1,0:T(8,128)(2,1)S(1)}, bf16[48,2560]{1,0:T(8,128)(2,1)S(1)}, u32[]{:S(2)}, u32[]{:S(2)}) collective-permute-start(bf16[48,2560]{1,0:T(8,128)(2,1)S(1)} %get-tuple-element.52), channel_id=1, source_target_pairs={{0,4},{12,8},{1,5},{13,9},{2,6},{14,10},{3,7},{15,11},{16,20},{28,... | collective-permute-start | bytes 737288 | tf_op jit(solution)/shard_map/ppermute | solution.py:289
  43.8 7.5 %collective-permute-start.17 = (bf16[48,2560]{1,0:T(8,128)(2,1)S(1)}, bf16[48,2560]{1,0:T(8,128)(2,1)S(1)}, u32[]{:S(2)}, u32[]{:S(2)}) collective-permute-start(bf16[48,2560]{1,0:T(8,128)(2,1)S(1)} %get-tuple-element.56.after_ref.mine_ref), channel_id=1, source_target_pairs={{4,8},{8,4},{5,9},{9,5},{6,10},{10,6},{7,11},{11,7},{20,24},{24,20... | collective-permute-start | bytes 737288 | tf_op jit(solution)/shard_map/ppermute | solution.py:291
  44.6 8.9 %collective-permute-start.16 = (bf16[48,2560]{1,0:T(8,128)(2,1)S(1)}, bf16[48,2560]{1,0:T(8,128)(2,1)S(1)}, u32[]{:S(2)}, u32[]{:S(2)}) collective-permute-start(bf16[48,2560]{1,0:T(8,128)(2,1)S(1)} %shard_map.126.after_ref.mine_ref), channel_id=1, source_target_pairs={{4,0},{8,12},{5,1},{9,13},{6,2},{10,14},{7,3},{11,15},{20,16},{24,... | collective-permute-start | bytes 737288 | tf_op jit(solution)/shard_map/ppermute | solution.py:292
  46.1 11.2 %collective-permute-start.15 = (bf16[48,2560]{1,0:T(8,128)(2,1)S(1)}, bf16[48,2560]{1,0:T(8,128)(2,1)S(1)}, u32[]{:S(2)}, u32[]{:S(2)}) collective-permute-start(bf16[48,2560]{1,0:T(8,128)(2,1)S(1)} %get-tuple-element.58), channel_id=1, source_target_pairs={{0,4},{12,8},{1,5},{13,9},{2,6},{14,10},{3,7},{15,11},{16,20},{28,... | collective-permute-start | bytes 737288 | tf_op jit(solution)/shard_map/ppermute | solution.py:289
  50.6 7.5 %collective-permute-start.14 = (bf16[48,2560]{1,0:T(8,128)(2,1)S(1)}, bf16[48,2560]{1,0:T(8,128)(2,1)S(1)}, u32[]{:S(2)}, u32[]{:S(2)}) collective-permute-start(bf16[48,2560]{1,0:T(8,128)(2,1)S(1)} %get-tuple-element.57.after_ref.mine_ref), channel_id=1, source_target_pairs={{4,8},{8,4},{5,9},{9,5},{6,10},{10,6},{7,11},{11,7},{20,24},{24,20... | collective-permute-start | bytes 737288 | tf_op jit(solution)/shard_map/ppermute | solution.py:291
  51.3 9.5 %collective-permute-start.21 = (bf16[48,2560]{1,0:T(8,128)(2,1)S(1)}, bf16[48,2560]{1,0:T(8,128)(2,1)S(1)}, u32[]{:S(2)}, u32[]{:S(2)}) collective-permute-start(bf16[48,2560]{1,0:T(8,128)(2,1)S(1)} %shard_map.129.after_ref.mine_ref), channel_id=1, source_target_pairs={{4,0},{8,12},{5,1},{9,13},{6,2},{10,14},{7,3},{11,15},{20,16},{24,... | collective-permute-start | bytes 737288 | tf_op jit(solution)/shard_map/ppermute | solution.py:292
  53.4 7.5 %collective-permute-start.20 = (bf16[48,2560]{1,0:T(8,128)(2,1)S(1)}, bf16[48,2560]{1,0:T(8,128)(2,1)S(1)}, u32[]{:S(2)}, u32[]{:S(2)}) collective-permute-start(bf16[48,2560]{1,0:T(8,128)(2,1)S(1)} %get-tuple-element.59), channel_id=1, source_target_pairs={{0,4},{12,8},{1,5},{13,9},{2,6},{14,10},{3,7},{15,11},{16,20},{28,... | collective-permute-start | bytes 737288 | tf_op jit(solution)/shard_map/ppermute | solution.py:289
  57.3 4.3 %collective-permute-start.19 = (bf16[48,2560]{1,0:T(8,128)(2,1)S(1)}, bf16[48,2560]{1,0:T(8,128)(2,1)S(1)}, u32[]{:S(2)}, u32[]{:S(2)}) collective-permute-start(bf16[48,2560]{1,0:T(8,128)(2,1)S(1)} %shard_map.131.after_ref.mine_ref), channel_id=1, source_target_pairs={{4,8},{8,4},{5,9},{9,5},{6,10},{10,6},{7,11},{11,7},{20,24},{24,20... | collective-permute-start | bytes 737288 | tf_op jit(solution)/shard_map/ppermute | solution.py:291
  58.1 10.7 %collective-permute-start.18 = (bf16[48,2560]{1,0:T(8,128)(2,1)S(1)}, bf16[48,2560]{1,0:T(8,128)(2,1)S(1)}, u32[]{:S(2)}, u32[]{:S(2)}) collective-permute-start(bf16[48,2560]{1,0:T(8,128)(2,1)S(1)} %shard_map.132.after_ref.mine_ref), channel_id=1, source_target_pairs={{4,0},{8,12},{5,1},{9,13},{6,2},{10,14},{7,3},{11,15},{20,16},{24,... | collective-permute-start | bytes 737288 | tf_op jit(solution)/shard_map/ppermute | solution.py:292
  61.0 11.2 %collective-permute-start.22 = (bf16[48,2560]{1,0:T(8,128)(2,1)S(1)}, bf16[48,2560]{1,0:T(8,128)(2,1)S(1)}, u32[]{:S(2)}, u32[]{:S(2)}) collective-permute-start(bf16[48,2560]{1,0:T(8,128)(2,1)S(1)} %shard_map.134.after_ref.mine_ref), channel_id=1, source_target_pairs={{4,8},{8,4},{5,9},{9,5},{6,10},{10,6},{7,11},{11,7},{20,24},{24,20... | collective-permute-start | bytes 737288 | tf_op jit(solution)/shard_map/ppermute | solution.py:291
  61.7 14.2 %collective-permute-start.24 = (bf16[48,2560]{1,0:T(8,128)(2,1)S(1)}, bf16[48,2560]{1,0:T(8,128)(2,1)S(1)}, u32[]{:S(2)}, u32[]{:S(2)}) collective-permute-start(bf16[48,2560]{1,0:T(8,128)(2,1)S(1)} %shard_map.135.after_ref.mine_ref), channel_id=1, source_target_pairs={{4,0},{8,12},{5,1},{9,13},{6,2},{10,14},{7,3},{11,15},{20,16},{24,... | collective-permute-start | bytes 737288 | tf_op jit(solution)/shard_map/ppermute | solution.py:292
  72.2 8.1 %collective-permute-start.23 = (bf16[48,2560]{1,0:T(8,128)(2,1)S(1)}, bf16[48,2560]{1,0:T(8,128)(2,1)S(1)}, u32[]{:S(2)}, u32[]{:S(2)}) collective-permute-start(bf16[48,2560]{1,0:T(8,128)(2,1)S(1)} %shard_map.140.after_ref.mine_ref), channel_id=1, source_target_pairs={{4,0},{8,12},{5,1},{9,13},{6,2},{10,14},{7,3},{11,15},{20,16},{24,... | collective-permute-start | bytes 737288 | tf_op jit(solution)/shard_map/ppermute | solution.py:292
  73.5 8.3 %collective-permute-start.27 = (bf16[96,320]{1,0:T(8,128)(2,1)S(1)}, bf16[96,320]{1,0:T(8,128)(2,1)S(1)}, u32[]{:S(2)}, u32[]{:S(2)}) collective-permute-start(bf16[96,320]{1,0:T(8,128)(2,1)S(1)} %get-tuple-element.66), channel_id=1, source_target_pairs={{0,16},{16,0},{1,17},{17,1},{2,18},{18,2},{3,19},{19,3},{4,20},{20... | collective-permute-start | bytes 184328 | tf_op jit(solution)/shard_map/ppermute | solution.py:322
  73.9 8.0 %collective-permute-start.26 = (bf16[96,320]{1,0:T(8,128)(2,1)S(1)}, bf16[96,320]{1,0:T(8,128)(2,1)S(1)}, u32[]{:S(2)}, u32[]{:S(2)}) collective-permute-start(bf16[96,320]{1,0:T(8,128)(2,1)S(1)} %get-tuple-element.65), channel_id=1, source_target_pairs={{0,16},{16,0},{1,17},{17,1},{2,18},{18,2},{3,19},{19,3},{4,20},{20... | collective-permute-start | bytes 184328 | tf_op jit(solution)/shard_map/ppermute | solution.py:322
  75.6 6.2 %collective-permute-start.25 = (bf16[96,320]{1,0:T(8,128)(2,1)S(1)}, bf16[96,320]{1,0:T(8,128)(2,1)S(1)}, u32[]{:S(2)}, u32[]{:S(2)}) collective-permute-start(bf16[96,320]{1,0:T(8,128)(2,1)S(1)} %get-tuple-element.64), channel_id=1, source_target_pairs={{0,16},{16,0},{1,17},{17,1},{2,18},{18,2},{3,19},{19,3},{4,20},{20... | collective-permute-start | bytes 184328 | tf_op jit(solution)/shard_map/ppermute | solution.py:322
  81.5 4.4 %collective-permute-start.28 = (bf16[96,320]{1,0:T(8,128)(2,1)S(1)}, bf16[96,320]{1,0:T(8,128)(2,1)S(1)}, u32[]{:S(2)}, u32[]{:S(2)}) collective-permute-start(bf16[96,320]{1,0:T(8,128)(2,1)S(1)} %get-tuple-element.67), channel_id=1, source_target_pairs={{0,16},{16,0},{1,17},{17,1},{2,18},{18,2},{3,19},{19,3},{4,20},{20... | collective-permute-start | bytes 184328 | tf_op jit(solution)/shard_map/ppermute | solution.py:322
  87.3 3.8 %collective-permute-start.30 = (f32[12,320]{1,0:T(8,128)S(1)}, f32[12,320]{1,0:T(8,128)S(1)}, u32[]{:S(2)}, u32[]{:S(2)}) collective-permute-start(f32[12,320]{1,0:T(8,128)S(1)} %add.9.one_ref), channel_id=1, source_target_pairs={{0,2},{1,3},{2,0},{3,1},{4,6},{5,7},{6,4},{7,5},{8,10},{9,11},{10,... | collective-permute-start | bytes 46088 | tf_op jit(solution)/shard_map/ppermute | solution.py:331
  92.3 3.6 %collective-permute-start.31 = (f32[1,12,8]{1,2,0:T(8,128)S(1)}, f32[1,12,8]{1,2,0:T(8,128)S(1)}, u32[]{:S(2)}, u32[]{:S(2)}) collective-permute-start(f32[1,12,8]{1,2,0:T(8,128)S(1)} %bitcast.15), channel_id=1, source_target_pairs={{0,4},{4,0},{8,12},{12,8},{1,5},{5,1},{9,13},{13,9},{2,6},{6,2},{1... | collective-permute-start | bytes 1160 | tf_op jit(solution)/shard_map/ppermute | solution.py:345
  96.0 4.5 %collective-permute-start.32 = (f32[2,12,8]{1,2,0:T(8,128)S(1)}, f32[2,12,8]{1,2,0:T(8,128)S(1)}, u32[]{:S(2)}, u32[]{:S(2)}) collective-permute-start(f32[2,12,8]{1,2,0:T(8,128)S(1)} %pad_maximum_fusion.1), channel_id=1, source_target_pairs={{0,8},{4,12},{8,0},{12,4},{1,9},{5,13},{9,1},{13,5},{2,10},{6,14},... | collective-permute-start | bytes 2312 | tf_op jit(solution)/shard_map/ppermute | solution.py:345
  (5 other events, 58.8 us)

commit v6 on v0

v6 whole, which is shorter than its diff:
```python
import functools

import jax
import jax.numpy as jnp
from jax import lax
from jax.experimental import pallas as pl
from jax.experimental.pallas import tpu as pltpu
from jax.sharding import PartitionSpec as P

RANK = 32
NT = (((1,), (1,)), ((), ()))


VMEM = pl.BlockSpec(memory_space=pltpu.VMEM)
HBM = pl.BlockSpec(memory_space=pltpu.HBM)
ANY = pl.BlockSpec(memory_space=pl.ANY)
MIB = 1024 * 1024
LANES = 128


def in_hbm(*arrays):
    return [pltpu.with_memory_space_constraint(array, pltpu.HBM) for array in arrays]


def bf16(*shape):
    return jax.ShapeDtypeStruct(shape, jnp.bfloat16)


def pull_kernel(chunks, acts_ref, grads_ref, basis_in_ref, basis_out_ref, query_in_ref, query_out_ref, *rest):
    outs, (tokens_ref, theirs_ref, basis, query, turned, sems) = rest[:chunks], rest[chunks:]
    rows = outs[0].shape[0]
    features = basis.shape[0]
    block = 512 if features % 512 == 0 else features
    spans = [pl.ds(first, block) for first in range(0, features, block)]

    def copies(mine, theirs, from_basis, from_query):
        pairs = [(from_query, query)]
        pairs += [(from_basis.at[span], basis.at[span]) for span in spans]
        pairs += [(mine, tokens_ref), (theirs, theirs_ref)]
        return [pltpu.make_async_copy(source, target, sems.at[i]) for i, (source, target) in enumerate(pairs)]

    side = lax.axis_index("parts")

    @pl.when(side == 0)
    def _():
        for copy in copies(acts_ref, grads_ref, basis_in_ref, query_in_ref):
            copy.start()

    @pl.when(side != 0)
    def _():
        for copy in copies(grads_ref, acts_ref, basis_out_ref, query_out_ref):
            copy.start()

    landed = copies(acts_ref, grads_ref, basis_in_ref, query_in_ref)
    landed[0].wait()
    turned[...] = query[...].T
    for copy, span in zip(landed[1:], spans):
        copy.wait()
        pulled = lax.dot_general(turned[...], basis[span], NT, preferred_element_type=jnp.float32)
        pulled = pulled.astype(jnp.bfloat16)
        for c, out in enumerate(outs):
            out[:, span] = pulled[c * rows : (c + 1) * rows]
    for copy in landed[1 + len(spans) :]:
        copy.wait()


def pull(acts, grads, basis_in, basis_out, query_in, query_out, rows):
    features, depth = basis_in.shape
    spread = query_in.shape[1]
    chunks = spread // rows
    blocks = features // 512 if features % 512 == 0 else 1
    out = pl.pallas_call(
        functools.partial(pull_kernel, chunks),
        out_shape=[bf16(rows, features)] * chunks + [bf16(*acts.shape)] * 2,
        in_specs=[HBM] * 6,
        out_specs=[VMEM] * (chunks + 2),
        scratch_shapes=[
            pltpu.VMEM((features, depth), jnp.bfloat16),
            pltpu.VMEM((depth, spread), jnp.bfloat16),
            pltpu.VMEM((spread, depth), jnp.bfloat16),
            pltpu.SemaphoreType.DMA((blocks + 3,)),
        ],
        compiler_params=pltpu.CompilerParams(vmem_limit_bytes=24 * MIB),
    )(*in_hbm(acts, grads, basis_in, basis_out, query_in, query_out))
    return list(out[:chunks]), out[-2], out[-1]


def at_depth(hop):
    z = lax.axis_index("dp")
    return jnp.minimum(z, lax.axis_size("dp") - 1 - z) == hop


def write_send(later_ref, value_ref, send_ref):
    @pl.when(at_depth(0))
    def _():
        send_ref[...] = later_ref[...]

    @pl.when(jnp.logical_not(at_depth(0)))
    def _():
        send_ref[...] = value_ref[...]


def total_kernel(shared, mine_ref, came_ref, after_ref, *rest):
    mine = mine_ref[...].astype(jnp.float32) + came_ref[...].astype(jnp.float32)
    rest[-1][...] = mine.astype(jnp.bfloat16)
    if shared:
        write_send(rest[0], rest[2], rest[1])
    elif len(rest) == 3:
        rest[1][...] = rest[0][...]


def total(after, mine, came, later=None, shared=False):
    extra = [] if later is None else [later]
    out = pl.pallas_call(
        functools.partial(total_kernel, shared),
        out_shape=[bf16(*a.shape) for a in extra + [mine]],
        in_specs=[VMEM, VMEM, ANY] + [VMEM] * len(extra),
        out_specs=[VMEM] * (1 + len(extra)),
        compiler_params=pltpu.CompilerParams(vmem_limit_bytes=8 * MIB),
    )(mine, came, after, *extra)
    return out[-1], (out[0] if extra else None)


def take_kernel(hop, shared, mine_ref, came_ref, after_ref, *rest):
    @pl.when(at_depth(hop))
    def _():
        rest[-1][...] = came_ref[...]

    @pl.when(jnp.logical_not(at_depth(hop)))
    def _():
        rest[-1][...] = mine_ref[...]

    if shared:
        write_send(rest[0], rest[2], rest[1])


def take(after, hop, mine, came, later=None):
    extra = [] if later is None else [later]
    out = pl.pallas_call(
        functools.partial(take_kernel, hop, later is not None),
        out_shape=[bf16(*a.shape) for a in extra + [mine]],
        in_specs=[VMEM, VMEM, ANY] + [VMEM] * len(extra),
        out_specs=[VMEM] * (1 + len(extra)),
        compiler_params=pltpu.CompilerParams(vmem_limit_bytes=8 * MIB),
    )(mine, came, after, *extra)
    return out[-1], (out[0] if extra else None)


def project_kernel(tokens_ref, after_ref, *rest):
    factors = jnp.concatenate([ref[...] for ref in rest[:-1]], axis=0)
    projected = lax.dot_general(factors, tokens_ref[...], NT, preferred_element_type=jnp.float32)
    rest[-1][...] = projected.astype(rest[-1].dtype)


def project(after, factors, tokens, dtype):
    rows = sum(chunk.shape[0] for chunk in factors)
    return pl.pallas_call(
        project_kernel,
        out_shape=jax.ShapeDtypeStruct((rows, tokens.shape[0]), dtype),
        in_specs=[VMEM, ANY] + [VMEM] * len(factors),
        out_specs=VMEM,
        compiler_params=pltpu.CompilerParams(vmem_limit_bytes=16 * MIB),
    )(tokens, after, *factors)


def score_kernel(count, counts_ref, *refs):
    out_ref = refs[-1]
    own = jnp.concatenate([ref[...] for ref in refs[:count]], axis=0)
    other = jnp.concatenate([ref[...] for ref in refs[count : 2 * count]], axis=0)
    product = own * other.astype(jnp.float32)
    queries, tokens = product.shape[0] // RANK, product.shape[1]
    scores = jnp.sum(product.reshape(queries, RANK, tokens), axis=1) * RANK ** (-0.5)
    out_ref[:, :tokens] = scores
    position = lax.broadcasted_iota(jnp.int32, scores.shape, 1)
    column = lax.broadcasted_iota(jnp.int32, (queries, LANES), 1)
    pooled = jnp.zeros((queries, LANES), jnp.float32)
    start = jnp.int32(0)
    for k in range(counts_ref.shape[1]):
        count = counts_ref[0, k]
        inside = (position >= start) & (position < start + count)
        found = jnp.sum(jnp.where(inside, scores, 0.0), axis=1, keepdims=True)
        root = jnp.sqrt(jnp.full((1, 1), count, jnp.int32).astype(jnp.float32))
        pooled = jnp.where(column == k, found / root, pooled)
        start = start + count
    out_ref[:, out_ref.shape[1] - LANES :] = pooled


def score(counts, own, other):
    rows = sum(piece.shape[0] for piece in own)
    tokens = own[0].shape[1]
    width = (tokens + LANES - 1) // LANES * LANES + LANES
    return pl.pallas_call(
        functools.partial(score_kernel, len(own)),
        out_shape=jax.ShapeDtypeStruct((rows // RANK, width), jnp.float32),
        in_specs=[pl.BlockSpec(memory_space=pltpu.SMEM)] + [VMEM] * (2 * len(own)),
        out_specs=VMEM,
        compiler_params=pltpu.CompilerParams(vmem_limit_bytes=16 * MIB),
    )(counts, *own, *other)


def chunk_rows(spread):
    return spread // 8 if spread % 128 == 0 else RANK


def is_power(number):
    return number & (number - 1) == 0


def per_device(
    acts,
    grads,
    basis_in,
    output_eigen_basis,
    query_in,
    query_out,
    doc_counts,
    pair_query,
    pair_device,
    pair_doc,
):
    n = lax.axis_size("dp")
    layers = lax.axis_size("layer")
    z = lax.axis_index("dp")
    spread = query_in.shape[2]
    queries = spread // RANK
    half = n // 2
    rows = chunk_rows(spread)
    chunks = spread // rows

    own, tokens, theirs = pull(
        acts[0], grads[0], basis_in[0], output_eigen_basis[0], query_in[0], query_out[0], rows
    )
    swap = [(0, 1), (1, 0)]

    stages = [("in", hop) for hop in range(half - 1)] + [("mid", 0)]
    stages += [("out", hop) for hop in range(half - 2, -1, -1)]
    last = len(stages) - 1

    def transfer(kinds, hop, value):
        pairs = []
        if "in" in kinds:
            pairs += [(hop, hop + 1), (n - 1 - hop, n - 2 - hop)]
        if "mid" in kinds:
            pairs += [(half - 1, half), (half, half - 1)]
        if "out" in kinds:
            pairs += [(hop + 1, hop), (n - 2 - hop, n - 1 - hop)]
        return lax.ppermute(value, "dp", pairs)

    part, came = list(own), [None] * chunks
    ahead = min(2, chunks)
    for c in range(ahead):
        came[c] = transfer(stages[0][:1], stages[0][1], part[c])
    others = lax.ppermute(theirs, "parts", swap)
    after = own[0]
    waiting, mine, back = [], [], []

    def project_waiting(after):
        away = project(after, waiting, others, jnp.bfloat16)
        back.append(lax.ppermute(away, "parts", swap))
        mine.append(project(away, waiting, tokens, jnp.float32))
        waiting.clear()
        return mine[-1]

    for turn in range(chunks + last):
        for s, (kind, hop) in enumerate(stages):
            c = turn - s
            if not 0 <= c < chunks:
                continue
            later = turn + ahead if turn + ahead < chunks else None
            if turn >= last - 1:
                use = later if s == last - 1 else None
            else:
                use = later if s == 0 else None
            shared = use is not None and turn >= last - 1
            chunk = None if use is None else own[use]
            if kind == "out":
                part[c], send = take(after, hop, part[c], came[c], chunk)
            else:
                part[c], send = total(after, part[c], came[c], chunk, shared)
            after = part[c]
            if shared:
                came[c] = came[use] = transfer(("in", "out"), 0, send)
                continue
            if use is not None:
                came[use] = transfer(stages[0][:1], stages[0][1], send)
            if s < last:
                came[c] = transfer(stages[s + 1][:1], stages[s + 1][1], part[c])
            else:
                waiting.append(part[c])
        if turn >= chunks - 1 and waiting:
            after = project_waiting(after)

    scores = score(doc_counts, mine, back)
    if not is_power(layers):
        scores = lax.psum(scores, "layer")
    steps = [1 << k for k in range(layers.bit_length() - 1)] if is_power(layers) else []

    def add_other(value, step):
        return value + lax.ppermute(value, "layer", [(i, i ^ step) for i in range(layers)])

    if steps:
        scores = add_other(scores, steps[0])
    token_scores, pooled = scores[:, : acts.shape[1]], scores[:, -LANES:]
    for step in steps[1:]:
        token_scores = add_other(token_scores, step)

    docs = doc_counts.shape[1]
    cells = queries * docs
    flat = pooled[:, :docs].reshape(1, cells)
    target = pair_device[:, 0]
    cell = pair_query * docs + pair_doc
    if n <= 8 and is_power(n):
        table = jnp.concatenate(
            [flat] + [lax.ppermute(flat, "dp", [(i, i ^ k) for i in range(n)]) for k in range(1, n)], axis=1
        )
        column = (z ^ target) * cells + cell
    else:
        table = lax.all_gather(flat, "dp", axis=1, tiled=True)
        column = target * cells + cell
    for step in steps[1:]:
        table = add_other(table, step)
    hit = column[:, None] == jnp.arange(n * cells, dtype=jnp.int32)[None, :]
    pair_scores = jnp.sum(jnp.where(hit, table, 0.0), axis=1)
    return (token_scores, pair_scores)


def solution(mesh):
    in_specs = (
        P("layer", ("parts", "dp"), None),
        P("layer", ("parts", "dp"), None),
        P("layer", None, "dp"),
        P("layer", None, "dp"),
        P("layer", "dp", None),
        P("layer", "dp", None),
        P(("parts", "dp"), None),
        P(("parts", "dp")),
        P(("parts", "dp"), None),
        P(("parts", "dp")),
    )
    out_specs = (P(None, ("parts", "dp")), P(("parts", "dp")))
    return jax.shard_map(
        per_device, mesh=mesh, in_specs=in_specs, out_specs=out_specs, check_vma=False
    )
```

time: 205 us -> 96.9 us (0.47)
  waiting for transfers between devices: 96.1 us -> 27.8 us
  local copies, waits for them, and re-layouts: 48.8 us -> 0.12 us
  starting transfers between devices: 11.4 us -> 55.9 us
  blocking collectives: 19.4 us -> 0 us
  between operations: 14.1 us -> 1.14 us
  Pallas kernels: 0 us -> 9.99 us
  matrix products: 9.88 us -> 0 us
  other arithmetic: 3.93 us -> 1.49 us
    psum x1 -> x0, waiting for transfers between devices: 90.5 us -> none  [per_device(): gathered_rows = lax.psum(partial_value.astype(jnp.bfloat16), 'dp')]
    ppermute x0 -> x29, starting transfers between devices: none -> 55.9 us  [the longest x19 44.6 us: transfer(): return lax.ppermute(value, 'dp', pairs)]
    scatter x2 -> x0, local copies, waits for them, and re-layouts: 39.3 us -> none  [the longest x1 19.7 us: per_device(): jnp.zeros((n_data, capacity), jnp.int32).at[target, slot].set(pair_query)]
    ppermute x0 -> x29, waiting for transfers between devices: none -> 27.8 us  [the longest x19 18.5 us: transfer(): return lax.ppermute(value, 'dp', pairs)]
    all_to_all x2 -> x0, starting transfers between devices: 11.4 us -> none  [the longest x1 6.32 us: per_device(): lax.all_to_all(send_query, 'dp', split_axis=0, concat_axis=0, tiled=True)]
    psum x1 -> x0, blocking collectives: 11.4 us -> none  [per_device(): token_scores = lax.psum(layer_scores, 'layer')]
    pallas_call x0 -> x32, Pallas kernels: none -> 9.99 us  [the longest x6 4.2 us: project(): pl.pallas_call(project_kernel, out_shape=jax.ShapeDtypeStruct((rows, toke...]
    dot_general x5 -> x0, matrix products: 9.88 us -> none  [the longest x1 3.19 us: per_device(): jnp.dot(right, gathered_rows[:, spread:], preferred_element_type=jnp.floa...]
  transfers between devices with their start and end apart: 3 -> 29, of which waited for: 2 -> 13; matrix products, arithmetic and copies ran while one was open for 20% -> 1% of each run, Pallas kernels for 0% -> 6%
where the time goes in v6:
time: 96.9 us; the launch traced here: 96.5 us
  starting transfers between devices  55.9 us (58%)
  waiting for transfers between devices  27.8 us (29%)
  Pallas kernels  9.99 us (10%)
  other arithmetic  1.49 us (2%)
  between operations  1.14 us (1%)
    ppermute x19, starting transfers between devices, transfer(): return lax.ppermute(value, 'dp', pairs)  44.6 us
    ppermute x19, waiting for transfers between devices, transfer(): return lax.ppermute(value, 'dp', pairs)  18.5 us
    ppermute x3, starting transfers between devices, per_device(): lax.ppermute(flat, 'dp', [(i, i ^ k) for i in range(n)])  4.44 us
    pallas_call x6, Pallas kernels, project(): pl.pallas_call(project_kernel, out_shape=jax.ShapeDtypeStruct((rows, toke...  4.2 us
    pallas_call x1, Pallas kernels, pull(): pl.pallas_call(functools.partial(pull_kernel, chunks), out_shape=[bf16(ro...  3.84 us
    ppermute x3, waiting for transfers between devices, add_other(): lax.ppermute(value, 'layer', [(i, i ^ step) for i in range(layers)])  3.77 us
    ppermute x1, starting transfers between devices, per_device(): others = lax.ppermute(theirs, 'parts', swap)  3.05 us
    ppermute x3, waiting for transfers between devices, project_waiting(): back.append(lax.ppermute(away, 'parts', swap))  2.86 us
  transfers between devices with their start and end apart: 29, of which 13 were waited for; matrix products, arithmetic and copies ran while one was open for 1% of the time, Pallas kernels for 6%

profile of v6, /device:TPU:0, one launch (start us, length us, event | category | flops | bytes accessed | tf_op | source)
XLA Modules:
  0.0 96.5 jit_solution(14858152722002079588)
XLA Ops:
  0.6 3.8 %shard_map.113 = (bf16[48,2560]{1,0:T(8,128)(2,1)S(1)}, bf16[48,2560]{1,0:T(8,128)(2,1)S(1)}, bf16[48,2560]{1,0:T(8,128)(2,1)S(1)}, bf16[48,2560]{1,0:T(8,128)(2...) custom-call(bf16[320,2560]{1,0:T(8,128)(2,1)} %bitcast.10, ...), custom_call_target="tpu_custom_call" | custom-call | tf_op jit(solution)/shard_map/pallas_call | solution.py:72
  4.5 3.0 %collective-permute-start = (bf16[320,2560]{1,0:T(8,128)(2,1)S(1)}, bf16[320,2560]{1,0:T(8,128)(2,1)S(1)}, u32[]{:S(2)}, u32[]{:S(2)}) collective-permute-start(bf16[320,2560]{1,0:T(8,128)(2,1)S(1)} %get-tuple-element.25), channel_id=1, source_target_pairs={{0,16},{16,0},{1,17},{17,1},{2,18},{18,2},{3,19},{19,3},{4,20},{20... | collective-permute-start | bytes 4915208 | tf_op jit(solution)/shard_map/ppermute | solution.py:253
  7.5 3.5 %collective-permute-start.1 = (bf16[48,2560]{1,0:T(8,128)(2,1)S(1)}, bf16[48,2560]{1,0:T(8,128)(2,1)S(1)}, u32[]{:S(2)}, u32[]{:S(2)}) collective-permute-start(bf16[48,2560]{1,0:T(8,128)(2,1)S(1)} %get-tuple-element.28.mine_ref.after_ref), channel_id=1, source_target_pairs={{0,4},{12,8},{1,5},{13,9},{2,6},{14,10},{3,7},{15,11},{16,20},{28,... | collective-permute-start | bytes 737288 | tf_op jit(solution)/shard_map/ppermute | solution.py:247
  11.0 1.3 %collective-permute-start.4 = (bf16[48,2560]{1,0:T(8,128)(2,1)S(1)}, bf16[48,2560]{1,0:T(8,128)(2,1)S(1)}, u32[]{:S(2)}, u32[]{:S(2)}) collective-permute-start(bf16[48,2560]{1,0:T(8,128)(2,1)S(1)} %get-tuple-element.31.mine_ref), channel_id=1, source_target_pairs={{0,4},{12,8},{1,5},{13,9},{2,6},{14,10},{3,7},{15,11},{16,20},{28,... | collective-permute-start | bytes 737288 | tf_op jit(solution)/shard_map/ppermute | solution.py:247
  12.3 5.1 %collective-permute-done.1.came_ref = bf16[48,2560]{1,0:T(8,128)(2,1)S(1)} collective-permute-done((bf16[48,2560]{1,0:T(8,128)(2,1)S(1)}, bf16[48,2560]{1,0:T(8,128)(2,1)S(1)}, u32[]{:S(2)}, u32[]{:S(2)}) %collective-permute-start.1) | collective-permute-done | bytes 245792 | tf_op jit(solution)/shard_map/ppermute | solution.py:247
  17.4 0.7 collective-permute-start.3
  18.1 7.2 %collective-permute-start.2 = (bf16[48,2560]{1,0:T(8,128)(2,1)S(1)}, bf16[48,2560]{1,0:T(8,128)(2,1)S(1)}, u32[]{:S(2)}, u32[]{:S(2)}) collective-permute-start(bf16[48,2560]{1,0:T(8,128)(2,1)S(1)} %get-tuple-element.29), channel_id=1, source_target_pairs={{0,4},{12,8},{1,5},{13,9},{2,6},{14,10},{3,7},{15,11},{16,20},{28,... | collective-permute-start | bytes 737288 | tf_op jit(solution)/shard_map/ppermute | solution.py:247
  26.2 3.0 %collective-permute-start.6 = (bf16[48,2560]{1,0:T(8,128)(2,1)S(1)}, bf16[48,2560]{1,0:T(8,128)(2,1)S(1)}, u32[]{:S(2)}, u32[]{:S(2)}) collective-permute-start(bf16[48,2560]{1,0:T(8,128)(2,1)S(1)} %get-tuple-element.34), channel_id=1, source_target_pairs={{0,4},{12,8},{4,0},{8,12},{1,5},{13,9},{5,1},{9,13},{2,6},{14,10},... | collective-permute-start | bytes 737288 | tf_op jit(solution)/shard_map/ppermute | solution.py:247
  29.3 1.9 %collective-permute-done.2.came_ref = bf16[48,2560]{1,0:T(8,128)(2,1)S(1)} collective-permute-done((bf16[48,2560]{1,0:T(8,128)(2,1)S(1)}, bf16[48,2560]{1,0:T(8,128)(2,1)S(1)}, u32[]{:S(2)}, u32[]{:S(2)}) %collective-permute-start.2) | collective-permute-done | bytes 245792 | tf_op jit(solution)/shard_map/ppermute | solution.py:247
  32.0 4.2 %collective-permute-start.10 = (bf16[48,2560]{1,0:T(8,128)(2,1)S(1)}, bf16[48,2560]{1,0:T(8,128)(2,1)S(1)}, u32[]{:S(2)}, u32[]{:S(2)}) collective-permute-start(bf16[48,2560]{1,0:T(8,128)(2,1)S(1)} %get-tuple-element.39), channel_id=1, source_target_pairs={{0,4},{12,8},{4,0},{8,12},{1,5},{13,9},{5,1},{9,13},{2,6},{14,10},... | collective-permute-start | bytes 737288 | tf_op jit(solution)/shard_map/ppermute | solution.py:247
  37.1 6.2 %collective-permute-start.8 = (bf16[48,2560]{1,0:T(8,128)(2,1)S(1)}, bf16[48,2560]{1,0:T(8,128)(2,1)S(1)}, u32[]{:S(2)}, u32[]{:S(2)}) collective-permute-start(bf16[48,2560]{1,0:T(8,128)(2,1)S(1)} %get-tuple-element.37), channel_id=1, source_target_pairs={{0,4},{12,8},{4,0},{8,12},{1,5},{13,9},{5,1},{9,13},{2,6},{14,10},... | collective-permute-start | bytes 737288 | tf_op jit(solution)/shard_map/ppermute | solution.py:247
  44.1 5.2 %collective-permute-start.12 = (bf16[48,2560]{1,0:T(8,128)(2,1)S(1)}, bf16[48,2560]{1,0:T(8,128)(2,1)S(1)}, u32[]{:S(2)}, u32[]{:S(2)}) collective-permute-start(bf16[48,2560]{1,0:T(8,128)(2,1)S(1)} %get-tuple-element.42), channel_id=1, source_target_pairs={{0,4},{12,8},{4,0},{8,12},{1,5},{13,9},{5,1},{9,13},{2,6},{14,10},... | collective-permute-start | bytes 737288 | tf_op jit(solution)/shard_map/ppermute | solution.py:247
  50.2 4.7 %collective-permute-start.16 = (bf16[48,2560]{1,0:T(8,128)(2,1)S(1)}, bf16[48,2560]{1,0:T(8,128)(2,1)S(1)}, u32[]{:S(2)}, u32[]{:S(2)}) collective-permute-start(bf16[48,2560]{1,0:T(8,128)(2,1)S(1)} %get-tuple-element.45), channel_id=1, source_target_pairs={{0,4},{12,8},{4,0},{8,12},{1,5},{13,9},{5,1},{9,13},{2,6},{14,10},... | collective-permute-start | bytes 737288 | tf_op jit(solution)/shard_map/ppermute | solution.py:247
  55.8 1.3 %collective-permute-start.14 = (bf16[48,2560]{1,0:T(8,128)(2,1)S(1)}, bf16[48,2560]{1,0:T(8,128)(2,1)S(1)}, u32[]{:S(2)}, u32[]{:S(2)}) collective-permute-start(bf16[48,2560]{1,0:T(8,128)(2,1)S(1)} %shard_map.130.after_ref.mine_ref), channel_id=1, source_target_pairs={{4,0},{8,12},{5,1},{9,13},{6,2},{10,14},{7,3},{11,15},{20,16},{24,... | collective-permute-start | bytes 737288 | tf_op jit(solution)/shard_map/ppermute | solution.py:247
  57.1 3.7 %collective-permute-done.16.came_ref = bf16[48,2560]{1,0:T(8,128)(2,1)S(1)} collective-permute-done((bf16[48,2560]{1,0:T(8,128)(2,1)S(1)}, bf16[48,2560]{1,0:T(8,128)(2,1)S(1)}, u32[]{:S(2)}, u32[]{:S(2)}) %collective-permute-start.16) | collective-permute-done | bytes 245792 | tf_op jit(solution)/shard_map/ppermute | solution.py:247
  61.6 1.3 %collective-permute-start.17 = (bf16[48,2560]{1,0:T(8,128)(2,1)S(1)}, bf16[48,2560]{1,0:T(8,128)(2,1)S(1)}, u32[]{:S(2)}, u32[]{:S(2)}) collective-permute-start(bf16[48,2560]{1,0:T(8,128)(2,1)S(1)} %shard_map.133.after_ref.mine_ref), channel_id=1, source_target_pairs={{4,0},{8,12},{5,1},{9,13},{6,2},{10,14},{7,3},{11,15},{20,16},{24,... | collective-permute-start | bytes 737288 | tf_op jit(solution)/shard_map/ppermute | solution.py:247
  62.9 3.3 %collective-permute-done.14.came_ref = bf16[48,2560]{1,0:T(8,128)(2,1)S(1)} collective-permute-done((bf16[48,2560]{1,0:T(8,128)(2,1)S(1)}, bf16[48,2560]{1,0:T(8,128)(2,1)S(1)}, u32[]{:S(2)}, u32[]{:S(2)}) %collective-permute-start.14) | collective-permute-done | bytes 245792 | tf_op jit(solution)/shard_map/ppermute | solution.py:247
  66.2 0.9 shard_map.135.after_ref
  67.2 0.9 shard_map.136.after_ref.refs_0_
  68.2 1.3 %collective-permute-start.19 = (bf16[48,2560]{1,0:T(8,128)(2,1)S(1)}, bf16[48,2560]{1,0:T(8,128)(2,1)S(1)}, u32[]{:S(2)}, u32[]{:S(2)}) collective-permute-start(bf16[48,2560]{1,0:T(8,128)(2,1)S(1)} %shard_map.137.after_ref.mine_ref), channel_id=1, source_target_pairs={{4,0},{8,12},{5,1},{9,13},{6,2},{10,14},{7,3},{11,15},{20,16},{24,... | collective-permute-start | bytes 737288 | tf_op jit(solution)/shard_map/ppermute | solution.py:247
  70.1 1.6 %collective-permute-done.17.came_ref = bf16[48,2560]{1,0:T(8,128)(2,1)S(1)} collective-permute-done((bf16[48,2560]{1,0:T(8,128)(2,1)S(1)}, bf16[48,2560]{1,0:T(8,128)(2,1)S(1)}, u32[]{:S(2)}, u32[]{:S(2)}) %collective-permute-start.17) | collective-permute-done | bytes 245792 | tf_op jit(solution)/shard_map/ppermute | solution.py:247
  73.5 2.8 %collective-permute-done.19.came_ref = bf16[48,2560]{1,0:T(8,128)(2,1)S(1)} collective-permute-done((bf16[48,2560]{1,0:T(8,128)(2,1)S(1)}, bf16[48,2560]{1,0:T(8,128)(2,1)S(1)}, u32[]{:S(2)}, u32[]{:S(2)}) %collective-permute-start.19) | collective-permute-done | bytes 245792 | tf_op jit(solution)/shard_map/ppermute | solution.py:247
  78.1 2.9 %collective-permute-done.22.refs_5_ = bf16[48,320]{1,0:T(8,128)(2,1)S(1)} collective-permute-done((bf16[48,320]{1,0:T(8,128)(2,1)S(1)}, bf16[48,320]{1,0:T(8,128)(2,1)S(1)}, u32[]{:S(2)}, u32[]{:S(2)}) %collective-permute-start.22) | collective-permute-done | bytes 30752 | tf_op jit(solution)/shard_map/ppermute | solution.py:259
  81.0 0.8 shard_map.144
  81.8 1.2 %collective-permute-done.23 = f32[12,512]{1,0:T(8,128)S(1)} collective-permute-done((f32[12,512]{1,0:T(8,128)S(1)}, f32[12,512]{1,0:T(8,128)S(1)}, u32[]{:S(2)}, u32[]{:S(2)}) %collective-permute-start.23) | collective-permute-done | bytes 24608 | tf_op jit(solution)/shard_map/ppermute | solution.py:299
  83.2 1.7 %collective-permute-start.26 = (f32[1,96]{1,0:T(1,128)S(1)}, f32[1,96]{1,0:T(1,128)S(1)}, u32[]{:S(2)}, u32[]{:S(2)}) collective-permute-start(f32[1,96]{1,0:T(1,128)S(1)} %reshape.12), channel_id=1, source_target_pairs={{0,8},{4,12},{8,0},{12,4},{1,9},{5,13},{9,1},{13,5},{2,10},{6,14},... | collective-permute-start | bytes 1160 | tf_op jit(solution)/shard_map/ppermute | solution.py:314
  85.0 2.6 %collective-permute-start.27 = (f32[1,96]{1,0:T(1,128)S(1)}, f32[1,96]{1,0:T(1,128)S(1)}, u32[]{:S(2)}, u32[]{:S(2)}) collective-permute-start(f32[1,96]{1,0:T(1,128)S(1)} %reshape.12), channel_id=1, source_target_pairs={{0,12},{4,8},{8,4},{12,0},{1,13},{5,9},{9,5},{13,1},{2,14},{6,10},... | collective-permute-start | bytes 1160 | tf_op jit(solution)/shard_map/ppermute | solution.py:314
  87.7 2.6 %collective-permute-done.27 = f32[1,96]{1,0:T(1,128)S(1)} collective-permute-done((f32[1,96]{1,0:T(1,128)S(1)}, f32[1,96]{1,0:T(1,128)S(1)}, u32[]{:S(2)}, u32[]{:S(2)}) %collective-permute-start.27) | collective-permute-done | bytes 416 | tf_op jit(solution)/shard_map/ppermute | solution.py:314
  90.4 1.6 %collective-permute-start.28 = (f32[1,384]{1,0:T(1,128)S(1)}, f32[1,384]{1,0:T(1,128)S(1)}, u32[]{:S(2)}, u32[]{:S(2)}) collective-permute-start(f32[1,384]{1,0:T(1,128)S(1)} %pad_maximum_fusion), channel_id=1, source_target_pairs={{0,2},{1,3},{2,0},{3,1},{4,6},{5,7},{6,4},{7,5},{8,10},{9,11},{10,... | collective-permute-start | bytes 4616 | tf_op jit(solution)/shard_map/ppermute | solution.py:299
  92.5 1.5 %collective-permute-done.28 = f32[1,384]{1,0:T(1,128)S(1)} collective-permute-done((f32[1,384]{1,0:T(1,128)S(1)}, f32[1,384]{1,0:T(1,128)S(1)}, u32[]{:S(2)}, u32[]{:S(2)}) %collective-permute-start.28) | collective-permute-done | bytes 1568 | tf_op jit(solution)/shard_map/ppermute | solution.py:299
  94.0 0.7 select_reduce_fusion
  94.7 1.1 %collective-permute-done.24 = f32[12,320]{1,0:T(8,128)S(1)} collective-permute-done((f32[12,320]{1,0:T(8,128)S(1)}, f32[12,320]{1,0:T(8,128)S(1)}, u32[]{:S(2)}, u32[]{:S(2)}) %collective-permute-start.24) | collective-permute-done | bytes 15392 | tf_op jit(solution)/shard_map/ppermute | solution.py:299
  (75 shorter events, 11.7 us)
Async XLA Ops:
  4.5 61.8 %collective-permute-start = (bf16[320,2560]{1,0:T(8,128)(2,1)S(1)}, bf16[320,2560]{1,0:T(8,128)(2,1)S(1)}, u32[]{:S(2)}, u32[]{:S(2)}) collective-permute-start(bf16[320,2560]{1,0:T(8,128)(2,1)S(1)} %get-tuple-element.25), channel_id=1, source_target_pairs={{0,16},{16,0},{1,17},{17,1},{2,18},{18,2},{3,19},{19,3},{4,20},{20... | collective-permute-start | bytes 4915208 | tf_op jit(solution)/shard_map/ppermute | solution.py:253
  7.5 9.9 %collective-permute-start.1 = (bf16[48,2560]{1,0:T(8,128)(2,1)S(1)}, bf16[48,2560]{1,0:T(8,128)(2,1)S(1)}, u32[]{:S(2)}, u32[]{:S(2)}) collective-permute-start(bf16[48,2560]{1,0:T(8,128)(2,1)S(1)} %get-tuple-element.28.mine_ref.after_ref), channel_id=1, source_target_pairs={{0,4},{12,8},{1,5},{13,9},{2,6},{14,10},{3,7},{15,11},{16,20},{28,... | collective-permute-start | bytes 737288 | tf_op jit(solution)/shard_map/ppermute | solution.py:247
  11.0 14.3 %collective-permute-start.4 = (bf16[48,2560]{1,0:T(8,128)(2,1)S(1)}, bf16[48,2560]{1,0:T(8,128)(2,1)S(1)}, u32[]{:S(2)}, u32[]{:S(2)}) collective-permute-start(bf16[48,2560]{1,0:T(8,128)(2,1)S(1)} %get-tuple-element.31.mine_ref), channel_id=1, source_target_pairs={{0,4},{12,8},{1,5},{13,9},{2,6},{14,10},{3,7},{15,11},{16,20},{28,... | collective-permute-start | bytes 737288 | tf_op jit(solution)/shard_map/ppermute | solution.py:247
  17.4 8.7 %collective-permute-start.3 = (bf16[48,2560]{1,0:T(8,128)(2,1)S(1)}, bf16[48,2560]{1,0:T(8,128)(2,1)S(1)}, u32[]{:S(2)}, u32[]{:S(2)}) collective-permute-start(bf16[48,2560]{1,0:T(8,128)(2,1)S(1)} %get-tuple-element.30.after_ref.mine_ref), channel_id=1, source_target_pairs={{4,8},{8,4},{5,9},{9,5},{6,10},{10,6},{7,11},{11,7},{20,24},{24,20... | collective-permute-start | bytes 737288 | tf_op jit(solution)/shard_map/ppermute | solution.py:247
  18.1 13.0 %collective-permute-start.2 = (bf16[48,2560]{1,0:T(8,128)(2,1)S(1)}, bf16[48,2560]{1,0:T(8,128)(2,1)S(1)}, u32[]{:S(2)}, u32[]{:S(2)}) collective-permute-start(bf16[48,2560]{1,0:T(8,128)(2,1)S(1)} %get-tuple-element.29), channel_id=1, source_target_pairs={{0,4},{12,8},{1,5},{13,9},{2,6},{14,10},{3,7},{15,11},{16,20},{28,... | collective-permute-start | bytes 737288 | tf_op jit(solution)/shard_map/ppermute | solution.py:247
  25.4 6.4 %collective-permute-start.7 = (bf16[48,2560]{1,0:T(8,128)(2,1)S(1)}, bf16[48,2560]{1,0:T(8,128)(2,1)S(1)}, u32[]{:S(2)}, u32[]{:S(2)}) collective-permute-start(bf16[48,2560]{1,0:T(8,128)(2,1)S(1)} %shard_map.115.after_ref.mine_ref), channel_id=1, source_target_pairs={{4,8},{8,4},{5,9},{9,5},{6,10},{10,6},{7,11},{11,7},{20,24},{24,20... | collective-permute-start | bytes 737288 | tf_op jit(solution)/shard_map/ppermute | solution.py:247
  26.2 10.0 %collective-permute-start.6 = (bf16[48,2560]{1,0:T(8,128)(2,1)S(1)}, bf16[48,2560]{1,0:T(8,128)(2,1)S(1)}, u32[]{:S(2)}, u32[]{:S(2)}) collective-permute-start(bf16[48,2560]{1,0:T(8,128)(2,1)S(1)} %get-tuple-element.34), channel_id=1, source_target_pairs={{0,4},{12,8},{4,0},{8,12},{1,5},{13,9},{5,1},{9,13},{2,6},{14,10},... | collective-permute-start | bytes 737288 | tf_op jit(solution)/shard_map/ppermute | solution.py:247
  31.2 5.8 %collective-permute-start.5 = (bf16[48,2560]{1,0:T(8,128)(2,1)S(1)}, bf16[48,2560]{1,0:T(8,128)(2,1)S(1)}, u32[]{:S(2)}, u32[]{:S(2)}) collective-permute-start(bf16[48,2560]{1,0:T(8,128)(2,1)S(1)} %shard_map.117.after_ref.mine_ref), channel_id=1, source_target_pairs={{4,8},{8,4},{5,9},{9,5},{6,10},{10,6},{7,11},{11,7},{20,24},{24,20... | collective-permute-start | bytes 737288 | tf_op jit(solution)/shard_map/ppermute | solution.py:247
  32.0 11.3 %collective-permute-start.10 = (bf16[48,2560]{1,0:T(8,128)(2,1)S(1)}, bf16[48,2560]{1,0:T(8,128)(2,1)S(1)}, u32[]{:S(2)}, u32[]{:S(2)}) collective-permute-start(bf16[48,2560]{1,0:T(8,128)(2,1)S(1)} %get-tuple-element.39), channel_id=1, source_target_pairs={{0,4},{12,8},{4,0},{8,12},{1,5},{13,9},{5,1},{9,13},{2,6},{14,10},... | collective-permute-start | bytes 737288 | tf_op jit(solution)/shard_map/ppermute | solution.py:247
  36.3 7.7 %collective-permute-start.9 = (bf16[48,2560]{1,0:T(8,128)(2,1)S(1)}, bf16[48,2560]{1,0:T(8,128)(2,1)S(1)}, u32[]{:S(2)}, u32[]{:S(2)}) collective-permute-start(bf16[48,2560]{1,0:T(8,128)(2,1)S(1)} %shard_map.120.after_ref.mine_ref), channel_id=1, source_target_pairs={{4,8},{8,4},{5,9},{9,5},{6,10},{10,6},{7,11},{11,7},{20,24},{24,20... | collective-permute-start | bytes 737288 | tf_op jit(solution)/shard_map/ppermute | solution.py:247
  37.1 12.2 %collective-permute-start.8 = (bf16[48,2560]{1,0:T(8,128)(2,1)S(1)}, bf16[48,2560]{1,0:T(8,128)(2,1)S(1)}, u32[]{:S(2)}, u32[]{:S(2)}) collective-permute-start(bf16[48,2560]{1,0:T(8,128)(2,1)S(1)} %get-tuple-element.37), channel_id=1, source_target_pairs={{0,4},{12,8},{4,0},{8,12},{1,5},{13,9},{5,1},{9,13},{2,6},{14,10},... | collective-permute-start | bytes 737288 | tf_op jit(solution)/shard_map/ppermute | solution.py:247
  43.3 6.7 %collective-permute-start.13 = (bf16[48,2560]{1,0:T(8,128)(2,1)S(1)}, bf16[48,2560]{1,0:T(8,128)(2,1)S(1)}, u32[]{:S(2)}, u32[]{:S(2)}) collective-permute-start(bf16[48,2560]{1,0:T(8,128)(2,1)S(1)} %shard_map.123.after_ref.mine_ref), channel_id=1, source_target_pairs={{4,8},{8,4},{5,9},{9,5},{6,10},{10,6},{7,11},{11,7},{20,24},{24,20... | collective-permute-start | bytes 737288 | tf_op jit(solution)/shard_map/ppermute | solution.py:247
  44.1 10.8 %collective-permute-start.12 = (bf16[48,2560]{1,0:T(8,128)(2,1)S(1)}, bf16[48,2560]{1,0:T(8,128)(2,1)S(1)}, u32[]{:S(2)}, u32[]{:S(2)}) collective-permute-start(bf16[48,2560]{1,0:T(8,128)(2,1)S(1)} %get-tuple-element.42), channel_id=1, source_target_pairs={{0,4},{12,8},{4,0},{8,12},{1,5},{13,9},{5,1},{9,13},{2,6},{14,10},... | collective-permute-start | bytes 737288 | tf_op jit(solution)/shard_map/ppermute | solution.py:247
  49.4 6.3 %collective-permute-start.11 = (bf16[48,2560]{1,0:T(8,128)(2,1)S(1)}, bf16[48,2560]{1,0:T(8,128)(2,1)S(1)}, u32[]{:S(2)}, u32[]{:S(2)}) collective-permute-start(bf16[48,2560]{1,0:T(8,128)(2,1)S(1)} %shard_map.126.after_ref.mine_ref), channel_id=1, source_target_pairs={{4,8},{8,4},{5,9},{9,5},{6,10},{10,6},{7,11},{11,7},{20,24},{24,20... | collective-permute-start | bytes 737288 | tf_op jit(solution)/shard_map/ppermute | solution.py:247
  50.2 10.6 %collective-permute-start.16 = (bf16[48,2560]{1,0:T(8,128)(2,1)S(1)}, bf16[48,2560]{1,0:T(8,128)(2,1)S(1)}, u32[]{:S(2)}, u32[]{:S(2)}) collective-permute-start(bf16[48,2560]{1,0:T(8,128)(2,1)S(1)} %get-tuple-element.45), channel_id=1, source_target_pairs={{0,4},{12,8},{4,0},{8,12},{1,5},{13,9},{5,1},{9,13},{2,6},{14,10},... | collective-permute-start | bytes 737288 | tf_op jit(solution)/shard_map/ppermute | solution.py:247
  55.0 6.5 %collective-permute-start.15 = (bf16[48,2560]{1,0:T(8,128)(2,1)S(1)}, bf16[48,2560]{1,0:T(8,128)(2,1)S(1)}, u32[]{:S(2)}, u32[]{:S(2)}) collective-permute-start(bf16[48,2560]{1,0:T(8,128)(2,1)S(1)} %shard_map.129.after_ref.mine_ref), channel_id=1, source_target_pairs={{4,8},{8,4},{5,9},{9,5},{6,10},{10,6},{7,11},{11,7},{20,24},{24,20... | collective-permute-start | bytes 737288 | tf_op jit(solution)/shard_map/ppermute | solution.py:247
  55.8 10.4 %collective-permute-start.14 = (bf16[48,2560]{1,0:T(8,128)(2,1)S(1)}, bf16[48,2560]{1,0:T(8,128)(2,1)S(1)}, u32[]{:S(2)}, u32[]{:S(2)}) collective-permute-start(bf16[48,2560]{1,0:T(8,128)(2,1)S(1)} %shard_map.130.after_ref.mine_ref), channel_id=1, source_target_pairs={{4,0},{8,12},{5,1},{9,13},{6,2},{10,14},{7,3},{11,15},{20,16},{24,... | collective-permute-start | bytes 737288 | tf_op jit(solution)/shard_map/ppermute | solution.py:247
  60.8 7.3 %collective-permute-start.18 = (bf16[48,2560]{1,0:T(8,128)(2,1)S(1)}, bf16[48,2560]{1,0:T(8,128)(2,1)S(1)}, u32[]{:S(2)}, u32[]{:S(2)}) collective-permute-start(bf16[48,2560]{1,0:T(8,128)(2,1)S(1)} %shard_map.132.after_ref.mine_ref), channel_id=1, source_target_pairs={{4,8},{8,4},{5,9},{9,5},{6,10},{10,6},{7,11},{11,7},{20,24},{24,20... | collective-permute-start | bytes 737288 | tf_op jit(solution)/shard_map/ppermute | solution.py:247
  61.6 10.1 %collective-permute-start.17 = (bf16[48,2560]{1,0:T(8,128)(2,1)S(1)}, bf16[48,2560]{1,0:T(8,128)(2,1)S(1)}, u32[]{:S(2)}, u32[]{:S(2)}) collective-permute-start(bf16[48,2560]{1,0:T(8,128)(2,1)S(1)} %shard_map.133.after_ref.mine_ref), channel_id=1, source_target_pairs={{4,0},{8,12},{5,1},{9,13},{6,2},{10,14},{7,3},{11,15},{20,16},{24,... | collective-permute-start | bytes 737288 | tf_op jit(solution)/shard_map/ppermute | solution.py:247
  68.2 8.1 %collective-permute-start.19 = (bf16[48,2560]{1,0:T(8,128)(2,1)S(1)}, bf16[48,2560]{1,0:T(8,128)(2,1)S(1)}, u32[]{:S(2)}, u32[]{:S(2)}) collective-permute-start(bf16[48,2560]{1,0:T(8,128)(2,1)S(1)} %shard_map.137.after_ref.mine_ref), channel_id=1, source_target_pairs={{4,0},{8,12},{5,1},{9,13},{6,2},{10,14},{7,3},{11,15},{20,16},{24,... | collective-permute-start | bytes 737288 | tf_op jit(solution)/shard_map/ppermute | solution.py:247
  69.5 8.6 %collective-permute-start.20 = (bf16[288,320]{1,0:T(8,128)(2,1)S(1)}, bf16[288,320]{1,0:T(8,128)(2,1)S(1)}, u32[]{:S(2)}, u32[]{:S(2)}) collective-permute-start(bf16[288,320]{1,0:T(8,128)(2,1)S(1)} %shard_map.135.after_ref), channel_id=1, source_target_pairs={{0,16},{16,0},{1,17},{17,1},{2,18},{18,2},{3,19},{19,3},{4,20},{20... | collective-permute-start | bytes 552968 | tf_op jit(solution)/shard_map/ppermute | solution.py:259
  72.9 5.2 %collective-permute-start.21 = (bf16[48,320]{1,0:T(8,128)(2,1)S(1)}, bf16[48,320]{1,0:T(8,128)(2,1)S(1)}, u32[]{:S(2)}, u32[]{:S(2)}) collective-permute-start(bf16[48,320]{1,0:T(8,128)(2,1)S(1)} %shard_map.139.after_ref), channel_id=1, source_target_pairs={{0,16},{16,0},{1,17},{17,1},{2,18},{18,2},{3,19},{19,3},{4,20},{20... | collective-permute-start | bytes 92168 | tf_op jit(solution)/shard_map/ppermute | solution.py:259
  76.9 15.0 %copy-start.1 = (s32[128]{0:T(128)S(1)}, s32[128]{0:T(128)}, u32[]{:S(2)}) copy-start(s32[128]{0:T(128)} %param.19) | copy-start | bytes 1540
  76.9 15.0 %copy-start.2 = (s32[128]{0:T(128)S(1)}, s32[128]{0:T(128)}, u32[]{:S(2)}) copy-start(s32[128]{0:T(128)} %param.17) | copy-start | bytes 1540
  76.9 15.0 %copy-start.3 = (s32[128,1]{0,1:T(1,128)S(1)}, s32[128,1]{0,1:T(1,128)}, u32[]{:S(2)}) copy-start(s32[128,1]{0,1:T(1,128)} %param.18) | copy-start | bytes 1540
  77.0 4.0 %collective-permute-start.22 = (bf16[48,320]{1,0:T(8,128)(2,1)S(1)}, bf16[48,320]{1,0:T(8,128)(2,1)S(1)}, u32[]{:S(2)}, u32[]{:S(2)}) collective-permute-start(bf16[48,320]{1,0:T(8,128)(2,1)S(1)} %shard_map.142.after_ref), channel_id=1, source_target_pairs={{0,16},{16,0},{1,17},{17,1},{2,18},{18,2},{3,19},{19,3},{4,20},{20... | collective-permute-start | bytes 92168 | tf_op jit(solution)/shard_map/ppermute | solution.py:259
  81.8 1.3 %collective-permute-start.23 = (f32[12,512]{1,0:T(8,128)S(1)}, f32[12,512]{1,0:T(8,128)S(1)}, u32[]{:S(2)}, u32[]{:S(2)}) collective-permute-start(f32[12,512]{1,0:T(8,128)S(1)} %shard_map.144), channel_id=1, source_target_pairs={{0,1},{1,0},{2,3},{3,2},{4,5},{5,4},{6,7},{7,6},{8,9},{9,8},{10,11... | collective-permute-start | bytes 73736 | tf_op jit(solution)/shard_map/ppermute | solution.py:299
  83.1 4.5 %collective-permute-start.25 = (f32[1,96]{1,0:T(1,128)S(1)}, f32[1,96]{1,0:T(1,128)S(1)}, u32[]{:S(2)}, u32[]{:S(2)}) collective-permute-start(f32[1,96]{1,0:T(1,128)S(1)} %reshape.12), channel_id=1, source_target_pairs={{0,4},{4,0},{8,12},{12,8},{1,5},{5,1},{9,13},{13,9},{2,6},{6,2},{1... | collective-permute-start | bytes 1160 | tf_op jit(solution)/shard_map/ppermute | solution.py:314
  83.2 4.5 %collective-permute-start.26 = (f32[1,96]{1,0:T(1,128)S(1)}, f32[1,96]{1,0:T(1,128)S(1)}, u32[]{:S(2)}, u32[]{:S(2)}) collective-permute-start(f32[1,96]{1,0:T(1,128)S(1)} %reshape.12), channel_id=1, source_target_pairs={{0,8},{4,12},{8,0},{12,4},{1,9},{5,13},{9,1},{13,5},{2,10},{6,14},... | collective-permute-start | bytes 1160 | tf_op jit(solution)/shard_map/ppermute | solution.py:314
  85.0 5.3 %collective-permute-start.27 = (f32[1,96]{1,0:T(1,128)S(1)}, f32[1,96]{1,0:T(1,128)S(1)}, u32[]{:S(2)}, u32[]{:S(2)}) collective-permute-start(f32[1,96]{1,0:T(1,128)S(1)} %reshape.12), channel_id=1, source_target_pairs={{0,12},{4,8},{8,4},{12,0},{1,13},{5,9},{9,5},{13,1},{2,14},{6,10},... | collective-permute-start | bytes 1160 | tf_op jit(solution)/shard_map/ppermute | solution.py:314
  90.4 3.6 %collective-permute-start.28 = (f32[1,384]{1,0:T(1,128)S(1)}, f32[1,384]{1,0:T(1,128)S(1)}, u32[]{:S(2)}, u32[]{:S(2)}) collective-permute-start(f32[1,384]{1,0:T(1,128)S(1)} %pad_maximum_fusion), channel_id=1, source_target_pairs={{0,2},{1,3},{2,0},{3,1},{4,6},{5,7},{6,4},{7,5},{8,10},{9,11},{10,... | collective-permute-start | bytes 4616 | tf_op jit(solution)/shard_map/ppermute | solution.py:299
  92.0 3.9 %collective-permute-start.24 = (f32[12,320]{1,0:T(8,128)S(1)}, f32[12,320]{1,0:T(8,128)S(1)}, u32[]{:S(2)}, u32[]{:S(2)}) collective-permute-start(f32[12,320]{1,0:T(8,128)S(1)} %slice.10), channel_id=1, source_target_pairs={{0,2},{1,3},{2,0},{3,1},{4,6},{5,7},{6,4},{7,5},{8,10},{9,11},{10,... | collective-permute-start | bytes 46088 | tf_op jit(solution)/shard_map/ppermute | solution.py:299
  (1 other events, 4.7 us)

commit v7 on v6

--- a/solution.py
+++ b/solution.py
@@ -26,62 +26,98 @@
     return jax.ShapeDtypeStruct(shape, jnp.bfloat16)
 
 
-def pull_kernel(chunks, acts_ref, grads_ref, basis_in_ref, basis_out_ref, query_in_ref, query_out_ref, *rest):
-    outs, (tokens_ref, theirs_ref, basis, query, turned, sems) = rest[:chunks], rest[chunks:]
-    rows = outs[0].shape[0]
-    features = basis.shape[0]
+def first_pull_kernel(basis_in_ref, basis_out_ref, query_in_ref, query_out_ref, out_ref, basis_ref, query_ref, turned_ref, sems):
+    rows = out_ref.shape[0]
+    features = basis_ref.shape[0]
     block = 512 if features % 512 == 0 else features
     spans = [pl.ds(first, block) for first in range(0, features, block)]
 
-    def copies(mine, theirs, from_basis, from_query):
-        pairs = [(from_query, query)]
-        pairs += [(from_basis.at[span], basis.at[span]) for span in spans]
-        pairs += [(mine, tokens_ref), (theirs, theirs_ref)]
-        return [pltpu.make_async_copy(source, target, sems.at[i]) for i, (source, target) in enumerate(pairs)]
+    def copies(from_basis, from_query):
+        return [pltpu.make_async_copy(from_query, query_ref, sems.at[0])] + [
+            pltpu.make_async_copy(from_basis.at[span], basis_ref.at[span], sems.at[1 + i])
+            for i, span in enumerate(spans)
+        ]
 
     side = lax.axis_index("parts")
 
     @pl.when(side == 0)
     def _():
-        for copy in copies(acts_ref, grads_ref, basis_in_ref, query_in_ref):
+        for copy in copies(basis_in_ref, query_in_ref):
             copy.start()
 
     @pl.when(side != 0)
     def _():
-        for copy in copies(grads_ref, acts_ref, basis_out_ref, query_out_ref):
+        for copy in copies(basis_out_ref, query_out_ref):
             copy.start()
 
-    landed = copies(acts_ref, grads_ref, basis_in_ref, query_in_ref)
+    landed = copies(basis_in_ref, query_in_ref)
     landed[0].wait()
-    turned[...] = query[...].T
+    turned_ref[...] = query_ref[...].T
     for copy, span in zip(landed[1:], spans):
         copy.wait()
-        pulled = lax.dot_general(turned[...], basis[span], NT, preferred_element_type=jnp.float32)
-        pulled = pulled.astype(jnp.bfloat16)
-        for c, out in enumerate(outs):
-            out[:, span] = pulled[c * rows : (c + 1) * rows]
-    for copy in landed[1 + len(spans) :]:
-        copy.wait()
-
-
-def pull(acts, grads, basis_in, basis_out, query_in, query_out, rows):
+        out_ref[:, span] = lax.dot_general(
+            turned_ref[:rows], basis_ref[span], NT, preferred_element_type=jnp.float32
+        ).astype(jnp.bfloat16)
+
+
+def first_pull(basis_in, basis_out, query_in, query_out, rows):
     features, depth = basis_in.shape
     spread = query_in.shape[1]
-    chunks = spread // rows
     blocks = features // 512 if features % 512 == 0 else 1
+    out, basis, _, turned = pl.pallas_call(
+        first_pull_kernel,
+        out_shape=[bf16(rows, features), bf16(features, depth), bf16(depth, spread), bf16(spread, depth)],
+        in_specs=[HBM] * 4,
+        out_specs=[VMEM] * 4,
+        scratch_shapes=[pltpu.SemaphoreType.DMA((1 + blocks,))],
+        compiler_params=pltpu.CompilerParams(vmem_limit_bytes=16 * MIB),
+    )(*in_hbm(basis_in, basis_out, query_in, query_out))
+    return out, basis, turned
+
+
+def pull_kernel(acts_ref, grads_ref, turned_ref, basis_ref, after_ref, *rest):
+    outs, (tokens_ref, theirs_ref, sems) = rest[:-3], rest[-3:]
+
+    def copies(mine, theirs):
+        return [
+            pltpu.make_async_copy(mine, tokens_ref, sems.at[0]),
+            pltpu.make_async_copy(theirs, theirs_ref, sems.at[1]),
+        ]
+
+    side = lax.axis_index("parts")
+
+    @pl.when(side == 0)
+    def _():
+        for copy in copies(acts_ref, grads_ref):
+            copy.start()
+
+    @pl.when(side != 0)
+    def _():
+        for copy in copies(grads_ref, acts_ref):
+            copy.start()
+
+    rows, features = outs[0].shape
+    block = 512 if features % 512 == 0 else features
+    for i in range(features // block):
+        pulled = lax.dot_general(
+            turned_ref[rows:], basis_ref[i * block : (i + 1) * block], NT, preferred_element_type=jnp.float32
+        ).astype(jnp.bfloat16)
+        for c, out in enumerate(outs):
+            out[:, i * block : (i + 1) * block] = pulled[c * rows : (c + 1) * rows]
+    for copy in copies(acts_ref, grads_ref):
+        copy.wait()
+
+
+def pull(after, turned, basis, acts, grads, rows):
+    chunks = turned.shape[0] // rows - 1
     out = pl.pallas_call(
-        functools.partial(pull_kernel, chunks),
-        out_shape=[bf16(rows, features)] * chunks + [bf16(*acts.shape)] * 2,
-        in_specs=[HBM] * 6,
+        pull_kernel,
+        out_shape=[bf16(rows, basis.shape[0])] * chunks + [bf16(*acts.shape)] * 2,
+        in_specs=[HBM, HBM, VMEM, VMEM, ANY],
         out_specs=[VMEM] * (chunks + 2),
-        scratch_shapes=[
-            pltpu.VMEM((features, depth), jnp.bfloat16),
-            pltpu.VMEM((depth, spread), jnp.bfloat16),
-            pltpu.VMEM((spread, depth), jnp.bfloat16),
-            pltpu.SemaphoreType.DMA((blocks + 3,)),
-        ],
+        scratch_shapes=[pltpu.SemaphoreType.DMA((2,))],
         compiler_params=pltpu.CompilerParams(vmem_limit_bytes=24 * MIB),
-    )(*in_hbm(acts, grads, basis_in, basis_out, query_in, query_out))
+    )(*in_hbm(acts, grads), turned, basis, after)
     return list(out[:chunks]), out[-2], out[-1]
 
 
@@ -227,9 +263,11 @@
     rows = chunk_rows(spread)
     chunks = spread // rows
 
-    own, tokens, theirs = pull(
-        acts[0], grads[0], basis_in[0], output_eigen_basis[0], query_in[0], query_out[0], rows
+    first, basis, turned = first_pull(
+        basis_in[0], output_eigen_basis[0], query_in[0], query_out[0], rows
     )
+    own, tokens, theirs = pull(first, turned, basis, acts[0], grads[0], rows)
+    own = [first] + own
     swap = [(0, 1), (1, 0)]
 
     stages = [("in", hop) for hop in range(half - 1)] + [("mid", 0)]
@@ -261,11 +299,12 @@
         waiting.clear()
         return mine[-1]
 
+    swapped = set()
     for turn in range(chunks + last):
-        for s, (kind, hop) in enumerate(stages):
-            c = turn - s
-            if not 0 <= c < chunks:
-                continue
+        steps = [(s, turn - s) for s in range(last) if 0 <= turn - s < chunks]
+        due = [c for c in range(chunks) if c + last + (c in swapped) == turn]
+        for s, c in steps + [(last, c) for c in due]:
+            kind, hop = stages[s]
             later = turn + ahead if turn + ahead < chunks else None
             if turn >= last - 1:
                 use = later if s == last - 1 else None
@@ -280,6 +319,7 @@
             after = part[c]
             if shared:
                 came[c] = came[use] = transfer(("in", "out"), 0, send)
+                swapped.add(c)
                 continue
             if use is not None:
                 came[use] = transfer(stages[0][:1], stages[0][1], send)
@@ -293,16 +333,10 @@
     scores = score(doc_counts, mine, back)
     if not is_power(layers):
         scores = lax.psum(scores, "layer")
-    steps = [1 << k for k in range(layers.bit_length() - 1)] if is_power(layers) else []
-
-    def add_other(value, step):
-        return value + lax.ppermute(value, "layer", [(i, i ^ step) for i in range(layers)])
-
-    if steps:
-        scores = add_other(scores, steps[0])
+    else:
+        for step in [1 << k for k in range(layers.bit_length() - 1)]:
+            scores = scores + lax.ppermute(scores, "layer", [(i, i ^ step) for i in range(layers)])
     token_scores, pooled = scores[:, : acts.shape[1]], scores[:, -LANES:]
-    for step in steps[1:]:
-        token_scores = add_other(token_scores, step)
 
     docs = doc_counts.shape[1]
     cells = queries * docs
@@ -317,8 +351,6 @@
     else:
         table = lax.all_gather(flat, "dp", axis=1, tiled=True)
         column = target * cells + cell
-    for step in steps[1:]:
-        table = add_other(table, step)
     hit = column[:, None] == jnp.arange(n * cells, dtype=jnp.int32)[None, :]
     pair_scores = jnp.sum(jnp.where(hit, table, 0.0), axis=1)
     return (token_scores, pair_scores)

time: 96.9 us -> 98.2 us (1.013)
  Pallas kernels: 9.99 us -> 12.8 us
    pallas_call x1 -> x2, Pallas kernels: 3.84 us -> 6.65 us  [the longest x1 3.44 us: first_pull(): pl.pallas_call(first_pull_kernel, out_shape=[bf16(rows, features), bf16(f...]
    ppermute x3 -> x2, starting transfers between devices: 2.17 us -> 1.56 us  [per_device(): lax.ppermute(scores, 'layer', [(i, i ^ step) for i in range(layers)])]
    ppermute x3 -> x2, waiting for transfers between devices: 3.77 us -> 3.62 us  [per_device(): lax.ppermute(scores, 'layer', [(i, i ^ step) for i in range(layers)])]
  transfers between devices with their start and end apart: 29 -> 28, of which waited for: 13 -> 10; matrix products, arithmetic and copies ran while one was open for 1% -> 1% of each run, Pallas kernels for 6% -> 6%
where the time goes in v7:
time: 98.2 us; the launch traced here: 97.8 us
  starting transfers between devices  55.3 us (56%)
  waiting for transfers between devices  26.9 us (27%)
  Pallas kernels  12.8 us (13%)
  between operations  1.14 us (1%)
    ppermute x19, starting transfers between devices, transfer(): return lax.ppermute(value, 'dp', pairs)  44.6 us
    ppermute x19, waiting for transfers between devices, transfer(): return lax.ppermute(value, 'dp', pairs)  18.4 us
    ppermute x3, starting transfers between devices, per_device(): lax.ppermute(flat, 'dp', [(i, i ^ k) for i in range(n)])  4.44 us
    pallas_call x6, Pallas kernels, project(): pl.pallas_call(project_kernel, out_shape=jax.ShapeDtypeStruct((rows, toke...  4.2 us
    ppermute x2, waiting for transfers between devices, per_device(): lax.ppermute(scores, 'layer', [(i, i ^ step) for i in range(layers)])  3.62 us
    pallas_call x1, Pallas kernels, first_pull(): pl.pallas_call(first_pull_kernel, out_shape=[bf16(rows, features), bf16(f...  3.44 us
    pallas_call x1, Pallas kernels, pull(): pl.pallas_call(pull_kernel, out_shape=[bf16(rows, basis.shape[0])] * chun...  3.21 us
    ppermute x1, starting transfers between devices, per_device(): others = lax.ppermute(theirs, 'parts', swap)  3.03 us
  transfers between devices with their start and end apart: 28, of which 10 were waited for; matrix products, arithmetic and copies ran while one was open for 1% of the time, Pallas kernels for 6%

profile of v7, /device:TPU:0, one launch (start us, length us, event | category | flops | bytes accessed | tf_op | source)
XLA Modules:
  0.0 97.8 jit_solution(13910655714388659343)
XLA Ops:
  0.6 3.4 %shard_map.113 = (bf16[48,2560]{1,0:T(8,128)(2,1)S(1)}, bf16[2560,640]{1,0:T(8,128)(2,1)S(1)}, bf16[640,384]{1,0:T(8,128)(2,1)}, bf16[384,640]{1,0:T(8,128)(2,1)S(1)}) custom-call(bf16[2560,640]{1,0:T(8,128)(2,1)} %bitcast.8, bf16[2560,640]{1,0:T(8,128)(2,1)} %bitcast.9, bf16[640,384]{1,0:T(8,128)(2,1)} %bitcast.12, bf16[640,384]{1,0:T(8,128)(2,1)} %bitcast.13), custom_call_target="tpu_custom_call" | custom-call | tf_op jit(solution)/shard_map/pallas_call | solution.py:67
  4.1 3.2 %shard_map.114 = (bf16[48,2560]{1,0:T(8,128)(2,1)S(1)}, bf16[48,2560]{1,0:T(8,128)(2,1)S(1)}, bf16[48,2560]{1,0:T(8,128)(2,1)S(1)}, bf16[48,2560]{1,0:T(8,128)(2...) custom-call(bf16[320,2560]{1,0:T(8,128)(2,1)} %bitcast.10, ...), custom_call_target="tpu_custom_call" | custom-call | tf_op jit(solution)/shard_map/pallas_call | solution.py:113
  7.3 3.0 %collective-permute-start = (bf16[320,2560]{1,0:T(8,128)(2,1)S(1)}, bf16[320,2560]{1,0:T(8,128)(2,1)S(1)}, u32[]{:S(2)}, u32[]{:S(2)}) collective-permute-start(bf16[320,2560]{1,0:T(8,128)(2,1)S(1)} %get-tuple-element.30), channel_id=1, source_target_pairs={{0,16},{16,0},{1,17},{17,1},{2,18},{18,2},{3,19},{19,3},{4,20},{20... | collective-permute-start | bytes 4915208 | tf_op jit(solution)/shard_map/ppermute | solution.py:291
  10.3 3.5 %collective-permute-start.1 = (bf16[48,2560]{1,0:T(8,128)(2,1)S(1)}, bf16[48,2560]{1,0:T(8,128)(2,1)S(1)}, u32[]{:S(2)}, u32[]{:S(2)}) collective-permute-start(bf16[48,2560]{1,0:T(8,128)(2,1)S(1)} %get-tuple-element.28.after_ref.mine_ref), channel_id=1, source_target_pairs={{0,4},{12,8},{1,5},{13,9},{2,6},{14,10},{3,7},{15,11},{16,20},{28,... | collective-permute-start | bytes 737288 | tf_op jit(solution)/shard_map/ppermute | solution.py:285
  13.8 1.3 %collective-permute-start.4 = (bf16[48,2560]{1,0:T(8,128)(2,1)S(1)}, bf16[48,2560]{1,0:T(8,128)(2,1)S(1)}, u32[]{:S(2)}, u32[]{:S(2)}) collective-permute-start(bf16[48,2560]{1,0:T(8,128)(2,1)S(1)} %get-tuple-element.35.mine_ref), channel_id=1, source_target_pairs={{0,4},{12,8},{1,5},{13,9},{2,6},{14,10},{3,7},{15,11},{16,20},{28,... | collective-permute-start | bytes 737288 | tf_op jit(solution)/shard_map/ppermute | solution.py:285
  15.1 5.1 %collective-permute-done.1.came_ref = bf16[48,2560]{1,0:T(8,128)(2,1)S(1)} collective-permute-done((bf16[48,2560]{1,0:T(8,128)(2,1)S(1)}, bf16[48,2560]{1,0:T(8,128)(2,1)S(1)}, u32[]{:S(2)}, u32[]{:S(2)}) %collective-permute-start.1) | collective-permute-done | bytes 245792 | tf_op jit(solution)/shard_map/ppermute | solution.py:285
  20.3 0.7 collective-permute-start.3
  20.9 7.2 %collective-permute-start.2 = (bf16[48,2560]{1,0:T(8,128)(2,1)S(1)}, bf16[48,2560]{1,0:T(8,128)(2,1)S(1)}, u32[]{:S(2)}, u32[]{:S(2)}) collective-permute-start(bf16[48,2560]{1,0:T(8,128)(2,1)S(1)} %get-tuple-element.33), channel_id=1, source_target_pairs={{0,4},{12,8},{1,5},{13,9},{2,6},{14,10},{3,7},{15,11},{16,20},{28,... | collective-permute-start | bytes 737288 | tf_op jit(solution)/shard_map/ppermute | solution.py:285
  29.0 3.0 %collective-permute-start.6 = (bf16[48,2560]{1,0:T(8,128)(2,1)S(1)}, bf16[48,2560]{1,0:T(8,128)(2,1)S(1)}, u32[]{:S(2)}, u32[]{:S(2)}) collective-permute-start(bf16[48,2560]{1,0:T(8,128)(2,1)S(1)} %get-tuple-element.38), channel_id=1, source_target_pairs={{0,4},{12,8},{4,0},{8,12},{1,5},{13,9},{5,1},{9,13},{2,6},{14,10},... | collective-permute-start | bytes 737288 | tf_op jit(solution)/shard_map/ppermute | solution.py:285
  32.1 1.9 %collective-permute-done.2.came_ref = bf16[48,2560]{1,0:T(8,128)(2,1)S(1)} collective-permute-done((bf16[48,2560]{1,0:T(8,128)(2,1)S(1)}, bf16[48,2560]{1,0:T(8,128)(2,1)S(1)}, u32[]{:S(2)}, u32[]{:S(2)}) %collective-permute-start.2) | collective-permute-done | bytes 245792 | tf_op jit(solution)/shard_map/ppermute | solution.py:285
  34.8 4.2 %collective-permute-start.9 = (bf16[48,2560]{1,0:T(8,128)(2,1)S(1)}, bf16[48,2560]{1,0:T(8,128)(2,1)S(1)}, u32[]{:S(2)}, u32[]{:S(2)}) collective-permute-start(bf16[48,2560]{1,0:T(8,128)(2,1)S(1)} %get-tuple-element.42), channel_id=1, source_target_pairs={{0,4},{12,8},{4,0},{8,12},{1,5},{13,9},{5,1},{9,13},{2,6},{14,10},... | collective-permute-start | bytes 737288 | tf_op jit(solution)/shard_map/ppermute | solution.py:285
  39.9 6.2 %collective-permute-start.8 = (bf16[48,2560]{1,0:T(8,128)(2,1)S(1)}, bf16[48,2560]{1,0:T(8,128)(2,1)S(1)}, u32[]{:S(2)}, u32[]{:S(2)}) collective-permute-start(bf16[48,2560]{1,0:T(8,128)(2,1)S(1)} %get-tuple-element.41), channel_id=1, source_target_pairs={{0,4},{12,8},{4,0},{8,12},{1,5},{13,9},{5,1},{9,13},{2,6},{14,10},... | collective-permute-start | bytes 737288 | tf_op jit(solution)/shard_map/ppermute | solution.py:285
  46.9 5.2 %collective-permute-start.12 = (bf16[48,2560]{1,0:T(8,128)(2,1)S(1)}, bf16[48,2560]{1,0:T(8,128)(2,1)S(1)}, u32[]{:S(2)}, u32[]{:S(2)}) collective-permute-start(bf16[48,2560]{1,0:T(8,128)(2,1)S(1)} %get-tuple-element.46), channel_id=1, source_target_pairs={{0,4},{12,8},{4,0},{8,12},{1,5},{13,9},{5,1},{9,13},{2,6},{14,10},... | collective-permute-start | bytes 737288 | tf_op jit(solution)/shard_map/ppermute | solution.py:285
  52.9 4.7 %collective-permute-start.15 = (bf16[48,2560]{1,0:T(8,128)(2,1)S(1)}, bf16[48,2560]{1,0:T(8,128)(2,1)S(1)}, u32[]{:S(2)}, u32[]{:S(2)}) collective-permute-start(bf16[48,2560]{1,0:T(8,128)(2,1)S(1)} %get-tuple-element.49), channel_id=1, source_target_pairs={{0,4},{12,8},{4,0},{8,12},{1,5},{13,9},{5,1},{9,13},{2,6},{14,10},... | collective-permute-start | bytes 737288 | tf_op jit(solution)/shard_map/ppermute | solution.py:285
  58.5 1.3 %collective-permute-start.14 = (bf16[48,2560]{1,0:T(8,128)(2,1)S(1)}, bf16[48,2560]{1,0:T(8,128)(2,1)S(1)}, u32[]{:S(2)}, u32[]{:S(2)}) collective-permute-start(bf16[48,2560]{1,0:T(8,128)(2,1)S(1)} %shard_map.130.after_ref.mine_ref), channel_id=1, source_target_pairs={{4,0},{8,12},{5,1},{9,13},{6,2},{10,14},{7,3},{11,15},{20,16},{24,... | collective-permute-start | bytes 737288 | tf_op jit(solution)/shard_map/ppermute | solution.py:285
  59.9 3.7 %collective-permute-done.15.came_ref = bf16[48,2560]{1,0:T(8,128)(2,1)S(1)} collective-permute-done((bf16[48,2560]{1,0:T(8,128)(2,1)S(1)}, bf16[48,2560]{1,0:T(8,128)(2,1)S(1)}, u32[]{:S(2)}, u32[]{:S(2)}) %collective-permute-start.15) | collective-permute-done | bytes 245792 | tf_op jit(solution)/shard_map/ppermute | solution.py:285
  64.4 1.3 %collective-permute-start.17 = (bf16[48,2560]{1,0:T(8,128)(2,1)S(1)}, bf16[48,2560]{1,0:T(8,128)(2,1)S(1)}, u32[]{:S(2)}, u32[]{:S(2)}) collective-permute-start(bf16[48,2560]{1,0:T(8,128)(2,1)S(1)} %shard_map.133.after_ref.mine_ref), channel_id=1, source_target_pairs={{4,0},{8,12},{5,1},{9,13},{6,2},{10,14},{7,3},{11,15},{20,16},{24,... | collective-permute-start | bytes 737288 | tf_op jit(solution)/shard_map/ppermute | solution.py:285
  65.7 3.3 %collective-permute-done.14.came_ref = bf16[48,2560]{1,0:T(8,128)(2,1)S(1)} collective-permute-done((bf16[48,2560]{1,0:T(8,128)(2,1)S(1)}, bf16[48,2560]{1,0:T(8,128)(2,1)S(1)}, u32[]{:S(2)}, u32[]{:S(2)}) %collective-permute-start.14) | collective-permute-done | bytes 245792 | tf_op jit(solution)/shard_map/ppermute | solution.py:285
  69.0 0.9 shard_map.136.after_ref
  69.9 0.9 shard_map.137.after_ref.refs_0_
  71.0 1.3 %collective-permute-start.19 = (bf16[48,2560]{1,0:T(8,128)(2,1)S(1)}, bf16[48,2560]{1,0:T(8,128)(2,1)S(1)}, u32[]{:S(2)}, u32[]{:S(2)}) collective-permute-start(bf16[48,2560]{1,0:T(8,128)(2,1)S(1)} %shard_map.138.after_ref.mine_ref), channel_id=1, source_target_pairs={{4,0},{8,12},{5,1},{9,13},{6,2},{10,14},{7,3},{11,15},{20,16},{24,... | collective-permute-start | bytes 737288 | tf_op jit(solution)/shard_map/ppermute | solution.py:285
  72.8 1.7 %collective-permute-done.17.came_ref = bf16[48,2560]{1,0:T(8,128)(2,1)S(1)} collective-permute-done((bf16[48,2560]{1,0:T(8,128)(2,1)S(1)}, bf16[48,2560]{1,0:T(8,128)(2,1)S(1)}, u32[]{:S(2)}, u32[]{:S(2)}) %collective-permute-start.17) | collective-permute-done | bytes 245792 | tf_op jit(solution)/shard_map/ppermute | solution.py:285
  76.3 2.8 %collective-permute-done.19.came_ref = bf16[48,2560]{1,0:T(8,128)(2,1)S(1)} collective-permute-done((bf16[48,2560]{1,0:T(8,128)(2,1)S(1)}, bf16[48,2560]{1,0:T(8,128)(2,1)S(1)}, u32[]{:S(2)}, u32[]{:S(2)}) %collective-permute-start.19) | collective-permute-done | bytes 245792 | tf_op jit(solution)/shard_map/ppermute | solution.py:285
  80.9 2.9 %collective-permute-done.22.refs_5_ = bf16[48,320]{1,0:T(8,128)(2,1)S(1)} collective-permute-done((bf16[48,320]{1,0:T(8,128)(2,1)S(1)}, bf16[48,320]{1,0:T(8,128)(2,1)S(1)}, u32[]{:S(2)}, u32[]{:S(2)}) %collective-permute-start.22) | collective-permute-done | bytes 30752 | tf_op jit(solution)/shard_map/ppermute | solution.py:297
  83.7 0.8 shard_map.145
  84.6 1.2 %collective-permute-done.23 = f32[12,512]{1,0:T(8,128)S(1)} collective-permute-done((f32[12,512]{1,0:T(8,128)S(1)}, f32[12,512]{1,0:T(8,128)S(1)}, u32[]{:S(2)}, u32[]{:S(2)}) %collective-permute-start.23) | collective-permute-done | bytes 24608 | tf_op jit(solution)/shard_map/ppermute | solution.py:338
  85.8 1.5 %collective-permute-start.24 = (f32[12,512]{1,0:T(8,128)S(1)}, f32[12,512]{1,0:T(8,128)S(1)}, u32[]{:S(2)}, u32[]{:S(2)}) collective-permute-start(f32[12,512]{1,0:T(8,128)S(1)} %add.12), channel_id=1, source_target_pairs={{0,2},{1,3},{2,0},{3,1},{4,6},{5,7},{6,4},{7,5},{8,10},{9,11},{10,... | collective-permute-start | bytes 73736 | tf_op jit(solution)/shard_map/ppermute | solution.py:338
  87.3 2.4 %collective-permute-done.24 = f32[12,512]{1,0:T(8,128)S(1)} collective-permute-done((f32[12,512]{1,0:T(8,128)S(1)}, f32[12,512]{1,0:T(8,128)S(1)}, u32[]{:S(2)}, u32[]{:S(2)}) %collective-permute-start.24) | collective-permute-done | bytes 24608 | tf_op jit(solution)/shard_map/ppermute | solution.py:338
  89.9 1.7 %collective-permute-start.26 = (f32[1,96]{1,0:T(1,128)S(1)}, f32[1,96]{1,0:T(1,128)S(1)}, u32[]{:S(2)}, u32[]{:S(2)}) collective-permute-start(f32[1,96]{1,0:T(1,128)S(1)} %reshape.12), channel_id=1, source_target_pairs={{0,8},{4,12},{8,0},{12,4},{1,9},{5,13},{9,1},{13,5},{2,10},{6,14},... | collective-permute-start | bytes 1160 | tf_op jit(solution)/shard_map/ppermute | solution.py:348
  91.6 2.6 %collective-permute-start.27 = (f32[1,96]{1,0:T(1,128)S(1)}, f32[1,96]{1,0:T(1,128)S(1)}, u32[]{:S(2)}, u32[]{:S(2)}) collective-permute-start(f32[1,96]{1,0:T(1,128)S(1)} %reshape.12), channel_id=1, source_target_pairs={{0,12},{4,8},{8,4},{12,0},{1,13},{5,9},{9,5},{13,1},{2,14},{6,10},... | collective-permute-start | bytes 1160 | tf_op jit(solution)/shard_map/ppermute | solution.py:348
  94.9 2.1 %collective-permute-done.27 = f32[1,96]{1,0:T(1,128)S(1)} collective-permute-done((f32[1,96]{1,0:T(1,128)S(1)}, f32[1,96]{1,0:T(1,128)S(1)}, u32[]{:S(2)}, u32[]{:S(2)}) %collective-permute-start.27) | collective-permute-done | bytes 416 | tf_op jit(solution)/shard_map/ppermute | solution.py:348
  97.1 0.7 select_reduce_fusion
  (73 shorter events, 11.0 us)
Async XLA Ops:
  7.3 61.7 %collective-permute-start = (bf16[320,2560]{1,0:T(8,128)(2,1)S(1)}, bf16[320,2560]{1,0:T(8,128)(2,1)S(1)}, u32[]{:S(2)}, u32[]{:S(2)}) collective-permute-start(bf16[320,2560]{1,0:T(8,128)(2,1)S(1)} %get-tuple-element.30), channel_id=1, source_target_pairs={{0,16},{16,0},{1,17},{17,1},{2,18},{18,2},{3,19},{19,3},{4,20},{20... | collective-permute-start | bytes 4915208 | tf_op jit(solution)/shard_map/ppermute | solution.py:291
  10.3 9.9 %collective-permute-start.1 = (bf16[48,2560]{1,0:T(8,128)(2,1)S(1)}, bf16[48,2560]{1,0:T(8,128)(2,1)S(1)}, u32[]{:S(2)}, u32[]{:S(2)}) collective-permute-start(bf16[48,2560]{1,0:T(8,128)(2,1)S(1)} %get-tuple-element.28.after_ref.mine_ref), channel_id=1, source_target_pairs={{0,4},{12,8},{1,5},{13,9},{2,6},{14,10},{3,7},{15,11},{16,20},{28,... | collective-permute-start | bytes 737288 | tf_op jit(solution)/shard_map/ppermute | solution.py:285
  13.8 14.3 %collective-permute-start.4 = (bf16[48,2560]{1,0:T(8,128)(2,1)S(1)}, bf16[48,2560]{1,0:T(8,128)(2,1)S(1)}, u32[]{:S(2)}, u32[]{:S(2)}) collective-permute-start(bf16[48,2560]{1,0:T(8,128)(2,1)S(1)} %get-tuple-element.35.mine_ref), channel_id=1, source_target_pairs={{0,4},{12,8},{1,5},{13,9},{2,6},{14,10},{3,7},{15,11},{16,20},{28,... | collective-permute-start | bytes 737288 | tf_op jit(solution)/shard_map/ppermute | solution.py:285
  20.3 8.7 %collective-permute-start.3 = (bf16[48,2560]{1,0:T(8,128)(2,1)S(1)}, bf16[48,2560]{1,0:T(8,128)(2,1)S(1)}, u32[]{:S(2)}, u32[]{:S(2)}) collective-permute-start(bf16[48,2560]{1,0:T(8,128)(2,1)S(1)} %get-tuple-element.34.after_ref.mine_ref), channel_id=1, source_target_pairs={{4,8},{8,4},{5,9},{9,5},{6,10},{10,6},{7,11},{11,7},{20,24},{24,20... | collective-permute-start | bytes 737288 | tf_op jit(solution)/shard_map/ppermute | solution.py:285
  20.9 13.0 %collective-permute-start.2 = (bf16[48,2560]{1,0:T(8,128)(2,1)S(1)}, bf16[48,2560]{1,0:T(8,128)(2,1)S(1)}, u32[]{:S(2)}, u32[]{:S(2)}) collective-permute-start(bf16[48,2560]{1,0:T(8,128)(2,1)S(1)} %get-tuple-element.33), channel_id=1, source_target_pairs={{0,4},{12,8},{1,5},{13,9},{2,6},{14,10},{3,7},{15,11},{16,20},{28,... | collective-permute-start | bytes 737288 | tf_op jit(solution)/shard_map/ppermute | solution.py:285
  28.2 6.4 %collective-permute-start.7 = (bf16[48,2560]{1,0:T(8,128)(2,1)S(1)}, bf16[48,2560]{1,0:T(8,128)(2,1)S(1)}, u32[]{:S(2)}, u32[]{:S(2)}) collective-permute-start(bf16[48,2560]{1,0:T(8,128)(2,1)S(1)} %shard_map.116.after_ref.mine_ref), channel_id=1, source_target_pairs={{4,8},{8,4},{5,9},{9,5},{6,10},{10,6},{7,11},{11,7},{20,24},{24,20... | collective-permute-start | bytes 737288 | tf_op jit(solution)/shard_map/ppermute | solution.py:285
  29.0 10.0 %collective-permute-start.6 = (bf16[48,2560]{1,0:T(8,128)(2,1)S(1)}, bf16[48,2560]{1,0:T(8,128)(2,1)S(1)}, u32[]{:S(2)}, u32[]{:S(2)}) collective-permute-start(bf16[48,2560]{1,0:T(8,128)(2,1)S(1)} %get-tuple-element.38), channel_id=1, source_target_pairs={{0,4},{12,8},{4,0},{8,12},{1,5},{13,9},{5,1},{9,13},{2,6},{14,10},... | collective-permute-start | bytes 737288 | tf_op jit(solution)/shard_map/ppermute | solution.py:285
  34.0 5.8 %collective-permute-start.5 = (bf16[48,2560]{1,0:T(8,128)(2,1)S(1)}, bf16[48,2560]{1,0:T(8,128)(2,1)S(1)}, u32[]{:S(2)}, u32[]{:S(2)}) collective-permute-start(bf16[48,2560]{1,0:T(8,128)(2,1)S(1)} %shard_map.118.after_ref.mine_ref), channel_id=1, source_target_pairs={{4,8},{8,4},{5,9},{9,5},{6,10},{10,6},{7,11},{11,7},{20,24},{24,20... | collective-permute-start | bytes 737288 | tf_op jit(solution)/shard_map/ppermute | solution.py:285
  34.8 11.3 %collective-permute-start.9 = (bf16[48,2560]{1,0:T(8,128)(2,1)S(1)}, bf16[48,2560]{1,0:T(8,128)(2,1)S(1)}, u32[]{:S(2)}, u32[]{:S(2)}) collective-permute-start(bf16[48,2560]{1,0:T(8,128)(2,1)S(1)} %get-tuple-element.42), channel_id=1, source_target_pairs={{0,4},{12,8},{4,0},{8,12},{1,5},{13,9},{5,1},{9,13},{2,6},{14,10},... | collective-permute-start | bytes 737288 | tf_op jit(solution)/shard_map/ppermute | solution.py:285
  39.1 7.7 %collective-permute-start.10 = (bf16[48,2560]{1,0:T(8,128)(2,1)S(1)}, bf16[48,2560]{1,0:T(8,128)(2,1)S(1)}, u32[]{:S(2)}, u32[]{:S(2)}) collective-permute-start(bf16[48,2560]{1,0:T(8,128)(2,1)S(1)} %shard_map.120.after_ref.mine_ref), channel_id=1, source_target_pairs={{4,8},{8,4},{5,9},{9,5},{6,10},{10,6},{7,11},{11,7},{20,24},{24,20... | collective-permute-start | bytes 737288 | tf_op jit(solution)/shard_map/ppermute | solution.py:285
  39.9 12.2 %collective-permute-start.8 = (bf16[48,2560]{1,0:T(8,128)(2,1)S(1)}, bf16[48,2560]{1,0:T(8,128)(2,1)S(1)}, u32[]{:S(2)}, u32[]{:S(2)}) collective-permute-start(bf16[48,2560]{1,0:T(8,128)(2,1)S(1)} %get-tuple-element.41), channel_id=1, source_target_pairs={{0,4},{12,8},{4,0},{8,12},{1,5},{13,9},{5,1},{9,13},{2,6},{14,10},... | collective-permute-start | bytes 737288 | tf_op jit(solution)/shard_map/ppermute | solution.py:285
  46.1 6.7 %collective-permute-start.13 = (bf16[48,2560]{1,0:T(8,128)(2,1)S(1)}, bf16[48,2560]{1,0:T(8,128)(2,1)S(1)}, u32[]{:S(2)}, u32[]{:S(2)}) collective-permute-start(bf16[48,2560]{1,0:T(8,128)(2,1)S(1)} %shard_map.123.after_ref.mine_ref), channel_id=1, source_target_pairs={{4,8},{8,4},{5,9},{9,5},{6,10},{10,6},{7,11},{11,7},{20,24},{24,20... | collective-permute-start | bytes 737288 | tf_op jit(solution)/shard_map/ppermute | solution.py:285
  46.9 10.8 %collective-permute-start.12 = (bf16[48,2560]{1,0:T(8,128)(2,1)S(1)}, bf16[48,2560]{1,0:T(8,128)(2,1)S(1)}, u32[]{:S(2)}, u32[]{:S(2)}) collective-permute-start(bf16[48,2560]{1,0:T(8,128)(2,1)S(1)} %get-tuple-element.46), channel_id=1, source_target_pairs={{0,4},{12,8},{4,0},{8,12},{1,5},{13,9},{5,1},{9,13},{2,6},{14,10},... | collective-permute-start | bytes 737288 | tf_op jit(solution)/shard_map/ppermute | solution.py:285
  52.2 6.3 %collective-permute-start.11 = (bf16[48,2560]{1,0:T(8,128)(2,1)S(1)}, bf16[48,2560]{1,0:T(8,128)(2,1)S(1)}, u32[]{:S(2)}, u32[]{:S(2)}) collective-permute-start(bf16[48,2560]{1,0:T(8,128)(2,1)S(1)} %shard_map.126.after_ref.mine_ref), channel_id=1, source_target_pairs={{4,8},{8,4},{5,9},{9,5},{6,10},{10,6},{7,11},{11,7},{20,24},{24,20... | collective-permute-start | bytes 737288 | tf_op jit(solution)/shard_map/ppermute | solution.py:285
  52.9 10.6 %collective-permute-start.15 = (bf16[48,2560]{1,0:T(8,128)(2,1)S(1)}, bf16[48,2560]{1,0:T(8,128)(2,1)S(1)}, u32[]{:S(2)}, u32[]{:S(2)}) collective-permute-start(bf16[48,2560]{1,0:T(8,128)(2,1)S(1)} %get-tuple-element.49), channel_id=1, source_target_pairs={{0,4},{12,8},{4,0},{8,12},{1,5},{13,9},{5,1},{9,13},{2,6},{14,10},... | collective-permute-start | bytes 737288 | tf_op jit(solution)/shard_map/ppermute | solution.py:285
  57.8 6.5 %collective-permute-start.16 = (bf16[48,2560]{1,0:T(8,128)(2,1)S(1)}, bf16[48,2560]{1,0:T(8,128)(2,1)S(1)}, u32[]{:S(2)}, u32[]{:S(2)}) collective-permute-start(bf16[48,2560]{1,0:T(8,128)(2,1)S(1)} %shard_map.129.after_ref.mine_ref), channel_id=1, source_target_pairs={{4,8},{8,4},{5,9},{9,5},{6,10},{10,6},{7,11},{11,7},{20,24},{24,20... | collective-permute-start | bytes 737288 | tf_op jit(solution)/shard_map/ppermute | solution.py:285
  58.5 10.4 %collective-permute-start.14 = (bf16[48,2560]{1,0:T(8,128)(2,1)S(1)}, bf16[48,2560]{1,0:T(8,128)(2,1)S(1)}, u32[]{:S(2)}, u32[]{:S(2)}) collective-permute-start(bf16[48,2560]{1,0:T(8,128)(2,1)S(1)} %shard_map.130.after_ref.mine_ref), channel_id=1, source_target_pairs={{4,0},{8,12},{5,1},{9,13},{6,2},{10,14},{7,3},{11,15},{20,16},{24,... | collective-permute-start | bytes 737288 | tf_op jit(solution)/shard_map/ppermute | solution.py:285
  63.6 7.3 %collective-permute-start.18 = (bf16[48,2560]{1,0:T(8,128)(2,1)S(1)}, bf16[48,2560]{1,0:T(8,128)(2,1)S(1)}, u32[]{:S(2)}, u32[]{:S(2)}) collective-permute-start(bf16[48,2560]{1,0:T(8,128)(2,1)S(1)} %shard_map.132.after_ref.mine_ref), channel_id=1, source_target_pairs={{4,8},{8,4},{5,9},{9,5},{6,10},{10,6},{7,11},{11,7},{20,24},{24,20... | collective-permute-start | bytes 737288 | tf_op jit(solution)/shard_map/ppermute | solution.py:285
  64.4 10.1 %collective-permute-start.17 = (bf16[48,2560]{1,0:T(8,128)(2,1)S(1)}, bf16[48,2560]{1,0:T(8,128)(2,1)S(1)}, u32[]{:S(2)}, u32[]{:S(2)}) collective-permute-start(bf16[48,2560]{1,0:T(8,128)(2,1)S(1)} %shard_map.133.after_ref.mine_ref), channel_id=1, source_target_pairs={{4,0},{8,12},{5,1},{9,13},{6,2},{10,14},{7,3},{11,15},{20,16},{24,... | collective-permute-start | bytes 737288 | tf_op jit(solution)/shard_map/ppermute | solution.py:285
  71.0 8.1 %collective-permute-start.19 = (bf16[48,2560]{1,0:T(8,128)(2,1)S(1)}, bf16[48,2560]{1,0:T(8,128)(2,1)S(1)}, u32[]{:S(2)}, u32[]{:S(2)}) collective-permute-start(bf16[48,2560]{1,0:T(8,128)(2,1)S(1)} %shard_map.138.after_ref.mine_ref), channel_id=1, source_target_pairs={{4,0},{8,12},{5,1},{9,13},{6,2},{10,14},{7,3},{11,15},{20,16},{24,... | collective-permute-start | bytes 737288 | tf_op jit(solution)/shard_map/ppermute | solution.py:285
  72.3 8.6 %collective-permute-start.20 = (bf16[288,320]{1,0:T(8,128)(2,1)S(1)}, bf16[288,320]{1,0:T(8,128)(2,1)S(1)}, u32[]{:S(2)}, u32[]{:S(2)}) collective-permute-start(bf16[288,320]{1,0:T(8,128)(2,1)S(1)} %shard_map.136.after_ref), channel_id=1, source_target_pairs={{0,16},{16,0},{1,17},{17,1},{2,18},{18,2},{3,19},{19,3},{4,20},{20... | collective-permute-start | bytes 552968 | tf_op jit(solution)/shard_map/ppermute | solution.py:297
  75.7 5.2 %collective-permute-start.21 = (bf16[48,320]{1,0:T(8,128)(2,1)S(1)}, bf16[48,320]{1,0:T(8,128)(2,1)S(1)}, u32[]{:S(2)}, u32[]{:S(2)}) collective-permute-start(bf16[48,320]{1,0:T(8,128)(2,1)S(1)} %shard_map.140.after_ref), channel_id=1, source_target_pairs={{0,16},{16,0},{1,17},{17,1},{2,18},{18,2},{3,19},{19,3},{4,20},{20... | collective-permute-start | bytes 92168 | tf_op jit(solution)/shard_map/ppermute | solution.py:297
  79.1 4.7 %copy-start = (s32[1,8]{1,0:T(1,128)S(1)}, s32[1,8]{1,0:T(1,128)}, u32[]{:S(2)}) copy-start(s32[1,8]{1,0:T(1,128)} %counts_ref.1) | copy-start | bytes 100
  79.7 14.6 %copy-start.1 = (s32[128]{0:T(128)S(1)}, s32[128]{0:T(128)}, u32[]{:S(2)}) copy-start(s32[128]{0:T(128)} %param.19) | copy-start | bytes 1540
  79.7 14.6 %copy-start.2 = (s32[128]{0:T(128)S(1)}, s32[128]{0:T(128)}, u32[]{:S(2)}) copy-start(s32[128]{0:T(128)} %param.17) | copy-start | bytes 1540
  79.7 14.6 %copy-start.3 = (s32[128,1]{0,1:T(1,128)S(1)}, s32[128,1]{0,1:T(1,128)}, u32[]{:S(2)}) copy-start(s32[128,1]{0,1:T(1,128)} %param.18) | copy-start | bytes 1540
  79.7 4.0 %collective-permute-start.22 = (bf16[48,320]{1,0:T(8,128)(2,1)S(1)}, bf16[48,320]{1,0:T(8,128)(2,1)S(1)}, u32[]{:S(2)}, u32[]{:S(2)}) collective-permute-start(bf16[48,320]{1,0:T(8,128)(2,1)S(1)} %shard_map.143.after_ref), channel_id=1, source_target_pairs={{0,16},{16,0},{1,17},{17,1},{2,18},{18,2},{3,19},{19,3},{4,20},{20... | collective-permute-start | bytes 92168 | tf_op jit(solution)/shard_map/ppermute | solution.py:297
  84.5 1.3 %collective-permute-start.23 = (f32[12,512]{1,0:T(8,128)S(1)}, f32[12,512]{1,0:T(8,128)S(1)}, u32[]{:S(2)}, u32[]{:S(2)}) collective-permute-start(f32[12,512]{1,0:T(8,128)S(1)} %shard_map.145), channel_id=1, source_target_pairs={{0,1},{1,0},{2,3},{3,2},{4,5},{5,4},{6,7},{7,6},{8,9},{9,8},{10,11... | collective-permute-start | bytes 73736 | tf_op jit(solution)/shard_map/ppermute | solution.py:338
  85.8 3.9 %collective-permute-start.24 = (f32[12,512]{1,0:T(8,128)S(1)}, f32[12,512]{1,0:T(8,128)S(1)}, u32[]{:S(2)}, u32[]{:S(2)}) collective-permute-start(f32[12,512]{1,0:T(8,128)S(1)} %add.12), channel_id=1, source_target_pairs={{0,2},{1,3},{2,0},{3,1},{4,6},{5,7},{6,4},{7,5},{8,10},{9,11},{10,... | collective-permute-start | bytes 73736 | tf_op jit(solution)/shard_map/ppermute | solution.py:338
  89.8 5.1 %collective-permute-start.25 = (f32[1,96]{1,0:T(1,128)S(1)}, f32[1,96]{1,0:T(1,128)S(1)}, u32[]{:S(2)}, u32[]{:S(2)}) collective-permute-start(f32[1,96]{1,0:T(1,128)S(1)} %reshape.12), channel_id=1, source_target_pairs={{0,4},{4,0},{8,12},{12,8},{1,5},{5,1},{9,13},{13,9},{2,6},{6,2},{1... | collective-permute-start | bytes 1160 | tf_op jit(solution)/shard_map/ppermute | solution.py:348
  89.9 5.0 %collective-permute-start.26 = (f32[1,96]{1,0:T(1,128)S(1)}, f32[1,96]{1,0:T(1,128)S(1)}, u32[]{:S(2)}, u32[]{:S(2)}) collective-permute-start(f32[1,96]{1,0:T(1,128)S(1)} %reshape.12), channel_id=1, source_target_pairs={{0,8},{4,12},{8,0},{12,4},{1,9},{5,13},{9,1},{13,5},{2,10},{6,14},... | collective-permute-start | bytes 1160 | tf_op jit(solution)/shard_map/ppermute | solution.py:348
  91.6 5.3 %collective-permute-start.27 = (f32[1,96]{1,0:T(1,128)S(1)}, f32[1,96]{1,0:T(1,128)S(1)}, u32[]{:S(2)}, u32[]{:S(2)}) collective-permute-start(f32[1,96]{1,0:T(1,128)S(1)} %reshape.12), channel_id=1, source_target_pairs={{0,12},{4,8},{8,4},{12,0},{1,13},{5,9},{9,5},{13,1},{2,14},{6,10},... | collective-permute-start | bytes 1160 | tf_op jit(solution)/shard_map/ppermute | solution.py:348

commit v8 on v7

--- a/solution.py
+++ b/solution.py
@@ -75,27 +75,7 @@
     return out, basis, turned
 
 
-def pull_kernel(acts_ref, grads_ref, turned_ref, basis_ref, after_ref, *rest):
-    outs, (tokens_ref, theirs_ref, sems) = rest[:-3], rest[-3:]
-
-    def copies(mine, theirs):
-        return [
-            pltpu.make_async_copy(mine, tokens_ref, sems.at[0]),
-            pltpu.make_async_copy(theirs, theirs_ref, sems.at[1]),
-        ]
-
-    side = lax.axis_index("parts")
-
-    @pl.when(side == 0)
-    def _():
-        for copy in copies(acts_ref, grads_ref):
-            copy.start()
-
-    @pl.when(side != 0)
-    def _():
-        for copy in copies(grads_ref, acts_ref):
-            copy.start()
-
+def pull_kernel(turned_ref, basis_ref, after_ref, *outs):
     rows, features = outs[0].shape
     block = 512 if features % 512 == 0 else features
     for i in range(features // block):
@@ -104,21 +84,51 @@
         ).astype(jnp.bfloat16)
         for c, out in enumerate(outs):
             out[:, i * block : (i + 1) * block] = pulled[c * rows : (c + 1) * rows]
+
+
+def pull(after, turned, basis, rows):
+    chunks = turned.shape[0] // rows - 1
+    return pl.pallas_call(
+        pull_kernel,
+        out_shape=[bf16(rows, basis.shape[0])] * chunks,
+        in_specs=[VMEM, VMEM, ANY],
+        out_specs=[VMEM] * chunks,
+        compiler_params=pltpu.CompilerParams(vmem_limit_bytes=16 * MIB),
+    )(turned, basis, after)
+
+
+def deal_kernel(acts_ref, grads_ref, after_ref, mine_ref, theirs_ref, sems):
+    def copies(mine, theirs):
+        return [
+            pltpu.make_async_copy(mine, mine_ref, sems.at[0]),
+            pltpu.make_async_copy(theirs, theirs_ref, sems.at[1]),
+        ]
+
+    side = lax.axis_index("parts")
+
+    @pl.when(side == 0)
+    def _():
+        for copy in copies(acts_ref, grads_ref):
+            copy.start()
+
+    @pl.when(side != 0)
+    def _():
+        for copy in copies(grads_ref, acts_ref):
+            copy.start()
+
     for copy in copies(acts_ref, grads_ref):
         copy.wait()
 
 
-def pull(after, turned, basis, acts, grads, rows):
-    chunks = turned.shape[0] // rows - 1
-    out = pl.pallas_call(
-        pull_kernel,
-        out_shape=[bf16(rows, basis.shape[0])] * chunks + [bf16(*acts.shape)] * 2,
-        in_specs=[HBM, HBM, VMEM, VMEM, ANY],
-        out_specs=[VMEM] * (chunks + 2),
+def deal(after, acts, grads):
+    return pl.pallas_call(
+        deal_kernel,
+        out_shape=[bf16(*acts.shape)] * 2,
+        in_specs=[HBM, HBM, ANY],
+        out_specs=[VMEM, VMEM],
         scratch_shapes=[pltpu.SemaphoreType.DMA((2,))],
-        compiler_params=pltpu.CompilerParams(vmem_limit_bytes=24 * MIB),
-    )(*in_hbm(acts, grads), turned, basis, after)
-    return list(out[:chunks]), out[-2], out[-1]
+        compiler_params=pltpu.CompilerParams(vmem_limit_bytes=8 * MIB),
+    )(*in_hbm(acts, grads), after)
 
 
 def at_depth(hop):
@@ -206,25 +216,26 @@
     product = own * other.astype(jnp.float32)
     queries, tokens = product.shape[0] // RANK, product.shape[1]
     scores = jnp.sum(product.reshape(queries, RANK, tokens), axis=1) * RANK ** (-0.5)
+    out_ref[...] = jnp.zeros(out_ref.shape, jnp.float32)
     out_ref[:, :tokens] = scores
     position = lax.broadcasted_iota(jnp.int32, scores.shape, 1)
-    column = lax.broadcasted_iota(jnp.int32, (queries, LANES), 1)
-    pooled = jnp.zeros((queries, LANES), jnp.float32)
+    docs = counts_ref.shape[1]
+    column = lax.broadcasted_iota(jnp.int32, (queries, docs), 1)
+    pooled = jnp.zeros((queries, docs), jnp.float32)
     start = jnp.int32(0)
-    for k in range(counts_ref.shape[1]):
+    for k in range(docs):
         count = counts_ref[0, k]
         inside = (position >= start) & (position < start + count)
         found = jnp.sum(jnp.where(inside, scores, 0.0), axis=1, keepdims=True)
         root = jnp.sqrt(jnp.full((1, 1), count, jnp.int32).astype(jnp.float32))
         pooled = jnp.where(column == k, found / root, pooled)
         start = start + count
-    out_ref[:, out_ref.shape[1] - LANES :] = pooled
+    out_ref[:, tokens : tokens + pooled.shape[1]] = pooled
 
 
 def score(counts, own, other):
     rows = sum(piece.shape[0] for piece in own)
-    tokens = own[0].shape[1]
-    width = (tokens + LANES - 1) // LANES * LANES + LANES
+    width = (own[0].shape[1] + counts.shape[1] + LANES - 1) // LANES * LANES
     return pl.pallas_call(
         functools.partial(score_kernel, len(own)),
         out_shape=jax.ShapeDtypeStruct((rows // RANK, width), jnp.float32),
@@ -266,8 +277,8 @@
     first, basis, turned = first_pull(
         basis_in[0], output_eigen_basis[0], query_in[0], query_out[0], rows
     )
-    own, tokens, theirs = pull(first, turned, basis, acts[0], grads[0], rows)
-    own = [first] + own
+    own = [first] + list(pull(first, turned, basis, rows))
+    tokens, theirs = deal(own[-1], acts[0], grads[0])
     swap = [(0, 1), (1, 0)]
 
     stages = [("in", hop) for hop in range(half - 1)] + [("mid", 0)]
@@ -327,7 +338,7 @@
                 came[c] = transfer(stages[s + 1][:1], stages[s + 1][1], part[c])
             else:
                 waiting.append(part[c])
-        if turn >= chunks - 1 and waiting:
+        if turn >= chunks + last - 2 and waiting:
             after = project_waiting(after)
 
     scores = score(doc_counts, mine, back)
@@ -336,11 +347,11 @@
     else:
         for step in [1 << k for k in range(layers.bit_length() - 1)]:
             scores = scores + lax.ppermute(scores, "layer", [(i, i ^ step) for i in range(layers)])
-    token_scores, pooled = scores[:, : acts.shape[1]], scores[:, -LANES:]
-
-    docs = doc_counts.shape[1]
+    tokens_here, docs = acts.shape[1], doc_counts.shape[1]
+    token_scores, pooled = scores[:, :tokens_here], scores[:, tokens_here : tokens_here + docs]
+
     cells = queries * docs
-    flat = pooled[:, :docs].reshape(1, cells)
+    flat = pooled.reshape(1, cells)
     target = pair_device[:, 0]
     cell = pair_query * docs + pair_doc
     if n <= 8 and is_power(n):

time: 98.2 us -> 94.6 us (0.963)
  waiting for transfers between devices: 26.9 us -> 22 us
  starting transfers between devices: 55.3 us -> 57.8 us
    ppermute x19, waiting for transfers between devices: 18.4 us -> 13 us  [transfer(): return lax.ppermute(value, 'dp', pairs)]
    ppermute x19, starting transfers between devices: 44.6 us -> 47 us  [transfer(): return lax.ppermute(value, 'dp', pairs)]
    pallas_call x0 -> x1, Pallas kernels: none -> 1.95 us  [deal(): pl.pallas_call(deal_kernel, out_shape=[bf16(*acts.shape)] * 2, in_specs=[...]
    pallas_call x1, Pallas kernels: 3.21 us -> 1.53 us  [pull(): pl.pallas_call(pull_kernel, out_shape=[bf16(rows, basis.shape[0])] * chun...]
    ppermute x3 -> x2, starting transfers between devices: 1.68 us -> 3.3 us  [project_waiting(): back.append(lax.ppermute(away, 'parts', swap))]
    ppermute x1, starting transfers between devices: 3.03 us -> 1.58 us  [per_device(): others = lax.ppermute(theirs, 'parts', swap)]
    ppermute x3, waiting for transfers between devices: 2.07 us -> 3.5 us  [per_device(): lax.ppermute(flat, 'dp', [(i, i ^ k) for i in range(n)])]
    ppermute x3 -> x2, waiting for transfers between devices: 2.87 us -> 1.94 us  [project_waiting(): back.append(lax.ppermute(away, 'parts', swap))]
  transfers between devices with their start and end apart: 28 -> 27, of which waited for: 10 -> 10; matrix products, arithmetic and copies ran while one was open for 1% -> 0% of each run, Pallas kernels for 6% -> 9%
where the time goes in v8:
time: 94.6 us; the launch traced here: 94.2 us
  starting transfers between devices  57.8 us (61%)
  waiting for transfers between devices  22 us (23%)
  Pallas kernels  12.3 us (13%)
  between operations  1.15 us (1%)
    ppermute x19, starting transfers between devices, transfer(): return lax.ppermute(value, 'dp', pairs)  47 us
    ppermute x19, waiting for transfers between devices, transfer(): return lax.ppermute(value, 'dp', pairs)  13 us
    ppermute x3, starting transfers between devices, per_device(): lax.ppermute(flat, 'dp', [(i, i ^ k) for i in range(n)])  4.44 us
    ppermute x2, waiting for transfers between devices, per_device(): lax.ppermute(scores, 'layer', [(i, i ^ step) for i in range(layers)])  3.55 us
    ppermute x3, waiting for transfers between devices, per_device(): lax.ppermute(flat, 'dp', [(i, i ^ k) for i in range(n)])  3.5 us
    pallas_call x1, Pallas kernels, first_pull(): pl.pallas_call(first_pull_kernel, out_shape=[bf16(rows, features), bf16(f...  3.44 us
    ppermute x2, starting transfers between devices, project_waiting(): back.append(lax.ppermute(away, 'parts', swap))  3.3 us
    pallas_call x4, Pallas kernels, project(): pl.pallas_call(project_kernel, out_shape=jax.ShapeDtypeStruct((rows, toke...  3.29 us
  transfers between devices with their start and end apart: 27, of which 10 were waited for; matrix products, arithmetic and copies ran while one was open for 0% of the time, Pallas kernels for 9%

profile of v8, /device:TPU:0, one launch (start us, length us, event | category | flops | bytes accessed | tf_op | source)
XLA Modules:
  0.0 94.2 jit_solution(3615847728329867246)
XLA Ops:
  0.6 3.4 %shard_map.113 = (bf16[48,2560]{1,0:T(8,128)(2,1)S(1)}, bf16[2560,640]{1,0:T(8,128)(2,1)S(1)}, bf16[640,384]{1,0:T(8,128)(2,1)}, bf16[384,640]{1,0:T(8,128)(2,1)S(1)}) custom-call(bf16[2560,640]{1,0:T(8,128)(2,1)} %bitcast.9, bf16[2560,640]{1,0:T(8,128)(2,1)} %bitcast.10, bf16[640,384]{1,0:T(8,128)(2,1)} %bitcast.13, bf16[640,384]{1,0:T(8,128)(2,1)} %bitcast.14), custom_call_target="tpu_custom_call" | custom-call | tf_op jit(solution)/shard_map/pallas_call | solution.py:67
  4.1 4.9 %collective-permute-start.1 = (bf16[48,2560]{1,0:T(8,128)(2,1)S(1)}, bf16[48,2560]{1,0:T(8,128)(2,1)S(1)}, u32[]{:S(2)}, u32[]{:S(2)}) collective-permute-start(bf16[48,2560]{1,0:T(8,128)(2,1)S(1)} %get-tuple-element.28.after_ref.mine_ref), channel_id=1, source_target_pairs={{0,4},{12,8},{1,5},{13,9},{2,6},{14,10},{3,7},{15,11},{16,20},{28,... | collective-permute-start | bytes 737288 | tf_op jit(solution)/shard_map/ppermute | solution.py:296
  9.0 1.5 %shard_map.114 = (bf16[48,2560]{1,0:T(8,128)(2,1)S(1)}, bf16[48,2560]{1,0:T(8,128)(2,1)S(1)}, bf16[48,2560]{1,0:T(8,128)(2,1)S(1)}, bf16[48,2560]{1,0:T(8,128)(2...) custom-call(bf16[384,640]{1,0:T(8,128)(2,1)S(1)} %get-tuple-element.26.turned_ref,, ...), custom_call_target="tpu_custom_call" | custom-call | tf_op jit(solution)/shard_map/pallas_call | solution.py:91
  10.6 2.0 %shard_map.115 = (bf16[320,2560]{1,0:T(8,128)(2,1)S(1)}, bf16[320,2560]{1,0:T(8,128)(2,1)S(1)}) custom-call(bf16[320,2560]{1,0:T(8,128)(2,1)} %bitcast.11, bf16[320,2560]{1,0:T(8,128)(2,1)} %bitcast.12, bf16[48,2560]{1,0:T(8,128)(2,1)S(1)} %get-tuple-element.29.after_ref.rest_0_.mine_ref), custom_call_target="tpu_custom_call" | custom-call | tf_op jit(solution)/shard_map/pallas_call | solution.py:124
  12.5 1.6 %collective-permute-start = (bf16[320,2560]{1,0:T(8,128)(2,1)S(1)}, bf16[320,2560]{1,0:T(8,128)(2,1)S(1)}, u32[]{:S(2)}, u32[]{:S(2)}) collective-permute-start(bf16[320,2560]{1,0:T(8,128)(2,1)S(1)} %get-tuple-element.31), channel_id=1, source_target_pairs={{0,16},{16,0},{1,17},{17,1},{2,18},{18,2},{3,19},{19,3},{4,20},{20... | collective-permute-start | bytes 4915208 | tf_op jit(solution)/shard_map/ppermute | solution.py:302
  14.1 1.3 %collective-permute-start.3 = (bf16[48,2560]{1,0:T(8,128)(2,1)S(1)}, bf16[48,2560]{1,0:T(8,128)(2,1)S(1)}, u32[]{:S(2)}, u32[]{:S(2)}) collective-permute-start(bf16[48,2560]{1,0:T(8,128)(2,1)S(1)} %get-tuple-element.36.mine_ref), channel_id=1, source_target_pairs={{0,4},{12,8},{1,5},{13,9},{2,6},{14,10},{3,7},{15,11},{16,20},{28,... | collective-permute-start | bytes 737288 | tf_op jit(solution)/shard_map/ppermute | solution.py:296
  15.5 0.7 collective-permute-start.2
  16.2 6.0 %collective-permute-start.6 = (bf16[48,2560]{1,0:T(8,128)(2,1)S(1)}, bf16[48,2560]{1,0:T(8,128)(2,1)S(1)}, u32[]{:S(2)}, u32[]{:S(2)}) collective-permute-start(bf16[48,2560]{1,0:T(8,128)(2,1)S(1)} %get-tuple-element.38), channel_id=1, source_target_pairs={{0,4},{12,8},{1,5},{13,9},{2,6},{14,10},{3,7},{15,11},{16,20},{28,... | collective-permute-start | bytes 737288 | tf_op jit(solution)/shard_map/ppermute | solution.py:296
  23.0 3.9 %collective-permute-start.4 = (bf16[48,2560]{1,0:T(8,128)(2,1)S(1)}, bf16[48,2560]{1,0:T(8,128)(2,1)S(1)}, u32[]{:S(2)}, u32[]{:S(2)}) collective-permute-start(bf16[48,2560]{1,0:T(8,128)(2,1)S(1)} %get-tuple-element.37), channel_id=1, source_target_pairs={{0,4},{12,8},{4,0},{8,12},{1,5},{13,9},{5,1},{9,13},{2,6},{14,10},... | collective-permute-start | bytes 737288 | tf_op jit(solution)/shard_map/ppermute | solution.py:296
  28.2 5.2 %collective-permute-start.8 = (bf16[48,2560]{1,0:T(8,128)(2,1)S(1)}, bf16[48,2560]{1,0:T(8,128)(2,1)S(1)}, u32[]{:S(2)}, u32[]{:S(2)}) collective-permute-start(bf16[48,2560]{1,0:T(8,128)(2,1)S(1)} %get-tuple-element.42), channel_id=1, source_target_pairs={{0,4},{12,8},{4,0},{8,12},{1,5},{13,9},{5,1},{9,13},{2,6},{14,10},... | collective-permute-start | bytes 737288 | tf_op jit(solution)/shard_map/ppermute | solution.py:296
  34.3 5.1 %collective-permute-start.11 = (bf16[48,2560]{1,0:T(8,128)(2,1)S(1)}, bf16[48,2560]{1,0:T(8,128)(2,1)S(1)}, u32[]{:S(2)}, u32[]{:S(2)}) collective-permute-start(bf16[48,2560]{1,0:T(8,128)(2,1)S(1)} %get-tuple-element.46), channel_id=1, source_target_pairs={{0,4},{12,8},{4,0},{8,12},{1,5},{13,9},{5,1},{9,13},{2,6},{14,10},... | collective-permute-start | bytes 737288 | tf_op jit(solution)/shard_map/ppermute | solution.py:296
  40.2 5.9 %collective-permute-start.10 = (bf16[48,2560]{1,0:T(8,128)(2,1)S(1)}, bf16[48,2560]{1,0:T(8,128)(2,1)S(1)}, u32[]{:S(2)}, u32[]{:S(2)}) collective-permute-start(bf16[48,2560]{1,0:T(8,128)(2,1)S(1)} %get-tuple-element.45), channel_id=1, source_target_pairs={{0,4},{12,8},{4,0},{8,12},{1,5},{13,9},{5,1},{9,13},{2,6},{14,10},... | collective-permute-start | bytes 737288 | tf_op jit(solution)/shard_map/ppermute | solution.py:296
  47.0 5.3 %collective-permute-start.14 = (bf16[48,2560]{1,0:T(8,128)(2,1)S(1)}, bf16[48,2560]{1,0:T(8,128)(2,1)S(1)}, u32[]{:S(2)}, u32[]{:S(2)}) collective-permute-start(bf16[48,2560]{1,0:T(8,128)(2,1)S(1)} %get-tuple-element.49), channel_id=1, source_target_pairs={{0,4},{12,8},{4,0},{8,12},{1,5},{13,9},{5,1},{9,13},{2,6},{14,10},... | collective-permute-start | bytes 737288 | tf_op jit(solution)/shard_map/ppermute | solution.py:296
  53.5 1.3 %collective-permute-start.18 = (bf16[48,2560]{1,0:T(8,128)(2,1)S(1)}, bf16[48,2560]{1,0:T(8,128)(2,1)S(1)}, u32[]{:S(2)}, u32[]{:S(2)}) collective-permute-start(bf16[48,2560]{1,0:T(8,128)(2,1)S(1)} %shard_map.131.after_ref.mine_ref), channel_id=1, source_target_pairs={{4,0},{8,12},{5,1},{9,13},{6,2},{10,14},{7,3},{11,15},{20,16},{24,... | collective-permute-start | bytes 737288 | tf_op jit(solution)/shard_map/ppermute | solution.py:296
  54.8 3.8 %collective-permute-done.14.came_ref = bf16[48,2560]{1,0:T(8,128)(2,1)S(1)} collective-permute-done((bf16[48,2560]{1,0:T(8,128)(2,1)S(1)}, bf16[48,2560]{1,0:T(8,128)(2,1)S(1)}, u32[]{:S(2)}, u32[]{:S(2)}) %collective-permute-start.14) | collective-permute-done | bytes 245792 | tf_op jit(solution)/shard_map/ppermute | solution.py:296
  59.5 1.3 %collective-permute-start.16 = (bf16[48,2560]{1,0:T(8,128)(2,1)S(1)}, bf16[48,2560]{1,0:T(8,128)(2,1)S(1)}, u32[]{:S(2)}, u32[]{:S(2)}) collective-permute-start(bf16[48,2560]{1,0:T(8,128)(2,1)S(1)} %shard_map.134.after_ref.mine_ref), channel_id=1, source_target_pairs={{4,0},{8,12},{5,1},{9,13},{6,2},{10,14},{7,3},{11,15},{20,16},{24,... | collective-permute-start | bytes 737288 | tf_op jit(solution)/shard_map/ppermute | solution.py:296
  60.8 5.4 %collective-permute-done.18.came_ref = bf16[48,2560]{1,0:T(8,128)(2,1)S(1)} collective-permute-done((bf16[48,2560]{1,0:T(8,128)(2,1)S(1)}, bf16[48,2560]{1,0:T(8,128)(2,1)S(1)}, u32[]{:S(2)}, u32[]{:S(2)}) %collective-permute-start.18) | collective-permute-done | bytes 245792 | tf_op jit(solution)/shard_map/ppermute | solution.py:296
  66.3 1.3 %collective-permute-start.19 = (bf16[48,2560]{1,0:T(8,128)(2,1)S(1)}, bf16[48,2560]{1,0:T(8,128)(2,1)S(1)}, u32[]{:S(2)}, u32[]{:S(2)}) collective-permute-start(bf16[48,2560]{1,0:T(8,128)(2,1)S(1)} %shard_map.137.after_ref.mine_ref), channel_id=1, source_target_pairs={{4,0},{8,12},{5,1},{9,13},{6,2},{10,14},{7,3},{11,15},{20,16},{24,... | collective-permute-start | bytes 737288 | tf_op jit(solution)/shard_map/ppermute | solution.py:296
  67.6 3.1 %collective-permute-done.16.came_ref = bf16[48,2560]{1,0:T(8,128)(2,1)S(1)} collective-permute-done((bf16[48,2560]{1,0:T(8,128)(2,1)S(1)}, bf16[48,2560]{1,0:T(8,128)(2,1)S(1)}, u32[]{:S(2)}, u32[]{:S(2)}) %collective-permute-start.16) | collective-permute-done | bytes 245792 | tf_op jit(solution)/shard_map/ppermute | solution.py:296
  70.7 1.1 %shard_map.139.after_ref = bf16[336,320]{1,0:T(8,128)(2,1)S(1)} custom-call(bf16[320,2560]{1,0:T(8,128)(2,1)S(1)} %collective-permute-done.tokens_ref, bf16[48,2560]{1,0:T(8,128)(2,1)S(1)} %shard_map.138.after_ref.rest_6_, bf16[48,2560]{1,0:T(8,128)(2,1)S(1)} %shard_map.123.after_ref.rest_0_, bf16[48,2560]{1,0:T(8,128)(2,1)S(1)} %shard_map.126.after_ref.rest_1_, ...), custom_call_target="tpu_custom_call" | custom-call | tf_op jit(solution)/shard_map/pallas_call | solution.py:203
  71.8 1.8 %collective-permute-start.20 = (bf16[336,320]{1,0:T(8,128)(2,1)S(1)}, bf16[336,320]{1,0:T(8,128)(2,1)S(1)}, u32[]{:S(2)}, u32[]{:S(2)}) collective-permute-start(bf16[336,320]{1,0:T(8,128)(2,1)S(1)} %shard_map.139.after_ref), channel_id=1, source_target_pairs={{0,16},{16,0},{1,17},{17,1},{2,18},{18,2},{3,19},{19,3},{4,20},{20... | collective-permute-start | bytes 645128 | tf_op jit(solution)/shard_map/ppermute | solution.py:308
  73.6 1.1 %shard_map.140.after_ref.refs_0_ = f32[336,320]{1,0:T(8,128)S(1)} custom-call(bf16[320,2560]{1,0:T(8,128)(2,1)S(1)} %get-tuple-element.30.tokens_ref, bf16[336,320]{1,0:T(8,128)(2,1)S(1)} %shard_map.139.after_ref, bf16[48,2560]{1,0:T(8,128)(2,1)S(1)} %shard_map.123.after_ref.rest_0_, bf16[48,2560]{1,0:T(8,128)(2,1)S(1)} %shard_map.126.after_ref.rest_1_, ...), custom_call_target="tpu_custom_call" | custom-call | tf_op jit(solution)/shard_map/pallas_call | solution.py:203
  75.3 1.5 %collective-permute-start.21 = (bf16[48,320]{1,0:T(8,128)(2,1)S(1)}, bf16[48,320]{1,0:T(8,128)(2,1)S(1)}, u32[]{:S(2)}, u32[]{:S(2)}) collective-permute-start(bf16[48,320]{1,0:T(8,128)(2,1)S(1)} %shard_map.142.after_ref), channel_id=1, source_target_pairs={{0,16},{16,0},{1,17},{17,1},{2,18},{18,2},{3,19},{19,3},{4,20},{20... | collective-permute-start | bytes 92168 | tf_op jit(solution)/shard_map/ppermute | solution.py:308
  77.4 1.9 %collective-permute-done.21.refs_3_ = bf16[48,320]{1,0:T(8,128)(2,1)S(1)} collective-permute-done((bf16[48,320]{1,0:T(8,128)(2,1)S(1)}, bf16[48,320]{1,0:T(8,128)(2,1)S(1)}, u32[]{:S(2)}, u32[]{:S(2)}) %collective-permute-start.21) | collective-permute-done | bytes 30752 | tf_op jit(solution)/shard_map/ppermute | solution.py:308
  79.4 0.8 shard_map.144
  80.2 1.2 %collective-permute-done.22 = f32[12,384]{1,0:T(8,128)S(1)} collective-permute-done((f32[12,384]{1,0:T(8,128)S(1)}, f32[12,384]{1,0:T(8,128)S(1)}, u32[]{:S(2)}, u32[]{:S(2)}) %collective-permute-start.22) | collective-permute-done | bytes 18464 | tf_op jit(solution)/shard_map/ppermute | solution.py:349
  81.4 1.5 %collective-permute-start.23 = (f32[12,384]{1,0:T(8,128)S(1)}, f32[12,384]{1,0:T(8,128)S(1)}, u32[]{:S(2)}, u32[]{:S(2)}) collective-permute-start(f32[12,384]{1,0:T(8,128)S(1)} %add.12), channel_id=1, source_target_pairs={{0,2},{1,3},{2,0},{3,1},{4,6},{5,7},{6,4},{7,5},{8,10},{9,11},{10,... | collective-permute-start | bytes 55304 | tf_op jit(solution)/shard_map/ppermute | solution.py:349
  82.9 2.4 %collective-permute-done.23 = f32[12,384]{1,0:T(8,128)S(1)} collective-permute-done((f32[12,384]{1,0:T(8,128)S(1)}, f32[12,384]{1,0:T(8,128)S(1)}, u32[]{:S(2)}, u32[]{:S(2)}) %collective-permute-start.23) | collective-permute-done | bytes 18464 | tf_op jit(solution)/shard_map/ppermute | solution.py:349
  85.5 2.6 %collective-permute-start.25 = (f32[1,96]{1,0:T(1,128)S(1)}, f32[1,96]{1,0:T(1,128)S(1)}, u32[]{:S(2)}, u32[]{:S(2)}) collective-permute-start(f32[1,96]{1,0:T(1,128)S(1)} %reshape.12), channel_id=1, source_target_pairs={{0,8},{4,12},{8,0},{12,4},{1,9},{5,13},{9,1},{13,5},{2,10},{6,14},... | collective-permute-start | bytes 1160 | tf_op jit(solution)/shard_map/ppermute | solution.py:359
  88.0 1.8 %collective-permute-start.26 = (f32[1,96]{1,0:T(1,128)S(1)}, f32[1,96]{1,0:T(1,128)S(1)}, u32[]{:S(2)}, u32[]{:S(2)}) collective-permute-start(f32[1,96]{1,0:T(1,128)S(1)} %reshape.12), channel_id=1, source_target_pairs={{0,12},{4,8},{8,4},{12,0},{1,13},{5,9},{9,5},{13,1},{2,14},{6,10},... | collective-permute-start | bytes 1160 | tf_op jit(solution)/shard_map/ppermute | solution.py:359
  90.0 3.4 %collective-permute-done.26 = f32[1,96]{1,0:T(1,128)S(1)} collective-permute-done((f32[1,96]{1,0:T(1,128)S(1)}, f32[1,96]{1,0:T(1,128)S(1)}, u32[]{:S(2)}, u32[]{:S(2)}) %collective-permute-start.26) | collective-permute-done | bytes 416 | tf_op jit(solution)/shard_map/ppermute | solution.py:359
  93.5 0.7 select_reduce_fusion
  (71 shorter events, 8.3 us)
Async XLA Ops:
  4.1 11.3 %collective-permute-start.1 = (bf16[48,2560]{1,0:T(8,128)(2,1)S(1)}, bf16[48,2560]{1,0:T(8,128)(2,1)S(1)}, u32[]{:S(2)}, u32[]{:S(2)}) collective-permute-start(bf16[48,2560]{1,0:T(8,128)(2,1)S(1)} %get-tuple-element.28.after_ref.mine_ref), channel_id=1, source_target_pairs={{0,4},{12,8},{1,5},{13,9},{2,6},{14,10},{3,7},{15,11},{16,20},{28,... | collective-permute-start | bytes 737288 | tf_op jit(solution)/shard_map/ppermute | solution.py:296
  12.5 58.2 %collective-permute-start = (bf16[320,2560]{1,0:T(8,128)(2,1)S(1)}, bf16[320,2560]{1,0:T(8,128)(2,1)S(1)}, u32[]{:S(2)}, u32[]{:S(2)}) collective-permute-start(bf16[320,2560]{1,0:T(8,128)(2,1)S(1)} %get-tuple-element.31), channel_id=1, source_target_pairs={{0,16},{16,0},{1,17},{17,1},{2,18},{18,2},{3,19},{19,3},{4,20},{20... | collective-permute-start | bytes 4915208 | tf_op jit(solution)/shard_map/ppermute | solution.py:302
  14.1 8.1 %collective-permute-start.3 = (bf16[48,2560]{1,0:T(8,128)(2,1)S(1)}, bf16[48,2560]{1,0:T(8,128)(2,1)S(1)}, u32[]{:S(2)}, u32[]{:S(2)}) collective-permute-start(bf16[48,2560]{1,0:T(8,128)(2,1)S(1)} %get-tuple-element.36.mine_ref), channel_id=1, source_target_pairs={{0,4},{12,8},{1,5},{13,9},{2,6},{14,10},{3,7},{15,11},{16,20},{28,... | collective-permute-start | bytes 737288 | tf_op jit(solution)/shard_map/ppermute | solution.py:296
  15.5 7.4 %collective-permute-start.2 = (bf16[48,2560]{1,0:T(8,128)(2,1)S(1)}, bf16[48,2560]{1,0:T(8,128)(2,1)S(1)}, u32[]{:S(2)}, u32[]{:S(2)}) collective-permute-start(bf16[48,2560]{1,0:T(8,128)(2,1)S(1)} %get-tuple-element.35.after_ref.mine_ref), channel_id=1, source_target_pairs={{4,8},{8,4},{5,9},{9,5},{6,10},{10,6},{7,11},{11,7},{20,24},{24,20... | collective-permute-start | bytes 737288 | tf_op jit(solution)/shard_map/ppermute | solution.py:296
  16.2 11.2 %collective-permute-start.6 = (bf16[48,2560]{1,0:T(8,128)(2,1)S(1)}, bf16[48,2560]{1,0:T(8,128)(2,1)S(1)}, u32[]{:S(2)}, u32[]{:S(2)}) collective-permute-start(bf16[48,2560]{1,0:T(8,128)(2,1)S(1)} %get-tuple-element.38), channel_id=1, source_target_pairs={{0,4},{12,8},{1,5},{13,9},{2,6},{14,10},{3,7},{15,11},{16,20},{28,... | collective-permute-start | bytes 737288 | tf_op jit(solution)/shard_map/ppermute | solution.py:296
  22.3 5.8 %collective-permute-start.5 = (bf16[48,2560]{1,0:T(8,128)(2,1)S(1)}, bf16[48,2560]{1,0:T(8,128)(2,1)S(1)}, u32[]{:S(2)}, u32[]{:S(2)}) collective-permute-start(bf16[48,2560]{1,0:T(8,128)(2,1)S(1)} %shard_map.117.after_ref.mine_ref), channel_id=1, source_target_pairs={{4,8},{8,4},{5,9},{9,5},{6,10},{10,6},{7,11},{11,7},{20,24},{24,20... | collective-permute-start | bytes 737288 | tf_op jit(solution)/shard_map/ppermute | solution.py:296
  23.0 10.4 %collective-permute-start.4 = (bf16[48,2560]{1,0:T(8,128)(2,1)S(1)}, bf16[48,2560]{1,0:T(8,128)(2,1)S(1)}, u32[]{:S(2)}, u32[]{:S(2)}) collective-permute-start(bf16[48,2560]{1,0:T(8,128)(2,1)S(1)} %get-tuple-element.37), channel_id=1, source_target_pairs={{0,4},{12,8},{4,0},{8,12},{1,5},{13,9},{5,1},{9,13},{2,6},{14,10},... | collective-permute-start | bytes 737288 | tf_op jit(solution)/shard_map/ppermute | solution.py:296
  27.4 6.8 %collective-permute-start.9 = (bf16[48,2560]{1,0:T(8,128)(2,1)S(1)}, bf16[48,2560]{1,0:T(8,128)(2,1)S(1)}, u32[]{:S(2)}, u32[]{:S(2)}) collective-permute-start(bf16[48,2560]{1,0:T(8,128)(2,1)S(1)} %shard_map.119.after_ref.mine_ref), channel_id=1, source_target_pairs={{4,8},{8,4},{5,9},{9,5},{6,10},{10,6},{7,11},{11,7},{20,24},{24,20... | collective-permute-start | bytes 737288 | tf_op jit(solution)/shard_map/ppermute | solution.py:296
  28.2 11.2 %collective-permute-start.8 = (bf16[48,2560]{1,0:T(8,128)(2,1)S(1)}, bf16[48,2560]{1,0:T(8,128)(2,1)S(1)}, u32[]{:S(2)}, u32[]{:S(2)}) collective-permute-start(bf16[48,2560]{1,0:T(8,128)(2,1)S(1)} %get-tuple-element.42), channel_id=1, source_target_pairs={{0,4},{12,8},{4,0},{8,12},{1,5},{13,9},{5,1},{9,13},{2,6},{14,10},... | collective-permute-start | bytes 737288 | tf_op jit(solution)/shard_map/ppermute | solution.py:296
  33.5 6.6 %collective-permute-start.7 = (bf16[48,2560]{1,0:T(8,128)(2,1)S(1)}, bf16[48,2560]{1,0:T(8,128)(2,1)S(1)}, u32[]{:S(2)}, u32[]{:S(2)}) collective-permute-start(bf16[48,2560]{1,0:T(8,128)(2,1)S(1)} %shard_map.121.after_ref.mine_ref), channel_id=1, source_target_pairs={{4,8},{8,4},{5,9},{9,5},{6,10},{10,6},{7,11},{11,7},{20,24},{24,20... | collective-permute-start | bytes 737288 | tf_op jit(solution)/shard_map/ppermute | solution.py:296
  34.3 11.9 %collective-permute-start.11 = (bf16[48,2560]{1,0:T(8,128)(2,1)S(1)}, bf16[48,2560]{1,0:T(8,128)(2,1)S(1)}, u32[]{:S(2)}, u32[]{:S(2)}) collective-permute-start(bf16[48,2560]{1,0:T(8,128)(2,1)S(1)} %get-tuple-element.46), channel_id=1, source_target_pairs={{0,4},{12,8},{4,0},{8,12},{1,5},{13,9},{5,1},{9,13},{2,6},{14,10},... | collective-permute-start | bytes 737288 | tf_op jit(solution)/shard_map/ppermute | solution.py:296
  39.4 7.5 %collective-permute-start.12 = (bf16[48,2560]{1,0:T(8,128)(2,1)S(1)}, bf16[48,2560]{1,0:T(8,128)(2,1)S(1)}, u32[]{:S(2)}, u32[]{:S(2)}) collective-permute-start(bf16[48,2560]{1,0:T(8,128)(2,1)S(1)} %shard_map.124.after_ref.mine_ref), channel_id=1, source_target_pairs={{4,8},{8,4},{5,9},{9,5},{6,10},{10,6},{7,11},{11,7},{20,24},{24,20... | collective-permute-start | bytes 737288 | tf_op jit(solution)/shard_map/ppermute | solution.py:296
  40.2 12.4 %collective-permute-start.10 = (bf16[48,2560]{1,0:T(8,128)(2,1)S(1)}, bf16[48,2560]{1,0:T(8,128)(2,1)S(1)}, u32[]{:S(2)}, u32[]{:S(2)}) collective-permute-start(bf16[48,2560]{1,0:T(8,128)(2,1)S(1)} %get-tuple-element.45), channel_id=1, source_target_pairs={{0,4},{12,8},{4,0},{8,12},{1,5},{13,9},{5,1},{9,13},{2,6},{14,10},... | collective-permute-start | bytes 737288 | tf_op jit(solution)/shard_map/ppermute | solution.py:296
  46.3 7.1 %collective-permute-start.15 = (bf16[48,2560]{1,0:T(8,128)(2,1)S(1)}, bf16[48,2560]{1,0:T(8,128)(2,1)S(1)}, u32[]{:S(2)}, u32[]{:S(2)}) collective-permute-start(bf16[48,2560]{1,0:T(8,128)(2,1)S(1)} %shard_map.127.after_ref.mine_ref), channel_id=1, source_target_pairs={{4,8},{8,4},{5,9},{9,5},{6,10},{10,6},{7,11},{11,7},{20,24},{24,20... | collective-permute-start | bytes 737288 | tf_op jit(solution)/shard_map/ppermute | solution.py:296
  47.0 11.6 %collective-permute-start.14 = (bf16[48,2560]{1,0:T(8,128)(2,1)S(1)}, bf16[48,2560]{1,0:T(8,128)(2,1)S(1)}, u32[]{:S(2)}, u32[]{:S(2)}) collective-permute-start(bf16[48,2560]{1,0:T(8,128)(2,1)S(1)} %get-tuple-element.49), channel_id=1, source_target_pairs={{0,4},{12,8},{4,0},{8,12},{1,5},{13,9},{5,1},{9,13},{2,6},{14,10},... | collective-permute-start | bytes 737288 | tf_op jit(solution)/shard_map/ppermute | solution.py:296
  52.7 6.7 %collective-permute-start.13 = (bf16[48,2560]{1,0:T(8,128)(2,1)S(1)}, bf16[48,2560]{1,0:T(8,128)(2,1)S(1)}, u32[]{:S(2)}, u32[]{:S(2)}) collective-permute-start(bf16[48,2560]{1,0:T(8,128)(2,1)S(1)} %shard_map.130.after_ref.mine_ref), channel_id=1, source_target_pairs={{4,8},{8,4},{5,9},{9,5},{6,10},{10,6},{7,11},{11,7},{20,24},{24,20... | collective-permute-start | bytes 737288 | tf_op jit(solution)/shard_map/ppermute | solution.py:296
  53.5 12.7 %collective-permute-start.18 = (bf16[48,2560]{1,0:T(8,128)(2,1)S(1)}, bf16[48,2560]{1,0:T(8,128)(2,1)S(1)}, u32[]{:S(2)}, u32[]{:S(2)}) collective-permute-start(bf16[48,2560]{1,0:T(8,128)(2,1)S(1)} %shard_map.131.after_ref.mine_ref), channel_id=1, source_target_pairs={{4,0},{8,12},{5,1},{9,13},{6,2},{10,14},{7,3},{11,15},{20,16},{24,... | collective-permute-start | bytes 737288 | tf_op jit(solution)/shard_map/ppermute | solution.py:296
  58.7 7.5 %collective-permute-start.17 = (bf16[48,2560]{1,0:T(8,128)(2,1)S(1)}, bf16[48,2560]{1,0:T(8,128)(2,1)S(1)}, u32[]{:S(2)}, u32[]{:S(2)}) collective-permute-start(bf16[48,2560]{1,0:T(8,128)(2,1)S(1)} %shard_map.133.after_ref.mine_ref), channel_id=1, source_target_pairs={{4,8},{8,4},{5,9},{9,5},{6,10},{10,6},{7,11},{11,7},{20,24},{24,20... | collective-permute-start | bytes 737288 | tf_op jit(solution)/shard_map/ppermute | solution.py:296
  59.5 11.2 %collective-permute-start.16 = (bf16[48,2560]{1,0:T(8,128)(2,1)S(1)}, bf16[48,2560]{1,0:T(8,128)(2,1)S(1)}, u32[]{:S(2)}, u32[]{:S(2)}) collective-permute-start(bf16[48,2560]{1,0:T(8,128)(2,1)S(1)} %shard_map.134.after_ref.mine_ref), channel_id=1, source_target_pairs={{4,0},{8,12},{5,1},{9,13},{6,2},{10,14},{7,3},{11,15},{20,16},{24,... | collective-permute-start | bytes 737288 | tf_op jit(solution)/shard_map/ppermute | solution.py:296
  66.3 8.4 %collective-permute-start.19 = (bf16[48,2560]{1,0:T(8,128)(2,1)S(1)}, bf16[48,2560]{1,0:T(8,128)(2,1)S(1)}, u32[]{:S(2)}, u32[]{:S(2)}) collective-permute-start(bf16[48,2560]{1,0:T(8,128)(2,1)S(1)} %shard_map.137.after_ref.mine_ref), channel_id=1, source_target_pairs={{4,0},{8,12},{5,1},{9,13},{6,2},{10,14},{7,3},{11,15},{20,16},{24,... | collective-permute-start | bytes 737288 | tf_op jit(solution)/shard_map/ppermute | solution.py:296
  71.8 7.6 %collective-permute-start.20 = (bf16[336,320]{1,0:T(8,128)(2,1)S(1)}, bf16[336,320]{1,0:T(8,128)(2,1)S(1)}, u32[]{:S(2)}, u32[]{:S(2)}) collective-permute-start(bf16[336,320]{1,0:T(8,128)(2,1)S(1)} %shard_map.139.after_ref), channel_id=1, source_target_pairs={{0,16},{16,0},{1,17},{17,1},{2,18},{18,2},{3,19},{19,3},{4,20},{20... | collective-permute-start | bytes 645128 | tf_op jit(solution)/shard_map/ppermute | solution.py:308
  74.7 4.7 %copy-start = (s32[1,8]{1,0:T(1,128)S(1)}, s32[1,8]{1,0:T(1,128)}, u32[]{:S(2)}) copy-start(s32[1,8]{1,0:T(1,128)} %counts_ref.1) | copy-start | bytes 100
  75.3 14.6 %copy-start.2 = (s32[128]{0:T(128)S(1)}, s32[128]{0:T(128)}, u32[]{:S(2)}) copy-start(s32[128]{0:T(128)} %param.19) | copy-start | bytes 1540
  75.3 14.5 %copy-start.3 = (s32[128]{0:T(128)S(1)}, s32[128]{0:T(128)}, u32[]{:S(2)}) copy-start(s32[128]{0:T(128)} %param.17) | copy-start | bytes 1540
  75.3 14.5 %copy-start.4 = (s32[128,1]{0,1:T(1,128)S(1)}, s32[128,1]{0,1:T(1,128)}, u32[]{:S(2)}) copy-start(s32[128,1]{0,1:T(1,128)} %param.18) | copy-start | bytes 1540
  75.3 4.0 %collective-permute-start.21 = (bf16[48,320]{1,0:T(8,128)(2,1)S(1)}, bf16[48,320]{1,0:T(8,128)(2,1)S(1)}, u32[]{:S(2)}, u32[]{:S(2)}) collective-permute-start(bf16[48,320]{1,0:T(8,128)(2,1)S(1)} %shard_map.142.after_ref), channel_id=1, source_target_pairs={{0,16},{16,0},{1,17},{17,1},{2,18},{18,2},{3,19},{19,3},{4,20},{20... | collective-permute-start | bytes 92168 | tf_op jit(solution)/shard_map/ppermute | solution.py:308
  80.2 1.2 %collective-permute-start.22 = (f32[12,384]{1,0:T(8,128)S(1)}, f32[12,384]{1,0:T(8,128)S(1)}, u32[]{:S(2)}, u32[]{:S(2)}) collective-permute-start(f32[12,384]{1,0:T(8,128)S(1)} %shard_map.144), channel_id=1, source_target_pairs={{0,1},{1,0},{2,3},{3,2},{4,5},{5,4},{6,7},{7,6},{8,9},{9,8},{10,11... | collective-permute-start | bytes 55304 | tf_op jit(solution)/shard_map/ppermute | solution.py:349
  81.4 3.8 %collective-permute-start.23 = (f32[12,384]{1,0:T(8,128)S(1)}, f32[12,384]{1,0:T(8,128)S(1)}, u32[]{:S(2)}, u32[]{:S(2)}) collective-permute-start(f32[12,384]{1,0:T(8,128)S(1)} %add.12), channel_id=1, source_target_pairs={{0,2},{1,3},{2,0},{3,1},{4,6},{5,7},{6,4},{7,5},{8,10},{9,11},{10,... | collective-permute-start | bytes 55304 | tf_op jit(solution)/shard_map/ppermute | solution.py:349
  85.2 8.9 %copy-start.1 = (f32[12,384]{1,0:T(8,128)}, f32[12,384]{1,0:T(8,128)S(1)}, u32[]{:S(2)}) copy-start(f32[12,384]{1,0:T(8,128)S(1)} %add.13) | copy-start | bytes 55300
  85.4 4.5 %collective-permute-start.24 = (f32[1,96]{1,0:T(1,128)S(1)}, f32[1,96]{1,0:T(1,128)S(1)}, u32[]{:S(2)}, u32[]{:S(2)}) collective-permute-start(f32[1,96]{1,0:T(1,128)S(1)} %reshape.12), channel_id=1, source_target_pairs={{0,4},{4,0},{8,12},{12,8},{1,5},{5,1},{9,13},{13,9},{2,6},{6,2},{1... | collective-permute-start | bytes 1160 | tf_op jit(solution)/shard_map/ppermute | solution.py:359
  85.5 4.5 %collective-permute-start.25 = (f32[1,96]{1,0:T(1,128)S(1)}, f32[1,96]{1,0:T(1,128)S(1)}, u32[]{:S(2)}, u32[]{:S(2)}) collective-permute-start(f32[1,96]{1,0:T(1,128)S(1)} %reshape.12), channel_id=1, source_target_pairs={{0,8},{4,12},{8,0},{12,4},{1,9},{5,13},{9,1},{13,5},{2,10},{6,14},... | collective-permute-start | bytes 1160 | tf_op jit(solution)/shard_map/ppermute | solution.py:359
  88.0 5.3 %collective-permute-start.26 = (f32[1,96]{1,0:T(1,128)S(1)}, f32[1,96]{1,0:T(1,128)S(1)}, u32[]{:S(2)}, u32[]{:S(2)}) collective-permute-start(f32[1,96]{1,0:T(1,128)S(1)} %reshape.12), channel_id=1, source_target_pairs={{0,12},{4,8},{8,4},{12,0},{1,13},{5,9},{9,5},{13,1},{2,14},{6,10},... | collective-permute-start | bytes 1160 | tf_op jit(solution)/shard_map/ppermute | solution.py:359

commit v9 on v8

--- a/solution.py
+++ b/solution.py
@@ -26,7 +26,14 @@
     return jax.ShapeDtypeStruct(shape, jnp.bfloat16)
 
 
-def first_pull_kernel(basis_in_ref, basis_out_ref, query_in_ref, query_out_ref, out_ref, basis_ref, query_ref, turned_ref, sems):
+def at_depth(hop):
+    z = lax.axis_index("dp")
+    return jnp.minimum(z, lax.axis_size("dp") - 1 - z) == hop
+
+
+def first_pull_kernel(
+    basis_in_ref, basis_out_ref, query_in_ref, query_out_ref, out_ref, send_ref, basis_ref, query_ref, turned_ref, sems
+):
     rows = out_ref.shape[0]
     features = basis_ref.shape[0]
     block = 512 if features % 512 == 0 else features
@@ -53,26 +60,29 @@
     landed = copies(basis_in_ref, query_in_ref)
     landed[0].wait()
     turned_ref[...] = query_ref[...].T
+    first = pl.multiple_of(jnp.where(at_depth(0), 0, turned_ref.shape[0] - rows), rows)
+    factors = jnp.concatenate([turned_ref[:rows], turned_ref[pl.ds(first, rows)]], axis=0)
     for copy, span in zip(landed[1:], spans):
         copy.wait()
-        out_ref[:, span] = lax.dot_general(
-            turned_ref[:rows], basis_ref[span], NT, preferred_element_type=jnp.float32
-        ).astype(jnp.bfloat16)
+        pulled = lax.dot_general(factors, basis_ref[span], NT, preferred_element_type=jnp.float32)
+        pulled = pulled.astype(jnp.bfloat16)
+        out_ref[:, span] = pulled[:rows]
+        send_ref[:, span] = pulled[rows:]
 
 
 def first_pull(basis_in, basis_out, query_in, query_out, rows):
     features, depth = basis_in.shape
     spread = query_in.shape[1]
     blocks = features // 512 if features % 512 == 0 else 1
-    out, basis, _, turned = pl.pallas_call(
+    out, send, basis, _, turned = pl.pallas_call(
         first_pull_kernel,
-        out_shape=[bf16(rows, features), bf16(features, depth), bf16(depth, spread), bf16(spread, depth)],
+        out_shape=[bf16(rows, features)] * 2 + [bf16(features, depth), bf16(depth, spread), bf16(spread, depth)],
         in_specs=[HBM] * 4,
-        out_specs=[VMEM] * 4,
+        out_specs=[VMEM] * 5,
         scratch_shapes=[pltpu.SemaphoreType.DMA((1 + blocks,))],
         compiler_params=pltpu.CompilerParams(vmem_limit_bytes=16 * MIB),
     )(*in_hbm(basis_in, basis_out, query_in, query_out))
-    return out, basis, turned
+    return out, send, basis, turned
 
 
 def pull_kernel(turned_ref, basis_ref, after_ref, *outs):
@@ -97,12 +107,15 @@
     )(turned, basis, after)
 
 
-def deal_kernel(acts_ref, grads_ref, after_ref, mine_ref, theirs_ref, sems):
+def deal_kernel(acts_ref, grads_ref, after_ref, *rest):
+    outs, sems = rest[:-1], rest[-1]
+
     def copies(mine, theirs):
-        return [
-            pltpu.make_async_copy(mine, mine_ref, sems.at[0]),
-            pltpu.make_async_copy(theirs, theirs_ref, sems.at[1]),
-        ]
+        pairs, first = [(mine, outs[0])], 0
+        for out in outs[1:]:
+            pairs.append((theirs.at[:, pl.ds(first, out.shape[1])], out))
+            first += out.shape[1]
+        return [pltpu.make_async_copy(source, target, sems.at[i]) for i, (source, target) in enumerate(pairs)]
 
     side = lax.axis_index("parts")
 
@@ -121,19 +134,18 @@
 
 
 def deal(after, acts, grads):
-    return pl.pallas_call(
+    tokens, features = acts.shape
+    larger = features * 3 // 4
+    widths = [larger, features - larger] if larger % LANES == 0 else [features]
+    out = pl.pallas_call(
         deal_kernel,
-        out_shape=[bf16(*acts.shape)] * 2,
+        out_shape=[bf16(tokens, features)] + [bf16(tokens, width) for width in widths],
         in_specs=[HBM, HBM, ANY],
-        out_specs=[VMEM, VMEM],
-        scratch_shapes=[pltpu.SemaphoreType.DMA((2,))],
+        out_specs=[VMEM] * (1 + len(widths)),
+        scratch_shapes=[pltpu.SemaphoreType.DMA((1 + len(widths),))],
         compiler_params=pltpu.CompilerParams(vmem_limit_bytes=8 * MIB),
     )(*in_hbm(acts, grads), after)
-
-
-def at_depth(hop):
-    z = lax.axis_index("dp")
-    return jnp.minimum(z, lax.axis_size("dp") - 1 - z) == hop
+    return out[0], out[1:]
 
 
 def write_send(later_ref, value_ref, send_ref):
@@ -144,6 +156,26 @@
     @pl.when(jnp.logical_not(at_depth(0)))
     def _():
         send_ref[...] = value_ref[...]
+
+
+def pair_kernel(mine_ref, came_ref, early_ref, after_ref, out_ref):
+    @pl.when(at_depth(0))
+    def _():
+        out_ref[...] = (mine_ref[...].astype(jnp.float32) + early_ref[...].astype(jnp.float32)).astype(jnp.bfloat16)
+
+    @pl.when(jnp.logical_not(at_depth(0)))
+    def _():
+        out_ref[...] = (mine_ref[...].astype(jnp.float32) + came_ref[...].astype(jnp.float32)).astype(jnp.bfloat16)
+
+
+def pair(after, mine, came, early):
+    return pl.pallas_call(
+        pair_kernel,
+        out_shape=bf16(*mine.shape),
+        in_specs=[VMEM, VMEM, VMEM, ANY],
+        out_specs=VMEM,
+        compiler_params=pltpu.CompilerParams(vmem_limit_bytes=8 * MIB),
+    )(mine, came, early, after)
 
 
 def total_kernel(shared, mine_ref, came_ref, after_ref, *rest):
@@ -192,21 +224,27 @@
     return out[-1], (out[0] if extra else None)
 
 
-def project_kernel(tokens_ref, after_ref, *rest):
-    factors = jnp.concatenate([ref[...] for ref in rest[:-1]], axis=0)
-    projected = lax.dot_general(factors, tokens_ref[...], NT, preferred_element_type=jnp.float32)
+def project_kernel(parts, after_ref, *rest):
+    factors = jnp.concatenate([ref[...] for ref in rest[parts:-1]], axis=0)
+    projected, first = 0.0, 0
+    for ref in rest[:parts]:
+        width = ref.shape[1]
+        projected += lax.dot_general(
+            factors[:, first : first + width], ref[...], NT, preferred_element_type=jnp.float32
+        )
+        first += width
     rest[-1][...] = projected.astype(rest[-1].dtype)
 
 
 def project(after, factors, tokens, dtype):
     rows = sum(chunk.shape[0] for chunk in factors)
     return pl.pallas_call(
-        project_kernel,
-        out_shape=jax.ShapeDtypeStruct((rows, tokens.shape[0]), dtype),
-        in_specs=[VMEM, ANY] + [VMEM] * len(factors),
+        functools.partial(project_kernel, len(tokens)),
+        out_shape=jax.ShapeDtypeStruct((rows, tokens[0].shape[0]), dtype),
+        in_specs=[ANY] + [VMEM] * (len(tokens) + len(factors)),
         out_specs=VMEM,
         compiler_params=pltpu.CompilerParams(vmem_limit_bytes=16 * MIB),
-    )(tokens, after, *factors)
+    )(after, *tokens, *factors)
 
 
 def score_kernel(count, counts_ref, *refs):
@@ -274,7 +312,7 @@
     rows = chunk_rows(spread)
     chunks = spread // rows
 
-    first, basis, turned = first_pull(
+    first, send, basis, turned = first_pull(
         basis_in[0], output_eigen_basis[0], query_in[0], query_out[0], rows
     )
     own = [first] + list(pull(first, turned, basis, rows))
@@ -295,27 +333,40 @@
             pairs += [(hop + 1, hop), (n - 2 - hop, n - 1 - hop)]
         return lax.ppermute(value, "dp", pairs)
 
+    short = n == 4
     part, came = list(own), [None] * chunks
     ahead = min(2, chunks)
-    for c in range(ahead):
-        came[c] = transfer(stages[0][:1], stages[0][1], part[c])
-    others = lax.ppermute(theirs, "parts", swap)
+    early = came[0] = transfer(("in", "out") if short else ("in",), 0, send)
+    for c in range(1, ahead):
+        came[c] = transfer(("in",), 0, part[c])
+    others = [lax.ppermute(piece, "parts", swap) for piece in theirs]
     after = own[0]
     waiting, mine, back = [], [], []
 
     def project_waiting(after):
-        away = project(after, waiting, others, jnp.bfloat16)
+        factors = [factor for _, factor in sorted(waiting, key=lambda entry: entry[0])]
+        away = project(after, factors, others, jnp.bfloat16)
         back.append(lax.ppermute(away, "parts", swap))
-        mine.append(project(away, waiting, tokens, jnp.float32))
+        mine.append(project(away, factors, [tokens], jnp.float32))
         waiting.clear()
         return mine[-1]
 
     swapped = set()
-    for turn in range(chunks + last):
+    turns = chunks + last - short
+    for turn in range(turns):
         steps = [(s, turn - s) for s in range(last) if 0 <= turn - s < chunks]
         due = [c for c in range(chunks) if c + last + (c in swapped) == turn]
         for s, c in steps + [(last, c) for c in due]:
             kind, hop = stages[s]
+            if short and c == chunks - 1:
+                if s == 0:
+                    after = part[c] = pair(after, own[c], came[c], early)
+                    came[c] = lax.ppermute(part[c], "dp", [(i, i ^ 2) for i in range(n)])
+                elif s == 1:
+                    part[c], _ = total(after, part[c], came[c])
+                    after = part[c]
+                    waiting.append((c, part[c]))
+                continue
             later = turn + ahead if turn + ahead < chunks else None
             if turn >= last - 1:
                 use = later if s == last - 1 else None
@@ -337,8 +388,8 @@
             if s < last:
                 came[c] = transfer(stages[s + 1][:1], stages[s + 1][1], part[c])
             else:
-                waiting.append(part[c])
-        if turn >= chunks + last - 2 and waiting:
+                waiting.append((c, part[c]))
+        if turn >= turns - 2 and waiting:
             after = project_waiting(after)
 
     scores = score(doc_counts, mine, back)

time: 94.6 us -> 92.3 us (0.976)
  waiting for transfers between devices: 22 us -> 20.1 us
    ppermute x19 -> x17, starting transfers between devices: 47 us -> 39.3 us  [transfer(): return lax.ppermute(value, 'dp', pairs)]
    ppermute x1 -> x3, starting transfers between devices: 1.58 us -> 6.84 us  [the longest x1 4.12 us: per_device(): came[c] = lax.ppermute(part[c], 'dp', [(i, i ^ 2) for i in range(n)])]
    ppermute x19 -> x17, waiting for transfers between devices: 13 us -> 10.6 us  [transfer(): return lax.ppermute(value, 'dp', pairs)]
    ppermute x2, starting transfers between devices: 3.3 us -> 5.53 us  [project_waiting(): back.append(lax.ppermute(away, 'parts', swap))]
    ppermute x2, waiting for transfers between devices: 1.94 us -> 3.08 us  [project_waiting(): back.append(lax.ppermute(away, 'parts', swap))]
    pallas_call x6 -> x7, Pallas kernels: 8.68 us -> 8.74 us  [the longest x1 3.6 us: first_pull(): pl.pallas_call(first_pull_kernel, out_shape=[bf16(rows, features)] * 2 +...]
  transfers between devices with their start and end apart: 27 -> 27, of which waited for: 10 -> 13; matrix products, arithmetic and copies ran while one was open for 0% -> 0% of each run, Pallas kernels for 9% -> 8%
where the time goes in v9:
time: 92.3 us; the launch traced here: 92 us
  starting transfers between devices  57.6 us (62%)
  waiting for transfers between devices  20.1 us (22%)
  Pallas kernels  12.2 us (13%)
  between operations  1.06 us (1%)
    ppermute x17, starting transfers between devices, transfer(): return lax.ppermute(value, 'dp', pairs)  39.3 us
    ppermute x17, waiting for transfers between devices, transfer(): return lax.ppermute(value, 'dp', pairs)  10.6 us
    ppermute x2, starting transfers between devices, project_waiting(): back.append(lax.ppermute(away, 'parts', swap))  5.53 us
    ppermute x3, starting transfers between devices, per_device(): lax.ppermute(flat, 'dp', [(i, i ^ k) for i in range(n)])  4.44 us
    ppermute x1, starting transfers between devices, per_device(): came[c] = lax.ppermute(part[c], 'dp', [(i, i ^ 2) for i in range(n)])  4.12 us
    pallas_call x1, Pallas kernels, first_pull(): pl.pallas_call(first_pull_kernel, out_shape=[bf16(rows, features)] * 2 +...  3.6 us
    ppermute x2, waiting for transfers between devices, per_device(): lax.ppermute(scores, 'layer', [(i, i ^ step) for i in range(layers)])  3.52 us
    pallas_call x4, Pallas kernels, project(): pl.pallas_call(functools.partial(project_kernel, len(tokens)), out_shape=...  3.18 us
  transfers between devices with their start and end apart: 27, of which 13 were waited for; matrix products, arithmetic and copies ran while one was open for 0% of the time, Pallas kernels for 8%

profile of v9, /device:TPU:0, one launch (start us, length us, event | category | flops | bytes accessed | tf_op | source)
XLA Modules:
  0.0 92.0 jit_solution(3496321654569032382)
XLA Ops:
  0.6 3.6 %shard_map.113 = (bf16[48,2560]{1,0:T(8,128)(2,1)S(1)}, bf16[48,2560]{1,0:T(8,128)(2,1)S(1)}, bf16[2560,640]{1,0:T(8,128)(2,1)S(1)}, bf16[640,384]{1,0:T(8,128)(2,1)}, bf16[384,640]{1,0:T(8,128)(2,1)S(1)}) custom-call(bf16[2560,640]{1,0:T(8,128)(2,1)} %bitcast.9, bf16[2560,640]{1,0:T(8,128)(2,1)} %bitcast.10, bf16[640,384]{1,0:T(8,128)(2,1)} %bitcast.13, ...), custom_call_target="tpu_custom_call" | custom-call | tf_op jit(solution)/shard_map/pallas_call | solution.py:77
  4.2 3.1 %collective-permute-start = (bf16[48,2560]{1,0:T(8,128)(2,1)S(1)}, bf16[48,2560]{1,0:T(8,128)(2,1)S(1)}, u32[]{:S(2)}, u32[]{:S(2)}) collective-permute-start(bf16[48,2560]{1,0:T(8,128)(2,1)S(1)} %get-tuple-element.33), channel_id=1, source_target_pairs={{0,4},{12,8},{4,0},{8,12},{1,5},{13,9},{5,1},{9,13},{2,6},{14,10},... | collective-permute-start | bytes 737288 | tf_op jit(solution)/shard_map/ppermute | solution.py:334
  7.3 1.5 %shard_map.114 = (bf16[48,2560]{1,0:T(8,128)(2,1)S(1)}, bf16[48,2560]{1,0:T(8,128)(2,1)S(1)}, bf16[48,2560]{1,0:T(8,128)(2,1)S(1)}, bf16[48,2560]{1,0:T(8,128)(2...) custom-call(bf16[384,640]{1,0:T(8,128)(2,1)S(1)} %get-tuple-element.28.turned_ref,, ...), custom_call_target="tpu_custom_call" | custom-call | tf_op jit(solution)/shard_map/pallas_call | solution.py:101
  8.9 1.9 %collective-permute-start.3 = (bf16[48,2560]{1,0:T(8,128)(2,1)S(1)}, bf16[48,2560]{1,0:T(8,128)(2,1)S(1)}, u32[]{:S(2)}, u32[]{:S(2)}) collective-permute-start(bf16[48,2560]{1,0:T(8,128)(2,1)S(1)} %get-tuple-element.36.mine_ref), channel_id=1, source_target_pairs={{0,4},{12,8},{1,5},{13,9},{2,6},{14,10},{3,7},{15,11},{16,20},{28,... | collective-permute-start | bytes 737288 | tf_op jit(solution)/shard_map/ppermute | solution.py:334
  10.8 2.9 %collective-permute-done.came_ref.early_ref = bf16[48,2560]{1,0:T(8,128)(2,1)S(1)} collective-permute-done((bf16[48,2560]{1,0:T(8,128)(2,1)S(1)}, bf16[48,2560]{1,0:T(8,128)(2,1)S(1)}, u32[]{:S(2)}, u32[]{:S(2)}) %collective-permute-start) | collective-permute-done | bytes 245792 | tf_op jit(solution)/shard_map/ppermute | solution.py:334
  14.4 6.5 %collective-permute-start.1 = (bf16[48,2560]{1,0:T(8,128)(2,1)S(1)}, bf16[48,2560]{1,0:T(8,128)(2,1)S(1)}, u32[]{:S(2)}, u32[]{:S(2)}) collective-permute-start(bf16[48,2560]{1,0:T(8,128)(2,1)S(1)} %get-tuple-element.34), channel_id=1, source_target_pairs={{0,4},{12,8},{1,5},{13,9},{2,6},{14,10},{3,7},{15,11},{16,20},{28,... | collective-permute-start | bytes 737288 | tf_op jit(solution)/shard_map/ppermute | solution.py:334
  21.0 1.9 %shard_map.136 = (bf16[320,2560]{1,0:T(8,128)(2,1)S(1)}, bf16[320,1920]{1,0:T(8,128)(2,1)S(1)}, bf16[320,640]{1,0:T(8,128)(2,1)S(1)}) custom-call(bf16[320,2560]{1,0:T(8,128)(2,1)} %bitcast.11, bf16[320,2560]{1,0:T(8,128)(2,1)} %bitcast.12, bf16[48,2560]{1,0:T(8,128)(2,1)S(1)} %get-tuple-element.48.rest_0_.mine_ref.after_ref), custom_call_target="tpu_custom_call" | custom-call | tf_op jit(solution)/shard_map/pallas_call | solution.py:140
  22.9 1.6 %collective-permute-start.16 = (bf16[320,1920]{1,0:T(8,128)(2,1)S(1)}, bf16[320,1920]{1,0:T(8,128)(2,1)S(1)}, u32[]{:S(2)}, u32[]{:S(2)}) collective-permute-start(bf16[320,1920]{1,0:T(8,128)(2,1)S(1)} %get-tuple-element.51), channel_id=1, source_target_pairs={{0,16},{16,0},{1,17},{17,1},{2,18},{18,2},{3,19},{19,3},{4,20},{20... | collective-permute-start | bytes 3686408 | tf_op jit(solution)/shard_map/ppermute | solution.py:342
  25.3 1.8 %collective-permute-start.5 = (bf16[48,2560]{1,0:T(8,128)(2,1)S(1)}, bf16[48,2560]{1,0:T(8,128)(2,1)S(1)}, u32[]{:S(2)}, u32[]{:S(2)}) collective-permute-start(bf16[48,2560]{1,0:T(8,128)(2,1)S(1)} %get-tuple-element.39), channel_id=1, source_target_pairs={{0,4},{12,8},{4,0},{8,12},{1,5},{13,9},{5,1},{9,13},{2,6},{14,10},... | collective-permute-start | bytes 737288 | tf_op jit(solution)/shard_map/ppermute | solution.py:334
  28.0 6.8 %collective-permute-start.8 = (bf16[48,2560]{1,0:T(8,128)(2,1)S(1)}, bf16[48,2560]{1,0:T(8,128)(2,1)S(1)}, u32[]{:S(2)}, u32[]{:S(2)}) collective-permute-start(bf16[48,2560]{1,0:T(8,128)(2,1)S(1)} %get-tuple-element.43), channel_id=1, source_target_pairs={{0,4},{12,8},{4,0},{8,12},{1,5},{13,9},{5,1},{9,13},{2,6},{14,10},... | collective-permute-start | bytes 737288 | tf_op jit(solution)/shard_map/ppermute | solution.py:334
  35.6 4.4 %collective-permute-start.7 = (bf16[48,2560]{1,0:T(8,128)(2,1)S(1)}, bf16[48,2560]{1,0:T(8,128)(2,1)S(1)}, u32[]{:S(2)}, u32[]{:S(2)}) collective-permute-start(bf16[48,2560]{1,0:T(8,128)(2,1)S(1)} %get-tuple-element.42), channel_id=1, source_target_pairs={{0,4},{12,8},{4,0},{8,12},{1,5},{13,9},{5,1},{9,13},{2,6},{14,10},... | collective-permute-start | bytes 737288 | tf_op jit(solution)/shard_map/ppermute | solution.py:334
  40.0 0.9 collective-permute-done.8.came_ref
  41.8 3.7 %collective-permute-start.11 = (bf16[48,2560]{1,0:T(8,128)(2,1)S(1)}, bf16[48,2560]{1,0:T(8,128)(2,1)S(1)}, u32[]{:S(2)}, u32[]{:S(2)}) collective-permute-start(bf16[48,2560]{1,0:T(8,128)(2,1)S(1)} %get-tuple-element.47), channel_id=1, source_target_pairs={{0,4},{12,8},{4,0},{8,12},{1,5},{13,9},{5,1},{9,13},{2,6},{14,10},... | collective-permute-start | bytes 737288 | tf_op jit(solution)/shard_map/ppermute | solution.py:334
  47.0 1.1 %collective-permute-start.17 = (bf16[320,640]{1,0:T(8,128)(2,1)S(1)}, bf16[320,640]{1,0:T(8,128)(2,1)S(1)}, u32[]{:S(2)}, u32[]{:S(2)}) collective-permute-start(bf16[320,640]{1,0:T(8,128)(2,1)S(1)} %get-tuple-element.52), channel_id=1, source_target_pairs={{0,16},{16,0},{1,17},{17,1},{2,18},{18,2},{3,19},{19,3},{4,20},{20... | collective-permute-start | bytes 1228808 | tf_op jit(solution)/shard_map/ppermute | solution.py:342
  48.2 3.7 %collective-permute-start.14 = (bf16[48,2560]{1,0:T(8,128)(2,1)S(1)}, bf16[48,2560]{1,0:T(8,128)(2,1)S(1)}, u32[]{:S(2)}, u32[]{:S(2)}) collective-permute-start(bf16[48,2560]{1,0:T(8,128)(2,1)S(1)} %get-tuple-element.50), channel_id=1, source_target_pairs={{0,4},{12,8},{4,0},{8,12},{1,5},{13,9},{5,1},{9,13},{2,6},{14,10},... | collective-permute-start | bytes 737288 | tf_op jit(solution)/shard_map/ppermute | solution.py:334
  52.8 1.3 %collective-permute-start.13 = (bf16[48,2560]{1,0:T(8,128)(2,1)S(1)}, bf16[48,2560]{1,0:T(8,128)(2,1)S(1)}, u32[]{:S(2)}, u32[]{:S(2)}) collective-permute-start(bf16[48,2560]{1,0:T(8,128)(2,1)S(1)} %shard_map.130.after_ref.mine_ref), channel_id=1, source_target_pairs={{4,0},{8,12},{5,1},{9,13},{6,2},{10,14},{7,3},{11,15},{20,16},{24,... | collective-permute-start | bytes 737288 | tf_op jit(solution)/shard_map/ppermute | solution.py:334
  54.1 5.1 %collective-permute-done.14.came_ref = bf16[48,2560]{1,0:T(8,128)(2,1)S(1)} collective-permute-done((bf16[48,2560]{1,0:T(8,128)(2,1)S(1)}, bf16[48,2560]{1,0:T(8,128)(2,1)S(1)}, u32[]{:S(2)}, u32[]{:S(2)}) %collective-permute-start.14) | collective-permute-done | bytes 245792 | tf_op jit(solution)/shard_map/ppermute | solution.py:334
  59.3 4.1 %collective-permute-start.19 = (bf16[48,2560]{1,0:T(8,128)(2,1)S(1)}, bf16[48,2560]{1,0:T(8,128)(2,1)S(1)}, u32[]{:S(2)}, u32[]{:S(2)}) collective-permute-start(bf16[48,2560]{1,0:T(8,128)(2,1)S(1)} %shard_map.132.after_ref.mine_ref), channel_id=1, source_target_pairs={{0,8},{4,12},{8,0},{12,4},{1,9},{5,13},{9,1},{13,5},{2,10},{6,14},... | collective-permute-start | bytes 737288 | tf_op jit(solution)/shard_map/ppermute | solution.py:364
  63.5 1.3 %collective-permute-start.18 = (bf16[48,2560]{1,0:T(8,128)(2,1)S(1)}, bf16[48,2560]{1,0:T(8,128)(2,1)S(1)}, u32[]{:S(2)}, u32[]{:S(2)}) collective-permute-start(bf16[48,2560]{1,0:T(8,128)(2,1)S(1)} %shard_map.133.after_ref.mine_ref), channel_id=1, source_target_pairs={{4,0},{8,12},{5,1},{9,13},{6,2},{10,14},{7,3},{11,15},{20,16},{24,... | collective-permute-start | bytes 737288 | tf_op jit(solution)/shard_map/ppermute | solution.py:334
  65.5 1.0 %shard_map.137.after_ref = bf16[288,320]{1,0:T(8,128)(2,1)S(1)} custom-call(bf16[48,2560]{1,0:T(8,128)(2,1)S(1)} %shard_map.135.after_ref.rest_7_.rest_6_, bf16[320,1920]{1,0:T(8,128)(2,1)S(1)} %collective-permute-done.16.rest_0_, bf16[320,640]{1,0:T(8,128)(2,1)S(1)} %collective-permute-done.17.rest_1_, ...), custom_call_target="tpu_custom_call" | custom-call | tf_op jit(solution)/shard_map/pallas_call | solution.py:241
  66.5 4.9 %collective-permute-start.20 = (bf16[288,320]{1,0:T(8,128)(2,1)S(1)}, bf16[288,320]{1,0:T(8,128)(2,1)S(1)}, u32[]{:S(2)}, u32[]{:S(2)}) collective-permute-start(bf16[288,320]{1,0:T(8,128)(2,1)S(1)} %shard_map.137.after_ref), channel_id=1, source_target_pairs={{0,16},{16,0},{1,17},{17,1},{2,18},{18,2},{3,19},{19,3},{4,20},{20... | collective-permute-start | bytes 552968 | tf_op jit(solution)/shard_map/ppermute | solution.py:349
  71.3 0.9 %shard_map.138.after_ref.refs_0_ = f32[288,320]{1,0:T(8,128)S(1)} custom-call(bf16[288,320]{1,0:T(8,128)(2,1)S(1)} %shard_map.137.after_ref, bf16[320,2560]{1,0:T(8,128)(2,1)S(1)} %get-tuple-element.53.rest_0_, bf16[48,2560]{1,0:T(8,128)(2,1)S(1)} %shard_map.122.after_ref.rest_2_.rest_1_, bf16[48,2560]{1,0:T(8,128)(2,1)S(1)} %shard_map.125.after_ref.rest_3_.rest_2_, ...), custom_call_target="tpu_custom_call" | custom-call | tf_op jit(solution)/shard_map/pallas_call | solution.py:241
  73.3 0.7 collective-permute-start.21
  75.2 2.5 %collective-permute-done.21.refs_3_ = bf16[96,320]{1,0:T(8,128)(2,1)S(1)} collective-permute-done((bf16[96,320]{1,0:T(8,128)(2,1)S(1)}, bf16[96,320]{1,0:T(8,128)(2,1)S(1)}, u32[]{:S(2)}, u32[]{:S(2)}) %collective-permute-start.21) | collective-permute-done | bytes 61472 | tf_op jit(solution)/shard_map/ppermute | solution.py:349
  77.8 0.8 shard_map.143
  78.6 1.2 %collective-permute-done.22 = f32[12,384]{1,0:T(8,128)S(1)} collective-permute-done((f32[12,384]{1,0:T(8,128)S(1)}, f32[12,384]{1,0:T(8,128)S(1)}, u32[]{:S(2)}, u32[]{:S(2)}) %collective-permute-start.22) | collective-permute-done | bytes 18464 | tf_op jit(solution)/shard_map/ppermute | solution.py:400
  79.8 1.5 %collective-permute-start.23 = (f32[12,384]{1,0:T(8,128)S(1)}, f32[12,384]{1,0:T(8,128)S(1)}, u32[]{:S(2)}, u32[]{:S(2)}) collective-permute-start(f32[12,384]{1,0:T(8,128)S(1)} %add.12), channel_id=1, source_target_pairs={{0,2},{1,3},{2,0},{3,1},{4,6},{5,7},{6,4},{7,5},{8,10},{9,11},{10,... | collective-permute-start | bytes 55304 | tf_op jit(solution)/shard_map/ppermute | solution.py:400
  81.3 2.3 %collective-permute-done.23 = f32[12,384]{1,0:T(8,128)S(1)} collective-permute-done((f32[12,384]{1,0:T(8,128)S(1)}, f32[12,384]{1,0:T(8,128)S(1)}, u32[]{:S(2)}, u32[]{:S(2)}) %collective-permute-start.23) | collective-permute-done | bytes 18464 | tf_op jit(solution)/shard_map/ppermute | solution.py:400
  83.9 2.0 %collective-permute-start.25 = (f32[1,96]{1,0:T(1,128)S(1)}, f32[1,96]{1,0:T(1,128)S(1)}, u32[]{:S(2)}, u32[]{:S(2)}) collective-permute-start(f32[1,96]{1,0:T(1,128)S(1)} %reshape.12), channel_id=1, source_target_pairs={{0,8},{4,12},{8,0},{12,4},{1,9},{5,13},{9,1},{13,5},{2,10},{6,14},... | collective-permute-start | bytes 1160 | tf_op jit(solution)/shard_map/ppermute | solution.py:410
  85.9 2.4 %collective-permute-start.26 = (f32[1,96]{1,0:T(1,128)S(1)}, f32[1,96]{1,0:T(1,128)S(1)}, u32[]{:S(2)}, u32[]{:S(2)}) collective-permute-start(f32[1,96]{1,0:T(1,128)S(1)} %reshape.12), channel_id=1, source_target_pairs={{0,12},{4,8},{8,4},{12,0},{1,13},{5,9},{9,5},{13,1},{2,14},{6,10},... | collective-permute-start | bytes 1160 | tf_op jit(solution)/shard_map/ppermute | solution.py:410
  88.4 2.8 %collective-permute-done.26 = f32[1,96]{1,0:T(1,128)S(1)} collective-permute-done((f32[1,96]{1,0:T(1,128)S(1)}, f32[1,96]{1,0:T(1,128)S(1)}, u32[]{:S(2)}, u32[]{:S(2)}) %collective-permute-start.26) | collective-permute-done | bytes 416 | tf_op jit(solution)/shard_map/ppermute | solution.py:410
  91.3 0.7 select_reduce_fusion
  (70 shorter events, 9.9 us)
Async XLA Ops:
  4.2 9.5 %collective-permute-start = (bf16[48,2560]{1,0:T(8,128)(2,1)S(1)}, bf16[48,2560]{1,0:T(8,128)(2,1)S(1)}, u32[]{:S(2)}, u32[]{:S(2)}) collective-permute-start(bf16[48,2560]{1,0:T(8,128)(2,1)S(1)} %get-tuple-element.33), channel_id=1, source_target_pairs={{0,4},{12,8},{4,0},{8,12},{1,5},{13,9},{5,1},{9,13},{2,6},{14,10},... | collective-permute-start | bytes 737288 | tf_op jit(solution)/shard_map/ppermute | solution.py:334
  8.9 15.6 %collective-permute-start.3 = (bf16[48,2560]{1,0:T(8,128)(2,1)S(1)}, bf16[48,2560]{1,0:T(8,128)(2,1)S(1)}, u32[]{:S(2)}, u32[]{:S(2)}) collective-permute-start(bf16[48,2560]{1,0:T(8,128)(2,1)S(1)} %get-tuple-element.36.mine_ref), channel_id=1, source_target_pairs={{0,4},{12,8},{1,5},{13,9},{2,6},{14,10},{3,7},{15,11},{16,20},{28,... | collective-permute-start | bytes 737288 | tf_op jit(solution)/shard_map/ppermute | solution.py:334
  13.8 11.5 %collective-permute-start.2 = (bf16[48,2560]{1,0:T(8,128)(2,1)S(1)}, bf16[48,2560]{1,0:T(8,128)(2,1)S(1)}, u32[]{:S(2)}, u32[]{:S(2)}) collective-permute-start(bf16[48,2560]{1,0:T(8,128)(2,1)S(1)} %get-tuple-element.35.after_ref.mine_ref), channel_id=1, source_target_pairs={{4,8},{8,4},{5,9},{9,5},{6,10},{10,6},{7,11},{11,7},{20,24},{24,20... | collective-permute-start | bytes 737288 | tf_op jit(solution)/shard_map/ppermute | solution.py:334
  14.4 12.7 %collective-permute-start.1 = (bf16[48,2560]{1,0:T(8,128)(2,1)S(1)}, bf16[48,2560]{1,0:T(8,128)(2,1)S(1)}, u32[]{:S(2)}, u32[]{:S(2)}) collective-permute-start(bf16[48,2560]{1,0:T(8,128)(2,1)S(1)} %get-tuple-element.34), channel_id=1, source_target_pairs={{0,4},{12,8},{1,5},{13,9},{2,6},{14,10},{3,7},{15,11},{16,20},{28,... | collective-permute-start | bytes 737288 | tf_op jit(solution)/shard_map/ppermute | solution.py:334
  22.9 42.6 %collective-permute-start.16 = (bf16[320,1920]{1,0:T(8,128)(2,1)S(1)}, bf16[320,1920]{1,0:T(8,128)(2,1)S(1)}, u32[]{:S(2)}, u32[]{:S(2)}) collective-permute-start(bf16[320,1920]{1,0:T(8,128)(2,1)S(1)} %get-tuple-element.51), channel_id=1, source_target_pairs={{0,16},{16,0},{1,17},{17,1},{2,18},{18,2},{3,19},{19,3},{4,20},{20... | collective-permute-start | bytes 3686408 | tf_op jit(solution)/shard_map/ppermute | solution.py:342
  24.5 3.3 %collective-permute-start.6 = (bf16[48,2560]{1,0:T(8,128)(2,1)S(1)}, bf16[48,2560]{1,0:T(8,128)(2,1)S(1)}, u32[]{:S(2)}, u32[]{:S(2)}) collective-permute-start(bf16[48,2560]{1,0:T(8,128)(2,1)S(1)} %shard_map.116.after_ref.mine_ref), channel_id=1, source_target_pairs={{4,8},{8,4},{5,9},{9,5},{6,10},{10,6},{7,11},{11,7},{20,24},{24,20... | collective-permute-start | bytes 737288 | tf_op jit(solution)/shard_map/ppermute | solution.py:334
  25.3 9.5 %collective-permute-start.5 = (bf16[48,2560]{1,0:T(8,128)(2,1)S(1)}, bf16[48,2560]{1,0:T(8,128)(2,1)S(1)}, u32[]{:S(2)}, u32[]{:S(2)}) collective-permute-start(bf16[48,2560]{1,0:T(8,128)(2,1)S(1)} %get-tuple-element.39), channel_id=1, source_target_pairs={{0,4},{12,8},{4,0},{8,12},{1,5},{13,9},{5,1},{9,13},{2,6},{14,10},... | collective-permute-start | bytes 737288 | tf_op jit(solution)/shard_map/ppermute | solution.py:334
  27.2 8.4 %collective-permute-start.4 = (bf16[48,2560]{1,0:T(8,128)(2,1)S(1)}, bf16[48,2560]{1,0:T(8,128)(2,1)S(1)}, u32[]{:S(2)}, u32[]{:S(2)}) collective-permute-start(bf16[48,2560]{1,0:T(8,128)(2,1)S(1)} %shard_map.118.after_ref.mine_ref), channel_id=1, source_target_pairs={{4,8},{8,4},{5,9},{9,5},{6,10},{10,6},{7,11},{11,7},{20,24},{24,20... | collective-permute-start | bytes 737288 | tf_op jit(solution)/shard_map/ppermute | solution.py:334
  28.0 13.0 %collective-permute-start.8 = (bf16[48,2560]{1,0:T(8,128)(2,1)S(1)}, bf16[48,2560]{1,0:T(8,128)(2,1)S(1)}, u32[]{:S(2)}, u32[]{:S(2)}) collective-permute-start(bf16[48,2560]{1,0:T(8,128)(2,1)S(1)} %get-tuple-element.43), channel_id=1, source_target_pairs={{0,4},{12,8},{4,0},{8,12},{1,5},{13,9},{5,1},{9,13},{2,6},{14,10},... | collective-permute-start | bytes 737288 | tf_op jit(solution)/shard_map/ppermute | solution.py:334
  34.9 6.8 %collective-permute-start.9 = (bf16[48,2560]{1,0:T(8,128)(2,1)S(1)}, bf16[48,2560]{1,0:T(8,128)(2,1)S(1)}, u32[]{:S(2)}, u32[]{:S(2)}) collective-permute-start(bf16[48,2560]{1,0:T(8,128)(2,1)S(1)} %shard_map.120.after_ref.mine_ref), channel_id=1, source_target_pairs={{4,8},{8,4},{5,9},{9,5},{6,10},{10,6},{7,11},{11,7},{20,24},{24,20... | collective-permute-start | bytes 737288 | tf_op jit(solution)/shard_map/ppermute | solution.py:334
  35.6 10.6 %collective-permute-start.7 = (bf16[48,2560]{1,0:T(8,128)(2,1)S(1)}, bf16[48,2560]{1,0:T(8,128)(2,1)S(1)}, u32[]{:S(2)}, u32[]{:S(2)}) collective-permute-start(bf16[48,2560]{1,0:T(8,128)(2,1)S(1)} %get-tuple-element.42), channel_id=1, source_target_pairs={{0,4},{12,8},{4,0},{8,12},{1,5},{13,9},{5,1},{9,13},{2,6},{14,10},... | collective-permute-start | bytes 737288 | tf_op jit(solution)/shard_map/ppermute | solution.py:334
  41.0 7.1 %collective-permute-start.12 = (bf16[48,2560]{1,0:T(8,128)(2,1)S(1)}, bf16[48,2560]{1,0:T(8,128)(2,1)S(1)}, u32[]{:S(2)}, u32[]{:S(2)}) collective-permute-start(bf16[48,2560]{1,0:T(8,128)(2,1)S(1)} %shard_map.123.after_ref.mine_ref), channel_id=1, source_target_pairs={{4,8},{8,4},{5,9},{9,5},{6,10},{10,6},{7,11},{11,7},{20,24},{24,20... | collective-permute-start | bytes 737288 | tf_op jit(solution)/shard_map/ppermute | solution.py:334
  41.8 10.2 %collective-permute-start.11 = (bf16[48,2560]{1,0:T(8,128)(2,1)S(1)}, bf16[48,2560]{1,0:T(8,128)(2,1)S(1)}, u32[]{:S(2)}, u32[]{:S(2)}) collective-permute-start(bf16[48,2560]{1,0:T(8,128)(2,1)S(1)} %get-tuple-element.47), channel_id=1, source_target_pairs={{0,4},{12,8},{4,0},{8,12},{1,5},{13,9},{5,1},{9,13},{2,6},{14,10},... | collective-permute-start | bytes 737288 | tf_op jit(solution)/shard_map/ppermute | solution.py:334
  46.3 6.5 %collective-permute-start.10 = (bf16[48,2560]{1,0:T(8,128)(2,1)S(1)}, bf16[48,2560]{1,0:T(8,128)(2,1)S(1)}, u32[]{:S(2)}, u32[]{:S(2)}) collective-permute-start(bf16[48,2560]{1,0:T(8,128)(2,1)S(1)} %shard_map.126.after_ref.mine_ref), channel_id=1, source_target_pairs={{4,8},{8,4},{5,9},{9,5},{6,10},{10,6},{7,11},{11,7},{20,24},{24,20... | collective-permute-start | bytes 737288 | tf_op jit(solution)/shard_map/ppermute | solution.py:334
  47.0 18.5 %collective-permute-start.17 = (bf16[320,640]{1,0:T(8,128)(2,1)S(1)}, bf16[320,640]{1,0:T(8,128)(2,1)S(1)}, u32[]{:S(2)}, u32[]{:S(2)}) collective-permute-start(bf16[320,640]{1,0:T(8,128)(2,1)S(1)} %get-tuple-element.52), channel_id=1, source_target_pairs={{0,16},{16,0},{1,17},{17,1},{2,18},{18,2},{3,19},{19,3},{4,20},{20... | collective-permute-start | bytes 1228808 | tf_op jit(solution)/shard_map/ppermute | solution.py:342
  48.2 11.0 %collective-permute-start.14 = (bf16[48,2560]{1,0:T(8,128)(2,1)S(1)}, bf16[48,2560]{1,0:T(8,128)(2,1)S(1)}, u32[]{:S(2)}, u32[]{:S(2)}) collective-permute-start(bf16[48,2560]{1,0:T(8,128)(2,1)S(1)} %get-tuple-element.50), channel_id=1, source_target_pairs={{0,4},{12,8},{4,0},{8,12},{1,5},{13,9},{5,1},{9,13},{2,6},{14,10},... | collective-permute-start | bytes 737288 | tf_op jit(solution)/shard_map/ppermute | solution.py:334
  52.0 11.4 %collective-permute-start.15 = (bf16[48,2560]{1,0:T(8,128)(2,1)S(1)}, bf16[48,2560]{1,0:T(8,128)(2,1)S(1)}, u32[]{:S(2)}, u32[]{:S(2)}) collective-permute-start(bf16[48,2560]{1,0:T(8,128)(2,1)S(1)} %shard_map.129.after_ref.mine_ref), channel_id=1, source_target_pairs={{4,8},{8,4},{5,9},{9,5},{6,10},{10,6},{7,11},{11,7},{20,24},{24,20... | collective-permute-start | bytes 737288 | tf_op jit(solution)/shard_map/ppermute | solution.py:334
  52.8 12.6 %collective-permute-start.13 = (bf16[48,2560]{1,0:T(8,128)(2,1)S(1)}, bf16[48,2560]{1,0:T(8,128)(2,1)S(1)}, u32[]{:S(2)}, u32[]{:S(2)}) collective-permute-start(bf16[48,2560]{1,0:T(8,128)(2,1)S(1)} %shard_map.130.after_ref.mine_ref), channel_id=1, source_target_pairs={{4,0},{8,12},{5,1},{9,13},{6,2},{10,14},{7,3},{11,15},{20,16},{24,... | collective-permute-start | bytes 737288 | tf_op jit(solution)/shard_map/ppermute | solution.py:334
  59.3 13.0 %collective-permute-start.19 = (bf16[48,2560]{1,0:T(8,128)(2,1)S(1)}, bf16[48,2560]{1,0:T(8,128)(2,1)S(1)}, u32[]{:S(2)}, u32[]{:S(2)}) collective-permute-start(bf16[48,2560]{1,0:T(8,128)(2,1)S(1)} %shard_map.132.after_ref.mine_ref), channel_id=1, source_target_pairs={{0,8},{4,12},{8,0},{12,4},{1,9},{5,13},{9,1},{13,5},{2,10},{6,14},... | collective-permute-start | bytes 737288 | tf_op jit(solution)/shard_map/ppermute | solution.py:364
  63.5 9.2 %collective-permute-start.18 = (bf16[48,2560]{1,0:T(8,128)(2,1)S(1)}, bf16[48,2560]{1,0:T(8,128)(2,1)S(1)}, u32[]{:S(2)}, u32[]{:S(2)}) collective-permute-start(bf16[48,2560]{1,0:T(8,128)(2,1)S(1)} %shard_map.133.after_ref.mine_ref), channel_id=1, source_target_pairs={{4,0},{8,12},{5,1},{9,13},{6,2},{10,14},{7,3},{11,15},{20,16},{24,... | collective-permute-start | bytes 737288 | tf_op jit(solution)/shard_map/ppermute | solution.py:334
  66.5 8.8 %collective-permute-start.20 = (bf16[288,320]{1,0:T(8,128)(2,1)S(1)}, bf16[288,320]{1,0:T(8,128)(2,1)S(1)}, u32[]{:S(2)}, u32[]{:S(2)}) collective-permute-start(bf16[288,320]{1,0:T(8,128)(2,1)S(1)} %shard_map.137.after_ref), channel_id=1, source_target_pairs={{0,16},{16,0},{1,17},{17,1},{2,18},{18,2},{3,19},{19,3},{4,20},{20... | collective-permute-start | bytes 552968 | tf_op jit(solution)/shard_map/ppermute | solution.py:349
  73.3 4.5 %copy-start = (s32[1,8]{1,0:T(1,128)S(1)}, s32[1,8]{1,0:T(1,128)}, u32[]{:S(2)}) copy-start(s32[1,8]{1,0:T(1,128)} %counts_ref.1) | copy-start | bytes 100
  73.3 14.9 %copy-start.2 = (s32[128]{0:T(128)S(1)}, s32[128]{0:T(128)}, u32[]{:S(2)}) copy-start(s32[128]{0:T(128)} %param.19) | copy-start | bytes 1540
  73.3 14.9 %copy-start.3 = (s32[128]{0:T(128)S(1)}, s32[128]{0:T(128)}, u32[]{:S(2)}) copy-start(s32[128]{0:T(128)} %param.17) | copy-start | bytes 1540
  73.3 14.9 %copy-start.4 = (s32[128,1]{0,1:T(1,128)S(1)}, s32[128,1]{0,1:T(1,128)}, u32[]{:S(2)}) copy-start(s32[128,1]{0,1:T(1,128)} %param.18) | copy-start | bytes 1540
  73.3 4.4 %collective-permute-start.21 = (bf16[96,320]{1,0:T(8,128)(2,1)S(1)}, bf16[96,320]{1,0:T(8,128)(2,1)S(1)}, u32[]{:S(2)}, u32[]{:S(2)}) collective-permute-start(bf16[96,320]{1,0:T(8,128)(2,1)S(1)} %shard_map.141.after_ref), channel_id=1, source_target_pairs={{0,16},{16,0},{1,17},{17,1},{2,18},{18,2},{3,19},{19,3},{4,20},{20... | collective-permute-start | bytes 184328 | tf_op jit(solution)/shard_map/ppermute | solution.py:349
  78.6 1.2 %collective-permute-start.22 = (f32[12,384]{1,0:T(8,128)S(1)}, f32[12,384]{1,0:T(8,128)S(1)}, u32[]{:S(2)}, u32[]{:S(2)}) collective-permute-start(f32[12,384]{1,0:T(8,128)S(1)} %shard_map.143), channel_id=1, source_target_pairs={{0,1},{1,0},{2,3},{3,2},{4,5},{5,4},{6,7},{7,6},{8,9},{9,8},{10,11... | collective-permute-start | bytes 55304 | tf_op jit(solution)/shard_map/ppermute | solution.py:400
  79.8 3.8 %collective-permute-start.23 = (f32[12,384]{1,0:T(8,128)S(1)}, f32[12,384]{1,0:T(8,128)S(1)}, u32[]{:S(2)}, u32[]{:S(2)}) collective-permute-start(f32[12,384]{1,0:T(8,128)S(1)} %add.12), channel_id=1, source_target_pairs={{0,2},{1,3},{2,0},{3,1},{4,6},{5,7},{6,4},{7,5},{8,10},{9,11},{10,... | collective-permute-start | bytes 55304 | tf_op jit(solution)/shard_map/ppermute | solution.py:400
  83.6 8.4 %copy-start.1 = (f32[12,384]{1,0:T(8,128)}, f32[12,384]{1,0:T(8,128)S(1)}, u32[]{:S(2)}) copy-start(f32[12,384]{1,0:T(8,128)S(1)} %add.13) | copy-start | bytes 55300
  83.8 4.5 %collective-permute-start.24 = (f32[1,96]{1,0:T(1,128)S(1)}, f32[1,96]{1,0:T(1,128)S(1)}, u32[]{:S(2)}, u32[]{:S(2)}) collective-permute-start(f32[1,96]{1,0:T(1,128)S(1)} %reshape.12), channel_id=1, source_target_pairs={{0,4},{4,0},{8,12},{12,8},{1,5},{5,1},{9,13},{13,9},{2,6},{6,2},{1... | collective-permute-start | bytes 1160 | tf_op jit(solution)/shard_map/ppermute | solution.py:410
  83.9 4.5 %collective-permute-start.25 = (f32[1,96]{1,0:T(1,128)S(1)}, f32[1,96]{1,0:T(1,128)S(1)}, u32[]{:S(2)}, u32[]{:S(2)}) collective-permute-start(f32[1,96]{1,0:T(1,128)S(1)} %reshape.12), channel_id=1, source_target_pairs={{0,8},{4,12},{8,0},{12,4},{1,9},{5,13},{9,1},{13,5},{2,10},{6,14},... | collective-permute-start | bytes 1160 | tf_op jit(solution)/shard_map/ppermute | solution.py:410
  85.9 5.3 %collective-permute-start.26 = (f32[1,96]{1,0:T(1,128)S(1)}, f32[1,96]{1,0:T(1,128)S(1)}, u32[]{:S(2)}, u32[]{:S(2)}) collective-permute-start(f32[1,96]{1,0:T(1,128)S(1)} %reshape.12), channel_id=1, source_target_pairs={{0,12},{4,8},{8,4},{12,0},{1,13},{5,9},{9,5},{13,1},{2,14},{6,10},... | collective-permute-start | bytes 1160 | tf_op jit(solution)/shard_map/ppermute | solution.py:410

commit v10 on v9

--- a/solution.py
+++ b/solution.py
@@ -183,12 +183,14 @@
     rest[-1][...] = mine.astype(jnp.bfloat16)
     if shared:
         write_send(rest[0], rest[2], rest[1])
-    elif len(rest) == 3:
-        rest[1][...] = rest[0][...]
-
-
-def total(after, mine, came, later=None, shared=False):
-    extra = [] if later is None else [later]
+    else:
+        count = len(rest) // 2
+        for later_ref, send_ref in zip(rest[:count], rest[count:]):
+            send_ref[...] = later_ref[...]
+
+
+def total(after, mine, came, extra=(), shared=False):
+    extra = list(extra)
     out = pl.pallas_call(
         functools.partial(total_kernel, shared),
         out_shape=[bf16(*a.shape) for a in extra + [mine]],
@@ -196,7 +198,7 @@
         out_specs=[VMEM] * (1 + len(extra)),
         compiler_params=pltpu.CompilerParams(vmem_limit_bytes=8 * MIB),
     )(mine, came, after, *extra)
-    return out[-1], (out[0] if extra else None)
+    return out[-1], out[:-1]
 
 
 def take_kernel(hop, shared, mine_ref, came_ref, after_ref, *rest):
@@ -212,16 +214,16 @@
         write_send(rest[0], rest[2], rest[1])
 
 
-def take(after, hop, mine, came, later=None):
-    extra = [] if later is None else [later]
+def take(after, hop, mine, came, extra=()):
+    extra = list(extra)
     out = pl.pallas_call(
-        functools.partial(take_kernel, hop, later is not None),
+        functools.partial(take_kernel, hop, len(extra) > 0),
         out_shape=[bf16(*a.shape) for a in extra + [mine]],
         in_specs=[VMEM, VMEM, ANY] + [VMEM] * len(extra),
         out_specs=[VMEM] * (1 + len(extra)),
         compiler_params=pltpu.CompilerParams(vmem_limit_bytes=8 * MIB),
     )(mine, came, after, *extra)
-    return out[-1], (out[0] if extra else None)
+    return out[-1], out[:-1]
 
 
 def project_kernel(parts, after_ref, *rest):
@@ -335,7 +337,7 @@
 
     short = n == 4
     part, came = list(own), [None] * chunks
-    ahead = min(2, chunks)
+    ahead, flying = min(2, chunks), 3
     early = came[0] = transfer(("in", "out") if short else ("in",), 0, send)
     for c in range(1, ahead):
         came[c] = transfer(("in",), 0, part[c])
@@ -355,7 +357,7 @@
     turns = chunks + last - short
     for turn in range(turns):
         steps = [(s, turn - s) for s in range(last) if 0 <= turn - s < chunks]
-        due = [c for c in range(chunks) if c + last + (c in swapped) == turn]
+        due = [c for c in range(chunks) if c + last + (flying - 1) * (c in swapped) == turn]
         for s, c in steps + [(last, c) for c in due]:
             kind, hop = stages[s]
             if short and c == chunks - 1:
@@ -367,24 +369,21 @@
                     after = part[c]
                     waiting.append((c, part[c]))
                 continue
-            later = turn + ahead if turn + ahead < chunks else None
-            if turn >= last - 1:
-                use = later if s == last - 1 else None
+            later = range(ahead, min(flying + 1, chunks)) if turn == 0 else range(turn + flying, min(turn + flying + 1, chunks))
+            shared = turn >= last - 1 and turn > 0 and s == last - 1 and len(later) == 1
+            use = later if shared or (s == 0 and (turn < last - 1 or turn == 0)) else ()
+            extra = [own[i] for i in use]
+            if kind == "out":
+                part[c], sends = take(after, hop, part[c], came[c], extra)
             else:
-                use = later if s == 0 else None
-            shared = use is not None and turn >= last - 1
-            chunk = None if use is None else own[use]
-            if kind == "out":
-                part[c], send = take(after, hop, part[c], came[c], chunk)
-            else:
-                part[c], send = total(after, part[c], came[c], chunk, shared)
+                part[c], sends = total(after, part[c], came[c], extra, shared)
             after = part[c]
             if shared:
-                came[c] = came[use] = transfer(("in", "out"), 0, send)
+                came[c] = came[use[0]] = transfer(("in", "out"), 0, sends[0])
                 swapped.add(c)
                 continue
-            if use is not None:
-                came[use] = transfer(stages[0][:1], stages[0][1], send)
+            for i, send in zip(use, sends):
+                came[i] = transfer(stages[0][:1], stages[0][1], send)
             if s < last:
                 came[c] = transfer(stages[s + 1][:1], stages[s + 1][1], part[c])
             else:

time: 92.3 us -> 97.2 us (1.053)
  waiting for transfers between devices: 20.1 us -> 36 us
  starting transfers between devices: 57.6 us -> 46.5 us
    ppermute x17 -> x18, waiting for transfers between devices: 10.6 us -> 23.8 us  [transfer(): return lax.ppermute(value, 'dp', pairs)]
    ppermute x2, starting transfers between devices: 5.53 us -> 1.12 us  [project_waiting(): back.append(lax.ppermute(away, 'parts', swap))]
    ppermute x1, starting transfers between devices: 4.12 us -> 0.13 us  [per_device(): came[c] = lax.ppermute(part[c], 'dp', [(i, i ^ 2) for i in range(n)])]
    ppermute x17 -> x18, starting transfers between devices: 39.3 us -> 37.2 us  [transfer(): return lax.ppermute(value, 'dp', pairs)]
    ppermute x1, waiting for transfers between devices: 0.01 us -> 1.99 us  [per_device(): came[c] = lax.ppermute(part[c], 'dp', [(i, i ^ 2) for i in range(n)])]
  transfers between devices with their start and end apart: 27 -> 28, of which waited for: 13 -> 13; matrix products, arithmetic and copies ran while one was open for 0% -> 0% of each run, Pallas kernels for 8% -> 8%
where the time goes in v10:
time: 97.2 us; the launch traced here: 96.9 us
  starting transfers between devices  46.5 us (48%)
  waiting for transfers between devices  36 us (37%)
  Pallas kernels  12.3 us (13%)
  between operations  1.09 us (1%)
    ppermute x18, starting transfers between devices, transfer(): return lax.ppermute(value, 'dp', pairs)  37.2 us
    ppermute x18, waiting for transfers between devices, transfer(): return lax.ppermute(value, 'dp', pairs)  23.8 us
    ppermute x3, starting transfers between devices, per_device(): lax.ppermute(flat, 'dp', [(i, i ^ k) for i in range(n)])  4.44 us
    pallas_call x1, Pallas kernels, first_pull(): pl.pallas_call(first_pull_kernel, out_shape=[bf16(rows, features)] * 2 +...  3.6 us
    ppermute x2, waiting for transfers between devices, per_device(): lax.ppermute(scores, 'layer', [(i, i ^ step) for i in range(layers)])  3.52 us
    ppermute x3, waiting for transfers between devices, per_device(): lax.ppermute(flat, 'dp', [(i, i ^ k) for i in range(n)])  3.43 us
    ppermute x2, waiting for transfers between devices, project_waiting(): back.append(lax.ppermute(away, 'parts', swap))  3.2 us
    pallas_call x4, Pallas kernels, project(): pl.pallas_call(functools.partial(project_kernel, len(tokens)), out_shape=...  3.18 us
  transfers between devices with their start and end apart: 28, of which 13 were waited for; matrix products, arithmetic and copies ran while one was open for 0% of the time, Pallas kernels for 8%

profile of v10, /device:TPU:0, one launch (start us, length us, event | category | flops | bytes accessed | tf_op | source)
XLA Modules:
  0.0 96.9 jit_solution(8203790825224413522)
XLA Ops:
  0.6 3.6 %shard_map.113 = (bf16[48,2560]{1,0:T(8,128)(2,1)S(1)}, bf16[48,2560]{1,0:T(8,128)(2,1)S(1)}, bf16[2560,640]{1,0:T(8,128)(2,1)S(1)}, bf16[640,384]{1,0:T(8,128)(2,1)}, bf16[384,640]{1,0:T(8,128)(2,1)S(1)}) custom-call(bf16[2560,640]{1,0:T(8,128)(2,1)} %bitcast.9, bf16[2560,640]{1,0:T(8,128)(2,1)} %bitcast.10, bf16[640,384]{1,0:T(8,128)(2,1)} %bitcast.13, ...), custom_call_target="tpu_custom_call" | custom-call | tf_op jit(solution)/shard_map/pallas_call | solution.py:77
  4.2 3.1 %collective-permute-start.1 = (bf16[48,2560]{1,0:T(8,128)(2,1)S(1)}, bf16[48,2560]{1,0:T(8,128)(2,1)S(1)}, u32[]{:S(2)}, u32[]{:S(2)}) collective-permute-start(bf16[48,2560]{1,0:T(8,128)(2,1)S(1)} %get-tuple-element.32), channel_id=1, source_target_pairs={{0,4},{12,8},{4,0},{8,12},{1,5},{13,9},{5,1},{9,13},{2,6},{14,10},... | collective-permute-start | bytes 737288 | tf_op jit(solution)/shard_map/ppermute | solution.py:336
  7.3 1.5 %shard_map.114 = (bf16[48,2560]{1,0:T(8,128)(2,1)S(1)}, bf16[48,2560]{1,0:T(8,128)(2,1)S(1)}, bf16[48,2560]{1,0:T(8,128)(2,1)S(1)}, bf16[48,2560]{1,0:T(8,128)(2...) custom-call(bf16[384,640]{1,0:T(8,128)(2,1)S(1)} %get-tuple-element.27.turned_ref,, ...), custom_call_target="tpu_custom_call" | custom-call | tf_op jit(solution)/shard_map/pallas_call | solution.py:101
  8.9 1.9 %collective-permute-start = (bf16[48,2560]{1,0:T(8,128)(2,1)S(1)}, bf16[48,2560]{1,0:T(8,128)(2,1)S(1)}, u32[]{:S(2)}, u32[]{:S(2)}) collective-permute-start(bf16[48,2560]{1,0:T(8,128)(2,1)S(1)} %get-tuple-element.31.mine_ref), channel_id=1, source_target_pairs={{0,4},{12,8},{1,5},{13,9},{2,6},{14,10},{3,7},{15,11},{16,20},{28,... | collective-permute-start | bytes 737288 | tf_op jit(solution)/shard_map/ppermute | solution.py:336
  10.8 2.9 %collective-permute-done.1.came_ref.early_ref = bf16[48,2560]{1,0:T(8,128)(2,1)S(1)} collective-permute-done((bf16[48,2560]{1,0:T(8,128)(2,1)S(1)}, bf16[48,2560]{1,0:T(8,128)(2,1)S(1)}, u32[]{:S(2)}, u32[]{:S(2)}) %collective-permute-start.1) | collective-permute-done | bytes 245792 | tf_op jit(solution)/shard_map/ppermute | solution.py:336
  14.5 6.5 %collective-permute-start.3 = (bf16[48,2560]{1,0:T(8,128)(2,1)S(1)}, bf16[48,2560]{1,0:T(8,128)(2,1)S(1)}, u32[]{:S(2)}, u32[]{:S(2)}) collective-permute-start(bf16[48,2560]{1,0:T(8,128)(2,1)S(1)} %get-tuple-element.36), channel_id=1, source_target_pairs={{0,4},{12,8},{1,5},{13,9},{2,6},{14,10},{3,7},{15,11},{16,20},{28,... | collective-permute-start | bytes 737288 | tf_op jit(solution)/shard_map/ppermute | solution.py:336
  21.0 1.9 %shard_map.136 = (bf16[320,2560]{1,0:T(8,128)(2,1)S(1)}, bf16[320,1920]{1,0:T(8,128)(2,1)S(1)}, bf16[320,640]{1,0:T(8,128)(2,1)S(1)}) custom-call(bf16[320,2560]{1,0:T(8,128)(2,1)} %bitcast.11, bf16[320,2560]{1,0:T(8,128)(2,1)} %bitcast.12, bf16[48,2560]{1,0:T(8,128)(2,1)S(1)} %get-tuple-element.45.rest_0_.mine_ref.after_ref), custom_call_target="tpu_custom_call" | custom-call | tf_op jit(solution)/shard_map/pallas_call | solution.py:140
  22.9 1.6 %collective-permute-start.17 = (bf16[320,1920]{1,0:T(8,128)(2,1)S(1)}, bf16[320,1920]{1,0:T(8,128)(2,1)S(1)}, u32[]{:S(2)}, u32[]{:S(2)}) collective-permute-start(bf16[320,1920]{1,0:T(8,128)(2,1)S(1)} %get-tuple-element.49), channel_id=1, source_target_pairs={{0,16},{16,0},{1,17},{17,1},{2,18},{18,2},{3,19},{19,3},{4,20},{20... | collective-permute-start | bytes 3686408 | tf_op jit(solution)/shard_map/ppermute | solution.py:344
  25.2 3.6 %collective-permute-start.7 = (bf16[48,2560]{1,0:T(8,128)(2,1)S(1)}, bf16[48,2560]{1,0:T(8,128)(2,1)S(1)}, u32[]{:S(2)}, u32[]{:S(2)}) collective-permute-start(bf16[48,2560]{1,0:T(8,128)(2,1)S(1)} %get-tuple-element.41), channel_id=1, source_target_pairs={{0,4},{12,8},{1,5},{13,9},{2,6},{14,10},{3,7},{15,11},{16,20},{28,... | collective-permute-start | bytes 737288 | tf_op jit(solution)/shard_map/ppermute | solution.py:336
  29.8 1.6 %collective-permute-start.6 = (bf16[48,2560]{1,0:T(8,128)(2,1)S(1)}, bf16[48,2560]{1,0:T(8,128)(2,1)S(1)}, u32[]{:S(2)}, u32[]{:S(2)}) collective-permute-start(bf16[48,2560]{1,0:T(8,128)(2,1)S(1)} %get-tuple-element.40), channel_id=1, source_target_pairs={{0,4},{12,8},{4,0},{8,12},{1,5},{13,9},{5,1},{9,13},{2,6},{14,10},... | collective-permute-start | bytes 737288 | tf_op jit(solution)/shard_map/ppermute | solution.py:336
  31.4 2.7 %collective-permute-done.7.came_ref = bf16[48,2560]{1,0:T(8,128)(2,1)S(1)} collective-permute-done((bf16[48,2560]{1,0:T(8,128)(2,1)S(1)}, bf16[48,2560]{1,0:T(8,128)(2,1)S(1)}, u32[]{:S(2)}, u32[]{:S(2)}) %collective-permute-start.7) | collective-permute-done | bytes 245792 | tf_op jit(solution)/shard_map/ppermute | solution.py:336
  34.8 5.4 %collective-permute-start.5 = (bf16[48,2560]{1,0:T(8,128)(2,1)S(1)}, bf16[48,2560]{1,0:T(8,128)(2,1)S(1)}, u32[]{:S(2)}, u32[]{:S(2)}) collective-permute-start(bf16[48,2560]{1,0:T(8,128)(2,1)S(1)} %get-tuple-element.39), channel_id=1, source_target_pairs={{0,4},{12,8},{4,0},{8,12},{1,5},{13,9},{5,1},{9,13},{2,6},{14,10},... | collective-permute-start | bytes 737288 | tf_op jit(solution)/shard_map/ppermute | solution.py:336
  41.1 4.4 %collective-permute-start.11 = (bf16[48,2560]{1,0:T(8,128)(2,1)S(1)}, bf16[48,2560]{1,0:T(8,128)(2,1)S(1)}, u32[]{:S(2)}, u32[]{:S(2)}) collective-permute-start(bf16[48,2560]{1,0:T(8,128)(2,1)S(1)} %get-tuple-element.47), channel_id=1, source_target_pairs={{0,4},{12,8},{4,0},{8,12},{1,5},{13,9},{5,1},{9,13},{2,6},{14,10},... | collective-permute-start | bytes 737288 | tf_op jit(solution)/shard_map/ppermute | solution.py:336
  46.5 1.3 %collective-permute-start.16 = (bf16[48,2560]{1,0:T(8,128)(2,1)S(1)}, bf16[48,2560]{1,0:T(8,128)(2,1)S(1)}, u32[]{:S(2)}, u32[]{:S(2)}) collective-permute-start(bf16[48,2560]{1,0:T(8,128)(2,1)S(1)} %shard_map.126.after_ref.mine_ref), channel_id=1, source_target_pairs={{4,0},{8,12},{5,1},{9,13},{6,2},{10,14},{7,3},{11,15},{20,16},{24,... | collective-permute-start | bytes 737288 | tf_op jit(solution)/shard_map/ppermute | solution.py:336
  48.3 4.0 %collective-permute-done.11.came_ref = bf16[48,2560]{1,0:T(8,128)(2,1)S(1)} collective-permute-done((bf16[48,2560]{1,0:T(8,128)(2,1)S(1)}, bf16[48,2560]{1,0:T(8,128)(2,1)S(1)}, u32[]{:S(2)}, u32[]{:S(2)}) %collective-permute-start.11) | collective-permute-done | bytes 245792 | tf_op jit(solution)/shard_map/ppermute | solution.py:336
  52.3 2.0 %collective-permute-start.14 = (bf16[48,2560]{1,0:T(8,128)(2,1)S(1)}, bf16[48,2560]{1,0:T(8,128)(2,1)S(1)}, u32[]{:S(2)}, u32[]{:S(2)}) collective-permute-start(bf16[48,2560]{1,0:T(8,128)(2,1)S(1)} %get-tuple-element.48), channel_id=1, source_target_pairs={{0,4},{12,8},{4,0},{8,12},{1,5},{13,9},{5,1},{9,13},{2,6},{14,10},... | collective-permute-start | bytes 737288 | tf_op jit(solution)/shard_map/ppermute | solution.py:336
  55.1 3.1 %collective-permute-done.16.came_ref = bf16[48,2560]{1,0:T(8,128)(2,1)S(1)} collective-permute-done((bf16[48,2560]{1,0:T(8,128)(2,1)S(1)}, bf16[48,2560]{1,0:T(8,128)(2,1)S(1)}, u32[]{:S(2)}, u32[]{:S(2)}) %collective-permute-start.16) | collective-permute-done | bytes 245792 | tf_op jit(solution)/shard_map/ppermute | solution.py:336
  58.2 1.3 %collective-permute-start.13 = (bf16[48,2560]{1,0:T(8,128)(2,1)S(1)}, bf16[48,2560]{1,0:T(8,128)(2,1)S(1)}, u32[]{:S(2)}, u32[]{:S(2)}) collective-permute-start(bf16[48,2560]{1,0:T(8,128)(2,1)S(1)} %shard_map.129.after_ref.mine_ref), channel_id=1, source_target_pairs={{4,0},{8,12},{5,1},{9,13},{6,2},{10,14},{7,3},{11,15},{20,16},{24,... | collective-permute-start | bytes 737288 | tf_op jit(solution)/shard_map/ppermute | solution.py:336
  59.6 6.5 %collective-permute-done.14.came_ref = bf16[48,2560]{1,0:T(8,128)(2,1)S(1)} collective-permute-done((bf16[48,2560]{1,0:T(8,128)(2,1)S(1)}, bf16[48,2560]{1,0:T(8,128)(2,1)S(1)}, u32[]{:S(2)}, u32[]{:S(2)}) %collective-permute-start.14) | collective-permute-done | bytes 245792 | tf_op jit(solution)/shard_map/ppermute | solution.py:336
  66.3 1.3 %collective-permute-start.19 = (bf16[48,2560]{1,0:T(8,128)(2,1)S(1)}, bf16[48,2560]{1,0:T(8,128)(2,1)S(1)}, u32[]{:S(2)}, u32[]{:S(2)}) collective-permute-start(bf16[48,2560]{1,0:T(8,128)(2,1)S(1)} %shard_map.133.after_ref.mine_ref), channel_id=1, source_target_pairs={{4,0},{8,12},{5,1},{9,13},{6,2},{10,14},{7,3},{11,15},{20,16},{24,... | collective-permute-start | bytes 737288 | tf_op jit(solution)/shard_map/ppermute | solution.py:336
  67.7 2.9 %collective-permute-done.13.came_ref = bf16[48,2560]{1,0:T(8,128)(2,1)S(1)} collective-permute-done((bf16[48,2560]{1,0:T(8,128)(2,1)S(1)}, bf16[48,2560]{1,0:T(8,128)(2,1)S(1)}, u32[]{:S(2)}, u32[]{:S(2)}) %collective-permute-start.13) | collective-permute-done | bytes 245792 | tf_op jit(solution)/shard_map/ppermute | solution.py:336
  70.7 1.0 shard_map.137.after_ref
  72.2 0.9 shard_map.138.after_ref.refs_0_
  73.1 2.0 %collective-permute-done.20.came_ref = bf16[48,2560]{1,0:T(8,128)(2,1)S(1)} collective-permute-done((bf16[48,2560]{1,0:T(8,128)(2,1)S(1)}, bf16[48,2560]{1,0:T(8,128)(2,1)S(1)}, u32[]{:S(2)}, u32[]{:S(2)}) %collective-permute-start.20) | collective-permute-done | bytes 245792 | tf_op jit(solution)/shard_map/ppermute | solution.py:366
  75.2 1.8 %collective-permute-done.19.came_ref = bf16[48,2560]{1,0:T(8,128)(2,1)S(1)} collective-permute-done((bf16[48,2560]{1,0:T(8,128)(2,1)S(1)}, bf16[48,2560]{1,0:T(8,128)(2,1)S(1)}, u32[]{:S(2)}, u32[]{:S(2)}) %collective-permute-start.19) | collective-permute-done | bytes 245792 | tf_op jit(solution)/shard_map/ppermute | solution.py:336
  78.9 3.2 %collective-permute-done.22.refs_3_ = bf16[96,320]{1,0:T(8,128)(2,1)S(1)} collective-permute-done((bf16[96,320]{1,0:T(8,128)(2,1)S(1)}, bf16[96,320]{1,0:T(8,128)(2,1)S(1)}, u32[]{:S(2)}, u32[]{:S(2)}) %collective-permute-start.22) | collective-permute-done | bytes 61472 | tf_op jit(solution)/shard_map/ppermute | solution.py:351
  83.0 1.2 %collective-permute-done.23 = f32[12,384]{1,0:T(8,128)S(1)} collective-permute-done((f32[12,384]{1,0:T(8,128)S(1)}, f32[12,384]{1,0:T(8,128)S(1)}, u32[]{:S(2)}, u32[]{:S(2)}) %collective-permute-start.23) | collective-permute-done | bytes 18464 | tf_op jit(solution)/shard_map/ppermute | solution.py:399
  84.1 1.5 %collective-permute-start.24 = (f32[12,384]{1,0:T(8,128)S(1)}, f32[12,384]{1,0:T(8,128)S(1)}, u32[]{:S(2)}, u32[]{:S(2)}) collective-permute-start(f32[12,384]{1,0:T(8,128)S(1)} %add.12), channel_id=1, source_target_pairs={{0,2},{1,3},{2,0},{3,1},{4,6},{5,7},{6,4},{7,5},{8,10},{9,11},{10,... | collective-permute-start | bytes 55304 | tf_op jit(solution)/shard_map/ppermute | solution.py:399
  85.6 2.3 %collective-permute-done.24 = f32[12,384]{1,0:T(8,128)S(1)} collective-permute-done((f32[12,384]{1,0:T(8,128)S(1)}, f32[12,384]{1,0:T(8,128)S(1)}, u32[]{:S(2)}, u32[]{:S(2)}) %collective-permute-start.24) | collective-permute-done | bytes 18464 | tf_op jit(solution)/shard_map/ppermute | solution.py:399
  88.2 2.5 %collective-permute-start.26 = (f32[1,96]{1,0:T(1,128)S(1)}, f32[1,96]{1,0:T(1,128)S(1)}, u32[]{:S(2)}, u32[]{:S(2)}) collective-permute-start(f32[1,96]{1,0:T(1,128)S(1)} %reshape.12), channel_id=1, source_target_pairs={{0,8},{4,12},{8,0},{12,4},{1,9},{5,13},{9,1},{13,5},{2,10},{6,14},... | collective-permute-start | bytes 1160 | tf_op jit(solution)/shard_map/ppermute | solution.py:409
  90.7 1.9 %collective-permute-start.27 = (f32[1,96]{1,0:T(1,128)S(1)}, f32[1,96]{1,0:T(1,128)S(1)}, u32[]{:S(2)}, u32[]{:S(2)}) collective-permute-start(f32[1,96]{1,0:T(1,128)S(1)} %reshape.12), channel_id=1, source_target_pairs={{0,12},{4,8},{8,4},{12,0},{1,13},{5,9},{9,5},{13,1},{2,14},{6,10},... | collective-permute-start | bytes 1160 | tf_op jit(solution)/shard_map/ppermute | solution.py:409
  92.7 3.3 %collective-permute-done.27 = f32[1,96]{1,0:T(1,128)S(1)} collective-permute-done((f32[1,96]{1,0:T(1,128)S(1)}, f32[1,96]{1,0:T(1,128)S(1)}, u32[]{:S(2)}, u32[]{:S(2)}) %collective-permute-start.27) | collective-permute-done | bytes 416 | tf_op jit(solution)/shard_map/ppermute | solution.py:409
  (72 shorter events, 11.1 us)
Async XLA Ops:
  4.2 9.5 %collective-permute-start.1 = (bf16[48,2560]{1,0:T(8,128)(2,1)S(1)}, bf16[48,2560]{1,0:T(8,128)(2,1)S(1)}, u32[]{:S(2)}, u32[]{:S(2)}) collective-permute-start(bf16[48,2560]{1,0:T(8,128)(2,1)S(1)} %get-tuple-element.32), channel_id=1, source_target_pairs={{0,4},{12,8},{4,0},{8,12},{1,5},{13,9},{5,1},{9,13},{2,6},{14,10},... | collective-permute-start | bytes 737288 | tf_op jit(solution)/shard_map/ppermute | solution.py:336
  8.9 15.6 %collective-permute-start = (bf16[48,2560]{1,0:T(8,128)(2,1)S(1)}, bf16[48,2560]{1,0:T(8,128)(2,1)S(1)}, u32[]{:S(2)}, u32[]{:S(2)}) collective-permute-start(bf16[48,2560]{1,0:T(8,128)(2,1)S(1)} %get-tuple-element.31.mine_ref), channel_id=1, source_target_pairs={{0,4},{12,8},{1,5},{13,9},{2,6},{14,10},{3,7},{15,11},{16,20},{28,... | collective-permute-start | bytes 737288 | tf_op jit(solution)/shard_map/ppermute | solution.py:336
  13.8 15.1 %collective-permute-start.4 = (bf16[48,2560]{1,0:T(8,128)(2,1)S(1)}, bf16[48,2560]{1,0:T(8,128)(2,1)S(1)}, u32[]{:S(2)}, u32[]{:S(2)}) collective-permute-start(bf16[48,2560]{1,0:T(8,128)(2,1)S(1)} %get-tuple-element.35.after_ref.mine_ref), channel_id=1, source_target_pairs={{4,8},{8,4},{5,9},{9,5},{6,10},{10,6},{7,11},{11,7},{20,24},{24,20... | collective-permute-start | bytes 737288 | tf_op jit(solution)/shard_map/ppermute | solution.py:336
  14.5 14.5 %collective-permute-start.3 = (bf16[48,2560]{1,0:T(8,128)(2,1)S(1)}, bf16[48,2560]{1,0:T(8,128)(2,1)S(1)}, u32[]{:S(2)}, u32[]{:S(2)}) collective-permute-start(bf16[48,2560]{1,0:T(8,128)(2,1)S(1)} %get-tuple-element.36), channel_id=1, source_target_pairs={{0,4},{12,8},{1,5},{13,9},{2,6},{14,10},{3,7},{15,11},{16,20},{28,... | collective-permute-start | bytes 737288 | tf_op jit(solution)/shard_map/ppermute | solution.py:336
  22.9 47.8 %collective-permute-start.17 = (bf16[320,1920]{1,0:T(8,128)(2,1)S(1)}, bf16[320,1920]{1,0:T(8,128)(2,1)S(1)}, u32[]{:S(2)}, u32[]{:S(2)}) collective-permute-start(bf16[320,1920]{1,0:T(8,128)(2,1)S(1)} %get-tuple-element.49), channel_id=1, source_target_pairs={{0,16},{16,0},{1,17},{17,1},{2,18},{18,2},{3,19},{19,3},{4,20},{20... | collective-permute-start | bytes 3686408 | tf_op jit(solution)/shard_map/ppermute | solution.py:344
  24.6 6.8 %collective-permute-start.2 = (bf16[48,2560]{1,0:T(8,128)(2,1)S(1)}, bf16[48,2560]{1,0:T(8,128)(2,1)S(1)}, u32[]{:S(2)}, u32[]{:S(2)}) collective-permute-start(bf16[48,2560]{1,0:T(8,128)(2,1)S(1)} %shard_map.116.after_ref.mine_ref), channel_id=1, source_target_pairs={{4,8},{8,4},{5,9},{9,5},{6,10},{10,6},{7,11},{11,7},{20,24},{24,20... | collective-permute-start | bytes 737288 | tf_op jit(solution)/shard_map/ppermute | solution.py:336
  25.2 8.8 %collective-permute-start.7 = (bf16[48,2560]{1,0:T(8,128)(2,1)S(1)}, bf16[48,2560]{1,0:T(8,128)(2,1)S(1)}, u32[]{:S(2)}, u32[]{:S(2)}) collective-permute-start(bf16[48,2560]{1,0:T(8,128)(2,1)S(1)} %get-tuple-element.41), channel_id=1, source_target_pairs={{0,4},{12,8},{1,5},{13,9},{2,6},{14,10},{3,7},{15,11},{16,20},{28,... | collective-permute-start | bytes 737288 | tf_op jit(solution)/shard_map/ppermute | solution.py:336
  29.1 11.2 %collective-permute-start.9 = (bf16[48,2560]{1,0:T(8,128)(2,1)S(1)}, bf16[48,2560]{1,0:T(8,128)(2,1)S(1)}, u32[]{:S(2)}, u32[]{:S(2)}) collective-permute-start(bf16[48,2560]{1,0:T(8,128)(2,1)S(1)} %shard_map.118.after_ref.mine_ref), channel_id=1, source_target_pairs={{4,8},{8,4},{5,9},{9,5},{6,10},{10,6},{7,11},{11,7},{20,24},{24,20... | collective-permute-start | bytes 737288 | tf_op jit(solution)/shard_map/ppermute | solution.py:336
  29.8 10.6 %collective-permute-start.6 = (bf16[48,2560]{1,0:T(8,128)(2,1)S(1)}, bf16[48,2560]{1,0:T(8,128)(2,1)S(1)}, u32[]{:S(2)}, u32[]{:S(2)}) collective-permute-start(bf16[48,2560]{1,0:T(8,128)(2,1)S(1)} %get-tuple-element.40), channel_id=1, source_target_pairs={{0,4},{12,8},{4,0},{8,12},{1,5},{13,9},{5,1},{9,13},{2,6},{14,10},... | collective-permute-start | bytes 737288 | tf_op jit(solution)/shard_map/ppermute | solution.py:336
  34.1 11.4 %collective-permute-start.8 = (bf16[48,2560]{1,0:T(8,128)(2,1)S(1)}, bf16[48,2560]{1,0:T(8,128)(2,1)S(1)}, u32[]{:S(2)}, u32[]{:S(2)}) collective-permute-start(bf16[48,2560]{1,0:T(8,128)(2,1)S(1)} %shard_map.120.after_ref.mine_ref), channel_id=1, source_target_pairs={{4,8},{8,4},{5,9},{9,5},{6,10},{10,6},{7,11},{11,7},{20,24},{24,20... | collective-permute-start | bytes 737288 | tf_op jit(solution)/shard_map/ppermute | solution.py:336
  34.8 10.8 %collective-permute-start.5 = (bf16[48,2560]{1,0:T(8,128)(2,1)S(1)}, bf16[48,2560]{1,0:T(8,128)(2,1)S(1)}, u32[]{:S(2)}, u32[]{:S(2)}) collective-permute-start(bf16[48,2560]{1,0:T(8,128)(2,1)S(1)} %get-tuple-element.39), channel_id=1, source_target_pairs={{0,4},{12,8},{4,0},{8,12},{1,5},{13,9},{5,1},{9,13},{2,6},{14,10},... | collective-permute-start | bytes 737288 | tf_op jit(solution)/shard_map/ppermute | solution.py:336
  40.4 6.0 %collective-permute-start.12 = (bf16[48,2560]{1,0:T(8,128)(2,1)S(1)}, bf16[48,2560]{1,0:T(8,128)(2,1)S(1)}, u32[]{:S(2)}, u32[]{:S(2)}) collective-permute-start(bf16[48,2560]{1,0:T(8,128)(2,1)S(1)} %shard_map.122.after_ref.mine_ref), channel_id=1, source_target_pairs={{4,8},{8,4},{5,9},{9,5},{6,10},{10,6},{7,11},{11,7},{20,24},{24,20... | collective-permute-start | bytes 737288 | tf_op jit(solution)/shard_map/ppermute | solution.py:336
  41.1 11.2 %collective-permute-start.11 = (bf16[48,2560]{1,0:T(8,128)(2,1)S(1)}, bf16[48,2560]{1,0:T(8,128)(2,1)S(1)}, u32[]{:S(2)}, u32[]{:S(2)}) collective-permute-start(bf16[48,2560]{1,0:T(8,128)(2,1)S(1)} %get-tuple-element.47), channel_id=1, source_target_pairs={{0,4},{12,8},{4,0},{8,12},{1,5},{13,9},{5,1},{9,13},{2,6},{14,10},... | collective-permute-start | bytes 737288 | tf_op jit(solution)/shard_map/ppermute | solution.py:336
  45.7 8.7 %collective-permute-start.10 = (bf16[48,2560]{1,0:T(8,128)(2,1)S(1)}, bf16[48,2560]{1,0:T(8,128)(2,1)S(1)}, u32[]{:S(2)}, u32[]{:S(2)}) collective-permute-start(bf16[48,2560]{1,0:T(8,128)(2,1)S(1)} %shard_map.125.after_ref.mine_ref), channel_id=1, source_target_pairs={{4,8},{8,4},{5,9},{9,5},{6,10},{10,6},{7,11},{11,7},{20,24},{24,20... | collective-permute-start | bytes 737288 | tf_op jit(solution)/shard_map/ppermute | solution.py:336
  46.5 11.7 %collective-permute-start.16 = (bf16[48,2560]{1,0:T(8,128)(2,1)S(1)}, bf16[48,2560]{1,0:T(8,128)(2,1)S(1)}, u32[]{:S(2)}, u32[]{:S(2)}) collective-permute-start(bf16[48,2560]{1,0:T(8,128)(2,1)S(1)} %shard_map.126.after_ref.mine_ref), channel_id=1, source_target_pairs={{4,0},{8,12},{5,1},{9,13},{6,2},{10,14},{7,3},{11,15},{20,16},{24,... | collective-permute-start | bytes 737288 | tf_op jit(solution)/shard_map/ppermute | solution.py:336
  47.8 22.9 %collective-permute-start.18 = (bf16[320,640]{1,0:T(8,128)(2,1)S(1)}, bf16[320,640]{1,0:T(8,128)(2,1)S(1)}, u32[]{:S(2)}, u32[]{:S(2)}) collective-permute-start(bf16[320,640]{1,0:T(8,128)(2,1)S(1)} %get-tuple-element.50), channel_id=1, source_target_pairs={{0,16},{16,0},{1,17},{17,1},{2,18},{18,2},{3,19},{19,3},{4,20},{20... | collective-permute-start | bytes 1228808 | tf_op jit(solution)/shard_map/ppermute | solution.py:344
  52.3 13.8 %collective-permute-start.14 = (bf16[48,2560]{1,0:T(8,128)(2,1)S(1)}, bf16[48,2560]{1,0:T(8,128)(2,1)S(1)}, u32[]{:S(2)}, u32[]{:S(2)}) collective-permute-start(bf16[48,2560]{1,0:T(8,128)(2,1)S(1)} %get-tuple-element.48), channel_id=1, source_target_pairs={{0,4},{12,8},{4,0},{8,12},{1,5},{13,9},{5,1},{9,13},{2,6},{14,10},... | collective-permute-start | bytes 737288 | tf_op jit(solution)/shard_map/ppermute | solution.py:336
  54.4 11.9 %collective-permute-start.15 = (bf16[48,2560]{1,0:T(8,128)(2,1)S(1)}, bf16[48,2560]{1,0:T(8,128)(2,1)S(1)}, u32[]{:S(2)}, u32[]{:S(2)}) collective-permute-start(bf16[48,2560]{1,0:T(8,128)(2,1)S(1)} %shard_map.128.after_ref.mine_ref), channel_id=1, source_target_pairs={{4,8},{8,4},{5,9},{9,5},{6,10},{10,6},{7,11},{11,7},{20,24},{24,20... | collective-permute-start | bytes 737288 | tf_op jit(solution)/shard_map/ppermute | solution.py:336
  58.2 12.4 %collective-permute-start.13 = (bf16[48,2560]{1,0:T(8,128)(2,1)S(1)}, bf16[48,2560]{1,0:T(8,128)(2,1)S(1)}, u32[]{:S(2)}, u32[]{:S(2)}) collective-permute-start(bf16[48,2560]{1,0:T(8,128)(2,1)S(1)} %shard_map.129.after_ref.mine_ref), channel_id=1, source_target_pairs={{4,0},{8,12},{5,1},{9,13},{6,2},{10,14},{7,3},{11,15},{20,16},{24,... | collective-permute-start | bytes 737288 | tf_op jit(solution)/shard_map/ppermute | solution.py:336
  66.2 9.0 %collective-permute-start.20 = (bf16[48,2560]{1,0:T(8,128)(2,1)S(1)}, bf16[48,2560]{1,0:T(8,128)(2,1)S(1)}, u32[]{:S(2)}, u32[]{:S(2)}) collective-permute-start(bf16[48,2560]{1,0:T(8,128)(2,1)S(1)} %shard_map.132.after_ref.mine_ref), channel_id=1, source_target_pairs={{0,8},{4,12},{8,0},{12,4},{1,9},{5,13},{9,1},{13,5},{2,10},{6,14},... | collective-permute-start | bytes 737288 | tf_op jit(solution)/shard_map/ppermute | solution.py:366
  66.3 10.6 %collective-permute-start.19 = (bf16[48,2560]{1,0:T(8,128)(2,1)S(1)}, bf16[48,2560]{1,0:T(8,128)(2,1)S(1)}, u32[]{:S(2)}, u32[]{:S(2)}) collective-permute-start(bf16[48,2560]{1,0:T(8,128)(2,1)S(1)} %shard_map.133.after_ref.mine_ref), channel_id=1, source_target_pairs={{4,0},{8,12},{5,1},{9,13},{6,2},{10,14},{7,3},{11,15},{20,16},{24,... | collective-permute-start | bytes 737288 | tf_op jit(solution)/shard_map/ppermute | solution.py:336
  71.6 7.3 %collective-permute-start.21 = (bf16[288,320]{1,0:T(8,128)(2,1)S(1)}, bf16[288,320]{1,0:T(8,128)(2,1)S(1)}, u32[]{:S(2)}, u32[]{:S(2)}) collective-permute-start(bf16[288,320]{1,0:T(8,128)(2,1)S(1)} %shard_map.137.after_ref), channel_id=1, source_target_pairs={{0,16},{16,0},{1,17},{17,1},{2,18},{18,2},{3,19},{19,3},{4,20},{20... | collective-permute-start | bytes 552968 | tf_op jit(solution)/shard_map/ppermute | solution.py:351
  77.7 14.9 %copy-start.2 = (s32[128]{0:T(128)S(1)}, s32[128]{0:T(128)}, u32[]{:S(2)}) copy-start(s32[128]{0:T(128)} %param.19) | copy-start | bytes 1540
  77.7 14.9 %copy-start.3 = (s32[128]{0:T(128)S(1)}, s32[128]{0:T(128)}, u32[]{:S(2)}) copy-start(s32[128]{0:T(128)} %param.17) | copy-start | bytes 1540
  77.7 14.9 %copy-start.4 = (s32[128,1]{0,1:T(1,128)S(1)}, s32[128,1]{0,1:T(1,128)}, u32[]{:S(2)}) copy-start(s32[128,1]{0,1:T(1,128)} %param.18) | copy-start | bytes 1540
  77.7 4.4 %collective-permute-start.22 = (bf16[96,320]{1,0:T(8,128)(2,1)S(1)}, bf16[96,320]{1,0:T(8,128)(2,1)S(1)}, u32[]{:S(2)}, u32[]{:S(2)}) collective-permute-start(bf16[96,320]{1,0:T(8,128)(2,1)S(1)} %shard_map.141.after_ref), channel_id=1, source_target_pairs={{0,16},{16,0},{1,17},{17,1},{2,18},{18,2},{3,19},{19,3},{4,20},{20... | collective-permute-start | bytes 184328 | tf_op jit(solution)/shard_map/ppermute | solution.py:351
  82.9 1.2 %collective-permute-start.23 = (f32[12,384]{1,0:T(8,128)S(1)}, f32[12,384]{1,0:T(8,128)S(1)}, u32[]{:S(2)}, u32[]{:S(2)}) collective-permute-start(f32[12,384]{1,0:T(8,128)S(1)} %shard_map.143), channel_id=1, source_target_pairs={{0,1},{1,0},{2,3},{3,2},{4,5},{5,4},{6,7},{7,6},{8,9},{9,8},{10,11... | collective-permute-start | bytes 55304 | tf_op jit(solution)/shard_map/ppermute | solution.py:399
  84.1 3.8 %collective-permute-start.24 = (f32[12,384]{1,0:T(8,128)S(1)}, f32[12,384]{1,0:T(8,128)S(1)}, u32[]{:S(2)}, u32[]{:S(2)}) collective-permute-start(f32[12,384]{1,0:T(8,128)S(1)} %add.12), channel_id=1, source_target_pairs={{0,2},{1,3},{2,0},{3,1},{4,6},{5,7},{6,4},{7,5},{8,10},{9,11},{10,... | collective-permute-start | bytes 55304 | tf_op jit(solution)/shard_map/ppermute | solution.py:399
  88.0 8.9 %copy-start.1 = (f32[12,384]{1,0:T(8,128)}, f32[12,384]{1,0:T(8,128)S(1)}, u32[]{:S(2)}) copy-start(f32[12,384]{1,0:T(8,128)S(1)} %add.13) | copy-start | bytes 55300
  88.1 4.5 %collective-permute-start.25 = (f32[1,96]{1,0:T(1,128)S(1)}, f32[1,96]{1,0:T(1,128)S(1)}, u32[]{:S(2)}, u32[]{:S(2)}) collective-permute-start(f32[1,96]{1,0:T(1,128)S(1)} %reshape.12), channel_id=1, source_target_pairs={{0,4},{4,0},{8,12},{12,8},{1,5},{5,1},{9,13},{13,9},{2,6},{6,2},{1... | collective-permute-start | bytes 1160 | tf_op jit(solution)/shard_map/ppermute | solution.py:409
  88.2 4.5 %collective-permute-start.26 = (f32[1,96]{1,0:T(1,128)S(1)}, f32[1,96]{1,0:T(1,128)S(1)}, u32[]{:S(2)}, u32[]{:S(2)}) collective-permute-start(f32[1,96]{1,0:T(1,128)S(1)} %reshape.12), channel_id=1, source_target_pairs={{0,8},{4,12},{8,0},{12,4},{1,9},{5,13},{9,1},{13,5},{2,10},{6,14},... | collective-permute-start | bytes 1160 | tf_op jit(solution)/shard_map/ppermute | solution.py:409
  90.7 5.3 %collective-permute-start.27 = (f32[1,96]{1,0:T(1,128)S(1)}, f32[1,96]{1,0:T(1,128)S(1)}, u32[]{:S(2)}, u32[]{:S(2)}) collective-permute-start(f32[1,96]{1,0:T(1,128)S(1)} %reshape.12), channel_id=1, source_target_pairs={{0,12},{4,8},{8,4},{12,0},{1,13},{5,9},{9,5},{13,1},{2,14},{6,10},... | collective-permute-start | bytes 1160 | tf_op jit(solution)/shard_map/ppermute | solution.py:409
  (1 other events, 4.5 us)

commit v11 on v9

--- a/solution.py
+++ b/solution.py
@@ -16,6 +16,7 @@
 ANY = pl.BlockSpec(memory_space=pl.ANY)
 MIB = 1024 * 1024
 LANES = 128
+BEFORE = 3
 
 
 def in_hbm(*arrays):
@@ -47,23 +48,26 @@
 
     side = lax.axis_index("parts")
 
-    @pl.when(side == 0)
-    def _():
-        for copy in copies(basis_in_ref, query_in_ref):
-            copy.start()
-
-    @pl.when(side != 0)
-    def _():
-        for copy in copies(basis_out_ref, query_out_ref):
-            copy.start()
-
+    def start(which):
+        @pl.when(side == 0)
+        def _():
+            for copy in copies(basis_in_ref, query_in_ref)[which]:
+                copy.start()
+
+        @pl.when(side != 0)
+        def _():
+            for copy in copies(basis_out_ref, query_out_ref)[which]:
+                copy.start()
+
+    start(slice(0, 1 + BEFORE))
     landed = copies(basis_in_ref, query_in_ref)
     landed[0].wait()
     turned_ref[...] = query_ref[...].T
     first = pl.multiple_of(jnp.where(at_depth(0), 0, turned_ref.shape[0] - rows), rows)
     factors = jnp.concatenate([turned_ref[:rows], turned_ref[pl.ds(first, rows)]], axis=0)
-    for copy, span in zip(landed[1:], spans):
+    for i, (copy, span) in enumerate(zip(landed[1:], spans)):
         copy.wait()
+        start(slice(1 + BEFORE + i, 2 + BEFORE + i))
         pulled = lax.dot_general(factors, basis_ref[span], NT, preferred_element_type=jnp.float32)
         pulled = pulled.astype(jnp.bfloat16)
         out_ref[:, span] = pulled[:rows]
@@ -135,7 +139,7 @@
 
 def deal(after, acts, grads):
     tokens, features = acts.shape
-    larger = features * 3 // 4
+    larger = features * 17 // 20
     widths = [larger, features - larger] if larger % LANES == 0 else [features]
     out = pl.pallas_call(
         deal_kernel,
@@ -247,15 +251,11 @@
     )(after, *tokens, *factors)
 
 
-def score_kernel(count, counts_ref, *refs):
-    out_ref = refs[-1]
-    own = jnp.concatenate([ref[...] for ref in refs[:count]], axis=0)
-    other = jnp.concatenate([ref[...] for ref in refs[count : 2 * count]], axis=0)
-    product = own * other.astype(jnp.float32)
+def score_kernel(counts_ref, own_ref, other_ref, *rest):
+    done, out_ref = rest[:-1], rest[-1]
+    product = own_ref[...] * other_ref[...].astype(jnp.float32)
     queries, tokens = product.shape[0] // RANK, product.shape[1]
     scores = jnp.sum(product.reshape(queries, RANK, tokens), axis=1) * RANK ** (-0.5)
-    out_ref[...] = jnp.zeros(out_ref.shape, jnp.float32)
-    out_ref[:, :tokens] = scores
     position = lax.broadcasted_iota(jnp.int32, scores.shape, 1)
     docs = counts_ref.shape[1]
     column = lax.broadcasted_iota(jnp.int32, (queries, docs), 1)
@@ -268,19 +268,25 @@
         root = jnp.sqrt(jnp.full((1, 1), count, jnp.int32).astype(jnp.float32))
         pooled = jnp.where(column == k, found / root, pooled)
         start = start + count
-    out_ref[:, tokens : tokens + pooled.shape[1]] = pooled
-
-
-def score(counts, own, other):
-    rows = sum(piece.shape[0] for piece in own)
-    width = (own[0].shape[1] + counts.shape[1] + LANES - 1) // LANES * LANES
+    first = 0
+    for ref in done:
+        out_ref[: ref.shape[0]] = ref[...]
+        first = ref.shape[0]
+    out_ref[first:] = jnp.zeros((queries, out_ref.shape[1]), jnp.float32)
+    out_ref[first:, :tokens] = scores
+    out_ref[first:, tokens : tokens + docs] = pooled
+
+
+def score(counts, own, other, done=()):
+    queries = own.shape[0] // RANK + sum(ref.shape[0] for ref in done)
+    width = (own.shape[1] + counts.shape[1] + LANES - 1) // LANES * LANES
     return pl.pallas_call(
-        functools.partial(score_kernel, len(own)),
-        out_shape=jax.ShapeDtypeStruct((rows // RANK, width), jnp.float32),
-        in_specs=[pl.BlockSpec(memory_space=pltpu.SMEM)] + [VMEM] * (2 * len(own)),
+        score_kernel,
+        out_shape=jax.ShapeDtypeStruct((queries, width), jnp.float32),
+        in_specs=[pl.BlockSpec(memory_space=pltpu.SMEM)] + [VMEM] * (2 + len(done)),
         out_specs=VMEM,
         compiler_params=pltpu.CompilerParams(vmem_limit_bytes=16 * MIB),
-    )(counts, *own, *other)
+    )(counts, own, other, *done)
 
 
 def chunk_rows(spread):
@@ -392,7 +398,12 @@
         if turn >= turns - 2 and waiting:
             after = project_waiting(after)
 
-    scores = score(doc_counts, mine, back)
+    if any(piece.shape[0] % RANK for piece in mine):
+        mine, back = [jnp.concatenate(mine, axis=0)], [jnp.concatenate(back, axis=0)]
+    done = ()
+    for piece, other in zip(mine, back):
+        done = (score(doc_counts, piece, other, done),)
+    scores = done[0]
     if not is_power(layers):
         scores = lax.psum(scores, "layer")
     else:

time: 92.3 us -> 94.6 us (1.025)
    ppermute x17, starting transfers between devices: 39.3 us -> 46.1 us  [transfer(): return lax.ppermute(value, 'dp', pairs)]
    ppermute x2, starting transfers between devices: 5.53 us -> 1.87 us  [project_waiting(): back.append(lax.ppermute(away, 'parts', swap))]
    ppermute x2, waiting for transfers between devices: 3.08 us -> 1.15 us  [project_waiting(): back.append(lax.ppermute(away, 'parts', swap))]
    ppermute x1, starting transfers between devices: 4.12 us -> 2.73 us  [per_device(): came[c] = lax.ppermute(part[c], 'dp', [(i, i ^ 2) for i in range(n)])]
    ppermute x2, starting transfers between devices: 2.73 us -> 1.66 us  [per_device(): others = [lax.ppermute(piece, 'parts', swap) for piece in theirs]]
    ppermute x17, waiting for transfers between devices: 10.6 us -> 11.6 us  [transfer(): return lax.ppermute(value, 'dp', pairs)]
    ppermute x1, waiting for transfers between devices: 0.01 us -> 0.99 us  [per_device(): came[c] = lax.ppermute(part[c], 'dp', [(i, i ^ 2) for i in range(n)])]
  transfers between devices with their start and end apart: 27 -> 27, of which waited for: 13 -> 11; matrix products, arithmetic and copies ran while one was open for 0% -> 0% of each run, Pallas kernels for 8% -> 9%
where the time goes in v11:
time: 94.6 us; the launch traced here: 94.2 us
  starting transfers between devices  58.3 us (62%)
  waiting for transfers between devices  20.7 us (22%)
  Pallas kernels  13.1 us (14%)
  between operations  1.11 us (1%)
    ppermute x17, starting transfers between devices, transfer(): return lax.ppermute(value, 'dp', pairs)  46.1 us
    ppermute x17, waiting for transfers between devices, transfer(): return lax.ppermute(value, 'dp', pairs)  11.6 us
    ppermute x3, starting transfers between devices, per_device(): lax.ppermute(flat, 'dp', [(i, i ^ k) for i in range(n)])  4.44 us
    pallas_call x1, Pallas kernels, first_pull(): pl.pallas_call(first_pull_kernel, out_shape=[bf16(rows, features)] * 2 +...  3.77 us
    ppermute x2, waiting for transfers between devices, per_device(): lax.ppermute(scores, 'layer', [(i, i ^ step) for i in range(layers)])  3.52 us
    ppermute x3, waiting for transfers between devices, per_device(): lax.ppermute(flat, 'dp', [(i, i ^ k) for i in range(n)])  3.39 us
    pallas_call x4, Pallas kernels, project(): pl.pallas_call(functools.partial(project_kernel, len(tokens)), out_shape=...  3.2 us
    ppermute x1, starting transfers between devices, per_device(): came[c] = lax.ppermute(part[c], 'dp', [(i, i ^ 2) for i in range(n)])  2.73 us
  transfers between devices with their start and end apart: 27, of which 11 were waited for; matrix products, arithmetic and copies ran while one was open for 0% of the time, Pallas kernels for 9%

profile of v11, /device:TPU:0, one launch (start us, length us, event | category | flops | bytes accessed | tf_op | source)
XLA Modules:
  0.0 94.2 jit_solution(16006108464793206477)
XLA Ops:
  0.6 3.8 %shard_map.113 = (bf16[48,2560]{1,0:T(8,128)(2,1)S(1)}, bf16[48,2560]{1,0:T(8,128)(2,1)S(1)}, bf16[2560,640]{1,0:T(8,128)(2,1)S(1)}, bf16[640,384]{1,0:T(8,128)(2,1)}, bf16[384,640]{1,0:T(8,128)(2,1)S(1)}) custom-call(bf16[2560,640]{1,0:T(8,128)(2,1)} %bitcast.9, bf16[2560,640]{1,0:T(8,128)(2,1)} %bitcast.10, bf16[640,384]{1,0:T(8,128)(2,1)} %bitcast.13, ...), custom_call_target="tpu_custom_call" | custom-call | tf_op jit(solution)/shard_map/pallas_call | solution.py:81
  4.4 3.1 %collective-permute-start = (bf16[48,2560]{1,0:T(8,128)(2,1)S(1)}, bf16[48,2560]{1,0:T(8,128)(2,1)S(1)}, u32[]{:S(2)}, u32[]{:S(2)}) collective-permute-start(bf16[48,2560]{1,0:T(8,128)(2,1)S(1)} %get-tuple-element.33), channel_id=1, source_target_pairs={{0,4},{12,8},{4,0},{8,12},{1,5},{13,9},{5,1},{9,13},{2,6},{14,10},... | collective-permute-start | bytes 737288 | tf_op jit(solution)/shard_map/ppermute | solution.py:340
  7.5 1.5 %shard_map.114 = (bf16[48,2560]{1,0:T(8,128)(2,1)S(1)}, bf16[48,2560]{1,0:T(8,128)(2,1)S(1)}, bf16[48,2560]{1,0:T(8,128)(2,1)S(1)}, bf16[48,2560]{1,0:T(8,128)(2...) custom-call(bf16[384,640]{1,0:T(8,128)(2,1)S(1)} %get-tuple-element.28.turned_ref,, ...), custom_call_target="tpu_custom_call" | custom-call | tf_op jit(solution)/shard_map/pallas_call | solution.py:105
  9.0 1.9 %shard_map.136 = (bf16[320,2560]{1,0:T(8,128)(2,1)S(1)}, bf16[320,2176]{1,0:T(8,128)(2,1)S(1)}, bf16[320,384]{1,0:T(8,128)(2,1)S(1)}) custom-call(bf16[320,2560]{1,0:T(8,128)(2,1)} %bitcast.11, bf16[320,2560]{1,0:T(8,128)(2,1)} %bitcast.12, bf16[48,2560]{1,0:T(8,128)(2,1)S(1)} %get-tuple-element.48.rest_0_.mine_ref.after_ref), custom_call_target="tpu_custom_call" | custom-call | tf_op jit(solution)/shard_map/pallas_call | solution.py:144
  10.9 1.6 %collective-permute-start.18 = (bf16[320,2176]{1,0:T(8,128)(2,1)S(1)}, bf16[320,2176]{1,0:T(8,128)(2,1)S(1)}, u32[]{:S(2)}, u32[]{:S(2)}) collective-permute-start(bf16[320,2176]{1,0:T(8,128)(2,1)S(1)} %get-tuple-element.51), channel_id=1, source_target_pairs={{0,16},{16,0},{1,17},{17,1},{2,18},{18,2},{3,19},{19,3},{4,20},{20... | collective-permute-start | bytes 4177928 | tf_op jit(solution)/shard_map/ppermute | solution.py:348
  12.5 2.4 %collective-permute-start.2 = (bf16[48,2560]{1,0:T(8,128)(2,1)S(1)}, bf16[48,2560]{1,0:T(8,128)(2,1)S(1)}, u32[]{:S(2)}, u32[]{:S(2)}) collective-permute-start(bf16[48,2560]{1,0:T(8,128)(2,1)S(1)} %get-tuple-element.36.mine_ref), channel_id=1, source_target_pairs={{0,4},{12,8},{1,5},{13,9},{2,6},{14,10},{3,7},{15,11},{16,20},{28,... | collective-permute-start | bytes 737288 | tf_op jit(solution)/shard_map/ppermute | solution.py:340
  15.7 5.2 %collective-permute-start.5 = (bf16[48,2560]{1,0:T(8,128)(2,1)S(1)}, bf16[48,2560]{1,0:T(8,128)(2,1)S(1)}, u32[]{:S(2)}, u32[]{:S(2)}) collective-permute-start(bf16[48,2560]{1,0:T(8,128)(2,1)S(1)} %get-tuple-element.38), channel_id=1, source_target_pairs={{0,4},{12,8},{1,5},{13,9},{2,6},{14,10},{3,7},{15,11},{16,20},{28,... | collective-permute-start | bytes 737288 | tf_op jit(solution)/shard_map/ppermute | solution.py:340
  21.7 6.8 %collective-permute-start.3 = (bf16[48,2560]{1,0:T(8,128)(2,1)S(1)}, bf16[48,2560]{1,0:T(8,128)(2,1)S(1)}, u32[]{:S(2)}, u32[]{:S(2)}) collective-permute-start(bf16[48,2560]{1,0:T(8,128)(2,1)S(1)} %get-tuple-element.37), channel_id=1, source_target_pairs={{0,4},{12,8},{4,0},{8,12},{1,5},{13,9},{5,1},{9,13},{2,6},{14,10},... | collective-permute-start | bytes 737288 | tf_op jit(solution)/shard_map/ppermute | solution.py:340
  29.4 4.7 %collective-permute-start.7 = (bf16[48,2560]{1,0:T(8,128)(2,1)S(1)}, bf16[48,2560]{1,0:T(8,128)(2,1)S(1)}, u32[]{:S(2)}, u32[]{:S(2)}) collective-permute-start(bf16[48,2560]{1,0:T(8,128)(2,1)S(1)} %get-tuple-element.42), channel_id=1, source_target_pairs={{0,4},{12,8},{4,0},{8,12},{1,5},{13,9},{5,1},{9,13},{2,6},{14,10},... | collective-permute-start | bytes 737288 | tf_op jit(solution)/shard_map/ppermute | solution.py:340
  35.4 4.7 %collective-permute-start.10 = (bf16[48,2560]{1,0:T(8,128)(2,1)S(1)}, bf16[48,2560]{1,0:T(8,128)(2,1)S(1)}, u32[]{:S(2)}, u32[]{:S(2)}) collective-permute-start(bf16[48,2560]{1,0:T(8,128)(2,1)S(1)} %get-tuple-element.46), channel_id=1, source_target_pairs={{0,4},{12,8},{4,0},{8,12},{1,5},{13,9},{5,1},{9,13},{2,6},{14,10},... | collective-permute-start | bytes 737288 | tf_op jit(solution)/shard_map/ppermute | solution.py:340
  41.2 6.3 %collective-permute-start.9 = (bf16[48,2560]{1,0:T(8,128)(2,1)S(1)}, bf16[48,2560]{1,0:T(8,128)(2,1)S(1)}, u32[]{:S(2)}, u32[]{:S(2)}) collective-permute-start(bf16[48,2560]{1,0:T(8,128)(2,1)S(1)} %get-tuple-element.45), channel_id=1, source_target_pairs={{0,4},{12,8},{4,0},{8,12},{1,5},{13,9},{5,1},{9,13},{2,6},{14,10},... | collective-permute-start | bytes 737288 | tf_op jit(solution)/shard_map/ppermute | solution.py:340
  48.4 5.7 %collective-permute-start.13 = (bf16[48,2560]{1,0:T(8,128)(2,1)S(1)}, bf16[48,2560]{1,0:T(8,128)(2,1)S(1)}, u32[]{:S(2)}, u32[]{:S(2)}) collective-permute-start(bf16[48,2560]{1,0:T(8,128)(2,1)S(1)} %get-tuple-element.50), channel_id=1, source_target_pairs={{0,4},{12,8},{4,0},{8,12},{1,5},{13,9},{5,1},{9,13},{2,6},{14,10},... | collective-permute-start | bytes 737288 | tf_op jit(solution)/shard_map/ppermute | solution.py:340
  54.9 1.3 %collective-permute-start.17 = (bf16[48,2560]{1,0:T(8,128)(2,1)S(1)}, bf16[48,2560]{1,0:T(8,128)(2,1)S(1)}, u32[]{:S(2)}, u32[]{:S(2)}) collective-permute-start(bf16[48,2560]{1,0:T(8,128)(2,1)S(1)} %shard_map.130.after_ref.mine_ref), channel_id=1, source_target_pairs={{4,0},{8,12},{5,1},{9,13},{6,2},{10,14},{7,3},{11,15},{20,16},{24,... | collective-permute-start | bytes 737288 | tf_op jit(solution)/shard_map/ppermute | solution.py:340
  56.3 5.7 %collective-permute-done.13.came_ref = bf16[48,2560]{1,0:T(8,128)(2,1)S(1)} collective-permute-done((bf16[48,2560]{1,0:T(8,128)(2,1)S(1)}, bf16[48,2560]{1,0:T(8,128)(2,1)S(1)}, u32[]{:S(2)}, u32[]{:S(2)}) %collective-permute-start.13) | collective-permute-done | bytes 245792 | tf_op jit(solution)/shard_map/ppermute | solution.py:340
  62.1 2.7 %collective-permute-start.16 = (bf16[48,2560]{1,0:T(8,128)(2,1)S(1)}, bf16[48,2560]{1,0:T(8,128)(2,1)S(1)}, u32[]{:S(2)}, u32[]{:S(2)}) collective-permute-start(bf16[48,2560]{1,0:T(8,128)(2,1)S(1)} %shard_map.132.after_ref.mine_ref), channel_id=1, source_target_pairs={{0,8},{4,12},{8,0},{12,4},{1,9},{5,13},{9,1},{13,5},{2,10},{6,14},... | collective-permute-start | bytes 737288 | tf_op jit(solution)/shard_map/ppermute | solution.py:370
  64.9 1.3 %collective-permute-start.15 = (bf16[48,2560]{1,0:T(8,128)(2,1)S(1)}, bf16[48,2560]{1,0:T(8,128)(2,1)S(1)}, u32[]{:S(2)}, u32[]{:S(2)}) collective-permute-start(bf16[48,2560]{1,0:T(8,128)(2,1)S(1)} %shard_map.133.after_ref.mine_ref), channel_id=1, source_target_pairs={{4,0},{8,12},{5,1},{9,13},{6,2},{10,14},{7,3},{11,15},{20,16},{24,... | collective-permute-start | bytes 737288 | tf_op jit(solution)/shard_map/ppermute | solution.py:340
  66.2 2.7 %collective-permute-done.17.came_ref = bf16[48,2560]{1,0:T(8,128)(2,1)S(1)} collective-permute-done((bf16[48,2560]{1,0:T(8,128)(2,1)S(1)}, bf16[48,2560]{1,0:T(8,128)(2,1)S(1)}, u32[]{:S(2)}, u32[]{:S(2)}) %collective-permute-start.17) | collective-permute-done | bytes 245792 | tf_op jit(solution)/shard_map/ppermute | solution.py:340
  69.0 1.0 %shard_map.137.after_ref = bf16[288,320]{1,0:T(8,128)(2,1)S(1)} custom-call(bf16[48,2560]{1,0:T(8,128)(2,1)S(1)} %shard_map.135.after_ref.rest_7_.rest_6_, bf16[320,2176]{1,0:T(8,128)(2,1)S(1)} %collective-permute-done.18.rest_0_, bf16[320,384]{1,0:T(8,128)(2,1)S(1)} %collective-permute-done.19.rest_1_, ...), custom_call_target="tpu_custom_call" | custom-call | tf_op jit(solution)/shard_map/pallas_call | solution.py:245
  70.0 0.9 shard_map.138.after_ref.own_ref
  71.0 1.0 %collective-permute-done.16.came_ref = bf16[48,2560]{1,0:T(8,128)(2,1)S(1)} collective-permute-done((bf16[48,2560]{1,0:T(8,128)(2,1)S(1)}, bf16[48,2560]{1,0:T(8,128)(2,1)S(1)}, u32[]{:S(2)}, u32[]{:S(2)}) %collective-permute-start.16) | collective-permute-done | bytes 245792 | tf_op jit(solution)/shard_map/ppermute | solution.py:370
  72.0 2.5 %collective-permute-done.15.came_ref = bf16[48,2560]{1,0:T(8,128)(2,1)S(1)} collective-permute-done((bf16[48,2560]{1,0:T(8,128)(2,1)S(1)}, bf16[48,2560]{1,0:T(8,128)(2,1)S(1)}, u32[]{:S(2)}, u32[]{:S(2)}) %collective-permute-start.15) | collective-permute-done | bytes 245792 | tf_op jit(solution)/shard_map/ppermute | solution.py:340
  75.2 1.8 %collective-permute-start.20 = (bf16[96,320]{1,0:T(8,128)(2,1)S(1)}, bf16[96,320]{1,0:T(8,128)(2,1)S(1)}, u32[]{:S(2)}, u32[]{:S(2)}) collective-permute-start(bf16[96,320]{1,0:T(8,128)(2,1)S(1)} %shard_map.141.after_ref), channel_id=1, source_target_pairs={{0,16},{16,0},{1,17},{17,1},{2,18},{18,2},{3,19},{19,3},{4,20},{20... | collective-permute-start | bytes 184328 | tf_op jit(solution)/shard_map/ppermute | solution.py:355
  77.0 0.8 shard_map.143.rest_0_
  78.5 1.2 %collective-permute-done.20.other_ref = bf16[96,320]{1,0:T(8,128)(2,1)S(1)} collective-permute-done((bf16[96,320]{1,0:T(8,128)(2,1)S(1)}, bf16[96,320]{1,0:T(8,128)(2,1)S(1)}, u32[]{:S(2)}, u32[]{:S(2)}) %collective-permute-start.20) | collective-permute-done | bytes 61472 | tf_op jit(solution)/shard_map/ppermute | solution.py:355
  79.6 0.7 shard_map.144
  80.4 1.2 %collective-permute-done.22 = f32[12,384]{1,0:T(8,128)S(1)} collective-permute-done((f32[12,384]{1,0:T(8,128)S(1)}, f32[12,384]{1,0:T(8,128)S(1)}, u32[]{:S(2)}, u32[]{:S(2)}) %collective-permute-start.22) | collective-permute-done | bytes 18464 | tf_op jit(solution)/shard_map/ppermute | solution.py:411
  81.6 1.5 %collective-permute-start.23 = (f32[12,384]{1,0:T(8,128)S(1)}, f32[12,384]{1,0:T(8,128)S(1)}, u32[]{:S(2)}, u32[]{:S(2)}) collective-permute-start(f32[12,384]{1,0:T(8,128)S(1)} %add.12), channel_id=1, source_target_pairs={{0,2},{1,3},{2,0},{3,1},{4,6},{5,7},{6,4},{7,5},{8,10},{9,11},{10,... | collective-permute-start | bytes 55304 | tf_op jit(solution)/shard_map/ppermute | solution.py:411
  83.1 2.3 %collective-permute-done.23 = f32[12,384]{1,0:T(8,128)S(1)} collective-permute-done((f32[12,384]{1,0:T(8,128)S(1)}, f32[12,384]{1,0:T(8,128)S(1)}, u32[]{:S(2)}, u32[]{:S(2)}) %collective-permute-start.23) | collective-permute-done | bytes 18464 | tf_op jit(solution)/shard_map/ppermute | solution.py:411
  85.6 2.5 %collective-permute-start.25 = (f32[1,96]{1,0:T(1,128)S(1)}, f32[1,96]{1,0:T(1,128)S(1)}, u32[]{:S(2)}, u32[]{:S(2)}) collective-permute-start(f32[1,96]{1,0:T(1,128)S(1)} %reshape.12), channel_id=1, source_target_pairs={{0,8},{4,12},{8,0},{12,4},{1,9},{5,13},{9,1},{13,5},{2,10},{6,14},... | collective-permute-start | bytes 1160 | tf_op jit(solution)/shard_map/ppermute | solution.py:421
  88.1 1.9 %collective-permute-start.26 = (f32[1,96]{1,0:T(1,128)S(1)}, f32[1,96]{1,0:T(1,128)S(1)}, u32[]{:S(2)}, u32[]{:S(2)}) collective-permute-start(f32[1,96]{1,0:T(1,128)S(1)} %reshape.12), channel_id=1, source_target_pairs={{0,12},{4,8},{8,4},{12,0},{1,13},{5,9},{9,5},{13,1},{2,14},{6,10},... | collective-permute-start | bytes 1160 | tf_op jit(solution)/shard_map/ppermute | solution.py:421
  90.1 3.3 %collective-permute-done.26 = f32[1,96]{1,0:T(1,128)S(1)} collective-permute-done((f32[1,96]{1,0:T(1,128)S(1)}, f32[1,96]{1,0:T(1,128)S(1)}, u32[]{:S(2)}, u32[]{:S(2)}) %collective-permute-start.26) | collective-permute-done | bytes 416 | tf_op jit(solution)/shard_map/ppermute | solution.py:421
  93.5 0.7 select_reduce_fusion
  (71 shorter events, 8.6 us)
Async XLA Ops:
  4.4 10.5 %collective-permute-start = (bf16[48,2560]{1,0:T(8,128)(2,1)S(1)}, bf16[48,2560]{1,0:T(8,128)(2,1)S(1)}, u32[]{:S(2)}, u32[]{:S(2)}) collective-permute-start(bf16[48,2560]{1,0:T(8,128)(2,1)S(1)} %get-tuple-element.33), channel_id=1, source_target_pairs={{0,4},{12,8},{4,0},{8,12},{1,5},{13,9},{5,1},{9,13},{2,6},{14,10},... | collective-permute-start | bytes 737288 | tf_op jit(solution)/shard_map/ppermute | solution.py:340
  10.9 58.0 %collective-permute-start.18 = (bf16[320,2176]{1,0:T(8,128)(2,1)S(1)}, bf16[320,2176]{1,0:T(8,128)(2,1)S(1)}, u32[]{:S(2)}, u32[]{:S(2)}) collective-permute-start(bf16[320,2176]{1,0:T(8,128)(2,1)S(1)} %get-tuple-element.51), channel_id=1, source_target_pairs={{0,16},{16,0},{1,17},{17,1},{2,18},{18,2},{3,19},{19,3},{4,20},{20... | collective-permute-start | bytes 4177928 | tf_op jit(solution)/shard_map/ppermute | solution.py:348
  12.5 8.4 %collective-permute-start.2 = (bf16[48,2560]{1,0:T(8,128)(2,1)S(1)}, bf16[48,2560]{1,0:T(8,128)(2,1)S(1)}, u32[]{:S(2)}, u32[]{:S(2)}) collective-permute-start(bf16[48,2560]{1,0:T(8,128)(2,1)S(1)} %get-tuple-element.36.mine_ref), channel_id=1, source_target_pairs={{0,4},{12,8},{1,5},{13,9},{2,6},{14,10},{3,7},{15,11},{16,20},{28,... | collective-permute-start | bytes 737288 | tf_op jit(solution)/shard_map/ppermute | solution.py:340
  15.0 6.7 %collective-permute-start.1 = (bf16[48,2560]{1,0:T(8,128)(2,1)S(1)}, bf16[48,2560]{1,0:T(8,128)(2,1)S(1)}, u32[]{:S(2)}, u32[]{:S(2)}) collective-permute-start(bf16[48,2560]{1,0:T(8,128)(2,1)S(1)} %get-tuple-element.35.after_ref.mine_ref), channel_id=1, source_target_pairs={{4,8},{8,4},{5,9},{9,5},{6,10},{10,6},{7,11},{11,7},{20,24},{24,20... | collective-permute-start | bytes 737288 | tf_op jit(solution)/shard_map/ppermute | solution.py:340
  15.7 12.9 %collective-permute-start.5 = (bf16[48,2560]{1,0:T(8,128)(2,1)S(1)}, bf16[48,2560]{1,0:T(8,128)(2,1)S(1)}, u32[]{:S(2)}, u32[]{:S(2)}) collective-permute-start(bf16[48,2560]{1,0:T(8,128)(2,1)S(1)} %get-tuple-element.38), channel_id=1, source_target_pairs={{0,4},{12,8},{1,5},{13,9},{2,6},{14,10},{3,7},{15,11},{16,20},{28,... | collective-permute-start | bytes 737288 | tf_op jit(solution)/shard_map/ppermute | solution.py:340
  21.0 8.4 %collective-permute-start.4 = (bf16[48,2560]{1,0:T(8,128)(2,1)S(1)}, bf16[48,2560]{1,0:T(8,128)(2,1)S(1)}, u32[]{:S(2)}, u32[]{:S(2)}) collective-permute-start(bf16[48,2560]{1,0:T(8,128)(2,1)S(1)} %shard_map.116.after_ref.mine_ref), channel_id=1, source_target_pairs={{4,8},{8,4},{5,9},{9,5},{6,10},{10,6},{7,11},{11,7},{20,24},{24,20... | collective-permute-start | bytes 737288 | tf_op jit(solution)/shard_map/ppermute | solution.py:340
  21.7 12.8 %collective-permute-start.3 = (bf16[48,2560]{1,0:T(8,128)(2,1)S(1)}, bf16[48,2560]{1,0:T(8,128)(2,1)S(1)}, u32[]{:S(2)}, u32[]{:S(2)}) collective-permute-start(bf16[48,2560]{1,0:T(8,128)(2,1)S(1)} %get-tuple-element.37), channel_id=1, source_target_pairs={{0,4},{12,8},{4,0},{8,12},{1,5},{13,9},{5,1},{9,13},{2,6},{14,10},... | collective-permute-start | bytes 737288 | tf_op jit(solution)/shard_map/ppermute | solution.py:340
  28.7 6.6 %collective-permute-start.8 = (bf16[48,2560]{1,0:T(8,128)(2,1)S(1)}, bf16[48,2560]{1,0:T(8,128)(2,1)S(1)}, u32[]{:S(2)}, u32[]{:S(2)}) collective-permute-start(bf16[48,2560]{1,0:T(8,128)(2,1)S(1)} %shard_map.118.after_ref.mine_ref), channel_id=1, source_target_pairs={{4,8},{8,4},{5,9},{9,5},{6,10},{10,6},{7,11},{11,7},{20,24},{24,20... | collective-permute-start | bytes 737288 | tf_op jit(solution)/shard_map/ppermute | solution.py:340
  29.4 11.0 %collective-permute-start.7 = (bf16[48,2560]{1,0:T(8,128)(2,1)S(1)}, bf16[48,2560]{1,0:T(8,128)(2,1)S(1)}, u32[]{:S(2)}, u32[]{:S(2)}) collective-permute-start(bf16[48,2560]{1,0:T(8,128)(2,1)S(1)} %get-tuple-element.42), channel_id=1, source_target_pairs={{0,4},{12,8},{4,0},{8,12},{1,5},{13,9},{5,1},{9,13},{2,6},{14,10},... | collective-permute-start | bytes 737288 | tf_op jit(solution)/shard_map/ppermute | solution.py:340
  34.6 6.6 %collective-permute-start.6 = (bf16[48,2560]{1,0:T(8,128)(2,1)S(1)}, bf16[48,2560]{1,0:T(8,128)(2,1)S(1)}, u32[]{:S(2)}, u32[]{:S(2)}) collective-permute-start(bf16[48,2560]{1,0:T(8,128)(2,1)S(1)} %shard_map.120.after_ref.mine_ref), channel_id=1, source_target_pairs={{4,8},{8,4},{5,9},{9,5},{6,10},{10,6},{7,11},{11,7},{20,24},{24,20... | collective-permute-start | bytes 737288 | tf_op jit(solution)/shard_map/ppermute | solution.py:340
  35.4 12.2 %collective-permute-start.10 = (bf16[48,2560]{1,0:T(8,128)(2,1)S(1)}, bf16[48,2560]{1,0:T(8,128)(2,1)S(1)}, u32[]{:S(2)}, u32[]{:S(2)}) collective-permute-start(bf16[48,2560]{1,0:T(8,128)(2,1)S(1)} %get-tuple-element.46), channel_id=1, source_target_pairs={{0,4},{12,8},{4,0},{8,12},{1,5},{13,9},{5,1},{9,13},{2,6},{14,10},... | collective-permute-start | bytes 737288 | tf_op jit(solution)/shard_map/ppermute | solution.py:340
  40.5 7.8 %collective-permute-start.11 = (bf16[48,2560]{1,0:T(8,128)(2,1)S(1)}, bf16[48,2560]{1,0:T(8,128)(2,1)S(1)}, u32[]{:S(2)}, u32[]{:S(2)}) collective-permute-start(bf16[48,2560]{1,0:T(8,128)(2,1)S(1)} %shard_map.123.after_ref.mine_ref), channel_id=1, source_target_pairs={{4,8},{8,4},{5,9},{9,5},{6,10},{10,6},{7,11},{11,7},{20,24},{24,20... | collective-permute-start | bytes 737288 | tf_op jit(solution)/shard_map/ppermute | solution.py:340
  41.2 12.8 %collective-permute-start.9 = (bf16[48,2560]{1,0:T(8,128)(2,1)S(1)}, bf16[48,2560]{1,0:T(8,128)(2,1)S(1)}, u32[]{:S(2)}, u32[]{:S(2)}) collective-permute-start(bf16[48,2560]{1,0:T(8,128)(2,1)S(1)} %get-tuple-element.45), channel_id=1, source_target_pairs={{0,4},{12,8},{4,0},{8,12},{1,5},{13,9},{5,1},{9,13},{2,6},{14,10},... | collective-permute-start | bytes 737288 | tf_op jit(solution)/shard_map/ppermute | solution.py:340
  47.6 7.2 %collective-permute-start.14 = (bf16[48,2560]{1,0:T(8,128)(2,1)S(1)}, bf16[48,2560]{1,0:T(8,128)(2,1)S(1)}, u32[]{:S(2)}, u32[]{:S(2)}) collective-permute-start(bf16[48,2560]{1,0:T(8,128)(2,1)S(1)} %shard_map.126.after_ref.mine_ref), channel_id=1, source_target_pairs={{4,8},{8,4},{5,9},{9,5},{6,10},{10,6},{7,11},{11,7},{20,24},{24,20... | collective-permute-start | bytes 737288 | tf_op jit(solution)/shard_map/ppermute | solution.py:340
  48.4 13.6 %collective-permute-start.13 = (bf16[48,2560]{1,0:T(8,128)(2,1)S(1)}, bf16[48,2560]{1,0:T(8,128)(2,1)S(1)}, u32[]{:S(2)}, u32[]{:S(2)}) collective-permute-start(bf16[48,2560]{1,0:T(8,128)(2,1)S(1)} %get-tuple-element.50), channel_id=1, source_target_pairs={{0,4},{12,8},{4,0},{8,12},{1,5},{13,9},{5,1},{9,13},{2,6},{14,10},... | collective-permute-start | bytes 737288 | tf_op jit(solution)/shard_map/ppermute | solution.py:340
  54.1 10.7 %collective-permute-start.12 = (bf16[48,2560]{1,0:T(8,128)(2,1)S(1)}, bf16[48,2560]{1,0:T(8,128)(2,1)S(1)}, u32[]{:S(2)}, u32[]{:S(2)}) collective-permute-start(bf16[48,2560]{1,0:T(8,128)(2,1)S(1)} %shard_map.129.after_ref.mine_ref), channel_id=1, source_target_pairs={{4,8},{8,4},{5,9},{9,5},{6,10},{10,6},{7,11},{11,7},{20,24},{24,20... | collective-permute-start | bytes 737288 | tf_op jit(solution)/shard_map/ppermute | solution.py:340
  54.9 14.0 %collective-permute-start.17 = (bf16[48,2560]{1,0:T(8,128)(2,1)S(1)}, bf16[48,2560]{1,0:T(8,128)(2,1)S(1)}, u32[]{:S(2)}, u32[]{:S(2)}) collective-permute-start(bf16[48,2560]{1,0:T(8,128)(2,1)S(1)} %shard_map.130.after_ref.mine_ref), channel_id=1, source_target_pairs={{4,0},{8,12},{5,1},{9,13},{6,2},{10,14},{7,3},{11,15},{20,16},{24,... | collective-permute-start | bytes 737288 | tf_op jit(solution)/shard_map/ppermute | solution.py:340
  56.2 12.8 %collective-permute-start.19 = (bf16[320,384]{1,0:T(8,128)(2,1)S(1)}, bf16[320,384]{1,0:T(8,128)(2,1)S(1)}, u32[]{:S(2)}, u32[]{:S(2)}) collective-permute-start(bf16[320,384]{1,0:T(8,128)(2,1)S(1)} %get-tuple-element.52), channel_id=1, source_target_pairs={{0,16},{16,0},{1,17},{17,1},{2,18},{18,2},{3,19},{19,3},{4,20},{20... | collective-permute-start | bytes 737288 | tf_op jit(solution)/shard_map/ppermute | solution.py:348
  62.1 9.9 %collective-permute-start.16 = (bf16[48,2560]{1,0:T(8,128)(2,1)S(1)}, bf16[48,2560]{1,0:T(8,128)(2,1)S(1)}, u32[]{:S(2)}, u32[]{:S(2)}) collective-permute-start(bf16[48,2560]{1,0:T(8,128)(2,1)S(1)} %shard_map.132.after_ref.mine_ref), channel_id=1, source_target_pairs={{0,8},{4,12},{8,0},{12,4},{1,9},{5,13},{9,1},{13,5},{2,10},{6,14},... | collective-permute-start | bytes 737288 | tf_op jit(solution)/shard_map/ppermute | solution.py:370
  64.9 9.6 %collective-permute-start.15 = (bf16[48,2560]{1,0:T(8,128)(2,1)S(1)}, bf16[48,2560]{1,0:T(8,128)(2,1)S(1)}, u32[]{:S(2)}, u32[]{:S(2)}) collective-permute-start(bf16[48,2560]{1,0:T(8,128)(2,1)S(1)} %shard_map.133.after_ref.mine_ref), channel_id=1, source_target_pairs={{4,0},{8,12},{5,1},{9,13},{6,2},{10,14},{7,3},{11,15},{20,16},{24,... | collective-permute-start | bytes 737288 | tf_op jit(solution)/shard_map/ppermute | solution.py:340
  70.0 7.0 %collective-permute-start.21 = (bf16[288,320]{1,0:T(8,128)(2,1)S(1)}, bf16[288,320]{1,0:T(8,128)(2,1)S(1)}, u32[]{:S(2)}, u32[]{:S(2)}) collective-permute-start(bf16[288,320]{1,0:T(8,128)(2,1)S(1)} %shard_map.137.after_ref), channel_id=1, source_target_pairs={{0,16},{16,0},{1,17},{17,1},{2,18},{18,2},{3,19},{19,3},{4,20},{20... | collective-permute-start | bytes 552968 | tf_op jit(solution)/shard_map/ppermute | solution.py:355
  72.0 5.0 %copy-start = (s32[1,8]{1,0:T(1,128)S(1)}, s32[1,8]{1,0:T(1,128)}, u32[]{:S(2)}) copy-start(s32[1,8]{1,0:T(1,128)} %counts_ref.3) | copy-start | bytes 100
  75.2 14.8 %copy-start.2 = (s32[128]{0:T(128)S(1)}, s32[128]{0:T(128)}, u32[]{:S(2)}) copy-start(s32[128]{0:T(128)} %param.19) | copy-start | bytes 1540
  75.2 14.8 %copy-start.3 = (s32[128]{0:T(128)S(1)}, s32[128]{0:T(128)}, u32[]{:S(2)}) copy-start(s32[128]{0:T(128)} %param.17) | copy-start | bytes 1540
  75.2 14.8 %copy-start.4 = (s32[128,1]{0,1:T(1,128)S(1)}, s32[128,1]{0,1:T(1,128)}, u32[]{:S(2)}) copy-start(s32[128,1]{0,1:T(1,128)} %param.18) | copy-start | bytes 1540
  75.2 4.4 %collective-permute-start.20 = (bf16[96,320]{1,0:T(8,128)(2,1)S(1)}, bf16[96,320]{1,0:T(8,128)(2,1)S(1)}, u32[]{:S(2)}, u32[]{:S(2)}) collective-permute-start(bf16[96,320]{1,0:T(8,128)(2,1)S(1)} %shard_map.141.after_ref), channel_id=1, source_target_pairs={{0,16},{16,0},{1,17},{17,1},{2,18},{18,2},{3,19},{19,3},{4,20},{20... | collective-permute-start | bytes 184328 | tf_op jit(solution)/shard_map/ppermute | solution.py:355
  80.4 1.2 %collective-permute-start.22 = (f32[12,384]{1,0:T(8,128)S(1)}, f32[12,384]{1,0:T(8,128)S(1)}, u32[]{:S(2)}, u32[]{:S(2)}) collective-permute-start(f32[12,384]{1,0:T(8,128)S(1)} %shard_map.144), channel_id=1, source_target_pairs={{0,1},{1,0},{2,3},{3,2},{4,5},{5,4},{6,7},{7,6},{8,9},{9,8},{10,11... | collective-permute-start | bytes 55304 | tf_op jit(solution)/shard_map/ppermute | solution.py:411
  81.6 3.8 %collective-permute-start.23 = (f32[12,384]{1,0:T(8,128)S(1)}, f32[12,384]{1,0:T(8,128)S(1)}, u32[]{:S(2)}, u32[]{:S(2)}) collective-permute-start(f32[12,384]{1,0:T(8,128)S(1)} %add.12), channel_id=1, source_target_pairs={{0,2},{1,3},{2,0},{3,1},{4,6},{5,7},{6,4},{7,5},{8,10},{9,11},{10,... | collective-permute-start | bytes 55304 | tf_op jit(solution)/shard_map/ppermute | solution.py:411
  85.4 8.8 %copy-start.1 = (f32[12,384]{1,0:T(8,128)}, f32[12,384]{1,0:T(8,128)S(1)}, u32[]{:S(2)}) copy-start(f32[12,384]{1,0:T(8,128)S(1)} %add.13) | copy-start | bytes 55300
  85.6 4.5 %collective-permute-start.24 = (f32[1,96]{1,0:T(1,128)S(1)}, f32[1,96]{1,0:T(1,128)S(1)}, u32[]{:S(2)}, u32[]{:S(2)}) collective-permute-start(f32[1,96]{1,0:T(1,128)S(1)} %reshape.12), channel_id=1, source_target_pairs={{0,4},{4,0},{8,12},{12,8},{1,5},{5,1},{9,13},{13,9},{2,6},{6,2},{1... | collective-permute-start | bytes 1160 | tf_op jit(solution)/shard_map/ppermute | solution.py:421
  85.6 4.5 %collective-permute-start.25 = (f32[1,96]{1,0:T(1,128)S(1)}, f32[1,96]{1,0:T(1,128)S(1)}, u32[]{:S(2)}, u32[]{:S(2)}) collective-permute-start(f32[1,96]{1,0:T(1,128)S(1)} %reshape.12), channel_id=1, source_target_pairs={{0,8},{4,12},{8,0},{12,4},{1,9},{5,13},{9,1},{13,5},{2,10},{6,14},... | collective-permute-start | bytes 1160 | tf_op jit(solution)/shard_map/ppermute | solution.py:421
  88.1 5.3 %collective-permute-start.26 = (f32[1,96]{1,0:T(1,128)S(1)}, f32[1,96]{1,0:T(1,128)S(1)}, u32[]{:S(2)}, u32[]{:S(2)}) collective-permute-start(f32[1,96]{1,0:T(1,128)S(1)} %reshape.12), channel_id=1, source_target_pairs={{0,12},{4,8},{8,4},{12,0},{1,13},{5,9},{9,5},{13,1},{2,14},{6,10},... | collective-permute-start | bytes 1160 | tf_op jit(solution)/shard_map/ppermute | solution.py:421

commit v12 on v9

--- a/solution.py
+++ b/solution.py
@@ -284,7 +284,7 @@
 
 
 def chunk_rows(spread):
-    return spread // 8 if spread % 128 == 0 else RANK
+    return spread // 6 if spread % 192 == 0 else RANK
 
 
 def is_power(number):

time: 92.3 us -> 95.7 us (1.037)
  waiting for transfers between devices: 20.1 us -> 30.8 us
  starting transfers between devices: 57.6 us -> 50.5 us
    ppermute x17 -> x13, starting transfers between devices: 39.3 us -> 27.6 us  [transfer(): return lax.ppermute(value, 'dp', pairs)]
    ppermute x17 -> x13, waiting for transfers between devices: 10.6 us -> 22 us  [transfer(): return lax.ppermute(value, 'dp', pairs)]
    ppermute x2, starting transfers between devices: 5.53 us -> 9.12 us  [project_waiting(): back.append(lax.ppermute(away, 'parts', swap))]
    ppermute x1, starting transfers between devices: 4.12 us -> 5.97 us  [per_device(): came[c] = lax.ppermute(part[c], 'dp', [(i, i ^ 2) for i in range(n)])]
  transfers between devices with their start and end apart: 27 -> 23, of which waited for: 13 -> 10; matrix products, arithmetic and copies ran while one was open for 0% -> 0% of each run, Pallas kernels for 8% -> 8%
where the time goes in v12:
time: 95.7 us; the launch traced here: 95.4 us
  starting transfers between devices  50.5 us (53%)
  waiting for transfers between devices  30.8 us (32%)
  Pallas kernels  12.2 us (13%)
  between operations  1 us (1%)
    ppermute x13, starting transfers between devices, transfer(): return lax.ppermute(value, 'dp', pairs)  27.6 us
    ppermute x13, waiting for transfers between devices, transfer(): return lax.ppermute(value, 'dp', pairs)  22 us
    ppermute x2, starting transfers between devices, project_waiting(): back.append(lax.ppermute(away, 'parts', swap))  9.12 us
    ppermute x1, starting transfers between devices, per_device(): came[c] = lax.ppermute(part[c], 'dp', [(i, i ^ 2) for i in range(n)])  5.97 us
    ppermute x3, starting transfers between devices, per_device(): lax.ppermute(flat, 'dp', [(i, i ^ k) for i in range(n)])  4.44 us
    pallas_call x1, Pallas kernels, first_pull(): pl.pallas_call(first_pull_kernel, out_shape=[bf16(rows, features)] * 2 +...  3.67 us
    ppermute x2, waiting for transfers between devices, per_device(): lax.ppermute(scores, 'layer', [(i, i ^ step) for i in range(layers)])  3.52 us
    pallas_call x4, Pallas kernels, project(): pl.pallas_call(functools.partial(project_kernel, len(tokens)), out_shape=...  3.16 us
  transfers between devices with their start and end apart: 23, of which 10 were waited for; matrix products, arithmetic and copies ran while one was open for 0% of the time, Pallas kernels for 8%

profile of v12, /device:TPU:0, one launch (start us, length us, event | category | flops | bytes accessed | tf_op | source)
XLA Modules:
  0.0 95.4 jit_solution(9458226551482743496)
XLA Ops:
  0.6 3.7 %shard_map.113 = (bf16[64,2560]{1,0:T(8,128)(2,1)S(1)}, bf16[64,2560]{1,0:T(8,128)(2,1)S(1)}, bf16[2560,640]{1,0:T(8,128)(2,1)S(1)}, bf16[640,384]{1,0:T(8,128)(2,1)}, bf16[384,640]{1,0:T(8,128)(2,1)S(1)}) custom-call(bf16[2560,640]{1,0:T(8,128)(2,1)} %bitcast.9, bf16[2560,640]{1,0:T(8,128)(2,1)} %bitcast.10, bf16[640,384]{1,0:T(8,128)(2,1)} %bitcast.13, ...), custom_call_target="tpu_custom_call" | custom-call | tf_op jit(solution)/shard_map/pallas_call | solution.py:77
  4.3 3.1 %collective-permute-start = (bf16[64,2560]{1,0:T(8,128)(2,1)S(1)}, bf16[64,2560]{1,0:T(8,128)(2,1)S(1)}, u32[]{:S(2)}, u32[]{:S(2)}) collective-permute-start(bf16[64,2560]{1,0:T(8,128)(2,1)S(1)} %get-tuple-element.26), channel_id=1, source_target_pairs={{0,4},{12,8},{4,0},{8,12},{1,5},{13,9},{5,1},{9,13},{2,6},{14,10},... | collective-permute-start | bytes 983048 | tf_op jit(solution)/shard_map/ppermute | solution.py:334
  7.4 1.5 %shard_map.114 = (bf16[64,2560]{1,0:T(8,128)(2,1)S(1)}, bf16[64,2560]{1,0:T(8,128)(2,1)S(1)}, bf16[64,2560]{1,0:T(8,128)(2,1)S(1)}, bf16[64,2560]{1,0:T(8,128)(2,1)S(1)}, bf16[64,2560]{1,0:T(8,128)(2,1)S(1)}) custom-call(bf16[384,640]{1,0:T(8,128)(2,1)S(1)} %get-tuple-element.22.turned_ref, bf16[2560,640]{1,0:T(8,128)(2,1)S(1)} %get-tuple-element.23.basis_ref, ...), custom_call_target="tpu_custom_call" | custom-call | tf_op jit(solution)/shard_map/pallas_call | solution.py:101
  8.9 1.9 %collective-permute-start.2 = (bf16[64,2560]{1,0:T(8,128)(2,1)S(1)}, bf16[64,2560]{1,0:T(8,128)(2,1)S(1)}, u32[]{:S(2)}, u32[]{:S(2)}) collective-permute-start(bf16[64,2560]{1,0:T(8,128)(2,1)S(1)} %get-tuple-element.29.mine_ref), channel_id=1, source_target_pairs={{0,4},{12,8},{1,5},{13,9},{2,6},{14,10},{3,7},{15,11},{16,20},{28,... | collective-permute-start | bytes 983048 | tf_op jit(solution)/shard_map/ppermute | solution.py:334
  10.8 4.7 %collective-permute-done.came_ref.early_ref = bf16[64,2560]{1,0:T(8,128)(2,1)S(1)} collective-permute-done((bf16[64,2560]{1,0:T(8,128)(2,1)S(1)}, bf16[64,2560]{1,0:T(8,128)(2,1)S(1)}, u32[]{:S(2)}, u32[]{:S(2)}) %collective-permute-start) | collective-permute-done | bytes 327712 | tf_op jit(solution)/shard_map/ppermute | solution.py:334
  16.3 7.2 %collective-permute-start.5 = (bf16[64,2560]{1,0:T(8,128)(2,1)S(1)}, bf16[64,2560]{1,0:T(8,128)(2,1)S(1)}, u32[]{:S(2)}, u32[]{:S(2)}) collective-permute-start(bf16[64,2560]{1,0:T(8,128)(2,1)S(1)} %get-tuple-element.31), channel_id=1, source_target_pairs={{0,4},{12,8},{1,5},{13,9},{2,6},{14,10},{3,7},{15,11},{16,20},{28,... | collective-permute-start | bytes 983048 | tf_op jit(solution)/shard_map/ppermute | solution.py:334
  24.3 1.9 %shard_map.130 = (bf16[320,2560]{1,0:T(8,128)(2,1)S(1)}, bf16[320,1920]{1,0:T(8,128)(2,1)S(1)}, bf16[320,640]{1,0:T(8,128)(2,1)S(1)}) custom-call(bf16[320,2560]{1,0:T(8,128)(2,1)} %bitcast.11, bf16[320,2560]{1,0:T(8,128)(2,1)} %bitcast.12, bf16[64,2560]{1,0:T(8,128)(2,1)S(1)} %get-tuple-element.36.rest_0_.mine_ref.after_ref), custom_call_target="tpu_custom_call" | custom-call | tf_op jit(solution)/shard_map/pallas_call | solution.py:140
  26.2 1.6 %collective-permute-start.12 = (bf16[320,1920]{1,0:T(8,128)(2,1)S(1)}, bf16[320,1920]{1,0:T(8,128)(2,1)S(1)}, u32[]{:S(2)}, u32[]{:S(2)}) collective-permute-start(bf16[320,1920]{1,0:T(8,128)(2,1)S(1)} %get-tuple-element.39), channel_id=1, source_target_pairs={{0,16},{16,0},{1,17},{17,1},{2,18},{18,2},{3,19},{19,3},{4,20},{20... | collective-permute-start | bytes 3686408 | tf_op jit(solution)/shard_map/ppermute | solution.py:342
  27.9 4.4 %collective-permute-start.3 = (bf16[64,2560]{1,0:T(8,128)(2,1)S(1)}, bf16[64,2560]{1,0:T(8,128)(2,1)S(1)}, u32[]{:S(2)}, u32[]{:S(2)}) collective-permute-start(bf16[64,2560]{1,0:T(8,128)(2,1)S(1)} %get-tuple-element.30), channel_id=1, source_target_pairs={{0,4},{12,8},{4,0},{8,12},{1,5},{13,9},{5,1},{9,13},{2,6},{14,10},... | collective-permute-start | bytes 983048 | tf_op jit(solution)/shard_map/ppermute | solution.py:334
  33.1 1.7 %collective-permute-start.7 = (bf16[64,2560]{1,0:T(8,128)(2,1)S(1)}, bf16[64,2560]{1,0:T(8,128)(2,1)S(1)}, u32[]{:S(2)}, u32[]{:S(2)}) collective-permute-start(bf16[64,2560]{1,0:T(8,128)(2,1)S(1)} %get-tuple-element.35), channel_id=1, source_target_pairs={{0,4},{12,8},{4,0},{8,12},{1,5},{13,9},{5,1},{9,13},{2,6},{14,10},... | collective-permute-start | bytes 983048 | tf_op jit(solution)/shard_map/ppermute | solution.py:334
  34.8 6.0 %collective-permute-done.3.came_ref = bf16[64,2560]{1,0:T(8,128)(2,1)S(1)} collective-permute-done((bf16[64,2560]{1,0:T(8,128)(2,1)S(1)}, bf16[64,2560]{1,0:T(8,128)(2,1)S(1)}, u32[]{:S(2)}, u32[]{:S(2)}) %collective-permute-start.3) | collective-permute-done | bytes 327712 | tf_op jit(solution)/shard_map/ppermute | solution.py:334
  41.8 3.3 %collective-permute-start.10 = (bf16[64,2560]{1,0:T(8,128)(2,1)S(1)}, bf16[64,2560]{1,0:T(8,128)(2,1)S(1)}, u32[]{:S(2)}, u32[]{:S(2)}) collective-permute-start(bf16[64,2560]{1,0:T(8,128)(2,1)S(1)} %get-tuple-element.38), channel_id=1, source_target_pairs={{0,4},{12,8},{4,0},{8,12},{1,5},{13,9},{5,1},{9,13},{2,6},{14,10},... | collective-permute-start | bytes 983048 | tf_op jit(solution)/shard_map/ppermute | solution.py:334
  45.1 2.8 %collective-permute-done.7.came_ref = bf16[64,2560]{1,0:T(8,128)(2,1)S(1)} collective-permute-done((bf16[64,2560]{1,0:T(8,128)(2,1)S(1)}, bf16[64,2560]{1,0:T(8,128)(2,1)S(1)}, u32[]{:S(2)}, u32[]{:S(2)}) %collective-permute-start.7) | collective-permute-done | bytes 327712 | tf_op jit(solution)/shard_map/ppermute | solution.py:334
  49.0 1.3 %collective-permute-start.9 = (bf16[64,2560]{1,0:T(8,128)(2,1)S(1)}, bf16[64,2560]{1,0:T(8,128)(2,1)S(1)}, u32[]{:S(2)}, u32[]{:S(2)}) collective-permute-start(bf16[64,2560]{1,0:T(8,128)(2,1)S(1)} %shard_map.124.after_ref.mine_ref), channel_id=1, source_target_pairs={{4,0},{8,12},{5,1},{9,13},{6,2},{10,14},{7,3},{11,15},{20,16},{24,... | collective-permute-start | bytes 983048 | tf_op jit(solution)/shard_map/ppermute | solution.py:334
  50.4 3.5 %collective-permute-done.10.came_ref = bf16[64,2560]{1,0:T(8,128)(2,1)S(1)} collective-permute-done((bf16[64,2560]{1,0:T(8,128)(2,1)S(1)}, bf16[64,2560]{1,0:T(8,128)(2,1)S(1)}, u32[]{:S(2)}, u32[]{:S(2)}) %collective-permute-start.10) | collective-permute-done | bytes 327712 | tf_op jit(solution)/shard_map/ppermute | solution.py:334
  54.0 6.0 %collective-permute-start.15 = (bf16[64,2560]{1,0:T(8,128)(2,1)S(1)}, bf16[64,2560]{1,0:T(8,128)(2,1)S(1)}, u32[]{:S(2)}, u32[]{:S(2)}) collective-permute-start(bf16[64,2560]{1,0:T(8,128)(2,1)S(1)} %shard_map.126.after_ref.mine_ref), channel_id=1, source_target_pairs={{0,8},{4,12},{8,0},{12,4},{1,9},{5,13},{9,1},{13,5},{2,10},{6,14},... | collective-permute-start | bytes 983048 | tf_op jit(solution)/shard_map/ppermute | solution.py:364
  60.0 1.3 %collective-permute-start.14 = (bf16[64,2560]{1,0:T(8,128)(2,1)S(1)}, bf16[64,2560]{1,0:T(8,128)(2,1)S(1)}, u32[]{:S(2)}, u32[]{:S(2)}) collective-permute-start(bf16[64,2560]{1,0:T(8,128)(2,1)S(1)} %shard_map.127.after_ref.mine_ref), channel_id=1, source_target_pairs={{4,0},{8,12},{5,1},{9,13},{6,2},{10,14},{7,3},{11,15},{20,16},{24,... | collective-permute-start | bytes 983048 | tf_op jit(solution)/shard_map/ppermute | solution.py:334
  61.4 5.0 %collective-permute-done.9.came_ref = bf16[64,2560]{1,0:T(8,128)(2,1)S(1)} collective-permute-done((bf16[64,2560]{1,0:T(8,128)(2,1)S(1)}, bf16[64,2560]{1,0:T(8,128)(2,1)S(1)}, u32[]{:S(2)}, u32[]{:S(2)}) %collective-permute-start.9) | collective-permute-done | bytes 327712 | tf_op jit(solution)/shard_map/ppermute | solution.py:334
  66.4 0.9 shard_map.131.after_ref
  67.3 7.5 %collective-permute-start.16 = (bf16[256,320]{1,0:T(8,128)(2,1)S(1)}, bf16[256,320]{1,0:T(8,128)(2,1)S(1)}, u32[]{:S(2)}, u32[]{:S(2)}) collective-permute-start(bf16[256,320]{1,0:T(8,128)(2,1)S(1)} %shard_map.131.after_ref), channel_id=1, source_target_pairs={{0,16},{16,0},{1,17},{17,1},{2,18},{18,2},{3,19},{19,3},{4,20},{20... | collective-permute-start | bytes 491528 | tf_op jit(solution)/shard_map/ppermute | solution.py:349
  74.8 0.9 shard_map.132.after_ref.refs_0_
  75.8 0.7 shard_map.135.after_ref
  76.6 1.6 %collective-permute-start.17 = (bf16[128,320]{1,0:T(8,128)(2,1)S(1)}, bf16[128,320]{1,0:T(8,128)(2,1)S(1)}, u32[]{:S(2)}, u32[]{:S(2)}) collective-permute-start(bf16[128,320]{1,0:T(8,128)(2,1)S(1)} %shard_map.135.after_ref), channel_id=1, source_target_pairs={{0,16},{16,0},{1,17},{17,1},{2,18},{18,2},{3,19},{19,3},{4,20},{20... | collective-permute-start | bytes 245768 | tf_op jit(solution)/shard_map/ppermute | solution.py:349
  78.2 0.7 shard_map.136.refs_1_
  78.9 2.4 %collective-permute-done.17.refs_3_ = bf16[128,320]{1,0:T(8,128)(2,1)S(1)} collective-permute-done((bf16[128,320]{1,0:T(8,128)(2,1)S(1)}, bf16[128,320]{1,0:T(8,128)(2,1)S(1)}, u32[]{:S(2)}, u32[]{:S(2)}) %collective-permute-start.17) | collective-permute-done | bytes 81952 | tf_op jit(solution)/shard_map/ppermute | solution.py:349
  81.3 0.8 shard_map.137
  82.1 1.2 %collective-permute-done.18 = f32[12,384]{1,0:T(8,128)S(1)} collective-permute-done((f32[12,384]{1,0:T(8,128)S(1)}, f32[12,384]{1,0:T(8,128)S(1)}, u32[]{:S(2)}, u32[]{:S(2)}) %collective-permute-start.18) | collective-permute-done | bytes 18464 | tf_op jit(solution)/shard_map/ppermute | solution.py:400
  83.3 1.5 %collective-permute-start.19 = (f32[12,384]{1,0:T(8,128)S(1)}, f32[12,384]{1,0:T(8,128)S(1)}, u32[]{:S(2)}, u32[]{:S(2)}) collective-permute-start(f32[12,384]{1,0:T(8,128)S(1)} %add.12), channel_id=1, source_target_pairs={{0,2},{1,3},{2,0},{3,1},{4,6},{5,7},{6,4},{7,5},{8,10},{9,11},{10,... | collective-permute-start | bytes 55304 | tf_op jit(solution)/shard_map/ppermute | solution.py:400
  84.8 2.3 %collective-permute-done.19 = f32[12,384]{1,0:T(8,128)S(1)} collective-permute-done((f32[12,384]{1,0:T(8,128)S(1)}, f32[12,384]{1,0:T(8,128)S(1)}, u32[]{:S(2)}, u32[]{:S(2)}) %collective-permute-start.19) | collective-permute-done | bytes 18464 | tf_op jit(solution)/shard_map/ppermute | solution.py:400
  87.4 1.9 %collective-permute-start.21 = (f32[1,96]{1,0:T(1,128)S(1)}, f32[1,96]{1,0:T(1,128)S(1)}, u32[]{:S(2)}, u32[]{:S(2)}) collective-permute-start(f32[1,96]{1,0:T(1,128)S(1)} %reshape.12), channel_id=1, source_target_pairs={{0,8},{4,12},{8,0},{12,4},{1,9},{5,13},{9,1},{13,5},{2,10},{6,14},... | collective-permute-start | bytes 1160 | tf_op jit(solution)/shard_map/ppermute | solution.py:410
  89.3 2.5 %collective-permute-start.22 = (f32[1,96]{1,0:T(1,128)S(1)}, f32[1,96]{1,0:T(1,128)S(1)}, u32[]{:S(2)}, u32[]{:S(2)}) collective-permute-start(f32[1,96]{1,0:T(1,128)S(1)} %reshape.12), channel_id=1, source_target_pairs={{0,12},{4,8},{8,4},{12,0},{1,13},{5,9},{9,5},{13,1},{2,14},{6,10},... | collective-permute-start | bytes 1160 | tf_op jit(solution)/shard_map/ppermute | solution.py:410
  91.9 2.7 %collective-permute-done.22 = f32[1,96]{1,0:T(1,128)S(1)} collective-permute-done((f32[1,96]{1,0:T(1,128)S(1)}, f32[1,96]{1,0:T(1,128)S(1)}, u32[]{:S(2)}, u32[]{:S(2)}) %collective-permute-start.22) | collective-permute-done | bytes 416 | tf_op jit(solution)/shard_map/ppermute | solution.py:410
  (56 shorter events, 6.0 us)
Async XLA Ops:
  4.3 11.2 %collective-permute-start = (bf16[64,2560]{1,0:T(8,128)(2,1)S(1)}, bf16[64,2560]{1,0:T(8,128)(2,1)S(1)}, u32[]{:S(2)}, u32[]{:S(2)}) collective-permute-start(bf16[64,2560]{1,0:T(8,128)(2,1)S(1)} %get-tuple-element.26), channel_id=1, source_target_pairs={{0,4},{12,8},{4,0},{8,12},{1,5},{13,9},{5,1},{9,13},{2,6},{14,10},... | collective-permute-start | bytes 983048 | tf_op jit(solution)/shard_map/ppermute | solution.py:334
  8.9 14.6 %collective-permute-start.2 = (bf16[64,2560]{1,0:T(8,128)(2,1)S(1)}, bf16[64,2560]{1,0:T(8,128)(2,1)S(1)}, u32[]{:S(2)}, u32[]{:S(2)}) collective-permute-start(bf16[64,2560]{1,0:T(8,128)(2,1)S(1)} %get-tuple-element.29.mine_ref), channel_id=1, source_target_pairs={{0,4},{12,8},{1,5},{13,9},{2,6},{14,10},{3,7},{15,11},{16,20},{28,... | collective-permute-start | bytes 983048 | tf_op jit(solution)/shard_map/ppermute | solution.py:334
  15.6 12.2 %collective-permute-start.1 = (bf16[64,2560]{1,0:T(8,128)(2,1)S(1)}, bf16[64,2560]{1,0:T(8,128)(2,1)S(1)}, u32[]{:S(2)}, u32[]{:S(2)}) collective-permute-start(bf16[64,2560]{1,0:T(8,128)(2,1)S(1)} %get-tuple-element.28.after_ref.mine_ref), channel_id=1, source_target_pairs={{4,8},{8,4},{5,9},{9,5},{6,10},{10,6},{7,11},{11,7},{20,24},{24,20... | collective-permute-start | bytes 983048 | tf_op jit(solution)/shard_map/ppermute | solution.py:334
  16.3 16.0 %collective-permute-start.5 = (bf16[64,2560]{1,0:T(8,128)(2,1)S(1)}, bf16[64,2560]{1,0:T(8,128)(2,1)S(1)}, u32[]{:S(2)}, u32[]{:S(2)}) collective-permute-start(bf16[64,2560]{1,0:T(8,128)(2,1)S(1)} %get-tuple-element.31), channel_id=1, source_target_pairs={{0,4},{12,8},{1,5},{13,9},{2,6},{14,10},{3,7},{15,11},{16,20},{28,... | collective-permute-start | bytes 983048 | tf_op jit(solution)/shard_map/ppermute | solution.py:334
  23.6 9.4 %collective-permute-start.4 = (bf16[64,2560]{1,0:T(8,128)(2,1)S(1)}, bf16[64,2560]{1,0:T(8,128)(2,1)S(1)}, u32[]{:S(2)}, u32[]{:S(2)}) collective-permute-start(bf16[64,2560]{1,0:T(8,128)(2,1)S(1)} %shard_map.116.after_ref.mine_ref), channel_id=1, source_target_pairs={{4,8},{8,4},{5,9},{9,5},{6,10},{10,6},{7,11},{11,7},{20,24},{24,20... | collective-permute-start | bytes 983048 | tf_op jit(solution)/shard_map/ppermute | solution.py:334
  26.2 40.2 %collective-permute-start.12 = (bf16[320,1920]{1,0:T(8,128)(2,1)S(1)}, bf16[320,1920]{1,0:T(8,128)(2,1)S(1)}, u32[]{:S(2)}, u32[]{:S(2)}) collective-permute-start(bf16[320,1920]{1,0:T(8,128)(2,1)S(1)} %get-tuple-element.39), channel_id=1, source_target_pairs={{0,16},{16,0},{1,17},{17,1},{2,18},{18,2},{3,19},{19,3},{4,20},{20... | collective-permute-start | bytes 3686408 | tf_op jit(solution)/shard_map/ppermute | solution.py:342
  27.9 13.0 %collective-permute-start.3 = (bf16[64,2560]{1,0:T(8,128)(2,1)S(1)}, bf16[64,2560]{1,0:T(8,128)(2,1)S(1)}, u32[]{:S(2)}, u32[]{:S(2)}) collective-permute-start(bf16[64,2560]{1,0:T(8,128)(2,1)S(1)} %get-tuple-element.30), channel_id=1, source_target_pairs={{0,4},{12,8},{4,0},{8,12},{1,5},{13,9},{5,1},{9,13},{2,6},{14,10},... | collective-permute-start | bytes 983048 | tf_op jit(solution)/shard_map/ppermute | solution.py:334
  32.3 9.3 %collective-permute-start.8 = (bf16[64,2560]{1,0:T(8,128)(2,1)S(1)}, bf16[64,2560]{1,0:T(8,128)(2,1)S(1)}, u32[]{:S(2)}, u32[]{:S(2)}) collective-permute-start(bf16[64,2560]{1,0:T(8,128)(2,1)S(1)} %shard_map.118.after_ref.mine_ref), channel_id=1, source_target_pairs={{4,8},{8,4},{5,9},{9,5},{6,10},{10,6},{7,11},{11,7},{20,24},{24,20... | collective-permute-start | bytes 983048 | tf_op jit(solution)/shard_map/ppermute | solution.py:334
  33.1 14.8 %collective-permute-start.7 = (bf16[64,2560]{1,0:T(8,128)(2,1)S(1)}, bf16[64,2560]{1,0:T(8,128)(2,1)S(1)}, u32[]{:S(2)}, u32[]{:S(2)}) collective-permute-start(bf16[64,2560]{1,0:T(8,128)(2,1)S(1)} %get-tuple-element.35), channel_id=1, source_target_pairs={{0,4},{12,8},{4,0},{8,12},{1,5},{13,9},{5,1},{9,13},{2,6},{14,10},... | collective-permute-start | bytes 983048 | tf_op jit(solution)/shard_map/ppermute | solution.py:334
  41.0 8.0 %collective-permute-start.6 = (bf16[64,2560]{1,0:T(8,128)(2,1)S(1)}, bf16[64,2560]{1,0:T(8,128)(2,1)S(1)}, u32[]{:S(2)}, u32[]{:S(2)}) collective-permute-start(bf16[64,2560]{1,0:T(8,128)(2,1)S(1)} %shard_map.120.after_ref.mine_ref), channel_id=1, source_target_pairs={{4,8},{8,4},{5,9},{9,5},{6,10},{10,6},{7,11},{11,7},{20,24},{24,20... | collective-permute-start | bytes 983048 | tf_op jit(solution)/shard_map/ppermute | solution.py:334
  41.8 12.1 %collective-permute-start.10 = (bf16[64,2560]{1,0:T(8,128)(2,1)S(1)}, bf16[64,2560]{1,0:T(8,128)(2,1)S(1)}, u32[]{:S(2)}, u32[]{:S(2)}) collective-permute-start(bf16[64,2560]{1,0:T(8,128)(2,1)S(1)} %get-tuple-element.38), channel_id=1, source_target_pairs={{0,4},{12,8},{4,0},{8,12},{1,5},{13,9},{5,1},{9,13},{2,6},{14,10},... | collective-permute-start | bytes 983048 | tf_op jit(solution)/shard_map/ppermute | solution.py:334
  48.0 12.0 %collective-permute-start.11 = (bf16[64,2560]{1,0:T(8,128)(2,1)S(1)}, bf16[64,2560]{1,0:T(8,128)(2,1)S(1)}, u32[]{:S(2)}, u32[]{:S(2)}) collective-permute-start(bf16[64,2560]{1,0:T(8,128)(2,1)S(1)} %shard_map.123.after_ref.mine_ref), channel_id=1, source_target_pairs={{4,8},{8,4},{5,9},{9,5},{6,10},{10,6},{7,11},{11,7},{20,24},{24,20... | collective-permute-start | bytes 983048 | tf_op jit(solution)/shard_map/ppermute | solution.py:334
  48.7 17.7 %collective-permute-start.13 = (bf16[320,640]{1,0:T(8,128)(2,1)S(1)}, bf16[320,640]{1,0:T(8,128)(2,1)S(1)}, u32[]{:S(2)}, u32[]{:S(2)}) collective-permute-start(bf16[320,640]{1,0:T(8,128)(2,1)S(1)} %get-tuple-element.40), channel_id=1, source_target_pairs={{0,16},{16,0},{1,17},{17,1},{2,18},{18,2},{3,19},{19,3},{4,20},{20... | collective-permute-start | bytes 1228808 | tf_op jit(solution)/shard_map/ppermute | solution.py:342
  49.0 17.4 %collective-permute-start.9 = (bf16[64,2560]{1,0:T(8,128)(2,1)S(1)}, bf16[64,2560]{1,0:T(8,128)(2,1)S(1)}, u32[]{:S(2)}, u32[]{:S(2)}) collective-permute-start(bf16[64,2560]{1,0:T(8,128)(2,1)S(1)} %shard_map.124.after_ref.mine_ref), channel_id=1, source_target_pairs={{4,0},{8,12},{5,1},{9,13},{6,2},{10,14},{7,3},{11,15},{20,16},{24,... | collective-permute-start | bytes 983048 | tf_op jit(solution)/shard_map/ppermute | solution.py:334
  54.0 21.7 %collective-permute-start.15 = (bf16[64,2560]{1,0:T(8,128)(2,1)S(1)}, bf16[64,2560]{1,0:T(8,128)(2,1)S(1)}, u32[]{:S(2)}, u32[]{:S(2)}) collective-permute-start(bf16[64,2560]{1,0:T(8,128)(2,1)S(1)} %shard_map.126.after_ref.mine_ref), channel_id=1, source_target_pairs={{0,8},{4,12},{8,0},{12,4},{1,9},{5,13},{9,1},{13,5},{2,10},{6,14},... | collective-permute-start | bytes 983048 | tf_op jit(solution)/shard_map/ppermute | solution.py:364
  60.0 15.7 %collective-permute-start.14 = (bf16[64,2560]{1,0:T(8,128)(2,1)S(1)}, bf16[64,2560]{1,0:T(8,128)(2,1)S(1)}, u32[]{:S(2)}, u32[]{:S(2)}) collective-permute-start(bf16[64,2560]{1,0:T(8,128)(2,1)S(1)} %shard_map.127.after_ref.mine_ref), channel_id=1, source_target_pairs={{4,0},{8,12},{5,1},{9,13},{6,2},{10,14},{7,3},{11,15},{20,16},{24,... | collective-permute-start | bytes 983048 | tf_op jit(solution)/shard_map/ppermute | solution.py:334
  67.3 14.0 %collective-permute-start.16 = (bf16[256,320]{1,0:T(8,128)(2,1)S(1)}, bf16[256,320]{1,0:T(8,128)(2,1)S(1)}, u32[]{:S(2)}, u32[]{:S(2)}) collective-permute-start(bf16[256,320]{1,0:T(8,128)(2,1)S(1)} %shard_map.131.after_ref), channel_id=1, source_target_pairs={{0,16},{16,0},{1,17},{17,1},{2,18},{18,2},{3,19},{19,3},{4,20},{20... | collective-permute-start | bytes 491528 | tf_op jit(solution)/shard_map/ppermute | solution.py:349
  76.6 4.7 %copy-start = (s32[1,8]{1,0:T(1,128)S(1)}, s32[1,8]{1,0:T(1,128)}, u32[]{:S(2)}) copy-start(s32[1,8]{1,0:T(1,128)} %counts_ref.1) | copy-start | bytes 100
  76.6 15.2 %copy-start.2 = (s32[128]{0:T(128)S(1)}, s32[128]{0:T(128)}, u32[]{:S(2)}) copy-start(s32[128]{0:T(128)} %param.19) | copy-start | bytes 1540
  76.6 15.2 %copy-start.3 = (s32[128]{0:T(128)S(1)}, s32[128]{0:T(128)}, u32[]{:S(2)}) copy-start(s32[128]{0:T(128)} %param.17) | copy-start | bytes 1540
  76.6 15.2 %copy-start.4 = (s32[128,1]{0,1:T(1,128)S(1)}, s32[128,1]{0,1:T(1,128)}, u32[]{:S(2)}) copy-start(s32[128,1]{0,1:T(1,128)} %param.18) | copy-start | bytes 1540
  76.6 4.7 %collective-permute-start.17 = (bf16[128,320]{1,0:T(8,128)(2,1)S(1)}, bf16[128,320]{1,0:T(8,128)(2,1)S(1)}, u32[]{:S(2)}, u32[]{:S(2)}) collective-permute-start(bf16[128,320]{1,0:T(8,128)(2,1)S(1)} %shard_map.135.after_ref), channel_id=1, source_target_pairs={{0,16},{16,0},{1,17},{17,1},{2,18},{18,2},{3,19},{19,3},{4,20},{20... | collective-permute-start | bytes 245768 | tf_op jit(solution)/shard_map/ppermute | solution.py:349
  82.1 1.2 %collective-permute-start.18 = (f32[12,384]{1,0:T(8,128)S(1)}, f32[12,384]{1,0:T(8,128)S(1)}, u32[]{:S(2)}, u32[]{:S(2)}) collective-permute-start(f32[12,384]{1,0:T(8,128)S(1)} %shard_map.137), channel_id=1, source_target_pairs={{0,1},{1,0},{2,3},{3,2},{4,5},{5,4},{6,7},{7,6},{8,9},{9,8},{10,11... | collective-permute-start | bytes 55304 | tf_op jit(solution)/shard_map/ppermute | solution.py:400
  83.3 3.8 %collective-permute-start.19 = (f32[12,384]{1,0:T(8,128)S(1)}, f32[12,384]{1,0:T(8,128)S(1)}, u32[]{:S(2)}, u32[]{:S(2)}) collective-permute-start(f32[12,384]{1,0:T(8,128)S(1)} %add.12), channel_id=1, source_target_pairs={{0,2},{1,3},{2,0},{3,1},{4,6},{5,7},{6,4},{7,5},{8,10},{9,11},{10,... | collective-permute-start | bytes 55304 | tf_op jit(solution)/shard_map/ppermute | solution.py:400
  87.2 8.3 %copy-start.1 = (f32[12,384]{1,0:T(8,128)}, f32[12,384]{1,0:T(8,128)S(1)}, u32[]{:S(2)}) copy-start(f32[12,384]{1,0:T(8,128)S(1)} %add.13) | copy-start | bytes 55300
  87.3 4.5 %collective-permute-start.20 = (f32[1,96]{1,0:T(1,128)S(1)}, f32[1,96]{1,0:T(1,128)S(1)}, u32[]{:S(2)}, u32[]{:S(2)}) collective-permute-start(f32[1,96]{1,0:T(1,128)S(1)} %reshape.12), channel_id=1, source_target_pairs={{0,4},{4,0},{8,12},{12,8},{1,5},{5,1},{9,13},{13,9},{2,6},{6,2},{1... | collective-permute-start | bytes 1160 | tf_op jit(solution)/shard_map/ppermute | solution.py:410
  87.4 4.5 %collective-permute-start.21 = (f32[1,96]{1,0:T(1,128)S(1)}, f32[1,96]{1,0:T(1,128)S(1)}, u32[]{:S(2)}, u32[]{:S(2)}) collective-permute-start(f32[1,96]{1,0:T(1,128)S(1)} %reshape.12), channel_id=1, source_target_pairs={{0,8},{4,12},{8,0},{12,4},{1,9},{5,13},{9,1},{13,5},{2,10},{6,14},... | collective-permute-start | bytes 1160 | tf_op jit(solution)/shard_map/ppermute | solution.py:410
  89.3 5.3 %collective-permute-start.22 = (f32[1,96]{1,0:T(1,128)S(1)}, f32[1,96]{1,0:T(1,128)S(1)}, u32[]{:S(2)}, u32[]{:S(2)}) collective-permute-start(f32[1,96]{1,0:T(1,128)S(1)} %reshape.12), channel_id=1, source_target_pairs={{0,12},{4,8},{8,4},{12,0},{1,13},{5,9},{9,5},{13,1},{2,14},{6,10},... | collective-permute-start | bytes 1160 | tf_op jit(solution)/shard_map/ppermute | solution.py:410

commit v13 on v9

--- a/solution.py
+++ b/solution.py
@@ -406,10 +406,11 @@
     target = pair_device[:, 0]
     cell = pair_query * docs + pair_doc
     if n <= 8 and is_power(n):
+        away = [0] + list(range(n - 1, 0, -1))
         table = jnp.concatenate(
-            [flat] + [lax.ppermute(flat, "dp", [(i, i ^ k) for i in range(n)]) for k in range(1, n)], axis=1
+            [flat] + [lax.ppermute(flat, "dp", [(i, i ^ k) for i in range(n)]) for k in away[1:]], axis=1
         )
-        column = (z ^ target) * cells + cell
+        column = lax.rem(n - (z ^ target), n) * cells + cell
     else:
         table = lax.all_gather(flat, "dp", axis=1, tiled=True)
         column = target * cells + cell

time: 92.3 us -> 90.9 us (0.985)
  waiting for transfers between devices: 20.1 us -> 18.7 us
    ppermute x3, waiting for transfers between devices: 2.93 us -> 1.49 us  [per_device(): lax.ppermute(flat, 'dp', [(i, i ^ k) for i in range(n)])]
  transfers between devices with their start and end apart: 27 -> 27, of which waited for: 13 -> 13; matrix products, arithmetic and copies ran while one was open for 0% -> 0% of each run, Pallas kernels for 8% -> 9%
where the time goes in v13:
time: 90.9 us; the launch traced here: 90.6 us
  starting transfers between devices  57.6 us (63%)
  waiting for transfers between devices  18.7 us (21%)
  Pallas kernels  12.2 us (13%)
  between operations  1.04 us (1%)
    ppermute x17, starting transfers between devices, transfer(): return lax.ppermute(value, 'dp', pairs)  39.3 us
    ppermute x17, waiting for transfers between devices, transfer(): return lax.ppermute(value, 'dp', pairs)  10.6 us
    ppermute x2, starting transfers between devices, project_waiting(): back.append(lax.ppermute(away, 'parts', swap))  5.53 us
    ppermute x3, starting transfers between devices, per_device(): lax.ppermute(flat, 'dp', [(i, i ^ k) for i in range(n)])  4.45 us
    ppermute x1, starting transfers between devices, per_device(): came[c] = lax.ppermute(part[c], 'dp', [(i, i ^ 2) for i in range(n)])  4.12 us
    pallas_call x1, Pallas kernels, first_pull(): pl.pallas_call(first_pull_kernel, out_shape=[bf16(rows, features)] * 2 +...  3.6 us
    ppermute x2, waiting for transfers between devices, per_device(): lax.ppermute(scores, 'layer', [(i, i ^ step) for i in range(layers)])  3.52 us
    pallas_call x4, Pallas kernels, project(): pl.pallas_call(functools.partial(project_kernel, len(tokens)), out_shape=...  3.18 us
  transfers between devices with their start and end apart: 27, of which 13 were waited for; matrix products, arithmetic and copies ran while one was open for 0% of the time, Pallas kernels for 9%

profile of v13, /device:TPU:0, one launch (start us, length us, event | category | flops | bytes accessed | tf_op | source)
XLA Modules:
  0.0 90.6 jit_solution(11867035961987905162)
XLA Ops:
  0.6 3.6 %shard_map.113 = (bf16[48,2560]{1,0:T(8,128)(2,1)S(1)}, bf16[48,2560]{1,0:T(8,128)(2,1)S(1)}, bf16[2560,640]{1,0:T(8,128)(2,1)S(1)}, bf16[640,384]{1,0:T(8,128)(2,1)}, bf16[384,640]{1,0:T(8,128)(2,1)S(1)}) custom-call(bf16[2560,640]{1,0:T(8,128)(2,1)} %bitcast.9, bf16[2560,640]{1,0:T(8,128)(2,1)} %bitcast.10, bf16[640,384]{1,0:T(8,128)(2,1)} %bitcast.13, ...), custom_call_target="tpu_custom_call" | custom-call | tf_op jit(solution)/shard_map/pallas_call | solution.py:77
  4.2 3.1 %collective-permute-start = (bf16[48,2560]{1,0:T(8,128)(2,1)S(1)}, bf16[48,2560]{1,0:T(8,128)(2,1)S(1)}, u32[]{:S(2)}, u32[]{:S(2)}) collective-permute-start(bf16[48,2560]{1,0:T(8,128)(2,1)S(1)} %get-tuple-element.33), channel_id=1, source_target_pairs={{0,4},{12,8},{4,0},{8,12},{1,5},{13,9},{5,1},{9,13},{2,6},{14,10},... | collective-permute-start | bytes 737288 | tf_op jit(solution)/shard_map/ppermute | solution.py:334
  7.3 1.5 %shard_map.114 = (bf16[48,2560]{1,0:T(8,128)(2,1)S(1)}, bf16[48,2560]{1,0:T(8,128)(2,1)S(1)}, bf16[48,2560]{1,0:T(8,128)(2,1)S(1)}, bf16[48,2560]{1,0:T(8,128)(2...) custom-call(bf16[384,640]{1,0:T(8,128)(2,1)S(1)} %get-tuple-element.28.turned_ref,, ...), custom_call_target="tpu_custom_call" | custom-call | tf_op jit(solution)/shard_map/pallas_call | solution.py:101
  8.9 1.9 %collective-permute-start.3 = (bf16[48,2560]{1,0:T(8,128)(2,1)S(1)}, bf16[48,2560]{1,0:T(8,128)(2,1)S(1)}, u32[]{:S(2)}, u32[]{:S(2)}) collective-permute-start(bf16[48,2560]{1,0:T(8,128)(2,1)S(1)} %get-tuple-element.36.mine_ref), channel_id=1, source_target_pairs={{0,4},{12,8},{1,5},{13,9},{2,6},{14,10},{3,7},{15,11},{16,20},{28,... | collective-permute-start | bytes 737288 | tf_op jit(solution)/shard_map/ppermute | solution.py:334
  10.8 2.9 %collective-permute-done.came_ref.early_ref = bf16[48,2560]{1,0:T(8,128)(2,1)S(1)} collective-permute-done((bf16[48,2560]{1,0:T(8,128)(2,1)S(1)}, bf16[48,2560]{1,0:T(8,128)(2,1)S(1)}, u32[]{:S(2)}, u32[]{:S(2)}) %collective-permute-start) | collective-permute-done | bytes 245792 | tf_op jit(solution)/shard_map/ppermute | solution.py:334
  14.4 6.5 %collective-permute-start.1 = (bf16[48,2560]{1,0:T(8,128)(2,1)S(1)}, bf16[48,2560]{1,0:T(8,128)(2,1)S(1)}, u32[]{:S(2)}, u32[]{:S(2)}) collective-permute-start(bf16[48,2560]{1,0:T(8,128)(2,1)S(1)} %get-tuple-element.34), channel_id=1, source_target_pairs={{0,4},{12,8},{1,5},{13,9},{2,6},{14,10},{3,7},{15,11},{16,20},{28,... | collective-permute-start | bytes 737288 | tf_op jit(solution)/shard_map/ppermute | solution.py:334
  21.0 1.9 %shard_map.136 = (bf16[320,2560]{1,0:T(8,128)(2,1)S(1)}, bf16[320,1920]{1,0:T(8,128)(2,1)S(1)}, bf16[320,640]{1,0:T(8,128)(2,1)S(1)}) custom-call(bf16[320,2560]{1,0:T(8,128)(2,1)} %bitcast.11, bf16[320,2560]{1,0:T(8,128)(2,1)} %bitcast.12, bf16[48,2560]{1,0:T(8,128)(2,1)S(1)} %get-tuple-element.48.rest_0_.mine_ref.after_ref), custom_call_target="tpu_custom_call" | custom-call | tf_op jit(solution)/shard_map/pallas_call | solution.py:140
  22.9 1.6 %collective-permute-start.16 = (bf16[320,1920]{1,0:T(8,128)(2,1)S(1)}, bf16[320,1920]{1,0:T(8,128)(2,1)S(1)}, u32[]{:S(2)}, u32[]{:S(2)}) collective-permute-start(bf16[320,1920]{1,0:T(8,128)(2,1)S(1)} %get-tuple-element.51), channel_id=1, source_target_pairs={{0,16},{16,0},{1,17},{17,1},{2,18},{18,2},{3,19},{19,3},{4,20},{20... | collective-permute-start | bytes 3686408 | tf_op jit(solution)/shard_map/ppermute | solution.py:342
  25.3 1.8 %collective-permute-start.5 = (bf16[48,2560]{1,0:T(8,128)(2,1)S(1)}, bf16[48,2560]{1,0:T(8,128)(2,1)S(1)}, u32[]{:S(2)}, u32[]{:S(2)}) collective-permute-start(bf16[48,2560]{1,0:T(8,128)(2,1)S(1)} %get-tuple-element.39), channel_id=1, source_target_pairs={{0,4},{12,8},{4,0},{8,12},{1,5},{13,9},{5,1},{9,13},{2,6},{14,10},... | collective-permute-start | bytes 737288 | tf_op jit(solution)/shard_map/ppermute | solution.py:334
  28.0 6.8 %collective-permute-start.8 = (bf16[48,2560]{1,0:T(8,128)(2,1)S(1)}, bf16[48,2560]{1,0:T(8,128)(2,1)S(1)}, u32[]{:S(2)}, u32[]{:S(2)}) collective-permute-start(bf16[48,2560]{1,0:T(8,128)(2,1)S(1)} %get-tuple-element.43), channel_id=1, source_target_pairs={{0,4},{12,8},{4,0},{8,12},{1,5},{13,9},{5,1},{9,13},{2,6},{14,10},... | collective-permute-start | bytes 737288 | tf_op jit(solution)/shard_map/ppermute | solution.py:334
  35.6 4.4 %collective-permute-start.7 = (bf16[48,2560]{1,0:T(8,128)(2,1)S(1)}, bf16[48,2560]{1,0:T(8,128)(2,1)S(1)}, u32[]{:S(2)}, u32[]{:S(2)}) collective-permute-start(bf16[48,2560]{1,0:T(8,128)(2,1)S(1)} %get-tuple-element.42), channel_id=1, source_target_pairs={{0,4},{12,8},{4,0},{8,12},{1,5},{13,9},{5,1},{9,13},{2,6},{14,10},... | collective-permute-start | bytes 737288 | tf_op jit(solution)/shard_map/ppermute | solution.py:334
  40.0 0.9 collective-permute-done.8.came_ref
  41.8 3.7 %collective-permute-start.11 = (bf16[48,2560]{1,0:T(8,128)(2,1)S(1)}, bf16[48,2560]{1,0:T(8,128)(2,1)S(1)}, u32[]{:S(2)}, u32[]{:S(2)}) collective-permute-start(bf16[48,2560]{1,0:T(8,128)(2,1)S(1)} %get-tuple-element.47), channel_id=1, source_target_pairs={{0,4},{12,8},{4,0},{8,12},{1,5},{13,9},{5,1},{9,13},{2,6},{14,10},... | collective-permute-start | bytes 737288 | tf_op jit(solution)/shard_map/ppermute | solution.py:334
  47.0 1.1 %collective-permute-start.17 = (bf16[320,640]{1,0:T(8,128)(2,1)S(1)}, bf16[320,640]{1,0:T(8,128)(2,1)S(1)}, u32[]{:S(2)}, u32[]{:S(2)}) collective-permute-start(bf16[320,640]{1,0:T(8,128)(2,1)S(1)} %get-tuple-element.52), channel_id=1, source_target_pairs={{0,16},{16,0},{1,17},{17,1},{2,18},{18,2},{3,19},{19,3},{4,20},{20... | collective-permute-start | bytes 1228808 | tf_op jit(solution)/shard_map/ppermute | solution.py:342
  48.2 3.7 %collective-permute-start.14 = (bf16[48,2560]{1,0:T(8,128)(2,1)S(1)}, bf16[48,2560]{1,0:T(8,128)(2,1)S(1)}, u32[]{:S(2)}, u32[]{:S(2)}) collective-permute-start(bf16[48,2560]{1,0:T(8,128)(2,1)S(1)} %get-tuple-element.50), channel_id=1, source_target_pairs={{0,4},{12,8},{4,0},{8,12},{1,5},{13,9},{5,1},{9,13},{2,6},{14,10},... | collective-permute-start | bytes 737288 | tf_op jit(solution)/shard_map/ppermute | solution.py:334
  52.8 1.3 %collective-permute-start.13 = (bf16[48,2560]{1,0:T(8,128)(2,1)S(1)}, bf16[48,2560]{1,0:T(8,128)(2,1)S(1)}, u32[]{:S(2)}, u32[]{:S(2)}) collective-permute-start(bf16[48,2560]{1,0:T(8,128)(2,1)S(1)} %shard_map.130.after_ref.mine_ref), channel_id=1, source_target_pairs={{4,0},{8,12},{5,1},{9,13},{6,2},{10,14},{7,3},{11,15},{20,16},{24,... | collective-permute-start | bytes 737288 | tf_op jit(solution)/shard_map/ppermute | solution.py:334
  54.1 5.1 %collective-permute-done.14.came_ref = bf16[48,2560]{1,0:T(8,128)(2,1)S(1)} collective-permute-done((bf16[48,2560]{1,0:T(8,128)(2,1)S(1)}, bf16[48,2560]{1,0:T(8,128)(2,1)S(1)}, u32[]{:S(2)}, u32[]{:S(2)}) %collective-permute-start.14) | collective-permute-done | bytes 245792 | tf_op jit(solution)/shard_map/ppermute | solution.py:334
  59.3 4.1 %collective-permute-start.19 = (bf16[48,2560]{1,0:T(8,128)(2,1)S(1)}, bf16[48,2560]{1,0:T(8,128)(2,1)S(1)}, u32[]{:S(2)}, u32[]{:S(2)}) collective-permute-start(bf16[48,2560]{1,0:T(8,128)(2,1)S(1)} %shard_map.132.after_ref.mine_ref), channel_id=1, source_target_pairs={{0,8},{4,12},{8,0},{12,4},{1,9},{5,13},{9,1},{13,5},{2,10},{6,14},... | collective-permute-start | bytes 737288 | tf_op jit(solution)/shard_map/ppermute | solution.py:364
  63.5 1.3 %collective-permute-start.18 = (bf16[48,2560]{1,0:T(8,128)(2,1)S(1)}, bf16[48,2560]{1,0:T(8,128)(2,1)S(1)}, u32[]{:S(2)}, u32[]{:S(2)}) collective-permute-start(bf16[48,2560]{1,0:T(8,128)(2,1)S(1)} %shard_map.133.after_ref.mine_ref), channel_id=1, source_target_pairs={{4,0},{8,12},{5,1},{9,13},{6,2},{10,14},{7,3},{11,15},{20,16},{24,... | collective-permute-start | bytes 737288 | tf_op jit(solution)/shard_map/ppermute | solution.py:334
  65.5 1.0 %shard_map.137.after_ref = bf16[288,320]{1,0:T(8,128)(2,1)S(1)} custom-call(bf16[48,2560]{1,0:T(8,128)(2,1)S(1)} %shard_map.135.after_ref.rest_7_.rest_6_, bf16[320,1920]{1,0:T(8,128)(2,1)S(1)} %collective-permute-done.16.rest_0_, bf16[320,640]{1,0:T(8,128)(2,1)S(1)} %collective-permute-done.17.rest_1_, ...), custom_call_target="tpu_custom_call" | custom-call | tf_op jit(solution)/shard_map/pallas_call | solution.py:241
  66.5 4.9 %collective-permute-start.20 = (bf16[288,320]{1,0:T(8,128)(2,1)S(1)}, bf16[288,320]{1,0:T(8,128)(2,1)S(1)}, u32[]{:S(2)}, u32[]{:S(2)}) collective-permute-start(bf16[288,320]{1,0:T(8,128)(2,1)S(1)} %shard_map.137.after_ref), channel_id=1, source_target_pairs={{0,16},{16,0},{1,17},{17,1},{2,18},{18,2},{3,19},{19,3},{4,20},{20... | collective-permute-start | bytes 552968 | tf_op jit(solution)/shard_map/ppermute | solution.py:349
  71.3 0.9 %shard_map.138.after_ref.refs_0_ = f32[288,320]{1,0:T(8,128)S(1)} custom-call(bf16[288,320]{1,0:T(8,128)(2,1)S(1)} %shard_map.137.after_ref, bf16[320,2560]{1,0:T(8,128)(2,1)S(1)} %get-tuple-element.53.rest_0_, bf16[48,2560]{1,0:T(8,128)(2,1)S(1)} %shard_map.122.after_ref.rest_2_.rest_1_, bf16[48,2560]{1,0:T(8,128)(2,1)S(1)} %shard_map.125.after_ref.rest_3_.rest_2_, ...), custom_call_target="tpu_custom_call" | custom-call | tf_op jit(solution)/shard_map/pallas_call | solution.py:241
  73.3 0.7 collective-permute-start.21
  75.2 2.5 %collective-permute-done.21.refs_3_ = bf16[96,320]{1,0:T(8,128)(2,1)S(1)} collective-permute-done((bf16[96,320]{1,0:T(8,128)(2,1)S(1)}, bf16[96,320]{1,0:T(8,128)(2,1)S(1)}, u32[]{:S(2)}, u32[]{:S(2)}) %collective-permute-start.21) | collective-permute-done | bytes 61472 | tf_op jit(solution)/shard_map/ppermute | solution.py:349
  77.8 0.8 shard_map.143
  78.6 1.2 %collective-permute-done.22 = f32[12,384]{1,0:T(8,128)S(1)} collective-permute-done((f32[12,384]{1,0:T(8,128)S(1)}, f32[12,384]{1,0:T(8,128)S(1)}, u32[]{:S(2)}, u32[]{:S(2)}) %collective-permute-start.22) | collective-permute-done | bytes 18464 | tf_op jit(solution)/shard_map/ppermute | solution.py:400
  79.8 1.5 %collective-permute-start.23 = (f32[12,384]{1,0:T(8,128)S(1)}, f32[12,384]{1,0:T(8,128)S(1)}, u32[]{:S(2)}, u32[]{:S(2)}) collective-permute-start(f32[12,384]{1,0:T(8,128)S(1)} %add.12), channel_id=1, source_target_pairs={{0,2},{1,3},{2,0},{3,1},{4,6},{5,7},{6,4},{7,5},{8,10},{9,11},{10,... | collective-permute-start | bytes 55304 | tf_op jit(solution)/shard_map/ppermute | solution.py:400
  81.3 2.3 %collective-permute-done.23 = f32[12,384]{1,0:T(8,128)S(1)} collective-permute-done((f32[12,384]{1,0:T(8,128)S(1)}, f32[12,384]{1,0:T(8,128)S(1)}, u32[]{:S(2)}, u32[]{:S(2)}) %collective-permute-start.23) | collective-permute-done | bytes 18464 | tf_op jit(solution)/shard_map/ppermute | solution.py:400
  83.8 1.5 %collective-permute-start.24 = (f32[1,96]{1,0:T(1,128)S(1)}, f32[1,96]{1,0:T(1,128)S(1)}, u32[]{:S(2)}, u32[]{:S(2)}) collective-permute-start(f32[1,96]{1,0:T(1,128)S(1)} %reshape.12), channel_id=1, source_target_pairs={{0,12},{4,8},{8,4},{12,0},{1,13},{5,9},{9,5},{13,1},{2,14},{6,10},... | collective-permute-start | bytes 1160 | tf_op jit(solution)/shard_map/ppermute | solution.py:411
  85.3 2.9 %collective-permute-start.26 = (f32[1,96]{1,0:T(1,128)S(1)}, f32[1,96]{1,0:T(1,128)S(1)}, u32[]{:S(2)}, u32[]{:S(2)}) collective-permute-start(f32[1,96]{1,0:T(1,128)S(1)} %reshape.12), channel_id=1, source_target_pairs={{0,4},{4,0},{8,12},{12,8},{1,5},{5,1},{9,13},{13,9},{2,6},{6,2},{1... | collective-permute-start | bytes 1160 | tf_op jit(solution)/shard_map/ppermute | solution.py:411
  88.3 0.9 %collective-permute-done.24 = f32[1,96]{1,0:T(1,128)S(1)} collective-permute-done((f32[1,96]{1,0:T(1,128)S(1)}, f32[1,96]{1,0:T(1,128)S(1)}, u32[]{:S(2)}, u32[]{:S(2)}) %collective-permute-start.24) | collective-permute-done | bytes 416 | tf_op jit(solution)/shard_map/ppermute | solution.py:411
  89.9 0.7 select_reduce_fusion
  (70 shorter events, 10.3 us)
Async XLA Ops:
  4.2 9.5 %collective-permute-start = (bf16[48,2560]{1,0:T(8,128)(2,1)S(1)}, bf16[48,2560]{1,0:T(8,128)(2,1)S(1)}, u32[]{:S(2)}, u32[]{:S(2)}) collective-permute-start(bf16[48,2560]{1,0:T(8,128)(2,1)S(1)} %get-tuple-element.33), channel_id=1, source_target_pairs={{0,4},{12,8},{4,0},{8,12},{1,5},{13,9},{5,1},{9,13},{2,6},{14,10},... | collective-permute-start | bytes 737288 | tf_op jit(solution)/shard_map/ppermute | solution.py:334
  8.9 15.6 %collective-permute-start.3 = (bf16[48,2560]{1,0:T(8,128)(2,1)S(1)}, bf16[48,2560]{1,0:T(8,128)(2,1)S(1)}, u32[]{:S(2)}, u32[]{:S(2)}) collective-permute-start(bf16[48,2560]{1,0:T(8,128)(2,1)S(1)} %get-tuple-element.36.mine_ref), channel_id=1, source_target_pairs={{0,4},{12,8},{1,5},{13,9},{2,6},{14,10},{3,7},{15,11},{16,20},{28,... | collective-permute-start | bytes 737288 | tf_op jit(solution)/shard_map/ppermute | solution.py:334
  13.8 11.5 %collective-permute-start.2 = (bf16[48,2560]{1,0:T(8,128)(2,1)S(1)}, bf16[48,2560]{1,0:T(8,128)(2,1)S(1)}, u32[]{:S(2)}, u32[]{:S(2)}) collective-permute-start(bf16[48,2560]{1,0:T(8,128)(2,1)S(1)} %get-tuple-element.35.after_ref.mine_ref), channel_id=1, source_target_pairs={{4,8},{8,4},{5,9},{9,5},{6,10},{10,6},{7,11},{11,7},{20,24},{24,20... | collective-permute-start | bytes 737288 | tf_op jit(solution)/shard_map/ppermute | solution.py:334
  14.4 12.7 %collective-permute-start.1 = (bf16[48,2560]{1,0:T(8,128)(2,1)S(1)}, bf16[48,2560]{1,0:T(8,128)(2,1)S(1)}, u32[]{:S(2)}, u32[]{:S(2)}) collective-permute-start(bf16[48,2560]{1,0:T(8,128)(2,1)S(1)} %get-tuple-element.34), channel_id=1, source_target_pairs={{0,4},{12,8},{1,5},{13,9},{2,6},{14,10},{3,7},{15,11},{16,20},{28,... | collective-permute-start | bytes 737288 | tf_op jit(solution)/shard_map/ppermute | solution.py:334
  22.9 42.6 %collective-permute-start.16 = (bf16[320,1920]{1,0:T(8,128)(2,1)S(1)}, bf16[320,1920]{1,0:T(8,128)(2,1)S(1)}, u32[]{:S(2)}, u32[]{:S(2)}) collective-permute-start(bf16[320,1920]{1,0:T(8,128)(2,1)S(1)} %get-tuple-element.51), channel_id=1, source_target_pairs={{0,16},{16,0},{1,17},{17,1},{2,18},{18,2},{3,19},{19,3},{4,20},{20... | collective-permute-start | bytes 3686408 | tf_op jit(solution)/shard_map/ppermute | solution.py:342
  24.5 3.3 %collective-permute-start.6 = (bf16[48,2560]{1,0:T(8,128)(2,1)S(1)}, bf16[48,2560]{1,0:T(8,128)(2,1)S(1)}, u32[]{:S(2)}, u32[]{:S(2)}) collective-permute-start(bf16[48,2560]{1,0:T(8,128)(2,1)S(1)} %shard_map.116.after_ref.mine_ref), channel_id=1, source_target_pairs={{4,8},{8,4},{5,9},{9,5},{6,10},{10,6},{7,11},{11,7},{20,24},{24,20... | collective-permute-start | bytes 737288 | tf_op jit(solution)/shard_map/ppermute | solution.py:334
  25.3 9.5 %collective-permute-start.5 = (bf16[48,2560]{1,0:T(8,128)(2,1)S(1)}, bf16[48,2560]{1,0:T(8,128)(2,1)S(1)}, u32[]{:S(2)}, u32[]{:S(2)}) collective-permute-start(bf16[48,2560]{1,0:T(8,128)(2,1)S(1)} %get-tuple-element.39), channel_id=1, source_target_pairs={{0,4},{12,8},{4,0},{8,12},{1,5},{13,9},{5,1},{9,13},{2,6},{14,10},... | collective-permute-start | bytes 737288 | tf_op jit(solution)/shard_map/ppermute | solution.py:334
  27.2 8.4 %collective-permute-start.4 = (bf16[48,2560]{1,0:T(8,128)(2,1)S(1)}, bf16[48,2560]{1,0:T(8,128)(2,1)S(1)}, u32[]{:S(2)}, u32[]{:S(2)}) collective-permute-start(bf16[48,2560]{1,0:T(8,128)(2,1)S(1)} %shard_map.118.after_ref.mine_ref), channel_id=1, source_target_pairs={{4,8},{8,4},{5,9},{9,5},{6,10},{10,6},{7,11},{11,7},{20,24},{24,20... | collective-permute-start | bytes 737288 | tf_op jit(solution)/shard_map/ppermute | solution.py:334
  28.0 13.0 %collective-permute-start.8 = (bf16[48,2560]{1,0:T(8,128)(2,1)S(1)}, bf16[48,2560]{1,0:T(8,128)(2,1)S(1)}, u32[]{:S(2)}, u32[]{:S(2)}) collective-permute-start(bf16[48,2560]{1,0:T(8,128)(2,1)S(1)} %get-tuple-element.43), channel_id=1, source_target_pairs={{0,4},{12,8},{4,0},{8,12},{1,5},{13,9},{5,1},{9,13},{2,6},{14,10},... | collective-permute-start | bytes 737288 | tf_op jit(solution)/shard_map/ppermute | solution.py:334
  34.9 6.8 %collective-permute-start.9 = (bf16[48,2560]{1,0:T(8,128)(2,1)S(1)}, bf16[48,2560]{1,0:T(8,128)(2,1)S(1)}, u32[]{:S(2)}, u32[]{:S(2)}) collective-permute-start(bf16[48,2560]{1,0:T(8,128)(2,1)S(1)} %shard_map.120.after_ref.mine_ref), channel_id=1, source_target_pairs={{4,8},{8,4},{5,9},{9,5},{6,10},{10,6},{7,11},{11,7},{20,24},{24,20... | collective-permute-start | bytes 737288 | tf_op jit(solution)/shard_map/ppermute | solution.py:334
  35.6 10.6 %collective-permute-start.7 = (bf16[48,2560]{1,0:T(8,128)(2,1)S(1)}, bf16[48,2560]{1,0:T(8,128)(2,1)S(1)}, u32[]{:S(2)}, u32[]{:S(2)}) collective-permute-start(bf16[48,2560]{1,0:T(8,128)(2,1)S(1)} %get-tuple-element.42), channel_id=1, source_target_pairs={{0,4},{12,8},{4,0},{8,12},{1,5},{13,9},{5,1},{9,13},{2,6},{14,10},... | collective-permute-start | bytes 737288 | tf_op jit(solution)/shard_map/ppermute | solution.py:334
  41.0 7.1 %collective-permute-start.12 = (bf16[48,2560]{1,0:T(8,128)(2,1)S(1)}, bf16[48,2560]{1,0:T(8,128)(2,1)S(1)}, u32[]{:S(2)}, u32[]{:S(2)}) collective-permute-start(bf16[48,2560]{1,0:T(8,128)(2,1)S(1)} %shard_map.123.after_ref.mine_ref), channel_id=1, source_target_pairs={{4,8},{8,4},{5,9},{9,5},{6,10},{10,6},{7,11},{11,7},{20,24},{24,20... | collective-permute-start | bytes 737288 | tf_op jit(solution)/shard_map/ppermute | solution.py:334
  41.8 10.2 %collective-permute-start.11 = (bf16[48,2560]{1,0:T(8,128)(2,1)S(1)}, bf16[48,2560]{1,0:T(8,128)(2,1)S(1)}, u32[]{:S(2)}, u32[]{:S(2)}) collective-permute-start(bf16[48,2560]{1,0:T(8,128)(2,1)S(1)} %get-tuple-element.47), channel_id=1, source_target_pairs={{0,4},{12,8},{4,0},{8,12},{1,5},{13,9},{5,1},{9,13},{2,6},{14,10},... | collective-permute-start | bytes 737288 | tf_op jit(solution)/shard_map/ppermute | solution.py:334
  46.3 6.5 %collective-permute-start.10 = (bf16[48,2560]{1,0:T(8,128)(2,1)S(1)}, bf16[48,2560]{1,0:T(8,128)(2,1)S(1)}, u32[]{:S(2)}, u32[]{:S(2)}) collective-permute-start(bf16[48,2560]{1,0:T(8,128)(2,1)S(1)} %shard_map.126.after_ref.mine_ref), channel_id=1, source_target_pairs={{4,8},{8,4},{5,9},{9,5},{6,10},{10,6},{7,11},{11,7},{20,24},{24,20... | collective-permute-start | bytes 737288 | tf_op jit(solution)/shard_map/ppermute | solution.py:334
  47.0 18.5 %collective-permute-start.17 = (bf16[320,640]{1,0:T(8,128)(2,1)S(1)}, bf16[320,640]{1,0:T(8,128)(2,1)S(1)}, u32[]{:S(2)}, u32[]{:S(2)}) collective-permute-start(bf16[320,640]{1,0:T(8,128)(2,1)S(1)} %get-tuple-element.52), channel_id=1, source_target_pairs={{0,16},{16,0},{1,17},{17,1},{2,18},{18,2},{3,19},{19,3},{4,20},{20... | collective-permute-start | bytes 1228808 | tf_op jit(solution)/shard_map/ppermute | solution.py:342
  48.2 11.0 %collective-permute-start.14 = (bf16[48,2560]{1,0:T(8,128)(2,1)S(1)}, bf16[48,2560]{1,0:T(8,128)(2,1)S(1)}, u32[]{:S(2)}, u32[]{:S(2)}) collective-permute-start(bf16[48,2560]{1,0:T(8,128)(2,1)S(1)} %get-tuple-element.50), channel_id=1, source_target_pairs={{0,4},{12,8},{4,0},{8,12},{1,5},{13,9},{5,1},{9,13},{2,6},{14,10},... | collective-permute-start | bytes 737288 | tf_op jit(solution)/shard_map/ppermute | solution.py:334
  52.0 11.4 %collective-permute-start.15 = (bf16[48,2560]{1,0:T(8,128)(2,1)S(1)}, bf16[48,2560]{1,0:T(8,128)(2,1)S(1)}, u32[]{:S(2)}, u32[]{:S(2)}) collective-permute-start(bf16[48,2560]{1,0:T(8,128)(2,1)S(1)} %shard_map.129.after_ref.mine_ref), channel_id=1, source_target_pairs={{4,8},{8,4},{5,9},{9,5},{6,10},{10,6},{7,11},{11,7},{20,24},{24,20... | collective-permute-start | bytes 737288 | tf_op jit(solution)/shard_map/ppermute | solution.py:334
  52.8 12.6 %collective-permute-start.13 = (bf16[48,2560]{1,0:T(8,128)(2,1)S(1)}, bf16[48,2560]{1,0:T(8,128)(2,1)S(1)}, u32[]{:S(2)}, u32[]{:S(2)}) collective-permute-start(bf16[48,2560]{1,0:T(8,128)(2,1)S(1)} %shard_map.130.after_ref.mine_ref), channel_id=1, source_target_pairs={{4,0},{8,12},{5,1},{9,13},{6,2},{10,14},{7,3},{11,15},{20,16},{24,... | collective-permute-start | bytes 737288 | tf_op jit(solution)/shard_map/ppermute | solution.py:334
  59.3 13.0 %collective-permute-start.19 = (bf16[48,2560]{1,0:T(8,128)(2,1)S(1)}, bf16[48,2560]{1,0:T(8,128)(2,1)S(1)}, u32[]{:S(2)}, u32[]{:S(2)}) collective-permute-start(bf16[48,2560]{1,0:T(8,128)(2,1)S(1)} %shard_map.132.after_ref.mine_ref), channel_id=1, source_target_pairs={{0,8},{4,12},{8,0},{12,4},{1,9},{5,13},{9,1},{13,5},{2,10},{6,14},... | collective-permute-start | bytes 737288 | tf_op jit(solution)/shard_map/ppermute | solution.py:364
  63.5 9.2 %collective-permute-start.18 = (bf16[48,2560]{1,0:T(8,128)(2,1)S(1)}, bf16[48,2560]{1,0:T(8,128)(2,1)S(1)}, u32[]{:S(2)}, u32[]{:S(2)}) collective-permute-start(bf16[48,2560]{1,0:T(8,128)(2,1)S(1)} %shard_map.133.after_ref.mine_ref), channel_id=1, source_target_pairs={{4,0},{8,12},{5,1},{9,13},{6,2},{10,14},{7,3},{11,15},{20,16},{24,... | collective-permute-start | bytes 737288 | tf_op jit(solution)/shard_map/ppermute | solution.py:334
  66.5 8.8 %collective-permute-start.20 = (bf16[288,320]{1,0:T(8,128)(2,1)S(1)}, bf16[288,320]{1,0:T(8,128)(2,1)S(1)}, u32[]{:S(2)}, u32[]{:S(2)}) collective-permute-start(bf16[288,320]{1,0:T(8,128)(2,1)S(1)} %shard_map.137.after_ref), channel_id=1, source_target_pairs={{0,16},{16,0},{1,17},{17,1},{2,18},{18,2},{3,19},{19,3},{4,20},{20... | collective-permute-start | bytes 552968 | tf_op jit(solution)/shard_map/ppermute | solution.py:349
  73.3 4.5 %copy-start = (s32[1,8]{1,0:T(1,128)S(1)}, s32[1,8]{1,0:T(1,128)}, u32[]{:S(2)}) copy-start(s32[1,8]{1,0:T(1,128)} %counts_ref.1) | copy-start | bytes 100
  73.3 14.9 %copy-start.2 = (s32[128]{0:T(128)S(1)}, s32[128]{0:T(128)}, u32[]{:S(2)}) copy-start(s32[128]{0:T(128)} %param.19) | copy-start | bytes 1540
  73.3 14.9 %copy-start.3 = (s32[128]{0:T(128)S(1)}, s32[128]{0:T(128)}, u32[]{:S(2)}) copy-start(s32[128]{0:T(128)} %param.17) | copy-start | bytes 1540
  73.3 14.9 %copy-start.4 = (s32[128,1]{0,1:T(1,128)S(1)}, s32[128,1]{0,1:T(1,128)}, u32[]{:S(2)}) copy-start(s32[128,1]{0,1:T(1,128)} %param.18) | copy-start | bytes 1540
  73.3 4.4 %collective-permute-start.21 = (bf16[96,320]{1,0:T(8,128)(2,1)S(1)}, bf16[96,320]{1,0:T(8,128)(2,1)S(1)}, u32[]{:S(2)}, u32[]{:S(2)}) collective-permute-start(bf16[96,320]{1,0:T(8,128)(2,1)S(1)} %shard_map.141.after_ref), channel_id=1, source_target_pairs={{0,16},{16,0},{1,17},{17,1},{2,18},{18,2},{3,19},{19,3},{4,20},{20... | collective-permute-start | bytes 184328 | tf_op jit(solution)/shard_map/ppermute | solution.py:349
  78.6 1.2 %collective-permute-start.22 = (f32[12,384]{1,0:T(8,128)S(1)}, f32[12,384]{1,0:T(8,128)S(1)}, u32[]{:S(2)}, u32[]{:S(2)}) collective-permute-start(f32[12,384]{1,0:T(8,128)S(1)} %shard_map.143), channel_id=1, source_target_pairs={{0,1},{1,0},{2,3},{3,2},{4,5},{5,4},{6,7},{7,6},{8,9},{9,8},{10,11... | collective-permute-start | bytes 55304 | tf_op jit(solution)/shard_map/ppermute | solution.py:400
  79.8 3.8 %collective-permute-start.23 = (f32[12,384]{1,0:T(8,128)S(1)}, f32[12,384]{1,0:T(8,128)S(1)}, u32[]{:S(2)}, u32[]{:S(2)}) collective-permute-start(f32[12,384]{1,0:T(8,128)S(1)} %add.12), channel_id=1, source_target_pairs={{0,2},{1,3},{2,0},{3,1},{4,6},{5,7},{6,4},{7,5},{8,10},{9,11},{10,... | collective-permute-start | bytes 55304 | tf_op jit(solution)/shard_map/ppermute | solution.py:400
  83.6 6.9 %copy-start.1 = (f32[12,384]{1,0:T(8,128)}, f32[12,384]{1,0:T(8,128)S(1)}, u32[]{:S(2)}) copy-start(f32[12,384]{1,0:T(8,128)S(1)} %add.13) | copy-start | bytes 55300
  83.8 5.4 %collective-permute-start.24 = (f32[1,96]{1,0:T(1,128)S(1)}, f32[1,96]{1,0:T(1,128)S(1)}, u32[]{:S(2)}, u32[]{:S(2)}) collective-permute-start(f32[1,96]{1,0:T(1,128)S(1)} %reshape.12), channel_id=1, source_target_pairs={{0,12},{4,8},{8,4},{12,0},{1,13},{5,9},{9,5},{13,1},{2,14},{6,10},... | collective-permute-start | bytes 1160 | tf_op jit(solution)/shard_map/ppermute | solution.py:411
  85.3 4.4 %collective-permute-start.25 = (f32[1,96]{1,0:T(1,128)S(1)}, f32[1,96]{1,0:T(1,128)S(1)}, u32[]{:S(2)}, u32[]{:S(2)}) collective-permute-start(f32[1,96]{1,0:T(1,128)S(1)} %reshape.12), channel_id=1, source_target_pairs={{0,8},{4,12},{8,0},{12,4},{1,9},{5,13},{9,1},{13,5},{2,10},{6,14},... | collective-permute-start | bytes 1160 | tf_op jit(solution)/shard_map/ppermute | solution.py:411
  85.3 4.5 %collective-permute-start.26 = (f32[1,96]{1,0:T(1,128)S(1)}, f32[1,96]{1,0:T(1,128)S(1)}, u32[]{:S(2)}, u32[]{:S(2)}) collective-permute-start(f32[1,96]{1,0:T(1,128)S(1)} %reshape.12), channel_id=1, source_target_pairs={{0,4},{4,0},{8,12},{12,8},{1,5},{5,1},{9,13},{13,9},{2,6},{6,2},{1... | collective-permute-start | bytes 1160 | tf_op jit(solution)/shard_map/ppermute | solution.py:411

commit v14 on v9

--- a/solution.py
+++ b/solution.py
@@ -256,18 +256,22 @@
     scores = jnp.sum(product.reshape(queries, RANK, tokens), axis=1) * RANK ** (-0.5)
     out_ref[...] = jnp.zeros(out_ref.shape, jnp.float32)
     out_ref[:, :tokens] = scores
-    position = lax.broadcasted_iota(jnp.int32, scores.shape, 1)
     docs = counts_ref.shape[1]
-    column = lax.broadcasted_iota(jnp.int32, (queries, docs), 1)
-    pooled = jnp.zeros((queries, docs), jnp.float32)
-    start = jnp.int32(0)
+    row = lax.broadcasted_iota(jnp.int32, (docs, 1), 0)
+    column = lax.broadcasted_iota(jnp.int32, (1, docs), 1)
+    starts, ends = jnp.zeros((docs, 1), jnp.int32), jnp.zeros((docs, 1), jnp.int32)
+    counts = jnp.ones((1, docs), jnp.int32)
+    end = jnp.int32(0)
     for k in range(docs):
-        count = counts_ref[0, k]
-        inside = (position >= start) & (position < start + count)
-        found = jnp.sum(jnp.where(inside, scores, 0.0), axis=1, keepdims=True)
-        root = jnp.sqrt(jnp.full((1, 1), count, jnp.int32).astype(jnp.float32))
-        pooled = jnp.where(column == k, found / root, pooled)
-        start = start + count
+        start, end = end, end + counts_ref[0, k]
+        starts, ends = jnp.where(row == k, start, starts), jnp.where(row == k, end, ends)
+        counts = jnp.where(column == k, end - start, counts)
+    position = lax.broadcasted_iota(jnp.int32, (docs, tokens), 1)
+    member = ((position >= starts) & (position < ends)).astype(jnp.float32)
+    pooled = lax.dot_general(
+        scores, member, NT, precision=lax.Precision.HIGHEST, preferred_element_type=jnp.float32
+    )
+    pooled = pooled / jnp.sqrt(counts.astype(jnp.float32))
     out_ref[:, tokens : tokens + pooled.shape[1]] = pooled
 
 
@@ -407,9 +411,10 @@
     cell = pair_query * docs + pair_doc
     if n <= 8 and is_power(n):
         table = jnp.concatenate(
-            [flat] + [lax.ppermute(flat, "dp", [(i, i ^ k) for i in range(n)]) for k in range(1, n)], axis=1
+            [flat] + [lax.ppermute(flat, "dp", [(i, i ^ k ^ (k >> 1)) for i in range(n)]) for k in range(1, n)], axis=1
         )
-        column = (z ^ target) * cells + cell
+        away = z ^ target
+        column = (away ^ (away >> 1) ^ (away >> 2)) * cells + cell
     else:
         table = lax.all_gather(flat, "dp", axis=1, tiled=True)
         column = target * cells + cell

time: 92.3 us -> 91 us (0.986)
  transfers between devices with their start and end apart: 27 -> 27, of which waited for: 13 -> 13; matrix products, arithmetic and copies ran while one was open for 0% -> 0% of each run, Pallas kernels for 8% -> 9%
where the time goes in v14:
time: 91 us; the launch traced here: 90.7 us
  starting transfers between devices  56.7 us (62%)
  waiting for transfers between devices  19.6 us (22%)
  Pallas kernels  12.3 us (14%)
  between operations  1.05 us (1%)
    ppermute x17, starting transfers between devices, transfer(): return lax.ppermute(value, 'dp', pairs)  39.3 us
    ppermute x17, waiting for transfers between devices, transfer(): return lax.ppermute(value, 'dp', pairs)  10.6 us
    ppermute x2, starting transfers between devices, project_waiting(): back.append(lax.ppermute(away, 'parts', swap))  5.53 us
    ppermute x1, starting transfers between devices, per_device(): came[c] = lax.ppermute(part[c], 'dp', [(i, i ^ 2) for i in range(n)])  4.12 us
    pallas_call x1, Pallas kernels, first_pull(): pl.pallas_call(first_pull_kernel, out_shape=[bf16(rows, features)] * 2 +...  3.6 us
    ppermute x3, starting transfers between devices, per_device(): lax.ppermute(flat, 'dp', [(i, i ^ k ^ k >> 1) for i in range(n)])  3.55 us
    ppermute x2, waiting for transfers between devices, per_device(): lax.ppermute(scores, 'layer', [(i, i ^ step) for i in range(layers)])  3.52 us
    pallas_call x4, Pallas kernels, project(): pl.pallas_call(functools.partial(project_kernel, len(tokens)), out_shape=...  3.18 us
  transfers between devices with their start and end apart: 27, of which 13 were waited for; matrix products, arithmetic and copies ran while one was open for 0% of the time, Pallas kernels for 9%

profile of v14, /device:TPU:0, one launch (start us, length us, event | category | flops | bytes accessed | tf_op | source)
XLA Modules:
  0.0 90.7 jit_solution(3807261246328416298)
XLA Ops:
  0.6 3.6 %shard_map.113 = (bf16[48,2560]{1,0:T(8,128)(2,1)S(1)}, bf16[48,2560]{1,0:T(8,128)(2,1)S(1)}, bf16[2560,640]{1,0:T(8,128)(2,1)S(1)}, bf16[640,384]{1,0:T(8,128)(2,1)}, bf16[384,640]{1,0:T(8,128)(2,1)S(1)}) custom-call(bf16[2560,640]{1,0:T(8,128)(2,1)} %bitcast.16, bf16[2560,640]{1,0:T(8,128)(2,1)} %bitcast.17, bf16[640,384]{1,0:T(8,128)(2,1)} %bitcast.20, ...), custom_call_target="tpu_custom_call" | custom-call | tf_op jit(solution)/shard_map/pallas_call | solution.py:77
  4.2 3.1 %collective-permute-start = (bf16[48,2560]{1,0:T(8,128)(2,1)S(1)}, bf16[48,2560]{1,0:T(8,128)(2,1)S(1)}, u32[]{:S(2)}, u32[]{:S(2)}) collective-permute-start(bf16[48,2560]{1,0:T(8,128)(2,1)S(1)} %get-tuple-element.33), channel_id=1, source_target_pairs={{0,4},{12,8},{4,0},{8,12},{1,5},{13,9},{5,1},{9,13},{2,6},{14,10},... | collective-permute-start | bytes 737288 | tf_op jit(solution)/shard_map/ppermute | solution.py:338
  7.3 1.5 %shard_map.114 = (bf16[48,2560]{1,0:T(8,128)(2,1)S(1)}, bf16[48,2560]{1,0:T(8,128)(2,1)S(1)}, bf16[48,2560]{1,0:T(8,128)(2,1)S(1)}, bf16[48,2560]{1,0:T(8,128)(2...) custom-call(bf16[384,640]{1,0:T(8,128)(2,1)S(1)} %get-tuple-element.28.turned_ref,, ...), custom_call_target="tpu_custom_call" | custom-call | tf_op jit(solution)/shard_map/pallas_call | solution.py:101
  8.9 1.9 %collective-permute-start.3 = (bf16[48,2560]{1,0:T(8,128)(2,1)S(1)}, bf16[48,2560]{1,0:T(8,128)(2,1)S(1)}, u32[]{:S(2)}, u32[]{:S(2)}) collective-permute-start(bf16[48,2560]{1,0:T(8,128)(2,1)S(1)} %get-tuple-element.36.mine_ref), channel_id=1, source_target_pairs={{0,4},{12,8},{1,5},{13,9},{2,6},{14,10},{3,7},{15,11},{16,20},{28,... | collective-permute-start | bytes 737288 | tf_op jit(solution)/shard_map/ppermute | solution.py:338
  10.8 2.9 %collective-permute-done.came_ref.early_ref = bf16[48,2560]{1,0:T(8,128)(2,1)S(1)} collective-permute-done((bf16[48,2560]{1,0:T(8,128)(2,1)S(1)}, bf16[48,2560]{1,0:T(8,128)(2,1)S(1)}, u32[]{:S(2)}, u32[]{:S(2)}) %collective-permute-start) | collective-permute-done | bytes 245792 | tf_op jit(solution)/shard_map/ppermute | solution.py:338
  14.4 6.5 %collective-permute-start.1 = (bf16[48,2560]{1,0:T(8,128)(2,1)S(1)}, bf16[48,2560]{1,0:T(8,128)(2,1)S(1)}, u32[]{:S(2)}, u32[]{:S(2)}) collective-permute-start(bf16[48,2560]{1,0:T(8,128)(2,1)S(1)} %get-tuple-element.34), channel_id=1, source_target_pairs={{0,4},{12,8},{1,5},{13,9},{2,6},{14,10},{3,7},{15,11},{16,20},{28,... | collective-permute-start | bytes 737288 | tf_op jit(solution)/shard_map/ppermute | solution.py:338
  21.0 1.9 %shard_map.136 = (bf16[320,2560]{1,0:T(8,128)(2,1)S(1)}, bf16[320,1920]{1,0:T(8,128)(2,1)S(1)}, bf16[320,640]{1,0:T(8,128)(2,1)S(1)}) custom-call(bf16[320,2560]{1,0:T(8,128)(2,1)} %bitcast.18, bf16[320,2560]{1,0:T(8,128)(2,1)} %bitcast.19, bf16[48,2560]{1,0:T(8,128)(2,1)S(1)} %get-tuple-element.48.rest_0_.mine_ref.after_ref), custom_call_target="tpu_custom_call" | custom-call | tf_op jit(solution)/shard_map/pallas_call | solution.py:140
  22.9 1.6 %collective-permute-start.16 = (bf16[320,1920]{1,0:T(8,128)(2,1)S(1)}, bf16[320,1920]{1,0:T(8,128)(2,1)S(1)}, u32[]{:S(2)}, u32[]{:S(2)}) collective-permute-start(bf16[320,1920]{1,0:T(8,128)(2,1)S(1)} %get-tuple-element.51), channel_id=1, source_target_pairs={{0,16},{16,0},{1,17},{17,1},{2,18},{18,2},{3,19},{19,3},{4,20},{20... | collective-permute-start | bytes 3686408 | tf_op jit(solution)/shard_map/ppermute | solution.py:346
  25.3 1.8 %collective-permute-start.5 = (bf16[48,2560]{1,0:T(8,128)(2,1)S(1)}, bf16[48,2560]{1,0:T(8,128)(2,1)S(1)}, u32[]{:S(2)}, u32[]{:S(2)}) collective-permute-start(bf16[48,2560]{1,0:T(8,128)(2,1)S(1)} %get-tuple-element.39), channel_id=1, source_target_pairs={{0,4},{12,8},{4,0},{8,12},{1,5},{13,9},{5,1},{9,13},{2,6},{14,10},... | collective-permute-start | bytes 737288 | tf_op jit(solution)/shard_map/ppermute | solution.py:338
  28.0 6.8 %collective-permute-start.8 = (bf16[48,2560]{1,0:T(8,128)(2,1)S(1)}, bf16[48,2560]{1,0:T(8,128)(2,1)S(1)}, u32[]{:S(2)}, u32[]{:S(2)}) collective-permute-start(bf16[48,2560]{1,0:T(8,128)(2,1)S(1)} %get-tuple-element.43), channel_id=1, source_target_pairs={{0,4},{12,8},{4,0},{8,12},{1,5},{13,9},{5,1},{9,13},{2,6},{14,10},... | collective-permute-start | bytes 737288 | tf_op jit(solution)/shard_map/ppermute | solution.py:338
  35.6 4.4 %collective-permute-start.7 = (bf16[48,2560]{1,0:T(8,128)(2,1)S(1)}, bf16[48,2560]{1,0:T(8,128)(2,1)S(1)}, u32[]{:S(2)}, u32[]{:S(2)}) collective-permute-start(bf16[48,2560]{1,0:T(8,128)(2,1)S(1)} %get-tuple-element.42), channel_id=1, source_target_pairs={{0,4},{12,8},{4,0},{8,12},{1,5},{13,9},{5,1},{9,13},{2,6},{14,10},... | collective-permute-start | bytes 737288 | tf_op jit(solution)/shard_map/ppermute | solution.py:338
  40.0 0.9 collective-permute-done.8.came_ref
  41.8 3.7 %collective-permute-start.11 = (bf16[48,2560]{1,0:T(8,128)(2,1)S(1)}, bf16[48,2560]{1,0:T(8,128)(2,1)S(1)}, u32[]{:S(2)}, u32[]{:S(2)}) collective-permute-start(bf16[48,2560]{1,0:T(8,128)(2,1)S(1)} %get-tuple-element.47), channel_id=1, source_target_pairs={{0,4},{12,8},{4,0},{8,12},{1,5},{13,9},{5,1},{9,13},{2,6},{14,10},... | collective-permute-start | bytes 737288 | tf_op jit(solution)/shard_map/ppermute | solution.py:338
  47.0 1.1 %collective-permute-start.17 = (bf16[320,640]{1,0:T(8,128)(2,1)S(1)}, bf16[320,640]{1,0:T(8,128)(2,1)S(1)}, u32[]{:S(2)}, u32[]{:S(2)}) collective-permute-start(bf16[320,640]{1,0:T(8,128)(2,1)S(1)} %get-tuple-element.52), channel_id=1, source_target_pairs={{0,16},{16,0},{1,17},{17,1},{2,18},{18,2},{3,19},{19,3},{4,20},{20... | collective-permute-start | bytes 1228808 | tf_op jit(solution)/shard_map/ppermute | solution.py:346
  48.2 3.7 %collective-permute-start.14 = (bf16[48,2560]{1,0:T(8,128)(2,1)S(1)}, bf16[48,2560]{1,0:T(8,128)(2,1)S(1)}, u32[]{:S(2)}, u32[]{:S(2)}) collective-permute-start(bf16[48,2560]{1,0:T(8,128)(2,1)S(1)} %get-tuple-element.50), channel_id=1, source_target_pairs={{0,4},{12,8},{4,0},{8,12},{1,5},{13,9},{5,1},{9,13},{2,6},{14,10},... | collective-permute-start | bytes 737288 | tf_op jit(solution)/shard_map/ppermute | solution.py:338
  52.8 1.3 %collective-permute-start.13 = (bf16[48,2560]{1,0:T(8,128)(2,1)S(1)}, bf16[48,2560]{1,0:T(8,128)(2,1)S(1)}, u32[]{:S(2)}, u32[]{:S(2)}) collective-permute-start(bf16[48,2560]{1,0:T(8,128)(2,1)S(1)} %shard_map.130.after_ref.mine_ref), channel_id=1, source_target_pairs={{4,0},{8,12},{5,1},{9,13},{6,2},{10,14},{7,3},{11,15},{20,16},{24,... | collective-permute-start | bytes 737288 | tf_op jit(solution)/shard_map/ppermute | solution.py:338
  54.1 5.1 %collective-permute-done.14.came_ref = bf16[48,2560]{1,0:T(8,128)(2,1)S(1)} collective-permute-done((bf16[48,2560]{1,0:T(8,128)(2,1)S(1)}, bf16[48,2560]{1,0:T(8,128)(2,1)S(1)}, u32[]{:S(2)}, u32[]{:S(2)}) %collective-permute-start.14) | collective-permute-done | bytes 245792 | tf_op jit(solution)/shard_map/ppermute | solution.py:338
  59.3 4.1 %collective-permute-start.19 = (bf16[48,2560]{1,0:T(8,128)(2,1)S(1)}, bf16[48,2560]{1,0:T(8,128)(2,1)S(1)}, u32[]{:S(2)}, u32[]{:S(2)}) collective-permute-start(bf16[48,2560]{1,0:T(8,128)(2,1)S(1)} %shard_map.132.after_ref.mine_ref), channel_id=1, source_target_pairs={{0,8},{4,12},{8,0},{12,4},{1,9},{5,13},{9,1},{13,5},{2,10},{6,14},... | collective-permute-start | bytes 737288 | tf_op jit(solution)/shard_map/ppermute | solution.py:368
  63.5 1.3 %collective-permute-start.18 = (bf16[48,2560]{1,0:T(8,128)(2,1)S(1)}, bf16[48,2560]{1,0:T(8,128)(2,1)S(1)}, u32[]{:S(2)}, u32[]{:S(2)}) collective-permute-start(bf16[48,2560]{1,0:T(8,128)(2,1)S(1)} %shard_map.133.after_ref.mine_ref), channel_id=1, source_target_pairs={{4,0},{8,12},{5,1},{9,13},{6,2},{10,14},{7,3},{11,15},{20,16},{24,... | collective-permute-start | bytes 737288 | tf_op jit(solution)/shard_map/ppermute | solution.py:338
  65.5 1.0 %shard_map.137.after_ref = bf16[288,320]{1,0:T(8,128)(2,1)S(1)} custom-call(bf16[48,2560]{1,0:T(8,128)(2,1)S(1)} %shard_map.135.after_ref.rest_7_.rest_6_, bf16[320,1920]{1,0:T(8,128)(2,1)S(1)} %collective-permute-done.16.rest_0_, bf16[320,640]{1,0:T(8,128)(2,1)S(1)} %collective-permute-done.17.rest_1_, ...), custom_call_target="tpu_custom_call" | custom-call | tf_op jit(solution)/shard_map/pallas_call | solution.py:241
  66.5 4.9 %collective-permute-start.20 = (bf16[288,320]{1,0:T(8,128)(2,1)S(1)}, bf16[288,320]{1,0:T(8,128)(2,1)S(1)}, u32[]{:S(2)}, u32[]{:S(2)}) collective-permute-start(bf16[288,320]{1,0:T(8,128)(2,1)S(1)} %shard_map.137.after_ref), channel_id=1, source_target_pairs={{0,16},{16,0},{1,17},{17,1},{2,18},{18,2},{3,19},{19,3},{4,20},{20... | collective-permute-start | bytes 552968 | tf_op jit(solution)/shard_map/ppermute | solution.py:353
  71.3 0.9 %shard_map.138.after_ref.refs_0_ = f32[288,320]{1,0:T(8,128)S(1)} custom-call(bf16[288,320]{1,0:T(8,128)(2,1)S(1)} %shard_map.137.after_ref, bf16[320,2560]{1,0:T(8,128)(2,1)S(1)} %get-tuple-element.53.rest_0_, bf16[48,2560]{1,0:T(8,128)(2,1)S(1)} %shard_map.122.after_ref.rest_2_.rest_1_, bf16[48,2560]{1,0:T(8,128)(2,1)S(1)} %shard_map.125.after_ref.rest_3_.rest_2_, ...), custom_call_target="tpu_custom_call" | custom-call | tf_op jit(solution)/shard_map/pallas_call | solution.py:241
  73.3 0.7 collective-permute-start.21
  75.2 2.5 %collective-permute-done.21.refs_3_ = bf16[96,320]{1,0:T(8,128)(2,1)S(1)} collective-permute-done((bf16[96,320]{1,0:T(8,128)(2,1)S(1)}, bf16[96,320]{1,0:T(8,128)(2,1)S(1)}, u32[]{:S(2)}, u32[]{:S(2)}) %collective-permute-start.21) | collective-permute-done | bytes 61472 | tf_op jit(solution)/shard_map/ppermute | solution.py:353
  77.8 0.9 shard_map.143
  78.6 1.2 %collective-permute-done.22 = f32[12,384]{1,0:T(8,128)S(1)} collective-permute-done((f32[12,384]{1,0:T(8,128)S(1)}, f32[12,384]{1,0:T(8,128)S(1)}, u32[]{:S(2)}, u32[]{:S(2)}) %collective-permute-start.22) | collective-permute-done | bytes 18464 | tf_op jit(solution)/shard_map/ppermute | solution.py:404
  79.8 1.5 %collective-permute-start.23 = (f32[12,384]{1,0:T(8,128)S(1)}, f32[12,384]{1,0:T(8,128)S(1)}, u32[]{:S(2)}, u32[]{:S(2)}) collective-permute-start(f32[12,384]{1,0:T(8,128)S(1)} %add.12), channel_id=1, source_target_pairs={{0,2},{1,3},{2,0},{3,1},{4,6},{5,7},{6,4},{7,5},{8,10},{9,11},{10,... | collective-permute-start | bytes 55304 | tf_op jit(solution)/shard_map/ppermute | solution.py:404
  81.3 2.3 %collective-permute-done.23 = f32[12,384]{1,0:T(8,128)S(1)} collective-permute-done((f32[12,384]{1,0:T(8,128)S(1)}, f32[12,384]{1,0:T(8,128)S(1)}, u32[]{:S(2)}, u32[]{:S(2)}) %collective-permute-start.23) | collective-permute-done | bytes 18464 | tf_op jit(solution)/shard_map/ppermute | solution.py:404
  83.9 1.5 %collective-permute-start.25 = (f32[1,96]{1,0:T(1,128)S(1)}, f32[1,96]{1,0:T(1,128)S(1)}, u32[]{:S(2)}, u32[]{:S(2)}) collective-permute-start(f32[1,96]{1,0:T(1,128)S(1)} %reshape.10), channel_id=1, source_target_pairs={{0,12},{4,8},{8,4},{12,0},{1,13},{5,9},{9,5},{13,1},{2,14},{6,10},... | collective-permute-start | bytes 1160 | tf_op jit(solution)/shard_map/ppermute | solution.py:414
  85.4 2.0 %collective-permute-start.26 = (f32[1,96]{1,0:T(1,128)S(1)}, f32[1,96]{1,0:T(1,128)S(1)}, u32[]{:S(2)}, u32[]{:S(2)}) collective-permute-start(f32[1,96]{1,0:T(1,128)S(1)} %reshape.10), channel_id=1, source_target_pairs={{0,8},{4,12},{8,0},{12,4},{1,9},{5,13},{9,1},{13,5},{2,10},{6,14},... | collective-permute-start | bytes 1160 | tf_op jit(solution)/shard_map/ppermute | solution.py:414
  87.4 1.9 %collective-permute-done.25 = f32[1,96]{1,0:T(1,128)S(1)} collective-permute-done((f32[1,96]{1,0:T(1,128)S(1)}, f32[1,96]{1,0:T(1,128)S(1)}, u32[]{:S(2)}, u32[]{:S(2)}) %collective-permute-start.25) | collective-permute-done | bytes 416 | tf_op jit(solution)/shard_map/ppermute | solution.py:414
  90.0 0.7 select_reduce_fusion
  (70 shorter events, 10.4 us)
Async XLA Ops:
  4.2 9.5 %collective-permute-start = (bf16[48,2560]{1,0:T(8,128)(2,1)S(1)}, bf16[48,2560]{1,0:T(8,128)(2,1)S(1)}, u32[]{:S(2)}, u32[]{:S(2)}) collective-permute-start(bf16[48,2560]{1,0:T(8,128)(2,1)S(1)} %get-tuple-element.33), channel_id=1, source_target_pairs={{0,4},{12,8},{4,0},{8,12},{1,5},{13,9},{5,1},{9,13},{2,6},{14,10},... | collective-permute-start | bytes 737288 | tf_op jit(solution)/shard_map/ppermute | solution.py:338
  8.9 15.6 %collective-permute-start.3 = (bf16[48,2560]{1,0:T(8,128)(2,1)S(1)}, bf16[48,2560]{1,0:T(8,128)(2,1)S(1)}, u32[]{:S(2)}, u32[]{:S(2)}) collective-permute-start(bf16[48,2560]{1,0:T(8,128)(2,1)S(1)} %get-tuple-element.36.mine_ref), channel_id=1, source_target_pairs={{0,4},{12,8},{1,5},{13,9},{2,6},{14,10},{3,7},{15,11},{16,20},{28,... | collective-permute-start | bytes 737288 | tf_op jit(solution)/shard_map/ppermute | solution.py:338
  13.8 11.5 %collective-permute-start.2 = (bf16[48,2560]{1,0:T(8,128)(2,1)S(1)}, bf16[48,2560]{1,0:T(8,128)(2,1)S(1)}, u32[]{:S(2)}, u32[]{:S(2)}) collective-permute-start(bf16[48,2560]{1,0:T(8,128)(2,1)S(1)} %get-tuple-element.35.after_ref.mine_ref), channel_id=1, source_target_pairs={{4,8},{8,4},{5,9},{9,5},{6,10},{10,6},{7,11},{11,7},{20,24},{24,20... | collective-permute-start | bytes 737288 | tf_op jit(solution)/shard_map/ppermute | solution.py:338
  14.4 12.7 %collective-permute-start.1 = (bf16[48,2560]{1,0:T(8,128)(2,1)S(1)}, bf16[48,2560]{1,0:T(8,128)(2,1)S(1)}, u32[]{:S(2)}, u32[]{:S(2)}) collective-permute-start(bf16[48,2560]{1,0:T(8,128)(2,1)S(1)} %get-tuple-element.34), channel_id=1, source_target_pairs={{0,4},{12,8},{1,5},{13,9},{2,6},{14,10},{3,7},{15,11},{16,20},{28,... | collective-permute-start | bytes 737288 | tf_op jit(solution)/shard_map/ppermute | solution.py:338
  22.9 42.6 %collective-permute-start.16 = (bf16[320,1920]{1,0:T(8,128)(2,1)S(1)}, bf16[320,1920]{1,0:T(8,128)(2,1)S(1)}, u32[]{:S(2)}, u32[]{:S(2)}) collective-permute-start(bf16[320,1920]{1,0:T(8,128)(2,1)S(1)} %get-tuple-element.51), channel_id=1, source_target_pairs={{0,16},{16,0},{1,17},{17,1},{2,18},{18,2},{3,19},{19,3},{4,20},{20... | collective-permute-start | bytes 3686408 | tf_op jit(solution)/shard_map/ppermute | solution.py:346
  24.5 3.3 %collective-permute-start.6 = (bf16[48,2560]{1,0:T(8,128)(2,1)S(1)}, bf16[48,2560]{1,0:T(8,128)(2,1)S(1)}, u32[]{:S(2)}, u32[]{:S(2)}) collective-permute-start(bf16[48,2560]{1,0:T(8,128)(2,1)S(1)} %shard_map.116.after_ref.mine_ref), channel_id=1, source_target_pairs={{4,8},{8,4},{5,9},{9,5},{6,10},{10,6},{7,11},{11,7},{20,24},{24,20... | collective-permute-start | bytes 737288 | tf_op jit(solution)/shard_map/ppermute | solution.py:338
  25.3 9.5 %collective-permute-start.5 = (bf16[48,2560]{1,0:T(8,128)(2,1)S(1)}, bf16[48,2560]{1,0:T(8,128)(2,1)S(1)}, u32[]{:S(2)}, u32[]{:S(2)}) collective-permute-start(bf16[48,2560]{1,0:T(8,128)(2,1)S(1)} %get-tuple-element.39), channel_id=1, source_target_pairs={{0,4},{12,8},{4,0},{8,12},{1,5},{13,9},{5,1},{9,13},{2,6},{14,10},... | collective-permute-start | bytes 737288 | tf_op jit(solution)/shard_map/ppermute | solution.py:338
  27.2 8.4 %collective-permute-start.4 = (bf16[48,2560]{1,0:T(8,128)(2,1)S(1)}, bf16[48,2560]{1,0:T(8,128)(2,1)S(1)}, u32[]{:S(2)}, u32[]{:S(2)}) collective-permute-start(bf16[48,2560]{1,0:T(8,128)(2,1)S(1)} %shard_map.118.after_ref.mine_ref), channel_id=1, source_target_pairs={{4,8},{8,4},{5,9},{9,5},{6,10},{10,6},{7,11},{11,7},{20,24},{24,20... | collective-permute-start | bytes 737288 | tf_op jit(solution)/shard_map/ppermute | solution.py:338
  28.0 13.0 %collective-permute-start.8 = (bf16[48,2560]{1,0:T(8,128)(2,1)S(1)}, bf16[48,2560]{1,0:T(8,128)(2,1)S(1)}, u32[]{:S(2)}, u32[]{:S(2)}) collective-permute-start(bf16[48,2560]{1,0:T(8,128)(2,1)S(1)} %get-tuple-element.43), channel_id=1, source_target_pairs={{0,4},{12,8},{4,0},{8,12},{1,5},{13,9},{5,1},{9,13},{2,6},{14,10},... | collective-permute-start | bytes 737288 | tf_op jit(solution)/shard_map/ppermute | solution.py:338
  34.9 6.8 %collective-permute-start.9 = (bf16[48,2560]{1,0:T(8,128)(2,1)S(1)}, bf16[48,2560]{1,0:T(8,128)(2,1)S(1)}, u32[]{:S(2)}, u32[]{:S(2)}) collective-permute-start(bf16[48,2560]{1,0:T(8,128)(2,1)S(1)} %shard_map.120.after_ref.mine_ref), channel_id=1, source_target_pairs={{4,8},{8,4},{5,9},{9,5},{6,10},{10,6},{7,11},{11,7},{20,24},{24,20... | collective-permute-start | bytes 737288 | tf_op jit(solution)/shard_map/ppermute | solution.py:338
  35.6 10.6 %collective-permute-start.7 = (bf16[48,2560]{1,0:T(8,128)(2,1)S(1)}, bf16[48,2560]{1,0:T(8,128)(2,1)S(1)}, u32[]{:S(2)}, u32[]{:S(2)}) collective-permute-start(bf16[48,2560]{1,0:T(8,128)(2,1)S(1)} %get-tuple-element.42), channel_id=1, source_target_pairs={{0,4},{12,8},{4,0},{8,12},{1,5},{13,9},{5,1},{9,13},{2,6},{14,10},... | collective-permute-start | bytes 737288 | tf_op jit(solution)/shard_map/ppermute | solution.py:338
  41.0 7.1 %collective-permute-start.12 = (bf16[48,2560]{1,0:T(8,128)(2,1)S(1)}, bf16[48,2560]{1,0:T(8,128)(2,1)S(1)}, u32[]{:S(2)}, u32[]{:S(2)}) collective-permute-start(bf16[48,2560]{1,0:T(8,128)(2,1)S(1)} %shard_map.123.after_ref.mine_ref), channel_id=1, source_target_pairs={{4,8},{8,4},{5,9},{9,5},{6,10},{10,6},{7,11},{11,7},{20,24},{24,20... | collective-permute-start | bytes 737288 | tf_op jit(solution)/shard_map/ppermute | solution.py:338
  41.8 10.2 %collective-permute-start.11 = (bf16[48,2560]{1,0:T(8,128)(2,1)S(1)}, bf16[48,2560]{1,0:T(8,128)(2,1)S(1)}, u32[]{:S(2)}, u32[]{:S(2)}) collective-permute-start(bf16[48,2560]{1,0:T(8,128)(2,1)S(1)} %get-tuple-element.47), channel_id=1, source_target_pairs={{0,4},{12,8},{4,0},{8,12},{1,5},{13,9},{5,1},{9,13},{2,6},{14,10},... | collective-permute-start | bytes 737288 | tf_op jit(solution)/shard_map/ppermute | solution.py:338
  46.3 6.5 %collective-permute-start.10 = (bf16[48,2560]{1,0:T(8,128)(2,1)S(1)}, bf16[48,2560]{1,0:T(8,128)(2,1)S(1)}, u32[]{:S(2)}, u32[]{:S(2)}) collective-permute-start(bf16[48,2560]{1,0:T(8,128)(2,1)S(1)} %shard_map.126.after_ref.mine_ref), channel_id=1, source_target_pairs={{4,8},{8,4},{5,9},{9,5},{6,10},{10,6},{7,11},{11,7},{20,24},{24,20... | collective-permute-start | bytes 737288 | tf_op jit(solution)/shard_map/ppermute | solution.py:338
  47.0 18.5 %collective-permute-start.17 = (bf16[320,640]{1,0:T(8,128)(2,1)S(1)}, bf16[320,640]{1,0:T(8,128)(2,1)S(1)}, u32[]{:S(2)}, u32[]{:S(2)}) collective-permute-start(bf16[320,640]{1,0:T(8,128)(2,1)S(1)} %get-tuple-element.52), channel_id=1, source_target_pairs={{0,16},{16,0},{1,17},{17,1},{2,18},{18,2},{3,19},{19,3},{4,20},{20... | collective-permute-start | bytes 1228808 | tf_op jit(solution)/shard_map/ppermute | solution.py:346
  48.2 11.0 %collective-permute-start.14 = (bf16[48,2560]{1,0:T(8,128)(2,1)S(1)}, bf16[48,2560]{1,0:T(8,128)(2,1)S(1)}, u32[]{:S(2)}, u32[]{:S(2)}) collective-permute-start(bf16[48,2560]{1,0:T(8,128)(2,1)S(1)} %get-tuple-element.50), channel_id=1, source_target_pairs={{0,4},{12,8},{4,0},{8,12},{1,5},{13,9},{5,1},{9,13},{2,6},{14,10},... | collective-permute-start | bytes 737288 | tf_op jit(solution)/shard_map/ppermute | solution.py:338
  52.0 11.4 %collective-permute-start.15 = (bf16[48,2560]{1,0:T(8,128)(2,1)S(1)}, bf16[48,2560]{1,0:T(8,128)(2,1)S(1)}, u32[]{:S(2)}, u32[]{:S(2)}) collective-permute-start(bf16[48,2560]{1,0:T(8,128)(2,1)S(1)} %shard_map.129.after_ref.mine_ref), channel_id=1, source_target_pairs={{4,8},{8,4},{5,9},{9,5},{6,10},{10,6},{7,11},{11,7},{20,24},{24,20... | collective-permute-start | bytes 737288 | tf_op jit(solution)/shard_map/ppermute | solution.py:338
  52.8 12.6 %collective-permute-start.13 = (bf16[48,2560]{1,0:T(8,128)(2,1)S(1)}, bf16[48,2560]{1,0:T(8,128)(2,1)S(1)}, u32[]{:S(2)}, u32[]{:S(2)}) collective-permute-start(bf16[48,2560]{1,0:T(8,128)(2,1)S(1)} %shard_map.130.after_ref.mine_ref), channel_id=1, source_target_pairs={{4,0},{8,12},{5,1},{9,13},{6,2},{10,14},{7,3},{11,15},{20,16},{24,... | collective-permute-start | bytes 737288 | tf_op jit(solution)/shard_map/ppermute | solution.py:338
  59.3 13.0 %collective-permute-start.19 = (bf16[48,2560]{1,0:T(8,128)(2,1)S(1)}, bf16[48,2560]{1,0:T(8,128)(2,1)S(1)}, u32[]{:S(2)}, u32[]{:S(2)}) collective-permute-start(bf16[48,2560]{1,0:T(8,128)(2,1)S(1)} %shard_map.132.after_ref.mine_ref), channel_id=1, source_target_pairs={{0,8},{4,12},{8,0},{12,4},{1,9},{5,13},{9,1},{13,5},{2,10},{6,14},... | collective-permute-start | bytes 737288 | tf_op jit(solution)/shard_map/ppermute | solution.py:368
  63.5 9.2 %collective-permute-start.18 = (bf16[48,2560]{1,0:T(8,128)(2,1)S(1)}, bf16[48,2560]{1,0:T(8,128)(2,1)S(1)}, u32[]{:S(2)}, u32[]{:S(2)}) collective-permute-start(bf16[48,2560]{1,0:T(8,128)(2,1)S(1)} %shard_map.133.after_ref.mine_ref), channel_id=1, source_target_pairs={{4,0},{8,12},{5,1},{9,13},{6,2},{10,14},{7,3},{11,15},{20,16},{24,... | collective-permute-start | bytes 737288 | tf_op jit(solution)/shard_map/ppermute | solution.py:338
  66.5 8.8 %collective-permute-start.20 = (bf16[288,320]{1,0:T(8,128)(2,1)S(1)}, bf16[288,320]{1,0:T(8,128)(2,1)S(1)}, u32[]{:S(2)}, u32[]{:S(2)}) collective-permute-start(bf16[288,320]{1,0:T(8,128)(2,1)S(1)} %shard_map.137.after_ref), channel_id=1, source_target_pairs={{0,16},{16,0},{1,17},{17,1},{2,18},{18,2},{3,19},{19,3},{4,20},{20... | collective-permute-start | bytes 552968 | tf_op jit(solution)/shard_map/ppermute | solution.py:353
  73.3 4.5 %copy-start = (s32[1,8]{1,0:T(1,128)S(1)}, s32[1,8]{1,0:T(1,128)}, u32[]{:S(2)}) copy-start(s32[1,8]{1,0:T(1,128)} %counts_ref.1) | copy-start | bytes 100
  73.3 14.1 %copy-start.2 = (s32[128]{0:T(128)S(1)}, s32[128]{0:T(128)}, u32[]{:S(2)}) copy-start(s32[128]{0:T(128)} %param.19) | copy-start | bytes 1540
  73.3 14.1 %copy-start.3 = (s32[128]{0:T(128)S(1)}, s32[128]{0:T(128)}, u32[]{:S(2)}) copy-start(s32[128]{0:T(128)} %param.17) | copy-start | bytes 1540
  73.3 14.1 %copy-start.4 = (s32[128,1]{0,1:T(1,128)S(1)}, s32[128,1]{0,1:T(1,128)}, u32[]{:S(2)}) copy-start(s32[128,1]{0,1:T(1,128)} %param.18) | copy-start | bytes 1540
  73.3 4.4 %collective-permute-start.21 = (bf16[96,320]{1,0:T(8,128)(2,1)S(1)}, bf16[96,320]{1,0:T(8,128)(2,1)S(1)}, u32[]{:S(2)}, u32[]{:S(2)}) collective-permute-start(bf16[96,320]{1,0:T(8,128)(2,1)S(1)} %shard_map.141.after_ref), channel_id=1, source_target_pairs={{0,16},{16,0},{1,17},{17,1},{2,18},{18,2},{3,19},{19,3},{4,20},{20... | collective-permute-start | bytes 184328 | tf_op jit(solution)/shard_map/ppermute | solution.py:353
  78.6 1.2 %collective-permute-start.22 = (f32[12,384]{1,0:T(8,128)S(1)}, f32[12,384]{1,0:T(8,128)S(1)}, u32[]{:S(2)}, u32[]{:S(2)}) collective-permute-start(f32[12,384]{1,0:T(8,128)S(1)} %shard_map.143), channel_id=1, source_target_pairs={{0,1},{1,0},{2,3},{3,2},{4,5},{5,4},{6,7},{7,6},{8,9},{9,8},{10,11... | collective-permute-start | bytes 55304 | tf_op jit(solution)/shard_map/ppermute | solution.py:404
  79.8 3.8 %collective-permute-start.23 = (f32[12,384]{1,0:T(8,128)S(1)}, f32[12,384]{1,0:T(8,128)S(1)}, u32[]{:S(2)}, u32[]{:S(2)}) collective-permute-start(f32[12,384]{1,0:T(8,128)S(1)} %add.12), channel_id=1, source_target_pairs={{0,2},{1,3},{2,0},{3,1},{4,6},{5,7},{6,4},{7,5},{8,10},{9,11},{10,... | collective-permute-start | bytes 55304 | tf_op jit(solution)/shard_map/ppermute | solution.py:404
  83.7 7.0 %copy-start.1 = (f32[12,384]{1,0:T(8,128)}, f32[12,384]{1,0:T(8,128)S(1)}, u32[]{:S(2)}) copy-start(f32[12,384]{1,0:T(8,128)S(1)} %add.13) | copy-start | bytes 55300
  83.8 3.6 %collective-permute-start.24 = (f32[1,96]{1,0:T(1,128)S(1)}, f32[1,96]{1,0:T(1,128)S(1)}, u32[]{:S(2)}, u32[]{:S(2)}) collective-permute-start(f32[1,96]{1,0:T(1,128)S(1)} %reshape.10), channel_id=1, source_target_pairs={{0,4},{4,0},{8,12},{12,8},{1,5},{5,1},{9,13},{13,9},{2,6},{6,2},{1... | collective-permute-start | bytes 1160 | tf_op jit(solution)/shard_map/ppermute | solution.py:414
  83.9 5.4 %collective-permute-start.25 = (f32[1,96]{1,0:T(1,128)S(1)}, f32[1,96]{1,0:T(1,128)S(1)}, u32[]{:S(2)}, u32[]{:S(2)}) collective-permute-start(f32[1,96]{1,0:T(1,128)S(1)} %reshape.10), channel_id=1, source_target_pairs={{0,12},{4,8},{8,4},{12,0},{1,13},{5,9},{9,5},{13,1},{2,14},{6,10},... | collective-permute-start | bytes 1160 | tf_op jit(solution)/shard_map/ppermute | solution.py:414
  85.4 4.4 %collective-permute-start.26 = (f32[1,96]{1,0:T(1,128)S(1)}, f32[1,96]{1,0:T(1,128)S(1)}, u32[]{:S(2)}, u32[]{:S(2)}) collective-permute-start(f32[1,96]{1,0:T(1,128)S(1)} %reshape.10), channel_id=1, source_target_pairs={{0,8},{4,12},{8,0},{12,4},{1,9},{5,13},{9,1},{13,5},{2,10},{6,14},... | collective-permute-start | bytes 1160 | tf_op jit(solution)/shard_map/ppermute | solution.py:414

commit v15 on v14

--- a/solution.py
+++ b/solution.py
@@ -178,7 +178,8 @@
     )(mine, came, early, after)
 
 
-def total_kernel(shared, mine_ref, came_ref, after_ref, *rest):
+def total_kernel(shared, paced, mine_ref, came_ref, after_ref, *rest):
+    rest = rest[paced:]
     mine = mine_ref[...].astype(jnp.float32) + came_ref[...].astype(jnp.float32)
     rest[-1][...] = mine.astype(jnp.bfloat16)
     if shared:
@@ -187,15 +188,16 @@
         rest[1][...] = rest[0][...]
 
 
-def total(after, mine, came, later=None, shared=False):
+def total(after, mine, came, later=None, shared=False, pace=None):
     extra = [] if later is None else [later]
+    paced = [] if pace is None else [pace]
     out = pl.pallas_call(
-        functools.partial(total_kernel, shared),
+        functools.partial(total_kernel, shared, len(paced)),
         out_shape=[bf16(*a.shape) for a in extra + [mine]],
-        in_specs=[VMEM, VMEM, ANY] + [VMEM] * len(extra),
+        in_specs=[VMEM, VMEM, ANY] + [ANY] * len(paced) + [VMEM] * len(extra),
         out_specs=[VMEM] * (1 + len(extra)),
         compiler_params=pltpu.CompilerParams(vmem_limit_bytes=8 * MIB),
-    )(mine, came, after, *extra)
+    )(mine, came, after, *paced, *extra)
     return out[-1], (out[0] if extra else None)
 
 
@@ -355,6 +357,7 @@
         waiting.clear()
         return mine[-1]
 
+    pace = None
     swapped = set()
     turns = chunks + last - short
     for turn in range(turns):
@@ -381,7 +384,9 @@
             if kind == "out":
                 part[c], send = take(after, hop, part[c], came[c], chunk)
             else:
-                part[c], send = total(after, part[c], came[c], chunk, shared)
+                part[c], send = total(after, part[c], came[c], chunk, shared, pace if s == 0 else None)
+            if s == 0 and kind == "in" and layers % 2 == 0:
+                pace = lax.ppermute(part[c], "layer", [(i, i ^ 1) for i in range(layers)])
             after = part[c]
             if shared:
                 came[c] = came[use] = transfer(("in", "out"), 0, send)

time: 91 us -> 97.5 us (1.071)
  waiting for transfers between devices: 19.6 us -> 30 us
  starting transfers between devices: 56.7 us -> 52.7 us
    ppermute x17, waiting for transfers between devices: 10.6 us -> 16 us  [transfer(): return lax.ppermute(value, 'dp', pairs)]
    ppermute x1, waiting for transfers between devices: 0.01 us -> 4.02 us  [per_device(): came[c] = lax.ppermute(part[c], 'dp', [(i, i ^ 2) for i in range(n)])]
    ppermute x2, starting transfers between devices: 5.53 us -> 2.11 us  [project_waiting(): back.append(lax.ppermute(away, 'parts', swap))]
    ppermute x1, starting transfers between devices: 4.12 us -> 2.57 us  [per_device(): came[c] = lax.ppermute(part[c], 'dp', [(i, i ^ 2) for i in range(n)])]
    ppermute x17, starting transfers between devices: 39.3 us -> 40.4 us  [transfer(): return lax.ppermute(value, 'dp', pairs)]
  transfers between devices with their start and end apart: 27 -> 33, of which waited for: 13 -> 12; matrix products, arithmetic and copies ran while one was open for 0% -> 0% of each run, Pallas kernels for 9% -> 8%
where the time goes in v15:
time: 97.5 us; the launch traced here: 97.2 us
  starting transfers between devices  52.7 us (54%)
  waiting for transfers between devices  30 us (31%)
  Pallas kernels  12.3 us (13%)
  between operations  1.15 us (1%)
    ppermute x17, starting transfers between devices, transfer(): return lax.ppermute(value, 'dp', pairs)  40.4 us
    ppermute x17, waiting for transfers between devices, transfer(): return lax.ppermute(value, 'dp', pairs)  16 us
    ppermute x1, waiting for transfers between devices, per_device(): came[c] = lax.ppermute(part[c], 'dp', [(i, i ^ 2) for i in range(n)])  4.02 us
    pallas_call x1, Pallas kernels, first_pull(): pl.pallas_call(first_pull_kernel, out_shape=[bf16(rows, features)] * 2 +...  3.61 us
    ppermute x3, starting transfers between devices, per_device(): lax.ppermute(flat, 'dp', [(i, i ^ k ^ k >> 1) for i in range(n)])  3.55 us
    ppermute x2, waiting for transfers between devices, per_device(): lax.ppermute(scores, 'layer', [(i, i ^ step) for i in range(layers)])  3.52 us
    ppermute x3, waiting for transfers between devices, per_device(): lax.ppermute(flat, 'dp', [(i, i ^ k ^ k >> 1) for i in range(n)])  3.25 us
    ppermute x2, waiting for transfers between devices, project_waiting(): back.append(lax.ppermute(away, 'parts', swap))  3.19 us
  transfers between devices with their start and end apart: 33, of which 12 were waited for; matrix products, arithmetic and copies ran while one was open for 0% of the time, Pallas kernels for 8%

profile of v15, /device:TPU:0, one launch (start us, length us, event | category | flops | bytes accessed | tf_op | source)
XLA Modules:
  0.0 97.2 jit_solution(17190043875613672087)
XLA Ops:
  0.6 3.6 %shard_map.113 = (bf16[48,2560]{1,0:T(8,128)(2,1)S(1)}, bf16[48,2560]{1,0:T(8,128)(2,1)S(1)}, bf16[2560,640]{1,0:T(8,128)(2,1)S(1)}, bf16[640,384]{1,0:T(8,128)(2,1)}, bf16[384,640]{1,0:T(8,128)(2,1)S(1)}) custom-call(bf16[2560,640]{1,0:T(8,128)(2,1)} %bitcast.16, bf16[2560,640]{1,0:T(8,128)(2,1)} %bitcast.17, bf16[640,384]{1,0:T(8,128)(2,1)} %bitcast.20, ...), custom_call_target="tpu_custom_call" | custom-call | tf_op jit(solution)/shard_map/pallas_call | solution.py:77
  4.2 3.1 %collective-permute-start = (bf16[48,2560]{1,0:T(8,128)(2,1)S(1)}, bf16[48,2560]{1,0:T(8,128)(2,1)S(1)}, u32[]{:S(2)}, u32[]{:S(2)}) collective-permute-start(bf16[48,2560]{1,0:T(8,128)(2,1)S(1)} %get-tuple-element.33), channel_id=1, source_target_pairs={{0,4},{12,8},{4,0},{8,12},{1,5},{13,9},{5,1},{9,13},{2,6},{14,10},... | collective-permute-start | bytes 737288 | tf_op jit(solution)/shard_map/ppermute | solution.py:340
  7.3 1.5 %shard_map.114 = (bf16[48,2560]{1,0:T(8,128)(2,1)S(1)}, bf16[48,2560]{1,0:T(8,128)(2,1)S(1)}, bf16[48,2560]{1,0:T(8,128)(2,1)S(1)}, bf16[48,2560]{1,0:T(8,128)(2...) custom-call(bf16[384,640]{1,0:T(8,128)(2,1)S(1)} %get-tuple-element.28.turned_ref,, ...), custom_call_target="tpu_custom_call" | custom-call | tf_op jit(solution)/shard_map/pallas_call | solution.py:101
  8.9 1.9 %collective-permute-start.3 = (bf16[48,2560]{1,0:T(8,128)(2,1)S(1)}, bf16[48,2560]{1,0:T(8,128)(2,1)S(1)}, u32[]{:S(2)}, u32[]{:S(2)}) collective-permute-start(bf16[48,2560]{1,0:T(8,128)(2,1)S(1)} %get-tuple-element.36.mine_ref), channel_id=1, source_target_pairs={{0,4},{12,8},{1,5},{13,9},{2,6},{14,10},{3,7},{15,11},{16,20},{28,... | collective-permute-start | bytes 737288 | tf_op jit(solution)/shard_map/ppermute | solution.py:340
  10.8 2.9 %collective-permute-done.came_ref.early_ref = bf16[48,2560]{1,0:T(8,128)(2,1)S(1)} collective-permute-done((bf16[48,2560]{1,0:T(8,128)(2,1)S(1)}, bf16[48,2560]{1,0:T(8,128)(2,1)S(1)}, u32[]{:S(2)}, u32[]{:S(2)}) %collective-permute-start) | collective-permute-done | bytes 245792 | tf_op jit(solution)/shard_map/ppermute | solution.py:340
  14.5 6.5 %collective-permute-start.1 = (bf16[48,2560]{1,0:T(8,128)(2,1)S(1)}, bf16[48,2560]{1,0:T(8,128)(2,1)S(1)}, u32[]{:S(2)}, u32[]{:S(2)}) collective-permute-start(bf16[48,2560]{1,0:T(8,128)(2,1)S(1)} %get-tuple-element.34), channel_id=1, source_target_pairs={{0,4},{12,8},{1,5},{13,9},{2,6},{14,10},{3,7},{15,11},{16,20},{28,... | collective-permute-start | bytes 737288 | tf_op jit(solution)/shard_map/ppermute | solution.py:340
  22.0 5.1 %collective-permute-start.7 = (bf16[48,2560]{1,0:T(8,128)(2,1)S(1)}, bf16[48,2560]{1,0:T(8,128)(2,1)S(1)}, u32[]{:S(2)}, u32[]{:S(2)}) collective-permute-start(bf16[48,2560]{1,0:T(8,128)(2,1)S(1)} %get-tuple-element.39), channel_id=1, source_target_pairs={{0,4},{12,8},{4,0},{8,12},{1,5},{13,9},{5,1},{9,13},{2,6},{14,10},... | collective-permute-start | bytes 737288 | tf_op jit(solution)/shard_map/ppermute | solution.py:340
  27.3 1.9 %shard_map.136 = (bf16[320,2560]{1,0:T(8,128)(2,1)S(1)}, bf16[320,1920]{1,0:T(8,128)(2,1)S(1)}, bf16[320,640]{1,0:T(8,128)(2,1)S(1)}) custom-call(bf16[320,2560]{1,0:T(8,128)(2,1)} %bitcast.18, bf16[320,2560]{1,0:T(8,128)(2,1)} %bitcast.19, bf16[48,2560]{1,0:T(8,128)(2,1)S(1)} %get-tuple-element.48.rest_0_.mine_ref.after_ref), custom_call_target="tpu_custom_call" | custom-call | tf_op jit(solution)/shard_map/pallas_call | solution.py:140
  29.2 1.6 %collective-permute-start.22 = (bf16[320,1920]{1,0:T(8,128)(2,1)S(1)}, bf16[320,1920]{1,0:T(8,128)(2,1)S(1)}, u32[]{:S(2)}, u32[]{:S(2)}) collective-permute-start(bf16[320,1920]{1,0:T(8,128)(2,1)S(1)} %get-tuple-element.51), channel_id=1, source_target_pairs={{0,16},{16,0},{1,17},{17,1},{2,18},{18,2},{3,19},{19,3},{4,20},{20... | collective-permute-start | bytes 3686408 | tf_op jit(solution)/shard_map/ppermute | solution.py:348
  31.5 4.7 %collective-permute-start.11 = (bf16[48,2560]{1,0:T(8,128)(2,1)S(1)}, bf16[48,2560]{1,0:T(8,128)(2,1)S(1)}, u32[]{:S(2)}, u32[]{:S(2)}) collective-permute-start(bf16[48,2560]{1,0:T(8,128)(2,1)S(1)} %get-tuple-element.43), channel_id=1, source_target_pairs={{0,4},{12,8},{4,0},{8,12},{1,5},{13,9},{5,1},{9,13},{2,6},{14,10},... | collective-permute-start | bytes 737288 | tf_op jit(solution)/shard_map/ppermute | solution.py:340
  37.1 6.5 %collective-permute-start.10 = (bf16[48,2560]{1,0:T(8,128)(2,1)S(1)}, bf16[48,2560]{1,0:T(8,128)(2,1)S(1)}, u32[]{:S(2)}, u32[]{:S(2)}) collective-permute-start(bf16[48,2560]{1,0:T(8,128)(2,1)S(1)} %get-tuple-element.42), channel_id=1, source_target_pairs={{0,4},{12,8},{4,0},{8,12},{1,5},{13,9},{5,1},{9,13},{2,6},{14,10},... | collective-permute-start | bytes 737288 | tf_op jit(solution)/shard_map/ppermute | solution.py:340
  44.6 3.6 %collective-permute-start.16 = (bf16[48,2560]{1,0:T(8,128)(2,1)S(1)}, bf16[48,2560]{1,0:T(8,128)(2,1)S(1)}, u32[]{:S(2)}, u32[]{:S(2)}) collective-permute-start(bf16[48,2560]{1,0:T(8,128)(2,1)S(1)} %get-tuple-element.47), channel_id=1, source_target_pairs={{0,4},{12,8},{4,0},{8,12},{1,5},{13,9},{5,1},{9,13},{2,6},{14,10},... | collective-permute-start | bytes 737288 | tf_op jit(solution)/shard_map/ppermute | solution.py:340
  49.9 3.7 %collective-permute-done.16.came_ref = bf16[48,2560]{1,0:T(8,128)(2,1)S(1)} collective-permute-done((bf16[48,2560]{1,0:T(8,128)(2,1)S(1)}, bf16[48,2560]{1,0:T(8,128)(2,1)S(1)}, u32[]{:S(2)}, u32[]{:S(2)}) %collective-permute-start.16) | collective-permute-done | bytes 245792 | tf_op jit(solution)/shard_map/ppermute | solution.py:340
  53.6 1.7 %collective-permute-start.20 = (bf16[48,2560]{1,0:T(8,128)(2,1)S(1)}, bf16[48,2560]{1,0:T(8,128)(2,1)S(1)}, u32[]{:S(2)}, u32[]{:S(2)}) collective-permute-start(bf16[48,2560]{1,0:T(8,128)(2,1)S(1)} %get-tuple-element.50), channel_id=1, source_target_pairs={{0,4},{12,8},{4,0},{8,12},{1,5},{13,9},{5,1},{9,13},{2,6},{14,10},... | collective-permute-start | bytes 737288 | tf_op jit(solution)/shard_map/ppermute | solution.py:340
  56.2 1.3 %collective-permute-start.19 = (bf16[48,2560]{1,0:T(8,128)(2,1)S(1)}, bf16[48,2560]{1,0:T(8,128)(2,1)S(1)}, u32[]{:S(2)}, u32[]{:S(2)}) collective-permute-start(bf16[48,2560]{1,0:T(8,128)(2,1)S(1)} %shard_map.130.after_ref.mine_ref), channel_id=1, source_target_pairs={{4,0},{8,12},{5,1},{9,13},{6,2},{10,14},{7,3},{11,15},{20,16},{24,... | collective-permute-start | bytes 737288 | tf_op jit(solution)/shard_map/ppermute | solution.py:340
  57.5 3.1 %collective-permute-done.20.came_ref = bf16[48,2560]{1,0:T(8,128)(2,1)S(1)} collective-permute-done((bf16[48,2560]{1,0:T(8,128)(2,1)S(1)}, bf16[48,2560]{1,0:T(8,128)(2,1)S(1)}, u32[]{:S(2)}, u32[]{:S(2)}) %collective-permute-start.20) | collective-permute-done | bytes 245792 | tf_op jit(solution)/shard_map/ppermute | solution.py:340
  60.7 2.6 %collective-permute-start.25 = (bf16[48,2560]{1,0:T(8,128)(2,1)S(1)}, bf16[48,2560]{1,0:T(8,128)(2,1)S(1)}, u32[]{:S(2)}, u32[]{:S(2)}) collective-permute-start(bf16[48,2560]{1,0:T(8,128)(2,1)S(1)} %shard_map.132.after_ref.mine_ref), channel_id=1, source_target_pairs={{0,8},{4,12},{8,0},{12,4},{1,9},{5,13},{9,1},{13,5},{2,10},{6,14},... | collective-permute-start | bytes 737288 | tf_op jit(solution)/shard_map/ppermute | solution.py:371
  63.3 1.3 %collective-permute-start.24 = (bf16[48,2560]{1,0:T(8,128)(2,1)S(1)}, bf16[48,2560]{1,0:T(8,128)(2,1)S(1)}, u32[]{:S(2)}, u32[]{:S(2)}) collective-permute-start(bf16[48,2560]{1,0:T(8,128)(2,1)S(1)} %shard_map.133.after_ref.mine_ref), channel_id=1, source_target_pairs={{4,0},{8,12},{5,1},{9,13},{6,2},{10,14},{7,3},{11,15},{20,16},{24,... | collective-permute-start | bytes 737288 | tf_op jit(solution)/shard_map/ppermute | solution.py:340
  64.6 3.6 %collective-permute-done.19.came_ref = bf16[48,2560]{1,0:T(8,128)(2,1)S(1)} collective-permute-done((bf16[48,2560]{1,0:T(8,128)(2,1)S(1)}, bf16[48,2560]{1,0:T(8,128)(2,1)S(1)}, u32[]{:S(2)}, u32[]{:S(2)}) %collective-permute-start.19) | collective-permute-done | bytes 245792 | tf_op jit(solution)/shard_map/ppermute | solution.py:340
  68.3 1.0 shard_map.137.after_ref
  69.3 1.5 %collective-permute-start.26 = (bf16[288,320]{1,0:T(8,128)(2,1)S(1)}, bf16[288,320]{1,0:T(8,128)(2,1)S(1)}, u32[]{:S(2)}, u32[]{:S(2)}) collective-permute-start(bf16[288,320]{1,0:T(8,128)(2,1)S(1)} %shard_map.137.after_ref), channel_id=1, source_target_pairs={{0,16},{16,0},{1,17},{17,1},{2,18},{18,2},{3,19},{19,3},{4,20},{20... | collective-permute-start | bytes 552968 | tf_op jit(solution)/shard_map/ppermute | solution.py:355
  70.9 0.9 shard_map.138.after_ref.refs_0_
  71.8 4.0 %collective-permute-done.25.came_ref = bf16[48,2560]{1,0:T(8,128)(2,1)S(1)} collective-permute-done((bf16[48,2560]{1,0:T(8,128)(2,1)S(1)}, bf16[48,2560]{1,0:T(8,128)(2,1)S(1)}, u32[]{:S(2)}, u32[]{:S(2)}) %collective-permute-start.25) | collective-permute-done | bytes 245792 | tf_op jit(solution)/shard_map/ppermute | solution.py:371
  75.9 2.5 %collective-permute-done.24.came_ref = bf16[48,2560]{1,0:T(8,128)(2,1)S(1)} collective-permute-done((bf16[48,2560]{1,0:T(8,128)(2,1)S(1)}, bf16[48,2560]{1,0:T(8,128)(2,1)S(1)}, u32[]{:S(2)}, u32[]{:S(2)}) %collective-permute-start.24) | collective-permute-done | bytes 245792 | tf_op jit(solution)/shard_map/ppermute | solution.py:340
  80.3 3.2 %collective-permute-done.27.refs_3_ = bf16[96,320]{1,0:T(8,128)(2,1)S(1)} collective-permute-done((bf16[96,320]{1,0:T(8,128)(2,1)S(1)}, bf16[96,320]{1,0:T(8,128)(2,1)S(1)}, u32[]{:S(2)}, u32[]{:S(2)}) %collective-permute-start.27) | collective-permute-done | bytes 61472 | tf_op jit(solution)/shard_map/ppermute | solution.py:355
  84.4 1.2 %collective-permute-done.28 = f32[12,384]{1,0:T(8,128)S(1)} collective-permute-done((f32[12,384]{1,0:T(8,128)S(1)}, f32[12,384]{1,0:T(8,128)S(1)}, u32[]{:S(2)}, u32[]{:S(2)}) %collective-permute-start.28) | collective-permute-done | bytes 18464 | tf_op jit(solution)/shard_map/ppermute | solution.py:409
  85.6 1.5 %collective-permute-start.29 = (f32[12,384]{1,0:T(8,128)S(1)}, f32[12,384]{1,0:T(8,128)S(1)}, u32[]{:S(2)}, u32[]{:S(2)}) collective-permute-start(f32[12,384]{1,0:T(8,128)S(1)} %add.12), channel_id=1, source_target_pairs={{0,2},{1,3},{2,0},{3,1},{4,6},{5,7},{6,4},{7,5},{8,10},{9,11},{10,... | collective-permute-start | bytes 55304 | tf_op jit(solution)/shard_map/ppermute | solution.py:409
  87.0 2.3 %collective-permute-done.29 = f32[12,384]{1,0:T(8,128)S(1)} collective-permute-done((f32[12,384]{1,0:T(8,128)S(1)}, f32[12,384]{1,0:T(8,128)S(1)}, u32[]{:S(2)}, u32[]{:S(2)}) %collective-permute-start.29) | collective-permute-done | bytes 18464 | tf_op jit(solution)/shard_map/ppermute | solution.py:409
  89.6 2.3 %collective-permute-start.31 = (f32[1,96]{1,0:T(1,128)S(1)}, f32[1,96]{1,0:T(1,128)S(1)}, u32[]{:S(2)}, u32[]{:S(2)}) collective-permute-start(f32[1,96]{1,0:T(1,128)S(1)} %reshape.10), channel_id=1, source_target_pairs={{0,12},{4,8},{8,4},{12,0},{1,13},{5,9},{9,5},{13,1},{2,14},{6,10},... | collective-permute-start | bytes 1160 | tf_op jit(solution)/shard_map/ppermute | solution.py:419
  91.9 1.2 %collective-permute-start.32 = (f32[1,96]{1,0:T(1,128)S(1)}, f32[1,96]{1,0:T(1,128)S(1)}, u32[]{:S(2)}, u32[]{:S(2)}) collective-permute-start(f32[1,96]{1,0:T(1,128)S(1)} %reshape.10), channel_id=1, source_target_pairs={{0,8},{4,12},{8,0},{12,4},{1,9},{5,13},{9,1},{13,5},{2,10},{6,14},... | collective-permute-start | bytes 1160 | tf_op jit(solution)/shard_map/ppermute | solution.py:419
  93.2 1.9 %collective-permute-done.31 = f32[1,96]{1,0:T(1,128)S(1)} collective-permute-done((f32[1,96]{1,0:T(1,128)S(1)}, f32[1,96]{1,0:T(1,128)S(1)}, u32[]{:S(2)}, u32[]{:S(2)}) %collective-permute-start.31) | collective-permute-done | bytes 416 | tf_op jit(solution)/shard_map/ppermute | solution.py:419
  95.0 1.3 %collective-permute-done.32 = f32[1,96]{1,0:T(1,128)S(1)} collective-permute-done((f32[1,96]{1,0:T(1,128)S(1)}, f32[1,96]{1,0:T(1,128)S(1)}, u32[]{:S(2)}, u32[]{:S(2)}) %collective-permute-start.32) | collective-permute-done | bytes 416 | tf_op jit(solution)/shard_map/ppermute | solution.py:419
  (82 shorter events, 11.0 us)
Async XLA Ops:
  4.2 9.5 %collective-permute-start = (bf16[48,2560]{1,0:T(8,128)(2,1)S(1)}, bf16[48,2560]{1,0:T(8,128)(2,1)S(1)}, u32[]{:S(2)}, u32[]{:S(2)}) collective-permute-start(bf16[48,2560]{1,0:T(8,128)(2,1)S(1)} %get-tuple-element.33), channel_id=1, source_target_pairs={{0,4},{12,8},{4,0},{8,12},{1,5},{13,9},{5,1},{9,13},{2,6},{14,10},... | collective-permute-start | bytes 737288 | tf_op jit(solution)/shard_map/ppermute | solution.py:340
  8.9 12.2 %collective-permute-start.3 = (bf16[48,2560]{1,0:T(8,128)(2,1)S(1)}, bf16[48,2560]{1,0:T(8,128)(2,1)S(1)}, u32[]{:S(2)}, u32[]{:S(2)}) collective-permute-start(bf16[48,2560]{1,0:T(8,128)(2,1)S(1)} %get-tuple-element.36.mine_ref), channel_id=1, source_target_pairs={{0,4},{12,8},{1,5},{13,9},{2,6},{14,10},{3,7},{15,11},{16,20},{28,... | collective-permute-start | bytes 737288 | tf_op jit(solution)/shard_map/ppermute | solution.py:340
  13.8 7.3 %collective-permute-start.4 = (bf16[48,2560]{1,0:T(8,128)(2,1)S(1)}, bf16[48,2560]{1,0:T(8,128)(2,1)S(1)}, u32[]{:S(2)}, u32[]{:S(2)}) collective-permute-start(bf16[48,2560]{1,0:T(8,128)(2,1)S(1)} %get-tuple-element.35.after_ref.mine_ref), channel_id=1, source_target_pairs={{0,1},{1,0},{2,3},{3,2},{4,5},{5,4},{6,7},{7,6},{8,9},{9,8},{10,11... | collective-permute-start | bytes 737288 | tf_op jit(solution)/shard_map/ppermute | solution.py:389
  13.8 8.1 %collective-permute-start.2 = (bf16[48,2560]{1,0:T(8,128)(2,1)S(1)}, bf16[48,2560]{1,0:T(8,128)(2,1)S(1)}, u32[]{:S(2)}, u32[]{:S(2)}) collective-permute-start(bf16[48,2560]{1,0:T(8,128)(2,1)S(1)} %get-tuple-element.35.after_ref.mine_ref), channel_id=1, source_target_pairs={{4,8},{8,4},{5,9},{9,5},{6,10},{10,6},{7,11},{11,7},{20,24},{24,20... | collective-permute-start | bytes 737288 | tf_op jit(solution)/shard_map/ppermute | solution.py:340
  14.5 12.6 %collective-permute-start.1 = (bf16[48,2560]{1,0:T(8,128)(2,1)S(1)}, bf16[48,2560]{1,0:T(8,128)(2,1)S(1)}, u32[]{:S(2)}, u32[]{:S(2)}) collective-permute-start(bf16[48,2560]{1,0:T(8,128)(2,1)S(1)} %get-tuple-element.34), channel_id=1, source_target_pairs={{0,4},{12,8},{1,5},{13,9},{2,6},{14,10},{3,7},{15,11},{16,20},{28,... | collective-permute-start | bytes 737288 | tf_op jit(solution)/shard_map/ppermute | solution.py:340
  21.1 6.0 %collective-permute-start.5 = (bf16[48,2560]{1,0:T(8,128)(2,1)S(1)}, bf16[48,2560]{1,0:T(8,128)(2,1)S(1)}, u32[]{:S(2)}, u32[]{:S(2)}) collective-permute-start(bf16[48,2560]{1,0:T(8,128)(2,1)S(1)} %shard_map.116.after_ref.mine_ref), channel_id=1, source_target_pairs={{0,1},{1,0},{2,3},{3,2},{4,5},{5,4},{6,7},{7,6},{8,9},{9,8},{10,11... | collective-permute-start | bytes 737288 | tf_op jit(solution)/shard_map/ppermute | solution.py:389
  21.2 10.2 %collective-permute-start.8 = (bf16[48,2560]{1,0:T(8,128)(2,1)S(1)}, bf16[48,2560]{1,0:T(8,128)(2,1)S(1)}, u32[]{:S(2)}, u32[]{:S(2)}) collective-permute-start(bf16[48,2560]{1,0:T(8,128)(2,1)S(1)} %shard_map.116.after_ref.mine_ref), channel_id=1, source_target_pairs={{4,8},{8,4},{5,9},{9,5},{6,10},{10,6},{7,11},{11,7},{20,24},{24,20... | collective-permute-start | bytes 737288 | tf_op jit(solution)/shard_map/ppermute | solution.py:340
  22.0 14.2 %collective-permute-start.7 = (bf16[48,2560]{1,0:T(8,128)(2,1)S(1)}, bf16[48,2560]{1,0:T(8,128)(2,1)S(1)}, u32[]{:S(2)}, u32[]{:S(2)}) collective-permute-start(bf16[48,2560]{1,0:T(8,128)(2,1)S(1)} %get-tuple-element.39), channel_id=1, source_target_pairs={{0,4},{12,8},{4,0},{8,12},{1,5},{13,9},{5,1},{9,13},{2,6},{14,10},... | collective-permute-start | bytes 737288 | tf_op jit(solution)/shard_map/ppermute | solution.py:340
  27.2 9.0 %collective-permute-start.9 = (bf16[48,2560]{1,0:T(8,128)(2,1)S(1)}, bf16[48,2560]{1,0:T(8,128)(2,1)S(1)}, u32[]{:S(2)}, u32[]{:S(2)}) collective-permute-start(bf16[48,2560]{1,0:T(8,128)(2,1)S(1)} %shard_map.118.after_ref.mine_ref), channel_id=1, source_target_pairs={{0,1},{1,0},{2,3},{3,2},{4,5},{5,4},{6,7},{7,6},{8,9},{9,8},{10,11... | collective-permute-start | bytes 737288 | tf_op jit(solution)/shard_map/ppermute | solution.py:389
  29.2 39.2 %collective-permute-start.22 = (bf16[320,1920]{1,0:T(8,128)(2,1)S(1)}, bf16[320,1920]{1,0:T(8,128)(2,1)S(1)}, u32[]{:S(2)}, u32[]{:S(2)}) collective-permute-start(bf16[320,1920]{1,0:T(8,128)(2,1)S(1)} %get-tuple-element.51), channel_id=1, source_target_pairs={{0,16},{16,0},{1,17},{17,1},{2,18},{18,2},{3,19},{19,3},{4,20},{20... | collective-permute-start | bytes 3686408 | tf_op jit(solution)/shard_map/ppermute | solution.py:348
  30.8 6.3 %collective-permute-start.6 = (bf16[48,2560]{1,0:T(8,128)(2,1)S(1)}, bf16[48,2560]{1,0:T(8,128)(2,1)S(1)}, u32[]{:S(2)}, u32[]{:S(2)}) collective-permute-start(bf16[48,2560]{1,0:T(8,128)(2,1)S(1)} %shard_map.118.after_ref.mine_ref), channel_id=1, source_target_pairs={{4,8},{8,4},{5,9},{9,5},{6,10},{10,6},{7,11},{11,7},{20,24},{24,20... | collective-permute-start | bytes 737288 | tf_op jit(solution)/shard_map/ppermute | solution.py:340
  31.5 12.1 %collective-permute-start.11 = (bf16[48,2560]{1,0:T(8,128)(2,1)S(1)}, bf16[48,2560]{1,0:T(8,128)(2,1)S(1)}, u32[]{:S(2)}, u32[]{:S(2)}) collective-permute-start(bf16[48,2560]{1,0:T(8,128)(2,1)S(1)} %get-tuple-element.43), channel_id=1, source_target_pairs={{0,4},{12,8},{4,0},{8,12},{1,5},{13,9},{5,1},{9,13},{2,6},{14,10},... | collective-permute-start | bytes 737288 | tf_op jit(solution)/shard_map/ppermute | solution.py:340
  36.2 7.4 %collective-permute-start.13 = (bf16[48,2560]{1,0:T(8,128)(2,1)S(1)}, bf16[48,2560]{1,0:T(8,128)(2,1)S(1)}, u32[]{:S(2)}, u32[]{:S(2)}) collective-permute-start(bf16[48,2560]{1,0:T(8,128)(2,1)S(1)} %shard_map.120.after_ref.mine_ref), channel_id=1, source_target_pairs={{0,1},{1,0},{2,3},{3,2},{4,5},{5,4},{6,7},{7,6},{8,9},{9,8},{10,11... | collective-permute-start | bytes 737288 | tf_op jit(solution)/shard_map/ppermute | solution.py:389
  36.3 8.1 %collective-permute-start.12 = (bf16[48,2560]{1,0:T(8,128)(2,1)S(1)}, bf16[48,2560]{1,0:T(8,128)(2,1)S(1)}, u32[]{:S(2)}, u32[]{:S(2)}) collective-permute-start(bf16[48,2560]{1,0:T(8,128)(2,1)S(1)} %shard_map.120.after_ref.mine_ref), channel_id=1, source_target_pairs={{4,8},{8,4},{5,9},{9,5},{6,10},{10,6},{7,11},{11,7},{20,24},{24,20... | collective-permute-start | bytes 737288 | tf_op jit(solution)/shard_map/ppermute | solution.py:340
  37.1 11.2 %collective-permute-start.10 = (bf16[48,2560]{1,0:T(8,128)(2,1)S(1)}, bf16[48,2560]{1,0:T(8,128)(2,1)S(1)}, u32[]{:S(2)}, u32[]{:S(2)}) collective-permute-start(bf16[48,2560]{1,0:T(8,128)(2,1)S(1)} %get-tuple-element.42), channel_id=1, source_target_pairs={{0,4},{12,8},{4,0},{8,12},{1,5},{13,9},{5,1},{9,13},{2,6},{14,10},... | collective-permute-start | bytes 737288 | tf_op jit(solution)/shard_map/ppermute | solution.py:340
  43.7 4.6 %collective-permute-start.14 = (bf16[48,2560]{1,0:T(8,128)(2,1)S(1)}, bf16[48,2560]{1,0:T(8,128)(2,1)S(1)}, u32[]{:S(2)}, u32[]{:S(2)}) collective-permute-start(bf16[48,2560]{1,0:T(8,128)(2,1)S(1)} %shard_map.123.after_ref.mine_ref), channel_id=1, source_target_pairs={{0,1},{1,0},{2,3},{3,2},{4,5},{5,4},{6,7},{7,6},{8,9},{9,8},{10,11... | collective-permute-start | bytes 737288 | tf_op jit(solution)/shard_map/ppermute | solution.py:389
  43.8 5.4 %collective-permute-start.17 = (bf16[48,2560]{1,0:T(8,128)(2,1)S(1)}, bf16[48,2560]{1,0:T(8,128)(2,1)S(1)}, u32[]{:S(2)}, u32[]{:S(2)}) collective-permute-start(bf16[48,2560]{1,0:T(8,128)(2,1)S(1)} %shard_map.123.after_ref.mine_ref), channel_id=1, source_target_pairs={{4,8},{8,4},{5,9},{9,5},{6,10},{10,6},{7,11},{11,7},{20,24},{24,20... | collective-permute-start | bytes 737288 | tf_op jit(solution)/shard_map/ppermute | solution.py:340
  44.6 9.1 %collective-permute-start.16 = (bf16[48,2560]{1,0:T(8,128)(2,1)S(1)}, bf16[48,2560]{1,0:T(8,128)(2,1)S(1)}, u32[]{:S(2)}, u32[]{:S(2)}) collective-permute-start(bf16[48,2560]{1,0:T(8,128)(2,1)S(1)} %get-tuple-element.47), channel_id=1, source_target_pairs={{0,4},{12,8},{4,0},{8,12},{1,5},{13,9},{5,1},{9,13},{2,6},{14,10},... | collective-permute-start | bytes 737288 | tf_op jit(solution)/shard_map/ppermute | solution.py:340
  48.4 6.9 %collective-permute-start.18 = (bf16[48,2560]{1,0:T(8,128)(2,1)S(1)}, bf16[48,2560]{1,0:T(8,128)(2,1)S(1)}, u32[]{:S(2)}, u32[]{:S(2)}) collective-permute-start(bf16[48,2560]{1,0:T(8,128)(2,1)S(1)} %shard_map.126.after_ref.mine_ref), channel_id=1, source_target_pairs={{0,1},{1,0},{2,3},{3,2},{4,5},{5,4},{6,7},{7,6},{8,9},{9,8},{10,11... | collective-permute-start | bytes 737288 | tf_op jit(solution)/shard_map/ppermute | solution.py:389
  48.5 7.6 %collective-permute-start.15 = (bf16[48,2560]{1,0:T(8,128)(2,1)S(1)}, bf16[48,2560]{1,0:T(8,128)(2,1)S(1)}, u32[]{:S(2)}, u32[]{:S(2)}) collective-permute-start(bf16[48,2560]{1,0:T(8,128)(2,1)S(1)} %shard_map.126.after_ref.mine_ref), channel_id=1, source_target_pairs={{4,8},{8,4},{5,9},{9,5},{6,10},{10,6},{7,11},{11,7},{20,24},{24,20... | collective-permute-start | bytes 737288 | tf_op jit(solution)/shard_map/ppermute | solution.py:340
  49.2 19.1 %collective-permute-start.23 = (bf16[320,640]{1,0:T(8,128)(2,1)S(1)}, bf16[320,640]{1,0:T(8,128)(2,1)S(1)}, u32[]{:S(2)}, u32[]{:S(2)}) collective-permute-start(bf16[320,640]{1,0:T(8,128)(2,1)S(1)} %get-tuple-element.52), channel_id=1, source_target_pairs={{0,16},{16,0},{1,17},{17,1},{2,18},{18,2},{3,19},{19,3},{4,20},{20... | collective-permute-start | bytes 1228808 | tf_op jit(solution)/shard_map/ppermute | solution.py:348
  53.6 7.0 %collective-permute-start.20 = (bf16[48,2560]{1,0:T(8,128)(2,1)S(1)}, bf16[48,2560]{1,0:T(8,128)(2,1)S(1)}, u32[]{:S(2)}, u32[]{:S(2)}) collective-permute-start(bf16[48,2560]{1,0:T(8,128)(2,1)S(1)} %get-tuple-element.50), channel_id=1, source_target_pairs={{0,4},{12,8},{4,0},{8,12},{1,5},{13,9},{5,1},{9,13},{2,6},{14,10},... | collective-permute-start | bytes 737288 | tf_op jit(solution)/shard_map/ppermute | solution.py:340
  55.4 7.8 %collective-permute-start.21 = (bf16[48,2560]{1,0:T(8,128)(2,1)S(1)}, bf16[48,2560]{1,0:T(8,128)(2,1)S(1)}, u32[]{:S(2)}, u32[]{:S(2)}) collective-permute-start(bf16[48,2560]{1,0:T(8,128)(2,1)S(1)} %shard_map.129.after_ref.mine_ref), channel_id=1, source_target_pairs={{4,8},{8,4},{5,9},{9,5},{6,10},{10,6},{7,11},{11,7},{20,24},{24,20... | collective-permute-start | bytes 737288 | tf_op jit(solution)/shard_map/ppermute | solution.py:340
  56.2 12.1 %collective-permute-start.19 = (bf16[48,2560]{1,0:T(8,128)(2,1)S(1)}, bf16[48,2560]{1,0:T(8,128)(2,1)S(1)}, u32[]{:S(2)}, u32[]{:S(2)}) collective-permute-start(bf16[48,2560]{1,0:T(8,128)(2,1)S(1)} %shard_map.130.after_ref.mine_ref), channel_id=1, source_target_pairs={{4,0},{8,12},{5,1},{9,13},{6,2},{10,14},{7,3},{11,15},{20,16},{24,... | collective-permute-start | bytes 737288 | tf_op jit(solution)/shard_map/ppermute | solution.py:340
  60.7 15.1 %collective-permute-start.25 = (bf16[48,2560]{1,0:T(8,128)(2,1)S(1)}, bf16[48,2560]{1,0:T(8,128)(2,1)S(1)}, u32[]{:S(2)}, u32[]{:S(2)}) collective-permute-start(bf16[48,2560]{1,0:T(8,128)(2,1)S(1)} %shard_map.132.after_ref.mine_ref), channel_id=1, source_target_pairs={{0,8},{4,12},{8,0},{12,4},{1,9},{5,13},{9,1},{13,5},{2,10},{6,14},... | collective-permute-start | bytes 737288 | tf_op jit(solution)/shard_map/ppermute | solution.py:371
  63.3 15.0 %collective-permute-start.24 = (bf16[48,2560]{1,0:T(8,128)(2,1)S(1)}, bf16[48,2560]{1,0:T(8,128)(2,1)S(1)}, u32[]{:S(2)}, u32[]{:S(2)}) collective-permute-start(bf16[48,2560]{1,0:T(8,128)(2,1)S(1)} %shard_map.133.after_ref.mine_ref), channel_id=1, source_target_pairs={{4,0},{8,12},{5,1},{9,13},{6,2},{10,14},{7,3},{11,15},{20,16},{24,... | collective-permute-start | bytes 737288 | tf_op jit(solution)/shard_map/ppermute | solution.py:340
  69.3 11.0 %collective-permute-start.26 = (bf16[288,320]{1,0:T(8,128)(2,1)S(1)}, bf16[288,320]{1,0:T(8,128)(2,1)S(1)}, u32[]{:S(2)}, u32[]{:S(2)}) collective-permute-start(bf16[288,320]{1,0:T(8,128)(2,1)S(1)} %shard_map.137.after_ref), channel_id=1, source_target_pairs={{0,16},{16,0},{1,17},{17,1},{2,18},{18,2},{3,19},{19,3},{4,20},{20... | collective-permute-start | bytes 552968 | tf_op jit(solution)/shard_map/ppermute | solution.py:355
  79.1 4.4 %collective-permute-start.27 = (bf16[96,320]{1,0:T(8,128)(2,1)S(1)}, bf16[96,320]{1,0:T(8,128)(2,1)S(1)}, u32[]{:S(2)}, u32[]{:S(2)}) collective-permute-start(bf16[96,320]{1,0:T(8,128)(2,1)S(1)} %shard_map.141.after_ref), channel_id=1, source_target_pairs={{0,16},{16,0},{1,17},{17,1},{2,18},{18,2},{3,19},{19,3},{4,20},{20... | collective-permute-start | bytes 184328 | tf_op jit(solution)/shard_map/ppermute | solution.py:355
  85.6 3.8 %collective-permute-start.29 = (f32[12,384]{1,0:T(8,128)S(1)}, f32[12,384]{1,0:T(8,128)S(1)}, u32[]{:S(2)}, u32[]{:S(2)}) collective-permute-start(f32[12,384]{1,0:T(8,128)S(1)} %add.12), channel_id=1, source_target_pairs={{0,2},{1,3},{2,0},{3,1},{4,6},{5,7},{6,4},{7,5},{8,10},{9,11},{10,... | collective-permute-start | bytes 55304 | tf_op jit(solution)/shard_map/ppermute | solution.py:409
  89.6 3.6 %collective-permute-start.30 = (f32[1,96]{1,0:T(1,128)S(1)}, f32[1,96]{1,0:T(1,128)S(1)}, u32[]{:S(2)}, u32[]{:S(2)}) collective-permute-start(f32[1,96]{1,0:T(1,128)S(1)} %reshape.10), channel_id=1, source_target_pairs={{0,4},{4,0},{8,12},{12,8},{1,5},{5,1},{9,13},{13,9},{2,6},{6,2},{1... | collective-permute-start | bytes 1160 | tf_op jit(solution)/shard_map/ppermute | solution.py:419
  89.6 5.4 %collective-permute-start.31 = (f32[1,96]{1,0:T(1,128)S(1)}, f32[1,96]{1,0:T(1,128)S(1)}, u32[]{:S(2)}, u32[]{:S(2)}) collective-permute-start(f32[1,96]{1,0:T(1,128)S(1)} %reshape.10), channel_id=1, source_target_pairs={{0,12},{4,8},{8,4},{12,0},{1,13},{5,9},{9,5},{13,1},{2,14},{6,10},... | collective-permute-start | bytes 1160 | tf_op jit(solution)/shard_map/ppermute | solution.py:419
  91.9 4.4 %collective-permute-start.32 = (f32[1,96]{1,0:T(1,128)S(1)}, f32[1,96]{1,0:T(1,128)S(1)}, u32[]{:S(2)}, u32[]{:S(2)}) collective-permute-start(f32[1,96]{1,0:T(1,128)S(1)} %reshape.10), channel_id=1, source_target_pairs={{0,8},{4,12},{8,0},{12,4},{1,9},{5,13},{9,1},{13,5},{2,10},{6,14},... | collective-permute-start | bytes 1160 | tf_op jit(solution)/shard_map/ppermute | solution.py:419
  (6 other events, 55.7 us)

commit v16 on v14

--- a/solution.py
+++ b/solution.py
@@ -360,7 +360,10 @@
     for turn in range(turns):
         steps = [(s, turn - s) for s in range(last) if 0 <= turn - s < chunks]
         due = [c for c in range(chunks) if c + last + (c in swapped) == turn]
-        for s, c in steps + [(last, c) for c in due]:
+        order = steps + [(last, c) for c in due]
+        if short and turn == chunks - 1:
+            order = [(last, c) for c in due if c in swapped] + steps[::-1] + [(last, c) for c in due if c not in swapped]
+        for s, c in order:
             kind, hop = stages[s]
             if short and c == chunks - 1:
                 if s == 0:

time: 91 us -> 94.7 us (1.041)
  waiting for transfers between devices: 19.6 us -> 22.4 us
    ppermute x1, starting transfers between devices: 4.12 us -> 6.94 us  [per_device(): came[c] = lax.ppermute(part[c], 'dp', [(i, i ^ 2) for i in range(n)])]
    ppermute x2, starting transfers between devices: 5.53 us -> 3.16 us  [project_waiting(): back.append(lax.ppermute(away, 'parts', swap))]
    ppermute x1, waiting for transfers between devices: 0.01 us -> 1.89 us  [per_device(): came[c] = lax.ppermute(part[c], 'dp', [(i, i ^ 2) for i in range(n)])]
    ppermute x3, waiting for transfers between devices: 2.45 us -> 3.92 us  [per_device(): lax.ppermute(flat, 'dp', [(i, i ^ k ^ k >> 1) for i in range(n)])]
  transfers between devices with their start and end apart: 27 -> 27, of which waited for: 13 -> 12; matrix products, arithmetic and copies ran while one was open for 0% -> 0% of each run, Pallas kernels for 9% -> 8%
where the time goes in v16:
time: 94.7 us; the launch traced here: 94.4 us
  starting transfers between devices  57.6 us (61%)
  waiting for transfers between devices  22.4 us (24%)
  Pallas kernels  12.3 us (13%)
  between operations  1.07 us (1%)
    ppermute x17, starting transfers between devices, transfer(): return lax.ppermute(value, 'dp', pairs)  39.3 us
    ppermute x17, waiting for transfers between devices, transfer(): return lax.ppermute(value, 'dp', pairs)  10.7 us
    ppermute x1, starting transfers between devices, per_device(): came[c] = lax.ppermute(part[c], 'dp', [(i, i ^ 2) for i in range(n)])  6.94 us
    ppermute x3, starting transfers between devices, per_device(): lax.ppermute(flat, 'dp', [(i, i ^ k ^ k >> 1) for i in range(n)])  3.98 us
    ppermute x3, waiting for transfers between devices, per_device(): lax.ppermute(flat, 'dp', [(i, i ^ k ^ k >> 1) for i in range(n)])  3.92 us
    pallas_call x1, Pallas kernels, first_pull(): pl.pallas_call(first_pull_kernel, out_shape=[bf16(rows, features)] * 2 +...  3.6 us
    ppermute x2, waiting for transfers between devices, per_device(): lax.ppermute(scores, 'layer', [(i, i ^ step) for i in range(layers)])  3.52 us
    pallas_call x4, Pallas kernels, project(): pl.pallas_call(functools.partial(project_kernel, len(tokens)), out_shape=...  3.18 us
  transfers between devices with their start and end apart: 27, of which 12 were waited for; matrix products, arithmetic and copies ran while one was open for 0% of the time, Pallas kernels for 8%

profile of v16, /device:TPU:0, one launch (start us, length us, event | category | flops | bytes accessed | tf_op | source)
XLA Modules:
  0.0 94.4 jit_solution(17645385721000714149)
XLA Ops:
  0.6 3.6 %shard_map.113 = (bf16[48,2560]{1,0:T(8,128)(2,1)S(1)}, bf16[48,2560]{1,0:T(8,128)(2,1)S(1)}, bf16[2560,640]{1,0:T(8,128)(2,1)S(1)}, bf16[640,384]{1,0:T(8,128)(2,1)}, bf16[384,640]{1,0:T(8,128)(2,1)S(1)}) custom-call(bf16[2560,640]{1,0:T(8,128)(2,1)} %bitcast.16, bf16[2560,640]{1,0:T(8,128)(2,1)} %bitcast.17, bf16[640,384]{1,0:T(8,128)(2,1)} %bitcast.20, ...), custom_call_target="tpu_custom_call" | custom-call | tf_op jit(solution)/shard_map/pallas_call | solution.py:77
  4.2 3.1 %collective-permute-start = (bf16[48,2560]{1,0:T(8,128)(2,1)S(1)}, bf16[48,2560]{1,0:T(8,128)(2,1)S(1)}, u32[]{:S(2)}, u32[]{:S(2)}) collective-permute-start(bf16[48,2560]{1,0:T(8,128)(2,1)S(1)} %get-tuple-element.33), channel_id=1, source_target_pairs={{0,4},{12,8},{4,0},{8,12},{1,5},{13,9},{5,1},{9,13},{2,6},{14,10},... | collective-permute-start | bytes 737288 | tf_op jit(solution)/shard_map/ppermute | solution.py:338
  7.3 1.5 %shard_map.114 = (bf16[48,2560]{1,0:T(8,128)(2,1)S(1)}, bf16[48,2560]{1,0:T(8,128)(2,1)S(1)}, bf16[48,2560]{1,0:T(8,128)(2,1)S(1)}, bf16[48,2560]{1,0:T(8,128)(2...) custom-call(bf16[384,640]{1,0:T(8,128)(2,1)S(1)} %get-tuple-element.28.turned_ref,, ...), custom_call_target="tpu_custom_call" | custom-call | tf_op jit(solution)/shard_map/pallas_call | solution.py:101
  8.9 1.9 %collective-permute-start.3 = (bf16[48,2560]{1,0:T(8,128)(2,1)S(1)}, bf16[48,2560]{1,0:T(8,128)(2,1)S(1)}, u32[]{:S(2)}, u32[]{:S(2)}) collective-permute-start(bf16[48,2560]{1,0:T(8,128)(2,1)S(1)} %get-tuple-element.36.mine_ref), channel_id=1, source_target_pairs={{0,4},{12,8},{1,5},{13,9},{2,6},{14,10},{3,7},{15,11},{16,20},{28,... | collective-permute-start | bytes 737288 | tf_op jit(solution)/shard_map/ppermute | solution.py:338
  10.8 2.9 %collective-permute-done.came_ref.early_ref = bf16[48,2560]{1,0:T(8,128)(2,1)S(1)} collective-permute-done((bf16[48,2560]{1,0:T(8,128)(2,1)S(1)}, bf16[48,2560]{1,0:T(8,128)(2,1)S(1)}, u32[]{:S(2)}, u32[]{:S(2)}) %collective-permute-start) | collective-permute-done | bytes 245792 | tf_op jit(solution)/shard_map/ppermute | solution.py:338
  14.4 6.5 %collective-permute-start.1 = (bf16[48,2560]{1,0:T(8,128)(2,1)S(1)}, bf16[48,2560]{1,0:T(8,128)(2,1)S(1)}, u32[]{:S(2)}, u32[]{:S(2)}) collective-permute-start(bf16[48,2560]{1,0:T(8,128)(2,1)S(1)} %get-tuple-element.34), channel_id=1, source_target_pairs={{0,4},{12,8},{1,5},{13,9},{2,6},{14,10},{3,7},{15,11},{16,20},{28,... | collective-permute-start | bytes 737288 | tf_op jit(solution)/shard_map/ppermute | solution.py:338
  21.0 1.9 %shard_map.136 = (bf16[320,2560]{1,0:T(8,128)(2,1)S(1)}, bf16[320,1920]{1,0:T(8,128)(2,1)S(1)}, bf16[320,640]{1,0:T(8,128)(2,1)S(1)}) custom-call(bf16[320,2560]{1,0:T(8,128)(2,1)} %bitcast.18, bf16[320,2560]{1,0:T(8,128)(2,1)} %bitcast.19, bf16[48,2560]{1,0:T(8,128)(2,1)S(1)} %get-tuple-element.48.rest_0_.mine_ref.after_ref), custom_call_target="tpu_custom_call" | custom-call | tf_op jit(solution)/shard_map/pallas_call | solution.py:140
  22.9 1.6 %collective-permute-start.16 = (bf16[320,1920]{1,0:T(8,128)(2,1)S(1)}, bf16[320,1920]{1,0:T(8,128)(2,1)S(1)}, u32[]{:S(2)}, u32[]{:S(2)}) collective-permute-start(bf16[320,1920]{1,0:T(8,128)(2,1)S(1)} %get-tuple-element.51), channel_id=1, source_target_pairs={{0,16},{16,0},{1,17},{17,1},{2,18},{18,2},{3,19},{19,3},{4,20},{20... | collective-permute-start | bytes 3686408 | tf_op jit(solution)/shard_map/ppermute | solution.py:346
  25.3 1.8 %collective-permute-start.5 = (bf16[48,2560]{1,0:T(8,128)(2,1)S(1)}, bf16[48,2560]{1,0:T(8,128)(2,1)S(1)}, u32[]{:S(2)}, u32[]{:S(2)}) collective-permute-start(bf16[48,2560]{1,0:T(8,128)(2,1)S(1)} %get-tuple-element.39), channel_id=1, source_target_pairs={{0,4},{12,8},{4,0},{8,12},{1,5},{13,9},{5,1},{9,13},{2,6},{14,10},... | collective-permute-start | bytes 737288 | tf_op jit(solution)/shard_map/ppermute | solution.py:338
  28.0 6.8 %collective-permute-start.8 = (bf16[48,2560]{1,0:T(8,128)(2,1)S(1)}, bf16[48,2560]{1,0:T(8,128)(2,1)S(1)}, u32[]{:S(2)}, u32[]{:S(2)}) collective-permute-start(bf16[48,2560]{1,0:T(8,128)(2,1)S(1)} %get-tuple-element.43), channel_id=1, source_target_pairs={{0,4},{12,8},{4,0},{8,12},{1,5},{13,9},{5,1},{9,13},{2,6},{14,10},... | collective-permute-start | bytes 737288 | tf_op jit(solution)/shard_map/ppermute | solution.py:338
  35.6 4.4 %collective-permute-start.7 = (bf16[48,2560]{1,0:T(8,128)(2,1)S(1)}, bf16[48,2560]{1,0:T(8,128)(2,1)S(1)}, u32[]{:S(2)}, u32[]{:S(2)}) collective-permute-start(bf16[48,2560]{1,0:T(8,128)(2,1)S(1)} %get-tuple-element.42), channel_id=1, source_target_pairs={{0,4},{12,8},{4,0},{8,12},{1,5},{13,9},{5,1},{9,13},{2,6},{14,10},... | collective-permute-start | bytes 737288 | tf_op jit(solution)/shard_map/ppermute | solution.py:338
  40.0 0.9 collective-permute-done.8.came_ref
  41.8 3.7 %collective-permute-start.11 = (bf16[48,2560]{1,0:T(8,128)(2,1)S(1)}, bf16[48,2560]{1,0:T(8,128)(2,1)S(1)}, u32[]{:S(2)}, u32[]{:S(2)}) collective-permute-start(bf16[48,2560]{1,0:T(8,128)(2,1)S(1)} %get-tuple-element.47), channel_id=1, source_target_pairs={{0,4},{12,8},{4,0},{8,12},{1,5},{13,9},{5,1},{9,13},{2,6},{14,10},... | collective-permute-start | bytes 737288 | tf_op jit(solution)/shard_map/ppermute | solution.py:338
  47.0 1.1 %collective-permute-start.17 = (bf16[320,640]{1,0:T(8,128)(2,1)S(1)}, bf16[320,640]{1,0:T(8,128)(2,1)S(1)}, u32[]{:S(2)}, u32[]{:S(2)}) collective-permute-start(bf16[320,640]{1,0:T(8,128)(2,1)S(1)} %get-tuple-element.52), channel_id=1, source_target_pairs={{0,16},{16,0},{1,17},{17,1},{2,18},{18,2},{3,19},{19,3},{4,20},{20... | collective-permute-start | bytes 1228808 | tf_op jit(solution)/shard_map/ppermute | solution.py:346
  48.2 3.7 %collective-permute-start.14 = (bf16[48,2560]{1,0:T(8,128)(2,1)S(1)}, bf16[48,2560]{1,0:T(8,128)(2,1)S(1)}, u32[]{:S(2)}, u32[]{:S(2)}) collective-permute-start(bf16[48,2560]{1,0:T(8,128)(2,1)S(1)} %get-tuple-element.50), channel_id=1, source_target_pairs={{0,4},{12,8},{4,0},{8,12},{1,5},{13,9},{5,1},{9,13},{2,6},{14,10},... | collective-permute-start | bytes 737288 | tf_op jit(solution)/shard_map/ppermute | solution.py:338
  52.8 1.3 %collective-permute-start.13 = (bf16[48,2560]{1,0:T(8,128)(2,1)S(1)}, bf16[48,2560]{1,0:T(8,128)(2,1)S(1)}, u32[]{:S(2)}, u32[]{:S(2)}) collective-permute-start(bf16[48,2560]{1,0:T(8,128)(2,1)S(1)} %shard_map.130.after_ref.mine_ref), channel_id=1, source_target_pairs={{4,0},{8,12},{5,1},{9,13},{6,2},{10,14},{7,3},{11,15},{20,16},{24,... | collective-permute-start | bytes 737288 | tf_op jit(solution)/shard_map/ppermute | solution.py:338
  54.1 4.7 %collective-permute-done.14.came_ref = bf16[48,2560]{1,0:T(8,128)(2,1)S(1)} collective-permute-done((bf16[48,2560]{1,0:T(8,128)(2,1)S(1)}, bf16[48,2560]{1,0:T(8,128)(2,1)S(1)}, u32[]{:S(2)}, u32[]{:S(2)}) %collective-permute-start.14) | collective-permute-done | bytes 245792 | tf_op jit(solution)/shard_map/ppermute | solution.py:338
  59.1 6.9 %collective-permute-start.19 = (bf16[48,2560]{1,0:T(8,128)(2,1)S(1)}, bf16[48,2560]{1,0:T(8,128)(2,1)S(1)}, u32[]{:S(2)}, u32[]{:S(2)}) collective-permute-start(bf16[48,2560]{1,0:T(8,128)(2,1)S(1)} %shard_map.134.after_ref.mine_ref), channel_id=1, source_target_pairs={{0,8},{4,12},{8,0},{12,4},{1,9},{5,13},{9,1},{13,5},{2,10},{6,14},... | collective-permute-start | bytes 737288 | tf_op jit(solution)/shard_map/ppermute | solution.py:371
  66.0 1.3 %collective-permute-start.18 = (bf16[48,2560]{1,0:T(8,128)(2,1)S(1)}, bf16[48,2560]{1,0:T(8,128)(2,1)S(1)}, u32[]{:S(2)}, u32[]{:S(2)}) collective-permute-start(bf16[48,2560]{1,0:T(8,128)(2,1)S(1)} %shard_map.133.after_ref.mine_ref), channel_id=1, source_target_pairs={{4,0},{8,12},{5,1},{9,13},{6,2},{10,14},{7,3},{11,15},{20,16},{24,... | collective-permute-start | bytes 737288 | tf_op jit(solution)/shard_map/ppermute | solution.py:338
  67.4 1.0 %shard_map.137.after_ref = bf16[288,320]{1,0:T(8,128)(2,1)S(1)} custom-call(bf16[48,2560]{1,0:T(8,128)(2,1)S(1)} %shard_map.135.after_ref.rest_7_.rest_6_, bf16[320,1920]{1,0:T(8,128)(2,1)S(1)} %collective-permute-done.16.rest_0_, bf16[320,640]{1,0:T(8,128)(2,1)S(1)} %collective-permute-done.17.rest_1_, ...), custom_call_target="tpu_custom_call" | custom-call | tf_op jit(solution)/shard_map/pallas_call | solution.py:241
  68.3 1.7 %collective-permute-start.20 = (bf16[288,320]{1,0:T(8,128)(2,1)S(1)}, bf16[288,320]{1,0:T(8,128)(2,1)S(1)}, u32[]{:S(2)}, u32[]{:S(2)}) collective-permute-start(bf16[288,320]{1,0:T(8,128)(2,1)S(1)} %shard_map.137.after_ref), channel_id=1, source_target_pairs={{0,16},{16,0},{1,17},{17,1},{2,18},{18,2},{3,19},{19,3},{4,20},{20... | collective-permute-start | bytes 552968 | tf_op jit(solution)/shard_map/ppermute | solution.py:353
  70.1 0.9 shard_map.138.after_ref.refs_0_
  71.0 1.9 %collective-permute-done.19.came_ref = bf16[48,2560]{1,0:T(8,128)(2,1)S(1)} collective-permute-done((bf16[48,2560]{1,0:T(8,128)(2,1)S(1)}, bf16[48,2560]{1,0:T(8,128)(2,1)S(1)}, u32[]{:S(2)}, u32[]{:S(2)}) %collective-permute-start.19) | collective-permute-done | bytes 245792 | tf_op jit(solution)/shard_map/ppermute | solution.py:371
  73.0 1.4 %collective-permute-done.18.came_ref = bf16[48,2560]{1,0:T(8,128)(2,1)S(1)} collective-permute-done((bf16[48,2560]{1,0:T(8,128)(2,1)S(1)}, bf16[48,2560]{1,0:T(8,128)(2,1)S(1)}, u32[]{:S(2)}, u32[]{:S(2)}) %collective-permute-start.18) | collective-permute-done | bytes 245792 | tf_op jit(solution)/shard_map/ppermute | solution.py:338
  75.1 1.4 %collective-permute-start.21 = (bf16[96,320]{1,0:T(8,128)(2,1)S(1)}, bf16[96,320]{1,0:T(8,128)(2,1)S(1)}, u32[]{:S(2)}, u32[]{:S(2)}) collective-permute-start(bf16[96,320]{1,0:T(8,128)(2,1)S(1)} %shard_map.141.after_ref), channel_id=1, source_target_pairs={{0,16},{16,0},{1,17},{17,1},{2,18},{18,2},{3,19},{19,3},{4,20},{20... | collective-permute-start | bytes 184328 | tf_op jit(solution)/shard_map/ppermute | solution.py:353
  77.2 2.3 %collective-permute-done.21.refs_3_ = bf16[96,320]{1,0:T(8,128)(2,1)S(1)} collective-permute-done((bf16[96,320]{1,0:T(8,128)(2,1)S(1)}, bf16[96,320]{1,0:T(8,128)(2,1)S(1)}, u32[]{:S(2)}, u32[]{:S(2)}) %collective-permute-start.21) | collective-permute-done | bytes 61472 | tf_op jit(solution)/shard_map/ppermute | solution.py:353
  80.4 1.2 %collective-permute-done.22 = f32[12,384]{1,0:T(8,128)S(1)} collective-permute-done((f32[12,384]{1,0:T(8,128)S(1)}, f32[12,384]{1,0:T(8,128)S(1)}, u32[]{:S(2)}, u32[]{:S(2)}) %collective-permute-start.22) | collective-permute-done | bytes 18464 | tf_op jit(solution)/shard_map/ppermute | solution.py:407
  81.6 1.5 %collective-permute-start.23 = (f32[12,384]{1,0:T(8,128)S(1)}, f32[12,384]{1,0:T(8,128)S(1)}, u32[]{:S(2)}, u32[]{:S(2)}) collective-permute-start(f32[12,384]{1,0:T(8,128)S(1)} %add.12), channel_id=1, source_target_pairs={{0,2},{1,3},{2,0},{3,1},{4,6},{5,7},{6,4},{7,5},{8,10},{9,11},{10,... | collective-permute-start | bytes 55304 | tf_op jit(solution)/shard_map/ppermute | solution.py:407
  83.1 2.3 %collective-permute-done.23 = f32[12,384]{1,0:T(8,128)S(1)} collective-permute-done((f32[12,384]{1,0:T(8,128)S(1)}, f32[12,384]{1,0:T(8,128)S(1)}, u32[]{:S(2)}, u32[]{:S(2)}) %collective-permute-start.23) | collective-permute-done | bytes 18464 | tf_op jit(solution)/shard_map/ppermute | solution.py:407
  85.7 3.4 %collective-permute-start.25 = (f32[1,96]{1,0:T(1,128)S(1)}, f32[1,96]{1,0:T(1,128)S(1)}, u32[]{:S(2)}, u32[]{:S(2)}) collective-permute-start(f32[1,96]{1,0:T(1,128)S(1)} %reshape.10), channel_id=1, source_target_pairs={{0,12},{4,8},{8,4},{12,0},{1,13},{5,9},{9,5},{13,1},{2,14},{6,10},... | collective-permute-start | bytes 1160 | tf_op jit(solution)/shard_map/ppermute | solution.py:417
  89.7 1.5 %collective-permute-done.25 = f32[1,96]{1,0:T(1,128)S(1)} collective-permute-done((f32[1,96]{1,0:T(1,128)S(1)}, f32[1,96]{1,0:T(1,128)S(1)}, u32[]{:S(2)}, u32[]{:S(2)}) %collective-permute-start.25) | collective-permute-done | bytes 416 | tf_op jit(solution)/shard_map/ppermute | solution.py:417
  91.1 2.5 %collective-permute-done.26 = f32[1,96]{1,0:T(1,128)S(1)} collective-permute-done((f32[1,96]{1,0:T(1,128)S(1)}, f32[1,96]{1,0:T(1,128)S(1)}, u32[]{:S(2)}, u32[]{:S(2)}) %collective-permute-start.26) | collective-permute-done | bytes 416 | tf_op jit(solution)/shard_map/ppermute | solution.py:417
  (70 shorter events, 10.5 us)
Async XLA Ops:
  4.2 9.5 %collective-permute-start = (bf16[48,2560]{1,0:T(8,128)(2,1)S(1)}, bf16[48,2560]{1,0:T(8,128)(2,1)S(1)}, u32[]{:S(2)}, u32[]{:S(2)}) collective-permute-start(bf16[48,2560]{1,0:T(8,128)(2,1)S(1)} %get-tuple-element.33), channel_id=1, source_target_pairs={{0,4},{12,8},{4,0},{8,12},{1,5},{13,9},{5,1},{9,13},{2,6},{14,10},... | collective-permute-start | bytes 737288 | tf_op jit(solution)/shard_map/ppermute | solution.py:338
  8.9 15.6 %collective-permute-start.3 = (bf16[48,2560]{1,0:T(8,128)(2,1)S(1)}, bf16[48,2560]{1,0:T(8,128)(2,1)S(1)}, u32[]{:S(2)}, u32[]{:S(2)}) collective-permute-start(bf16[48,2560]{1,0:T(8,128)(2,1)S(1)} %get-tuple-element.36.mine_ref), channel_id=1, source_target_pairs={{0,4},{12,8},{1,5},{13,9},{2,6},{14,10},{3,7},{15,11},{16,20},{28,... | collective-permute-start | bytes 737288 | tf_op jit(solution)/shard_map/ppermute | solution.py:338
  13.8 11.5 %collective-permute-start.2 = (bf16[48,2560]{1,0:T(8,128)(2,1)S(1)}, bf16[48,2560]{1,0:T(8,128)(2,1)S(1)}, u32[]{:S(2)}, u32[]{:S(2)}) collective-permute-start(bf16[48,2560]{1,0:T(8,128)(2,1)S(1)} %get-tuple-element.35.after_ref.mine_ref), channel_id=1, source_target_pairs={{4,8},{8,4},{5,9},{9,5},{6,10},{10,6},{7,11},{11,7},{20,24},{24,20... | collective-permute-start | bytes 737288 | tf_op jit(solution)/shard_map/ppermute | solution.py:338
  14.4 12.7 %collective-permute-start.1 = (bf16[48,2560]{1,0:T(8,128)(2,1)S(1)}, bf16[48,2560]{1,0:T(8,128)(2,1)S(1)}, u32[]{:S(2)}, u32[]{:S(2)}) collective-permute-start(bf16[48,2560]{1,0:T(8,128)(2,1)S(1)} %get-tuple-element.34), channel_id=1, source_target_pairs={{0,4},{12,8},{1,5},{13,9},{2,6},{14,10},{3,7},{15,11},{16,20},{28,... | collective-permute-start | bytes 737288 | tf_op jit(solution)/shard_map/ppermute | solution.py:338
  22.9 44.5 %collective-permute-start.16 = (bf16[320,1920]{1,0:T(8,128)(2,1)S(1)}, bf16[320,1920]{1,0:T(8,128)(2,1)S(1)}, u32[]{:S(2)}, u32[]{:S(2)}) collective-permute-start(bf16[320,1920]{1,0:T(8,128)(2,1)S(1)} %get-tuple-element.51), channel_id=1, source_target_pairs={{0,16},{16,0},{1,17},{17,1},{2,18},{18,2},{3,19},{19,3},{4,20},{20... | collective-permute-start | bytes 3686408 | tf_op jit(solution)/shard_map/ppermute | solution.py:346
  24.5 3.3 %collective-permute-start.6 = (bf16[48,2560]{1,0:T(8,128)(2,1)S(1)}, bf16[48,2560]{1,0:T(8,128)(2,1)S(1)}, u32[]{:S(2)}, u32[]{:S(2)}) collective-permute-start(bf16[48,2560]{1,0:T(8,128)(2,1)S(1)} %shard_map.116.after_ref.mine_ref), channel_id=1, source_target_pairs={{4,8},{8,4},{5,9},{9,5},{6,10},{10,6},{7,11},{11,7},{20,24},{24,20... | collective-permute-start | bytes 737288 | tf_op jit(solution)/shard_map/ppermute | solution.py:338
  25.3 9.5 %collective-permute-start.5 = (bf16[48,2560]{1,0:T(8,128)(2,1)S(1)}, bf16[48,2560]{1,0:T(8,128)(2,1)S(1)}, u32[]{:S(2)}, u32[]{:S(2)}) collective-permute-start(bf16[48,2560]{1,0:T(8,128)(2,1)S(1)} %get-tuple-element.39), channel_id=1, source_target_pairs={{0,4},{12,8},{4,0},{8,12},{1,5},{13,9},{5,1},{9,13},{2,6},{14,10},... | collective-permute-start | bytes 737288 | tf_op jit(solution)/shard_map/ppermute | solution.py:338
  27.2 8.4 %collective-permute-start.4 = (bf16[48,2560]{1,0:T(8,128)(2,1)S(1)}, bf16[48,2560]{1,0:T(8,128)(2,1)S(1)}, u32[]{:S(2)}, u32[]{:S(2)}) collective-permute-start(bf16[48,2560]{1,0:T(8,128)(2,1)S(1)} %shard_map.118.after_ref.mine_ref), channel_id=1, source_target_pairs={{4,8},{8,4},{5,9},{9,5},{6,10},{10,6},{7,11},{11,7},{20,24},{24,20... | collective-permute-start | bytes 737288 | tf_op jit(solution)/shard_map/ppermute | solution.py:338
  28.0 13.0 %collective-permute-start.8 = (bf16[48,2560]{1,0:T(8,128)(2,1)S(1)}, bf16[48,2560]{1,0:T(8,128)(2,1)S(1)}, u32[]{:S(2)}, u32[]{:S(2)}) collective-permute-start(bf16[48,2560]{1,0:T(8,128)(2,1)S(1)} %get-tuple-element.43), channel_id=1, source_target_pairs={{0,4},{12,8},{4,0},{8,12},{1,5},{13,9},{5,1},{9,13},{2,6},{14,10},... | collective-permute-start | bytes 737288 | tf_op jit(solution)/shard_map/ppermute | solution.py:338
  34.9 6.8 %collective-permute-start.9 = (bf16[48,2560]{1,0:T(8,128)(2,1)S(1)}, bf16[48,2560]{1,0:T(8,128)(2,1)S(1)}, u32[]{:S(2)}, u32[]{:S(2)}) collective-permute-start(bf16[48,2560]{1,0:T(8,128)(2,1)S(1)} %shard_map.120.after_ref.mine_ref), channel_id=1, source_target_pairs={{4,8},{8,4},{5,9},{9,5},{6,10},{10,6},{7,11},{11,7},{20,24},{24,20... | collective-permute-start | bytes 737288 | tf_op jit(solution)/shard_map/ppermute | solution.py:338
  35.6 10.6 %collective-permute-start.7 = (bf16[48,2560]{1,0:T(8,128)(2,1)S(1)}, bf16[48,2560]{1,0:T(8,128)(2,1)S(1)}, u32[]{:S(2)}, u32[]{:S(2)}) collective-permute-start(bf16[48,2560]{1,0:T(8,128)(2,1)S(1)} %get-tuple-element.42), channel_id=1, source_target_pairs={{0,4},{12,8},{4,0},{8,12},{1,5},{13,9},{5,1},{9,13},{2,6},{14,10},... | collective-permute-start | bytes 737288 | tf_op jit(solution)/shard_map/ppermute | solution.py:338
  41.0 7.1 %collective-permute-start.12 = (bf16[48,2560]{1,0:T(8,128)(2,1)S(1)}, bf16[48,2560]{1,0:T(8,128)(2,1)S(1)}, u32[]{:S(2)}, u32[]{:S(2)}) collective-permute-start(bf16[48,2560]{1,0:T(8,128)(2,1)S(1)} %shard_map.123.after_ref.mine_ref), channel_id=1, source_target_pairs={{4,8},{8,4},{5,9},{9,5},{6,10},{10,6},{7,11},{11,7},{20,24},{24,20... | collective-permute-start | bytes 737288 | tf_op jit(solution)/shard_map/ppermute | solution.py:338
  41.8 10.2 %collective-permute-start.11 = (bf16[48,2560]{1,0:T(8,128)(2,1)S(1)}, bf16[48,2560]{1,0:T(8,128)(2,1)S(1)}, u32[]{:S(2)}, u32[]{:S(2)}) collective-permute-start(bf16[48,2560]{1,0:T(8,128)(2,1)S(1)} %get-tuple-element.47), channel_id=1, source_target_pairs={{0,4},{12,8},{4,0},{8,12},{1,5},{13,9},{5,1},{9,13},{2,6},{14,10},... | collective-permute-start | bytes 737288 | tf_op jit(solution)/shard_map/ppermute | solution.py:338
  46.3 6.5 %collective-permute-start.10 = (bf16[48,2560]{1,0:T(8,128)(2,1)S(1)}, bf16[48,2560]{1,0:T(8,128)(2,1)S(1)}, u32[]{:S(2)}, u32[]{:S(2)}) collective-permute-start(bf16[48,2560]{1,0:T(8,128)(2,1)S(1)} %shard_map.126.after_ref.mine_ref), channel_id=1, source_target_pairs={{4,8},{8,4},{5,9},{9,5},{6,10},{10,6},{7,11},{11,7},{20,24},{24,20... | collective-permute-start | bytes 737288 | tf_op jit(solution)/shard_map/ppermute | solution.py:338
  47.0 20.4 %collective-permute-start.17 = (bf16[320,640]{1,0:T(8,128)(2,1)S(1)}, bf16[320,640]{1,0:T(8,128)(2,1)S(1)}, u32[]{:S(2)}, u32[]{:S(2)}) collective-permute-start(bf16[320,640]{1,0:T(8,128)(2,1)S(1)} %get-tuple-element.52), channel_id=1, source_target_pairs={{0,16},{16,0},{1,17},{17,1},{2,18},{18,2},{3,19},{19,3},{4,20},{20... | collective-permute-start | bytes 1228808 | tf_op jit(solution)/shard_map/ppermute | solution.py:346
  48.2 10.7 %collective-permute-start.14 = (bf16[48,2560]{1,0:T(8,128)(2,1)S(1)}, bf16[48,2560]{1,0:T(8,128)(2,1)S(1)}, u32[]{:S(2)}, u32[]{:S(2)}) collective-permute-start(bf16[48,2560]{1,0:T(8,128)(2,1)S(1)} %get-tuple-element.50), channel_id=1, source_target_pairs={{0,4},{12,8},{4,0},{8,12},{1,5},{13,9},{5,1},{9,13},{2,6},{14,10},... | collective-permute-start | bytes 737288 | tf_op jit(solution)/shard_map/ppermute | solution.py:338
  52.0 6.9 %collective-permute-start.15 = (bf16[48,2560]{1,0:T(8,128)(2,1)S(1)}, bf16[48,2560]{1,0:T(8,128)(2,1)S(1)}, u32[]{:S(2)}, u32[]{:S(2)}) collective-permute-start(bf16[48,2560]{1,0:T(8,128)(2,1)S(1)} %shard_map.129.after_ref.mine_ref), channel_id=1, source_target_pairs={{4,8},{8,4},{5,9},{9,5},{6,10},{10,6},{7,11},{11,7},{20,24},{24,20... | collective-permute-start | bytes 737288 | tf_op jit(solution)/shard_map/ppermute | solution.py:338
  52.8 14.5 %collective-permute-start.13 = (bf16[48,2560]{1,0:T(8,128)(2,1)S(1)}, bf16[48,2560]{1,0:T(8,128)(2,1)S(1)}, u32[]{:S(2)}, u32[]{:S(2)}) collective-permute-start(bf16[48,2560]{1,0:T(8,128)(2,1)S(1)} %shard_map.130.after_ref.mine_ref), channel_id=1, source_target_pairs={{4,0},{8,12},{5,1},{9,13},{6,2},{10,14},{7,3},{11,15},{20,16},{24,... | collective-permute-start | bytes 737288 | tf_op jit(solution)/shard_map/ppermute | solution.py:338
  59.1 13.9 %collective-permute-start.19 = (bf16[48,2560]{1,0:T(8,128)(2,1)S(1)}, bf16[48,2560]{1,0:T(8,128)(2,1)S(1)}, u32[]{:S(2)}, u32[]{:S(2)}) collective-permute-start(bf16[48,2560]{1,0:T(8,128)(2,1)S(1)} %shard_map.134.after_ref.mine_ref), channel_id=1, source_target_pairs={{0,8},{4,12},{8,0},{12,4},{1,9},{5,13},{9,1},{13,5},{2,10},{6,14},... | collective-permute-start | bytes 737288 | tf_op jit(solution)/shard_map/ppermute | solution.py:371
  66.0 8.4 %collective-permute-start.18 = (bf16[48,2560]{1,0:T(8,128)(2,1)S(1)}, bf16[48,2560]{1,0:T(8,128)(2,1)S(1)}, u32[]{:S(2)}, u32[]{:S(2)}) collective-permute-start(bf16[48,2560]{1,0:T(8,128)(2,1)S(1)} %shard_map.133.after_ref.mine_ref), channel_id=1, source_target_pairs={{4,0},{8,12},{5,1},{9,13},{6,2},{10,14},{7,3},{11,15},{20,16},{24,... | collective-permute-start | bytes 737288 | tf_op jit(solution)/shard_map/ppermute | solution.py:338
  68.3 8.9 %collective-permute-start.20 = (bf16[288,320]{1,0:T(8,128)(2,1)S(1)}, bf16[288,320]{1,0:T(8,128)(2,1)S(1)}, u32[]{:S(2)}, u32[]{:S(2)}) collective-permute-start(bf16[288,320]{1,0:T(8,128)(2,1)S(1)} %shard_map.137.after_ref), channel_id=1, source_target_pairs={{0,16},{16,0},{1,17},{17,1},{2,18},{18,2},{3,19},{19,3},{4,20},{20... | collective-permute-start | bytes 552968 | tf_op jit(solution)/shard_map/ppermute | solution.py:353
  75.1 4.5 %copy-start = (s32[1,8]{1,0:T(1,128)S(1)}, s32[1,8]{1,0:T(1,128)}, u32[]{:S(2)}) copy-start(s32[1,8]{1,0:T(1,128)} %counts_ref.1) | copy-start | bytes 100
  75.1 14.5 %copy-start.2 = (s32[128]{0:T(128)S(1)}, s32[128]{0:T(128)}, u32[]{:S(2)}) copy-start(s32[128]{0:T(128)} %param.19) | copy-start | bytes 1540
  75.1 14.5 %copy-start.3 = (s32[128]{0:T(128)S(1)}, s32[128]{0:T(128)}, u32[]{:S(2)}) copy-start(s32[128]{0:T(128)} %param.17) | copy-start | bytes 1540
  75.1 14.5 %copy-start.4 = (s32[128,1]{0,1:T(1,128)S(1)}, s32[128,1]{0,1:T(1,128)}, u32[]{:S(2)}) copy-start(s32[128,1]{0,1:T(1,128)} %param.18) | copy-start | bytes 1540
  75.1 4.4 %collective-permute-start.21 = (bf16[96,320]{1,0:T(8,128)(2,1)S(1)}, bf16[96,320]{1,0:T(8,128)(2,1)S(1)}, u32[]{:S(2)}, u32[]{:S(2)}) collective-permute-start(bf16[96,320]{1,0:T(8,128)(2,1)S(1)} %shard_map.141.after_ref), channel_id=1, source_target_pairs={{0,16},{16,0},{1,17},{17,1},{2,18},{18,2},{3,19},{19,3},{4,20},{20... | collective-permute-start | bytes 184328 | tf_op jit(solution)/shard_map/ppermute | solution.py:353
  80.4 1.2 %collective-permute-start.22 = (f32[12,384]{1,0:T(8,128)S(1)}, f32[12,384]{1,0:T(8,128)S(1)}, u32[]{:S(2)}, u32[]{:S(2)}) collective-permute-start(f32[12,384]{1,0:T(8,128)S(1)} %shard_map.143), channel_id=1, source_target_pairs={{0,1},{1,0},{2,3},{3,2},{4,5},{5,4},{6,7},{7,6},{8,9},{9,8},{10,11... | collective-permute-start | bytes 55304 | tf_op jit(solution)/shard_map/ppermute | solution.py:407
  81.6 3.8 %collective-permute-start.23 = (f32[12,384]{1,0:T(8,128)S(1)}, f32[12,384]{1,0:T(8,128)S(1)}, u32[]{:S(2)}, u32[]{:S(2)}) collective-permute-start(f32[12,384]{1,0:T(8,128)S(1)} %add.12), channel_id=1, source_target_pairs={{0,2},{1,3},{2,0},{3,1},{4,6},{5,7},{6,4},{7,5},{8,10},{9,11},{10,... | collective-permute-start | bytes 55304 | tf_op jit(solution)/shard_map/ppermute | solution.py:407
  85.5 8.9 %copy-start.1 = (f32[12,384]{1,0:T(8,128)}, f32[12,384]{1,0:T(8,128)S(1)}, u32[]{:S(2)}) copy-start(f32[12,384]{1,0:T(8,128)S(1)} %add.13) | copy-start | bytes 55300
  85.6 4.0 %collective-permute-start.24 = (f32[1,96]{1,0:T(1,128)S(1)}, f32[1,96]{1,0:T(1,128)S(1)}, u32[]{:S(2)}, u32[]{:S(2)}) collective-permute-start(f32[1,96]{1,0:T(1,128)S(1)} %reshape.10), channel_id=1, source_target_pairs={{0,4},{4,0},{8,12},{12,8},{1,5},{5,1},{9,13},{13,9},{2,6},{6,2},{1... | collective-permute-start | bytes 1160 | tf_op jit(solution)/shard_map/ppermute | solution.py:417
  85.7 5.4 %collective-permute-start.25 = (f32[1,96]{1,0:T(1,128)S(1)}, f32[1,96]{1,0:T(1,128)S(1)}, u32[]{:S(2)}, u32[]{:S(2)}) collective-permute-start(f32[1,96]{1,0:T(1,128)S(1)} %reshape.10), channel_id=1, source_target_pairs={{0,12},{4,8},{8,4},{12,0},{1,13},{5,9},{9,5},{13,1},{2,14},{6,10},... | collective-permute-start | bytes 1160 | tf_op jit(solution)/shard_map/ppermute | solution.py:417
  89.1 4.4 %collective-permute-start.26 = (f32[1,96]{1,0:T(1,128)S(1)}, f32[1,96]{1,0:T(1,128)S(1)}, u32[]{:S(2)}, u32[]{:S(2)}) collective-permute-start(f32[1,96]{1,0:T(1,128)S(1)} %reshape.10), channel_id=1, source_target_pairs={{0,8},{4,12},{8,0},{12,4},{1,9},{5,13},{9,1},{13,5},{2,10},{6,14},... | collective-permute-start | bytes 1160 | tf_op jit(solution)/shard_map/ppermute | solution.py:417

commit v17 on v14

--- a/solution.py
+++ b/solution.py
@@ -135,7 +135,7 @@
 
 def deal(after, acts, grads):
     tokens, features = acts.shape
-    larger = features * 3 // 4
+    larger = features * 13 // 20
     widths = [larger, features - larger] if larger % LANES == 0 else [features]
     out = pl.pallas_call(
         deal_kernel,

time: 91 us -> 91.1 us (level)
  waiting for transfers between devices: 19.6 us -> 21 us
  starting transfers between devices: 56.7 us -> 55.4 us
    ppermute x2, starting transfers between devices: 5.53 us -> 2.99 us  [project_waiting(): back.append(lax.ppermute(away, 'parts', swap))]
    ppermute x17, waiting for transfers between devices: 10.6 us -> 12.8 us  [transfer(): return lax.ppermute(value, 'dp', pairs)]
    ppermute x1, starting transfers between devices: 4.12 us -> 5.26 us  [per_device(): came[c] = lax.ppermute(part[c], 'dp', [(i, i ^ 2) for i in range(n)])]
  transfers between devices with their start and end apart: 27 -> 27, of which waited for: 13 -> 11; matrix products, arithmetic and copies ran while one was open for 0% -> 0% of each run, Pallas kernels for 9% -> 9%
where the time goes in v17:
time: 91.1 us; the launch traced here: 90.7 us
  starting transfers between devices  55.4 us (61%)
  waiting for transfers between devices  21 us (23%)
  Pallas kernels  12.3 us (14%)
  between operations  1.09 us (1%)
    ppermute x17, starting transfers between devices, transfer(): return lax.ppermute(value, 'dp', pairs)  39 us
    ppermute x17, waiting for transfers between devices, transfer(): return lax.ppermute(value, 'dp', pairs)  12.8 us
    ppermute x1, starting transfers between devices, per_device(): came[c] = lax.ppermute(part[c], 'dp', [(i, i ^ 2) for i in range(n)])  5.26 us
    pallas_call x1, Pallas kernels, first_pull(): pl.pallas_call(first_pull_kernel, out_shape=[bf16(rows, features)] * 2 +...  3.6 us
    ppermute x3, starting transfers between devices, per_device(): lax.ppermute(flat, 'dp', [(i, i ^ k ^ k >> 1) for i in range(n)])  3.55 us
    ppermute x2, waiting for transfers between devices, per_device(): lax.ppermute(scores, 'layer', [(i, i ^ step) for i in range(layers)])  3.5 us
    pallas_call x4, Pallas kernels, project(): pl.pallas_call(functools.partial(project_kernel, len(tokens)), out_shape=...  3.17 us
    ppermute x2, starting transfers between devices, per_device(): others = [lax.ppermute(piece, 'parts', swap) for piece in theirs]  3.12 us
  transfers between devices with their start and end apart: 27, of which 11 were waited for; matrix products, arithmetic and copies ran while one was open for 0% of the time, Pallas kernels for 9%

profile of v17, /device:TPU:0, one launch (start us, length us, event | category | flops | bytes accessed | tf_op | source)
XLA Modules:
  0.0 90.7 jit_solution(14731368990532049059)
XLA Ops:
  0.6 3.6 %shard_map.113 = (bf16[48,2560]{1,0:T(8,128)(2,1)S(1)}, bf16[48,2560]{1,0:T(8,128)(2,1)S(1)}, bf16[2560,640]{1,0:T(8,128)(2,1)S(1)}, bf16[640,384]{1,0:T(8,128)(2,1)}, bf16[384,640]{1,0:T(8,128)(2,1)S(1)}) custom-call(bf16[2560,640]{1,0:T(8,128)(2,1)} %bitcast.16, bf16[2560,640]{1,0:T(8,128)(2,1)} %bitcast.17, bf16[640,384]{1,0:T(8,128)(2,1)} %bitcast.20, ...), custom_call_target="tpu_custom_call" | custom-call | tf_op jit(solution)/shard_map/pallas_call | solution.py:77
  4.2 3.1 %collective-permute-start = (bf16[48,2560]{1,0:T(8,128)(2,1)S(1)}, bf16[48,2560]{1,0:T(8,128)(2,1)S(1)}, u32[]{:S(2)}, u32[]{:S(2)}) collective-permute-start(bf16[48,2560]{1,0:T(8,128)(2,1)S(1)} %get-tuple-element.33), channel_id=1, source_target_pairs={{0,4},{12,8},{4,0},{8,12},{1,5},{13,9},{5,1},{9,13},{2,6},{14,10},... | collective-permute-start | bytes 737288 | tf_op jit(solution)/shard_map/ppermute | solution.py:338
  7.3 1.5 %shard_map.114 = (bf16[48,2560]{1,0:T(8,128)(2,1)S(1)}, bf16[48,2560]{1,0:T(8,128)(2,1)S(1)}, bf16[48,2560]{1,0:T(8,128)(2,1)S(1)}, bf16[48,2560]{1,0:T(8,128)(2...) custom-call(bf16[384,640]{1,0:T(8,128)(2,1)S(1)} %get-tuple-element.28.turned_ref,, ...), custom_call_target="tpu_custom_call" | custom-call | tf_op jit(solution)/shard_map/pallas_call | solution.py:101
  8.9 1.9 %collective-permute-start.3 = (bf16[48,2560]{1,0:T(8,128)(2,1)S(1)}, bf16[48,2560]{1,0:T(8,128)(2,1)S(1)}, u32[]{:S(2)}, u32[]{:S(2)}) collective-permute-start(bf16[48,2560]{1,0:T(8,128)(2,1)S(1)} %get-tuple-element.36.mine_ref), channel_id=1, source_target_pairs={{0,4},{12,8},{1,5},{13,9},{2,6},{14,10},{3,7},{15,11},{16,20},{28,... | collective-permute-start | bytes 737288 | tf_op jit(solution)/shard_map/ppermute | solution.py:338
  10.8 2.9 %collective-permute-done.came_ref.early_ref = bf16[48,2560]{1,0:T(8,128)(2,1)S(1)} collective-permute-done((bf16[48,2560]{1,0:T(8,128)(2,1)S(1)}, bf16[48,2560]{1,0:T(8,128)(2,1)S(1)}, u32[]{:S(2)}, u32[]{:S(2)}) %collective-permute-start) | collective-permute-done | bytes 245792 | tf_op jit(solution)/shard_map/ppermute | solution.py:338
  14.4 6.5 %collective-permute-start.1 = (bf16[48,2560]{1,0:T(8,128)(2,1)S(1)}, bf16[48,2560]{1,0:T(8,128)(2,1)S(1)}, u32[]{:S(2)}, u32[]{:S(2)}) collective-permute-start(bf16[48,2560]{1,0:T(8,128)(2,1)S(1)} %get-tuple-element.34), channel_id=1, source_target_pairs={{0,4},{12,8},{1,5},{13,9},{2,6},{14,10},{3,7},{15,11},{16,20},{28,... | collective-permute-start | bytes 737288 | tf_op jit(solution)/shard_map/ppermute | solution.py:338
  21.8 3.0 %collective-permute-start.5 = (bf16[48,2560]{1,0:T(8,128)(2,1)S(1)}, bf16[48,2560]{1,0:T(8,128)(2,1)S(1)}, u32[]{:S(2)}, u32[]{:S(2)}) collective-permute-start(bf16[48,2560]{1,0:T(8,128)(2,1)S(1)} %get-tuple-element.39), channel_id=1, source_target_pairs={{0,4},{12,8},{4,0},{8,12},{1,5},{13,9},{5,1},{9,13},{2,6},{14,10},... | collective-permute-start | bytes 737288 | tf_op jit(solution)/shard_map/ppermute | solution.py:338
  24.9 1.9 %shard_map.136 = (bf16[320,2560]{1,0:T(8,128)(2,1)S(1)}, bf16[320,1664]{1,0:T(8,128)(2,1)S(1)}, bf16[320,896]{1,0:T(8,128)(2,1)S(1)}) custom-call(bf16[320,2560]{1,0:T(8,128)(2,1)} %bitcast.18, bf16[320,2560]{1,0:T(8,128)(2,1)} %bitcast.19, bf16[48,2560]{1,0:T(8,128)(2,1)S(1)} %get-tuple-element.48.rest_0_.mine_ref.after_ref), custom_call_target="tpu_custom_call" | custom-call | tf_op jit(solution)/shard_map/pallas_call | solution.py:140
  26.8 1.6 %collective-permute-start.16 = (bf16[320,1664]{1,0:T(8,128)(2,1)S(1)}, bf16[320,1664]{1,0:T(8,128)(2,1)S(1)}, u32[]{:S(2)}, u32[]{:S(2)}) collective-permute-start(bf16[320,1664]{1,0:T(8,128)(2,1)S(1)} %get-tuple-element.51), channel_id=1, source_target_pairs={{0,16},{16,0},{1,17},{17,1},{2,18},{18,2},{3,19},{19,3},{4,20},{20... | collective-permute-start | bytes 3194888 | tf_op jit(solution)/shard_map/ppermute | solution.py:346
  29.2 3.7 %collective-permute-start.8 = (bf16[48,2560]{1,0:T(8,128)(2,1)S(1)}, bf16[48,2560]{1,0:T(8,128)(2,1)S(1)}, u32[]{:S(2)}, u32[]{:S(2)}) collective-permute-start(bf16[48,2560]{1,0:T(8,128)(2,1)S(1)} %get-tuple-element.43), channel_id=1, source_target_pairs={{0,4},{12,8},{4,0},{8,12},{1,5},{13,9},{5,1},{9,13},{2,6},{14,10},... | collective-permute-start | bytes 737288 | tf_op jit(solution)/shard_map/ppermute | solution.py:338
  33.7 5.0 %collective-permute-start.7 = (bf16[48,2560]{1,0:T(8,128)(2,1)S(1)}, bf16[48,2560]{1,0:T(8,128)(2,1)S(1)}, u32[]{:S(2)}, u32[]{:S(2)}) collective-permute-start(bf16[48,2560]{1,0:T(8,128)(2,1)S(1)} %get-tuple-element.42), channel_id=1, source_target_pairs={{0,4},{12,8},{4,0},{8,12},{1,5},{13,9},{5,1},{9,13},{2,6},{14,10},... | collective-permute-start | bytes 737288 | tf_op jit(solution)/shard_map/ppermute | solution.py:338
  38.8 0.9 collective-permute-done.8.came_ref
  40.5 4.3 %collective-permute-start.11 = (bf16[48,2560]{1,0:T(8,128)(2,1)S(1)}, bf16[48,2560]{1,0:T(8,128)(2,1)S(1)}, u32[]{:S(2)}, u32[]{:S(2)}) collective-permute-start(bf16[48,2560]{1,0:T(8,128)(2,1)S(1)} %get-tuple-element.47), channel_id=1, source_target_pairs={{0,4},{12,8},{4,0},{8,12},{1,5},{13,9},{5,1},{9,13},{2,6},{14,10},... | collective-permute-start | bytes 737288 | tf_op jit(solution)/shard_map/ppermute | solution.py:338
  44.8 1.5 %collective-permute-start.17 = (bf16[320,896]{1,0:T(8,128)(2,1)S(1)}, bf16[320,896]{1,0:T(8,128)(2,1)S(1)}, u32[]{:S(2)}, u32[]{:S(2)}) collective-permute-start(bf16[320,896]{1,0:T(8,128)(2,1)S(1)} %get-tuple-element.52), channel_id=1, source_target_pairs={{0,16},{16,0},{1,17},{17,1},{2,18},{18,2},{3,19},{19,3},{4,20},{20... | collective-permute-start | bytes 1720328 | tf_op jit(solution)/shard_map/ppermute | solution.py:346
  47.3 4.0 %collective-permute-start.14 = (bf16[48,2560]{1,0:T(8,128)(2,1)S(1)}, bf16[48,2560]{1,0:T(8,128)(2,1)S(1)}, u32[]{:S(2)}, u32[]{:S(2)}) collective-permute-start(bf16[48,2560]{1,0:T(8,128)(2,1)S(1)} %get-tuple-element.50), channel_id=1, source_target_pairs={{0,4},{12,8},{4,0},{8,12},{1,5},{13,9},{5,1},{9,13},{2,6},{14,10},... | collective-permute-start | bytes 737288 | tf_op jit(solution)/shard_map/ppermute | solution.py:338
  52.1 1.3 %collective-permute-start.13 = (bf16[48,2560]{1,0:T(8,128)(2,1)S(1)}, bf16[48,2560]{1,0:T(8,128)(2,1)S(1)}, u32[]{:S(2)}, u32[]{:S(2)}) collective-permute-start(bf16[48,2560]{1,0:T(8,128)(2,1)S(1)} %shard_map.130.after_ref.mine_ref), channel_id=1, source_target_pairs={{4,0},{8,12},{5,1},{9,13},{6,2},{10,14},{7,3},{11,15},{20,16},{24,... | collective-permute-start | bytes 737288 | tf_op jit(solution)/shard_map/ppermute | solution.py:338
  53.5 4.2 %collective-permute-done.14.came_ref = bf16[48,2560]{1,0:T(8,128)(2,1)S(1)} collective-permute-done((bf16[48,2560]{1,0:T(8,128)(2,1)S(1)}, bf16[48,2560]{1,0:T(8,128)(2,1)S(1)}, u32[]{:S(2)}, u32[]{:S(2)}) %collective-permute-start.14) | collective-permute-done | bytes 245792 | tf_op jit(solution)/shard_map/ppermute | solution.py:338
  57.7 5.3 %collective-permute-start.19 = (bf16[48,2560]{1,0:T(8,128)(2,1)S(1)}, bf16[48,2560]{1,0:T(8,128)(2,1)S(1)}, u32[]{:S(2)}, u32[]{:S(2)}) collective-permute-start(bf16[48,2560]{1,0:T(8,128)(2,1)S(1)} %shard_map.132.after_ref.mine_ref), channel_id=1, source_target_pairs={{0,8},{4,12},{8,0},{12,4},{1,9},{5,13},{9,1},{13,5},{2,10},{6,14},... | collective-permute-start | bytes 737288 | tf_op jit(solution)/shard_map/ppermute | solution.py:368
  63.0 1.3 %collective-permute-start.18 = (bf16[48,2560]{1,0:T(8,128)(2,1)S(1)}, bf16[48,2560]{1,0:T(8,128)(2,1)S(1)}, u32[]{:S(2)}, u32[]{:S(2)}) collective-permute-start(bf16[48,2560]{1,0:T(8,128)(2,1)S(1)} %shard_map.133.after_ref.mine_ref), channel_id=1, source_target_pairs={{4,0},{8,12},{5,1},{9,13},{6,2},{10,14},{7,3},{11,15},{20,16},{24,... | collective-permute-start | bytes 737288 | tf_op jit(solution)/shard_map/ppermute | solution.py:338
  64.4 4.5 %collective-permute-done.13.came_ref = bf16[48,2560]{1,0:T(8,128)(2,1)S(1)} collective-permute-done((bf16[48,2560]{1,0:T(8,128)(2,1)S(1)}, bf16[48,2560]{1,0:T(8,128)(2,1)S(1)}, u32[]{:S(2)}, u32[]{:S(2)}) %collective-permute-start.13) | collective-permute-done | bytes 245792 | tf_op jit(solution)/shard_map/ppermute | solution.py:338
  68.9 1.0 %shard_map.137.after_ref = bf16[288,320]{1,0:T(8,128)(2,1)S(1)} custom-call(bf16[48,2560]{1,0:T(8,128)(2,1)S(1)} %shard_map.135.after_ref.rest_7_.rest_6_, bf16[320,1664]{1,0:T(8,128)(2,1)S(1)} %collective-permute-done.16.rest_0_, bf16[320,896]{1,0:T(8,128)(2,1)S(1)} %collective-permute-done.17.rest_1_, ...), custom_call_target="tpu_custom_call" | custom-call | tf_op jit(solution)/shard_map/pallas_call | solution.py:241
  69.9 1.5 %collective-permute-start.20 = (bf16[288,320]{1,0:T(8,128)(2,1)S(1)}, bf16[288,320]{1,0:T(8,128)(2,1)S(1)}, u32[]{:S(2)}, u32[]{:S(2)}) collective-permute-start(bf16[288,320]{1,0:T(8,128)(2,1)S(1)} %shard_map.137.after_ref), channel_id=1, source_target_pairs={{0,16},{16,0},{1,17},{17,1},{2,18},{18,2},{3,19},{19,3},{4,20},{20... | collective-permute-start | bytes 552968 | tf_op jit(solution)/shard_map/ppermute | solution.py:353
  71.4 0.9 %shard_map.138.after_ref.refs_0_ = f32[288,320]{1,0:T(8,128)S(1)} custom-call(bf16[288,320]{1,0:T(8,128)(2,1)S(1)} %shard_map.137.after_ref, bf16[320,2560]{1,0:T(8,128)(2,1)S(1)} %get-tuple-element.53.rest_0_, bf16[48,2560]{1,0:T(8,128)(2,1)S(1)} %shard_map.122.after_ref.rest_2_.rest_1_, bf16[48,2560]{1,0:T(8,128)(2,1)S(1)} %shard_map.125.after_ref.rest_3_.rest_2_, ...), custom_call_target="tpu_custom_call" | custom-call | tf_op jit(solution)/shard_map/pallas_call | solution.py:241
  73.5 1.5 %collective-permute-start.21 = (bf16[96,320]{1,0:T(8,128)(2,1)S(1)}, bf16[96,320]{1,0:T(8,128)(2,1)S(1)}, u32[]{:S(2)}, u32[]{:S(2)}) collective-permute-start(bf16[96,320]{1,0:T(8,128)(2,1)S(1)} %shard_map.141.after_ref), channel_id=1, source_target_pairs={{0,16},{16,0},{1,17},{17,1},{2,18},{18,2},{3,19},{19,3},{4,20},{20... | collective-permute-start | bytes 184328 | tf_op jit(solution)/shard_map/ppermute | solution.py:353
  75.9 2.0 %collective-permute-done.21.refs_3_ = bf16[96,320]{1,0:T(8,128)(2,1)S(1)} collective-permute-done((bf16[96,320]{1,0:T(8,128)(2,1)S(1)}, bf16[96,320]{1,0:T(8,128)(2,1)S(1)}, u32[]{:S(2)}, u32[]{:S(2)}) %collective-permute-start.21) | collective-permute-done | bytes 61472 | tf_op jit(solution)/shard_map/ppermute | solution.py:353
  77.9 0.9 shard_map.143
  78.8 1.2 %collective-permute-done.22 = f32[12,384]{1,0:T(8,128)S(1)} collective-permute-done((f32[12,384]{1,0:T(8,128)S(1)}, f32[12,384]{1,0:T(8,128)S(1)}, u32[]{:S(2)}, u32[]{:S(2)}) %collective-permute-start.22) | collective-permute-done | bytes 18464 | tf_op jit(solution)/shard_map/ppermute | solution.py:404
  80.0 1.5 %collective-permute-start.23 = (f32[12,384]{1,0:T(8,128)S(1)}, f32[12,384]{1,0:T(8,128)S(1)}, u32[]{:S(2)}, u32[]{:S(2)}) collective-permute-start(f32[12,384]{1,0:T(8,128)S(1)} %add.12), channel_id=1, source_target_pairs={{0,2},{1,3},{2,0},{3,1},{4,6},{5,7},{6,4},{7,5},{8,10},{9,11},{10,... | collective-permute-start | bytes 55304 | tf_op jit(solution)/shard_map/ppermute | solution.py:404
  81.5 2.3 %collective-permute-done.23 = f32[12,384]{1,0:T(8,128)S(1)} collective-permute-done((f32[12,384]{1,0:T(8,128)S(1)}, f32[12,384]{1,0:T(8,128)S(1)}, u32[]{:S(2)}, u32[]{:S(2)}) %collective-permute-start.23) | collective-permute-done | bytes 18464 | tf_op jit(solution)/shard_map/ppermute | solution.py:404
  84.0 1.4 %collective-permute-start.25 = (f32[1,96]{1,0:T(1,128)S(1)}, f32[1,96]{1,0:T(1,128)S(1)}, u32[]{:S(2)}, u32[]{:S(2)}) collective-permute-start(f32[1,96]{1,0:T(1,128)S(1)} %reshape.10), channel_id=1, source_target_pairs={{0,12},{4,8},{8,4},{12,0},{1,13},{5,9},{9,5},{13,1},{2,14},{6,10},... | collective-permute-start | bytes 1160 | tf_op jit(solution)/shard_map/ppermute | solution.py:414
  85.4 2.1 %collective-permute-start.26 = (f32[1,96]{1,0:T(1,128)S(1)}, f32[1,96]{1,0:T(1,128)S(1)}, u32[]{:S(2)}, u32[]{:S(2)}) collective-permute-start(f32[1,96]{1,0:T(1,128)S(1)} %reshape.10), channel_id=1, source_target_pairs={{0,8},{4,12},{8,0},{12,4},{1,9},{5,13},{9,1},{13,5},{2,10},{6,14},... | collective-permute-start | bytes 1160 | tf_op jit(solution)/shard_map/ppermute | solution.py:414
  87.6 1.9 %collective-permute-done.25 = f32[1,96]{1,0:T(1,128)S(1)} collective-permute-done((f32[1,96]{1,0:T(1,128)S(1)}, f32[1,96]{1,0:T(1,128)S(1)}, u32[]{:S(2)}, u32[]{:S(2)}) %collective-permute-start.25) | collective-permute-done | bytes 416 | tf_op jit(solution)/shard_map/ppermute | solution.py:414
  (70 shorter events, 9.4 us)
Async XLA Ops:
  4.2 9.5 %collective-permute-start = (bf16[48,2560]{1,0:T(8,128)(2,1)S(1)}, bf16[48,2560]{1,0:T(8,128)(2,1)S(1)}, u32[]{:S(2)}, u32[]{:S(2)}) collective-permute-start(bf16[48,2560]{1,0:T(8,128)(2,1)S(1)} %get-tuple-element.33), channel_id=1, source_target_pairs={{0,4},{12,8},{4,0},{8,12},{1,5},{13,9},{5,1},{9,13},{2,6},{14,10},... | collective-permute-start | bytes 737288 | tf_op jit(solution)/shard_map/ppermute | solution.py:338
  8.9 12.1 %collective-permute-start.3 = (bf16[48,2560]{1,0:T(8,128)(2,1)S(1)}, bf16[48,2560]{1,0:T(8,128)(2,1)S(1)}, u32[]{:S(2)}, u32[]{:S(2)}) collective-permute-start(bf16[48,2560]{1,0:T(8,128)(2,1)S(1)} %get-tuple-element.36.mine_ref), channel_id=1, source_target_pairs={{0,4},{12,8},{1,5},{13,9},{2,6},{14,10},{3,7},{15,11},{16,20},{28,... | collective-permute-start | bytes 737288 | tf_op jit(solution)/shard_map/ppermute | solution.py:338
  13.8 8.0 %collective-permute-start.2 = (bf16[48,2560]{1,0:T(8,128)(2,1)S(1)}, bf16[48,2560]{1,0:T(8,128)(2,1)S(1)}, u32[]{:S(2)}, u32[]{:S(2)}) collective-permute-start(bf16[48,2560]{1,0:T(8,128)(2,1)S(1)} %get-tuple-element.35.after_ref.mine_ref), channel_id=1, source_target_pairs={{4,8},{8,4},{5,9},{9,5},{6,10},{10,6},{7,11},{11,7},{20,24},{24,20... | collective-permute-start | bytes 737288 | tf_op jit(solution)/shard_map/ppermute | solution.py:338
  14.4 13.9 %collective-permute-start.1 = (bf16[48,2560]{1,0:T(8,128)(2,1)S(1)}, bf16[48,2560]{1,0:T(8,128)(2,1)S(1)}, u32[]{:S(2)}, u32[]{:S(2)}) collective-permute-start(bf16[48,2560]{1,0:T(8,128)(2,1)S(1)} %get-tuple-element.34), channel_id=1, source_target_pairs={{0,4},{12,8},{1,5},{13,9},{2,6},{14,10},{3,7},{15,11},{16,20},{28,... | collective-permute-start | bytes 737288 | tf_op jit(solution)/shard_map/ppermute | solution.py:338
  21.1 8.1 %collective-permute-start.6 = (bf16[48,2560]{1,0:T(8,128)(2,1)S(1)}, bf16[48,2560]{1,0:T(8,128)(2,1)S(1)}, u32[]{:S(2)}, u32[]{:S(2)}) collective-permute-start(bf16[48,2560]{1,0:T(8,128)(2,1)S(1)} %shard_map.116.after_ref.mine_ref), channel_id=1, source_target_pairs={{4,8},{8,4},{5,9},{9,5},{6,10},{10,6},{7,11},{11,7},{20,24},{24,20... | collective-permute-start | bytes 737288 | tf_op jit(solution)/shard_map/ppermute | solution.py:338
  21.8 11.1 %collective-permute-start.5 = (bf16[48,2560]{1,0:T(8,128)(2,1)S(1)}, bf16[48,2560]{1,0:T(8,128)(2,1)S(1)}, u32[]{:S(2)}, u32[]{:S(2)}) collective-permute-start(bf16[48,2560]{1,0:T(8,128)(2,1)S(1)} %get-tuple-element.39), channel_id=1, source_target_pairs={{0,4},{12,8},{4,0},{8,12},{1,5},{13,9},{5,1},{9,13},{2,6},{14,10},... | collective-permute-start | bytes 737288 | tf_op jit(solution)/shard_map/ppermute | solution.py:338
  26.8 42.2 %collective-permute-start.16 = (bf16[320,1664]{1,0:T(8,128)(2,1)S(1)}, bf16[320,1664]{1,0:T(8,128)(2,1)S(1)}, u32[]{:S(2)}, u32[]{:S(2)}) collective-permute-start(bf16[320,1664]{1,0:T(8,128)(2,1)S(1)} %get-tuple-element.51), channel_id=1, source_target_pairs={{0,16},{16,0},{1,17},{17,1},{2,18},{18,2},{3,19},{19,3},{4,20},{20... | collective-permute-start | bytes 3194888 | tf_op jit(solution)/shard_map/ppermute | solution.py:346
  28.4 5.2 %collective-permute-start.4 = (bf16[48,2560]{1,0:T(8,128)(2,1)S(1)}, bf16[48,2560]{1,0:T(8,128)(2,1)S(1)}, u32[]{:S(2)}, u32[]{:S(2)}) collective-permute-start(bf16[48,2560]{1,0:T(8,128)(2,1)S(1)} %shard_map.118.after_ref.mine_ref), channel_id=1, source_target_pairs={{4,8},{8,4},{5,9},{9,5},{6,10},{10,6},{7,11},{11,7},{20,24},{24,20... | collective-permute-start | bytes 737288 | tf_op jit(solution)/shard_map/ppermute | solution.py:338
  29.2 10.5 %collective-permute-start.8 = (bf16[48,2560]{1,0:T(8,128)(2,1)S(1)}, bf16[48,2560]{1,0:T(8,128)(2,1)S(1)}, u32[]{:S(2)}, u32[]{:S(2)}) collective-permute-start(bf16[48,2560]{1,0:T(8,128)(2,1)S(1)} %get-tuple-element.43), channel_id=1, source_target_pairs={{0,4},{12,8},{4,0},{8,12},{1,5},{13,9},{5,1},{9,13},{2,6},{14,10},... | collective-permute-start | bytes 737288 | tf_op jit(solution)/shard_map/ppermute | solution.py:338
  33.0 7.5 %collective-permute-start.9 = (bf16[48,2560]{1,0:T(8,128)(2,1)S(1)}, bf16[48,2560]{1,0:T(8,128)(2,1)S(1)}, u32[]{:S(2)}, u32[]{:S(2)}) collective-permute-start(bf16[48,2560]{1,0:T(8,128)(2,1)S(1)} %shard_map.120.after_ref.mine_ref), channel_id=1, source_target_pairs={{4,8},{8,4},{5,9},{9,5},{6,10},{10,6},{7,11},{11,7},{20,24},{24,20... | collective-permute-start | bytes 737288 | tf_op jit(solution)/shard_map/ppermute | solution.py:338
  33.7 12.7 %collective-permute-start.7 = (bf16[48,2560]{1,0:T(8,128)(2,1)S(1)}, bf16[48,2560]{1,0:T(8,128)(2,1)S(1)}, u32[]{:S(2)}, u32[]{:S(2)}) collective-permute-start(bf16[48,2560]{1,0:T(8,128)(2,1)S(1)} %get-tuple-element.42), channel_id=1, source_target_pairs={{0,4},{12,8},{4,0},{8,12},{1,5},{13,9},{5,1},{9,13},{2,6},{14,10},... | collective-permute-start | bytes 737288 | tf_op jit(solution)/shard_map/ppermute | solution.py:338
  39.7 7.4 %collective-permute-start.12 = (bf16[48,2560]{1,0:T(8,128)(2,1)S(1)}, bf16[48,2560]{1,0:T(8,128)(2,1)S(1)}, u32[]{:S(2)}, u32[]{:S(2)}) collective-permute-start(bf16[48,2560]{1,0:T(8,128)(2,1)S(1)} %shard_map.123.after_ref.mine_ref), channel_id=1, source_target_pairs={{4,8},{8,4},{5,9},{9,5},{6,10},{10,6},{7,11},{11,7},{20,24},{24,20... | collective-permute-start | bytes 737288 | tf_op jit(solution)/shard_map/ppermute | solution.py:338
  40.5 10.8 %collective-permute-start.11 = (bf16[48,2560]{1,0:T(8,128)(2,1)S(1)}, bf16[48,2560]{1,0:T(8,128)(2,1)S(1)}, u32[]{:S(2)}, u32[]{:S(2)}) collective-permute-start(bf16[48,2560]{1,0:T(8,128)(2,1)S(1)} %get-tuple-element.47), channel_id=1, source_target_pairs={{0,4},{12,8},{4,0},{8,12},{1,5},{13,9},{5,1},{9,13},{2,6},{14,10},... | collective-permute-start | bytes 737288 | tf_op jit(solution)/shard_map/ppermute | solution.py:338
  44.8 24.1 %collective-permute-start.17 = (bf16[320,896]{1,0:T(8,128)(2,1)S(1)}, bf16[320,896]{1,0:T(8,128)(2,1)S(1)}, u32[]{:S(2)}, u32[]{:S(2)}) collective-permute-start(bf16[320,896]{1,0:T(8,128)(2,1)S(1)} %get-tuple-element.52), channel_id=1, source_target_pairs={{0,16},{16,0},{1,17},{17,1},{2,18},{18,2},{3,19},{19,3},{4,20},{20... | collective-permute-start | bytes 1720328 | tf_op jit(solution)/shard_map/ppermute | solution.py:346
  46.5 5.6 %collective-permute-start.10 = (bf16[48,2560]{1,0:T(8,128)(2,1)S(1)}, bf16[48,2560]{1,0:T(8,128)(2,1)S(1)}, u32[]{:S(2)}, u32[]{:S(2)}) collective-permute-start(bf16[48,2560]{1,0:T(8,128)(2,1)S(1)} %shard_map.126.after_ref.mine_ref), channel_id=1, source_target_pairs={{4,8},{8,4},{5,9},{9,5},{6,10},{10,6},{7,11},{11,7},{20,24},{24,20... | collective-permute-start | bytes 737288 | tf_op jit(solution)/shard_map/ppermute | solution.py:338
  47.3 10.4 %collective-permute-start.14 = (bf16[48,2560]{1,0:T(8,128)(2,1)S(1)}, bf16[48,2560]{1,0:T(8,128)(2,1)S(1)}, u32[]{:S(2)}, u32[]{:S(2)}) collective-permute-start(bf16[48,2560]{1,0:T(8,128)(2,1)S(1)} %get-tuple-element.50), channel_id=1, source_target_pairs={{0,4},{12,8},{4,0},{8,12},{1,5},{13,9},{5,1},{9,13},{2,6},{14,10},... | collective-permute-start | bytes 737288 | tf_op jit(solution)/shard_map/ppermute | solution.py:338
  51.4 11.6 %collective-permute-start.15 = (bf16[48,2560]{1,0:T(8,128)(2,1)S(1)}, bf16[48,2560]{1,0:T(8,128)(2,1)S(1)}, u32[]{:S(2)}, u32[]{:S(2)}) collective-permute-start(bf16[48,2560]{1,0:T(8,128)(2,1)S(1)} %shard_map.129.after_ref.mine_ref), channel_id=1, source_target_pairs={{4,8},{8,4},{5,9},{9,5},{6,10},{10,6},{7,11},{11,7},{20,24},{24,20... | collective-permute-start | bytes 737288 | tf_op jit(solution)/shard_map/ppermute | solution.py:338
  52.1 16.8 %collective-permute-start.13 = (bf16[48,2560]{1,0:T(8,128)(2,1)S(1)}, bf16[48,2560]{1,0:T(8,128)(2,1)S(1)}, u32[]{:S(2)}, u32[]{:S(2)}) collective-permute-start(bf16[48,2560]{1,0:T(8,128)(2,1)S(1)} %shard_map.130.after_ref.mine_ref), channel_id=1, source_target_pairs={{4,0},{8,12},{5,1},{9,13},{6,2},{10,14},{7,3},{11,15},{20,16},{24,... | collective-permute-start | bytes 737288 | tf_op jit(solution)/shard_map/ppermute | solution.py:338
  57.7 14.7 %collective-permute-start.19 = (bf16[48,2560]{1,0:T(8,128)(2,1)S(1)}, bf16[48,2560]{1,0:T(8,128)(2,1)S(1)}, u32[]{:S(2)}, u32[]{:S(2)}) collective-permute-start(bf16[48,2560]{1,0:T(8,128)(2,1)S(1)} %shard_map.132.after_ref.mine_ref), channel_id=1, source_target_pairs={{0,8},{4,12},{8,0},{12,4},{1,9},{5,13},{9,1},{13,5},{2,10},{6,14},... | collective-permute-start | bytes 737288 | tf_op jit(solution)/shard_map/ppermute | solution.py:368
  63.0 9.7 %collective-permute-start.18 = (bf16[48,2560]{1,0:T(8,128)(2,1)S(1)}, bf16[48,2560]{1,0:T(8,128)(2,1)S(1)}, u32[]{:S(2)}, u32[]{:S(2)}) collective-permute-start(bf16[48,2560]{1,0:T(8,128)(2,1)S(1)} %shard_map.133.after_ref.mine_ref), channel_id=1, source_target_pairs={{4,0},{8,12},{5,1},{9,13},{6,2},{10,14},{7,3},{11,15},{20,16},{24,... | collective-permute-start | bytes 737288 | tf_op jit(solution)/shard_map/ppermute | solution.py:338
  69.9 6.0 %collective-permute-start.20 = (bf16[288,320]{1,0:T(8,128)(2,1)S(1)}, bf16[288,320]{1,0:T(8,128)(2,1)S(1)}, u32[]{:S(2)}, u32[]{:S(2)}) collective-permute-start(bf16[288,320]{1,0:T(8,128)(2,1)S(1)} %shard_map.137.after_ref), channel_id=1, source_target_pairs={{0,16},{16,0},{1,17},{17,1},{2,18},{18,2},{3,19},{19,3},{4,20},{20... | collective-permute-start | bytes 552968 | tf_op jit(solution)/shard_map/ppermute | solution.py:353
  73.4 4.5 %copy-start = (s32[1,8]{1,0:T(1,128)S(1)}, s32[1,8]{1,0:T(1,128)}, u32[]{:S(2)}) copy-start(s32[1,8]{1,0:T(1,128)} %counts_ref.1) | copy-start | bytes 100
  73.4 14.1 %copy-start.2 = (s32[128]{0:T(128)S(1)}, s32[128]{0:T(128)}, u32[]{:S(2)}) copy-start(s32[128]{0:T(128)} %param.19) | copy-start | bytes 1540
  73.4 14.1 %copy-start.3 = (s32[128]{0:T(128)S(1)}, s32[128]{0:T(128)}, u32[]{:S(2)}) copy-start(s32[128]{0:T(128)} %param.17) | copy-start | bytes 1540
  73.5 14.1 %copy-start.4 = (s32[128,1]{0,1:T(1,128)S(1)}, s32[128,1]{0,1:T(1,128)}, u32[]{:S(2)}) copy-start(s32[128,1]{0,1:T(1,128)} %param.18) | copy-start | bytes 1540
  73.5 4.4 %collective-permute-start.21 = (bf16[96,320]{1,0:T(8,128)(2,1)S(1)}, bf16[96,320]{1,0:T(8,128)(2,1)S(1)}, u32[]{:S(2)}, u32[]{:S(2)}) collective-permute-start(bf16[96,320]{1,0:T(8,128)(2,1)S(1)} %shard_map.141.after_ref), channel_id=1, source_target_pairs={{0,16},{16,0},{1,17},{17,1},{2,18},{18,2},{3,19},{19,3},{4,20},{20... | collective-permute-start | bytes 184328 | tf_op jit(solution)/shard_map/ppermute | solution.py:353
  78.8 1.2 %collective-permute-start.22 = (f32[12,384]{1,0:T(8,128)S(1)}, f32[12,384]{1,0:T(8,128)S(1)}, u32[]{:S(2)}, u32[]{:S(2)}) collective-permute-start(f32[12,384]{1,0:T(8,128)S(1)} %shard_map.143), channel_id=1, source_target_pairs={{0,1},{1,0},{2,3},{3,2},{4,5},{5,4},{6,7},{7,6},{8,9},{9,8},{10,11... | collective-permute-start | bytes 55304 | tf_op jit(solution)/shard_map/ppermute | solution.py:404
  80.0 3.8 %collective-permute-start.23 = (f32[12,384]{1,0:T(8,128)S(1)}, f32[12,384]{1,0:T(8,128)S(1)}, u32[]{:S(2)}, u32[]{:S(2)}) collective-permute-start(f32[12,384]{1,0:T(8,128)S(1)} %add.12), channel_id=1, source_target_pairs={{0,2},{1,3},{2,0},{3,1},{4,6},{5,7},{6,4},{7,5},{8,10},{9,11},{10,... | collective-permute-start | bytes 55304 | tf_op jit(solution)/shard_map/ppermute | solution.py:404
  83.8 6.9 %copy-start.1 = (f32[12,384]{1,0:T(8,128)}, f32[12,384]{1,0:T(8,128)S(1)}, u32[]{:S(2)}) copy-start(f32[12,384]{1,0:T(8,128)S(1)} %add.13) | copy-start | bytes 55300
  84.0 3.6 %collective-permute-start.24 = (f32[1,96]{1,0:T(1,128)S(1)}, f32[1,96]{1,0:T(1,128)S(1)}, u32[]{:S(2)}, u32[]{:S(2)}) collective-permute-start(f32[1,96]{1,0:T(1,128)S(1)} %reshape.10), channel_id=1, source_target_pairs={{0,4},{4,0},{8,12},{12,8},{1,5},{5,1},{9,13},{13,9},{2,6},{6,2},{1... | collective-permute-start | bytes 1160 | tf_op jit(solution)/shard_map/ppermute | solution.py:414
  84.0 5.4 %collective-permute-start.25 = (f32[1,96]{1,0:T(1,128)S(1)}, f32[1,96]{1,0:T(1,128)S(1)}, u32[]{:S(2)}, u32[]{:S(2)}) collective-permute-start(f32[1,96]{1,0:T(1,128)S(1)} %reshape.10), channel_id=1, source_target_pairs={{0,12},{4,8},{8,4},{12,0},{1,13},{5,9},{9,5},{13,1},{2,14},{6,10},... | collective-permute-start | bytes 1160 | tf_op jit(solution)/shard_map/ppermute | solution.py:414
  85.4 4.4 %collective-permute-start.26 = (f32[1,96]{1,0:T(1,128)S(1)}, f32[1,96]{1,0:T(1,128)S(1)}, u32[]{:S(2)}, u32[]{:S(2)}) collective-permute-start(f32[1,96]{1,0:T(1,128)S(1)} %reshape.10), channel_id=1, source_target_pairs={{0,8},{4,12},{8,0},{12,4},{1,9},{5,13},{9,1},{13,5},{2,10},{6,14},... | collective-permute-start | bytes 1160 | tf_op jit(solution)/shard_map/ppermute | solution.py:414

commit v18 on v17

--- a/solution.py
+++ b/solution.py
@@ -176,6 +176,43 @@
         out_specs=VMEM,
         compiler_params=pltpu.CompilerParams(vmem_limit_bytes=8 * MIB),
     )(mine, came, early, after)
+
+
+def join_kernel(mine_ref, one_ref, two_ref, after_ref, out_ref):
+    came = one_ref[...].astype(jnp.float32) + two_ref[...].astype(jnp.float32)
+    out_ref[...] = (mine_ref[...].astype(jnp.float32) + came).astype(jnp.bfloat16)
+
+
+def join(after, mine, one, two):
+    return pl.pallas_call(
+        join_kernel,
+        out_shape=bf16(*mine.shape),
+        in_specs=[VMEM, VMEM, VMEM, ANY],
+        out_specs=VMEM,
+        compiler_params=pltpu.CompilerParams(vmem_limit_bytes=8 * MIB),
+    )(mine, one, two, after)
+
+
+def late_kernel(mine_ref, came_ref, after_ref, out_ref):
+    here = at_depth(0) & (lax.rem(lax.axis_index("layer"), 2) == 1)
+
+    @pl.when(here)
+    def _():
+        out_ref[...] = came_ref[...]
+
+    @pl.when(jnp.logical_not(here))
+    def _():
+        out_ref[...] = mine_ref[...]
+
+
+def late(after, mine, came):
+    return pl.pallas_call(
+        late_kernel,
+        out_shape=bf16(*mine.shape),
+        in_specs=[VMEM, VMEM, ANY],
+        out_specs=VMEM,
+        compiler_params=pltpu.CompilerParams(vmem_limit_bytes=8 * MIB),
+    )(mine, came, after)
 
 
 def total_kernel(shared, mine_ref, came_ref, after_ref, *rest):
@@ -338,6 +375,10 @@
         return lax.ppermute(value, "dp", pairs)
 
     short = n == 4
+    def on_cores(core, value, pairs):
+        pairs = [(a * layers + i, b * layers + i) for a, b in pairs for i in range(core, layers, 2)]
+        return lax.ppermute(value, ("dp", "layer"), pairs)
+
     part, came = list(own), [None] * chunks
     ahead = min(2, chunks)
     early = came[0] = transfer(("in", "out") if short else ("in",), 0, send)
@@ -365,11 +406,13 @@
             if short and c == chunks - 1:
                 if s == 0:
                     after = part[c] = pair(after, own[c], came[c], early)
-                    came[c] = lax.ppermute(part[c], "dp", [(i, i ^ 2) for i in range(n)])
+                    came[c] = [
+                        on_cores(0, part[c], [(i, i ^ 2) for i in range(n)]),
+                        on_cores(1, part[c], [(1, 2), (2, 1)]),
+                    ]
                 elif s == 1:
-                    part[c], _ = total(after, part[c], came[c])
-                    after = part[c]
-                    waiting.append((c, part[c]))
+                    after = part[c] = join(after, part[c], *came[c])
+                    came[c] = on_cores(1, part[c], [(1, 0), (2, 3)])
                 continue
             later = turn + ahead if turn + ahead < chunks else None
             if turn >= last - 1:
@@ -393,6 +436,10 @@
                 came[c] = transfer(stages[s + 1][:1], stages[s + 1][1], part[c])
             else:
                 waiting.append((c, part[c]))
+        if short and turn == turns - 1:
+            c = chunks - 1
+            after = part[c] = late(after, part[c], came[c])
+            waiting.append((c, part[c]))
         if turn >= turns - 2 and waiting:
             after = project_waiting(after)
 

time: 91.1 us -> 92.8 us (1.019)
  waiting for transfers between devices: 21 us -> 22.8 us
    ppermute x1 -> x3, starting transfers between devices: 5.26 us -> 4.38 us  [on_cores(): return lax.ppermute(value, ('dp', 'layer'), pairs)]
  transfers between devices with their start and end apart: 27 -> 29, of which waited for: 11 -> 11; matrix products, arithmetic and copies ran while one was open for 0% -> 0% of each run, Pallas kernels for 9% -> 9%
where the time goes in v18:
time: 92.8 us; the launch traced here: 92.3 us
  starting transfers between devices  55.1 us (59%)
  waiting for transfers between devices  22.8 us (25%)
  Pallas kernels  12.3 us (13%)
  between operations  1.13 us (1%)
    ppermute x17, starting transfers between devices, transfer(): return lax.ppermute(value, 'dp', pairs)  39 us
    ppermute x17, waiting for transfers between devices, transfer(): return lax.ppermute(value, 'dp', pairs)  13.6 us
    ppermute x3, starting transfers between devices, on_cores(): return lax.ppermute(value, ('dp', 'layer'), pairs)  4.38 us
    pallas_call x1, Pallas kernels, first_pull(): pl.pallas_call(first_pull_kernel, out_shape=[bf16(rows, features)] * 2 +...  3.6 us
    ppermute x2, starting transfers between devices, project_waiting(): back.append(lax.ppermute(away, 'parts', swap))  3.58 us
    ppermute x3, starting transfers between devices, per_device(): lax.ppermute(flat, 'dp', [(i, i ^ k ^ k >> 1) for i in range(n)])  3.55 us
    ppermute x2, waiting for transfers between devices, per_device(): lax.ppermute(scores, 'layer', [(i, i ^ step) for i in range(layers)])  3.51 us
    pallas_call x4, Pallas kernels, project(): pl.pallas_call(functools.partial(project_kernel, len(tokens)), out_shape=...  3.17 us
  transfers between devices with their start and end apart: 29, of which 11 were waited for; matrix products, arithmetic and copies ran while one was open for 0% of the time, Pallas kernels for 9%

profile of v18, /device:TPU:0, one launch (start us, length us, event | category | flops | bytes accessed | tf_op | source)
XLA Modules:
  0.0 92.3 jit_solution(14292933775099882539)
XLA Ops:
  0.6 3.6 %shard_map.113 = (bf16[48,2560]{1,0:T(8,128)(2,1)S(1)}, bf16[48,2560]{1,0:T(8,128)(2,1)S(1)}, bf16[2560,640]{1,0:T(8,128)(2,1)S(1)}, bf16[640,384]{1,0:T(8,128)(2,1)}, bf16[384,640]{1,0:T(8,128)(2,1)S(1)}) custom-call(bf16[2560,640]{1,0:T(8,128)(2,1)} %bitcast.16, bf16[2560,640]{1,0:T(8,128)(2,1)} %bitcast.17, bf16[640,384]{1,0:T(8,128)(2,1)} %bitcast.20, ...), custom_call_target="tpu_custom_call" | custom-call | tf_op jit(solution)/shard_map/pallas_call | solution.py:77
  4.2 3.1 %collective-permute-start = (bf16[48,2560]{1,0:T(8,128)(2,1)S(1)}, bf16[48,2560]{1,0:T(8,128)(2,1)S(1)}, u32[]{:S(2)}, u32[]{:S(2)}) collective-permute-start(bf16[48,2560]{1,0:T(8,128)(2,1)S(1)} %get-tuple-element.33), channel_id=1, source_target_pairs={{0,4},{12,8},{4,0},{8,12},{1,5},{13,9},{5,1},{9,13},{2,6},{14,10},... | collective-permute-start | bytes 737288 | tf_op jit(solution)/shard_map/ppermute | solution.py:375
  7.3 1.5 %shard_map.114 = (bf16[48,2560]{1,0:T(8,128)(2,1)S(1)}, bf16[48,2560]{1,0:T(8,128)(2,1)S(1)}, bf16[48,2560]{1,0:T(8,128)(2,1)S(1)}, bf16[48,2560]{1,0:T(8,128)(2...) custom-call(bf16[384,640]{1,0:T(8,128)(2,1)S(1)} %get-tuple-element.28.turned_ref,, ...), custom_call_target="tpu_custom_call" | custom-call | tf_op jit(solution)/shard_map/pallas_call | solution.py:101
  8.9 1.9 %collective-permute-start.3 = (bf16[48,2560]{1,0:T(8,128)(2,1)S(1)}, bf16[48,2560]{1,0:T(8,128)(2,1)S(1)}, u32[]{:S(2)}, u32[]{:S(2)}) collective-permute-start(bf16[48,2560]{1,0:T(8,128)(2,1)S(1)} %get-tuple-element.36.mine_ref), channel_id=1, source_target_pairs={{0,4},{12,8},{1,5},{13,9},{2,6},{14,10},{3,7},{15,11},{16,20},{28,... | collective-permute-start | bytes 737288 | tf_op jit(solution)/shard_map/ppermute | solution.py:375
  10.8 2.9 %collective-permute-done.came_ref.early_ref = bf16[48,2560]{1,0:T(8,128)(2,1)S(1)} collective-permute-done((bf16[48,2560]{1,0:T(8,128)(2,1)S(1)}, bf16[48,2560]{1,0:T(8,128)(2,1)S(1)}, u32[]{:S(2)}, u32[]{:S(2)}) %collective-permute-start) | collective-permute-done | bytes 245792 | tf_op jit(solution)/shard_map/ppermute | solution.py:375
  14.4 6.5 %collective-permute-start.1 = (bf16[48,2560]{1,0:T(8,128)(2,1)S(1)}, bf16[48,2560]{1,0:T(8,128)(2,1)S(1)}, u32[]{:S(2)}, u32[]{:S(2)}) collective-permute-start(bf16[48,2560]{1,0:T(8,128)(2,1)S(1)} %get-tuple-element.34), channel_id=1, source_target_pairs={{0,4},{12,8},{1,5},{13,9},{2,6},{14,10},{3,7},{15,11},{16,20},{28,... | collective-permute-start | bytes 737288 | tf_op jit(solution)/shard_map/ppermute | solution.py:375
  21.8 3.0 %collective-permute-start.5 = (bf16[48,2560]{1,0:T(8,128)(2,1)S(1)}, bf16[48,2560]{1,0:T(8,128)(2,1)S(1)}, u32[]{:S(2)}, u32[]{:S(2)}) collective-permute-start(bf16[48,2560]{1,0:T(8,128)(2,1)S(1)} %get-tuple-element.39), channel_id=1, source_target_pairs={{0,4},{12,8},{4,0},{8,12},{1,5},{13,9},{5,1},{9,13},{2,6},{14,10},... | collective-permute-start | bytes 737288 | tf_op jit(solution)/shard_map/ppermute | solution.py:375
  24.9 1.9 %shard_map.136 = (bf16[320,2560]{1,0:T(8,128)(2,1)S(1)}, bf16[320,1664]{1,0:T(8,128)(2,1)S(1)}, bf16[320,896]{1,0:T(8,128)(2,1)S(1)}) custom-call(bf16[320,2560]{1,0:T(8,128)(2,1)} %bitcast.18, bf16[320,2560]{1,0:T(8,128)(2,1)} %bitcast.19, bf16[48,2560]{1,0:T(8,128)(2,1)S(1)} %get-tuple-element.48.rest_0_.mine_ref.after_ref), custom_call_target="tpu_custom_call" | custom-call | tf_op jit(solution)/shard_map/pallas_call | solution.py:140
  26.8 1.6 %collective-permute-start.16 = (bf16[320,1664]{1,0:T(8,128)(2,1)S(1)}, bf16[320,1664]{1,0:T(8,128)(2,1)S(1)}, u32[]{:S(2)}, u32[]{:S(2)}) collective-permute-start(bf16[320,1664]{1,0:T(8,128)(2,1)S(1)} %get-tuple-element.51), channel_id=1, source_target_pairs={{0,16},{16,0},{1,17},{17,1},{2,18},{18,2},{3,19},{19,3},{4,20},{20... | collective-permute-start | bytes 3194888 | tf_op jit(solution)/shard_map/ppermute | solution.py:387
  29.2 3.7 %collective-permute-start.8 = (bf16[48,2560]{1,0:T(8,128)(2,1)S(1)}, bf16[48,2560]{1,0:T(8,128)(2,1)S(1)}, u32[]{:S(2)}, u32[]{:S(2)}) collective-permute-start(bf16[48,2560]{1,0:T(8,128)(2,1)S(1)} %get-tuple-element.43), channel_id=1, source_target_pairs={{0,4},{12,8},{4,0},{8,12},{1,5},{13,9},{5,1},{9,13},{2,6},{14,10},... | collective-permute-start | bytes 737288 | tf_op jit(solution)/shard_map/ppermute | solution.py:375
  33.7 5.0 %collective-permute-start.7 = (bf16[48,2560]{1,0:T(8,128)(2,1)S(1)}, bf16[48,2560]{1,0:T(8,128)(2,1)S(1)}, u32[]{:S(2)}, u32[]{:S(2)}) collective-permute-start(bf16[48,2560]{1,0:T(8,128)(2,1)S(1)} %get-tuple-element.42), channel_id=1, source_target_pairs={{0,4},{12,8},{4,0},{8,12},{1,5},{13,9},{5,1},{9,13},{2,6},{14,10},... | collective-permute-start | bytes 737288 | tf_op jit(solution)/shard_map/ppermute | solution.py:375
  38.8 0.9 collective-permute-done.8.came_ref
  40.5 4.3 %collective-permute-start.11 = (bf16[48,2560]{1,0:T(8,128)(2,1)S(1)}, bf16[48,2560]{1,0:T(8,128)(2,1)S(1)}, u32[]{:S(2)}, u32[]{:S(2)}) collective-permute-start(bf16[48,2560]{1,0:T(8,128)(2,1)S(1)} %get-tuple-element.47), channel_id=1, source_target_pairs={{0,4},{12,8},{4,0},{8,12},{1,5},{13,9},{5,1},{9,13},{2,6},{14,10},... | collective-permute-start | bytes 737288 | tf_op jit(solution)/shard_map/ppermute | solution.py:375
  44.8 1.5 %collective-permute-start.17 = (bf16[320,896]{1,0:T(8,128)(2,1)S(1)}, bf16[320,896]{1,0:T(8,128)(2,1)S(1)}, u32[]{:S(2)}, u32[]{:S(2)}) collective-permute-start(bf16[320,896]{1,0:T(8,128)(2,1)S(1)} %get-tuple-element.52), channel_id=1, source_target_pairs={{0,16},{16,0},{1,17},{17,1},{2,18},{18,2},{3,19},{19,3},{4,20},{20... | collective-permute-start | bytes 1720328 | tf_op jit(solution)/shard_map/ppermute | solution.py:387
  47.2 4.0 %collective-permute-start.14 = (bf16[48,2560]{1,0:T(8,128)(2,1)S(1)}, bf16[48,2560]{1,0:T(8,128)(2,1)S(1)}, u32[]{:S(2)}, u32[]{:S(2)}) collective-permute-start(bf16[48,2560]{1,0:T(8,128)(2,1)S(1)} %get-tuple-element.50), channel_id=1, source_target_pairs={{0,4},{12,8},{4,0},{8,12},{1,5},{13,9},{5,1},{9,13},{2,6},{14,10},... | collective-permute-start | bytes 737288 | tf_op jit(solution)/shard_map/ppermute | solution.py:375
  52.1 1.3 %collective-permute-start.13 = (bf16[48,2560]{1,0:T(8,128)(2,1)S(1)}, bf16[48,2560]{1,0:T(8,128)(2,1)S(1)}, u32[]{:S(2)}, u32[]{:S(2)}) collective-permute-start(bf16[48,2560]{1,0:T(8,128)(2,1)S(1)} %shard_map.130.after_ref.mine_ref), channel_id=1, source_target_pairs={{4,0},{8,12},{5,1},{9,13},{6,2},{10,14},{7,3},{11,15},{20,16},{24,... | collective-permute-start | bytes 737288 | tf_op jit(solution)/shard_map/ppermute | solution.py:375
  53.5 4.1 %collective-permute-done.14.came_ref = bf16[48,2560]{1,0:T(8,128)(2,1)S(1)} collective-permute-done((bf16[48,2560]{1,0:T(8,128)(2,1)S(1)}, bf16[48,2560]{1,0:T(8,128)(2,1)S(1)}, u32[]{:S(2)}, u32[]{:S(2)}) %collective-permute-start.14) | collective-permute-done | bytes 245792 | tf_op jit(solution)/shard_map/ppermute | solution.py:375
  57.6 3.0 %collective-permute-start.18 = (bf16[48,2560]{1,0:T(8,128)(2,1)S(1)}, bf16[48,2560]{1,0:T(8,128)(2,1)S(1)}, u32[]{:S(2)}, u32[]{:S(2)}) collective-permute-start(bf16[48,2560]{1,0:T(8,128)(2,1)S(1)} %shard_map.132.after_ref.mine_ref), channel_id=1, source_target_pairs={{0,8},{2,10},{4,12},{6,14},{8,0},{10,2},{12,4},{14,6},{16,24},{18,... | collective-permute-start | bytes 737288 | tf_op jit(solution)/shard_map/ppermute | solution.py:380
  61.5 3.8 %collective-permute-done.13.came_ref = bf16[48,2560]{1,0:T(8,128)(2,1)S(1)} collective-permute-done((bf16[48,2560]{1,0:T(8,128)(2,1)S(1)}, bf16[48,2560]{1,0:T(8,128)(2,1)S(1)}, u32[]{:S(2)}, u32[]{:S(2)}) %collective-permute-start.13) | collective-permute-done | bytes 245792 | tf_op jit(solution)/shard_map/ppermute | solution.py:375
  65.2 1.3 %collective-permute-start.21 = (bf16[48,2560]{1,0:T(8,128)(2,1)S(1)}, bf16[48,2560]{1,0:T(8,128)(2,1)S(1)}, u32[]{:S(2)}, u32[]{:S(2)}) collective-permute-start(bf16[48,2560]{1,0:T(8,128)(2,1)S(1)} %shard_map.133.after_ref.mine_ref), channel_id=1, source_target_pairs={{4,0},{8,12},{5,1},{9,13},{6,2},{10,14},{7,3},{11,15},{20,16},{24,... | collective-permute-start | bytes 737288 | tf_op jit(solution)/shard_map/ppermute | solution.py:375
  66.6 1.0 %shard_map.137.after_ref = bf16[288,320]{1,0:T(8,128)(2,1)S(1)} custom-call(bf16[48,2560]{1,0:T(8,128)(2,1)S(1)} %shard_map.135.after_ref.rest_7_.rest_6_, bf16[320,1664]{1,0:T(8,128)(2,1)S(1)} %collective-permute-done.16.rest_0_, bf16[320,896]{1,0:T(8,128)(2,1)S(1)} %collective-permute-done.17.rest_1_, ...), custom_call_target="tpu_custom_call" | custom-call | tf_op jit(solution)/shard_map/pallas_call | solution.py:278
  67.6 0.9 %shard_map.138.after_ref.refs_0_ = f32[288,320]{1,0:T(8,128)S(1)} custom-call(bf16[288,320]{1,0:T(8,128)(2,1)S(1)} %shard_map.137.after_ref, bf16[320,2560]{1,0:T(8,128)(2,1)S(1)} %get-tuple-element.53.rest_0_, bf16[48,2560]{1,0:T(8,128)(2,1)S(1)} %shard_map.122.after_ref.rest_2_.rest_1_, bf16[48,2560]{1,0:T(8,128)(2,1)S(1)} %shard_map.125.after_ref.rest_3_.rest_2_, ...), custom_call_target="tpu_custom_call" | custom-call | tf_op jit(solution)/shard_map/pallas_call | solution.py:278
  70.1 1.5 %collective-permute-start.22 = (bf16[288,320]{1,0:T(8,128)(2,1)S(1)}, bf16[288,320]{1,0:T(8,128)(2,1)S(1)}, u32[]{:S(2)}, u32[]{:S(2)}) collective-permute-start(bf16[288,320]{1,0:T(8,128)(2,1)S(1)} %shard_map.137.after_ref), channel_id=1, source_target_pairs={{0,16},{16,0},{1,17},{17,1},{2,18},{18,2},{3,19},{19,3},{4,20},{20... | collective-permute-start | bytes 552968 | tf_op jit(solution)/shard_map/ppermute | solution.py:394
  71.6 1.9 %collective-permute-done.21.came_ref = bf16[48,2560]{1,0:T(8,128)(2,1)S(1)} collective-permute-done((bf16[48,2560]{1,0:T(8,128)(2,1)S(1)}, bf16[48,2560]{1,0:T(8,128)(2,1)S(1)}, u32[]{:S(2)}, u32[]{:S(2)}) %collective-permute-start.21) | collective-permute-done | bytes 245792 | tf_op jit(solution)/shard_map/ppermute | solution.py:375
  74.3 2.1 %collective-permute-start.23 = (bf16[96,320]{1,0:T(8,128)(2,1)S(1)}, bf16[96,320]{1,0:T(8,128)(2,1)S(1)}, u32[]{:S(2)}, u32[]{:S(2)}) collective-permute-start(bf16[96,320]{1,0:T(8,128)(2,1)S(1)} %shard_map.142.after_ref), channel_id=1, source_target_pairs={{0,16},{16,0},{1,17},{17,1},{2,18},{18,2},{3,19},{19,3},{4,20},{20... | collective-permute-start | bytes 184328 | tf_op jit(solution)/shard_map/ppermute | solution.py:394
  77.1 1.7 %collective-permute-done.23.refs_3_ = bf16[96,320]{1,0:T(8,128)(2,1)S(1)} collective-permute-done((bf16[96,320]{1,0:T(8,128)(2,1)S(1)}, bf16[96,320]{1,0:T(8,128)(2,1)S(1)}, u32[]{:S(2)}, u32[]{:S(2)}) %collective-permute-start.23) | collective-permute-done | bytes 61472 | tf_op jit(solution)/shard_map/ppermute | solution.py:394
  79.6 1.2 %collective-permute-done.24 = f32[12,384]{1,0:T(8,128)S(1)} collective-permute-done((f32[12,384]{1,0:T(8,128)S(1)}, f32[12,384]{1,0:T(8,128)S(1)}, u32[]{:S(2)}, u32[]{:S(2)}) %collective-permute-start.24) | collective-permute-done | bytes 18464 | tf_op jit(solution)/shard_map/ppermute | solution.py:451
  80.8 1.5 %collective-permute-start.25 = (f32[12,384]{1,0:T(8,128)S(1)}, f32[12,384]{1,0:T(8,128)S(1)}, u32[]{:S(2)}, u32[]{:S(2)}) collective-permute-start(f32[12,384]{1,0:T(8,128)S(1)} %add.12), channel_id=1, source_target_pairs={{0,2},{1,3},{2,0},{3,1},{4,6},{5,7},{6,4},{7,5},{8,10},{9,11},{10,... | collective-permute-start | bytes 55304 | tf_op jit(solution)/shard_map/ppermute | solution.py:451
  82.3 2.3 %collective-permute-done.25 = f32[12,384]{1,0:T(8,128)S(1)} collective-permute-done((f32[12,384]{1,0:T(8,128)S(1)}, f32[12,384]{1,0:T(8,128)S(1)}, u32[]{:S(2)}, u32[]{:S(2)}) %collective-permute-start.25) | collective-permute-done | bytes 18464 | tf_op jit(solution)/shard_map/ppermute | solution.py:451
  85.6 1.5 %collective-permute-start.27 = (f32[1,96]{1,0:T(1,128)S(1)}, f32[1,96]{1,0:T(1,128)S(1)}, u32[]{:S(2)}, u32[]{:S(2)}) collective-permute-start(f32[1,96]{1,0:T(1,128)S(1)} %reshape.10), channel_id=1, source_target_pairs={{0,12},{4,8},{8,4},{12,0},{1,13},{5,9},{9,5},{13,1},{2,14},{6,10},... | collective-permute-start | bytes 1160 | tf_op jit(solution)/shard_map/ppermute | solution.py:461
  87.1 1.3 %collective-permute-start.28 = (f32[1,96]{1,0:T(1,128)S(1)}, f32[1,96]{1,0:T(1,128)S(1)}, u32[]{:S(2)}, u32[]{:S(2)}) collective-permute-start(f32[1,96]{1,0:T(1,128)S(1)} %reshape.10), channel_id=1, source_target_pairs={{0,8},{4,12},{8,0},{12,4},{1,9},{5,13},{9,1},{13,5},{2,10},{6,14},... | collective-permute-start | bytes 1160 | tf_op jit(solution)/shard_map/ppermute | solution.py:461
  88.4 2.5 %collective-permute-done.27 = f32[1,96]{1,0:T(1,128)S(1)} collective-permute-done((f32[1,96]{1,0:T(1,128)S(1)}, f32[1,96]{1,0:T(1,128)S(1)}, u32[]{:S(2)}, u32[]{:S(2)}) %collective-permute-start.27) | collective-permute-done | bytes 416 | tf_op jit(solution)/shard_map/ppermute | solution.py:461
  (75 shorter events, 12.9 us)
Async XLA Ops:
  4.2 9.5 %collective-permute-start = (bf16[48,2560]{1,0:T(8,128)(2,1)S(1)}, bf16[48,2560]{1,0:T(8,128)(2,1)S(1)}, u32[]{:S(2)}, u32[]{:S(2)}) collective-permute-start(bf16[48,2560]{1,0:T(8,128)(2,1)S(1)} %get-tuple-element.33), channel_id=1, source_target_pairs={{0,4},{12,8},{4,0},{8,12},{1,5},{13,9},{5,1},{9,13},{2,6},{14,10},... | collective-permute-start | bytes 737288 | tf_op jit(solution)/shard_map/ppermute | solution.py:375
  8.9 12.1 %collective-permute-start.3 = (bf16[48,2560]{1,0:T(8,128)(2,1)S(1)}, bf16[48,2560]{1,0:T(8,128)(2,1)S(1)}, u32[]{:S(2)}, u32[]{:S(2)}) collective-permute-start(bf16[48,2560]{1,0:T(8,128)(2,1)S(1)} %get-tuple-element.36.mine_ref), channel_id=1, source_target_pairs={{0,4},{12,8},{1,5},{13,9},{2,6},{14,10},{3,7},{15,11},{16,20},{28,... | collective-permute-start | bytes 737288 | tf_op jit(solution)/shard_map/ppermute | solution.py:375
  13.8 8.0 %collective-permute-start.2 = (bf16[48,2560]{1,0:T(8,128)(2,1)S(1)}, bf16[48,2560]{1,0:T(8,128)(2,1)S(1)}, u32[]{:S(2)}, u32[]{:S(2)}) collective-permute-start(bf16[48,2560]{1,0:T(8,128)(2,1)S(1)} %get-tuple-element.35.after_ref.mine_ref), channel_id=1, source_target_pairs={{4,8},{8,4},{5,9},{9,5},{6,10},{10,6},{7,11},{11,7},{20,24},{24,20... | collective-permute-start | bytes 737288 | tf_op jit(solution)/shard_map/ppermute | solution.py:375
  14.4 13.9 %collective-permute-start.1 = (bf16[48,2560]{1,0:T(8,128)(2,1)S(1)}, bf16[48,2560]{1,0:T(8,128)(2,1)S(1)}, u32[]{:S(2)}, u32[]{:S(2)}) collective-permute-start(bf16[48,2560]{1,0:T(8,128)(2,1)S(1)} %get-tuple-element.34), channel_id=1, source_target_pairs={{0,4},{12,8},{1,5},{13,9},{2,6},{14,10},{3,7},{15,11},{16,20},{28,... | collective-permute-start | bytes 737288 | tf_op jit(solution)/shard_map/ppermute | solution.py:375
  21.1 8.1 %collective-permute-start.6 = (bf16[48,2560]{1,0:T(8,128)(2,1)S(1)}, bf16[48,2560]{1,0:T(8,128)(2,1)S(1)}, u32[]{:S(2)}, u32[]{:S(2)}) collective-permute-start(bf16[48,2560]{1,0:T(8,128)(2,1)S(1)} %shard_map.116.after_ref.mine_ref), channel_id=1, source_target_pairs={{4,8},{8,4},{5,9},{9,5},{6,10},{10,6},{7,11},{11,7},{20,24},{24,20... | collective-permute-start | bytes 737288 | tf_op jit(solution)/shard_map/ppermute | solution.py:375
  21.8 11.1 %collective-permute-start.5 = (bf16[48,2560]{1,0:T(8,128)(2,1)S(1)}, bf16[48,2560]{1,0:T(8,128)(2,1)S(1)}, u32[]{:S(2)}, u32[]{:S(2)}) collective-permute-start(bf16[48,2560]{1,0:T(8,128)(2,1)S(1)} %get-tuple-element.39), channel_id=1, source_target_pairs={{0,4},{12,8},{4,0},{8,12},{1,5},{13,9},{5,1},{9,13},{2,6},{14,10},... | collective-permute-start | bytes 737288 | tf_op jit(solution)/shard_map/ppermute | solution.py:375
  26.8 39.8 %collective-permute-start.16 = (bf16[320,1664]{1,0:T(8,128)(2,1)S(1)}, bf16[320,1664]{1,0:T(8,128)(2,1)S(1)}, u32[]{:S(2)}, u32[]{:S(2)}) collective-permute-start(bf16[320,1664]{1,0:T(8,128)(2,1)S(1)} %get-tuple-element.51), channel_id=1, source_target_pairs={{0,16},{16,0},{1,17},{17,1},{2,18},{18,2},{3,19},{19,3},{4,20},{20... | collective-permute-start | bytes 3194888 | tf_op jit(solution)/shard_map/ppermute | solution.py:387
  28.4 5.2 %collective-permute-start.4 = (bf16[48,2560]{1,0:T(8,128)(2,1)S(1)}, bf16[48,2560]{1,0:T(8,128)(2,1)S(1)}, u32[]{:S(2)}, u32[]{:S(2)}) collective-permute-start(bf16[48,2560]{1,0:T(8,128)(2,1)S(1)} %shard_map.118.after_ref.mine_ref), channel_id=1, source_target_pairs={{4,8},{8,4},{5,9},{9,5},{6,10},{10,6},{7,11},{11,7},{20,24},{24,20... | collective-permute-start | bytes 737288 | tf_op jit(solution)/shard_map/ppermute | solution.py:375
  29.2 10.5 %collective-permute-start.8 = (bf16[48,2560]{1,0:T(8,128)(2,1)S(1)}, bf16[48,2560]{1,0:T(8,128)(2,1)S(1)}, u32[]{:S(2)}, u32[]{:S(2)}) collective-permute-start(bf16[48,2560]{1,0:T(8,128)(2,1)S(1)} %get-tuple-element.43), channel_id=1, source_target_pairs={{0,4},{12,8},{4,0},{8,12},{1,5},{13,9},{5,1},{9,13},{2,6},{14,10},... | collective-permute-start | bytes 737288 | tf_op jit(solution)/shard_map/ppermute | solution.py:375
  33.0 7.5 %collective-permute-start.9 = (bf16[48,2560]{1,0:T(8,128)(2,1)S(1)}, bf16[48,2560]{1,0:T(8,128)(2,1)S(1)}, u32[]{:S(2)}, u32[]{:S(2)}) collective-permute-start(bf16[48,2560]{1,0:T(8,128)(2,1)S(1)} %shard_map.120.after_ref.mine_ref), channel_id=1, source_target_pairs={{4,8},{8,4},{5,9},{9,5},{6,10},{10,6},{7,11},{11,7},{20,24},{24,20... | collective-permute-start | bytes 737288 | tf_op jit(solution)/shard_map/ppermute | solution.py:375
  33.7 12.6 %collective-permute-start.7 = (bf16[48,2560]{1,0:T(8,128)(2,1)S(1)}, bf16[48,2560]{1,0:T(8,128)(2,1)S(1)}, u32[]{:S(2)}, u32[]{:S(2)}) collective-permute-start(bf16[48,2560]{1,0:T(8,128)(2,1)S(1)} %get-tuple-element.42), channel_id=1, source_target_pairs={{0,4},{12,8},{4,0},{8,12},{1,5},{13,9},{5,1},{9,13},{2,6},{14,10},... | collective-permute-start | bytes 737288 | tf_op jit(solution)/shard_map/ppermute | solution.py:375
  39.7 7.4 %collective-permute-start.12 = (bf16[48,2560]{1,0:T(8,128)(2,1)S(1)}, bf16[48,2560]{1,0:T(8,128)(2,1)S(1)}, u32[]{:S(2)}, u32[]{:S(2)}) collective-permute-start(bf16[48,2560]{1,0:T(8,128)(2,1)S(1)} %shard_map.123.after_ref.mine_ref), channel_id=1, source_target_pairs={{4,8},{8,4},{5,9},{9,5},{6,10},{10,6},{7,11},{11,7},{20,24},{24,20... | collective-permute-start | bytes 737288 | tf_op jit(solution)/shard_map/ppermute | solution.py:375
  40.5 10.8 %collective-permute-start.11 = (bf16[48,2560]{1,0:T(8,128)(2,1)S(1)}, bf16[48,2560]{1,0:T(8,128)(2,1)S(1)}, u32[]{:S(2)}, u32[]{:S(2)}) collective-permute-start(bf16[48,2560]{1,0:T(8,128)(2,1)S(1)} %get-tuple-element.47), channel_id=1, source_target_pairs={{0,4},{12,8},{4,0},{8,12},{1,5},{13,9},{5,1},{9,13},{2,6},{14,10},... | collective-permute-start | bytes 737288 | tf_op jit(solution)/shard_map/ppermute | solution.py:375
  44.8 21.7 %collective-permute-start.17 = (bf16[320,896]{1,0:T(8,128)(2,1)S(1)}, bf16[320,896]{1,0:T(8,128)(2,1)S(1)}, u32[]{:S(2)}, u32[]{:S(2)}) collective-permute-start(bf16[320,896]{1,0:T(8,128)(2,1)S(1)} %get-tuple-element.52), channel_id=1, source_target_pairs={{0,16},{16,0},{1,17},{17,1},{2,18},{18,2},{3,19},{19,3},{4,20},{20... | collective-permute-start | bytes 1720328 | tf_op jit(solution)/shard_map/ppermute | solution.py:387
  46.5 5.6 %collective-permute-start.10 = (bf16[48,2560]{1,0:T(8,128)(2,1)S(1)}, bf16[48,2560]{1,0:T(8,128)(2,1)S(1)}, u32[]{:S(2)}, u32[]{:S(2)}) collective-permute-start(bf16[48,2560]{1,0:T(8,128)(2,1)S(1)} %shard_map.126.after_ref.mine_ref), channel_id=1, source_target_pairs={{4,8},{8,4},{5,9},{9,5},{6,10},{10,6},{7,11},{11,7},{20,24},{24,20... | collective-permute-start | bytes 737288 | tf_op jit(solution)/shard_map/ppermute | solution.py:375
  47.2 10.3 %collective-permute-start.14 = (bf16[48,2560]{1,0:T(8,128)(2,1)S(1)}, bf16[48,2560]{1,0:T(8,128)(2,1)S(1)}, u32[]{:S(2)}, u32[]{:S(2)}) collective-permute-start(bf16[48,2560]{1,0:T(8,128)(2,1)S(1)} %get-tuple-element.50), channel_id=1, source_target_pairs={{0,4},{12,8},{4,0},{8,12},{1,5},{13,9},{5,1},{9,13},{2,6},{14,10},... | collective-permute-start | bytes 737288 | tf_op jit(solution)/shard_map/ppermute | solution.py:375
  51.4 9.3 %collective-permute-start.15 = (bf16[48,2560]{1,0:T(8,128)(2,1)S(1)}, bf16[48,2560]{1,0:T(8,128)(2,1)S(1)}, u32[]{:S(2)}, u32[]{:S(2)}) collective-permute-start(bf16[48,2560]{1,0:T(8,128)(2,1)S(1)} %shard_map.129.after_ref.mine_ref), channel_id=1, source_target_pairs={{4,8},{8,4},{5,9},{9,5},{6,10},{10,6},{7,11},{11,7},{20,24},{24,20... | collective-permute-start | bytes 737288 | tf_op jit(solution)/shard_map/ppermute | solution.py:375
  52.1 13.1 %collective-permute-start.13 = (bf16[48,2560]{1,0:T(8,128)(2,1)S(1)}, bf16[48,2560]{1,0:T(8,128)(2,1)S(1)}, u32[]{:S(2)}, u32[]{:S(2)}) collective-permute-start(bf16[48,2560]{1,0:T(8,128)(2,1)S(1)} %shard_map.130.after_ref.mine_ref), channel_id=1, source_target_pairs={{4,0},{8,12},{5,1},{9,13},{6,2},{10,14},{7,3},{11,15},{20,16},{24,... | collective-permute-start | bytes 737288 | tf_op jit(solution)/shard_map/ppermute | solution.py:375
  57.6 11.7 %collective-permute-start.18 = (bf16[48,2560]{1,0:T(8,128)(2,1)S(1)}, bf16[48,2560]{1,0:T(8,128)(2,1)S(1)}, u32[]{:S(2)}, u32[]{:S(2)}) collective-permute-start(bf16[48,2560]{1,0:T(8,128)(2,1)S(1)} %shard_map.132.after_ref.mine_ref), channel_id=1, source_target_pairs={{0,8},{2,10},{4,12},{6,14},{8,0},{10,2},{12,4},{14,6},{16,24},{18,... | collective-permute-start | bytes 737288 | tf_op jit(solution)/shard_map/ppermute | solution.py:380
  60.7 8.7 %collective-permute-start.19 = (bf16[48,2560]{1,0:T(8,128)(2,1)S(1)}, bf16[48,2560]{1,0:T(8,128)(2,1)S(1)}, u32[]{:S(2)}, u32[]{:S(2)}) collective-permute-start(bf16[48,2560]{1,0:T(8,128)(2,1)S(1)} %shard_map.132.after_ref.mine_ref), channel_id=1, source_target_pairs={{5,9},{7,11},{9,5},{11,7},{21,25},{23,27},{25,21},{27,23}} | collective-permute-start | bytes 737288 | tf_op jit(solution)/shard_map/ppermute | solution.py:380
  65.2 8.3 %collective-permute-start.21 = (bf16[48,2560]{1,0:T(8,128)(2,1)S(1)}, bf16[48,2560]{1,0:T(8,128)(2,1)S(1)}, u32[]{:S(2)}, u32[]{:S(2)}) collective-permute-start(bf16[48,2560]{1,0:T(8,128)(2,1)S(1)} %shard_map.133.after_ref.mine_ref), channel_id=1, source_target_pairs={{4,0},{8,12},{5,1},{9,13},{6,2},{10,14},{7,3},{11,15},{20,16},{24,... | collective-permute-start | bytes 737288 | tf_op jit(solution)/shard_map/ppermute | solution.py:375
  69.5 4.1 %collective-permute-start.20 = (bf16[48,2560]{1,0:T(8,128)(2,1)S(1)}, bf16[48,2560]{1,0:T(8,128)(2,1)S(1)}, u32[]{:S(2)}, u32[]{:S(2)}) collective-permute-start(bf16[48,2560]{1,0:T(8,128)(2,1)S(1)} %shard_map.139.after_ref.mine_ref), channel_id=1, source_target_pairs={{5,1},{7,3},{9,13},{11,15},{21,17},{23,19},{25,29},{27,31}} | collective-permute-start | bytes 737288 | tf_op jit(solution)/shard_map/ppermute | solution.py:380
  70.1 6.9 %collective-permute-start.22 = (bf16[288,320]{1,0:T(8,128)(2,1)S(1)}, bf16[288,320]{1,0:T(8,128)(2,1)S(1)}, u32[]{:S(2)}, u32[]{:S(2)}) collective-permute-start(bf16[288,320]{1,0:T(8,128)(2,1)S(1)} %shard_map.137.after_ref), channel_id=1, source_target_pairs={{0,16},{16,0},{1,17},{17,1},{2,18},{18,2},{3,19},{19,3},{4,20},{20... | collective-permute-start | bytes 552968 | tf_op jit(solution)/shard_map/ppermute | solution.py:394
  74.3 14.1 %copy-start.2 = (s32[128]{0:T(128)S(1)}, s32[128]{0:T(128)}, u32[]{:S(2)}) copy-start(s32[128]{0:T(128)} %param.19) | copy-start | bytes 1540
  74.3 14.1 %copy-start.3 = (s32[128]{0:T(128)S(1)}, s32[128]{0:T(128)}, u32[]{:S(2)}) copy-start(s32[128]{0:T(128)} %param.17) | copy-start | bytes 1540
  74.3 14.1 %copy-start.4 = (s32[128,1]{0,1:T(1,128)S(1)}, s32[128,1]{0,1:T(1,128)}, u32[]{:S(2)}) copy-start(s32[128,1]{0,1:T(1,128)} %param.18) | copy-start | bytes 1540
  74.3 4.4 %collective-permute-start.23 = (bf16[96,320]{1,0:T(8,128)(2,1)S(1)}, bf16[96,320]{1,0:T(8,128)(2,1)S(1)}, u32[]{:S(2)}, u32[]{:S(2)}) collective-permute-start(bf16[96,320]{1,0:T(8,128)(2,1)S(1)} %shard_map.142.after_ref), channel_id=1, source_target_pairs={{0,16},{16,0},{1,17},{17,1},{2,18},{18,2},{3,19},{19,3},{4,20},{20... | collective-permute-start | bytes 184328 | tf_op jit(solution)/shard_map/ppermute | solution.py:394
  79.6 1.2 %collective-permute-start.24 = (f32[12,384]{1,0:T(8,128)S(1)}, f32[12,384]{1,0:T(8,128)S(1)}, u32[]{:S(2)}, u32[]{:S(2)}) collective-permute-start(f32[12,384]{1,0:T(8,128)S(1)} %shard_map.144), channel_id=1, source_target_pairs={{0,1},{1,0},{2,3},{3,2},{4,5},{5,4},{6,7},{7,6},{8,9},{9,8},{10,11... | collective-permute-start | bytes 55304 | tf_op jit(solution)/shard_map/ppermute | solution.py:451
  80.8 3.8 %collective-permute-start.25 = (f32[12,384]{1,0:T(8,128)S(1)}, f32[12,384]{1,0:T(8,128)S(1)}, u32[]{:S(2)}, u32[]{:S(2)}) collective-permute-start(f32[12,384]{1,0:T(8,128)S(1)} %add.12), channel_id=1, source_target_pairs={{0,2},{1,3},{2,0},{3,1},{4,6},{5,7},{6,4},{7,5},{8,10},{9,11},{10,... | collective-permute-start | bytes 55304 | tf_op jit(solution)/shard_map/ppermute | solution.py:451
  84.8 3.6 %collective-permute-start.26 = (f32[1,96]{1,0:T(1,128)S(1)}, f32[1,96]{1,0:T(1,128)S(1)}, u32[]{:S(2)}, u32[]{:S(2)}) collective-permute-start(f32[1,96]{1,0:T(1,128)S(1)} %reshape.10), channel_id=1, source_target_pairs={{0,4},{4,0},{8,12},{12,8},{1,5},{5,1},{9,13},{13,9},{2,6},{6,2},{1... | collective-permute-start | bytes 1160 | tf_op jit(solution)/shard_map/ppermute | solution.py:461
  85.6 5.3 %collective-permute-start.27 = (f32[1,96]{1,0:T(1,128)S(1)}, f32[1,96]{1,0:T(1,128)S(1)}, u32[]{:S(2)}, u32[]{:S(2)}) collective-permute-start(f32[1,96]{1,0:T(1,128)S(1)} %reshape.10), channel_id=1, source_target_pairs={{0,12},{4,8},{8,4},{12,0},{1,13},{5,9},{9,5},{13,1},{2,14},{6,10},... | collective-permute-start | bytes 1160 | tf_op jit(solution)/shard_map/ppermute | solution.py:461
  87.1 4.4 %collective-permute-start.28 = (f32[1,96]{1,0:T(1,128)S(1)}, f32[1,96]{1,0:T(1,128)S(1)}, u32[]{:S(2)}, u32[]{:S(2)}) collective-permute-start(f32[1,96]{1,0:T(1,128)S(1)} %reshape.10), channel_id=1, source_target_pairs={{0,8},{4,12},{8,0},{12,4},{1,9},{5,13},{9,1},{13,5},{2,10},{6,14},... | collective-permute-start | bytes 1160 | tf_op jit(solution)/shard_map/ppermute | solution.py:461
  (2 other events, 12.2 us)

commit v19 on v18

--- a/solution.py
+++ b/solution.py
@@ -176,21 +176,6 @@
         out_specs=VMEM,
         compiler_params=pltpu.CompilerParams(vmem_limit_bytes=8 * MIB),
     )(mine, came, early, after)
-
-
-def join_kernel(mine_ref, one_ref, two_ref, after_ref, out_ref):
-    came = one_ref[...].astype(jnp.float32) + two_ref[...].astype(jnp.float32)
-    out_ref[...] = (mine_ref[...].astype(jnp.float32) + came).astype(jnp.bfloat16)
-
-
-def join(after, mine, one, two):
-    return pl.pallas_call(
-        join_kernel,
-        out_shape=bf16(*mine.shape),
-        in_specs=[VMEM, VMEM, VMEM, ANY],
-        out_specs=VMEM,
-        compiler_params=pltpu.CompilerParams(vmem_limit_bytes=8 * MIB),
-    )(mine, one, two, after)
 
 
 def late_kernel(mine_ref, came_ref, after_ref, out_ref):
@@ -375,8 +360,8 @@
         return lax.ppermute(value, "dp", pairs)
 
     short = n == 4
-    def on_cores(core, value, pairs):
-        pairs = [(a * layers + i, b * layers + i) for a, b in pairs for i in range(core, layers, 2)]
+    def on_cores(value, *pairs):
+        pairs = [(a * layers + i, b * layers + i) for i in range(layers) for a, b in pairs[i % 2]]
         return lax.ppermute(value, ("dp", "layer"), pairs)
 
     part, came = list(own), [None] * chunks
@@ -406,13 +391,11 @@
             if short and c == chunks - 1:
                 if s == 0:
                     after = part[c] = pair(after, own[c], came[c], early)
-                    came[c] = [
-                        on_cores(0, part[c], [(i, i ^ 2) for i in range(n)]),
-                        on_cores(1, part[c], [(1, 2), (2, 1)]),
-                    ]
+                    came[c] = on_cores(part[c], [(i, i ^ 2) for i in range(n)], [(1, 2), (2, 1)])
                 elif s == 1:
-                    after = part[c] = join(after, part[c], *came[c])
-                    came[c] = on_cores(1, part[c], [(1, 0), (2, 3)])
+                    part[c], _ = total(after, part[c], came[c])
+                    after = part[c]
+                    came[c] = on_cores(part[c], [], [(1, 0), (2, 3)])
                 continue
             later = turn + ahead if turn + ahead < chunks else None
             if turn >= last - 1:

time: 92.8 us -> 91.8 us (0.989)
  starting transfers between devices: 55.1 us -> 49.4 us
  waiting for transfers between devices: 22.8 us -> 27.6 us
    ppermute x3 -> x2, waiting for transfers between devices: 0.87 us -> 3.69 us  [on_cores(): return lax.ppermute(value, ('dp', 'layer'), pairs)]
    ppermute x2, starting transfers between devices: 3.58 us -> 1.52 us  [project_waiting(): back.append(lax.ppermute(away, 'parts', swap))]
    ppermute x17, starting transfers between devices: 39 us -> 37 us  [transfer(): return lax.ppermute(value, 'dp', pairs)]
    ppermute x17, waiting for transfers between devices: 13.6 us -> 15.1 us  [transfer(): return lax.ppermute(value, 'dp', pairs)]
    ppermute x2, waiting for transfers between devices: 1.67 us -> 2.98 us  [project_waiting(): back.append(lax.ppermute(away, 'parts', swap))]
    ppermute x2, starting transfers between devices: 3.09 us -> 2.16 us  [per_device(): others = [lax.ppermute(piece, 'parts', swap) for piece in theirs]]
    ppermute x3 -> x2, starting transfers between devices: 4.38 us -> 3.69 us  [on_cores(): return lax.ppermute(value, ('dp', 'layer'), pairs)]
  transfers between devices with their start and end apart: 29 -> 28, of which waited for: 11 -> 14; matrix products, arithmetic and copies ran while one was open for 0% -> 0% of each run, Pallas kernels for 9% -> 9%
where the time goes in v19:
time: 91.8 us; the launch traced here: 91.4 us
  starting transfers between devices  49.4 us (54%)
  waiting for transfers between devices  27.6 us (30%)
  Pallas kernels  12.3 us (13%)
  between operations  1.1 us (1%)
    ppermute x17, starting transfers between devices, transfer(): return lax.ppermute(value, 'dp', pairs)  37 us
    ppermute x17, waiting for transfers between devices, transfer(): return lax.ppermute(value, 'dp', pairs)  15.1 us
    ppermute x2, starting transfers between devices, on_cores(): return lax.ppermute(value, ('dp', 'layer'), pairs)  3.69 us
    ppermute x2, waiting for transfers between devices, on_cores(): return lax.ppermute(value, ('dp', 'layer'), pairs)  3.69 us
    pallas_call x1, Pallas kernels, first_pull(): pl.pallas_call(first_pull_kernel, out_shape=[bf16(rows, features)] * 2 +...  3.6 us
    ppermute x3, starting transfers between devices, per_device(): lax.ppermute(flat, 'dp', [(i, i ^ k ^ k >> 1) for i in range(n)])  3.55 us
    ppermute x2, waiting for transfers between devices, per_device(): lax.ppermute(scores, 'layer', [(i, i ^ step) for i in range(layers)])  3.52 us
    pallas_call x4, Pallas kernels, project(): pl.pallas_call(functools.partial(project_kernel, len(tokens)), out_shape=...  3.17 us
  transfers between devices with their start and end apart: 28, of which 14 were waited for; matrix products, arithmetic and copies ran while one was open for 0% of the time, Pallas kernels for 9%

profile of v19, /device:TPU:0, one launch (start us, length us, event | category | flops | bytes accessed | tf_op | source)
XLA Modules:
  0.0 91.4 jit_solution(4237962749507055661)
XLA Ops:
  0.6 3.6 %shard_map.113 = (bf16[48,2560]{1,0:T(8,128)(2,1)S(1)}, bf16[48,2560]{1,0:T(8,128)(2,1)S(1)}, bf16[2560,640]{1,0:T(8,128)(2,1)S(1)}, bf16[640,384]{1,0:T(8,128)(2,1)}, bf16[384,640]{1,0:T(8,128)(2,1)S(1)}) custom-call(bf16[2560,640]{1,0:T(8,128)(2,1)} %bitcast.16, bf16[2560,640]{1,0:T(8,128)(2,1)} %bitcast.17, bf16[640,384]{1,0:T(8,128)(2,1)} %bitcast.20, ...), custom_call_target="tpu_custom_call" | custom-call | tf_op jit(solution)/shard_map/pallas_call | solution.py:77
  4.2 3.1 %collective-permute-start = (bf16[48,2560]{1,0:T(8,128)(2,1)S(1)}, bf16[48,2560]{1,0:T(8,128)(2,1)S(1)}, u32[]{:S(2)}, u32[]{:S(2)}) collective-permute-start(bf16[48,2560]{1,0:T(8,128)(2,1)S(1)} %get-tuple-element.33), channel_id=1, source_target_pairs={{0,4},{12,8},{4,0},{8,12},{1,5},{13,9},{5,1},{9,13},{2,6},{14,10},... | collective-permute-start | bytes 737288 | tf_op jit(solution)/shard_map/ppermute | solution.py:360
  7.3 1.5 %shard_map.114 = (bf16[48,2560]{1,0:T(8,128)(2,1)S(1)}, bf16[48,2560]{1,0:T(8,128)(2,1)S(1)}, bf16[48,2560]{1,0:T(8,128)(2,1)S(1)}, bf16[48,2560]{1,0:T(8,128)(2...) custom-call(bf16[384,640]{1,0:T(8,128)(2,1)S(1)} %get-tuple-element.28.turned_ref,, ...), custom_call_target="tpu_custom_call" | custom-call | tf_op jit(solution)/shard_map/pallas_call | solution.py:101
  8.9 1.9 %collective-permute-start.3 = (bf16[48,2560]{1,0:T(8,128)(2,1)S(1)}, bf16[48,2560]{1,0:T(8,128)(2,1)S(1)}, u32[]{:S(2)}, u32[]{:S(2)}) collective-permute-start(bf16[48,2560]{1,0:T(8,128)(2,1)S(1)} %get-tuple-element.36.mine_ref), channel_id=1, source_target_pairs={{0,4},{12,8},{1,5},{13,9},{2,6},{14,10},{3,7},{15,11},{16,20},{28,... | collective-permute-start | bytes 737288 | tf_op jit(solution)/shard_map/ppermute | solution.py:360
  10.8 2.9 %collective-permute-done.came_ref.early_ref = bf16[48,2560]{1,0:T(8,128)(2,1)S(1)} collective-permute-done((bf16[48,2560]{1,0:T(8,128)(2,1)S(1)}, bf16[48,2560]{1,0:T(8,128)(2,1)S(1)}, u32[]{:S(2)}, u32[]{:S(2)}) %collective-permute-start) | collective-permute-done | bytes 245792 | tf_op jit(solution)/shard_map/ppermute | solution.py:360
  14.4 6.5 %collective-permute-start.1 = (bf16[48,2560]{1,0:T(8,128)(2,1)S(1)}, bf16[48,2560]{1,0:T(8,128)(2,1)S(1)}, u32[]{:S(2)}, u32[]{:S(2)}) collective-permute-start(bf16[48,2560]{1,0:T(8,128)(2,1)S(1)} %get-tuple-element.34), channel_id=1, source_target_pairs={{0,4},{12,8},{1,5},{13,9},{2,6},{14,10},{3,7},{15,11},{16,20},{28,... | collective-permute-start | bytes 737288 | tf_op jit(solution)/shard_map/ppermute | solution.py:360
  21.7 1.9 %shard_map.136 = (bf16[320,2560]{1,0:T(8,128)(2,1)S(1)}, bf16[320,1664]{1,0:T(8,128)(2,1)S(1)}, bf16[320,896]{1,0:T(8,128)(2,1)S(1)}) custom-call(bf16[320,2560]{1,0:T(8,128)(2,1)} %bitcast.18, bf16[320,2560]{1,0:T(8,128)(2,1)} %bitcast.19, bf16[48,2560]{1,0:T(8,128)(2,1)S(1)} %get-tuple-element.48.rest_0_.mine_ref.after_ref), custom_call_target="tpu_custom_call" | custom-call | tf_op jit(solution)/shard_map/pallas_call | solution.py:140
  23.7 1.6 %collective-permute-start.16 = (bf16[320,1664]{1,0:T(8,128)(2,1)S(1)}, bf16[320,1664]{1,0:T(8,128)(2,1)S(1)}, u32[]{:S(2)}, u32[]{:S(2)}) collective-permute-start(bf16[320,1664]{1,0:T(8,128)(2,1)S(1)} %get-tuple-element.51), channel_id=1, source_target_pairs={{0,16},{16,0},{1,17},{17,1},{2,18},{18,2},{3,19},{19,3},{4,20},{20... | collective-permute-start | bytes 3194888 | tf_op jit(solution)/shard_map/ppermute | solution.py:372
  25.3 2.2 %collective-permute-start.5 = (bf16[48,2560]{1,0:T(8,128)(2,1)S(1)}, bf16[48,2560]{1,0:T(8,128)(2,1)S(1)}, u32[]{:S(2)}, u32[]{:S(2)}) collective-permute-start(bf16[48,2560]{1,0:T(8,128)(2,1)S(1)} %get-tuple-element.39), channel_id=1, source_target_pairs={{0,4},{12,8},{4,0},{8,12},{1,5},{13,9},{5,1},{9,13},{2,6},{14,10},... | collective-permute-start | bytes 737288 | tf_op jit(solution)/shard_map/ppermute | solution.py:360
  28.4 2.3 %collective-permute-start.8 = (bf16[48,2560]{1,0:T(8,128)(2,1)S(1)}, bf16[48,2560]{1,0:T(8,128)(2,1)S(1)}, u32[]{:S(2)}, u32[]{:S(2)}) collective-permute-start(bf16[48,2560]{1,0:T(8,128)(2,1)S(1)} %get-tuple-element.43), channel_id=1, source_target_pairs={{0,4},{12,8},{4,0},{8,12},{1,5},{13,9},{5,1},{9,13},{2,6},{14,10},... | collective-permute-start | bytes 737288 | tf_op jit(solution)/shard_map/ppermute | solution.py:360
  30.7 3.7 %collective-permute-done.5.came_ref = bf16[48,2560]{1,0:T(8,128)(2,1)S(1)} collective-permute-done((bf16[48,2560]{1,0:T(8,128)(2,1)S(1)}, bf16[48,2560]{1,0:T(8,128)(2,1)S(1)}, u32[]{:S(2)}, u32[]{:S(2)}) %collective-permute-start.5) | collective-permute-done | bytes 245792 | tf_op jit(solution)/shard_map/ppermute | solution.py:360
  35.2 3.3 %collective-permute-start.7 = (bf16[48,2560]{1,0:T(8,128)(2,1)S(1)}, bf16[48,2560]{1,0:T(8,128)(2,1)S(1)}, u32[]{:S(2)}, u32[]{:S(2)}) collective-permute-start(bf16[48,2560]{1,0:T(8,128)(2,1)S(1)} %get-tuple-element.42), channel_id=1, source_target_pairs={{0,4},{12,8},{4,0},{8,12},{1,5},{13,9},{5,1},{9,13},{2,6},{14,10},... | collective-permute-start | bytes 737288 | tf_op jit(solution)/shard_map/ppermute | solution.py:360
  38.6 1.1 %collective-permute-done.8.came_ref = bf16[48,2560]{1,0:T(8,128)(2,1)S(1)} collective-permute-done((bf16[48,2560]{1,0:T(8,128)(2,1)S(1)}, bf16[48,2560]{1,0:T(8,128)(2,1)S(1)}, u32[]{:S(2)}, u32[]{:S(2)}) %collective-permute-start.8) | collective-permute-done | bytes 245792 | tf_op jit(solution)/shard_map/ppermute | solution.py:360
  41.0 6.0 %collective-permute-start.11 = (bf16[48,2560]{1,0:T(8,128)(2,1)S(1)}, bf16[48,2560]{1,0:T(8,128)(2,1)S(1)}, u32[]{:S(2)}, u32[]{:S(2)}) collective-permute-start(bf16[48,2560]{1,0:T(8,128)(2,1)S(1)} %get-tuple-element.47), channel_id=1, source_target_pairs={{0,4},{12,8},{4,0},{8,12},{1,5},{13,9},{5,1},{9,13},{2,6},{14,10},... | collective-permute-start | bytes 737288 | tf_op jit(solution)/shard_map/ppermute | solution.py:360
  47.9 4.2 %collective-permute-start.14 = (bf16[48,2560]{1,0:T(8,128)(2,1)S(1)}, bf16[48,2560]{1,0:T(8,128)(2,1)S(1)}, u32[]{:S(2)}, u32[]{:S(2)}) collective-permute-start(bf16[48,2560]{1,0:T(8,128)(2,1)S(1)} %get-tuple-element.50), channel_id=1, source_target_pairs={{0,4},{12,8},{4,0},{8,12},{1,5},{13,9},{5,1},{9,13},{2,6},{14,10},... | collective-permute-start | bytes 737288 | tf_op jit(solution)/shard_map/ppermute | solution.py:360
  53.6 1.3 %collective-permute-start.13 = (bf16[48,2560]{1,0:T(8,128)(2,1)S(1)}, bf16[48,2560]{1,0:T(8,128)(2,1)S(1)}, u32[]{:S(2)}, u32[]{:S(2)}) collective-permute-start(bf16[48,2560]{1,0:T(8,128)(2,1)S(1)} %shard_map.130.after_ref.mine_ref), channel_id=1, source_target_pairs={{4,0},{8,12},{5,1},{9,13},{6,2},{10,14},{7,3},{11,15},{20,16},{24,... | collective-permute-start | bytes 737288 | tf_op jit(solution)/shard_map/ppermute | solution.py:360
  55.0 3.7 %collective-permute-done.14.came_ref = bf16[48,2560]{1,0:T(8,128)(2,1)S(1)} collective-permute-done((bf16[48,2560]{1,0:T(8,128)(2,1)S(1)}, bf16[48,2560]{1,0:T(8,128)(2,1)S(1)}, u32[]{:S(2)}, u32[]{:S(2)}) %collective-permute-start.14) | collective-permute-done | bytes 245792 | tf_op jit(solution)/shard_map/ppermute | solution.py:360
  58.8 3.0 %collective-permute-start.18 = (bf16[48,2560]{1,0:T(8,128)(2,1)S(1)}, bf16[48,2560]{1,0:T(8,128)(2,1)S(1)}, u32[]{:S(2)}, u32[]{:S(2)}) collective-permute-start(bf16[48,2560]{1,0:T(8,128)(2,1)S(1)} %shard_map.132.after_ref.mine_ref), channel_id=1, source_target_pairs={{0,8},{4,12},{8,0},{12,4},{5,9},{9,5},{2,10},{6,14},{10,2},{14,6},... | collective-permute-start | bytes 737288 | tf_op jit(solution)/shard_map/ppermute | solution.py:365
  61.9 1.3 %collective-permute-start.20 = (bf16[48,2560]{1,0:T(8,128)(2,1)S(1)}, bf16[48,2560]{1,0:T(8,128)(2,1)S(1)}, u32[]{:S(2)}, u32[]{:S(2)}) collective-permute-start(bf16[48,2560]{1,0:T(8,128)(2,1)S(1)} %shard_map.133.after_ref.mine_ref), channel_id=1, source_target_pairs={{4,0},{8,12},{5,1},{9,13},{6,2},{10,14},{7,3},{11,15},{20,16},{24,... | collective-permute-start | bytes 737288 | tf_op jit(solution)/shard_map/ppermute | solution.py:360
  63.2 1.1 %collective-permute-done.13.came_ref = bf16[48,2560]{1,0:T(8,128)(2,1)S(1)} collective-permute-done((bf16[48,2560]{1,0:T(8,128)(2,1)S(1)}, bf16[48,2560]{1,0:T(8,128)(2,1)S(1)}, u32[]{:S(2)}, u32[]{:S(2)}) %collective-permute-start.13) | collective-permute-done | bytes 245792 | tf_op jit(solution)/shard_map/ppermute | solution.py:360
  64.4 1.0 %shard_map.137.after_ref = bf16[288,320]{1,0:T(8,128)(2,1)S(1)} custom-call(bf16[48,2560]{1,0:T(8,128)(2,1)S(1)} %shard_map.135.after_ref.rest_7_.rest_6_, bf16[320,1664]{1,0:T(8,128)(2,1)S(1)} %collective-permute-done.16.rest_0_, bf16[320,896]{1,0:T(8,128)(2,1)S(1)} %collective-permute-done.17.rest_1_, ...), custom_call_target="tpu_custom_call" | custom-call | tf_op jit(solution)/shard_map/pallas_call | solution.py:263
  65.4 0.9 %shard_map.138.after_ref.refs_0_ = f32[288,320]{1,0:T(8,128)S(1)} custom-call(bf16[288,320]{1,0:T(8,128)(2,1)S(1)} %shard_map.137.after_ref, bf16[320,2560]{1,0:T(8,128)(2,1)S(1)} %get-tuple-element.53.rest_0_, bf16[48,2560]{1,0:T(8,128)(2,1)S(1)} %shard_map.122.after_ref.rest_2_.rest_1_, bf16[48,2560]{1,0:T(8,128)(2,1)S(1)} %shard_map.125.after_ref.rest_3_.rest_2_, ...), custom_call_target="tpu_custom_call" | custom-call | tf_op jit(solution)/shard_map/pallas_call | solution.py:263
  66.3 3.7 %collective-permute-done.18.came_ref = bf16[48,2560]{1,0:T(8,128)(2,1)S(1)} collective-permute-done((bf16[48,2560]{1,0:T(8,128)(2,1)S(1)}, bf16[48,2560]{1,0:T(8,128)(2,1)S(1)}, u32[]{:S(2)}, u32[]{:S(2)}) %collective-permute-start.18) | collective-permute-done | bytes 245792 | tf_op jit(solution)/shard_map/ppermute | solution.py:365
  71.5 2.0 %collective-permute-done.20.came_ref = bf16[48,2560]{1,0:T(8,128)(2,1)S(1)} collective-permute-done((bf16[48,2560]{1,0:T(8,128)(2,1)S(1)}, bf16[48,2560]{1,0:T(8,128)(2,1)S(1)}, u32[]{:S(2)}, u32[]{:S(2)}) %collective-permute-start.20) | collective-permute-done | bytes 245792 | tf_op jit(solution)/shard_map/ppermute | solution.py:360
  75.7 1.8 %collective-permute-done.21.refs_2_ = bf16[288,320]{1,0:T(8,128)(2,1)S(1)} collective-permute-done((bf16[288,320]{1,0:T(8,128)(2,1)S(1)}, bf16[288,320]{1,0:T(8,128)(2,1)S(1)}, u32[]{:S(2)}, u32[]{:S(2)}) %collective-permute-start.21) | collective-permute-done | bytes 184352 | tf_op jit(solution)/shard_map/ppermute | solution.py:379
  77.5 1.1 %collective-permute-done.22.refs_3_ = bf16[96,320]{1,0:T(8,128)(2,1)S(1)} collective-permute-done((bf16[96,320]{1,0:T(8,128)(2,1)S(1)}, bf16[96,320]{1,0:T(8,128)(2,1)S(1)}, u32[]{:S(2)}, u32[]{:S(2)}) %collective-permute-start.22) | collective-permute-done | bytes 61472 | tf_op jit(solution)/shard_map/ppermute | solution.py:379
  79.6 1.2 %collective-permute-done.23 = f32[12,384]{1,0:T(8,128)S(1)} collective-permute-done((f32[12,384]{1,0:T(8,128)S(1)}, f32[12,384]{1,0:T(8,128)S(1)}, u32[]{:S(2)}, u32[]{:S(2)}) %collective-permute-start.23) | collective-permute-done | bytes 18464 | tf_op jit(solution)/shard_map/ppermute | solution.py:434
  80.7 1.5 %collective-permute-start.24 = (f32[12,384]{1,0:T(8,128)S(1)}, f32[12,384]{1,0:T(8,128)S(1)}, u32[]{:S(2)}, u32[]{:S(2)}) collective-permute-start(f32[12,384]{1,0:T(8,128)S(1)} %add.12), channel_id=1, source_target_pairs={{0,2},{1,3},{2,0},{3,1},{4,6},{5,7},{6,4},{7,5},{8,10},{9,11},{10,... | collective-permute-start | bytes 55304 | tf_op jit(solution)/shard_map/ppermute | solution.py:434
  82.2 2.3 %collective-permute-done.24 = f32[12,384]{1,0:T(8,128)S(1)} collective-permute-done((f32[12,384]{1,0:T(8,128)S(1)}, f32[12,384]{1,0:T(8,128)S(1)}, u32[]{:S(2)}, u32[]{:S(2)}) %collective-permute-start.24) | collective-permute-done | bytes 18464 | tf_op jit(solution)/shard_map/ppermute | solution.py:434
  84.8 1.3 %collective-permute-start.26 = (f32[1,96]{1,0:T(1,128)S(1)}, f32[1,96]{1,0:T(1,128)S(1)}, u32[]{:S(2)}, u32[]{:S(2)}) collective-permute-start(f32[1,96]{1,0:T(1,128)S(1)} %reshape.10), channel_id=1, source_target_pairs={{0,12},{4,8},{8,4},{12,0},{1,13},{5,9},{9,5},{13,1},{2,14},{6,10},... | collective-permute-start | bytes 1160 | tf_op jit(solution)/shard_map/ppermute | solution.py:444
  86.2 2.1 %collective-permute-start.27 = (f32[1,96]{1,0:T(1,128)S(1)}, f32[1,96]{1,0:T(1,128)S(1)}, u32[]{:S(2)}, u32[]{:S(2)}) collective-permute-start(f32[1,96]{1,0:T(1,128)S(1)} %reshape.10), channel_id=1, source_target_pairs={{0,8},{4,12},{8,0},{12,4},{1,9},{5,13},{9,1},{13,5},{2,10},{6,14},... | collective-permute-start | bytes 1160 | tf_op jit(solution)/shard_map/ppermute | solution.py:444
  88.3 1.9 %collective-permute-done.26 = f32[1,96]{1,0:T(1,128)S(1)} collective-permute-done((f32[1,96]{1,0:T(1,128)S(1)}, f32[1,96]{1,0:T(1,128)S(1)}, u32[]{:S(2)}, u32[]{:S(2)}) %collective-permute-start.26) | collective-permute-done | bytes 416 | tf_op jit(solution)/shard_map/ppermute | solution.py:444
  (73 shorter events, 13.0 us)
Async XLA Ops:
  4.2 9.5 %collective-permute-start = (bf16[48,2560]{1,0:T(8,128)(2,1)S(1)}, bf16[48,2560]{1,0:T(8,128)(2,1)S(1)}, u32[]{:S(2)}, u32[]{:S(2)}) collective-permute-start(bf16[48,2560]{1,0:T(8,128)(2,1)S(1)} %get-tuple-element.33), channel_id=1, source_target_pairs={{0,4},{12,8},{4,0},{8,12},{1,5},{13,9},{5,1},{9,13},{2,6},{14,10},... | collective-permute-start | bytes 737288 | tf_op jit(solution)/shard_map/ppermute | solution.py:360
  8.9 12.1 %collective-permute-start.3 = (bf16[48,2560]{1,0:T(8,128)(2,1)S(1)}, bf16[48,2560]{1,0:T(8,128)(2,1)S(1)}, u32[]{:S(2)}, u32[]{:S(2)}) collective-permute-start(bf16[48,2560]{1,0:T(8,128)(2,1)S(1)} %get-tuple-element.36.mine_ref), channel_id=1, source_target_pairs={{0,4},{12,8},{1,5},{13,9},{2,6},{14,10},{3,7},{15,11},{16,20},{28,... | collective-permute-start | bytes 737288 | tf_op jit(solution)/shard_map/ppermute | solution.py:360
  13.8 11.5 %collective-permute-start.2 = (bf16[48,2560]{1,0:T(8,128)(2,1)S(1)}, bf16[48,2560]{1,0:T(8,128)(2,1)S(1)}, u32[]{:S(2)}, u32[]{:S(2)}) collective-permute-start(bf16[48,2560]{1,0:T(8,128)(2,1)S(1)} %get-tuple-element.35.after_ref.mine_ref), channel_id=1, source_target_pairs={{4,8},{8,4},{5,9},{9,5},{6,10},{10,6},{7,11},{11,7},{20,24},{24,20... | collective-permute-start | bytes 737288 | tf_op jit(solution)/shard_map/ppermute | solution.py:360
  14.4 13.1 %collective-permute-start.1 = (bf16[48,2560]{1,0:T(8,128)(2,1)S(1)}, bf16[48,2560]{1,0:T(8,128)(2,1)S(1)}, u32[]{:S(2)}, u32[]{:S(2)}) collective-permute-start(bf16[48,2560]{1,0:T(8,128)(2,1)S(1)} %get-tuple-element.34), channel_id=1, source_target_pairs={{0,4},{12,8},{1,5},{13,9},{2,6},{14,10},{3,7},{15,11},{16,20},{28,... | collective-permute-start | bytes 737288 | tf_op jit(solution)/shard_map/ppermute | solution.py:360
  21.1 7.2 %collective-permute-start.6 = (bf16[48,2560]{1,0:T(8,128)(2,1)S(1)}, bf16[48,2560]{1,0:T(8,128)(2,1)S(1)}, u32[]{:S(2)}, u32[]{:S(2)}) collective-permute-start(bf16[48,2560]{1,0:T(8,128)(2,1)S(1)} %shard_map.116.after_ref.mine_ref), channel_id=1, source_target_pairs={{4,8},{8,4},{5,9},{9,5},{6,10},{10,6},{7,11},{11,7},{20,24},{24,20... | collective-permute-start | bytes 737288 | tf_op jit(solution)/shard_map/ppermute | solution.py:360
  23.7 40.7 %collective-permute-start.16 = (bf16[320,1664]{1,0:T(8,128)(2,1)S(1)}, bf16[320,1664]{1,0:T(8,128)(2,1)S(1)}, u32[]{:S(2)}, u32[]{:S(2)}) collective-permute-start(bf16[320,1664]{1,0:T(8,128)(2,1)S(1)} %get-tuple-element.51), channel_id=1, source_target_pairs={{0,16},{16,0},{1,17},{17,1},{2,18},{18,2},{3,19},{19,3},{4,20},{20... | collective-permute-start | bytes 3194888 | tf_op jit(solution)/shard_map/ppermute | solution.py:372
  25.3 9.0 %collective-permute-start.5 = (bf16[48,2560]{1,0:T(8,128)(2,1)S(1)}, bf16[48,2560]{1,0:T(8,128)(2,1)S(1)}, u32[]{:S(2)}, u32[]{:S(2)}) collective-permute-start(bf16[48,2560]{1,0:T(8,128)(2,1)S(1)} %get-tuple-element.39), channel_id=1, source_target_pairs={{0,4},{12,8},{4,0},{8,12},{1,5},{13,9},{5,1},{9,13},{2,6},{14,10},... | collective-permute-start | bytes 737288 | tf_op jit(solution)/shard_map/ppermute | solution.py:360
  27.6 7.6 %collective-permute-start.4 = (bf16[48,2560]{1,0:T(8,128)(2,1)S(1)}, bf16[48,2560]{1,0:T(8,128)(2,1)S(1)}, u32[]{:S(2)}, u32[]{:S(2)}) collective-permute-start(bf16[48,2560]{1,0:T(8,128)(2,1)S(1)} %shard_map.118.after_ref.mine_ref), channel_id=1, source_target_pairs={{4,8},{8,4},{5,9},{9,5},{6,10},{10,6},{7,11},{11,7},{20,24},{24,20... | collective-permute-start | bytes 737288 | tf_op jit(solution)/shard_map/ppermute | solution.py:360
  28.4 11.3 %collective-permute-start.8 = (bf16[48,2560]{1,0:T(8,128)(2,1)S(1)}, bf16[48,2560]{1,0:T(8,128)(2,1)S(1)}, u32[]{:S(2)}, u32[]{:S(2)}) collective-permute-start(bf16[48,2560]{1,0:T(8,128)(2,1)S(1)} %get-tuple-element.43), channel_id=1, source_target_pairs={{0,4},{12,8},{4,0},{8,12},{1,5},{13,9},{5,1},{9,13},{2,6},{14,10},... | collective-permute-start | bytes 737288 | tf_op jit(solution)/shard_map/ppermute | solution.py:360
  34.4 6.5 %collective-permute-start.9 = (bf16[48,2560]{1,0:T(8,128)(2,1)S(1)}, bf16[48,2560]{1,0:T(8,128)(2,1)S(1)}, u32[]{:S(2)}, u32[]{:S(2)}) collective-permute-start(bf16[48,2560]{1,0:T(8,128)(2,1)S(1)} %shard_map.120.after_ref.mine_ref), channel_id=1, source_target_pairs={{4,8},{8,4},{5,9},{9,5},{6,10},{10,6},{7,11},{11,7},{20,24},{24,20... | collective-permute-start | bytes 737288 | tf_op jit(solution)/shard_map/ppermute | solution.py:360
  35.2 11.9 %collective-permute-start.7 = (bf16[48,2560]{1,0:T(8,128)(2,1)S(1)}, bf16[48,2560]{1,0:T(8,128)(2,1)S(1)}, u32[]{:S(2)}, u32[]{:S(2)}) collective-permute-start(bf16[48,2560]{1,0:T(8,128)(2,1)S(1)} %get-tuple-element.42), channel_id=1, source_target_pairs={{0,4},{12,8},{4,0},{8,12},{1,5},{13,9},{5,1},{9,13},{2,6},{14,10},... | collective-permute-start | bytes 737288 | tf_op jit(solution)/shard_map/ppermute | solution.py:360
  39.7 8.2 %collective-permute-start.12 = (bf16[48,2560]{1,0:T(8,128)(2,1)S(1)}, bf16[48,2560]{1,0:T(8,128)(2,1)S(1)}, u32[]{:S(2)}, u32[]{:S(2)}) collective-permute-start(bf16[48,2560]{1,0:T(8,128)(2,1)S(1)} %shard_map.123.after_ref.mine_ref), channel_id=1, source_target_pairs={{4,8},{8,4},{5,9},{9,5},{6,10},{10,6},{7,11},{11,7},{20,24},{24,20... | collective-permute-start | bytes 737288 | tf_op jit(solution)/shard_map/ppermute | solution.py:360
  40.4 24.0 %collective-permute-start.17 = (bf16[320,896]{1,0:T(8,128)(2,1)S(1)}, bf16[320,896]{1,0:T(8,128)(2,1)S(1)}, u32[]{:S(2)}, u32[]{:S(2)}) collective-permute-start(bf16[320,896]{1,0:T(8,128)(2,1)S(1)} %get-tuple-element.52), channel_id=1, source_target_pairs={{0,16},{16,0},{1,17},{17,1},{2,18},{18,2},{3,19},{19,3},{4,20},{20... | collective-permute-start | bytes 1720328 | tf_op jit(solution)/shard_map/ppermute | solution.py:372
  41.0 11.8 %collective-permute-start.11 = (bf16[48,2560]{1,0:T(8,128)(2,1)S(1)}, bf16[48,2560]{1,0:T(8,128)(2,1)S(1)}, u32[]{:S(2)}, u32[]{:S(2)}) collective-permute-start(bf16[48,2560]{1,0:T(8,128)(2,1)S(1)} %get-tuple-element.47), channel_id=1, source_target_pairs={{0,4},{12,8},{4,0},{8,12},{1,5},{13,9},{5,1},{9,13},{2,6},{14,10},... | collective-permute-start | bytes 737288 | tf_op jit(solution)/shard_map/ppermute | solution.py:360
  47.2 6.4 %collective-permute-start.10 = (bf16[48,2560]{1,0:T(8,128)(2,1)S(1)}, bf16[48,2560]{1,0:T(8,128)(2,1)S(1)}, u32[]{:S(2)}, u32[]{:S(2)}) collective-permute-start(bf16[48,2560]{1,0:T(8,128)(2,1)S(1)} %shard_map.126.after_ref.mine_ref), channel_id=1, source_target_pairs={{4,8},{8,4},{5,9},{9,5},{6,10},{10,6},{7,11},{11,7},{20,24},{24,20... | collective-permute-start | bytes 737288 | tf_op jit(solution)/shard_map/ppermute | solution.py:360
  47.9 10.8 %collective-permute-start.14 = (bf16[48,2560]{1,0:T(8,128)(2,1)S(1)}, bf16[48,2560]{1,0:T(8,128)(2,1)S(1)}, u32[]{:S(2)}, u32[]{:S(2)}) collective-permute-start(bf16[48,2560]{1,0:T(8,128)(2,1)S(1)} %get-tuple-element.50), channel_id=1, source_target_pairs={{0,4},{12,8},{4,0},{8,12},{1,5},{13,9},{5,1},{9,13},{2,6},{14,10},... | collective-permute-start | bytes 737288 | tf_op jit(solution)/shard_map/ppermute | solution.py:360
  52.9 8.9 %collective-permute-start.15 = (bf16[48,2560]{1,0:T(8,128)(2,1)S(1)}, bf16[48,2560]{1,0:T(8,128)(2,1)S(1)}, u32[]{:S(2)}, u32[]{:S(2)}) collective-permute-start(bf16[48,2560]{1,0:T(8,128)(2,1)S(1)} %shard_map.129.after_ref.mine_ref), channel_id=1, source_target_pairs={{4,8},{8,4},{5,9},{9,5},{6,10},{10,6},{7,11},{11,7},{20,24},{24,20... | collective-permute-start | bytes 737288 | tf_op jit(solution)/shard_map/ppermute | solution.py:360
  53.6 10.7 %collective-permute-start.13 = (bf16[48,2560]{1,0:T(8,128)(2,1)S(1)}, bf16[48,2560]{1,0:T(8,128)(2,1)S(1)}, u32[]{:S(2)}, u32[]{:S(2)}) collective-permute-start(bf16[48,2560]{1,0:T(8,128)(2,1)S(1)} %shard_map.130.after_ref.mine_ref), channel_id=1, source_target_pairs={{4,0},{8,12},{5,1},{9,13},{6,2},{10,14},{7,3},{11,15},{20,16},{24,... | collective-permute-start | bytes 737288 | tf_op jit(solution)/shard_map/ppermute | solution.py:360
  58.8 11.2 %collective-permute-start.18 = (bf16[48,2560]{1,0:T(8,128)(2,1)S(1)}, bf16[48,2560]{1,0:T(8,128)(2,1)S(1)}, u32[]{:S(2)}, u32[]{:S(2)}) collective-permute-start(bf16[48,2560]{1,0:T(8,128)(2,1)S(1)} %shard_map.132.after_ref.mine_ref), channel_id=1, source_target_pairs={{0,8},{4,12},{8,0},{12,4},{5,9},{9,5},{2,10},{6,14},{10,2},{14,6},... | collective-permute-start | bytes 737288 | tf_op jit(solution)/shard_map/ppermute | solution.py:365
  61.9 11.6 %collective-permute-start.20 = (bf16[48,2560]{1,0:T(8,128)(2,1)S(1)}, bf16[48,2560]{1,0:T(8,128)(2,1)S(1)}, u32[]{:S(2)}, u32[]{:S(2)}) collective-permute-start(bf16[48,2560]{1,0:T(8,128)(2,1)S(1)} %shard_map.133.after_ref.mine_ref), channel_id=1, source_target_pairs={{4,0},{8,12},{5,1},{9,13},{6,2},{10,14},{7,3},{11,15},{20,16},{24,... | collective-permute-start | bytes 737288 | tf_op jit(solution)/shard_map/ppermute | solution.py:360
  70.0 3.5 %collective-permute-start.19 = (bf16[48,2560]{1,0:T(8,128)(2,1)S(1)}, bf16[48,2560]{1,0:T(8,128)(2,1)S(1)}, u32[]{:S(2)}, u32[]{:S(2)}) collective-permute-start(bf16[48,2560]{1,0:T(8,128)(2,1)S(1)} %shard_map.139.after_ref.mine_ref), channel_id=1, source_target_pairs={{5,1},{9,13},{7,3},{11,15},{21,17},{25,29},{23,19},{27,31}} | collective-permute-start | bytes 737288 | tf_op jit(solution)/shard_map/ppermute | solution.py:365
  70.7 6.8 %collective-permute-start.21 = (bf16[288,320]{1,0:T(8,128)(2,1)S(1)}, bf16[288,320]{1,0:T(8,128)(2,1)S(1)}, u32[]{:S(2)}, u32[]{:S(2)}) collective-permute-start(bf16[288,320]{1,0:T(8,128)(2,1)S(1)} %shard_map.137.after_ref), channel_id=1, source_target_pairs={{0,16},{16,0},{1,17},{17,1},{2,18},{18,2},{3,19},{19,3},{4,20},{20... | collective-permute-start | bytes 552968 | tf_op jit(solution)/shard_map/ppermute | solution.py:379
  74.2 14.1 %copy-start.2 = (s32[128]{0:T(128)S(1)}, s32[128]{0:T(128)}, u32[]{:S(2)}) copy-start(s32[128]{0:T(128)} %param.19) | copy-start | bytes 1540
  74.2 14.1 %copy-start.3 = (s32[128]{0:T(128)S(1)}, s32[128]{0:T(128)}, u32[]{:S(2)}) copy-start(s32[128]{0:T(128)} %param.17) | copy-start | bytes 1540
  74.2 14.1 %copy-start.4 = (s32[128,1]{0,1:T(1,128)S(1)}, s32[128,1]{0,1:T(1,128)}, u32[]{:S(2)}) copy-start(s32[128,1]{0,1:T(1,128)} %param.18) | copy-start | bytes 1540
  74.2 4.4 %collective-permute-start.22 = (bf16[96,320]{1,0:T(8,128)(2,1)S(1)}, bf16[96,320]{1,0:T(8,128)(2,1)S(1)}, u32[]{:S(2)}, u32[]{:S(2)}) collective-permute-start(bf16[96,320]{1,0:T(8,128)(2,1)S(1)} %shard_map.142.after_ref), channel_id=1, source_target_pairs={{0,16},{16,0},{1,17},{17,1},{2,18},{18,2},{3,19},{19,3},{4,20},{20... | collective-permute-start | bytes 184328 | tf_op jit(solution)/shard_map/ppermute | solution.py:379
  79.5 1.2 %collective-permute-start.23 = (f32[12,384]{1,0:T(8,128)S(1)}, f32[12,384]{1,0:T(8,128)S(1)}, u32[]{:S(2)}, u32[]{:S(2)}) collective-permute-start(f32[12,384]{1,0:T(8,128)S(1)} %shard_map.144), channel_id=1, source_target_pairs={{0,1},{1,0},{2,3},{3,2},{4,5},{5,4},{6,7},{7,6},{8,9},{9,8},{10,11... | collective-permute-start | bytes 55304 | tf_op jit(solution)/shard_map/ppermute | solution.py:434
  80.7 3.8 %collective-permute-start.24 = (f32[12,384]{1,0:T(8,128)S(1)}, f32[12,384]{1,0:T(8,128)S(1)}, u32[]{:S(2)}, u32[]{:S(2)}) collective-permute-start(f32[12,384]{1,0:T(8,128)S(1)} %add.12), channel_id=1, source_target_pairs={{0,2},{1,3},{2,0},{3,1},{4,6},{5,7},{6,4},{7,5},{8,10},{9,11},{10,... | collective-permute-start | bytes 55304 | tf_op jit(solution)/shard_map/ppermute | solution.py:434
  84.6 6.8 %copy-start.1 = (f32[12,384]{1,0:T(8,128)}, f32[12,384]{1,0:T(8,128)S(1)}, u32[]{:S(2)}) copy-start(f32[12,384]{1,0:T(8,128)S(1)} %add.13) | copy-start | bytes 55300
  84.7 3.6 %collective-permute-start.25 = (f32[1,96]{1,0:T(1,128)S(1)}, f32[1,96]{1,0:T(1,128)S(1)}, u32[]{:S(2)}, u32[]{:S(2)}) collective-permute-start(f32[1,96]{1,0:T(1,128)S(1)} %reshape.10), channel_id=1, source_target_pairs={{0,4},{4,0},{8,12},{12,8},{1,5},{5,1},{9,13},{13,9},{2,6},{6,2},{1... | collective-permute-start | bytes 1160 | tf_op jit(solution)/shard_map/ppermute | solution.py:444
  84.8 5.4 %collective-permute-start.26 = (f32[1,96]{1,0:T(1,128)S(1)}, f32[1,96]{1,0:T(1,128)S(1)}, u32[]{:S(2)}, u32[]{:S(2)}) collective-permute-start(f32[1,96]{1,0:T(1,128)S(1)} %reshape.10), channel_id=1, source_target_pairs={{0,12},{4,8},{8,4},{12,0},{1,13},{5,9},{9,5},{13,1},{2,14},{6,10},... | collective-permute-start | bytes 1160 | tf_op jit(solution)/shard_map/ppermute | solution.py:444
  86.2 4.4 %collective-permute-start.27 = (f32[1,96]{1,0:T(1,128)S(1)}, f32[1,96]{1,0:T(1,128)S(1)}, u32[]{:S(2)}, u32[]{:S(2)}) collective-permute-start(f32[1,96]{1,0:T(1,128)S(1)} %reshape.10), channel_id=1, source_target_pairs={{0,8},{4,12},{8,0},{12,4},{1,9},{5,13},{9,1},{13,5},{2,10},{6,14},... | collective-permute-start | bytes 1160 | tf_op jit(solution)/shard_map/ppermute | solution.py:444
  (1 other events, 4.5 us)

commit v20 on v17

--- a/solution.py
+++ b/solution.py
@@ -401,7 +401,12 @@
         scores = lax.psum(scores, "layer")
     else:
         for step in [1 << k for k in range(layers.bit_length() - 1)]:
-            scores = scores + lax.ppermute(scores, "layer", [(i, i ^ step) for i in range(layers)])
+            pairs = [(i, i ^ step) for i in range(layers)]
+            if step == 1:
+                scores = scores + lax.ppermute(scores, "layer", pairs)
+                continue
+            scores = lax.reduce_precision(scores, 8, 7)
+            scores = scores + lax.ppermute(scores.astype(jnp.bfloat16), "layer", pairs).astype(jnp.float32)
     tokens_here, docs = acts.shape[1], doc_counts.shape[1]
     token_scores, pooled = scores[:, :tokens_here], scores[:, tokens_here : tokens_here + docs]
 

time: 91.1 us -> 90.9 us (level)
  no operation moved by 1% of the time
where the time goes in v20:
time: 90.9 us; the launch traced here: 90.6 us
  starting transfers between devices  55.4 us (61%)
  waiting for transfers between devices  20.8 us (23%)
  Pallas kernels  12.3 us (14%)
  between operations  1.1 us (1%)
    ppermute x17, starting transfers between devices, transfer(): return lax.ppermute(value, 'dp', pairs)  39 us
    ppermute x17, waiting for transfers between devices, transfer(): return lax.ppermute(value, 'dp', pairs)  12.8 us
    ppermute x1, starting transfers between devices, per_device(): came[c] = lax.ppermute(part[c], 'dp', [(i, i ^ 2) for i in range(n)])  5.26 us
    pallas_call x1, Pallas kernels, first_pull(): pl.pallas_call(first_pull_kernel, out_shape=[bf16(rows, features)] * 2 +...  3.6 us
    ppermute x3, starting transfers between devices, per_device(): lax.ppermute(flat, 'dp', [(i, i ^ k ^ k >> 1) for i in range(n)])  3.55 us
    pallas_call x4, Pallas kernels, project(): pl.pallas_call(functools.partial(project_kernel, len(tokens)), out_shape=...  3.17 us
    ppermute x2, starting transfers between devices, per_device(): others = [lax.ppermute(piece, 'parts', swap) for piece in theirs]  3.12 us
    ppermute x2, starting transfers between devices, project_waiting(): back.append(lax.ppermute(away, 'parts', swap))  2.99 us
  transfers between devices with their start and end apart: 27, of which 11 were waited for; matrix products, arithmetic and copies ran while one was open for 0% of the time, Pallas kernels for 9%

profile of v20, /device:TPU:0, one launch (start us, length us, event | category | flops | bytes accessed | tf_op | source)
XLA Modules:
  0.0 90.6 jit_solution(848296513819574690)
XLA Ops:
  0.6 3.6 %shard_map.113 = (bf16[48,2560]{1,0:T(8,128)(2,1)S(1)}, bf16[48,2560]{1,0:T(8,128)(2,1)S(1)}, bf16[2560,640]{1,0:T(8,128)(2,1)S(1)}, bf16[640,384]{1,0:T(8,128)(2,1)}, bf16[384,640]{1,0:T(8,128)(2,1)S(1)}) custom-call(bf16[2560,640]{1,0:T(8,128)(2,1)} %bitcast.16, bf16[2560,640]{1,0:T(8,128)(2,1)} %bitcast.17, bf16[640,384]{1,0:T(8,128)(2,1)} %bitcast.20, ...), custom_call_target="tpu_custom_call" | custom-call | tf_op jit(solution)/shard_map/pallas_call | solution.py:77
  4.2 3.1 %collective-permute-start = (bf16[48,2560]{1,0:T(8,128)(2,1)S(1)}, bf16[48,2560]{1,0:T(8,128)(2,1)S(1)}, u32[]{:S(2)}, u32[]{:S(2)}) collective-permute-start(bf16[48,2560]{1,0:T(8,128)(2,1)S(1)} %get-tuple-element.33), channel_id=1, source_target_pairs={{0,4},{12,8},{4,0},{8,12},{1,5},{13,9},{5,1},{9,13},{2,6},{14,10},... | collective-permute-start | bytes 737288 | tf_op jit(solution)/shard_map/ppermute | solution.py:338
  7.3 1.5 %shard_map.114 = (bf16[48,2560]{1,0:T(8,128)(2,1)S(1)}, bf16[48,2560]{1,0:T(8,128)(2,1)S(1)}, bf16[48,2560]{1,0:T(8,128)(2,1)S(1)}, bf16[48,2560]{1,0:T(8,128)(2...) custom-call(bf16[384,640]{1,0:T(8,128)(2,1)S(1)} %get-tuple-element.28.turned_ref,, ...), custom_call_target="tpu_custom_call" | custom-call | tf_op jit(solution)/shard_map/pallas_call | solution.py:101
  8.9 1.9 %collective-permute-start.3 = (bf16[48,2560]{1,0:T(8,128)(2,1)S(1)}, bf16[48,2560]{1,0:T(8,128)(2,1)S(1)}, u32[]{:S(2)}, u32[]{:S(2)}) collective-permute-start(bf16[48,2560]{1,0:T(8,128)(2,1)S(1)} %get-tuple-element.36.mine_ref), channel_id=1, source_target_pairs={{0,4},{12,8},{1,5},{13,9},{2,6},{14,10},{3,7},{15,11},{16,20},{28,... | collective-permute-start | bytes 737288 | tf_op jit(solution)/shard_map/ppermute | solution.py:338
  10.8 2.9 %collective-permute-done.came_ref.early_ref = bf16[48,2560]{1,0:T(8,128)(2,1)S(1)} collective-permute-done((bf16[48,2560]{1,0:T(8,128)(2,1)S(1)}, bf16[48,2560]{1,0:T(8,128)(2,1)S(1)}, u32[]{:S(2)}, u32[]{:S(2)}) %collective-permute-start) | collective-permute-done | bytes 245792 | tf_op jit(solution)/shard_map/ppermute | solution.py:338
  14.4 6.5 %collective-permute-start.1 = (bf16[48,2560]{1,0:T(8,128)(2,1)S(1)}, bf16[48,2560]{1,0:T(8,128)(2,1)S(1)}, u32[]{:S(2)}, u32[]{:S(2)}) collective-permute-start(bf16[48,2560]{1,0:T(8,128)(2,1)S(1)} %get-tuple-element.34), channel_id=1, source_target_pairs={{0,4},{12,8},{1,5},{13,9},{2,6},{14,10},{3,7},{15,11},{16,20},{28,... | collective-permute-start | bytes 737288 | tf_op jit(solution)/shard_map/ppermute | solution.py:338
  21.8 3.0 %collective-permute-start.5 = (bf16[48,2560]{1,0:T(8,128)(2,1)S(1)}, bf16[48,2560]{1,0:T(8,128)(2,1)S(1)}, u32[]{:S(2)}, u32[]{:S(2)}) collective-permute-start(bf16[48,2560]{1,0:T(8,128)(2,1)S(1)} %get-tuple-element.39), channel_id=1, source_target_pairs={{0,4},{12,8},{4,0},{8,12},{1,5},{13,9},{5,1},{9,13},{2,6},{14,10},... | collective-permute-start | bytes 737288 | tf_op jit(solution)/shard_map/ppermute | solution.py:338
  24.9 1.9 %shard_map.136 = (bf16[320,2560]{1,0:T(8,128)(2,1)S(1)}, bf16[320,1664]{1,0:T(8,128)(2,1)S(1)}, bf16[320,896]{1,0:T(8,128)(2,1)S(1)}) custom-call(bf16[320,2560]{1,0:T(8,128)(2,1)} %bitcast.18, bf16[320,2560]{1,0:T(8,128)(2,1)} %bitcast.19, bf16[48,2560]{1,0:T(8,128)(2,1)S(1)} %get-tuple-element.48.rest_0_.mine_ref.after_ref), custom_call_target="tpu_custom_call" | custom-call | tf_op jit(solution)/shard_map/pallas_call | solution.py:140
  26.8 1.6 %collective-permute-start.16 = (bf16[320,1664]{1,0:T(8,128)(2,1)S(1)}, bf16[320,1664]{1,0:T(8,128)(2,1)S(1)}, u32[]{:S(2)}, u32[]{:S(2)}) collective-permute-start(bf16[320,1664]{1,0:T(8,128)(2,1)S(1)} %get-tuple-element.51), channel_id=1, source_target_pairs={{0,16},{16,0},{1,17},{17,1},{2,18},{18,2},{3,19},{19,3},{4,20},{20... | collective-permute-start | bytes 3194888 | tf_op jit(solution)/shard_map/ppermute | solution.py:346
  29.2 3.7 %collective-permute-start.8 = (bf16[48,2560]{1,0:T(8,128)(2,1)S(1)}, bf16[48,2560]{1,0:T(8,128)(2,1)S(1)}, u32[]{:S(2)}, u32[]{:S(2)}) collective-permute-start(bf16[48,2560]{1,0:T(8,128)(2,1)S(1)} %get-tuple-element.43), channel_id=1, source_target_pairs={{0,4},{12,8},{4,0},{8,12},{1,5},{13,9},{5,1},{9,13},{2,6},{14,10},... | collective-permute-start | bytes 737288 | tf_op jit(solution)/shard_map/ppermute | solution.py:338
  33.7 5.0 %collective-permute-start.7 = (bf16[48,2560]{1,0:T(8,128)(2,1)S(1)}, bf16[48,2560]{1,0:T(8,128)(2,1)S(1)}, u32[]{:S(2)}, u32[]{:S(2)}) collective-permute-start(bf16[48,2560]{1,0:T(8,128)(2,1)S(1)} %get-tuple-element.42), channel_id=1, source_target_pairs={{0,4},{12,8},{4,0},{8,12},{1,5},{13,9},{5,1},{9,13},{2,6},{14,10},... | collective-permute-start | bytes 737288 | tf_op jit(solution)/shard_map/ppermute | solution.py:338
  38.8 0.9 collective-permute-done.8.came_ref
  40.5 4.3 %collective-permute-start.11 = (bf16[48,2560]{1,0:T(8,128)(2,1)S(1)}, bf16[48,2560]{1,0:T(8,128)(2,1)S(1)}, u32[]{:S(2)}, u32[]{:S(2)}) collective-permute-start(bf16[48,2560]{1,0:T(8,128)(2,1)S(1)} %get-tuple-element.47), channel_id=1, source_target_pairs={{0,4},{12,8},{4,0},{8,12},{1,5},{13,9},{5,1},{9,13},{2,6},{14,10},... | collective-permute-start | bytes 737288 | tf_op jit(solution)/shard_map/ppermute | solution.py:338
  44.8 1.5 %collective-permute-start.17 = (bf16[320,896]{1,0:T(8,128)(2,1)S(1)}, bf16[320,896]{1,0:T(8,128)(2,1)S(1)}, u32[]{:S(2)}, u32[]{:S(2)}) collective-permute-start(bf16[320,896]{1,0:T(8,128)(2,1)S(1)} %get-tuple-element.52), channel_id=1, source_target_pairs={{0,16},{16,0},{1,17},{17,1},{2,18},{18,2},{3,19},{19,3},{4,20},{20... | collective-permute-start | bytes 1720328 | tf_op jit(solution)/shard_map/ppermute | solution.py:346
  47.3 4.0 %collective-permute-start.14 = (bf16[48,2560]{1,0:T(8,128)(2,1)S(1)}, bf16[48,2560]{1,0:T(8,128)(2,1)S(1)}, u32[]{:S(2)}, u32[]{:S(2)}) collective-permute-start(bf16[48,2560]{1,0:T(8,128)(2,1)S(1)} %get-tuple-element.50), channel_id=1, source_target_pairs={{0,4},{12,8},{4,0},{8,12},{1,5},{13,9},{5,1},{9,13},{2,6},{14,10},... | collective-permute-start | bytes 737288 | tf_op jit(solution)/shard_map/ppermute | solution.py:338
  52.1 1.3 %collective-permute-start.13 = (bf16[48,2560]{1,0:T(8,128)(2,1)S(1)}, bf16[48,2560]{1,0:T(8,128)(2,1)S(1)}, u32[]{:S(2)}, u32[]{:S(2)}) collective-permute-start(bf16[48,2560]{1,0:T(8,128)(2,1)S(1)} %shard_map.130.after_ref.mine_ref), channel_id=1, source_target_pairs={{4,0},{8,12},{5,1},{9,13},{6,2},{10,14},{7,3},{11,15},{20,16},{24,... | collective-permute-start | bytes 737288 | tf_op jit(solution)/shard_map/ppermute | solution.py:338
  53.5 4.2 %collective-permute-done.14.came_ref = bf16[48,2560]{1,0:T(8,128)(2,1)S(1)} collective-permute-done((bf16[48,2560]{1,0:T(8,128)(2,1)S(1)}, bf16[48,2560]{1,0:T(8,128)(2,1)S(1)}, u32[]{:S(2)}, u32[]{:S(2)}) %collective-permute-start.14) | collective-permute-done | bytes 245792 | tf_op jit(solution)/shard_map/ppermute | solution.py:338
  57.7 5.3 %collective-permute-start.19 = (bf16[48,2560]{1,0:T(8,128)(2,1)S(1)}, bf16[48,2560]{1,0:T(8,128)(2,1)S(1)}, u32[]{:S(2)}, u32[]{:S(2)}) collective-permute-start(bf16[48,2560]{1,0:T(8,128)(2,1)S(1)} %shard_map.132.after_ref.mine_ref), channel_id=1, source_target_pairs={{0,8},{4,12},{8,0},{12,4},{1,9},{5,13},{9,1},{13,5},{2,10},{6,14},... | collective-permute-start | bytes 737288 | tf_op jit(solution)/shard_map/ppermute | solution.py:368
  63.0 1.3 %collective-permute-start.18 = (bf16[48,2560]{1,0:T(8,128)(2,1)S(1)}, bf16[48,2560]{1,0:T(8,128)(2,1)S(1)}, u32[]{:S(2)}, u32[]{:S(2)}) collective-permute-start(bf16[48,2560]{1,0:T(8,128)(2,1)S(1)} %shard_map.133.after_ref.mine_ref), channel_id=1, source_target_pairs={{4,0},{8,12},{5,1},{9,13},{6,2},{10,14},{7,3},{11,15},{20,16},{24,... | collective-permute-start | bytes 737288 | tf_op jit(solution)/shard_map/ppermute | solution.py:338
  64.4 4.5 %collective-permute-done.13.came_ref = bf16[48,2560]{1,0:T(8,128)(2,1)S(1)} collective-permute-done((bf16[48,2560]{1,0:T(8,128)(2,1)S(1)}, bf16[48,2560]{1,0:T(8,128)(2,1)S(1)}, u32[]{:S(2)}, u32[]{:S(2)}) %collective-permute-start.13) | collective-permute-done | bytes 245792 | tf_op jit(solution)/shard_map/ppermute | solution.py:338
  68.9 1.0 %shard_map.137.after_ref = bf16[288,320]{1,0:T(8,128)(2,1)S(1)} custom-call(bf16[48,2560]{1,0:T(8,128)(2,1)S(1)} %shard_map.135.after_ref.rest_7_.rest_6_, bf16[320,1664]{1,0:T(8,128)(2,1)S(1)} %collective-permute-done.16.rest_0_, bf16[320,896]{1,0:T(8,128)(2,1)S(1)} %collective-permute-done.17.rest_1_, ...), custom_call_target="tpu_custom_call" | custom-call | tf_op jit(solution)/shard_map/pallas_call | solution.py:241
  69.9 1.5 %collective-permute-start.20 = (bf16[288,320]{1,0:T(8,128)(2,1)S(1)}, bf16[288,320]{1,0:T(8,128)(2,1)S(1)}, u32[]{:S(2)}, u32[]{:S(2)}) collective-permute-start(bf16[288,320]{1,0:T(8,128)(2,1)S(1)} %shard_map.137.after_ref), channel_id=1, source_target_pairs={{0,16},{16,0},{1,17},{17,1},{2,18},{18,2},{3,19},{19,3},{4,20},{20... | collective-permute-start | bytes 552968 | tf_op jit(solution)/shard_map/ppermute | solution.py:353
  71.4 0.9 %shard_map.138.after_ref.refs_0_ = f32[288,320]{1,0:T(8,128)S(1)} custom-call(bf16[288,320]{1,0:T(8,128)(2,1)S(1)} %shard_map.137.after_ref, bf16[320,2560]{1,0:T(8,128)(2,1)S(1)} %get-tuple-element.53.rest_0_, bf16[48,2560]{1,0:T(8,128)(2,1)S(1)} %shard_map.122.after_ref.rest_2_.rest_1_, bf16[48,2560]{1,0:T(8,128)(2,1)S(1)} %shard_map.125.after_ref.rest_3_.rest_2_, ...), custom_call_target="tpu_custom_call" | custom-call | tf_op jit(solution)/shard_map/pallas_call | solution.py:241
  73.5 1.5 %collective-permute-start.21 = (bf16[96,320]{1,0:T(8,128)(2,1)S(1)}, bf16[96,320]{1,0:T(8,128)(2,1)S(1)}, u32[]{:S(2)}, u32[]{:S(2)}) collective-permute-start(bf16[96,320]{1,0:T(8,128)(2,1)S(1)} %shard_map.141.after_ref), channel_id=1, source_target_pairs={{0,16},{16,0},{1,17},{17,1},{2,18},{18,2},{3,19},{19,3},{4,20},{20... | collective-permute-start | bytes 184328 | tf_op jit(solution)/shard_map/ppermute | solution.py:353
  75.9 2.0 %collective-permute-done.21.refs_3_ = bf16[96,320]{1,0:T(8,128)(2,1)S(1)} collective-permute-done((bf16[96,320]{1,0:T(8,128)(2,1)S(1)}, bf16[96,320]{1,0:T(8,128)(2,1)S(1)}, u32[]{:S(2)}, u32[]{:S(2)}) %collective-permute-start.21) | collective-permute-done | bytes 61472 | tf_op jit(solution)/shard_map/ppermute | solution.py:353
  77.9 0.9 shard_map.143
  78.8 1.2 %collective-permute-done.22 = f32[12,384]{1,0:T(8,128)S(1)} collective-permute-done((f32[12,384]{1,0:T(8,128)S(1)}, f32[12,384]{1,0:T(8,128)S(1)}, u32[]{:S(2)}, u32[]{:S(2)}) %collective-permute-start.22) | collective-permute-done | bytes 18464 | tf_op jit(solution)/shard_map/ppermute | solution.py:406
  80.0 1.5 %collective-permute-start.23 = (bf16[12,384]{1,0:T(8,128)(2,1)S(1)}, bf16[12,384]{1,0:T(8,128)(2,1)S(1)}, u32[]{:S(2)}, u32[]{:S(2)}) collective-permute-start(bf16[12,384]{1,0:T(8,128)(2,1)S(1)} %fusion), channel_id=1, source_target_pairs={{0,2},{1,3},{2,0},{3,1},{4,6},{5,7},{6,4},{7,5},{8,10},{9,11},{10,... | collective-permute-start | bytes 27656 | tf_op jit(solution)/shard_map/ppermute | solution.py:409
  81.5 2.2 %collective-permute-done.23 = bf16[12,384]{1,0:T(8,128)(2,1)S(1)} collective-permute-done((bf16[12,384]{1,0:T(8,128)(2,1)S(1)}, bf16[12,384]{1,0:T(8,128)(2,1)S(1)}, u32[]{:S(2)}, u32[]{:S(2)}) %collective-permute-start.23) | collective-permute-done | bytes 9248 | tf_op jit(solution)/shard_map/ppermute | solution.py:409
  83.9 1.4 %collective-permute-start.25 = (f32[1,96]{1,0:T(1,128)S(1)}, f32[1,96]{1,0:T(1,128)S(1)}, u32[]{:S(2)}, u32[]{:S(2)}) collective-permute-start(f32[1,96]{1,0:T(1,128)S(1)} %reshape.10), channel_id=1, source_target_pairs={{0,12},{4,8},{8,4},{12,0},{1,13},{5,9},{9,5},{13,1},{2,14},{6,10},... | collective-permute-start | bytes 1160 | tf_op jit(solution)/shard_map/ppermute | solution.py:419
  85.3 2.1 %collective-permute-start.26 = (f32[1,96]{1,0:T(1,128)S(1)}, f32[1,96]{1,0:T(1,128)S(1)}, u32[]{:S(2)}, u32[]{:S(2)}) collective-permute-start(f32[1,96]{1,0:T(1,128)S(1)} %reshape.10), channel_id=1, source_target_pairs={{0,8},{4,12},{8,0},{12,4},{1,9},{5,13},{9,1},{13,5},{2,10},{6,14},... | collective-permute-start | bytes 1160 | tf_op jit(solution)/shard_map/ppermute | solution.py:419
  87.5 1.9 %collective-permute-done.25 = f32[1,96]{1,0:T(1,128)S(1)} collective-permute-done((f32[1,96]{1,0:T(1,128)S(1)}, f32[1,96]{1,0:T(1,128)S(1)}, u32[]{:S(2)}, u32[]{:S(2)}) %collective-permute-start.25) | collective-permute-done | bytes 416 | tf_op jit(solution)/shard_map/ppermute | solution.py:419
  (70 shorter events, 9.4 us)
Async XLA Ops:
  4.2 9.5 %collective-permute-start = (bf16[48,2560]{1,0:T(8,128)(2,1)S(1)}, bf16[48,2560]{1,0:T(8,128)(2,1)S(1)}, u32[]{:S(2)}, u32[]{:S(2)}) collective-permute-start(bf16[48,2560]{1,0:T(8,128)(2,1)S(1)} %get-tuple-element.33), channel_id=1, source_target_pairs={{0,4},{12,8},{4,0},{8,12},{1,5},{13,9},{5,1},{9,13},{2,6},{14,10},... | collective-permute-start | bytes 737288 | tf_op jit(solution)/shard_map/ppermute | solution.py:338
  8.9 12.1 %collective-permute-start.3 = (bf16[48,2560]{1,0:T(8,128)(2,1)S(1)}, bf16[48,2560]{1,0:T(8,128)(2,1)S(1)}, u32[]{:S(2)}, u32[]{:S(2)}) collective-permute-start(bf16[48,2560]{1,0:T(8,128)(2,1)S(1)} %get-tuple-element.36.mine_ref), channel_id=1, source_target_pairs={{0,4},{12,8},{1,5},{13,9},{2,6},{14,10},{3,7},{15,11},{16,20},{28,... | collective-permute-start | bytes 737288 | tf_op jit(solution)/shard_map/ppermute | solution.py:338
  13.8 8.0 %collective-permute-start.2 = (bf16[48,2560]{1,0:T(8,128)(2,1)S(1)}, bf16[48,2560]{1,0:T(8,128)(2,1)S(1)}, u32[]{:S(2)}, u32[]{:S(2)}) collective-permute-start(bf16[48,2560]{1,0:T(8,128)(2,1)S(1)} %get-tuple-element.35.after_ref.mine_ref), channel_id=1, source_target_pairs={{4,8},{8,4},{5,9},{9,5},{6,10},{10,6},{7,11},{11,7},{20,24},{24,20... | collective-permute-start | bytes 737288 | tf_op jit(solution)/shard_map/ppermute | solution.py:338
  14.4 13.9 %collective-permute-start.1 = (bf16[48,2560]{1,0:T(8,128)(2,1)S(1)}, bf16[48,2560]{1,0:T(8,128)(2,1)S(1)}, u32[]{:S(2)}, u32[]{:S(2)}) collective-permute-start(bf16[48,2560]{1,0:T(8,128)(2,1)S(1)} %get-tuple-element.34), channel_id=1, source_target_pairs={{0,4},{12,8},{1,5},{13,9},{2,6},{14,10},{3,7},{15,11},{16,20},{28,... | collective-permute-start | bytes 737288 | tf_op jit(solution)/shard_map/ppermute | solution.py:338
  21.1 8.1 %collective-permute-start.6 = (bf16[48,2560]{1,0:T(8,128)(2,1)S(1)}, bf16[48,2560]{1,0:T(8,128)(2,1)S(1)}, u32[]{:S(2)}, u32[]{:S(2)}) collective-permute-start(bf16[48,2560]{1,0:T(8,128)(2,1)S(1)} %shard_map.116.after_ref.mine_ref), channel_id=1, source_target_pairs={{4,8},{8,4},{5,9},{9,5},{6,10},{10,6},{7,11},{11,7},{20,24},{24,20... | collective-permute-start | bytes 737288 | tf_op jit(solution)/shard_map/ppermute | solution.py:338
  21.8 11.1 %collective-permute-start.5 = (bf16[48,2560]{1,0:T(8,128)(2,1)S(1)}, bf16[48,2560]{1,0:T(8,128)(2,1)S(1)}, u32[]{:S(2)}, u32[]{:S(2)}) collective-permute-start(bf16[48,2560]{1,0:T(8,128)(2,1)S(1)} %get-tuple-element.39), channel_id=1, source_target_pairs={{0,4},{12,8},{4,0},{8,12},{1,5},{13,9},{5,1},{9,13},{2,6},{14,10},... | collective-permute-start | bytes 737288 | tf_op jit(solution)/shard_map/ppermute | solution.py:338
  26.8 42.2 %collective-permute-start.16 = (bf16[320,1664]{1,0:T(8,128)(2,1)S(1)}, bf16[320,1664]{1,0:T(8,128)(2,1)S(1)}, u32[]{:S(2)}, u32[]{:S(2)}) collective-permute-start(bf16[320,1664]{1,0:T(8,128)(2,1)S(1)} %get-tuple-element.51), channel_id=1, source_target_pairs={{0,16},{16,0},{1,17},{17,1},{2,18},{18,2},{3,19},{19,3},{4,20},{20... | collective-permute-start | bytes 3194888 | tf_op jit(solution)/shard_map/ppermute | solution.py:346
  28.4 5.2 %collective-permute-start.4 = (bf16[48,2560]{1,0:T(8,128)(2,1)S(1)}, bf16[48,2560]{1,0:T(8,128)(2,1)S(1)}, u32[]{:S(2)}, u32[]{:S(2)}) collective-permute-start(bf16[48,2560]{1,0:T(8,128)(2,1)S(1)} %shard_map.118.after_ref.mine_ref), channel_id=1, source_target_pairs={{4,8},{8,4},{5,9},{9,5},{6,10},{10,6},{7,11},{11,7},{20,24},{24,20... | collective-permute-start | bytes 737288 | tf_op jit(solution)/shard_map/ppermute | solution.py:338
  29.2 10.5 %collective-permute-start.8 = (bf16[48,2560]{1,0:T(8,128)(2,1)S(1)}, bf16[48,2560]{1,0:T(8,128)(2,1)S(1)}, u32[]{:S(2)}, u32[]{:S(2)}) collective-permute-start(bf16[48,2560]{1,0:T(8,128)(2,1)S(1)} %get-tuple-element.43), channel_id=1, source_target_pairs={{0,4},{12,8},{4,0},{8,12},{1,5},{13,9},{5,1},{9,13},{2,6},{14,10},... | collective-permute-start | bytes 737288 | tf_op jit(solution)/shard_map/ppermute | solution.py:338
  33.0 7.5 %collective-permute-start.9 = (bf16[48,2560]{1,0:T(8,128)(2,1)S(1)}, bf16[48,2560]{1,0:T(8,128)(2,1)S(1)}, u32[]{:S(2)}, u32[]{:S(2)}) collective-permute-start(bf16[48,2560]{1,0:T(8,128)(2,1)S(1)} %shard_map.120.after_ref.mine_ref), channel_id=1, source_target_pairs={{4,8},{8,4},{5,9},{9,5},{6,10},{10,6},{7,11},{11,7},{20,24},{24,20... | collective-permute-start | bytes 737288 | tf_op jit(solution)/shard_map/ppermute | solution.py:338
  33.7 12.7 %collective-permute-start.7 = (bf16[48,2560]{1,0:T(8,128)(2,1)S(1)}, bf16[48,2560]{1,0:T(8,128)(2,1)S(1)}, u32[]{:S(2)}, u32[]{:S(2)}) collective-permute-start(bf16[48,2560]{1,0:T(8,128)(2,1)S(1)} %get-tuple-element.42), channel_id=1, source_target_pairs={{0,4},{12,8},{4,0},{8,12},{1,5},{13,9},{5,1},{9,13},{2,6},{14,10},... | collective-permute-start | bytes 737288 | tf_op jit(solution)/shard_map/ppermute | solution.py:338
  39.7 7.4 %collective-permute-start.12 = (bf16[48,2560]{1,0:T(8,128)(2,1)S(1)}, bf16[48,2560]{1,0:T(8,128)(2,1)S(1)}, u32[]{:S(2)}, u32[]{:S(2)}) collective-permute-start(bf16[48,2560]{1,0:T(8,128)(2,1)S(1)} %shard_map.123.after_ref.mine_ref), channel_id=1, source_target_pairs={{4,8},{8,4},{5,9},{9,5},{6,10},{10,6},{7,11},{11,7},{20,24},{24,20... | collective-permute-start | bytes 737288 | tf_op jit(solution)/shard_map/ppermute | solution.py:338
  40.5 10.8 %collective-permute-start.11 = (bf16[48,2560]{1,0:T(8,128)(2,1)S(1)}, bf16[48,2560]{1,0:T(8,128)(2,1)S(1)}, u32[]{:S(2)}, u32[]{:S(2)}) collective-permute-start(bf16[48,2560]{1,0:T(8,128)(2,1)S(1)} %get-tuple-element.47), channel_id=1, source_target_pairs={{0,4},{12,8},{4,0},{8,12},{1,5},{13,9},{5,1},{9,13},{2,6},{14,10},... | collective-permute-start | bytes 737288 | tf_op jit(solution)/shard_map/ppermute | solution.py:338
  44.8 24.1 %collective-permute-start.17 = (bf16[320,896]{1,0:T(8,128)(2,1)S(1)}, bf16[320,896]{1,0:T(8,128)(2,1)S(1)}, u32[]{:S(2)}, u32[]{:S(2)}) collective-permute-start(bf16[320,896]{1,0:T(8,128)(2,1)S(1)} %get-tuple-element.52), channel_id=1, source_target_pairs={{0,16},{16,0},{1,17},{17,1},{2,18},{18,2},{3,19},{19,3},{4,20},{20... | collective-permute-start | bytes 1720328 | tf_op jit(solution)/shard_map/ppermute | solution.py:346
  46.5 5.6 %collective-permute-start.10 = (bf16[48,2560]{1,0:T(8,128)(2,1)S(1)}, bf16[48,2560]{1,0:T(8,128)(2,1)S(1)}, u32[]{:S(2)}, u32[]{:S(2)}) collective-permute-start(bf16[48,2560]{1,0:T(8,128)(2,1)S(1)} %shard_map.126.after_ref.mine_ref), channel_id=1, source_target_pairs={{4,8},{8,4},{5,9},{9,5},{6,10},{10,6},{7,11},{11,7},{20,24},{24,20... | collective-permute-start | bytes 737288 | tf_op jit(solution)/shard_map/ppermute | solution.py:338
  47.3 10.4 %collective-permute-start.14 = (bf16[48,2560]{1,0:T(8,128)(2,1)S(1)}, bf16[48,2560]{1,0:T(8,128)(2,1)S(1)}, u32[]{:S(2)}, u32[]{:S(2)}) collective-permute-start(bf16[48,2560]{1,0:T(8,128)(2,1)S(1)} %get-tuple-element.50), channel_id=1, source_target_pairs={{0,4},{12,8},{4,0},{8,12},{1,5},{13,9},{5,1},{9,13},{2,6},{14,10},... | collective-permute-start | bytes 737288 | tf_op jit(solution)/shard_map/ppermute | solution.py:338
  51.4 11.6 %collective-permute-start.15 = (bf16[48,2560]{1,0:T(8,128)(2,1)S(1)}, bf16[48,2560]{1,0:T(8,128)(2,1)S(1)}, u32[]{:S(2)}, u32[]{:S(2)}) collective-permute-start(bf16[48,2560]{1,0:T(8,128)(2,1)S(1)} %shard_map.129.after_ref.mine_ref), channel_id=1, source_target_pairs={{4,8},{8,4},{5,9},{9,5},{6,10},{10,6},{7,11},{11,7},{20,24},{24,20... | collective-permute-start | bytes 737288 | tf_op jit(solution)/shard_map/ppermute | solution.py:338
  52.1 16.8 %collective-permute-start.13 = (bf16[48,2560]{1,0:T(8,128)(2,1)S(1)}, bf16[48,2560]{1,0:T(8,128)(2,1)S(1)}, u32[]{:S(2)}, u32[]{:S(2)}) collective-permute-start(bf16[48,2560]{1,0:T(8,128)(2,1)S(1)} %shard_map.130.after_ref.mine_ref), channel_id=1, source_target_pairs={{4,0},{8,12},{5,1},{9,13},{6,2},{10,14},{7,3},{11,15},{20,16},{24,... | collective-permute-start | bytes 737288 | tf_op jit(solution)/shard_map/ppermute | solution.py:338
  57.7 14.7 %collective-permute-start.19 = (bf16[48,2560]{1,0:T(8,128)(2,1)S(1)}, bf16[48,2560]{1,0:T(8,128)(2,1)S(1)}, u32[]{:S(2)}, u32[]{:S(2)}) collective-permute-start(bf16[48,2560]{1,0:T(8,128)(2,1)S(1)} %shard_map.132.after_ref.mine_ref), channel_id=1, source_target_pairs={{0,8},{4,12},{8,0},{12,4},{1,9},{5,13},{9,1},{13,5},{2,10},{6,14},... | collective-permute-start | bytes 737288 | tf_op jit(solution)/shard_map/ppermute | solution.py:368
  63.0 9.7 %collective-permute-start.18 = (bf16[48,2560]{1,0:T(8,128)(2,1)S(1)}, bf16[48,2560]{1,0:T(8,128)(2,1)S(1)}, u32[]{:S(2)}, u32[]{:S(2)}) collective-permute-start(bf16[48,2560]{1,0:T(8,128)(2,1)S(1)} %shard_map.133.after_ref.mine_ref), channel_id=1, source_target_pairs={{4,0},{8,12},{5,1},{9,13},{6,2},{10,14},{7,3},{11,15},{20,16},{24,... | collective-permute-start | bytes 737288 | tf_op jit(solution)/shard_map/ppermute | solution.py:338
  69.9 6.0 %collective-permute-start.20 = (bf16[288,320]{1,0:T(8,128)(2,1)S(1)}, bf16[288,320]{1,0:T(8,128)(2,1)S(1)}, u32[]{:S(2)}, u32[]{:S(2)}) collective-permute-start(bf16[288,320]{1,0:T(8,128)(2,1)S(1)} %shard_map.137.after_ref), channel_id=1, source_target_pairs={{0,16},{16,0},{1,17},{17,1},{2,18},{18,2},{3,19},{19,3},{4,20},{20... | collective-permute-start | bytes 552968 | tf_op jit(solution)/shard_map/ppermute | solution.py:353
  73.4 4.5 %copy-start = (s32[1,8]{1,0:T(1,128)S(1)}, s32[1,8]{1,0:T(1,128)}, u32[]{:S(2)}) copy-start(s32[1,8]{1,0:T(1,128)} %counts_ref.1) | copy-start | bytes 100
  73.4 14.0 %copy-start.2 = (s32[128]{0:T(128)S(1)}, s32[128]{0:T(128)}, u32[]{:S(2)}) copy-start(s32[128]{0:T(128)} %param.19) | copy-start | bytes 1540
  73.4 14.0 %copy-start.3 = (s32[128]{0:T(128)S(1)}, s32[128]{0:T(128)}, u32[]{:S(2)}) copy-start(s32[128]{0:T(128)} %param.17) | copy-start | bytes 1540
  73.5 14.0 %copy-start.4 = (s32[128,1]{0,1:T(1,128)S(1)}, s32[128,1]{0,1:T(1,128)}, u32[]{:S(2)}) copy-start(s32[128,1]{0,1:T(1,128)} %param.18) | copy-start | bytes 1540
  73.5 4.4 %collective-permute-start.21 = (bf16[96,320]{1,0:T(8,128)(2,1)S(1)}, bf16[96,320]{1,0:T(8,128)(2,1)S(1)}, u32[]{:S(2)}, u32[]{:S(2)}) collective-permute-start(bf16[96,320]{1,0:T(8,128)(2,1)S(1)} %shard_map.141.after_ref), channel_id=1, source_target_pairs={{0,16},{16,0},{1,17},{17,1},{2,18},{18,2},{3,19},{19,3},{4,20},{20... | collective-permute-start | bytes 184328 | tf_op jit(solution)/shard_map/ppermute | solution.py:353
  78.8 1.2 %collective-permute-start.22 = (f32[12,384]{1,0:T(8,128)S(1)}, f32[12,384]{1,0:T(8,128)S(1)}, u32[]{:S(2)}, u32[]{:S(2)}) collective-permute-start(f32[12,384]{1,0:T(8,128)S(1)} %shard_map.143), channel_id=1, source_target_pairs={{0,1},{1,0},{2,3},{3,2},{4,5},{5,4},{6,7},{7,6},{8,9},{9,8},{10,11... | collective-permute-start | bytes 55304 | tf_op jit(solution)/shard_map/ppermute | solution.py:406
  80.0 3.7 %collective-permute-start.23 = (bf16[12,384]{1,0:T(8,128)(2,1)S(1)}, bf16[12,384]{1,0:T(8,128)(2,1)S(1)}, u32[]{:S(2)}, u32[]{:S(2)}) collective-permute-start(bf16[12,384]{1,0:T(8,128)(2,1)S(1)} %fusion), channel_id=1, source_target_pairs={{0,2},{1,3},{2,0},{3,1},{4,6},{5,7},{6,4},{7,5},{8,10},{9,11},{10,... | collective-permute-start | bytes 27656 | tf_op jit(solution)/shard_map/ppermute | solution.py:409
  83.7 6.9 %copy-start.1 = (f32[12,384]{1,0:T(8,128)}, f32[12,384]{1,0:T(8,128)S(1)}, u32[]{:S(2)}) copy-start(f32[12,384]{1,0:T(8,128)S(1)} %convert_add_fusion) | copy-start | bytes 55300
  83.9 3.6 %collective-permute-start.24 = (f32[1,96]{1,0:T(1,128)S(1)}, f32[1,96]{1,0:T(1,128)S(1)}, u32[]{:S(2)}, u32[]{:S(2)}) collective-permute-start(f32[1,96]{1,0:T(1,128)S(1)} %reshape.10), channel_id=1, source_target_pairs={{0,4},{4,0},{8,12},{12,8},{1,5},{5,1},{9,13},{13,9},{2,6},{6,2},{1... | collective-permute-start | bytes 1160 | tf_op jit(solution)/shard_map/ppermute | solution.py:419
  83.9 5.4 %collective-permute-start.25 = (f32[1,96]{1,0:T(1,128)S(1)}, f32[1,96]{1,0:T(1,128)S(1)}, u32[]{:S(2)}, u32[]{:S(2)}) collective-permute-start(f32[1,96]{1,0:T(1,128)S(1)} %reshape.10), channel_id=1, source_target_pairs={{0,12},{4,8},{8,4},{12,0},{1,13},{5,9},{9,5},{13,1},{2,14},{6,10},... | collective-permute-start | bytes 1160 | tf_op jit(solution)/shard_map/ppermute | solution.py:419
  85.3 4.4 %collective-permute-start.26 = (f32[1,96]{1,0:T(1,128)S(1)}, f32[1,96]{1,0:T(1,128)S(1)}, u32[]{:S(2)}, u32[]{:S(2)}) collective-permute-start(f32[1,96]{1,0:T(1,128)S(1)} %reshape.10), channel_id=1, source_target_pairs={{0,8},{4,12},{8,0},{12,4},{1,9},{5,13},{9,1},{13,5},{2,10},{6,14},... | collective-permute-start | bytes 1160 | tf_op jit(solution)/shard_map/ppermute | solution.py:419
